TPU v7x, 32 devices: a whole 2x2x4 slice. The times are simulated.
32 devices in a mesh: tm: 4 (over y, x), sx: 2 (over core), sy: 4 (over z).
Axes of the slice: x: 2, y: 2, z: 4, core: 2. Of those that a mesh axis runs over, the one named last changes fastest.
Arguments:
- frames: bfloat16 [8, 64, 64, 512], P('tm', 'sx', 'sy'), may hold values from -6 to 6
- input_weight: bfloat16 [3, 3, 512, 512], replicated, may hold values from -0.09375 to 0.09375
- output_weight: bfloat16 [3, 3, 512, 512], replicated, may hold values from -0.09375 to 0.09375
- pole_index: int32 [512], replicated, may hold values from 0 to 15
- gelu_scale: float32 [512], replicated, may hold values from 0.15 to 0.6
- start_state: float32 [64, 64, 512], P('sx', 'sy'), may hold values from -12 to 12
Outputs:
- result: bfloat16 [8, 64, 64, 512], P('tm', 'sx', 'sy')
All inputs are finite; a program needn't handle non-finite values.
Results may differ from a plain program's by a relative error of at most 0.0049.
Values may be sent and summed in bfloat16 or wider, within the bound.
No kernel may reach another device: no remote copies, remote signals or barrier semaphores. Data moves between devices by JAX's collectives and lax.ppermute only.
A program may use at most 128 MiB of HBM per device.

v0:
```python
import math

import jax
import jax.numpy as jnp
from jax import lax
from jax.sharding import PartitionSpec as P

NPOLES = 16


def extended(cells, sides, width):
    for axis, dim in sides:
        count = lax.axis_size(axis)
        ends = count - 1
        head = lax.slice_in_dim(cells, 0, width, axis=dim)
        tail = lax.slice_in_dim(cells, cells.shape[dim] - width, cells.shape[dim], axis=dim)
        cells = jnp.concatenate(
            [
                lax.ppermute(tail, axis, [(i, (i + 1) % count) for i in range(ends)]),
                cells,
                lax.ppermute(head, axis, [((i + 1) % count, i) for i in range(ends)]),
            ],
            axis=dim,
        )
    return cells


def convolve_tile(padded, weight, rows, cols):
    count = padded.shape[0]
    channels = weight.shape[2]
    total = jnp.zeros((count * rows * cols, channels), jnp.float32)
    for row_shift in range(3):
        for col_shift in range(3):
            window = padded[
                :, row_shift : row_shift + rows, col_shift : col_shift + cols, :
            ].reshape(-1, channels)
            total = total + jnp.dot(
                window, weight[row_shift, col_shift], preferred_element_type=jnp.float32
            )
    return total.reshape(count, rows, cols, channels)


def on_device(frames, input_weight, output_weight, pole_index, gelu_scale, start_state):
    count, rows, cols, channels = frames.shape
    padded = extended(frames, (("sx", 1), ("sy", 2)), 1)
    drive = convolve_tile(padded, input_weight, rows, cols)
    decay = jnp.exp(
        -0.001 * jnp.exp(pole_index.astype(jnp.float32) * (math.log(300.0) / (NPOLES - 1)))
    )
    state = jnp.zeros(drive.shape[1:], jnp.float32)
    partial_states = []
    for step in range(count):
        state = decay * state + drive[step]
        partial_states.append(state)
    carried = decay**count
    all_decay, all_state = (
        lax.all_gather(carried[None], "tm", axis=0, tiled=True),
        lax.all_gather(state[None], "tm", axis=0, tiled=True),
    )
    position = lax.axis_index("tm")

    def fold_step(index, current):
        updated = all_decay[index] * current + all_state[index]
        return jnp.where(index < position, updated, current)

    incoming = lax.fori_loop(0, lax.axis_size("tm"), fold_step, start_state)
    activated = []
    for step in range(count):
        full_state = decay ** (step + 1) * incoming + partial_states[step]
        activated.append(jax.nn.gelu(gelu_scale * full_state).astype(jnp.bfloat16))
    mixed = jnp.stack(activated, axis=0)
    padded_mixed = extended(mixed, (("sx", 1), ("sy", 2)), 1)
    return convolve_tile(padded_mixed, output_weight, rows, cols).astype(jnp.bfloat16)


def solution(mesh):
    return jax.shard_map(
        on_device,
        mesh=mesh,
        in_specs=(P("tm", "sx", "sy", None), P(), P(), P(), P(), P("sx", "sy", None)),
        out_specs=P("tm", "sx", "sy", None),
        check_vma=False,
    )
```

profile of v0, /device:TPU:0, one launch (start us, length us, event | category | flops | bytes accessed | tf_op | source)
XLA Modules:
  0.0 127.1 jit_solution(17529359763058014917)
XLA Ops:
  6.5 0.0 all-gather.4.cloned.1.call-start
  6.5 1.2 copy-done.1
  7.8 2.5 %collective-permute-start = (bf16[2,1,16,512]{3,2,1,0:T(8,128)(2,1)S(1)}, bf16[2,1,16,512]{3,2,1,0:T(8,128)(2,1)S(1)}, u32[]{:S(2)}, u32[]{:S(2)}) collective-permute-start(bf16[2,1,16,512]{3,2,1,0:T(8,128)(2,1)S(1)} %get-tuple-element.143), channel_id=1, source_target_pairs={{0,4},{1,5},{2,6},{3,7},{8,12},{9,13},{10,14},{11,15},{16,20},{17,... | collective-permute-start | bytes 98312 | tf_op jit(solution)/shard_map/ppermute | solution.py:19
  10.3 1.3 %collective-permute-start.1 = (bf16[2,1,16,512]{3,2,1,0:T(8,128)(2,1)S(1)}, bf16[2,1,16,512]{3,2,1,0:T(8,128)(2,1)S(1)}, u32[]{:S(2)}, u32[]{:S(2)}) collective-permute-start(bf16[2,1,16,512]{3,2,1,0:T(8,128)(2,1)S(1)} %get-tuple-element.144), channel_id=1, source_target_pairs={{4,0},{5,1},{6,2},{7,3},{12,8},{13,9},{14,10},{15,11},{20,16},{21,... | collective-permute-start | bytes 98312 | tf_op jit(solution)/shard_map/ppermute | solution.py:21
  11.6 0.0 slice-start.1
  11.6 1.8 %fusion.51 = f32[1024,512]{1,0:T(8,128)S(1)} fusion(bf16[1024,512]{1,0:T(8,128)(2,1)S(1)} %bitcast.124, bf16[3,3,512,512]{3,2,1,0:T(8,128)(2,1)} %param.9), kind=kOutput, calls=%fused_computation.77 | convolution fusion | flops 536870912 | bytes 3670016 | tf_op jit(solution)/shard_map/dot_general | solution.py:37
  13.4 0.0 copy-done.3
  13.4 0.0 collective-permute-done
  13.4 0.0 collective-permute-done.1
  13.4 0.3 pad_maximum_fusion.9
  13.7 0.2 fusion.87
  14.0 4.3 %collective-permute-start.2 = (bf16[2,34,1,512]{3,1,2,0:T(8,128)(2,1)S(1)}, bf16[2,34,1,512]{3,1,2,0:T(8,128)(2,1)S(1)}, u32[]{:S(2)}, u32[]{:S(2)}) collective-permute-start(bf16[2,34,1,512]{3,1,2,0:T(8,128)(2,1)S(1)} %copy.12), channel_id=1, source_target_pairs={{0,1},{1,2},{2,3},{4,5},{5,6},{6,7},{8,9},{9,10},{10,11},{12,13},{... | collective-permute-start | bytes 208904 | tf_op jit(solution)/shard_map/ppermute | solution.py:19
  18.3 1.3 %collective-permute-start.3 = (bf16[2,34,1,512]{3,1,2,0:T(8,128)(2,1)S(1)}, bf16[2,34,1,512]{3,1,2,0:T(8,128)(2,1)S(1)}, u32[]{:S(2)}, u32[]{:S(2)}) collective-permute-start(bf16[2,34,1,512]{3,1,2,0:T(8,128)(2,1)S(1)} %copy.14), channel_id=1, source_target_pairs={{1,0},{2,1},{3,2},{5,4},{6,5},{7,6},{9,8},{10,9},{11,10},{13,12},{... | collective-permute-start | bytes 208904 | tf_op jit(solution)/shard_map/ppermute | solution.py:21
  19.6 0.0 slice-done
  19.6 0.0 slice-done.1
  19.7 0.7 fusion.45
  20.4 0.7 fusion.57
  21.1 0.0 collective-permute-done.2
  21.1 0.1 copy.13
  21.2 4.2 %collective-permute-done.3 = bf16[2,34,1,512]{3,1,2,0:T(8,128)(2,1)S(1)} collective-permute-done((bf16[2,34,1,512]{3,1,2,0:T(8,128)(2,1)S(1)}, bf16[2,34,1,512]{3,1,2,0:T(8,128)(2,1)S(1)}, u32[]{:S(2)}, u32[]{:S(2)}) %collective-permute-start.3) | collective-permute-done | bytes 69664 | tf_op jit(solution)/shard_map/ppermute | solution.py:21
  25.4 0.1 copy.15
  25.5 3.3 %pad_maximum_fusion.6 = (bf16[2,32,16,512]{3,2,1,0:T(8,128)(2,1)S(1)}, bf16[2,32,16,512]{3,2,1,0:T(8,128)(2,1)S(1)}, bf16[2,32,16,512]{3,2,1,0:T(8,128)(2,1)S(1)...) fusion(bf16[2,34,1,512]{3,2,1,0:T(2,128)(2,1)S(1)} %copy.15, ...), kind=kLoop, calls=%fused_computation.46 | loop fusion | flops 12582912 | bytes 7544832 | tf_op jit(solution)/shard_map/concatenate | solution.py:17
  28.8 0.7 fusion.47
  29.5 0.7 fusion.49
  30.2 0.7 fusion.53
  30.9 0.7 fusion.55
  31.6 0.7 fusion.59
  32.3 1.2 add_add_fusion
  33.5 0.2 fusion.84
  33.7 0.0 copy-start
  33.7 1.2 multiply_add_fusion
  34.9 0.0 all-gather.4.cloned.1.call-update
  35.0 8.1 %all-gather.1 = f32[4,1,512]{2,1,0:T(1,128)S(1)} all-gather(f32[1,1,512]{2,1,0:T(1,128)S(1)} %bitcast.144), channel_id=2, replica_groups=mesh['tm'=4,'sx'=2,'sy'=4] {'tm'}, dimensions={0}, use_global_device_ids=true | all-gather | bytes 10240 | tf_op jit(solution)/shard_map/all_gather | solution.py:57
  43.0 45.0 %all-gather.4.cloned.1.call-done = f32[4,32,16,512]{3,2,1,0:T(8,128)} async-done(((f32[1,32,16,512]{3,2,1,0:T(8,128)}), f32[4,32,16,512]{3,2,1,0:T(8,128)}) %all-gather.4.cloned.1.call-update) | async-done | bytes 4194320 | tf_op jit(solution)/shard_map/all_gather | solution.py:58
  88.1 0.0 copy-done
  88.1 6.9 %while.13 = (s32[]{:T(128)}, f32[32,16,512]{2,1,0:T(8,128)S(1)}, s32[]{:T(128)}, f32[4,512]{1,0:T(4,128)S(1)}, f32[4,32,16,512]{3,2,1,0:T(8,128)}, /*index=5*/s32[]{:T(128)}) while((s32[]{:T(128)}, f32[32,16,512]{2,1,0:T(8,128)S(1)}, s32[]{:T(128)}, f32[4,512]{1,0:T(4,128)S(1)}, f32[4,32,16,512]{3,2,1,0:T(8,128)}, /*index=5*/s32[]{:T(128)}) %tuple.61), condition=%wide.region_1.2_spmd, body=%wide.region_0.1_spmd.sunk | while | flops 786435 | bytes 3151959 | solution.py:66
  88.1 1.7 %fusion.108 = f32[32,16,512]{2,1,0:T(8,128)S(1)} fusion(f32[32,16,512]{2,1,0:T(8,128)S(1)} %get-tuple-element.189, f32[4,32,16,512]{3,2,1,0:T(8,128)} %get-tuple-element.198, s32[]{:T(128)} %get-tuple-element.188, f32[512]{0:T(512)S(1)} %bitcast.142, pred[]{:T(512)S(6)} %lt.20), kind=kLoop, calls=%fused_computation.1.clone.1 | loop fusion | flops 786432 | bytes 3147781 | tf_op jit(solution)/shard_map/while/body/eval_jaxpr/jit(_where)/select_n | solution.py:64
  89.8 1.7 %fusion.108 = f32[32,16,512]{2,1,0:T(8,128)S(1)} fusion(f32[32,16,512]{2,1,0:T(8,128)S(1)} %get-tuple-element.189, f32[4,32,16,512]{3,2,1,0:T(8,128)} %get-tuple-element.198, s32[]{:T(128)} %get-tuple-element.188, f32[512]{0:T(512)S(1)} %bitcast.142, pred[]{:T(512)S(6)} %lt.20), kind=kLoop, calls=%fused_computation.1.clone.1 | loop fusion | flops 786432 | bytes 3147781 | tf_op jit(solution)/shard_map/while/body/eval_jaxpr/jit(_where)/select_n | solution.py:64
  91.6 1.7 %fusion.108 = f32[32,16,512]{2,1,0:T(8,128)S(1)} fusion(f32[32,16,512]{2,1,0:T(8,128)S(1)} %get-tuple-element.189, f32[4,32,16,512]{3,2,1,0:T(8,128)} %get-tuple-element.198, s32[]{:T(128)} %get-tuple-element.188, f32[512]{0:T(512)S(1)} %bitcast.142, pred[]{:T(512)S(6)} %lt.20), kind=kLoop, calls=%fused_computation.1.clone.1 | loop fusion | flops 786432 | bytes 3147781 | tf_op jit(solution)/shard_map/while/body/eval_jaxpr/jit(_where)/select_n | solution.py:64
  93.3 1.7 %fusion.108 = f32[32,16,512]{2,1,0:T(8,128)S(1)} fusion(f32[32,16,512]{2,1,0:T(8,128)S(1)} %get-tuple-element.189, f32[4,32,16,512]{3,2,1,0:T(8,128)} %get-tuple-element.198, s32[]{:T(128)} %get-tuple-element.188, f32[512]{0:T(512)S(1)} %bitcast.142, pred[]{:T(512)S(6)} %lt.20), kind=kLoop, calls=%fused_computation.1.clone.1 | loop fusion | flops 786432 | bytes 3147781 | tf_op jit(solution)/shard_map/while/body/eval_jaxpr/jit(_where)/select_n | solution.py:64
  95.0 0.0 copy-done.2
  95.0 1.0 fusion.80
  96.0 1.7 %collective-permute-start.4 = (bf16[2,1,16,512]{3,2,1,0:T(8,128)(2,1)S(1)}, bf16[2,1,16,512]{3,2,1,0:T(8,128)(2,1)S(1)}, u32[]{:S(2)}, u32[]{:S(2)}) collective-permute-start(bf16[2,1,16,512]{3,2,1,0:T(8,128)(2,1)S(1)} %get-tuple-element.138), channel_id=1, source_target_pairs={{0,4},{1,5},{2,6},{3,7},{8,12},{9,13},{10,14},{11,15},{16,20},{17,... | collective-permute-start | bytes 98312 | tf_op jit(solution)/shard_map/ppermute | solution.py:19
  97.8 1.3 %collective-permute-start.5 = (bf16[2,1,16,512]{3,2,1,0:T(8,128)(2,1)S(1)}, bf16[2,1,16,512]{3,2,1,0:T(8,128)(2,1)S(1)}, u32[]{:S(2)}, u32[]{:S(2)}) collective-permute-start(bf16[2,1,16,512]{3,2,1,0:T(8,128)(2,1)S(1)} %get-tuple-element.139), channel_id=1, source_target_pairs={{4,0},{5,1},{6,2},{7,3},{12,8},{13,9},{14,10},{15,11},{20,16},{21,... | collective-permute-start | bytes 98312 | tf_op jit(solution)/shard_map/ppermute | solution.py:21
  99.1 0.0 collective-permute-done.4
  99.1 1.8 %collective-permute-done.5 = bf16[2,1,16,512]{3,2,1,0:T(8,128)(2,1)S(1)} collective-permute-done((bf16[2,1,16,512]{3,2,1,0:T(8,128)(2,1)S(1)}, bf16[2,1,16,512]{3,2,1,0:T(8,128)(2,1)S(1)}, u32[]{:S(2)}, u32[]{:S(2)}) %collective-permute-start.5) | collective-permute-done | bytes 32800 | tf_op jit(solution)/shard_map/ppermute | solution.py:21
  100.9 0.2 pad_maximum_fusion.10
  101.1 3.7 %collective-permute-start.6 = (bf16[2,34,1,512]{3,2,1,0:T(2,128)(2,1)S(1)}, bf16[2,34,1,512]{3,2,1,0:T(2,128)(2,1)S(1)}, u32[]{:S(2)}, u32[]{:S(2)}) collective-permute-start(bf16[2,34,1,512]{3,2,1,0:T(2,128)(2,1)S(1)} %get-tuple-element.129), channel_id=1, source_target_pairs={{0,1},{1,2},{2,3},{4,5},{5,6},{6,7},{8,9},{9,10},{10,11},{12,13},{... | collective-permute-start | bytes 208904 | tf_op jit(solution)/shard_map/ppermute | solution.py:19
  104.7 0.0 slice-start.3
  104.8 1.6 %collective-permute-start.7 = (bf16[2,34,1,512]{3,2,1,0:T(2,128)(2,1)S(1)}, bf16[2,34,1,512]{3,2,1,0:T(2,128)(2,1)S(1)}, u32[]{:S(2)}, u32[]{:S(2)}) collective-permute-start(bf16[2,34,1,512]{3,2,1,0:T(2,128)(2,1)S(1)} %get-tuple-element.128), channel_id=1, source_target_pairs={{1,0},{2,1},{3,2},{5,4},{6,5},{7,6},{9,8},{10,9},{11,10},{13,12},{... | collective-permute-start | bytes 208904 | tf_op jit(solution)/shard_map/ppermute | solution.py:21
  106.4 0.2 pad_maximum_fusion.4
  106.6 1.7 %fusion.25 = f32[1024,512]{1,0:T(8,128)S(1)} fusion(bf16[1024,512]{1,0:T(8,128)(2,1)S(1)} %bitcast.135, bf16[3,3,512,512]{3,2,1,0:T(8,128)(2,1)} %param.10), kind=kOutput, calls=%fused_computation.53 | convolution fusion | flops 536870912 | bytes 3670016 | tf_op jit(solution)/shard_map/dot_general | solution.py:37
  108.4 0.7 fusion.31
  109.1 0.7 fusion.37
  109.8 0.0 collective-permute-done.6
  109.8 2.5 %collective-permute-done.7 = bf16[2,34,1,512]{3,2,1,0:T(2,128)(2,1)S(1)} collective-permute-done((bf16[2,34,1,512]{3,2,1,0:T(2,128)(2,1)S(1)}, bf16[2,34,1,512]{3,2,1,0:T(2,128)(2,1)S(1)}, u32[]{:S(2)}, u32[]{:S(2)}) %collective-permute-start.7) | collective-permute-done | bytes 69664 | tf_op jit(solution)/shard_map/ppermute | solution.py:21
  112.2 1.1 pad_maximum_fusion
  113.3 0.9 fusion.85
  114.2 0.7 fusion.27
  114.9 0.7 fusion.29
  115.6 0.7 fusion.33
  116.3 0.7 fusion.35
  117.0 0.7 fusion.39
  117.8 2.5 %add_convert_fusion = bf16[1024,512]{1,0:T(8,128)(2,1)} fusion(f32[1024,512]{1,0:T(8,128)S(1)} %fusion.25, f32[1024,512]{1,0:T(8,128)S(1)} %fusion.27, f32[1024,512]{1,0:T(8,128)S(1)} %fusion.29, f32[1024,512]{1,0:T(8,128)S(1)} %fusion.31, f32[1024,512]{1,0:T(8,128)S(1)} %fusion.33, f32[1024,512]{1,0:T(8,128)S(1)} %fusion.35, f32[1024,512]{1,0:T(8,128)S(1)} %fusion.39, ...), kind=kOutput, calls=%fused_computation.7 | convolution fusion | flops 541589504 | bytes 19398656 | tf_op jit(solution)/shard_map/dot_general | solution.py:37
  (21 shorter events, 0.1 us)
Async XLA Ops:
  6.5 1.2 copy-start.1
  6.5 81.5 %all-gather.4.cloned.1.call-start = ((), (), s32[]{:S(2)}) async-start(), calls=%async_computation | async-start | bytes 5242880 | tf_op jit(solution)/shard_map/all_gather | solution.py:58
  6.5 13.1 %slice-start = ((s8[4718592]{0:T(1024)(128)(4,1)}), s8[4194304]{0:T(1024)(128)(4,1)S(1)}, s32[]{:S(2)}) async-start(s8[4718592]{0:T(1024)(128)(4,1)} %bitcast.120), calls=%async_computation.1 | async-start | bytes 8388608
  7.8 5.6 %copy-start.3 = (s32[512]{0:T(512)S(1)}, s32[512]{0:T(512)}, u32[]{:S(2)}) copy-start(s32[512]{0:T(512)} %param.11) | copy-start | bytes 6148
  7.8 5.6 %collective-permute-start = (bf16[2,1,16,512]{3,2,1,0:T(8,128)(2,1)S(1)}, bf16[2,1,16,512]{3,2,1,0:T(8,128)(2,1)S(1)}, u32[]{:S(2)}, u32[]{:S(2)}) collective-permute-start(bf16[2,1,16,512]{3,2,1,0:T(8,128)(2,1)S(1)} %get-tuple-element.143), channel_id=1, source_target_pairs={{0,4},{1,5},{2,6},{3,7},{8,12},{9,13},{10,14},{11,15},{16,20},{17,... | collective-permute-start | bytes 98312 | tf_op jit(solution)/shard_map/ppermute | solution.py:19
  10.3 3.2 %collective-permute-start.1 = (bf16[2,1,16,512]{3,2,1,0:T(8,128)(2,1)S(1)}, bf16[2,1,16,512]{3,2,1,0:T(8,128)(2,1)S(1)}, u32[]{:S(2)}, u32[]{:S(2)}) collective-permute-start(bf16[2,1,16,512]{3,2,1,0:T(8,128)(2,1)S(1)} %get-tuple-element.144), channel_id=1, source_target_pairs={{4,0},{5,1},{6,2},{7,3},{12,8},{13,9},{14,10},{15,11},{20,16},{21,... | collective-permute-start | bytes 98312 | tf_op jit(solution)/shard_map/ppermute | solution.py:21
  11.6 8.1 %slice-start.1 = ((s8[4718592]{0:T(1024)(128)(4,1)}), s8[524288]{0:T(1024)(128)(4,1)S(1)}, s32[]{:S(2)}) async-start(s8[4718592]{0:T(1024)(128)(4,1)} %bitcast.120), calls=%async_computation.2 | async-start | bytes 1048576
  14.0 7.1 %collective-permute-start.2 = (bf16[2,34,1,512]{3,1,2,0:T(8,128)(2,1)S(1)}, bf16[2,34,1,512]{3,1,2,0:T(8,128)(2,1)S(1)}, u32[]{:S(2)}, u32[]{:S(2)}) collective-permute-start(bf16[2,34,1,512]{3,1,2,0:T(8,128)(2,1)S(1)} %copy.12), channel_id=1, source_target_pairs={{0,1},{1,2},{2,3},{4,5},{5,6},{6,7},{8,9},{9,10},{10,11},{12,13},{... | collective-permute-start | bytes 208904 | tf_op jit(solution)/shard_map/ppermute | solution.py:19
  18.3 7.1 %collective-permute-start.3 = (bf16[2,34,1,512]{3,1,2,0:T(8,128)(2,1)S(1)}, bf16[2,34,1,512]{3,1,2,0:T(8,128)(2,1)S(1)}, u32[]{:S(2)}, u32[]{:S(2)}) collective-permute-start(bf16[2,34,1,512]{3,1,2,0:T(8,128)(2,1)S(1)} %copy.14), channel_id=1, source_target_pairs={{1,0},{2,1},{3,2},{5,4},{6,5},{7,6},{9,8},{10,9},{11,10},{13,12},{... | collective-permute-start | bytes 208904 | tf_op jit(solution)/shard_map/ppermute | solution.py:21
  33.7 54.4 %copy-start = (f32[32,16,512]{2,1,0:T(8,128)S(1)}, f32[32,16,512]{2,1,0:T(8,128)}, u32[]{:S(2)}) copy-start(f32[32,16,512]{2,1,0:T(8,128)} %param.13) | copy-start | bytes 3145732
  88.1 7.0 %copy-start.2 = (f32[512]{0:T(512)S(1)}, f32[512]{0:T(512)}, u32[]{:S(2)}) copy-start(f32[512]{0:T(512)} %param.12) | copy-start | bytes 6148
  96.0 3.1 %collective-permute-start.4 = (bf16[2,1,16,512]{3,2,1,0:T(8,128)(2,1)S(1)}, bf16[2,1,16,512]{3,2,1,0:T(8,128)(2,1)S(1)}, u32[]{:S(2)}, u32[]{:S(2)}) collective-permute-start(bf16[2,1,16,512]{3,2,1,0:T(8,128)(2,1)S(1)} %get-tuple-element.138), channel_id=1, source_target_pairs={{0,4},{1,5},{2,6},{3,7},{8,12},{9,13},{10,14},{11,15},{16,20},{17,... | collective-permute-start | bytes 98312 | tf_op jit(solution)/shard_map/ppermute | solution.py:19
  97.8 3.1 %collective-permute-start.5 = (bf16[2,1,16,512]{3,2,1,0:T(8,128)(2,1)S(1)}, bf16[2,1,16,512]{3,2,1,0:T(8,128)(2,1)S(1)}, u32[]{:S(2)}, u32[]{:S(2)}) collective-permute-start(bf16[2,1,16,512]{3,2,1,0:T(8,128)(2,1)S(1)} %get-tuple-element.139), channel_id=1, source_target_pairs={{4,0},{5,1},{6,2},{7,3},{12,8},{13,9},{14,10},{15,11},{20,16},{21,... | collective-permute-start | bytes 98312 | tf_op jit(solution)/shard_map/ppermute | solution.py:21
  100.9 7.5 %slice-start.2 = ((s8[4718592]{0:T(1024)(128)(4,1)}), s8[4194304]{0:T(1024)(128)(4,1)S(1)}, s32[]{:S(2)}) async-start(s8[4718592]{0:T(1024)(128)(4,1)} %bitcast.122), calls=%async_computation.3 | async-start | bytes 8388608
  101.1 8.7 %collective-permute-start.6 = (bf16[2,34,1,512]{3,2,1,0:T(2,128)(2,1)S(1)}, bf16[2,34,1,512]{3,2,1,0:T(2,128)(2,1)S(1)}, u32[]{:S(2)}, u32[]{:S(2)}) collective-permute-start(bf16[2,34,1,512]{3,2,1,0:T(2,128)(2,1)S(1)} %get-tuple-element.129), channel_id=1, source_target_pairs={{0,1},{1,2},{2,3},{4,5},{5,6},{6,7},{8,9},{9,10},{10,11},{12,13},{... | collective-permute-start | bytes 208904 | tf_op jit(solution)/shard_map/ppermute | solution.py:19
  104.7 3.6 %slice-start.3 = ((s8[4718592]{0:T(1024)(128)(4,1)}), s8[524288]{0:T(1024)(128)(4,1)S(1)}, s32[]{:S(2)}) async-start(s8[4718592]{0:T(1024)(128)(4,1)} %bitcast.122), calls=%async_computation.4 | async-start | bytes 1048576
  104.8 7.5 %collective-permute-start.7 = (bf16[2,34,1,512]{3,2,1,0:T(2,128)(2,1)S(1)}, bf16[2,34,1,512]{3,2,1,0:T(2,128)(2,1)S(1)}, u32[]{:S(2)}, u32[]{:S(2)}) collective-permute-start(bf16[2,34,1,512]{3,2,1,0:T(2,128)(2,1)S(1)} %get-tuple-element.128), channel_id=1, source_target_pairs={{1,0},{2,1},{3,2},{5,4},{6,5},{7,6},{9,8},{10,9},{11,10},{13,12},{... | collective-permute-start | bytes 208904 | tf_op jit(solution)/shard_map/ppermute | solution.py:21
Sparse Core Ops, SparseCore 0:
  35.1 52.9 all-gather.3
where the time goes:
time: 128 us; the launch traced here: 127 us
  waiting for transfers between devices  53.5 us (42%)
  starting transfers between devices  17.7 us (14%)
  matrix products  17 us (13%)
  other arithmetic  14.1 us (11%)
  between operations  13.8 us (11%)
  blocking collectives  8.07 us (6%)
  local copies, waits for them, and re-layouts  2.8 us (2%)
    all_gather x1, waiting for transfers between devices, on_device(): lax.all_gather(state[None], 'tm', axis=0, tiled=True)  45 us
    dot_general x18, matrix products, convolve_tile(): jnp.dot(window, weight[row_shift, col_shift], preferred_element_type=jnp....  17 us
    ppermute x4, starting transfers between devices, extended(): lax.ppermute(tail, axis, [(i, (i + 1) % count) for i in range(ends)])  12.2 us
    ppermute x4, waiting for transfers between devices, extended(): lax.ppermute(head, axis, [((i + 1) % count, i) for i in range(ends)])  8.48 us
    all_gather x1, blocking collectives, on_device(): lax.all_gather(carried[None], 'tm', axis=0, tiled=True)  8.07 us
    select_n x4, other arithmetic, fold_step(): return jnp.where(index < position, updated, current)  6.81 us
    ppermute x4, starting transfers between devices, extended(): lax.ppermute(head, axis, [((i + 1) % count, i) for i in range(ends)])  5.48 us
    concatenate x5, other arithmetic, extended(): jnp.concatenate([lax.ppermute(tail, axis, [(i, (i + 1) % count) for i in...  5.07 us
  transfers between devices with their start and end apart: 9, of which 4 were waited for; matrix products, arithmetic and copies ran while one was open for 5% of the time, Pallas kernels for 0%

commit v1 on v0

v1 whole, which is shorter than its diff:
```python
import math

import jax
import jax.numpy as jnp
from jax import lax
from jax.sharding import PartitionSpec as P

NPOLES = 16


def from_neighbours(before, after, axis):
    count = lax.axis_size(axis)
    if count == 2:
        first = lax.axis_index(axis) == 0
        got = lax.ppermute(jnp.where(first, before, after), axis, [(0, 1), (1, 0)])
        zero = jnp.zeros_like(got)
        return jnp.where(first, zero, got), jnp.where(first, got, zero)
    return (
        lax.ppermute(before, axis, [(i, i + 1) for i in range(count - 1)]),
        lax.ppermute(after, axis, [(i + 1, i) for i in range(count - 1)]),
    )


def pack(parts):
    return jnp.concatenate([part.reshape(-1, part.shape[-1]) for part in parts], axis=0)


def unpack(packed, parts):
    out, at = [], 0
    for part in parts:
        size = math.prod(part.shape[:-1])
        out.append(packed[at : at + size].reshape(part.shape))
        at += size
    return out


def extended(cells, start, axis, dim):
    def ends(width, array, where):
        size = array.shape[where]
        return (
            lax.slice_in_dim(array, size - width, size, axis=where),
            lax.slice_in_dim(array, 0, width, axis=where),
        )

    tail, head = ends(2, cells, dim + 1)
    start_tail, start_head = ends(1, start, dim)
    before = [tail, start_tail.astype(jnp.bfloat16)]
    after = [head, start_head.astype(jnp.bfloat16)]
    low, high = from_neighbours(pack(before), pack(after), axis)
    low, high = unpack(low, before), unpack(high, after)
    cells = jnp.concatenate([low[0], cells, high[0]], axis=dim + 1)
    start = jnp.concatenate(
        [low[1].astype(jnp.float32), start, high[1].astype(jnp.float32)], axis=dim
    )
    return cells, start


def convolve(cells, weight):
    return lax.conv_general_dilated(
        cells,
        weight,
        (1, 1),
        "VALID",
        dimension_numbers=("NHWC", "HWIO", "NHWC"),
        preferred_element_type=jnp.float32,
    )


def on_device(frames, input_weight, output_weight, pole_index, gelu_scale, start_state):
    count, rows, cols, channels = frames.shape
    groups = lax.axis_size("tm")
    position = lax.axis_index("tm")
    rate = -0.001 * jnp.exp(pole_index.astype(jnp.float32) * (math.log(300.0) / (NPOLES - 1)))
    decay = jnp.exp(rate)

    cells, start = extended(frames, start_state, "sx", 0)
    cells, start = extended(cells, start, "sy", 1)
    drive = convolve(cells, input_weight)
    state = drive[0]
    partial_states = [state]
    for step in range(1, count):
        state = decay * state + drive[step]
        partial_states.append(state)

    flat = state.reshape(-1, channels).astype(jnp.bfloat16)
    used = flat.shape[0]
    block = -(-used // (groups * 16)) * 16
    flat = jnp.pad(flat, ((0, groups * block - used), (0, 0)))
    ends = lax.all_to_all(flat.reshape(groups, block, channels), "tm", 0, 0)
    carried = jnp.exp(count * rate)
    entry = jnp.zeros((block, channels), jnp.float32)
    entries = [entry]
    for index in range(groups - 1):
        entry = carried * entry + ends[index].astype(jnp.float32)
        entries.append(entry)
    entries = lax.all_to_all(jnp.stack(entries).astype(jnp.bfloat16), "tm", 0, 0)
    entry = entries.reshape(-1, channels)[:used].reshape(state.shape).astype(jnp.float32)
    incoming = jnp.exp((count * position).astype(jnp.float32) * rate) * start + entry

    row = lax.axis_index("sx") * rows + jnp.arange(-1, rows + 1)
    col = lax.axis_index("sy") * cols + jnp.arange(-1, cols + 1)
    row_in = (row >= 0) & (row < lax.axis_size("sx") * rows)
    col_in = (col >= 0) & (col < lax.axis_size("sy") * cols)
    inside = (row_in[:, None] & col_in[None, :])[:, :, None]
    activated = []
    for step in range(count):
        full_state = jnp.exp((step + 1) * rate) * incoming + partial_states[step]
        mixed = jax.nn.gelu(gelu_scale * full_state)
        activated.append(jnp.where(inside, mixed, 0.0).astype(jnp.bfloat16))
    return convolve(jnp.stack(activated, axis=0), output_weight).astype(jnp.bfloat16)


def solution(mesh):
    return jax.shard_map(
        on_device,
        mesh=mesh,
        in_specs=(P("tm", "sx", "sy", None), P(), P(), P(), P(), P("sx", "sy", None)),
        out_specs=P("tm", "sx", "sy", None),
        check_vma=False,
    )
```

time: 128 us -> 107 us (0.84)
  waiting for transfers between devices: 53.5 us -> 19.6 us
  local copies, waits for them, and re-layouts: 2.8 us -> 29.8 us
  between operations: 13.8 us -> 0.53 us
  other arithmetic: 14.1 us -> 25.3 us
  blocking collectives: 8.07 us -> 0 us
  starting transfers between devices: 17.7 us -> 15.8 us
  matrix products: 17 us -> 15.6 us
    all_gather x1 -> x0, waiting for transfers between devices: 45 us -> none  [on_device(): lax.all_gather(state[None], 'tm', axis=0, tiled=True)]
    dot_general x18 -> x0, matrix products: 17 us -> none  [convolve_tile(): jnp.dot(window, weight[row_shift, col_shift], preferred_element_type=jnp....]
    conv_general_dilated x0 -> x2, matrix products: none -> 15.6 us  [convolve(): lax.conv_general_dilated(cells, weight, (1, 1), 'VALID', dimension_number...]
    all_to_all x0 -> x2, waiting for transfers between devices: none -> 15.1 us  [the longest x1 9.12 us: on_device(): ends = lax.all_to_all(flat.reshape(groups, block, channels), 'tm', 0, 0)]
    ppermute x8 -> x3, starting transfers between devices: 17.7 us -> 7.28 us  [the longest x1 5.47 us: from_neighbours(): lax.ppermute(before, axis, [(i, i + 1) for i in range(count - 1)])]
    conv_general_dilated x0 -> x2, other arithmetic: none -> 9.26 us  [convolve(): lax.conv_general_dilated(cells, weight, (1, 1), 'VALID', dimension_number...]
    all_to_all x0 -> x2, starting transfers between devices: none -> 8.57 us  [the longest x1 4.39 us: on_device(): lax.all_to_all(jnp.stack(entries).astype(jnp.bfloat16), 'tm', 0, 0)]
    all_gather x1 -> x0, blocking collectives: 8.07 us -> none  [on_device(): lax.all_gather(carried[None], 'tm', axis=0, tiled=True)]
  transfers between devices with their start and end apart: 9 -> 5, of which waited for: 4 -> 5; matrix products, arithmetic and copies ran while one was open for 5% -> 3% of each run, Pallas kernels for 0% -> 0%
where the time goes in v1:
time: 107 us
  local copies, waits for them, and re-layouts  29.8 us (28%)
  other arithmetic  25.3 us (24%)
  waiting for transfers between devices  19.6 us (18%)
  starting transfers between devices  15.8 us (15%)
  matrix products  15.6 us (15%)
    conv_general_dilated x2, matrix products, convolve(): lax.conv_general_dilated(cells, weight, (1, 1), 'VALID', dimension_number...  15.6 us
    conv_general_dilated x2, other arithmetic, convolve(): lax.conv_general_dilated(cells, weight, (1, 1), 'VALID', dimension_number...  9.26 us
    all_to_all x1, waiting for transfers between devices, on_device(): ends = lax.all_to_all(flat.reshape(groups, block, channels), 'tm', 0, 0)  9.12 us
    all_to_all x1, waiting for transfers between devices, on_device(): lax.all_to_all(jnp.stack(entries).astype(jnp.bfloat16), 'tm', 0, 0)  6.01 us
    ppermute x1, starting transfers between devices, from_neighbours(): lax.ppermute(before, axis, [(i, i + 1) for i in range(count - 1)])  5.47 us
    all_to_all x1, starting transfers between devices, on_device(): lax.all_to_all(jnp.stack(entries).astype(jnp.bfloat16), 'tm', 0, 0)  4.39 us
    all_to_all x1, starting transfers between devices, on_device(): ends = lax.all_to_all(flat.reshape(groups, block, channels), 'tm', 0, 0)  4.17 us
    convert_element_type x1, other arithmetic, on_device(): activated.append(jnp.where(inside, mixed, 0.0).astype(jnp.bfloat16))  3.76 us
  transfers between devices with their start and end apart: 5, of which 5 were waited for; matrix products, arithmetic and copies ran while one was open for 3% of the time, Pallas kernels for 0%

profile of v1, /device:TPU:0, one launch (start us, length us, event | category | flops | bytes accessed | tf_op | source)
XLA Modules:
  0.0 106.6 jit_solution(12647091308303822141)
XLA Ops:
  0.0 1.0 fusion.40
  1.0 1.3 %convert.24 = bf16[32,16,512]{2,1,0:T(8,128)(2,1)S(1)} convert(f32[32,16,512]{2,1,0:T(8,128)} %param.11) | non-fusion elementwise | flops 262144 | bytes 1572864 | tf_op jit(solution)/shard_map/convert.12
  2.3 0.0 copy-start.1
  2.3 0.5 collective-permute-start
  2.9 0.0 copy-done.2
  2.9 0.6 copy.13
  3.5 0.0 copy-start
  3.5 0.3 collective-permute-done
  3.9 0.0 copy-done.1
  4.0 0.2 pad_maximum_fusion.6
  4.2 0.0 copy-start.3
  4.2 0.1 reshape.231
  4.3 0.1 reshape.233
  4.3 0.2 fusion.33
  4.5 0.0 copy-done
  4.6 1.3 %collective-permute-start.2 = (bf16[178,512]{1,0:T(8,128)(2,1)S(1)}, bf16[178,512]{1,0:T(8,128)(2,1)S(1)}, u32[]{:S(2)}, u32[]{:S(2)}) collective-permute-start(bf16[178,512]{1,0:T(8,128)(2,1)S(1)} %pad_maximum_fusion.3), channel_id=1, source_target_pairs={{1,0},{2,1},{3,2},{5,4},{6,5},{7,6},{9,8},{10,9},{11,10},{13,12},{... | collective-permute-start | bytes 546824 | tf_op jit(solution)/shard_map/ppermute | solution.py:20
  5.9 5.5 %collective-permute-start.1 = (bf16[178,512]{1,0:T(8,128)(2,1)S(1)}, bf16[178,512]{1,0:T(8,128)(2,1)S(1)}, u32[]{:S(2)}, u32[]{:S(2)}) collective-permute-start(bf16[178,512]{1,0:T(8,128)(2,1)S(1)} %pad_maximum_fusion.2), channel_id=1, source_target_pairs={{0,1},{1,2},{2,3},{4,5},{5,6},{6,7},{8,9},{9,10},{10,11},{12,13},{... | collective-permute-start | bytes 546824 | tf_op jit(solution)/shard_map/ppermute | solution.py:19
  11.4 0.0 copy-done.3
  11.4 3.0 %collective-permute-done.2 = bf16[178,512]{1,0:T(8,128)(2,1)S(1)} collective-permute-done((bf16[178,512]{1,0:T(8,128)(2,1)S(1)}, bf16[178,512]{1,0:T(8,128)(2,1)S(1)}, u32[]{:S(2)}, u32[]{:S(2)}) %collective-permute-start.2) | collective-permute-done | bytes 182304 | tf_op jit(solution)/shard_map/ppermute | solution.py:20
  14.5 0.1 reshape.236
  14.5 1.1 %collective-permute-done.1 = bf16[178,512]{1,0:T(8,128)(2,1)S(1)} collective-permute-done((bf16[178,512]{1,0:T(8,128)(2,1)S(1)}, bf16[178,512]{1,0:T(8,128)(2,1)S(1)}, u32[]{:S(2)}, u32[]{:S(2)}) %collective-permute-start.1) | collective-permute-done | bytes 182304 | tf_op jit(solution)/shard_map/ppermute | solution.py:19
  15.7 0.1 reshape.235
  15.8 1.2 %maximum_bitcast_fusion = bf16[36,2,20,512]{3,2,0,1:T(8,128)(2,1)S(1)} fusion(bf16[2,36,2,512]{3,2,1,0:T(2,128)(2,1)S(1)} %reshape.236, bf16[2,2,16,512]{3,2,1,0:T(8,128)(2,1)S(1)} %bitcast.66, bf16[2,32,16,512]{3,2,1,0:T(8,128)(2,1)S(1)} %copy-done.1, bf16[2,2,16,512]{3,2,1,0:T(8,128)(2,1)S(1)} %bitcast.64, bf16[2,36,2,512]{3,2,1,0:T(2,128)(2,1)S(1)} %reshape.235), kind=kLoop, calls=%fused_computation.14 | loop fusion | flops 7372800 | bytes 2949120 | tf_op jit(solution)/shard_map/concatenate | solution.py:51
  16.9 0.0 slice-start
  16.9 1.5 %copy.24 = bf16[36,2,20,512]{3,1,2,0:T(2,128)(2,1)S(1)} copy(bf16[36,2,20,512]{3,2,0,1:T(8,128)(2,1)S(1)} %maximum_bitcast_fusion) | data formatting | bytes 2949120
  18.5 1.8 %pad.5.clone = bf16[36,2,24,512]{3,1,2,0:T(2,128)(2,1)S(1)} pad(bf16[36,2,20,512]{3,1,2,0:T(2,128)(2,1)S(1)} %copy.24, bf16[]{:T(256)} %constant.12.clone.1), padding=0_0x0_0x0_4x0_0 | pad | bytes 3244034 | tf_op jit(solution)/shard_map/concatenate | solution.py:51
  20.3 0.0 slice-start.1
  20.3 0.7 slice.108
  21.1 0.0 copy-start.6
  21.1 2.8 %fusion = bf16[36,2,8,5,512]{4,1,3,2,0:T(2,128)(2,1)S(1)} fusion(bf16[36,2,7,2,512]{4,1,3,2,0:T(2,128)(2,1)S(1)} %slice.108, bf16[36,2,8,3,512]{4,1,3,2,0:T(2,128)(2,1)S(1)} %bitcast.58), kind=kLoop, calls=%fused_computation.3 | loop fusion | flops 8847360 | bytes 5750784 | tf_op jit(solution)/shard_map/conv_general_dilated | solution.py:59
  23.9 0.0 slice-done
  23.9 8.1 %fusion.8 = f32[34,16,3,512]{3,1,2,0:T(8,128)S(1)} fusion(bf16[3,3,512,512]{3,2,1,0:T(8,128)(2,1)S(1)} %bitcast.70, bf16[36,2,8,5,512]{4,1,3,2,0:T(2,128)(2,1)S(1)} %fusion, pred[16,3]{0,1:T(4,128)(4,1)S(1)} %copy-done.6), kind=kOutput, calls=%fused_computation.15 | convolution fusion | flops 7701577728 | bytes 11010096 | tf_op jit(solution)/shard_map/conv_general_dilated | solution.py:59
  32.0 2.0 %copy.16 = f32[34,16,3,512]{3,0,2,1:T(8,128)S(1)} copy(f32[34,16,3,512]{3,1,2,0:T(8,128)S(1)} %fusion.8) | data formatting | bytes 6684672 | tf_op jit(solution)/shard_map/conv_general_dilated | solution.py:59
  33.9 0.3 slice_bitcast_fusion
  34.2 1.4 %fusion.39 = (f32[1,34,18,512]{3,1,2,0:T(8,128)S(1)}, f32[1,34,18,512]{3,1,2,0:T(8,128)}) fusion(f32[2,34,18,512]{3,1,2,0:T(8,128)S(1)} %slice_bitcast_fusion), kind=kLoop, calls=%fused_computation.76 | loop fusion | bytes 5013504 | tf_op jit(solution)/shard_map/slice | solution.py:79
  35.6 1.9 %copy.17 = f32[1,34,18,512]{3,2,1,0:T(8,128)} copy(f32[1,34,18,512]{3,1,2,0:T(8,128)S(1)} %get-tuple-element.7) | data formatting | bytes 2506752 | tf_op jit(solution)/shard_map/slice | solution.py:79
  37.6 2.5 %squeeze.4 = f32[612,512]{1,0:T(8,128)} reshape(f32[1,34,18,512]{3,2,1,0:T(8,128)} %copy.17) | data formatting | bytes 2506752 | tf_op jit(solution)/shard_map/squeeze | solution.py:79
  40.1 3.3 %copy.18 = f32[1,34,18,512]{3,2,1,0:T(8,128)} copy(f32[1,34,18,512]{3,1,2,0:T(8,128)} %get-tuple-element.8) | data formatting | bytes 2506752 | tf_op jit(solution)/shard_map/slice | solution.py:82
  43.4 2.5 %squeeze.10 = f32[612,512]{1,0:T(8,128)} reshape(f32[1,34,18,512]{3,2,1,0:T(8,128)} %copy.18) | data formatting | bytes 2506752 | tf_op jit(solution)/shard_map/squeeze | solution.py:82
  46.0 2.0 %add_convert_fusion = bf16[612,512]{1,0:T(8,128)(2,1)S(1)} fusion(f32[612,512]{1,0:T(8,128)} %squeeze.10, f32[612,512]{1,0:T(8,128)} %squeeze.4, f32[512]{0:T(512)S(1)} %get-tuple-element.25), kind=kLoop, calls=%fused_computation.38 | loop fusion | flops 940032 | bytes 3135488 | tf_op jit(solution)/shard_map/convert_element_type | solution.py:85
  48.0 0.9 pad.4
  48.9 4.2 %all-to-all-start = ((bf16[4,160,512]{2,1,0:T(8,128)(2,1)}), bf16[4,160,512]{2,1,0:T(8,128)(2,1)}, u32[]{:S(2)}, u32[]{:S(2)}) async-start(bf16[4,160,512]{2,1,0:T(8,128)(2,1)} %bitcast.62), calls=%async_computation | async-start | bytes 1310720 | tf_op jit(solution)/shard_map/all_to_all | solution.py:89
  53.1 0.1 broadcast_and_fusion
  53.2 9.1 %all-to-all-done = bf16[4,160,512]{2,1,0:T(8,128)(2,1)} async-done(((bf16[4,160,512]{2,1,0:T(8,128)(2,1)}), bf16[4,160,512]{2,1,0:T(8,128)(2,1)}, u32[]{:S(2)}, u32[]{:S(2)}) %all-to-all-start) | async-done | bytes 655392 | tf_op jit(solution)/shard_map/all_to_all | solution.py:89
  62.3 1.2 %fusion.35 = (bf16[1,160,512]{2,1,0:T(8,128)(2,1)S(1)}, bf16[1,160,512]{2,1,0:T(8,128)(2,1)S(1)}, bf16[1,160,512]{2,1,0:T(8,128)(2,1)S(1)}) fusion(f32[512]{0:T(512)S(1)} %get-tuple-element.24, f32[512]{0:T(512)S(1)} %get-tuple-element.23, bf16[4,160,512]{2,1,0:T(8,128)(2,1)} %all-to-all-done), kind=kLoop, calls=%fused_computation.48 | loop fusion | flops 901120 | bytes 987136 | tf_op jit(solution)/shard_map/convert.7
  63.5 1.0 pad_maximum_fusion.1
  64.5 4.4 %all-to-all-start.1 = ((bf16[4,160,512]{2,1,0:T(8,128)(2,1)}), bf16[4,160,512]{2,1,0:T(8,128)(2,1)}, u32[]{:S(2)}, u32[]{:S(2)}) async-start(bf16[4,160,512]{2,1,0:T(8,128)(2,1)} %pad_maximum_fusion.1), calls=%async_computation.1 | async-start | bytes 1310720 | tf_op jit(solution)/shard_map/all_to_all | solution.py:96
  68.9 2.5 %fusion.32 = f32[1,34,16,512]{3,1,2,0:T(8,128)} fusion(f32[1,16,512]{2,0,1:T(1,128)S(1)} %reshape.254, f32[32,16,512]{2,0,1:T(8,128)} %copy-done, f32[1,16,512]{2,0,1:T(1,128)S(1)} %copy.12), kind=kLoop, calls=%fused_computation.40 | loop fusion | flops 557056 | bytes 2228224 | tf_op jit(solution)/shard_map/concatenate | solution.py:52
  71.4 6.0 %all-to-all-done.1 = bf16[4,160,512]{2,1,0:T(8,128)(2,1)} async-done(((bf16[4,160,512]{2,1,0:T(8,128)(2,1)}), bf16[4,160,512]{2,1,0:T(8,128)(2,1)}, u32[]{:S(2)}, u32[]{:S(2)}) %all-to-all-start.1) | async-done | bytes 655392 | tf_op jit(solution)/shard_map/all_to_all | solution.py:96
  77.5 2.3 %slice_convert_fusion = f32[612,512]{1,0:T(8,128)} fusion(bf16[640,512]{1,0:T(8,128)(2,1)} %bitcast.18), kind=kLoop, calls=%fused_computation.43 | loop fusion | flops 313344 | bytes 1880064 | tf_op jit(solution)/shard_map/convert_element_type | solution.py:97
  79.8 2.6 %reshape.257 = f32[1,34,18,512]{3,2,1,0:T(8,128)} reshape(f32[612,512]{1,0:T(8,128)} %slice_convert_fusion) | data formatting | bytes 2506752 | tf_op jit(solution)/shard_map/convert_element_type | solution.py:97
  82.3 3.8 %fusion.21 = (bf16[1,34,18,512]{3,1,2,0:T(8,128)(2,1)S(1)}, bf16[1,34,18,512]{3,1,2,0:T(8,128)(2,1)S(1)}) fusion(f32[512]{0:T(512)S(1)} %get-tuple-element.25, f32[512]{0:T(512)S(1)} %copy-done.4, pred[34,18]{0,1:T(8,128)(4,1)S(1)} %broadcast_and_fusion, f32[1,34,18,512]{3,2,1,0:T(8,128)} %reshape.257, f32[1,34,1,512]{3,1,2,0:T(8,128)S(1)} %fusion.36, ...), kind=kLoop, calls=%fused_computation.24 | loop fusion | flops 10027008 | bytes 6275684 | tf_op jit(solution)/shard_map/convert_element_type | solution.py:109
  86.1 0.0 slice-start.2
  86.1 0.1 maximum_bitcast_fusion.1
  86.3 1.3 %copy.25 = bf16[34,2,18,512]{3,1,2,0:T(2,128)(2,1)S(1)} copy(bf16[34,2,18,512]{3,0,2,1:T(8,128)(2,1)S(1)} %maximum_bitcast_fusion.1) | data formatting | bytes 2506752
  87.6 0.0 slice-start.3
  87.6 1.7 %pad.7.clone = bf16[34,2,24,512]{3,1,2,0:T(2,128)(2,1)S(1)} pad(bf16[34,2,18,512]{3,1,2,0:T(2,128)(2,1)S(1)} %copy.25, bf16[]{:T(256)} %constant.12.clone.1), padding=0_0x0_0x0_6x0_0 | pad | bytes 2924546 | tf_op jit(solution)/shard_map/stack | solution.py:110
  89.3 0.7 slice.116
  90.0 0.0 copy-start.5
  90.0 6.5 %fusion.4 = bf16[34,2,8,5,512]{4,1,3,2,0:T(2,128)(2,1)S(1)} fusion(bf16[34,2,7,2,512]{4,1,3,2,0:T(2,128)(2,1)S(1)} %slice.116, bf16[34,2,8,3,512]{4,1,3,2,0:T(2,128)(2,1)S(1)} %bitcast.60), kind=kLoop, calls=%fused_computation.8 | loop fusion | flops 8355840 | bytes 5431296 | tf_op jit(solution)/shard_map/conv_general_dilated | solution.py:59
  96.5 7.6 %select_convert_fusion = bf16[32,16,3,512]{3,1,2,0:T(8,128)(2,1)S(1)} fusion(pred[16,3]{0,1:T(4,128)(4,1)S(1)} %copy-done.5, bf16[3,3,512,512]{3,2,1,0:T(8,128)(2,1)S(1)} %bitcast.72, bf16[34,2,8,5,512]{4,1,3,2,0:T(2,128)(2,1)S(1)} %fusion.4), kind=kOutput, calls=%fused_computation.2 | convolution fusion | flops 7249330176 | bytes 9076784 | tf_op jit(solution)/shard_map/conv_general_dilated | solution.py:59
  104.1 0.9 copy.22
  105.0 0.1 slice_bitcast_fusion.1
  105.0 1.6 %copy.23 = bf16[2,32,16,512]{3,2,1,0:T(8,128)(2,1)} copy(bf16[2,32,16,512]{3,1,2,0:T(8,128)(2,1)S(1)} %slice_bitcast_fusion.1) | data formatting | bytes 2097152 | tf_op jit(solution)/shard_map/convert_element_type | solution.py:110
  (30 shorter events, 0.3 us)
Async XLA Ops:
  0.0 2.9 %copy-start.2 = (f32[32,16,512]{2,1,0:T(8,128)S(1)}, f32[32,16,512]{2,1,0:T(8,128)}, u32[]{:S(2)}) copy-start(f32[32,16,512]{2,1,0:T(8,128)} %param.11) | copy-start | bytes 3145732
  2.3 1.6 %copy-start.1 = (bf16[2,32,16,512]{3,2,1,0:T(8,128)(2,1)S(1)}, bf16[2,32,16,512]{3,2,1,0:T(8,128)(2,1)}, u32[]{:S(2)}) copy-start(bf16[2,32,16,512]{3,2,1,0:T(8,128)(2,1)} %param.6) | copy-start | bytes 3145732
  2.3 1.4 %collective-permute-start = (bf16[80,512]{1,0:T(8,128)(2,1)S(1)}, bf16[80,512]{1,0:T(8,128)(2,1)S(1)}, u32[]{:S(2)}, u32[]{:S(2)}) collective-permute-start(bf16[80,512]{1,0:T(8,128)(2,1)S(1)} %maximum_select_fusion), channel_id=1, source_target_pairs={{0,4},{4,0},{1,5},{5,1},{2,6},{6,2},{3,7},{7,3},{8,12},{12,8},{9,1... | collective-permute-start | bytes 245768 | tf_op jit(solution)/shard_map/ppermute | solution.py:15
  3.5 1.1 copy-start
  4.2 7.2 %copy-start.3 = (s32[512]{0:T(512)S(1)}, s32[512]{0:T(512)}, u32[]{:S(2)}) copy-start(s32[512]{0:T(512)} %param.9) | copy-start | bytes 6148
  4.6 9.9 %collective-permute-start.2 = (bf16[178,512]{1,0:T(8,128)(2,1)S(1)}, bf16[178,512]{1,0:T(8,128)(2,1)S(1)}, u32[]{:S(2)}, u32[]{:S(2)}) collective-permute-start(bf16[178,512]{1,0:T(8,128)(2,1)S(1)} %pad_maximum_fusion.3), channel_id=1, source_target_pairs={{1,0},{2,1},{3,2},{5,4},{6,5},{7,6},{9,8},{10,9},{11,10},{13,12},{... | collective-permute-start | bytes 546824 | tf_op jit(solution)/shard_map/ppermute | solution.py:20
  5.9 9.8 %collective-permute-start.1 = (bf16[178,512]{1,0:T(8,128)(2,1)S(1)}, bf16[178,512]{1,0:T(8,128)(2,1)S(1)}, u32[]{:S(2)}, u32[]{:S(2)}) collective-permute-start(bf16[178,512]{1,0:T(8,128)(2,1)S(1)} %pad_maximum_fusion.2), channel_id=1, source_target_pairs={{0,1},{1,2},{2,3},{4,5},{5,6},{6,7},{8,9},{9,10},{10,11},{12,13},{... | collective-permute-start | bytes 546824 | tf_op jit(solution)/shard_map/ppermute | solution.py:19
  16.9 6.9 %slice-start = ((s8[4718592]{0:T(1024)(128)(4,1)}), s8[524288]{0:T(1024)(128)(4,1)S(1)}, s32[]{:S(2)}) async-start(s8[4718592]{0:T(1024)(128)(4,1)} %bitcast.69), calls=%async_computation.2 | async-start | bytes 1048576
  20.3 3.6 %slice-start.1 = ((s8[4718592]{0:T(1024)(128)(4,1)}), s8[4194304]{0:T(1024)(128)(4,1)S(1)}, s32[]{:S(2)}) async-start(s8[4718592]{0:T(1024)(128)(4,1)} %bitcast.69), calls=%async_computation.3 | async-start | bytes 8388608
  21.1 2.8 %copy-start.6 = (pred[16,3]{0,1:T(4,128)(4,1)S(1)}, pred[16,3]{0,1:T(4,128)(4,1)}, u32[]{:S(2)}) copy-start(pred[16,3]{0,1:T(4,128)(4,1)} %constant.63) | copy-start | bytes 148
  48.9 13.4 %all-to-all-start = ((bf16[4,160,512]{2,1,0:T(8,128)(2,1)}), bf16[4,160,512]{2,1,0:T(8,128)(2,1)}, u32[]{:S(2)}, u32[]{:S(2)}) async-start(bf16[4,160,512]{2,1,0:T(8,128)(2,1)} %bitcast.62), calls=%async_computation | async-start | bytes 1310720 | tf_op jit(solution)/shard_map/all_to_all | solution.py:89
  64.5 12.9 %all-to-all-start.1 = ((bf16[4,160,512]{2,1,0:T(8,128)(2,1)}), bf16[4,160,512]{2,1,0:T(8,128)(2,1)}, u32[]{:S(2)}, u32[]{:S(2)}) async-start(bf16[4,160,512]{2,1,0:T(8,128)(2,1)} %pad_maximum_fusion.1), calls=%async_computation.1 | async-start | bytes 1310720 | tf_op jit(solution)/shard_map/all_to_all | solution.py:96
  79.8 2.6 %copy-start.4 = (f32[512]{0:T(512)S(1)}, f32[512]{0:T(512)}, u32[]{:S(2)}) copy-start(f32[512]{0:T(512)} %param.10) | copy-start | bytes 6148
  86.1 10.4 %slice-start.2 = ((s8[4718592]{0:T(1024)(128)(4,1)}), s8[4194304]{0:T(1024)(128)(4,1)S(1)}, s32[]{:S(2)}) async-start(s8[4718592]{0:T(1024)(128)(4,1)} %bitcast.71), calls=%async_computation.4 | async-start | bytes 8388608
  87.6 8.9 %slice-start.3 = ((s8[4718592]{0:T(1024)(128)(4,1)}), s8[524288]{0:T(1024)(128)(4,1)S(1)}, s32[]{:S(2)}) async-start(s8[4718592]{0:T(1024)(128)(4,1)} %bitcast.71), calls=%async_computation.5 | async-start | bytes 1048576
  90.0 6.5 %copy-start.5 = (pred[16,3]{0,1:T(4,128)(4,1)S(1)}, pred[16,3]{0,1:T(4,128)(4,1)}, u32[]{:S(2)}) copy-start(pred[16,3]{0,1:T(4,128)(4,1)} %constant.62) | copy-start | bytes 148

commit v2 on v1

v2 whole, which is shorter than its diff:
```python
import math

import jax
import jax.numpy as jnp
from jax import lax
from jax.experimental import pallas as pl
from jax.experimental.pallas import tpu as pltpu
from jax.sharding import PartitionSpec as P

NPOLES = 16
VMEM_LIMIT = 48 * 1024 * 1024
WHOLE = pl.BlockSpec(memory_space=pltpu.VMEM)


def from_neighbours(before, after, axis):
    count = lax.axis_size(axis)
    if count == 2:
        first = lax.axis_index(axis) == 0
        got = lax.ppermute(jnp.where(first, before, after), axis, [(0, 1), (1, 0)])
        zero = jnp.zeros_like(got)
        return jnp.where(first, zero, got), jnp.where(first, got, zero)
    return (
        lax.ppermute(before, axis, [(i, i + 1) for i in range(count - 1)]),
        lax.ppermute(after, axis, [(i + 1, i) for i in range(count - 1)]),
    )


def halos(cells):
    top, bottom = from_neighbours(cells[:, -1:], cells[:, :1], "sx")

    def column(at):
        return jnp.concatenate([top[:, :, at], cells[:, :, at], bottom[:, :, at]], axis=1)

    left, right = from_neighbours(column(-1), column(0), "sy")
    return top, bottom, left, right


def shifted(product, step):
    if step == 0:
        return product
    cols = product.shape[1]
    col = lax.broadcasted_iota(jnp.int32, product.shape, 1)
    if step == 1:
        return jnp.where(col == cols - 1, 0.0, pltpu.roll(product, cols - 1, 1))
    return jnp.where(col == 0, 0.0, pltpu.roll(product, 1, 1))


def tile_kernel(cells_ref, top_ref, bottom_ref, weight_ref, out_ref, held_ref):
    count, rows, cols, channels = cells_ref.shape
    step = pl.program_id(0)
    block = 16

    @pl.when(step == 0)
    def _():
        held_ref[:, :1] = top_ref[...]
        held_ref[:, 1 : rows + 1] = cells_ref[...]
        held_ref[:, rows + 1 :] = bottom_ref[...]

    for which in range(3):

        @pl.when(step == which)
        def _():
            for frame in range(count):
                for row in range(0, rows, block):
                    taps = [
                        held_ref[frame, row + tap : row + tap + block].reshape(-1, channels)
                        for tap in range(3)
                    ]
                    product = jnp.dot(
                        jnp.concatenate(taps, axis=1),
                        weight_ref[...].reshape(3 * channels, -1),
                        preferred_element_type=jnp.float32,
                    ).reshape(block, cols, -1)
                    product = shifted(product, which)
                    here = (frame, slice(row, row + block))
                    if which == 0:
                        out_ref[here] = product
                    else:
                        out_ref[here] += product


def conv_tile(cells, top, bottom, weight):
    count, rows, cols, channels = cells.shape
    outs = weight.shape[-1]
    return pl.pallas_call(
        tile_kernel,
        grid=(3,),
        in_specs=[
            WHOLE,
            WHOLE,
            WHOLE,
            pl.BlockSpec((3, 1, channels, outs), lambda step: (0, (step + 1) % 3, 0, 0)),
        ],
        out_specs=pl.BlockSpec((count, rows, cols, outs), lambda step: (0, 0, 0, 0)),
        out_shape=jax.ShapeDtypeStruct((count, rows, cols, outs), jnp.float32),
        scratch_shapes=[pltpu.VMEM((count, rows + 2, cols, channels), cells.dtype)],
        compiler_params=pltpu.CompilerParams(vmem_limit_bytes=VMEM_LIMIT),
        cost_estimate=pl.CostEstimate(
            flops=18 * count * rows * cols * channels * outs,
            bytes_accessed=2 * weight.size + 6 * cells.size,
            transcendentals=0,
        ),
    )(cells, top, bottom, weight)


def add_column(total_ref, side_ref, weight_ref, out_ref):
    count, rows, cols, _ = total_ref.shape
    part = jnp.dot(
        side_ref[0],
        weight_ref[...].reshape(side_ref.shape[2], -1),
        preferred_element_type=jnp.float32,
    )
    part = part.reshape(count, rows, 1, -1)

    @pl.when(pl.program_id(0) == 0)
    def _():
        out_ref[...] = total_ref[...]
        out_ref[:, :, :1] += part

    @pl.when(pl.program_id(0) == 1)
    def _():
        out_ref[:, :, cols - 1 :] += part


def drive_kernel(total_ref, side_ref, weight_ref, decay_ref, out_ref, end_ref):
    add_column(total_ref, side_ref, weight_ref, out_ref)

    @pl.when(pl.program_id(0) == 1)
    def _():
        state = out_ref[0]
        for frame in range(1, out_ref.shape[0]):
            state = decay_ref[...] * state + out_ref[frame]
        end_ref[...] = state.astype(end_ref.dtype)


def result_kernel(total_ref, side_ref, weight_ref, out_ref, sum_ref):
    add_column(total_ref, side_ref, weight_ref, sum_ref)

    @pl.when(pl.program_id(0) == 1)
    def _():
        out_ref[...] = sum_ref[...].astype(out_ref.dtype)


def taps_of(left, right, rows):
    sides = jnp.stack([left, right])
    taps = [sides[:, :, tap : tap + rows] for tap in range(3)]
    taps = jnp.concatenate(taps, axis=-1)
    return taps.reshape(2, -1, taps.shape[-1])


def side_specs(total, sides, weight):
    return [
        WHOLE,
        pl.BlockSpec((1, *sides.shape[1:]), lambda step: (step, 0, 0)),
        pl.BlockSpec((3, 1, *weight.shape[2:]), lambda step: (0, 2 * step, 0, 0)),
    ]


def params():
    return pltpu.CompilerParams(vmem_limit_bytes=VMEM_LIMIT)


def finish_drive(total, sides, weight, decay):
    return pl.pallas_call(
        drive_kernel,
        grid=(2,),
        in_specs=[*side_specs(total, sides, weight), WHOLE],
        out_specs=[
            pl.BlockSpec(total.shape, lambda step: (0, 0, 0, 0)),
            pl.BlockSpec(total.shape[1:], lambda step: (0, 0, 0)),
        ],
        out_shape=[
            jax.ShapeDtypeStruct(total.shape, jnp.float32),
            jax.ShapeDtypeStruct(total.shape[1:], jnp.bfloat16),
        ],
        compiler_params=params(),
    )(total, sides, weight, decay)


def finish_result(total, sides, weight):
    return pl.pallas_call(
        result_kernel,
        grid=(2,),
        in_specs=side_specs(total, sides, weight),
        out_specs=pl.BlockSpec(total.shape, lambda step: (0, 0, 0, 0)),
        out_shape=jax.ShapeDtypeStruct(total.shape, jnp.bfloat16),
        scratch_shapes=[pltpu.VMEM(total.shape, jnp.float32)],
        compiler_params=params(),
    )(total, sides, weight)


def entry_kernel(ends_ref, carried_ref, out_ref):
    entry = jnp.zeros(ends_ref.shape[1:], jnp.float32)
    out_ref[0] = entry.astype(out_ref.dtype)
    for index in range(ends_ref.shape[0] - 1):
        entry = carried_ref[...] * entry + ends_ref[index].astype(jnp.float32)
        out_ref[index + 1] = entry.astype(out_ref.dtype)


def mixed_kernel(drive_ref, entry_ref, start_ref, reach_ref, decay_ref, scale_ref, out_ref):
    state = reach_ref[...] * start_ref[...] + entry_ref[...].astype(jnp.float32)
    for frame in range(drive_ref.shape[0]):
        state = decay_ref[...] * state + drive_ref[frame]
        out_ref[frame] = jax.nn.gelu(scale_ref[...] * state).astype(out_ref.dtype)


def mix(drive, entry, start, reach, decay, scale):
    count, rows, cols, channels = drive.shape
    block = 8
    lane = pl.BlockSpec((1, channels), lambda step: (0, 0))
    tile = pl.BlockSpec((block, cols, channels), lambda step: (step, 0, 0))
    tiles = pl.BlockSpec((count, block, cols, channels), lambda step: (0, step, 0, 0))
    return pl.pallas_call(
        mixed_kernel,
        grid=(rows // block,),
        in_specs=[tiles, tile, tile, lane, lane, lane],
        out_specs=tiles,
        out_shape=jax.ShapeDtypeStruct(drive.shape, jnp.bfloat16),
        compiler_params=params(),
    )(drive, entry, start, reach, decay, scale)


def on_device(frames, input_weight, output_weight, pole_index, gelu_scale, start_state):
    count, rows, cols, channels = frames.shape
    groups = lax.axis_size("tm")
    position = lax.axis_index("tm")
    rate = -0.001 * jnp.exp(pole_index.astype(jnp.float32) * (math.log(300.0) / (NPOLES - 1)))
    rate = rate[None]
    decay = jnp.exp(rate)

    top, bottom, left, right = halos(frames)
    total = conv_tile(frames, top, bottom, input_weight)
    drive, end = finish_drive(total, taps_of(left, right, rows), input_weight, decay)

    ends = lax.all_to_all(end.reshape(groups, -1, channels), "tm", 0, 0)
    entries = pl.pallas_call(
        entry_kernel,
        in_specs=[WHOLE, WHOLE],
        out_specs=WHOLE,
        out_shape=jax.ShapeDtypeStruct(ends.shape, ends.dtype),
        compiler_params=params(),
    )(ends, jnp.exp(count * rate))
    entry = lax.all_to_all(entries, "tm", 0, 0).reshape(rows, cols, channels)

    reach = jnp.exp((count * position).astype(jnp.float32) * rate)
    mixed = mix(drive, entry, start_state, reach, decay, gelu_scale[None])

    top, bottom, left, right = halos(mixed)
    total = conv_tile(mixed, top, bottom, output_weight)
    return finish_result(total, taps_of(left, right, rows), output_weight)


def solution(mesh):
    return jax.shard_map(
        on_device,
        mesh=mesh,
        in_specs=(P("tm", "sx", "sy", None), P(), P(), P(), P(), P("sx", "sy", None)),
        out_specs=P("tm", "sx", "sy", None),
        check_vma=False,
    )
```

time: 107 us -> 63.2 us (0.59)
  local copies, waits for them, and re-layouts: 29.8 us -> 2.94 us
  other arithmetic: 25.3 us -> 1.85 us
  blocking collectives: 0 us -> 22.4 us
  Pallas kernels: 0 us -> 21.6 us
  waiting for transfers between devices: 19.6 us -> 0.95 us
  matrix products: 15.6 us -> 0 us
  starting transfers between devices: 15.8 us -> 12.8 us
    all_to_all x0 -> x2, blocking collectives: none -> 22.4 us  [the longest x1 12.7 us: on_device(): ends = lax.all_to_all(end.reshape(groups, -1, channels), 'tm', 0, 0)]
    pallas_call x0 -> x6, Pallas kernels: none -> 21.6 us  [the longest x2 13.9 us: conv_tile(): pl.pallas_call(tile_kernel, grid=(3,), in_specs=[WHOLE, WHOLE, WHOLE, pl....]
    conv_general_dilated x2 -> x0, matrix products: 15.6 us -> none  [convolve(): lax.conv_general_dilated(cells, weight, (1, 1), 'VALID', dimension_number...]
    all_to_all x2 -> x0, waiting for transfers between devices: 15.1 us -> none  [the longest x1 9.12 us: on_device(): ends = lax.all_to_all(flat.reshape(groups, block, channels), 'tm', 0, 0)]
    conv_general_dilated x2 -> x0, other arithmetic: 9.26 us -> none  [convolve(): lax.conv_general_dilated(cells, weight, (1, 1), 'VALID', dimension_number...]
    all_to_all x2 -> x0, starting transfers between devices: 8.57 us -> none  [the longest x1 4.39 us: on_device(): lax.all_to_all(jnp.stack(entries).astype(jnp.bfloat16), 'tm', 0, 0)]
    convert_element_type x5 -> x0, other arithmetic: 8.05 us -> none  [the longest x1 3.76 us: on_device(): activated.append(jnp.where(inside, mixed, 0.0).astype(jnp.bfloat16))]
    slice x8 -> x2, local copies, waits for them, and re-layouts: 7.66 us -> 1.61 us  [column(): cells[:, :, at]]
  transfers between devices with their start and end apart: 5 -> 6, of which waited for: 5 -> 1; matrix products, arithmetic and copies ran while one was open for 3% -> 4% of each run, Pallas kernels for 0% -> 22%
where the time goes in v2:
time: 63.2 us; the launch traced here: 62.8 us
  blocking collectives  22.4 us (35%)
  Pallas kernels  21.6 us (34%)
  starting transfers between devices  12.8 us (20%)
  local copies, waits for them, and re-layouts  2.94 us (5%)
  other arithmetic  1.85 us (3%)
  waiting for transfers between devices  0.95 us (2%)
    pallas_call x2, Pallas kernels, conv_tile(): pl.pallas_call(tile_kernel, grid=(3,), in_specs=[WHOLE, WHOLE, WHOLE, pl....  13.9 us
    all_to_all x1, blocking collectives, on_device(): ends = lax.all_to_all(end.reshape(groups, -1, channels), 'tm', 0, 0)  12.7 us
    all_to_all x1, blocking collectives, on_device(): entry = lax.all_to_all(entries, 'tm', 0, 0).reshape(rows, cols, channels)  9.67 us
    ppermute x2, starting transfers between devices, from_neighbours(): lax.ppermute(before, axis, [(i, i + 1) for i in range(count - 1)])  9.67 us
    pallas_call x1, Pallas kernels, finish_result(): pl.pallas_call(result_kernel, grid=(2,), in_specs=side_specs(total, sides...  3.58 us
    pallas_call x1, Pallas kernels, finish_drive(): pl.pallas_call(drive_kernel, grid=(2,), in_specs=[*side_specs(total, side...  2.75 us
    ppermute x2, starting transfers between devices, from_neighbours(): lax.ppermute(after, axis, [(i + 1, i) for i in range(count - 1)])  2.58 us
    slice x2, local copies, waits for them, and re-layouts, column(): cells[:, :, at]  1.61 us
  transfers between devices with their start and end apart: 6, of which 1 were waited for; matrix products, arithmetic and copies ran while one was open for 4% of the time, Pallas kernels for 22%

profile of v2, /device:TPU:0, one launch (start us, length us, event | category | flops | bytes accessed | tf_op | source)
XLA Modules:
  0.0 62.8 jit_solution(9740401480679647024)
XLA Ops:
  0.0 0.8 %slice_select_fusion.1 = bf16[2,1,16,512]{3,2,1,0:T(8,128)(2,1)S(1)} fusion(bf16[2,32,16,512]{3,2,1,0:T(8,128)(2,1)} %cells_ref.1, pred[]{:T(512)S(6)} %eq.4), kind=kLoop, calls=%fused_computation.25 | loop fusion | flops 16384 | bytes 98305 | tf_op jit(solution)/shard_map/jit(_where)/select_n | solution.py:19
  0.8 0.5 collective-permute-start
  1.2 1.4 %fusion.7 = (bf16[2,32,1,512]{3,2,1,0:T(2,128)(2,1)S(1)}, bf16[2,32,1,512]{3,2,1,0:T(2,128)(2,1)S(1)}) fusion(bf16[2,32,16,512]{3,2,1,0:T(8,128)(2,1)} %cells_ref.1), kind=kLoop, calls=%fused_computation.43 | loop fusion | bytes 262144 | tf_op jit(solution)/shard_map/slice | solution.py:32
  2.6 0.7 %multiply_exponential_fusion = (f32[512]{0:T(512)S(1)}, f32[512]{0:T(512)S(1)}, f32[512]{0:T(512)S(1)}) fusion(s32[512]{0:T(512)} %param.9, f32[]{:T(128)S(6)} %mul.34), kind=kLoop, calls=%fused_computation.38 | loop fusion | flops 2560 | bytes 8196 | tf_op jit(solution)/shard_map/exp | solution.py:245
  3.4 0.0 collective-permute-done
  3.5 1.3 %collective-permute-start.2 = (bf16[2,34,512]{2,1,0:T(8,128)(2,1)S(1)}, bf16[2,34,512]{2,1,0:T(8,128)(2,1)S(1)}, u32[]{:S(2)}, u32[]{:S(2)}) collective-permute-start(bf16[2,34,512]{2,1,0:T(8,128)(2,1)S(1)} %pad_maximum_fusion.3), channel_id=1, source_target_pairs={{1,0},{2,1},{3,2},{5,4},{6,5},{7,6},{9,8},{10,9},{11,10},{13,12},{... | collective-permute-start | bytes 208904 | tf_op jit(solution)/shard_map/ppermute | solution.py:24
  4.8 5.1 %collective-permute-start.1 = (bf16[2,34,512]{2,1,0:T(8,128)(2,1)S(1)}, bf16[2,34,512]{2,1,0:T(8,128)(2,1)S(1)}, u32[]{:S(2)}, u32[]{:S(2)}) collective-permute-start(bf16[2,34,512]{2,1,0:T(8,128)(2,1)S(1)} %pad_maximum_fusion.2), channel_id=1, source_target_pairs={{0,1},{1,2},{2,3},{4,5},{5,6},{6,7},{8,9},{9,10},{10,11},{12,13},{... | collective-permute-start | bytes 208904 | tf_op jit(solution)/shard_map/ppermute | solution.py:23
  9.9 0.0 copy-start.1
  10.0 1.2 %copy-done.1 = bf16[2,32,16,512]{3,2,1,0:T(8,128)(2,1)S(1)} copy-done((bf16[2,32,16,512]{3,2,1,0:T(8,128)(2,1)S(1)}, bf16[2,32,16,512]{3,2,1,0:T(8,128)(2,1)}, u32[]{:S(2)}) %copy-start.1) | copy-done | bytes 1048600
  11.2 7.0 %shard_map.64.total_ref = f32[2,32,16,512]{3,2,1,0:T(8,128)S(1)} custom-call(bf16[2,32,16,512]{3,2,1,0:T(8,128)(2,1)S(1)} %copy-done.1, bf16[2,1,16,512]{3,2,1,0:T(8,128)(2,1)S(1)} %get-tuple-element.28.top_ref, bf16[2,1,16,512]{3,2,1,0:T(8,128)(2,1)S(1)} %get-tuple-element.27.bottom_ref, bf16[3,3,512,512]{3,2,1,0:T(8,128)(2,1)} %weight_ref.5), custom_call_target="tpu_custom_call" | custom-call | flops 4831838208 | bytes 7864320 | tf_op jit(solution)/shard_map/pallas_call | solution.py:85
  18.2 0.0 collective-permute-done.2
  18.2 0.0 collective-permute-done.1
  18.2 0.1 fusion.5
  18.3 0.1 fusion.1
  18.3 2.8 %shard_map.65 = (f32[2,32,16,512]{3,2,1,0:T(8,128)S(1)}, bf16[32,16,512]{2,1,0:T(8,128)(2,1)S(1)}) custom-call(f32[2,32,16,512]{3,2,1,0:T(8,128)S(1)} %shard_map.64.total_ref, bf16[2,64,1536]{2,1,0:T(8,128)(2,1)S(1)} %bitcast.42, bf16[3,3,512,512]{3,2,1,0:T(8,128)(2,1)} %weight_ref.5, f32[1,512]{1,0:T(1,128)S(1)} %bitcast.44), custom_call_target="tpu_custom_call" | custom-call | tf_op jit(solution)/shard_map/pallas_call | solution.py:164
  21.1 0.0 copy-start
  21.1 0.0 copy-start.2
  21.1 12.7 %all_to_all.10.ends_ref = bf16[4,128,512]{2,1,0:T(8,128)(2,1)S(1)} all-to-all(bf16[4,128,512]{2,1,0:T(8,128)(2,1)S(1)} %bitcast.43), channel_id=1, replica_groups=mesh['tm'=4,'sx'=2,'sy'=4] {'tm'}, dimensions={0} | all-to-all | bytes 1048576 | tf_op jit(solution)/shard_map/all_to_all | solution.py:235
  33.8 0.1 shard_map.66
  33.9 9.7 %all_to_all.11 = bf16[4,128,512]{2,1,0:T(8,128)(2,1)S(1)} all-to-all(bf16[4,128,512]{2,1,0:T(8,128)(2,1)S(1)} %shard_map.66), channel_id=1, replica_groups=mesh['tm'=4,'sx'=2,'sy'=4] {'tm'}, dimensions={0} | all-to-all | bytes 1048576 | tf_op jit(solution)/shard_map/all_to_all | solution.py:243
  43.6 0.0 copy-done
  43.6 0.0 copy-done.2
  43.6 1.2 %shard_map.67.cells_ref = bf16[2,32,16,512]{3,2,1,0:T(8,128)(2,1)S(1)} custom-call(f32[2,32,16,512]{3,2,1,0:T(8,128)S(1)} %get-tuple-element.7.drive_ref, bf16[32,16,512]{2,1,0:T(8,128)(2,1)S(1)} %bitcast.40, f32[32,16,512]{2,1,0:T(8,128)S(1)} %copy-done, f32[1,512]{1,0:T(1,128)S(1)} %bitcast.46, f32[1,512]{1,0:T(1,128)S(1)} %bitcast.45, f32[1,512]{1,0:T(1,128)S(1)} %bitcast.48), custom_call_target="tpu_custom_call" | custom-call | tf_op jit(solution)/shard_map/pallas_call | solution.py:213
  44.9 0.1 collective-permute-start.3
  44.9 0.2 fusion.6
  45.2 0.9 %collective-permute-done.3 = bf16[2,1,16,512]{3,2,1,0:T(8,128)(2,1)S(1)} collective-permute-done((bf16[2,1,16,512]{3,2,1,0:T(8,128)(2,1)S(1)}, bf16[2,1,16,512]{3,2,1,0:T(8,128)(2,1)S(1)}, u32[]{:S(2)}, u32[]{:S(2)}) %collective-permute-start.3) | collective-permute-done | bytes 32800 | tf_op jit(solution)/shard_map/ppermute | solution.py:19
  46.2 1.3 %collective-permute-start.5 = (bf16[2,34,512]{2,1,0:T(8,128)(2,1)S(1)}, bf16[2,34,512]{2,1,0:T(8,128)(2,1)S(1)}, u32[]{:S(2)}, u32[]{:S(2)}) collective-permute-start(bf16[2,34,512]{2,1,0:T(8,128)(2,1)S(1)} %pad_maximum_fusion.5), channel_id=1, source_target_pairs={{1,0},{2,1},{3,2},{5,4},{6,5},{7,6},{9,8},{10,9},{11,10},{13,12},{... | collective-permute-start | bytes 208904 | tf_op jit(solution)/shard_map/ppermute | solution.py:24
  47.6 4.6 %collective-permute-start.4 = (bf16[2,34,512]{2,1,0:T(8,128)(2,1)S(1)}, bf16[2,34,512]{2,1,0:T(8,128)(2,1)S(1)}, u32[]{:S(2)}, u32[]{:S(2)}) collective-permute-start(bf16[2,34,512]{2,1,0:T(8,128)(2,1)S(1)} %pad_maximum_fusion.4), channel_id=1, source_target_pairs={{0,1},{1,2},{2,3},{4,5},{5,6},{6,7},{8,9},{9,10},{10,11},{12,13},{... | collective-permute-start | bytes 208904 | tf_op jit(solution)/shard_map/ppermute | solution.py:23
  52.1 6.9 %shard_map.68.total_ref = f32[2,32,16,512]{3,2,1,0:T(8,128)S(1)} custom-call(bf16[2,32,16,512]{3,2,1,0:T(8,128)(2,1)S(1)} %shard_map.67.cells_ref, bf16[2,1,16,512]{3,2,1,0:T(8,128)(2,1)S(1)} %get-tuple-element.22.top_ref, bf16[2,1,16,512]{3,2,1,0:T(8,128)(2,1)S(1)} %get-tuple-element.21.bottom_ref, bf16[3,3,512,512]{3,2,1,0:T(8,128)(2,1)} %weight_ref.7), custom_call_target="tpu_custom_call" | custom-call | flops 4831838208 | bytes 7864320 | tf_op jit(solution)/shard_map/pallas_call | solution.py:85
  59.0 0.0 collective-permute-done.5
  59.0 0.0 collective-permute-done.4
  59.1 0.1 fusion.3
  59.1 0.1 fusion
  59.2 3.6 %shard_map.69 = bf16[2,32,16,512]{3,2,1,0:T(8,128)(2,1)} custom-call(f32[2,32,16,512]{3,2,1,0:T(8,128)S(1)} %shard_map.68.total_ref, bf16[2,64,1536]{2,1,0:T(8,128)(2,1)S(1)} %bitcast.41, bf16[3,3,512,512]{3,2,1,0:T(8,128)(2,1)} %weight_ref.7), custom_call_target="tpu_custom_call" | custom-call | tf_op jit(solution)/shard_map/pallas_call | solution.py:181
  (14 shorter events, 0.3 us)
Async XLA Ops:
  0.8 2.6 %collective-permute-start = (bf16[2,1,16,512]{3,2,1,0:T(8,128)(2,1)S(1)}, bf16[2,1,16,512]{3,2,1,0:T(8,128)(2,1)S(1)}, u32[]{:S(2)}, u32[]{:S(2)}) collective-permute-start(bf16[2,1,16,512]{3,2,1,0:T(8,128)(2,1)S(1)} %slice_select_fusion.1), channel_id=1, source_target_pairs={{0,4},{4,0},{1,5},{5,1},{2,6},{6,2},{3,7},{7,3},{8,12},{12,8},{9,1... | collective-permute-start | bytes 98312 | tf_op jit(solution)/shard_map/ppermute | solution.py:19
  3.5 14.7 %collective-permute-start.2 = (bf16[2,34,512]{2,1,0:T(8,128)(2,1)S(1)}, bf16[2,34,512]{2,1,0:T(8,128)(2,1)S(1)}, u32[]{:S(2)}, u32[]{:S(2)}) collective-permute-start(bf16[2,34,512]{2,1,0:T(8,128)(2,1)S(1)} %pad_maximum_fusion.3), channel_id=1, source_target_pairs={{1,0},{2,1},{3,2},{5,4},{6,5},{7,6},{9,8},{10,9},{11,10},{13,12},{... | collective-permute-start | bytes 208904 | tf_op jit(solution)/shard_map/ppermute | solution.py:24
  4.8 13.4 %collective-permute-start.1 = (bf16[2,34,512]{2,1,0:T(8,128)(2,1)S(1)}, bf16[2,34,512]{2,1,0:T(8,128)(2,1)S(1)}, u32[]{:S(2)}, u32[]{:S(2)}) collective-permute-start(bf16[2,34,512]{2,1,0:T(8,128)(2,1)S(1)} %pad_maximum_fusion.2), channel_id=1, source_target_pairs={{0,1},{1,2},{2,3},{4,5},{5,6},{6,7},{8,9},{9,10},{10,11},{12,13},{... | collective-permute-start | bytes 208904 | tf_op jit(solution)/shard_map/ppermute | solution.py:23
  9.9 1.2 %copy-start.1 = (bf16[2,32,16,512]{3,2,1,0:T(8,128)(2,1)S(1)}, bf16[2,32,16,512]{3,2,1,0:T(8,128)(2,1)}, u32[]{:S(2)}) copy-start(bf16[2,32,16,512]{3,2,1,0:T(8,128)(2,1)} %cells_ref.1) | copy-start | bytes 3145732
  21.1 22.5 %copy-start = (f32[32,16,512]{2,1,0:T(8,128)S(1)}, f32[32,16,512]{2,1,0:T(8,128)}, u32[]{:S(2)}) copy-start(f32[32,16,512]{2,1,0:T(8,128)} %start_ref.1) | copy-start | bytes 3145732
  21.1 22.5 %copy-start.2 = (f32[512]{0:T(512)S(1)}, f32[512]{0:T(512)}, u32[]{:S(2)}) copy-start(f32[512]{0:T(512)} %param.10) | copy-start | bytes 6148
  44.9 1.3 %collective-permute-start.3 = (bf16[2,1,16,512]{3,2,1,0:T(8,128)(2,1)S(1)}, bf16[2,1,16,512]{3,2,1,0:T(8,128)(2,1)S(1)}, u32[]{:S(2)}, u32[]{:S(2)}) collective-permute-start(bf16[2,1,16,512]{3,2,1,0:T(8,128)(2,1)S(1)} %slice_select_fusion), channel_id=1, source_target_pairs={{0,4},{4,0},{1,5},{5,1},{2,6},{6,2},{3,7},{7,3},{8,12},{12,8},{9,1... | collective-permute-start | bytes 98312 | tf_op jit(solution)/shard_map/ppermute | solution.py:19
  46.2 12.8 %collective-permute-start.5 = (bf16[2,34,512]{2,1,0:T(8,128)(2,1)S(1)}, bf16[2,34,512]{2,1,0:T(8,128)(2,1)S(1)}, u32[]{:S(2)}, u32[]{:S(2)}) collective-permute-start(bf16[2,34,512]{2,1,0:T(8,128)(2,1)S(1)} %pad_maximum_fusion.5), channel_id=1, source_target_pairs={{1,0},{2,1},{3,2},{5,4},{6,5},{7,6},{9,8},{10,9},{11,10},{13,12},{... | collective-permute-start | bytes 208904 | tf_op jit(solution)/shard_map/ppermute | solution.py:24
  47.6 11.5 %collective-permute-start.4 = (bf16[2,34,512]{2,1,0:T(8,128)(2,1)S(1)}, bf16[2,34,512]{2,1,0:T(8,128)(2,1)S(1)}, u32[]{:S(2)}, u32[]{:S(2)}) collective-permute-start(bf16[2,34,512]{2,1,0:T(8,128)(2,1)S(1)} %pad_maximum_fusion.4), channel_id=1, source_target_pairs={{0,1},{1,2},{2,3},{4,5},{5,6},{6,7},{8,9},{9,10},{10,11},{12,13},{... | collective-permute-start | bytes 208904 | tf_op jit(solution)/shard_map/ppermute | solution.py:23

commit v3 on v0

v3 whole, which is shorter than its diff:
```python
import math

import jax
import jax.numpy as jnp
from jax import lax
from jax.experimental import pallas as pl
from jax.experimental.pallas import tpu as pltpu
from jax.sharding import PartitionSpec as P

NPOLES = 16
VMEM_LIMIT = 24 * 1024 * 1024
WHOLE = pl.BlockSpec(memory_space=pltpu.VMEM)
LANES = 256


def call(kernel, out_shape, *args, scratch=(), flops=0):
    outs = jax.tree.leaves(out_shape)
    moved = sum(leaf.size * leaf.dtype.itemsize for leaf in (*args, *outs))
    return pl.pallas_call(
        kernel,
        in_specs=[WHOLE] * len(args),
        out_specs=jax.tree.map(lambda _: WHOLE, out_shape),
        out_shape=out_shape,
        scratch_shapes=scratch,
        compiler_params=pltpu.CompilerParams(vmem_limit_bytes=VMEM_LIMIT),
        cost_estimate=pl.CostEstimate(flops=flops, bytes_accessed=moved, transcendentals=0),
    )(*args)


def is_core(which):
    return (lax.axis_index("sx") == which).astype(jnp.float32)


def rate_of(pole_ref):
    pole = pole_ref[...].astype(jnp.float32)
    return -0.001 * jnp.exp(pole * (math.log(300.0) / (NPOLES - 1)))


def put_edges(frame, tile, give_ref, keep_ref):
    rows, cols, _ = tile.shape
    zero, one = is_core(0), is_core(1)
    left, right = tile[:, 0, :], tile[:, cols - 1, :]
    give_ref[frame, :cols] = (zero * tile[rows - 1] + one * tile[0]).astype(give_ref.dtype)
    give_ref[frame, cols:] = (zero * right + one * left).astype(give_ref.dtype)
    keep_ref[frame] = (zero * left + one * right).astype(keep_ref.dtype)


def edges_kernel(cells_ref, give_ref, keep_ref):
    for frame in range(cells_ref.shape[0]):
        put_edges(frame, cells_ref[frame].astype(jnp.float32), give_ref, keep_ref)


def edge_shapes(cells):
    count, rows, cols, channels = cells.shape
    return (
        jax.ShapeDtypeStruct((count, cols + rows, channels), jnp.bfloat16),
        jax.ShapeDtypeStruct((count, rows, channels), jnp.bfloat16),
    )


def swap_cores(array):
    return lax.ppermute(array, "sx", [(0, 1), (1, 0)])


def trade_columns(give, keep, cols):
    chips = lax.axis_size("sy")
    got = swap_cores(give)
    pairs = [(chip, chips + chip - 1) for chip in range(1, chips)]
    pairs += [(after, before) for before, after in pairs]
    column = jnp.concatenate([keep, got[:, cols:]], axis=1)
    return got, lax.ppermute(column, ("sx", "sy"), pairs)


def fill(lhs_ref, frame, at, cells_ref, got_ref):
    _, rows, cols, channels = cells_ref.shape
    size = rows * cols
    row = got_ref[frame, :cols].astype(jnp.float32)
    above = (is_core(1) * row).astype(lhs_ref.dtype)
    below = (is_core(0) * row).astype(lhs_ref.dtype)
    cells = cells_ref[frame].reshape(size, channels)
    mid, low = slice(channels, 2 * channels), slice(2 * channels, 3 * channels)
    lhs_ref[frame, at : at + cols, :channels] = above
    lhs_ref[frame, at + cols : at + size, :channels] = cells[: size - cols]
    lhs_ref[frame, at : at + size, mid] = cells
    lhs_ref[frame, at : at + size - cols, low] = cells[cols:]
    lhs_ref[frame, at + size - cols : at + size, low] = below


def centre_kernel(cells_ref, got_ref, weight_ref, total_ref, lhs_ref):
    count, rows, cols, channels = cells_ref.shape
    for frame in range(count):
        fill(lhs_ref, frame, 0, cells_ref, got_ref)
    for lane in range(0, weight_ref.shape[-1], LANES):
        lanes = slice(lane, lane + LANES)
        weight = weight_ref[:, 1, :, lanes].reshape(3 * channels, LANES)
        for frame in range(count):
            total = jnp.dot(lhs_ref[frame], weight, preferred_element_type=jnp.float32)
            total_ref[frame, :, :, lanes] = total.reshape(rows, cols, LANES)


def centre(cells, got, weight):
    count, rows, cols, channels = cells.shape
    outs = weight.shape[-1]
    return call(
        centre_kernel,
        jax.ShapeDtypeStruct((count, rows, cols, outs), jnp.float32),
        cells,
        got,
        weight,
        scratch=[pltpu.VMEM((count, rows * cols, 3 * channels), cells.dtype)],
        flops=6 * count * rows * cols * channels * outs,
    )


def row_taps(mid, above, below):
    rows = mid.shape[0]
    row = lax.broadcasted_iota(jnp.int32, mid.shape, 0)
    up = jnp.where(row == 0, above, pltpu.roll(mid, 1, 0))
    down = jnp.where(row == rows - 1, below, pltpu.roll(mid, rows - 1, 0))
    return jnp.concatenate([up, mid, down], axis=1)


def fill_sides(lhs_ref, frame, rows, mine_ref, theirs_ref):
    zero, one = is_core(0), is_core(1)
    mine = mine_ref[frame].astype(jnp.float32)
    theirs = theirs_ref[frame].astype(jnp.float32)
    mine = row_taps(mine[rows:], one * mine[rows - 1 : rows], zero * mine[:1])
    theirs = row_taps(
        theirs[:rows], one * theirs[2 * rows - 1 :], zero * theirs[rows : rows + 1]
    )
    lhs_ref[frame, :rows] = (zero * mine + one * theirs).astype(lhs_ref.dtype)
    lhs_ref[frame, lhs_ref.shape[1] - rows :] = (zero * theirs + one * mine).astype(lhs_ref.dtype)


def outer_taps(cells_ref, got_ref, mine_ref, theirs_ref, weight_ref, total_ref, lhs_ref, finish):
    count, rows, cols, channels = cells_ref.shape
    size = rows * cols
    for frame in range(count):
        fill(lhs_ref, frame, rows, cells_ref, got_ref)
        fill_sides(lhs_ref, frame, rows, mine_ref, theirs_ref)
    col = lax.broadcasted_iota(jnp.int32, (rows, cols, LANES), 1)
    for lane in range(0, weight_ref.shape[-1], LANES):
        lanes = slice(lane, lane + LANES)
        first = weight_ref[:, 0, :, lanes].reshape(3 * channels, LANES)
        last = weight_ref[:, 2, :, lanes].reshape(3 * channels, LANES)
        totals = []
        for frame in range(count):
            before = jnp.dot(
                lhs_ref[frame, : rows + size], first, preferred_element_type=jnp.float32
            )
            after = jnp.dot(lhs_ref[frame, rows:], last, preferred_element_type=jnp.float32)
            side, before = before[:rows], before[rows:].reshape(rows, cols, LANES)
            total = total_ref[frame, :, :, lanes]
            total += jnp.where(col == 0, side.reshape(rows, 1, LANES), pltpu.roll(before, 1, 1))
            side, after = after[size:], after[:size].reshape(rows, cols, LANES)
            total += jnp.where(
                col == cols - 1, side.reshape(rows, 1, LANES), pltpu.roll(after, cols - 1, 1)
            )
            totals.append(total)
        finish(lanes, totals)


def drive_kernel(
    cells_ref, got_ref, mine_ref, theirs_ref, weight_ref, total_ref, pole_ref, out_ref, end_ref, lhs_ref
):
    decay = jnp.exp(rate_of(pole_ref))

    def finish(lanes, totals):
        state = None
        for frame, total in enumerate(totals):
            out_ref[frame, :, :, lanes] = total
            state = total if state is None else decay[:, lanes] * state + total
        end_ref[:, :, lanes] = state.astype(end_ref.dtype)

    outer_taps(cells_ref, got_ref, mine_ref, theirs_ref, weight_ref, total_ref, lhs_ref, finish)


def result_kernel(
    cells_ref, got_ref, mine_ref, theirs_ref, weight_ref, total_ref, out_ref, lhs_ref
):
    def finish(lanes, totals):
        for frame, total in enumerate(totals):
            out_ref[frame, :, :, lanes] = total.astype(out_ref.dtype)

    outer_taps(cells_ref, got_ref, mine_ref, theirs_ref, weight_ref, total_ref, lhs_ref, finish)


def convolve(cells, give, keep, weight, kernel, out_shape, *more):
    count, rows, cols, channels = cells.shape
    got, mine = trade_columns(give, keep, cols)
    mine, total = lax.optimization_barrier((mine, centre(cells, got, weight)))
    return call(
        kernel,
        out_shape,
        cells,
        got,
        mine,
        swap_cores(mine),
        weight,
        total,
        *more,
        scratch=[pltpu.VMEM((count, rows * (cols + 2), 3 * channels), cells.dtype)],
        flops=12 * cells.size * weight.shape[-1],
    )


def entry_kernel(frames, ends_ref, pole_ref, out_ref):
    carried = jnp.exp(frames * rate_of(pole_ref))
    entry = jnp.zeros(ends_ref.shape[1:], jnp.float32)
    out_ref[0] = entry.astype(out_ref.dtype)
    for index in range(ends_ref.shape[0] - 1):
        entry = carried * entry + ends_ref[index].astype(jnp.float32)
        out_ref[index + 1] = entry.astype(out_ref.dtype)


def mixed_kernel(
    drive_ref, entry_ref, start_ref, pole_ref, scale_ref, out_ref, give_ref, keep_ref
):
    rate = rate_of(pole_ref)
    decay = jnp.exp(rate)
    count = drive_ref.shape[0]
    reach = jnp.exp((count * lax.axis_index("tm")).astype(jnp.float32) * rate)
    state = reach * start_ref[...] + entry_ref[...].astype(jnp.float32)
    for frame in range(count):
        state = decay * state + drive_ref[frame]
        mixed = jax.nn.gelu(scale_ref[...] * state)
        out_ref[frame] = mixed.astype(out_ref.dtype)
        put_edges(frame, mixed, give_ref, keep_ref)


def on_device(frames, input_weight, output_weight, pole_index, gelu_scale, start_state):
    count, rows, cols, channels = frames.shape
    groups = lax.axis_size("tm")
    assert lax.axis_size("sx") == 2
    pole = pole_index[None]

    give, keep = call(edges_kernel, edge_shapes(frames), frames)
    drive, end = convolve(
        frames,
        give,
        keep,
        input_weight,
        drive_kernel,
        (
            jax.ShapeDtypeStruct((count, rows, cols, channels), jnp.float32),
            jax.ShapeDtypeStruct((rows, cols, channels), jnp.bfloat16),
        ),
        pole,
    )

    ends = lax.all_to_all(end.reshape(groups, -1, channels), "tm", 0, 0)
    entries = call(
        lambda *refs: entry_kernel(count, *refs),
        jax.ShapeDtypeStruct(ends.shape, ends.dtype),
        ends,
        pole,
    )
    entry = lax.all_to_all(entries, "tm", 0, 0).reshape(rows, cols, channels)

    mixed, give, keep = call(
        mixed_kernel,
        (jax.ShapeDtypeStruct(frames.shape, jnp.bfloat16), *edge_shapes(frames)),
        drive,
        entry,
        start_state,
        pole,
        gelu_scale[None],
    )
    return convolve(
        mixed,
        give,
        keep,
        output_weight,
        result_kernel,
        jax.ShapeDtypeStruct(frames.shape, jnp.bfloat16),
    )


def solution(mesh):
    return jax.shard_map(
        on_device,
        mesh=mesh,
        in_specs=(P("tm", "sx", "sy", None), P(), P(), P(), P(), P("sx", "sy", None)),
        out_specs=P("tm", "sx", "sy", None),
        check_vma=False,
    )
```

time: 128 us -> 55.8 us (0.44)
  waiting for transfers between devices: 53.5 us -> 4.21 us
  matrix products: 17 us -> 0 us
  blocking collectives: 8.07 us -> 22.9 us
  Pallas kernels: 0 us -> 14.4 us
  other arithmetic: 14.1 us -> 0.02 us
  between operations: 13.8 us -> 0.13 us
  starting transfers between devices: 17.7 us -> 10.2 us
    all_gather x1 -> x0, waiting for transfers between devices: 45 us -> none  [on_device(): lax.all_gather(state[None], 'tm', axis=0, tiled=True)]
    all_to_all x0 -> x2, blocking collectives: none -> 22.9 us  [the longest x1 12.7 us: on_device(): ends = lax.all_to_all(end.reshape(groups, -1, channels), 'tm', 0, 0)]
    dot_general x18 -> x0, matrix products: 17 us -> none  [convolve_tile(): jnp.dot(window, weight[row_shift, col_shift], preferred_element_type=jnp....]
    pallas_call x0 -> x7, Pallas kernels: none -> 14.4 us  [call(): pl.pallas_call(kernel, in_specs=[WHOLE] * len(args), out_specs=jax.tree.m...]
    all_gather x1 -> x0, blocking collectives: 8.07 us -> none  [on_device(): lax.all_gather(carried[None], 'tm', axis=0, tiled=True)]
    ppermute x8 -> x6, starting transfers between devices: 17.7 us -> 10.2 us  [the longest x4 8.86 us: swap_cores(): return lax.ppermute(array, 'sx', [(0, 1), (1, 0)])]
    select_n x4 -> x0, other arithmetic: 6.81 us -> none  [fold_step(): return jnp.where(index < position, updated, current)]
    concatenate x5 -> x2, other arithmetic: 5.07 us -> 0.02 us  [trade_columns(): column = jnp.concatenate([keep, got[:, cols:]], axis=1)]
  transfers between devices with their start and end apart: 9 -> 6, of which waited for: 4 -> 4; matrix products, arithmetic and copies ran while one was open for 5% -> 0% of each run, Pallas kernels for 0% -> 6%
where the time goes in v3:
time: 55.8 us; the launch traced here: 55.5 us
  blocking collectives  22.9 us (41%)
  Pallas kernels  14.4 us (26%)
  starting transfers between devices  10.2 us (18%)
  waiting for transfers between devices  4.21 us (8%)
  local copies, waits for them, and re-layouts  3.59 us (6%)
    pallas_call x7, Pallas kernels, call(): pl.pallas_call(kernel, in_specs=[WHOLE] * len(args), out_specs=jax.tree.m...  14.4 us
    all_to_all x1, blocking collectives, on_device(): ends = lax.all_to_all(end.reshape(groups, -1, channels), 'tm', 0, 0)  12.7 us
    all_to_all x1, blocking collectives, on_device(): entry = lax.all_to_all(entries, 'tm', 0, 0).reshape(rows, cols, channels)  10.2 us
    ppermute x4, starting transfers between devices, swap_cores(): return lax.ppermute(array, 'sx', [(0, 1), (1, 0)])  8.86 us
    ppermute x4, waiting for transfers between devices, swap_cores(): return lax.ppermute(array, 'sx', [(0, 1), (1, 0)])  4.2 us
    unnamed x14, local copies, waits for them, and re-layouts  3.58 us
    ppermute x2, starting transfers between devices, trade_columns(): return (got, lax.ppermute(column, ('sx', 'sy'), pairs))  1.34 us
  transfers between devices with their start and end apart: 6, of which 4 were waited for; matrix products, arithmetic and copies ran while one was open for 0% of the time, Pallas kernels for 6%

profile of v3, /device:TPU:0, one launch (start us, length us, event | category | flops | bytes accessed | tf_op | source)
XLA Modules:
  0.0 55.5 jit_solution(10945902049113115149)
XLA Ops:
  0.0 0.0 copy-start.1
  0.0 1.2 %copy-done.1 = bf16[2,32,16,512]{3,2,1,0:T(8,128)(2,1)S(1)} copy-done((bf16[2,32,16,512]{3,2,1,0:T(8,128)(2,1)S(1)}, bf16[2,32,16,512]{3,2,1,0:T(8,128)(2,1)}, u32[]{:S(2)}) %copy-start.1) | copy-done | bytes 1048600
  1.2 0.7 %shard_map.64 = (bf16[2,48,512]{2,1,0:T(8,128)(2,1)S(1)}, bf16[2,32,512]{2,1,0:T(8,128)(2,1)S(1)}) custom-call(bf16[2,32,16,512]{3,2,1,0:T(8,128)(2,1)S(1)} %copy-done.1), custom_call_target="tpu_custom_call" | custom-call | bytes 1212416 | tf_op jit(solution)/shard_map/pallas_call | solution.py:19
  1.9 0.5 collective-permute-start
  2.4 0.9 %collective-permute-done.got_ref = bf16[2,48,512]{2,1,0:T(8,128)(2,1)S(1)} collective-permute-done((bf16[2,48,512]{2,1,0:T(8,128)(2,1)S(1)}, bf16[2,48,512]{2,1,0:T(8,128)(2,1)S(1)}, u32[]{:S(2)}, u32[]{:S(2)}) %collective-permute-start) | collective-permute-done | bytes 98336 | tf_op jit(solution)/shard_map/ppermute | solution.py:62
  3.4 0.7 %collective-permute-start.1 = (bf16[2,64,512]{2,1,0:T(8,128)(2,1)S(1)}, bf16[2,64,512]{2,1,0:T(8,128)(2,1)S(1)}, u32[]{:S(2)}, u32[]{:S(2)}) collective-permute-start(bf16[2,64,512]{2,1,0:T(8,128)(2,1)S(1)} %pad_maximum_fusion), channel_id=1, source_target_pairs={{1,4},{2,5},{3,6},{4,1},{5,2},{6,3},{9,12},{10,13},{11,14},{12,9},... | collective-permute-start | bytes 393224 | tf_op jit(solution)/shard_map/ppermute | solution.py:71
  4.1 0.0 copy-start
  4.1 2.3 %copy-done = bf16[3,3,512,512]{3,2,1,0:T(8,128)(2,1)S(1)} copy-done((bf16[3,3,512,512]{3,2,1,0:T(8,128)(2,1)S(1)}, bf16[3,3,512,512]{3,2,1,0:T(8,128)(2,1)}, u32[]{:S(2)}) %copy-start) | copy-done | bytes 4718616
  6.4 0.0 copy-start.3
  6.4 1.8 %shard_map.65.total_ref = f32[2,32,16,512]{3,2,1,0:T(8,128)S(1)} custom-call(bf16[2,32,16,512]{3,2,1,0:T(8,128)(2,1)S(1)} %copy-done.1, bf16[2,48,512]{2,1,0:T(8,128)(2,1)S(1)} %collective-permute-done.got_ref, bf16[3,3,512,512]{3,2,1,0:T(8,128)(2,1)S(1)} %copy-done), custom_call_target="tpu_custom_call" | custom-call | flops 1610612736 | bytes 7962624 | tf_op jit(solution)/shard_map/pallas_call | solution.py:19
  8.2 0.0 collective-permute-done.1.mine_ref
  8.2 4.3 %collective-permute-start.2 = (bf16[2,64,512]{2,1,0:T(8,128)(2,1)S(1)}, bf16[2,64,512]{2,1,0:T(8,128)(2,1)S(1)}, u32[]{:S(2)}, u32[]{:S(2)}) collective-permute-start(bf16[2,64,512]{2,1,0:T(8,128)(2,1)S(1)} %collective-permute-done.1.mine_ref), channel_id=1, source_target_pairs={{0,4},{4,0},{1,5},{5,1},{2,6},{6,2},{3,7},{7,3},{8,12},{12,8},{9,1... | collective-permute-start | bytes 393224 | tf_op jit(solution)/shard_map/ppermute | solution.py:62
  12.6 1.0 %collective-permute-done.2.theirs_ref = bf16[2,64,512]{2,1,0:T(8,128)(2,1)S(1)} collective-permute-done((bf16[2,64,512]{2,1,0:T(8,128)(2,1)S(1)}, bf16[2,64,512]{2,1,0:T(8,128)(2,1)S(1)}, u32[]{:S(2)}, u32[]{:S(2)}) %collective-permute-start.2) | collective-permute-done | bytes 131104 | tf_op jit(solution)/shard_map/ppermute | solution.py:62
  13.5 0.0 slice-start
  13.5 0.0 copy-done.3
  13.5 0.0 slice-start.1
  13.5 3.8 %shard_map.66 = (f32[2,32,16,512]{3,2,1,0:T(8,128)S(1)}, bf16[32,16,512]{2,1,0:T(8,128)(2,1)S(1)}) custom-call(bf16[2,32,16,512]{3,2,1,0:T(8,128)(2,1)S(1)} %copy-done.1, bf16[2,48,512]{2,1,0:T(8,128)(2,1)S(1)} %collective-permute-done.got_ref, bf16[2,64,512]{2,1,0:T(8,128)(2,1)S(1)} %collective-permute-done.1.mine_ref, ...), custom_call_target="tpu_custom_call" | custom-call | flops 3221225472 | bytes 10848256 | tf_op jit(solution)/shard_map/pallas_call | solution.py:19
  17.3 0.0 copy-start.2
  17.4 0.0 copy-start.4
  17.4 12.7 %all_to_all.10.refs_0_ = bf16[4,128,512]{2,1,0:T(8,128)(2,1)S(1)} all-to-all(bf16[4,128,512]{2,1,0:T(8,128)(2,1)S(1)} %bitcast.7), channel_id=1, replica_groups=mesh['tm'=4,'sx'=2,'sy'=4] {'tm'}, dimensions={0} | all-to-all | bytes 1048576 | tf_op jit(solution)/shard_map/all_to_all | solution.py:251
  30.1 0.1 shard_map.67
  30.2 10.2 %all_to_all.11 = bf16[4,128,512]{2,1,0:T(8,128)(2,1)S(1)} all-to-all(bf16[4,128,512]{2,1,0:T(8,128)(2,1)S(1)} %shard_map.67), channel_id=1, replica_groups=mesh['tm'=4,'sx'=2,'sy'=4] {'tm'}, dimensions={0} | all-to-all | bytes 1048576 | tf_op jit(solution)/shard_map/all_to_all | solution.py:258
  40.4 0.0 copy-done.2
  40.4 0.0 copy-done.4
  40.4 1.5 %shard_map.68 = (bf16[2,32,16,512]{3,2,1,0:T(8,128)(2,1)S(1)}, bf16[2,48,512]{2,1,0:T(8,128)(2,1)S(1)}, bf16[2,32,512]{2,1,0:T(8,128)(2,1)S(1)}) custom-call(f32[2,32,16,512]{3,2,1,0:T(8,128)S(1)} %get-tuple-element.20.drive_ref, bf16[32,16,512]{2,1,0:T(8,128)(2,1)S(1)} %bitcast.6, f32[32,16,512]{2,1,0:T(8,128)S(1)} %copy-done.2, s32[1,512]{1,0:T(1,128)S(1)} %bitcast.10, ...), custom_call_target="tpu_custom_call" | custom-call | bytes 4886528 | tf_op jit(solution)/shard_map/pallas_call | solution.py:19
  42.0 0.1 collective-permute-start.3
  42.0 1.3 %collective-permute-done.3.got_ref = bf16[2,48,512]{2,1,0:T(8,128)(2,1)S(1)} collective-permute-done((bf16[2,48,512]{2,1,0:T(8,128)(2,1)S(1)}, bf16[2,48,512]{2,1,0:T(8,128)(2,1)S(1)}, u32[]{:S(2)}, u32[]{:S(2)}) %collective-permute-start.3) | collective-permute-done | bytes 98336 | tf_op jit(solution)/shard_map/ppermute | solution.py:62
  43.3 0.7 %collective-permute-start.4 = (bf16[2,64,512]{2,1,0:T(8,128)(2,1)S(1)}, bf16[2,64,512]{2,1,0:T(8,128)(2,1)S(1)}, u32[]{:S(2)}, u32[]{:S(2)}) collective-permute-start(bf16[2,64,512]{2,1,0:T(8,128)(2,1)S(1)} %pad_maximum_fusion.1), channel_id=1, source_target_pairs={{1,4},{2,5},{3,6},{4,1},{5,2},{6,3},{9,12},{10,13},{11,14},{12,9},... | collective-permute-start | bytes 393224 | tf_op jit(solution)/shard_map/ppermute | solution.py:71
  44.0 0.0 slice-done
  44.0 0.0 slice-done.1
  44.1 1.8 %shard_map.69.total_ref = f32[2,32,16,512]{3,2,1,0:T(8,128)S(1)} custom-call(bf16[2,32,16,512]{3,2,1,0:T(8,128)(2,1)S(1)} %get-tuple-element.22.cells_ref, bf16[2,48,512]{2,1,0:T(8,128)(2,1)S(1)} %collective-permute-done.3.got_ref, bf16[3,3,512,512]{3,2,1,0:T(8,128)(2,1)S(1)} %bitcast.5), custom_call_target="tpu_custom_call" | custom-call | flops 1610612736 | bytes 7962624 | tf_op jit(solution)/shard_map/pallas_call | solution.py:19
  45.9 0.0 collective-permute-done.4.mine_ref
  45.9 3.9 %collective-permute-start.5 = (bf16[2,64,512]{2,1,0:T(8,128)(2,1)S(1)}, bf16[2,64,512]{2,1,0:T(8,128)(2,1)S(1)}, u32[]{:S(2)}, u32[]{:S(2)}) collective-permute-start(bf16[2,64,512]{2,1,0:T(8,128)(2,1)S(1)} %collective-permute-done.4.mine_ref), channel_id=1, source_target_pairs={{0,4},{4,0},{1,5},{5,1},{2,6},{6,2},{3,7},{7,3},{8,12},{12,8},{9,1... | collective-permute-start | bytes 393224 | tf_op jit(solution)/shard_map/ppermute | solution.py:62
  49.8 1.0 %collective-permute-done.5.theirs_ref = bf16[2,64,512]{2,1,0:T(8,128)(2,1)S(1)} collective-permute-done((bf16[2,64,512]{2,1,0:T(8,128)(2,1)S(1)}, bf16[2,64,512]{2,1,0:T(8,128)(2,1)S(1)}, u32[]{:S(2)}, u32[]{:S(2)}) %collective-permute-start.5) | collective-permute-done | bytes 131104 | tf_op jit(solution)/shard_map/ppermute | solution.py:62
  50.8 4.7 %shard_map.70 = bf16[2,32,16,512]{3,2,1,0:T(8,128)(2,1)} custom-call(bf16[2,32,16,512]{3,2,1,0:T(8,128)(2,1)S(1)} %get-tuple-element.22.cells_ref, bf16[2,48,512]{2,1,0:T(8,128)(2,1)S(1)} %collective-permute-done.3.got_ref, bf16[2,64,512]{2,1,0:T(8,128)(2,1)S(1)} %collective-permute-done.4.mine_ref, ...), custom_call_target="tpu_custom_call" | custom-call | flops 3221225472 | bytes 9273344 | tf_op jit(solution)/shard_map/pallas_call | solution.py:19
  (5 shorter events, 0.0 us)
Async XLA Ops:
  0.0 1.2 %copy-start.1 = (bf16[2,32,16,512]{3,2,1,0:T(8,128)(2,1)S(1)}, bf16[2,32,16,512]{3,2,1,0:T(8,128)(2,1)}, u32[]{:S(2)}) copy-start(bf16[2,32,16,512]{3,2,1,0:T(8,128)(2,1)} %cells_ref.5) | copy-start | bytes 3145732
  1.9 1.5 %collective-permute-start = (bf16[2,48,512]{2,1,0:T(8,128)(2,1)S(1)}, bf16[2,48,512]{2,1,0:T(8,128)(2,1)S(1)}, u32[]{:S(2)}, u32[]{:S(2)}) collective-permute-start(bf16[2,48,512]{2,1,0:T(8,128)(2,1)S(1)} %get-tuple-element.16), channel_id=1, source_target_pairs={{0,4},{4,0},{1,5},{5,1},{2,6},{6,2},{3,7},{7,3},{8,12},{12,8},{9,1... | collective-permute-start | bytes 294920 | tf_op jit(solution)/shard_map/ppermute | solution.py:62
  3.4 4.8 %collective-permute-start.1 = (bf16[2,64,512]{2,1,0:T(8,128)(2,1)S(1)}, bf16[2,64,512]{2,1,0:T(8,128)(2,1)S(1)}, u32[]{:S(2)}, u32[]{:S(2)}) collective-permute-start(bf16[2,64,512]{2,1,0:T(8,128)(2,1)S(1)} %pad_maximum_fusion), channel_id=1, source_target_pairs={{1,4},{2,5},{3,6},{4,1},{5,2},{6,3},{9,12},{10,13},{11,14},{12,9},... | collective-permute-start | bytes 393224 | tf_op jit(solution)/shard_map/ppermute | solution.py:71
  4.1 2.3 %copy-start = (bf16[3,3,512,512]{3,2,1,0:T(8,128)(2,1)S(1)}, bf16[3,3,512,512]{3,2,1,0:T(8,128)(2,1)}, u32[]{:S(2)}) copy-start(bf16[3,3,512,512]{3,2,1,0:T(8,128)(2,1)} %weight_ref.5) | copy-start | bytes 14155780
  6.4 7.1 %copy-start.3 = (s32[512]{0:T(512)S(1)}, s32[512]{0:T(512)}, u32[]{:S(2)}) copy-start(s32[512]{0:T(512)} %param.9) | copy-start | bytes 6148
  8.2 5.3 %collective-permute-start.2 = (bf16[2,64,512]{2,1,0:T(8,128)(2,1)S(1)}, bf16[2,64,512]{2,1,0:T(8,128)(2,1)S(1)}, u32[]{:S(2)}, u32[]{:S(2)}) collective-permute-start(bf16[2,64,512]{2,1,0:T(8,128)(2,1)S(1)} %collective-permute-done.1.mine_ref), channel_id=1, source_target_pairs={{0,4},{4,0},{1,5},{5,1},{2,6},{6,2},{3,7},{7,3},{8,12},{12,8},{9,1... | collective-permute-start | bytes 393224 | tf_op jit(solution)/shard_map/ppermute | solution.py:62
  13.5 30.5 %slice-start = ((s8[4718592]{0:T(1024)(128)(4,1)}), s8[4194304]{0:T(1024)(128)(4,1)S(1)}, s32[]{:S(2)}) async-start(s8[4718592]{0:T(1024)(128)(4,1)} %bitcast.4), calls=%async_computation.2 | async-start | bytes 8388608
  13.5 30.5 %slice-start.1 = ((s8[4718592]{0:T(1024)(128)(4,1)}), s8[524288]{0:T(1024)(128)(4,1)S(1)}, s32[]{:S(2)}) async-start(s8[4718592]{0:T(1024)(128)(4,1)} %bitcast.4), calls=%async_computation.3 | async-start | bytes 1048576
  17.3 23.1 %copy-start.2 = (f32[32,16,512]{2,1,0:T(8,128)S(1)}, f32[32,16,512]{2,1,0:T(8,128)}, u32[]{:S(2)}) copy-start(f32[32,16,512]{2,1,0:T(8,128)} %start_ref.1) | copy-start | bytes 3145732
  17.4 23.1 %copy-start.4 = (f32[512]{0:T(512)S(1)}, f32[512]{0:T(512)}, u32[]{:S(2)}) copy-start(f32[512]{0:T(512)} %param.10) | copy-start | bytes 6148
  42.0 1.4 %collective-permute-start.3 = (bf16[2,48,512]{2,1,0:T(8,128)(2,1)S(1)}, bf16[2,48,512]{2,1,0:T(8,128)(2,1)S(1)}, u32[]{:S(2)}, u32[]{:S(2)}) collective-permute-start(bf16[2,48,512]{2,1,0:T(8,128)(2,1)S(1)} %get-tuple-element.23), channel_id=1, source_target_pairs={{0,4},{4,0},{1,5},{5,1},{2,6},{6,2},{3,7},{7,3},{8,12},{12,8},{9,1... | collective-permute-start | bytes 294920 | tf_op jit(solution)/shard_map/ppermute | solution.py:62
  43.3 2.5 %collective-permute-start.4 = (bf16[2,64,512]{2,1,0:T(8,128)(2,1)S(1)}, bf16[2,64,512]{2,1,0:T(8,128)(2,1)S(1)}, u32[]{:S(2)}, u32[]{:S(2)}) collective-permute-start(bf16[2,64,512]{2,1,0:T(8,128)(2,1)S(1)} %pad_maximum_fusion.1), channel_id=1, source_target_pairs={{1,4},{2,5},{3,6},{4,1},{5,2},{6,3},{9,12},{10,13},{11,14},{12,9},... | collective-permute-start | bytes 393224 | tf_op jit(solution)/shard_map/ppermute | solution.py:71
  45.9 4.9 %collective-permute-start.5 = (bf16[2,64,512]{2,1,0:T(8,128)(2,1)S(1)}, bf16[2,64,512]{2,1,0:T(8,128)(2,1)S(1)}, u32[]{:S(2)}, u32[]{:S(2)}) collective-permute-start(bf16[2,64,512]{2,1,0:T(8,128)(2,1)S(1)} %collective-permute-done.4.mine_ref), channel_id=1, source_target_pairs={{0,4},{4,0},{1,5},{5,1},{2,6},{6,2},{3,7},{7,3},{8,12},{12,8},{9,1... | collective-permute-start | bytes 393224 | tf_op jit(solution)/shard_map/ppermute | solution.py:62

commit v4 on v3

v4 whole, which is shorter than its diff:
```python
import math

import jax
import jax.numpy as jnp
from jax import lax
from jax.experimental import pallas as pl
from jax.experimental.pallas import tpu as pltpu
from jax.sharding import PartitionSpec as P

NPOLES = 16
VMEM_LIMIT = 24 * 1024 * 1024
WHOLE = pl.BlockSpec(memory_space=pltpu.VMEM)
HBM = pl.BlockSpec(memory_space=pltpu.HBM)
LANES = 256


def call(kernel, out_shape, *args, scratch=(), flops=0, out_specs=None, aliases=None):
    outs = jax.tree.leaves(out_shape)
    moved = sum(leaf.size * leaf.dtype.itemsize for leaf in (*args, *outs))
    return pl.pallas_call(
        kernel,
        in_specs=[WHOLE] * len(args),
        out_specs=out_specs or jax.tree.map(lambda _: WHOLE, out_shape),
        out_shape=out_shape,
        scratch_shapes=scratch,
        input_output_aliases=aliases or {},
        compiler_params=pltpu.CompilerParams(vmem_limit_bytes=VMEM_LIMIT),
        cost_estimate=pl.CostEstimate(flops=flops, bytes_accessed=moved, transcendentals=0),
    )(*args)


def is_core(which):
    return (lax.axis_index("sx") == which).astype(jnp.float32)


def rate_of(pole_ref):
    pole = pole_ref[...].astype(jnp.float32)
    return -0.001 * jnp.exp(pole * (math.log(300.0) / (NPOLES - 1)))


def put_edges(frame, row, left, right, give_ref, keep_ref):
    cols = row.shape[0]
    zero, one = is_core(0), is_core(1)
    give_ref[frame, :cols] = row.astype(give_ref.dtype)
    give_ref[frame, cols:] = (zero * right + one * left).astype(give_ref.dtype)
    keep_ref[frame] = (zero * left + one * right).astype(keep_ref.dtype)


def inner_row(rows):
    return jnp.where(lax.axis_index("sx") == 0, rows - 1, 0)


def edge_shapes(cells):
    count, rows, cols, channels = cells.shape
    return (
        jax.ShapeDtypeStruct((count, cols + rows, channels), jnp.bfloat16),
        jax.ShapeDtypeStruct((count, rows, channels), jnp.bfloat16),
    )


def edges_kernel(cells_ref, give_ref, keep_ref):
    count, rows, cols, _ = cells_ref.shape
    for frame in range(count):
        tile = cells_ref[frame].astype(jnp.float32)
        row = cells_ref[frame, inner_row(rows)]
        put_edges(frame, row, tile[:, 0, :], tile[:, cols - 1, :], give_ref, keep_ref)


def swap_cores(array):
    return lax.ppermute(array, "sx", [(0, 1), (1, 0)])


def trade_columns(give, keep, cols):
    chips = lax.axis_size("sy")
    got = swap_cores(give)
    pairs = [(chip, chips + chip - 1) for chip in range(1, chips)]
    pairs += [(after, before) for before, after in pairs]
    column = jnp.concatenate([keep, got[:, cols:]], axis=1)
    return got, lax.ppermute(column, ("sx", "sy"), pairs)


def centre_kernel(cells_ref, got_ref, weight_ref, total_ref, lhs_ref):
    count, rows, cols, channels = cells_ref.shape
    size = rows * cols
    room = count * rows
    tap = weight_ref.shape[1] // 2
    mid, low = slice(channels, 2 * channels), slice(2 * channels, 3 * channels)
    for frame in range(count):
        at = room + frame * size
        row = got_ref[frame, :cols].astype(jnp.float32)
        cells = cells_ref[frame].reshape(size, channels)
        lhs_ref[at : at + cols, :channels] = (is_core(1) * row).astype(lhs_ref.dtype)
        lhs_ref[at + cols : at + size, :channels] = cells[: size - cols]
        lhs_ref[at : at + size, mid] = cells
        lhs_ref[at : at + size - cols, low] = cells[cols:]
        lhs_ref[at + size - cols : at + size, low] = (is_core(0) * row).astype(lhs_ref.dtype)
    for lane in range(0, weight_ref.shape[-1], LANES):
        lanes = slice(lane, lane + LANES)
        weight = weight_ref[:, tap, :, lanes].reshape(3 * channels, LANES)
        total = jnp.dot(lhs_ref[room:], weight, preferred_element_type=jnp.float32)
        total_ref[:, :, :, lanes] = total.reshape(count, rows, cols, LANES)


def centre(cells, got, weight):
    count, rows, cols, channels = cells.shape
    outs = weight.shape[-1]
    return call(
        centre_kernel,
        (
            jax.ShapeDtypeStruct((count, rows, cols, outs), jnp.float32),
            jax.ShapeDtypeStruct((count * rows * (cols + 1), 3 * channels), cells.dtype),
        ),
        cells,
        got,
        weight,
        flops=6 * count * rows * cols * channels * outs,
    )


def outer_taps(mine, halo_ref, weight_ref, total_ref, lhs_ref, finish):
    count, rows, cols, _ = total_ref.shape
    room = count * rows
    zero, one = is_core(0), is_core(1)
    row = lax.broadcasted_iota(jnp.int32, (rows, halo_ref.shape[2]), 0)
    for frame in range(count):
        halo = halo_ref[frame].astype(jnp.float32)
        if mine:
            mid, above, below = halo[rows:], halo[rows - 1 : rows], halo[:1]
        else:
            mid, above, below = halo[:rows], halo[2 * rows - 1 :], halo[rows : rows + 1]
        up = jnp.where(row == 0, one * above, pltpu.roll(mid, 1, 0))
        down = jnp.where(row == rows - 1, zero * below, pltpu.roll(mid, rows - 1, 0))
        taps = jnp.concatenate([up, mid, down], axis=1)
        lhs_ref[frame * rows : (frame + 1) * rows] = taps.astype(lhs_ref.dtype)

    def side(column, shift, edge):
        col = lax.broadcasted_iota(jnp.int32, (count, rows, cols, LANES), 2)
        for lane in range(0, weight_ref.shape[-1], LANES):
            lanes = slice(lane, lane + LANES)
            weight = weight_ref[:, column, :, lanes].reshape(-1, LANES)
            product = jnp.dot(lhs_ref[...], weight, preferred_element_type=jnp.float32)
            halo = product[:room].reshape(count, rows, 1, LANES)
            product = pltpu.roll(product[room:].reshape(count, rows, cols, LANES), shift, 2)
            finish(lanes, total_ref[:, :, :, lanes] + jnp.where(col == edge, halo, product))

    pl.when(lax.axis_index("sx") == (0 if mine else 1))(lambda: side(0, 1, 0))
    pl.when(lax.axis_index("sx") == (1 if mine else 0))(
        lambda: side(weight_ref.shape[1] - 1, cols - 1, cols - 1)
    )


def own_kernel(halo_ref, weight_ref, total_ref, _, out_ref, lhs_ref):
    def finish(lanes, total):
        out_ref[:, :, :, lanes] = total

    outer_taps(True, halo_ref, weight_ref, total_ref, lhs_ref, finish)


def drive_kernel(halo_ref, weight_ref, total_ref, _, pole_ref, out_ref, end_ref, lhs_ref):
    decay = jnp.exp(rate_of(pole_ref))

    def finish(lanes, total):
        out_ref[:, :, :, lanes] = total
        state = total[0]
        for frame in range(1, total.shape[0]):
            state = decay[:, lanes] * state + total[frame]
        end_ref[:, :, lanes] = state.astype(end_ref.dtype)

    outer_taps(False, halo_ref, weight_ref, total_ref, lhs_ref, finish)


def result_kernel(halo_ref, weight_ref, total_ref, _, out_ref, lhs_ref, held_ref, sems):
    def store(lanes):
        return pltpu.make_async_copy(
            held_ref.at[:, :, :, lanes],
            out_ref.at[:, :, :, lanes],
            sems.at[lanes.start // LANES],
        )

    def finish(lanes, total):
        held_ref[:, :, :, lanes] = total.astype(held_ref.dtype)
        store(lanes).start()

    outer_taps(False, halo_ref, weight_ref, total_ref, lhs_ref, finish)
    for lane in range(0, held_ref.shape[-1], LANES):
        store(slice(lane, lane + LANES)).wait()


def convolve(cells, give, keep, weight, middle, kernel, out_shape, *more, out_specs, scratch=()):
    got, mine = trade_columns(give, keep, cells.shape[2])
    mine, (total, lhs) = lax.optimization_barrier((mine, centre(cells, got, middle)))
    theirs = swap_cores(mine)
    flops = 6 * cells.size * weight.shape[-1]
    held = jax.ShapeDtypeStruct(lhs.shape, lhs.dtype)
    total, lhs = call(
        own_kernel,
        (jax.ShapeDtypeStruct(total.shape, total.dtype), held),
        mine,
        weight,
        total,
        lhs,
        flops=flops,
        aliases={3: 1},
    )
    *outs, _ = call(
        kernel,
        (*out_shape, held),
        theirs,
        weight,
        total,
        lhs,
        *more,
        flops=flops,
        out_specs=(*out_specs, WHOLE),
        aliases={3: len(out_shape)},
        scratch=scratch,
    )
    return outs


def entry_kernel(frames, ends_ref, pole_ref, out_ref):
    carried = jnp.exp(frames * rate_of(pole_ref))
    entry = jnp.zeros(ends_ref.shape[1:], jnp.float32)
    out_ref[0] = entry.astype(out_ref.dtype)
    for index in range(ends_ref.shape[0] - 1):
        entry = carried * entry + ends_ref[index].astype(jnp.float32)
        out_ref[index + 1] = entry.astype(out_ref.dtype)


def activated(drives, entry, start, pole_ref, scale_ref):
    rate = rate_of(pole_ref)
    decay = jnp.exp(rate)
    reach = jnp.exp((len(drives) * lax.axis_index("tm")).astype(jnp.float32) * rate)
    state = reach * start + entry.astype(jnp.float32)
    for drive in drives:
        state = decay * state + drive
        yield jax.nn.gelu(scale_ref[...] * state)


def mixed_edges_kernel(
    drive_ref, entry_ref, start_ref, pole_ref, scale_ref, give_ref, keep_ref
):
    count, rows, cols, _ = drive_ref.shape
    inner = inner_row(rows)
    entry = entry_ref[...].astype(jnp.float32)

    def column(col):
        drives = [drive_ref[frame][:, col, :] for frame in range(count)]
        return activated(drives, entry[:, col, :], start_ref[...][:, col, :], pole_ref, scale_ref)

    drives = [drive_ref[frame, inner] for frame in range(count)]
    row = activated(drives, entry_ref[inner], start_ref[inner], pole_ref, scale_ref)
    edges = (row, column(0), column(cols - 1))
    for frame, (row, left, right) in enumerate(zip(*edges)):
        put_edges(frame, row, left, right, give_ref, keep_ref)


def mixed_kernel(drive_ref, entry_ref, start_ref, pole_ref, scale_ref, out_ref):
    count, rows, _, _ = drive_ref.shape
    block = 8
    for row in range(0, rows, block):
        here = slice(row, row + block)
        drives = [drive_ref[frame, here] for frame in range(count)]
        mixed = activated(drives, entry_ref[here], start_ref[here], pole_ref, scale_ref)
        for frame, tile in enumerate(mixed):
            out_ref[frame, here] = tile.astype(out_ref.dtype)


def on_device(frames, input_weight, output_weight, pole_index, gelu_scale, start_state):
    count, rows, cols, channels = frames.shape
    groups = lax.axis_size("tm")
    assert lax.axis_size("sx") == 2
    pole = pole_index[None]

    give, keep = call(edges_kernel, edge_shapes(frames), frames)
    middle = input_weight[:, 1:2]
    drive, end = convolve(
        frames,
        give,
        keep,
        input_weight,
        middle,
        drive_kernel,
        (
            jax.ShapeDtypeStruct((count, rows, cols, channels), jnp.float32),
            jax.ShapeDtypeStruct((rows, cols, channels), jnp.bfloat16),
        ),
        pole,
        out_specs=(WHOLE, WHOLE),
    )

    ends = lax.all_to_all(end.reshape(groups, -1, channels), "tm", 0, 0)
    entries = call(
        lambda *refs: entry_kernel(count, *refs),
        jax.ShapeDtypeStruct(ends.shape, ends.dtype),
        ends,
        pole,
    )
    entry = lax.all_to_all(entries, "tm", 0, 0).reshape(rows, cols, channels)

    states = (drive, entry, start_state, pole, gelu_scale[None])
    shape = jax.ShapeDtypeStruct(frames.shape, jnp.bfloat16)
    give, keep = call(mixed_edges_kernel, edge_shapes(frames), *states)
    mixed = call(mixed_kernel, shape, *states)
    (result,) = convolve(
        mixed,
        give,
        keep,
        output_weight,
        output_weight,
        result_kernel,
        (shape,),
        out_specs=(HBM,),
        scratch=[
            pltpu.VMEM(frames.shape, jnp.bfloat16),
            pltpu.SemaphoreType.DMA((channels // LANES,)),
        ],
    )
    return result


def solution(mesh):
    return jax.shard_map(
        on_device,
        mesh=mesh,
        in_specs=(P("tm", "sx", "sy", None), P(), P(), P(), P(), P("sx", "sy", None)),
        out_specs=P("tm", "sx", "sy", None),
        check_vma=False,
    )
```

time: 55.8 us -> 52.4 us (0.939)
  waiting for transfers between devices: 4.21 us -> 0.27 us
  local copies, waits for them, and re-layouts: 3.59 us -> 2.78 us
  starting transfers between devices: 10.2 us -> 11 us
  Pallas kernels: 14.4 us -> 15.1 us
    ppermute x4, waiting for transfers between devices: 4.2 us -> 0.26 us  [swap_cores(): return lax.ppermute(array, 'sx', [(0, 1), (1, 0)])]
    unnamed x14, local copies, waits for them, and re-layouts: 3.58 us -> 1.26 us
    slice x0 -> x1, local copies, waits for them, and re-layouts: none -> 1.51 us  [on_device(): middle = input_weight[:, 1:2]]
    pallas_call x7 -> x10, Pallas kernels: 14.4 us -> 15.1 us  [call(): pl.pallas_call(kernel, in_specs=[WHOLE] * len(args), out_specs=out_specs...]
    ppermute x4, starting transfers between devices: 8.86 us -> 9.52 us  [swap_cores(): return lax.ppermute(array, 'sx', [(0, 1), (1, 0)])]
  transfers between devices with their start and end apart: 6 -> 6, of which waited for: 4 -> 1; matrix products, arithmetic and copies ran while one was open for 0% -> 3% of each run, Pallas kernels for 6% -> 17%
where the time goes in v4:
time: 52.4 us; the launch traced here: 52.1 us
  blocking collectives  22.8 us (44%)
  Pallas kernels  15.1 us (29%)
  starting transfers between devices  11 us (21%)
  local copies, waits for them, and re-layouts  2.78 us (5%)
    pallas_call x10, Pallas kernels, call(): pl.pallas_call(kernel, in_specs=[WHOLE] * len(args), out_specs=out_specs...  15.1 us
    all_to_all x1, blocking collectives, on_device(): ends = lax.all_to_all(end.reshape(groups, -1, channels), 'tm', 0, 0)  12.9 us
    all_to_all x1, blocking collectives, on_device(): entry = lax.all_to_all(entries, 'tm', 0, 0).reshape(rows, cols, channels)  9.91 us
    ppermute x4, starting transfers between devices, swap_cores(): return lax.ppermute(array, 'sx', [(0, 1), (1, 0)])  9.52 us
    slice x1, local copies, waits for them, and re-layouts, on_device(): middle = input_weight[:, 1:2]  1.51 us
    ppermute x2, starting transfers between devices, trade_columns(): return (got, lax.ppermute(column, ('sx', 'sy'), pairs))  1.47 us
    unnamed x14, local copies, waits for them, and re-layouts  1.26 us
  transfers between devices with their start and end apart: 6, of which 1 were waited for; matrix products, arithmetic and copies ran while one was open for 3% of the time, Pallas kernels for 17%

profile of v4, /device:TPU:0, one launch (start us, length us, event | category | flops | bytes accessed | tf_op | source)
XLA Modules:
  0.0 52.1 jit_solution(11085346865491891321)
XLA Ops:
  0.0 0.0 copy-start.2
  0.0 1.2 %copy-done.2 = bf16[2,32,16,512]{3,2,1,0:T(8,128)(2,1)S(1)} copy-done((bf16[2,32,16,512]{3,2,1,0:T(8,128)(2,1)S(1)}, bf16[2,32,16,512]{3,2,1,0:T(8,128)(2,1)}, u32[]{:S(2)}) %copy-start.2) | copy-done | bytes 1048600
  1.2 0.7 %shard_map.64 = (bf16[2,48,512]{2,1,0:T(8,128)(2,1)S(1)}, bf16[2,32,512]{2,1,0:T(8,128)(2,1)S(1)}) custom-call(bf16[2,32,16,512]{3,2,1,0:T(8,128)(2,1)S(1)} %copy-done.2), custom_call_target="tpu_custom_call" | custom-call | bytes 1212416 | tf_op jit(solution)/shard_map/pallas_call | solution.py:20
  1.9 0.5 collective-permute-start
  2.4 1.5 %slice.10.weight_ref = bf16[3,1,512,512]{3,2,1,0:T(8,128)(2,1)S(1)} slice(bf16[3,3,512,512]{3,2,1,0:T(8,128)(2,1)} %weight_ref.6), slice={[0:3], [1:2], [0:512], [0:512]} | slice | bytes 3145728 | tf_op jit(solution)/shard_map/slice | solution.py:276
  3.9 0.0 copy-start
  3.9 0.0 collective-permute-done.got_ref
  4.0 0.8 %collective-permute-start.1 = (bf16[2,64,512]{2,1,0:T(8,128)(2,1)S(1)}, bf16[2,64,512]{2,1,0:T(8,128)(2,1)S(1)}, u32[]{:S(2)}, u32[]{:S(2)}) collective-permute-start(bf16[2,64,512]{2,1,0:T(8,128)(2,1)S(1)} %pad_maximum_fusion), channel_id=1, source_target_pairs={{1,4},{2,5},{3,6},{4,1},{5,2},{6,3},{9,12},{10,13},{11,14},{12,9},... | collective-permute-start | bytes 393224 | tf_op jit(solution)/shard_map/ppermute | solution.py:79
  4.8 1.8 %shard_map.65 = (f32[2,32,16,512]{3,2,1,0:T(8,128)S(1)}, bf16[1088,1536]{1,0:T(8,128)(2,1)S(1)}) custom-call(bf16[2,32,16,512]{3,2,1,0:T(8,128)(2,1)S(1)} %copy-done.2, bf16[2,48,512]{2,1,0:T(8,128)(2,1)S(1)} %collective-permute-done.got_ref, bf16[3,1,512,512]{3,2,1,0:T(8,128)(2,1)S(1)} %slice.10.weight_ref), custom_call_target="tpu_custom_call" | custom-call | flops 1610612736 | bytes 8159232 | tf_op jit(solution)/shard_map/pallas_call | solution.py:20
  6.6 0.0 collective-permute-done.1.halo_ref
  6.6 0.0 copy-start.3
  6.6 4.9 %collective-permute-start.2 = (bf16[2,64,512]{2,1,0:T(8,128)(2,1)S(1)}, bf16[2,64,512]{2,1,0:T(8,128)(2,1)S(1)}, u32[]{:S(2)}, u32[]{:S(2)}) collective-permute-start(bf16[2,64,512]{2,1,0:T(8,128)(2,1)S(1)} %collective-permute-done.1.halo_ref), channel_id=1, source_target_pairs={{0,4},{4,0},{1,5},{5,1},{2,6},{6,2},{3,7},{7,3},{8,12},{12,8},{9,1... | collective-permute-start | bytes 393224 | tf_op jit(solution)/shard_map/ppermute | solution.py:70
  11.5 0.0 copy-done
  11.5 2.0 %shard_map.66 = (f32[2,32,16,512]{3,2,1,0:T(8,128)S(1)}, bf16[1088,1536]{1,0:T(8,128)(2,1)S(1)}) custom-call(bf16[2,64,512]{2,1,0:T(8,128)(2,1)S(1)} %collective-permute-done.1.halo_ref, bf16[3,3,512,512]{3,2,1,0:T(8,128)(2,1)S(1)} %copy-done, f32[2,32,16,512]{3,2,1,0:T(8,128)S(1)} %get-tuple-element.31.total_ref, ...), custom_call_target="tpu_custom_call", output_to_operand_aliasing={{1}: (3, {})} | custom-call | flops 1610612736 | bytes 15728640 | tf_op jit(solution)/shard_map/pallas_call | solution.py:20
  13.5 0.0 collective-permute-done.2.halo_ref
  13.6 0.0 copy-done.3
  13.6 0.0 copy-start.4
  13.6 2.2 %shard_map.67 = (f32[2,32,16,512]{3,2,1,0:T(8,128)S(1)}, bf16[32,16,512]{2,1,0:T(8,128)(2,1)S(1)}, bf16[1088,1536]{1,0:T(8,128)(2,1)S(1)}) custom-call(bf16[2,64,512]{2,1,0:T(8,128)(2,1)S(1)} %collective-permute-done.2.halo_ref, bf16[3,3,512,512]{3,2,1,0:T(8,128)(2,1)S(1)} %copy-done, ...), custom_call_target="tpu_custom_call", output_to_operand_aliasing={{2}: (3, {})} | custom-call | flops 1610612736 | bytes 16254976 | tf_op jit(solution)/shard_map/pallas_call | solution.py:20
  15.8 0.0 copy-start.1
  15.8 12.9 %all_to_all.10.refs_0_ = bf16[4,128,512]{2,1,0:T(8,128)(2,1)S(1)} all-to-all(bf16[4,128,512]{2,1,0:T(8,128)(2,1)S(1)} %bitcast.8), channel_id=1, replica_groups=mesh['tm'=4,'sx'=2,'sy'=4] {'tm'}, dimensions={0} | all-to-all | bytes 1048576 | tf_op jit(solution)/shard_map/all_to_all | solution.py:292
  28.6 0.0 slice-start
  28.6 0.1 shard_map.68
  28.7 9.9 %all_to_all.11 = bf16[4,128,512]{2,1,0:T(8,128)(2,1)S(1)} all-to-all(bf16[4,128,512]{2,1,0:T(8,128)(2,1)S(1)} %shard_map.68), channel_id=1, replica_groups=mesh['tm'=4,'sx'=2,'sy'=4] {'tm'}, dimensions={0} | all-to-all | bytes 1048576 | tf_op jit(solution)/shard_map/all_to_all | solution.py:299
  38.7 0.0 copy-done.4
  38.7 0.0 copy-done.1
  38.7 0.0 slice-start.1
  38.7 0.5 shard_map.69
  39.1 0.1 collective-permute-start.3
  39.2 1.0 %shard_map.70.cells_ref = bf16[2,32,16,512]{3,2,1,0:T(8,128)(2,1)S(1)} custom-call(f32[2,32,16,512]{3,2,1,0:T(8,128)S(1)} %get-tuple-element.35.drive_ref, bf16[32,16,512]{2,1,0:T(8,128)(2,1)S(1)} %bitcast.7, f32[32,16,512]{2,1,0:T(8,128)S(1)} %copy-done.1, s32[1,512]{1,0:T(1,128)S(1)} %bitcast.12, f32[1,512]{1,0:T(1,128)S(1)} %bitcast.14), custom_call_target="tpu_custom_call" | custom-call | bytes 4722688 | tf_op jit(solution)/shard_map/pallas_call | solution.py:20
  40.3 0.3 collective-permute-done.3.got_ref
  40.5 0.7 %collective-permute-start.4 = (bf16[2,64,512]{2,1,0:T(8,128)(2,1)S(1)}, bf16[2,64,512]{2,1,0:T(8,128)(2,1)S(1)}, u32[]{:S(2)}, u32[]{:S(2)}) collective-permute-start(bf16[2,64,512]{2,1,0:T(8,128)(2,1)S(1)} %pad_maximum_fusion.1), channel_id=1, source_target_pairs={{1,4},{2,5},{3,6},{4,1},{5,2},{6,3},{9,12},{10,13},{11,14},{12,9},... | collective-permute-start | bytes 393224 | tf_op jit(solution)/shard_map/ppermute | solution.py:79
  41.2 0.0 slice-done
  41.2 0.0 slice-done.1
  41.2 1.8 %shard_map.71 = (f32[2,32,16,512]{3,2,1,0:T(8,128)S(1)}, bf16[1088,1536]{1,0:T(8,128)(2,1)S(1)}) custom-call(bf16[2,32,16,512]{3,2,1,0:T(8,128)(2,1)S(1)} %shard_map.70.cells_ref, bf16[2,48,512]{2,1,0:T(8,128)(2,1)S(1)} %collective-permute-done.3.got_ref, bf16[3,3,512,512]{3,2,1,0:T(8,128)(2,1)S(1)} %bitcast.5), custom_call_target="tpu_custom_call" | custom-call | flops 1610612736 | bytes 11304960 | tf_op jit(solution)/shard_map/pallas_call | solution.py:20
  43.0 0.0 collective-permute-done.4.halo_ref
  43.0 4.0 %collective-permute-start.5 = (bf16[2,64,512]{2,1,0:T(8,128)(2,1)S(1)}, bf16[2,64,512]{2,1,0:T(8,128)(2,1)S(1)}, u32[]{:S(2)}, u32[]{:S(2)}) collective-permute-start(bf16[2,64,512]{2,1,0:T(8,128)(2,1)S(1)} %collective-permute-done.4.halo_ref), channel_id=1, source_target_pairs={{0,4},{4,0},{1,5},{5,1},{2,6},{6,2},{3,7},{7,3},{8,12},{12,8},{9,1... | collective-permute-start | bytes 393224 | tf_op jit(solution)/shard_map/ppermute | solution.py:70
  47.1 2.0 %shard_map.72 = (f32[2,32,16,512]{3,2,1,0:T(8,128)S(1)}, bf16[1088,1536]{1,0:T(8,128)(2,1)S(1)}) custom-call(bf16[2,64,512]{2,1,0:T(8,128)(2,1)S(1)} %collective-permute-done.4.halo_ref, bf16[3,3,512,512]{3,2,1,0:T(8,128)(2,1)S(1)} %bitcast.5, f32[2,32,16,512]{3,2,1,0:T(8,128)S(1)} %get-tuple-element.42.total_ref, ...), custom_call_target="tpu_custom_call", output_to_operand_aliasing={{1}: (3, {})} | custom-call | flops 1610612736 | bytes 15728640 | tf_op jit(solution)/shard_map/pallas_call | solution.py:20
  49.1 0.0 collective-permute-done.5.halo_ref
  49.1 3.0 %shard_map.73 = (bf16[2,32,16,512]{3,2,1,0:T(8,128)(2,1)}, bf16[1088,1536]{1,0:T(8,128)(2,1)S(1)}) custom-call(bf16[2,64,512]{2,1,0:T(8,128)(2,1)S(1)} %collective-permute-done.5.halo_ref, bf16[3,3,512,512]{3,2,1,0:T(8,128)(2,1)S(1)} %bitcast.5, f32[2,32,16,512]{3,2,1,0:T(8,128)S(1)} %get-tuple-element.44.total_ref, ...), custom_call_target="tpu_custom_call", output_to_operand_aliasing={{1}: (3, {})} | custom-call | flops 1610612736 | bytes 14680064 | tf_op jit(solution)/shard_map/pallas_call | solution.py:20
  (5 shorter events, 0.0 us)
Async XLA Ops:
  0.0 1.2 %copy-start.2 = (bf16[2,32,16,512]{3,2,1,0:T(8,128)(2,1)S(1)}, bf16[2,32,16,512]{3,2,1,0:T(8,128)(2,1)}, u32[]{:S(2)}) copy-start(bf16[2,32,16,512]{3,2,1,0:T(8,128)(2,1)} %cells_ref.3) | copy-start | bytes 3145732
  1.9 2.0 %collective-permute-start = (bf16[2,48,512]{2,1,0:T(8,128)(2,1)S(1)}, bf16[2,48,512]{2,1,0:T(8,128)(2,1)S(1)}, u32[]{:S(2)}, u32[]{:S(2)}) collective-permute-start(bf16[2,48,512]{2,1,0:T(8,128)(2,1)S(1)} %get-tuple-element.27), channel_id=1, source_target_pairs={{0,4},{4,0},{1,5},{5,1},{2,6},{6,2},{3,7},{7,3},{8,12},{12,8},{9,1... | collective-permute-start | bytes 294920 | tf_op jit(solution)/shard_map/ppermute | solution.py:70
  3.9 7.6 %copy-start = (bf16[3,3,512,512]{3,2,1,0:T(8,128)(2,1)S(1)}, bf16[3,3,512,512]{3,2,1,0:T(8,128)(2,1)}, u32[]{:S(2)}) copy-start(bf16[3,3,512,512]{3,2,1,0:T(8,128)(2,1)} %weight_ref.6) | copy-start | bytes 14155780
  4.0 2.6 %collective-permute-start.1 = (bf16[2,64,512]{2,1,0:T(8,128)(2,1)S(1)}, bf16[2,64,512]{2,1,0:T(8,128)(2,1)S(1)}, u32[]{:S(2)}, u32[]{:S(2)}) collective-permute-start(bf16[2,64,512]{2,1,0:T(8,128)(2,1)S(1)} %pad_maximum_fusion), channel_id=1, source_target_pairs={{1,4},{2,5},{3,6},{4,1},{5,2},{6,3},{9,12},{10,13},{11,14},{12,9},... | collective-permute-start | bytes 393224 | tf_op jit(solution)/shard_map/ppermute | solution.py:79
  6.6 6.9 %copy-start.3 = (s32[512]{0:T(512)S(1)}, s32[512]{0:T(512)}, u32[]{:S(2)}) copy-start(s32[512]{0:T(512)} %param.9) | copy-start | bytes 6148
  6.6 6.9 %collective-permute-start.2 = (bf16[2,64,512]{2,1,0:T(8,128)(2,1)S(1)}, bf16[2,64,512]{2,1,0:T(8,128)(2,1)S(1)}, u32[]{:S(2)}, u32[]{:S(2)}) collective-permute-start(bf16[2,64,512]{2,1,0:T(8,128)(2,1)S(1)} %collective-permute-done.1.halo_ref), channel_id=1, source_target_pairs={{0,4},{4,0},{1,5},{5,1},{2,6},{6,2},{3,7},{7,3},{8,12},{12,8},{9,1... | collective-permute-start | bytes 393224 | tf_op jit(solution)/shard_map/ppermute | solution.py:70
  13.6 25.1 %copy-start.4 = (f32[512]{0:T(512)S(1)}, f32[512]{0:T(512)}, u32[]{:S(2)}) copy-start(f32[512]{0:T(512)} %param.10) | copy-start | bytes 6148
  15.8 22.9 %copy-start.1 = (f32[32,16,512]{2,1,0:T(8,128)S(1)}, f32[32,16,512]{2,1,0:T(8,128)}, u32[]{:S(2)}) copy-start(f32[32,16,512]{2,1,0:T(8,128)} %start_ref.3) | copy-start | bytes 3145732
  28.6 12.6 %slice-start = ((s8[4718592]{0:T(1024)(128)(4,1)}), s8[4194304]{0:T(1024)(128)(4,1)S(1)}, s32[]{:S(2)}) async-start(s8[4718592]{0:T(1024)(128)(4,1)} %bitcast.4), calls=%async_computation.2 | async-start | bytes 8388608
  38.7 2.6 %slice-start.1 = ((s8[4718592]{0:T(1024)(128)(4,1)}), s8[524288]{0:T(1024)(128)(4,1)S(1)}, s32[]{:S(2)}) async-start(s8[4718592]{0:T(1024)(128)(4,1)} %bitcast.4), calls=%async_computation.3 | async-start | bytes 1048576
  39.1 1.4 %collective-permute-start.3 = (bf16[2,48,512]{2,1,0:T(8,128)(2,1)S(1)}, bf16[2,48,512]{2,1,0:T(8,128)(2,1)S(1)}, u32[]{:S(2)}, u32[]{:S(2)}) collective-permute-start(bf16[2,48,512]{2,1,0:T(8,128)(2,1)S(1)} %get-tuple-element.38), channel_id=1, source_target_pairs={{0,4},{4,0},{1,5},{5,1},{2,6},{6,2},{3,7},{7,3},{8,12},{12,8},{9,1... | collective-permute-start | bytes 294920 | tf_op jit(solution)/shard_map/ppermute | solution.py:70
  40.5 2.5 %collective-permute-start.4 = (bf16[2,64,512]{2,1,0:T(8,128)(2,1)S(1)}, bf16[2,64,512]{2,1,0:T(8,128)(2,1)S(1)}, u32[]{:S(2)}, u32[]{:S(2)}) collective-permute-start(bf16[2,64,512]{2,1,0:T(8,128)(2,1)S(1)} %pad_maximum_fusion.1), channel_id=1, source_target_pairs={{1,4},{2,5},{3,6},{4,1},{5,2},{6,3},{9,12},{10,13},{11,14},{12,9},... | collective-permute-start | bytes 393224 | tf_op jit(solution)/shard_map/ppermute | solution.py:79
  43.0 6.0 %collective-permute-start.5 = (bf16[2,64,512]{2,1,0:T(8,128)(2,1)S(1)}, bf16[2,64,512]{2,1,0:T(8,128)(2,1)S(1)}, u32[]{:S(2)}, u32[]{:S(2)}) collective-permute-start(bf16[2,64,512]{2,1,0:T(8,128)(2,1)S(1)} %collective-permute-done.4.halo_ref), channel_id=1, source_target_pairs={{0,4},{4,0},{1,5},{5,1},{2,6},{6,2},{3,7},{7,3},{8,12},{12,8},{9,1... | collective-permute-start | bytes 393224 | tf_op jit(solution)/shard_map/ppermute | solution.py:70

commit v5 on v0

v5 whole, which is shorter than its diff:
```python
import math

import jax
import jax.numpy as jnp
from jax import lax
from jax.experimental import pallas as pl
from jax.experimental.pallas import tpu as pltpu
from jax.sharding import PartitionSpec as P

NPOLES = 16
VMEM_LIMIT = 24 * 1024 * 1024
WHOLE = pl.BlockSpec(memory_space=pltpu.VMEM)
HBM = pl.BlockSpec(memory_space=pltpu.HBM)
LANES = 256


def call(kernel, out_shape, *args, scratch=(), flops=0, out_specs=None, aliases=None):
    outs = jax.tree.leaves(out_shape)
    moved = sum(leaf.size * leaf.dtype.itemsize for leaf in (*args, *outs))
    return pl.pallas_call(
        kernel,
        in_specs=[WHOLE] * len(args),
        out_specs=out_specs or jax.tree.map(lambda _: WHOLE, out_shape),
        out_shape=out_shape,
        scratch_shapes=scratch,
        input_output_aliases=aliases or {},
        compiler_params=pltpu.CompilerParams(vmem_limit_bytes=VMEM_LIMIT),
        cost_estimate=pl.CostEstimate(flops=flops, bytes_accessed=moved, transcendentals=0),
    )(*args)


def of(shape, dtype):
    return jax.ShapeDtypeStruct(shape, dtype)


def is_core(which):
    return (lax.axis_index("sx") == which).astype(jnp.float32)


def rate_of(pole_ref):
    pole = pole_ref[...].astype(jnp.float32)
    return -0.001 * jnp.exp(pole * (math.log(300.0) / (NPOLES - 1)))


def inner_row(rows):
    return jnp.where(lax.axis_index("sx") == 0, rows - 1, 0)


def swap_cores(array):
    return lax.ppermute(array, "sx", [(0, 1), (1, 0)])


def put_columns(index, left, right, give_ref, keep_ref):
    zero, one = is_core(0), is_core(1)
    count, rows, _ = keep_ref.shape
    at = give_ref.shape[0] - (count - index) * rows
    give_ref[at : at + rows] = (zero * right + one * left).astype(give_ref.dtype)
    keep_ref[index] = (zero * left + one * right).astype(keep_ref.dtype)


def edges_kernel(cells_ref, give_ref, keep_ref):
    count, rows, cols, _ = cells_ref.shape
    for frame in range(count):
        give_ref[frame * cols : (frame + 1) * cols] = cells_ref[frame, inner_row(rows)]
        tile = cells_ref[frame].astype(jnp.float32)
        for depth in range(2):
            left, right = tile[:, depth, :], tile[:, cols - 1 - depth, :]
            put_columns(2 * frame + depth, left, right, give_ref, keep_ref)


def start_edges_kernel(start_ref, _, __, give_ref, keep_ref):
    cols = start_ref.shape[1]
    tile = start_ref[...]
    index = keep_ref.shape[0] - 1
    put_columns(index, tile[:, 0, :], tile[:, cols - 1, :], give_ref, keep_ref)


def trade_columns(give, keep, at):
    chips = lax.axis_size("sy")
    got = swap_cores(give)
    pairs = [(chip, chips + chip - 1) for chip in range(1, chips)]
    pairs += [(after, before) for before, after in pairs]
    columns = jnp.concatenate([keep, got[at:].reshape(keep.shape)], axis=1)
    return got, lax.ppermute(columns, ("sx", "sy"), pairs)


def fill(lhs_ref, at, cells_ref, frame, row):
    _, rows, cols, channels = cells_ref.shape
    size = rows * cols
    row = row.astype(jnp.float32)
    cells = cells_ref[frame].reshape(size, channels)
    mid, low = slice(channels, 2 * channels), slice(2 * channels, 3 * channels)
    lhs_ref[at : at + cols, :channels] = (is_core(1) * row).astype(lhs_ref.dtype)
    lhs_ref[at + cols : at + size, :channels] = cells[: size - cols]
    lhs_ref[at : at + size, mid] = cells
    lhs_ref[at : at + size - cols, low] = cells[cols:]
    lhs_ref[at + size - cols : at + size, low] = (is_core(0) * row).astype(lhs_ref.dtype)


def row_taps(column, above, below):
    rows = column.shape[0]
    row = lax.broadcasted_iota(jnp.int32, column.shape, 0)
    up = jnp.where(row == 0, is_core(1) * above, pltpu.roll(column, 1, 0))
    down = jnp.where(row == rows - 1, is_core(0) * below, pltpu.roll(column, rows - 1, 0))
    return jnp.concatenate([up, column, down], axis=1)


def dot(lhs, weight_ref, column, lanes):
    weight = weight_ref[:, column, :, lanes].reshape(lhs.shape[1], -1)
    return jnp.dot(lhs, weight, preferred_element_type=jnp.float32)


def main_kernel(cells_ref, got_ref, weight_ref, total_ref, spill_ref, lhs_ref):
    count, rows, cols, _ = cells_ref.shape
    size = rows * cols
    for frame in range(count):
        fill(lhs_ref, frame * size, cells_ref, frame, got_ref[frame * cols : (frame + 1) * cols])
    tile = (count, rows, cols, LANES)
    col = lax.broadcasted_iota(jnp.int32, tile, 2)
    for lane in range(0, weight_ref.shape[-1], LANES):
        lanes = slice(lane, lane + LANES)
        total = dot(lhs_ref[...], weight_ref, 1, lanes).reshape(tile)
        first = dot(lhs_ref[...], weight_ref, 0, lanes).reshape(tile)
        spill_ref[1, :, lanes] = first[:, :, cols - 1, :].reshape(count * rows, LANES)
        total += jnp.where(col == 0, 0.0, pltpu.roll(first, 1, 2))
        last = dot(lhs_ref[...], weight_ref, 2, lanes).reshape(tile)
        spill_ref[0, :, lanes] = last[:, :, 0, :].reshape(count * rows, LANES)
        total_ref[:, :, :, lanes] = total + jnp.where(
            col == cols - 1, 0.0, pltpu.roll(last, cols - 1, 2)
        )


def drive_kernel(
    mine_ref, theirs_ref, weight_ref, total_ref, spill_ref, pole_ref,
    drive_ref, beside_ref, end_ref, start_ref, lhs_ref,
):
    count, rows, cols, _ = total_ref.shape
    room = count * rows
    zero, one = is_core(0), is_core(1)
    core = lax.axis_index("sx")
    slots = ((1, 0), (2, 3))
    for frame in range(count):
        for depth in range(2):
            own = mine_ref[2 * frame + depth].astype(jnp.float32)
            other = theirs_ref[2 * frame + depth].astype(jnp.float32)
            own = row_taps(own[rows:], own[rows - 1 : rows], own[:1])
            other = row_taps(other[:rows], other[2 * rows - 1 :], other[rows : rows + 1])
            for swapped, taps in enumerate((own, other)):
                slot = jnp.where(core == swapped, slots[0][depth], slots[1][depth])
                at = pl.multiple_of(slot * room + frame * rows, rows)
                lhs_ref[pl.ds(at, rows)] = taps.astype(lhs_ref.dtype)
    own = mine_ref[2 * count, rows:].astype(jnp.float32)
    other = theirs_ref[2 * count, :rows].astype(jnp.float32)
    start_ref[:rows] = zero * own + one * other
    start_ref[rows:] = zero * other + one * own

    decay = jnp.exp(rate_of(pole_ref))
    tile = (count, rows, cols, LANES)
    col = lax.broadcasted_iota(jnp.int32, tile, 2)
    for lane in range(0, weight_ref.shape[-1], LANES):
        lanes = slice(lane, lane + LANES)
        first = dot(lhs_ref[: 2 * room], weight_ref, 0, lanes)
        middle = dot(lhs_ref[room : 3 * room], weight_ref, 1, lanes)
        last = dot(lhs_ref[2 * room :], weight_ref, 2, lanes)
        left = (spill_ref[0, :, lanes] + first[:room] + middle[:room]).reshape(count, rows, LANES)
        right = (spill_ref[1, :, lanes] + middle[room:] + last[room:]).reshape(count, rows, LANES)
        near = first[room:].reshape(count, rows, 1, LANES)
        total = total_ref[:, :, :, lanes] + jnp.where(col == 0, near, 0.0)
        near = last[:room].reshape(count, rows, 1, LANES)
        total += jnp.where(col == cols - 1, near, 0.0)
        drive_ref[:, :, :, lanes] = total
        beside_ref[:, :rows, lanes] = left
        beside_ref[:, rows:, lanes] = right
        state, left_state, right_state = total[0], left[0], right[0]
        for frame in range(1, count):
            state = decay[:, lanes] * state + total[frame]
            left_state = decay[:, lanes] * left_state + left[frame]
            right_state = decay[:, lanes] * right_state + right[frame]
        size = rows * cols
        end_ref[:size, lanes] = state.reshape(size, LANES).astype(end_ref.dtype)
        end_ref[size : size + rows, lanes] = left_state.astype(end_ref.dtype)
        end_ref[size + rows :, lanes] = right_state.astype(end_ref.dtype)


def entry_kernel(frames, ends_ref, pole_ref, out_ref):
    carried = jnp.exp(frames * rate_of(pole_ref))
    entry = jnp.zeros(ends_ref.shape[1:], jnp.float32)
    out_ref[0] = entry.astype(out_ref.dtype)
    for index in range(ends_ref.shape[0] - 1):
        entry = carried * entry + ends_ref[index].astype(jnp.float32)
        out_ref[index + 1] = entry.astype(out_ref.dtype)


def activated(drives, entry, start, pole_ref, scale_ref):
    rate = rate_of(pole_ref)
    decay = jnp.exp(rate)
    reach = jnp.exp((len(drives) * lax.axis_index("tm")).astype(jnp.float32) * rate)
    state = reach * start + entry.astype(jnp.float32)
    for drive in drives:
        state = decay * state + drive
        yield jax.nn.gelu(scale_ref[...] * state)


def beside_kernel(
    drive_ref, beside_ref, entry_ref, start_ref, sides_ref, pole_ref, scale_ref, give_ref, out_ref
):
    count, rows, cols, channels = drive_ref.shape
    size = rows * cols
    inner = inner_row(rows)
    at = pl.multiple_of(inner * cols, cols)
    chip, chips = lax.axis_index("sy"), lax.axis_size("sy")
    row = lax.broadcasted_iota(jnp.int32, (2 * rows, channels), 0)
    side = jnp.where(row < rows, (chip > 0).astype(jnp.float32), (chip < chips - 1).astype(jnp.float32))
    beside = activated(
        [beside_ref[frame] for frame in range(count)],
        entry_ref[size:],
        sides_ref[...],
        pole_ref,
        scale_ref,
    )
    tile = activated(
        [drive_ref[frame, inner] for frame in range(count)],
        entry_ref[pl.ds(at, cols)],
        start_ref[inner],
        pole_ref,
        scale_ref,
    )
    zero, one = is_core(0), is_core(1)
    for frame, (cells, mixed) in enumerate(zip(tile, beside)):
        mixed = side * mixed
        out_ref[frame] = mixed.astype(out_ref.dtype)
        give_ref[frame, :cols] = cells.astype(give_ref.dtype)
        left = zero * mixed[rows - 1 : rows] + one * mixed[:1]
        right = zero * mixed[2 * rows - 1 :] + one * mixed[rows : rows + 1]
        which = lax.broadcasted_iota(jnp.int32, (cols, channels), 0)
        ends = jnp.where(which == 0, left, right)
        give_ref[frame, cols:] = ends.astype(give_ref.dtype)


def mixed_kernel(drive_ref, entry_ref, start_ref, pole_ref, scale_ref, out_ref):
    count, rows, cols, channels = drive_ref.shape
    block = 8
    for row in range(0, rows, block):
        here = slice(row, row + block)
        drives = [drive_ref[frame, here] for frame in range(count)]
        entry = entry_ref[row * cols : (row + block) * cols].reshape(block, cols, channels)
        mixed = activated(drives, entry, start_ref[here], pole_ref, scale_ref)
        for frame, tile in enumerate(mixed):
            out_ref[frame, here] = tile.astype(out_ref.dtype)


def result_kernel(cells_ref, got_ref, beside_ref, weight_ref, out_ref, lhs_ref, held_ref, sems):
    count, rows, cols, _ = cells_ref.shape
    size, room = rows * cols, count * rows
    for frame in range(count):
        fill(lhs_ref, room + frame * size, cells_ref, frame, got_ref[frame, :cols])
        ends = got_ref[frame, cols:].astype(jnp.float32)
        beside = beside_ref[frame].astype(jnp.float32)
        for side, at in enumerate((0, room + count * size)):
            column, end = beside[side * rows : (side + 1) * rows], ends[side : side + 1]
            here = slice(at + frame * rows, at + (frame + 1) * rows)
            lhs_ref[here] = row_taps(column, end, end).astype(lhs_ref.dtype)

    def store(lanes):
        return pltpu.make_async_copy(
            held_ref.at[:, :, :, lanes],
            out_ref.at[:, :, :, lanes],
            sems.at[lanes.start // LANES],
        )

    inner = count * size
    tile = (count, rows, cols, LANES)
    col = lax.broadcasted_iota(jnp.int32, tile, 2)
    for lane in range(0, weight_ref.shape[-1], LANES):
        lanes = slice(lane, lane + LANES)
        total = dot(lhs_ref[room : room + inner], weight_ref, 1, lanes).reshape(tile)
        first = dot(lhs_ref[: room + inner], weight_ref, 0, lanes)
        halo = first[:room].reshape(count, rows, 1, LANES)
        total += jnp.where(col == 0, halo, pltpu.roll(first[room:].reshape(tile), 1, 2))
        last = dot(lhs_ref[room:], weight_ref, 2, lanes)
        halo = last[inner:].reshape(count, rows, 1, LANES)
        total += jnp.where(
            col == cols - 1, halo, pltpu.roll(last[:inner].reshape(tile), cols - 1, 2)
        )
        held_ref[:, :, :, lanes] = total.astype(held_ref.dtype)
        store(lanes).start()
    for lane in range(0, weight_ref.shape[-1], LANES):
        store(slice(lane, lane + LANES)).wait()


def on_device(frames, input_weight, output_weight, pole_index, gelu_scale, start_state):
    count, rows, cols, channels = frames.shape
    size, room = rows * cols, count * rows
    wide = 3 * channels
    groups = lax.axis_size("tm")
    assert lax.axis_size("sx") == 2
    narrow = frames.dtype
    pole, scale = pole_index[None], gelu_scale[None]

    shapes = (
        of((count * cols + (2 * count + 1) * rows, channels), narrow),
        of((2 * count + 1, rows, channels), narrow),
    )
    edges = call(edges_kernel, shapes, frames, flops=2000000000)
    give, keep = call(start_edges_kernel, shapes, start_state, *edges, aliases={1: 0, 2: 1})
    got, mine = trade_columns(give, keep, count * cols)
    main = call(
        main_kernel,
        (of(frames.shape, jnp.float32), of((2, room, channels), jnp.float32)),
        frames,
        got,
        input_weight,
        scratch=[pltpu.VMEM((count * size, wide), narrow)],
        flops=18 * frames.size * channels,
    )
    mine, (total, spill) = lax.optimization_barrier((mine, main))
    drive, beside, end, sides = call(
        drive_kernel,
        (
            of(frames.shape, jnp.float32),
            of((count, 2 * rows, channels), jnp.float32),
            of((size + 2 * rows, channels), narrow),
            of((2 * rows, channels), jnp.float32),
        ),
        mine,
        swap_cores(mine),
        input_weight,
        total,
        spill,
        pole,
        scratch=[pltpu.VMEM((4 * room, wide), narrow)],
        flops=36 * room * channels * channels,
    )

    ends = lax.all_to_all(end.reshape(groups, -1, channels), "tm", 0, 0)
    entries = call(
        lambda *refs: entry_kernel(count, *refs), of(ends.shape, narrow), ends, pole
    )
    entry = lax.all_to_all(entries, "tm", 0, 0).reshape(end.shape)

    give, beside = call(
        beside_kernel,
        (of((count, 2 * cols, channels), narrow), of(beside.shape, narrow)),
        drive,
        beside,
        entry,
        start_state,
        sides,
        pole,
        scale,
    )
    got = swap_cores(give)
    mixed = call(mixed_kernel, of(frames.shape, narrow), drive, entry, start_state, pole, scale)
    return call(
        result_kernel,
        of(frames.shape, narrow),
        mixed,
        got,
        beside,
        output_weight,
        out_specs=HBM,
        scratch=[
            pltpu.VMEM((count * size + 2 * room, wide), narrow),
            pltpu.VMEM(frames.shape, narrow),
            pltpu.SemaphoreType.DMA((channels // LANES,)),
        ],
        flops=18 * frames.size * channels,
    )


def solution(mesh):
    return jax.shard_map(
        on_device,
        mesh=mesh,
        in_specs=(P("tm", "sx", "sy", None), P(), P(), P(), P(), P("sx", "sy", None)),
        out_specs=P("tm", "sx", "sy", None),
        check_vma=False,
    )
```

time: 128 us -> 50.2 us (0.39)
  waiting for transfers between devices: 53.5 us -> 2.53 us
  matrix products: 17 us -> 0 us
  blocking collectives: 8.07 us -> 25 us
  Pallas kernels: 0 us -> 15.2 us
  other arithmetic: 14.1 us -> 0.02 us
  between operations: 13.8 us -> 0.12 us
  starting transfers between devices: 17.7 us -> 5.62 us
  local copies, waits for them, and re-layouts: 2.8 us -> 1.41 us
    all_gather x1 -> x0, waiting for transfers between devices: 45 us -> none  [on_device(): lax.all_gather(state[None], 'tm', axis=0, tiled=True)]
    all_to_all x0 -> x2, blocking collectives: none -> 25 us  [the longest x1 13.5 us: on_device(): ends = lax.all_to_all(end.reshape(groups, -1, channels), 'tm', 0, 0)]
    dot_general x18 -> x0, matrix products: 17 us -> none  [convolve_tile(): jnp.dot(window, weight[row_shift, col_shift], preferred_element_type=jnp....]
    pallas_call x0 -> x8, Pallas kernels: none -> 15.2 us  [call(): pl.pallas_call(kernel, in_specs=[WHOLE] * len(args), out_specs=out_specs...]
    ppermute x8 -> x4, starting transfers between devices: 17.7 us -> 5.62 us  [the longest x3 4.94 us: swap_cores(): return lax.ppermute(array, 'sx', [(0, 1), (1, 0)])]
    all_gather x1 -> x0, blocking collectives: 8.07 us -> none  [on_device(): lax.all_gather(carried[None], 'tm', axis=0, tiled=True)]
    select_n x4 -> x0, other arithmetic: 6.81 us -> none  [fold_step(): return jnp.where(index < position, updated, current)]
    ppermute x8 -> x4, waiting for transfers between devices: 8.49 us -> 2.53 us  [the longest x3 2.53 us: swap_cores(): return lax.ppermute(array, 'sx', [(0, 1), (1, 0)])]
  transfers between devices with their start and end apart: 9 -> 4, of which waited for: 4 -> 3; matrix products, arithmetic and copies ran while one was open for 5% -> 0% of each run, Pallas kernels for 0% -> 12%
where the time goes in v5:
time: 50.2 us; the launch traced here: 50 us
  blocking collectives  25 us (50%)
  Pallas kernels  15.2 us (30%)
  starting transfers between devices  5.62 us (11%)
  waiting for transfers between devices  2.53 us (5%)
  local copies, waits for them, and re-layouts  1.41 us (3%)
    pallas_call x8, Pallas kernels, call(): pl.pallas_call(kernel, in_specs=[WHOLE] * len(args), out_specs=out_specs...  15.2 us
    all_to_all x1, blocking collectives, on_device(): ends = lax.all_to_all(end.reshape(groups, -1, channels), 'tm', 0, 0)  13.5 us
    all_to_all x1, blocking collectives, on_device(): entry = lax.all_to_all(entries, 'tm', 0, 0).reshape(end.shape)  11.6 us
    ppermute x3, starting transfers between devices, swap_cores(): return lax.ppermute(array, 'sx', [(0, 1), (1, 0)])  4.94 us
    ppermute x3, waiting for transfers between devices, swap_cores(): return lax.ppermute(array, 'sx', [(0, 1), (1, 0)])  2.53 us
    unnamed x14, local copies, waits for them, and re-layouts  1.4 us
  transfers between devices with their start and end apart: 4, of which 3 were waited for; matrix products, arithmetic and copies ran while one was open for 0% of the time, Pallas kernels for 12%

profile of v5, /device:TPU:0, one launch (start us, length us, event | category | flops | bytes accessed | tf_op | source)
XLA Modules:
  0.0 50.0 jit_solution(9638260023956333048)
XLA Ops:
  0.0 0.0 copy-start
  0.0 0.0 copy-start.1
  0.0 0.0 copy-start.4
  0.0 1.4 %copy-done.4 = bf16[2,32,16,512]{3,2,1,0:T(8,128)(2,1)S(1)} copy-done((bf16[2,32,16,512]{3,2,1,0:T(8,128)(2,1)S(1)}, bf16[2,32,16,512]{3,2,1,0:T(8,128)(2,1)}, u32[]{:S(2)}) %copy-start.4) | copy-done | bytes 1048600
  1.4 1.1 %shard_map.64 = (bf16[192,512]{1,0:T(8,128)(2,1)S(1)}, bf16[5,32,512]{2,1,0:T(8,128)(2,1)S(1)}) custom-call(bf16[2,32,16,512]{3,2,1,0:T(8,128)(2,1)S(1)} %copy-done.4), custom_call_target="tpu_custom_call" | custom-call | flops 2000000000 | bytes 1409024 | tf_op jit(solution)/shard_map/pallas_call | solution.py:20
  2.5 0.0 copy-done
  2.5 0.3 shard_map.65
  2.8 0.5 %collective-permute-start = (bf16[192,512]{1,0:T(8,128)(2,1)S(1)}, bf16[192,512]{1,0:T(8,128)(2,1)S(1)}, u32[]{:S(2)}, u32[]{:S(2)}) collective-permute-start(bf16[192,512]{1,0:T(8,128)(2,1)S(1)} %get-tuple-element.23), channel_id=1, source_target_pairs={{0,4},{4,0},{1,5},{5,1},{2,6},{6,2},{3,7},{7,3},{8,12},{12,8},{9,1... | collective-permute-start | bytes 589832 | tf_op jit(solution)/shard_map/ppermute | solution.py:50
  3.3 1.1 %collective-permute-done.got_ref = bf16[192,512]{1,0:T(8,128)(2,1)S(1)} collective-permute-done((bf16[192,512]{1,0:T(8,128)(2,1)S(1)}, bf16[192,512]{1,0:T(8,128)(2,1)S(1)}, u32[]{:S(2)}, u32[]{:S(2)}) %collective-permute-start) | collective-permute-done | bytes 196640 | tf_op jit(solution)/shard_map/ppermute | solution.py:50
  4.4 0.0 copy-start.2
  4.4 0.7 %collective-permute-start.1 = (bf16[5,64,512]{2,1,0:T(8,128)(2,1)S(1)}, bf16[5,64,512]{2,1,0:T(8,128)(2,1)S(1)}, u32[]{:S(2)}, u32[]{:S(2)}) collective-permute-start(bf16[5,64,512]{2,1,0:T(8,128)(2,1)S(1)} %pad_maximum_fusion), channel_id=1, source_target_pairs={{1,4},{2,5},{3,6},{4,1},{5,2},{6,3},{9,12},{10,13},{11,14},{12,9},... | collective-permute-start | bytes 983048 | tf_op jit(solution)/shard_map/ppermute | solution.py:84
  5.1 0.0 copy-done.1
  5.1 5.1 %shard_map.66 = (f32[2,32,16,512]{3,2,1,0:T(8,128)S(1)}, f32[2,64,512]{2,1,0:T(8,128)S(1)}) custom-call(bf16[2,32,16,512]{3,2,1,0:T(8,128)(2,1)S(1)} %copy-done.4, bf16[192,512]{1,0:T(8,128)(2,1)S(1)} %collective-permute-done.got_ref, bf16[3,3,512,512]{3,2,1,0:T(8,128)(2,1)S(1)} %copy-done.1), custom_call_target="tpu_custom_call" | custom-call | flops 4831838208 | bytes 8323072 | tf_op jit(solution)/shard_map/pallas_call | solution.py:20
  10.2 0.0 collective-permute-done.1.mine_ref
  10.2 4.4 %collective-permute-start.2 = (bf16[5,64,512]{2,1,0:T(8,128)(2,1)S(1)}, bf16[5,64,512]{2,1,0:T(8,128)(2,1)S(1)}, u32[]{:S(2)}, u32[]{:S(2)}) collective-permute-start(bf16[5,64,512]{2,1,0:T(8,128)(2,1)S(1)} %collective-permute-done.1.mine_ref), channel_id=1, source_target_pairs={{0,4},{4,0},{1,5},{5,1},{2,6},{6,2},{3,7},{7,3},{8,12},{12,8},{9,1... | collective-permute-start | bytes 983048 | tf_op jit(solution)/shard_map/ppermute | solution.py:50
  14.5 1.3 %collective-permute-done.2.theirs_ref = bf16[5,64,512]{2,1,0:T(8,128)(2,1)S(1)} collective-permute-done((bf16[5,64,512]{2,1,0:T(8,128)(2,1)S(1)}, bf16[5,64,512]{2,1,0:T(8,128)(2,1)S(1)}, u32[]{:S(2)}, u32[]{:S(2)}) %collective-permute-start.2) | collective-permute-done | bytes 327712 | tf_op jit(solution)/shard_map/ppermute | solution.py:50
  15.8 0.0 copy-done.2
  15.8 0.0 copy-start.3
  15.8 1.3 %shard_map.67 = (f32[2,32,16,512]{3,2,1,0:T(8,128)S(1)}, f32[2,64,512]{2,1,0:T(8,128)S(1)}, bf16[576,512]{1,0:T(8,128)(2,1)S(1)}, f32[64,512]{1,0:T(8,128)S(1)}) custom-call(bf16[5,64,512]{2,1,0:T(8,128)(2,1)S(1)} %collective-permute-done.1.mine_ref, bf16[5,64,512]{2,1,0:T(8,128)(2,1)S(1)} %collective-permute-done.2.theirs_ref, ...), custom_call_target="tpu_custom_call" | custom-call | flops 603979776 | bytes 10815488 | tf_op jit(solution)/shard_map/pallas_call | solution.py:20
  17.1 13.5 %all_to_all.10.refs_0_ = bf16[4,144,512]{2,1,0:T(8,128)(2,1)S(1)} all-to-all(bf16[4,144,512]{2,1,0:T(8,128)(2,1)S(1)} %bitcast.7), channel_id=1, replica_groups=mesh['tm'=4,'sx'=2,'sy'=4] {'tm'}, dimensions={0} | all-to-all | bytes 1179648 | tf_op jit(solution)/shard_map/all_to_all | solution.py:335
  30.5 0.1 shard_map.68
  30.7 0.0 slice-start
  30.7 11.6 %all_to_all.11 = bf16[4,144,512]{2,1,0:T(8,128)(2,1)S(1)} all-to-all(bf16[4,144,512]{2,1,0:T(8,128)(2,1)S(1)} %shard_map.68), channel_id=1, replica_groups=mesh['tm'=4,'sx'=2,'sy'=4] {'tm'}, dimensions={0} | all-to-all | bytes 1179648 | tf_op jit(solution)/shard_map/all_to_all | solution.py:339
  42.2 0.0 copy-done.3
  42.2 0.0 slice-start.1
  42.2 0.2 shard_map.70
  42.4 0.1 collective-permute-start.3
  42.5 1.0 %shard_map.69.cells_ref = bf16[2,32,16,512]{3,2,1,0:T(8,128)(2,1)S(1)} custom-call(f32[2,32,16,512]{3,2,1,0:T(8,128)S(1)} %get-tuple-element.29.drive_ref, bf16[576,512]{1,0:T(8,128)(2,1)S(1)} %bitcast.6, f32[32,16,512]{2,1,0:T(8,128)S(1)} %copy-done, s32[1,512]{1,0:T(1,128)S(1)} %bitcast.11, f32[1,512]{1,0:T(1,128)S(1)} %bitcast.13), custom_call_target="tpu_custom_call" | custom-call | bytes 4788224 | tf_op jit(solution)/shard_map/pallas_call | solution.py:20
  43.6 0.2 collective-permute-done.3.got_ref
  43.8 0.0 slice-done
  43.8 0.0 slice-done.1
  43.8 6.2 %shard_map.71 = bf16[2,32,16,512]{3,2,1,0:T(8,128)(2,1)} custom-call(bf16[2,32,16,512]{3,2,1,0:T(8,128)(2,1)S(1)} %shard_map.69.cells_ref, bf16[2,32,512]{2,1,0:T(8,128)(2,1)S(1)} %collective-permute-done.3.got_ref, bf16[2,64,512]{2,1,0:T(8,128)(2,1)S(1)} %get-tuple-element.34.beside_ref, bf16[3,3,512,512]{3,2,1,0:T(8,128)(2,1)S(1)} %bitcast.15), custom_call_target="tpu_custom_call" | custom-call | flops 4831838208 | bytes 7012352 | tf_op jit(solution)/shard_map/pallas_call | solution.py:20
  (3 shorter events, 0.0 us)
Async XLA Ops:
  0.0 2.5 %copy-start = (f32[32,16,512]{2,1,0:T(8,128)S(1)}, f32[32,16,512]{2,1,0:T(8,128)}, u32[]{:S(2)}) copy-start(f32[32,16,512]{2,1,0:T(8,128)} %start_ref.5) | copy-start | bytes 3145732
  0.0 5.1 %copy-start.1 = (bf16[3,3,512,512]{3,2,1,0:T(8,128)(2,1)S(1)}, bf16[3,3,512,512]{3,2,1,0:T(8,128)(2,1)}, u32[]{:S(2)}) copy-start(bf16[3,3,512,512]{3,2,1,0:T(8,128)(2,1)} %weight_ref.4) | copy-start | bytes 14155780
  0.0 1.4 %copy-start.4 = (bf16[2,32,16,512]{3,2,1,0:T(8,128)(2,1)S(1)}, bf16[2,32,16,512]{3,2,1,0:T(8,128)(2,1)}, u32[]{:S(2)}) copy-start(bf16[2,32,16,512]{3,2,1,0:T(8,128)(2,1)} %cells_ref.3) | copy-start | bytes 3145732
  2.8 1.6 %collective-permute-start = (bf16[192,512]{1,0:T(8,128)(2,1)S(1)}, bf16[192,512]{1,0:T(8,128)(2,1)S(1)}, u32[]{:S(2)}, u32[]{:S(2)}) collective-permute-start(bf16[192,512]{1,0:T(8,128)(2,1)S(1)} %get-tuple-element.23), channel_id=1, source_target_pairs={{0,4},{4,0},{1,5},{5,1},{2,6},{6,2},{3,7},{7,3},{8,12},{12,8},{9,1... | collective-permute-start | bytes 589832 | tf_op jit(solution)/shard_map/ppermute | solution.py:50
  4.4 11.4 %copy-start.2 = (s32[512]{0:T(512)S(1)}, s32[512]{0:T(512)}, u32[]{:S(2)}) copy-start(s32[512]{0:T(512)} %param.9) | copy-start | bytes 6148
  4.4 5.8 %collective-permute-start.1 = (bf16[5,64,512]{2,1,0:T(8,128)(2,1)S(1)}, bf16[5,64,512]{2,1,0:T(8,128)(2,1)S(1)}, u32[]{:S(2)}, u32[]{:S(2)}) collective-permute-start(bf16[5,64,512]{2,1,0:T(8,128)(2,1)S(1)} %pad_maximum_fusion), channel_id=1, source_target_pairs={{1,4},{2,5},{3,6},{4,1},{5,2},{6,3},{9,12},{10,13},{11,14},{12,9},... | collective-permute-start | bytes 983048 | tf_op jit(solution)/shard_map/ppermute | solution.py:84
  10.2 5.6 %collective-permute-start.2 = (bf16[5,64,512]{2,1,0:T(8,128)(2,1)S(1)}, bf16[5,64,512]{2,1,0:T(8,128)(2,1)S(1)}, u32[]{:S(2)}, u32[]{:S(2)}) collective-permute-start(bf16[5,64,512]{2,1,0:T(8,128)(2,1)S(1)} %collective-permute-done.1.mine_ref), channel_id=1, source_target_pairs={{0,4},{4,0},{1,5},{5,1},{2,6},{6,2},{3,7},{7,3},{8,12},{12,8},{9,1... | collective-permute-start | bytes 983048 | tf_op jit(solution)/shard_map/ppermute | solution.py:50
  15.8 26.4 %copy-start.3 = (f32[512]{0:T(512)S(1)}, f32[512]{0:T(512)}, u32[]{:S(2)}) copy-start(f32[512]{0:T(512)} %param.10) | copy-start | bytes 6148
  30.7 13.1 %slice-start = ((s8[4718592]{0:T(1024)(128)(4,1)}), s8[4194304]{0:T(1024)(128)(4,1)S(1)}, s32[]{:S(2)}) async-start(s8[4718592]{0:T(1024)(128)(4,1)} %bitcast.14), calls=%async_computation.2 | async-start | bytes 8388608
  42.2 1.5 %slice-start.1 = ((s8[4718592]{0:T(1024)(128)(4,1)}), s8[524288]{0:T(1024)(128)(4,1)S(1)}, s32[]{:S(2)}) async-start(s8[4718592]{0:T(1024)(128)(4,1)} %bitcast.14), calls=%async_computation.3 | async-start | bytes 1048576
  42.4 1.3 %collective-permute-start.3 = (bf16[2,32,512]{2,1,0:T(8,128)(2,1)S(1)}, bf16[2,32,512]{2,1,0:T(8,128)(2,1)S(1)}, u32[]{:S(2)}, u32[]{:S(2)}) collective-permute-start(bf16[2,32,512]{2,1,0:T(8,128)(2,1)S(1)} %get-tuple-element.33), channel_id=1, source_target_pairs={{0,4},{4,0},{1,5},{5,1},{2,6},{6,2},{3,7},{7,3},{8,12},{12,8},{9,1... | collective-permute-start | bytes 196616 | tf_op jit(solution)/shard_map/ppermute | solution.py:50

commit v6 on v5

--- a/solution.py
+++ b/solution.py
@@ -1,3 +1,4 @@
+import functools
 import math
 
 import jax
@@ -12,6 +13,7 @@
 WHOLE = pl.BlockSpec(memory_space=pltpu.VMEM)
 HBM = pl.BlockSpec(memory_space=pltpu.HBM)
 LANES = 256
+EDGES_COST = 2_000_000_000
 
 
 def call(kernel, out_shape, *args, scratch=(), flops=0, out_specs=None, aliases=None):
@@ -58,19 +60,29 @@
     keep_ref[index] = (zero * left + one * right).astype(keep_ref.dtype)
 
 
-def edges_kernel(cells_ref, give_ref, keep_ref):
-    count, rows, cols, _ = cells_ref.shape
+def edges_kernel(cells_ref, give_ref, keep_ref, wide_ref):
+    count, rows, cols, channels = cells_ref.shape
     for frame in range(count):
         give_ref[frame * cols : (frame + 1) * cols] = cells_ref[frame, inner_row(rows)]
-        tile = cells_ref[frame].astype(jnp.float32)
+        tile = cells_ref[frame].reshape(rows * cols, channels).astype(jnp.float32)
+        lanes = wide_ref.shape[-1]
+        for part in range(channels // lanes):
+            wide_ref[frame, part] = tile[:, part * lanes : (part + 1) * lanes]
+
+        def column(col):
+            parts = [
+                wide_ref[frame, part, pl.ds(col, rows, stride=cols), :]
+                for part in range(channels // lanes)
+            ]
+            return jnp.concatenate(parts, axis=1)
+
         for depth in range(2):
-            left, right = tile[:, depth, :], tile[:, cols - 1 - depth, :]
+            left, right = column(depth), column(cols - 1 - depth)
             put_columns(2 * frame + depth, left, right, give_ref, keep_ref)
 
 
 def start_edges_kernel(start_ref, _, __, give_ref, keep_ref):
-    cols = start_ref.shape[1]
-    tile = start_ref[...]
+    tile, cols = start_ref[...], start_ref.shape[1]
     index = keep_ref.shape[0] - 1
     put_columns(index, tile[:, 0, :], tile[:, cols - 1, :], give_ref, keep_ref)
 
@@ -132,10 +144,11 @@
 
 def drive_kernel(
     mine_ref, theirs_ref, weight_ref, total_ref, spill_ref, pole_ref,
-    drive_ref, beside_ref, end_ref, start_ref, lhs_ref,
+    drive_ref, beside_ref, start_ref, *more_refs,
 ):
     count, rows, cols, _ = total_ref.shape
     room = count * rows
+    *end_refs, lhs_ref = more_refs
     zero, one = is_core(0), is_core(1)
     core = lax.axis_index("sx")
     slots = ((1, 0), (2, 3))
@@ -177,9 +190,10 @@
             left_state = decay[:, lanes] * left_state + left[frame]
             right_state = decay[:, lanes] * right_state + right[frame]
         size = rows * cols
-        end_ref[:size, lanes] = state.reshape(size, LANES).astype(end_ref.dtype)
-        end_ref[size : size + rows, lanes] = left_state.astype(end_ref.dtype)
-        end_ref[size + rows :, lanes] = right_state.astype(end_ref.dtype)
+        end_ref = end_refs[lane // LANES]
+        end_ref[:size] = state.reshape(size, LANES).astype(end_ref.dtype)
+        end_ref[size : size + rows] = left_state.astype(end_ref.dtype)
+        end_ref[size + rows :] = right_state.astype(end_ref.dtype)
 
 
 def entry_kernel(frames, ends_ref, pole_ref, out_ref):
@@ -189,6 +203,83 @@
     for index in range(ends_ref.shape[0] - 1):
         entry = carried * entry + ends_ref[index].astype(jnp.float32)
         out_ref[index + 1] = entry.astype(out_ref.dtype)
+
+
+def exchange(ends, pole, frames):
+    groups = lax.axis_size("tm")
+    end = jnp.concatenate(ends, axis=1)
+    shares = lax.all_to_all(end.reshape(groups, -1, end.shape[1]), "tm", 0, 0)
+    entries = call(
+        functools.partial(entry_kernel, frames), of(shares.shape, end.dtype), shares, pole
+    )
+    return lax.all_to_all(entries, "tm", 0, 0).reshape(end.shape)
+
+
+def pick(values):
+    group = lax.axis_index("tm")
+    picked = values[-1]
+    for index, value in enumerate(values[:-1]):
+        picked = jnp.where(group == index, value, picked)
+    return picked
+
+
+def on_core(first, second):
+    return jnp.where(lax.axis_index("sx") == 0, first, second)
+
+
+def weigh(one, by_one, other, by_other):
+    return by_one * one[...].astype(jnp.float32) + by_other * other[...].astype(jnp.float32)
+
+
+def relay_kernel(frames, part, end_ref, got_ref, pole_ref, out_ref):
+    rate = rate_of(pole_ref)[:, part * LANES : (part + 1) * LANES]
+    carried, twice = jnp.exp(frames * rate), jnp.exp(2 * frames * rate)
+    none, same = jnp.zeros_like(rate), jnp.ones_like(rate)
+    own = on_core(pick([carried, same, same, same]), pick([same, same, same, none]))
+    got = on_core(pick([same, carried, carried, carried]), pick([none, none, twice, same]))
+    out_ref[...] = weigh(end_ref, own, got_ref, got).astype(out_ref.dtype)
+
+
+def arrived_kernel(frames, parts, *refs):
+    *got_refs, pole_ref, out_ref = refs
+    rate = rate_of(pole_ref)
+    carried = jnp.exp(frames * rate)
+    none, same = jnp.zeros_like(rate), jnp.ones_like(rate)
+    early = on_core(pick([none, same, none, same]), pick([none, none, carried, carried]))
+    late = on_core(pick([none, none, same, carried]), pick([none, same, same, same]))
+    for part in range(parts):
+        lanes = slice(part * LANES, (part + 1) * LANES)
+        first, second = got_refs[part], got_refs[parts + part]
+        out_ref[:, lanes] = weigh(first, early[:, lanes], second, late[:, lanes])
+
+
+def exchange_four(ends, pole, frames):
+    def along(pairs, core):
+        return [(2 * source + core, 2 * target + core) for source, target in pairs]
+
+    axes = ("tm", "sx")
+    down = [(0, 2), (1, 3)]
+    first_round = along([(0, 1), (1, 0), (2, 3)], 0) + along(down, 1)
+    second_round = along(down, 0) + along([(0, 1), (2, 3), (3, 2)], 1)
+    got = [lax.ppermute(end, axes, first_round) for end in ends]
+    relayed = [
+        call(
+            functools.partial(relay_kernel, frames, part),
+            of(end.shape, end.dtype),
+            end,
+            here,
+            pole,
+        )
+        for part, (end, here) in enumerate(zip(ends, got))
+    ]
+    last = [lax.ppermute(end, axes, second_round) for end in relayed]
+    return call(
+        functools.partial(arrived_kernel, frames, len(ends)),
+        of((ends[0].shape[0], pole.shape[1]), jnp.float32),
+        *got,
+        *last,
+        pole,
+    )
 
 
 def activated(drives, entry, start, pole_ref, scale_ref):
@@ -261,11 +352,11 @@
             here = slice(at + frame * rows, at + (frame + 1) * rows)
             lhs_ref[here] = row_taps(column, end, end).astype(lhs_ref.dtype)
 
-    def store(lanes):
+    def store(frame, lanes):
         return pltpu.make_async_copy(
-            held_ref.at[:, :, :, lanes],
-            out_ref.at[:, :, :, lanes],
-            sems.at[lanes.start // LANES],
+            held_ref.at[frame, :, :, lanes],
+            out_ref.at[frame, :, :, lanes],
+            sems.at[frame, lanes.start // LANES],
         )
 
     inner = count * size
@@ -282,17 +373,18 @@
         total += jnp.where(
             col == cols - 1, halo, pltpu.roll(last[:inner].reshape(tile), cols - 1, 2)
         )
-        held_ref[:, :, :, lanes] = total.astype(held_ref.dtype)
-        store(lanes).start()
+        for frame in range(count):
+            held_ref[frame, :, :, lanes] = total[frame].astype(held_ref.dtype)
+            store(frame, lanes).start()
     for lane in range(0, weight_ref.shape[-1], LANES):
-        store(slice(lane, lane + LANES)).wait()
+        for frame in range(count):
+            store(frame, slice(lane, lane + LANES)).wait()
 
 
 def on_device(frames, input_weight, output_weight, pole_index, gelu_scale, start_state):
     count, rows, cols, channels = frames.shape
     size, room = rows * cols, count * rows
     wide = 3 * channels
-    groups = lax.axis_size("tm")
     assert lax.axis_size("sx") == 2
     narrow = frames.dtype
     pole, scale = pole_index[None], gelu_scale[None]
@@ -301,8 +393,20 @@
         of((count * cols + (2 * count + 1) * rows, channels), narrow),
         of((2 * count + 1, rows, channels), narrow),
     )
-    edges = call(edges_kernel, shapes, frames, flops=2000000000)
-    give, keep = call(start_edges_kernel, shapes, start_state, *edges, aliases={1: 0, 2: 1})
+    edges = call(
+        edges_kernel,
+        shapes,
+        frames,
+        scratch=[pltpu.VMEM((count, channels // 128, size, 128), jnp.float32)],
+        flops=EDGES_COST,
+    )
+    give, keep = call(
+        start_edges_kernel,
+        shapes,
+        start_state,
+        *edges,
+        aliases={1: 0, 2: 1},
+    )
     got, mine = trade_columns(give, keep, count * cols)
     main = call(
         main_kernel,
@@ -314,13 +418,14 @@
         flops=18 * frames.size * channels,
     )
     mine, (total, spill) = lax.optimization_barrier((mine, main))
-    drive, beside, end, sides = call(
+    parts = channels // LANES
+    drive, beside, sides, *ends = call(
         drive_kernel,
         (
             of(frames.shape, jnp.float32),
             of((count, 2 * rows, channels), jnp.float32),
-            of((size + 2 * rows, channels), narrow),
             of((2 * rows, channels), jnp.float32),
+            *[of((size + 2 * rows, LANES), narrow)] * parts,
         ),
         mine,
         swap_cores(mine),
@@ -331,12 +436,7 @@
         scratch=[pltpu.VMEM((4 * room, wide), narrow)],
         flops=36 * room * channels * channels,
     )
-
-    ends = lax.all_to_all(end.reshape(groups, -1, channels), "tm", 0, 0)
-    entries = call(
-        lambda *refs: entry_kernel(count, *refs), of(ends.shape, narrow), ends, pole
-    )
-    entry = lax.all_to_all(entries, "tm", 0, 0).reshape(end.shape)
+    entry = (exchange_four if lax.axis_size("tm") == 4 else exchange)(ends, pole, count)
 
     give, beside = call(
         beside_kernel,
@@ -362,7 +462,7 @@
         scratch=[
             pltpu.VMEM((count * size + 2 * room, wide), narrow),
             pltpu.VMEM(frames.shape, narrow),
-            pltpu.SemaphoreType.DMA((channels // LANES,)),
+            pltpu.SemaphoreType.DMA((count, parts)),
         ],
         flops=18 * frames.size * channels,
     )

time: 50.2 us -> 44.2 us (0.88)
  the two profiles are of different devices: /device:TPU:0 before, /device:TPU:23 now
where the time goes in v6:
time: 44.2 us; the launch traced here: 43.8 us
  Pallas kernels  14.8 us (33%)
  waiting for transfers between devices  14.3 us (32%)
  starting transfers between devices  13.1 us (30%)
  local copies, waits for them, and re-layouts  1.36 us (3%)
    pallas_call x10, Pallas kernels, call(): pl.pallas_call(kernel, in_specs=[WHOLE] * len(args), out_specs=out_specs...  14.8 us
    ppermute x2, waiting for transfers between devices, exchange_four(): got = [lax.ppermute(end, axes, first_round) for end in ends]  6.25 us
    ppermute x2, waiting for transfers between devices, exchange_four(): last = [lax.ppermute(end, axes, second_round) for end in relayed]  5.48 us
    ppermute x2, starting transfers between devices, exchange_four(): last = [lax.ppermute(end, axes, second_round) for end in relayed]  4.21 us
    ppermute x1, starting transfers between devices, trade_columns(): return (got, lax.ppermute(columns, ('sx', 'sy'), pairs))  3.46 us
    ppermute x3, starting transfers between devices, swap_cores(): return lax.ppermute(array, 'sx', [(0, 1), (1, 0)])  2.85 us
    ppermute x2, starting transfers between devices, exchange_four(): got = [lax.ppermute(end, axes, first_round) for end in ends]  2.58 us
    ppermute x3, waiting for transfers between devices, swap_cores(): return lax.ppermute(array, 'sx', [(0, 1), (1, 0)])  2.57 us
  transfers between devices with their start and end apart: 8, of which 6 were waited for; matrix products, arithmetic and copies ran while one was open for 0% of the time, Pallas kernels for 14%

profile of v6, /device:TPU:23, one launch (start us, length us, event | category | flops | bytes accessed | tf_op | source)
XLA Modules:
  0.0 43.8 jit_solution(8259706524758866124)
XLA Ops:
  0.0 0.0 copy-start
  0.0 0.0 copy-start.4
  0.0 1.3 %copy-done.4 = bf16[2,32,16,512]{3,2,1,0:T(8,128)(2,1)S(1)} copy-done((bf16[2,32,16,512]{3,2,1,0:T(8,128)(2,1)S(1)}, bf16[2,32,16,512]{3,2,1,0:T(8,128)(2,1)}, u32[]{:S(2)}) %copy-start.4) | copy-done | bytes 1048600
  1.3 0.0 copy-start.1
  1.3 0.3 shard_map.64
  1.7 0.0 copy-done
  1.7 0.3 shard_map.65
  1.9 0.7 %collective-permute-start = (bf16[192,512]{1,0:T(8,128)(2,1)S(1)}, bf16[192,512]{1,0:T(8,128)(2,1)S(1)}, u32[]{:S(2)}, u32[]{:S(2)}) collective-permute-start(bf16[192,512]{1,0:T(8,128)(2,1)S(1)} %get-tuple-element.24), channel_id=1, source_target_pairs={{0,4},{4,0},{1,5},{5,1},{2,6},{6,2},{3,7},{7,3},{8,12},{12,8},{9,1... | collective-permute-start | bytes 589832 | tf_op jit(solution)/shard_map/ppermute | solution.py:52
  2.7 1.1 %collective-permute-done.got_ref = bf16[192,512]{1,0:T(8,128)(2,1)S(1)} collective-permute-done((bf16[192,512]{1,0:T(8,128)(2,1)S(1)}, bf16[192,512]{1,0:T(8,128)(2,1)S(1)}, u32[]{:S(2)}, u32[]{:S(2)}) %collective-permute-start) | collective-permute-done | bytes 196640 | tf_op jit(solution)/shard_map/ppermute | solution.py:52
  3.8 0.0 copy-start.2
  3.8 3.5 %collective-permute-start.1 = (bf16[5,64,512]{2,1,0:T(8,128)(2,1)S(1)}, bf16[5,64,512]{2,1,0:T(8,128)(2,1)S(1)}, u32[]{:S(2)}, u32[]{:S(2)}) collective-permute-start(bf16[5,64,512]{2,1,0:T(8,128)(2,1)S(1)} %pad_maximum_fusion), channel_id=1, source_target_pairs={{1,4},{2,5},{3,6},{4,1},{5,2},{6,3},{9,12},{10,13},{11,14},{12,9},... | collective-permute-start | bytes 983048 | tf_op jit(solution)/shard_map/ppermute | solution.py:96
  7.3 0.0 copy-done.1
  7.3 5.1 %shard_map.66 = (f32[2,32,16,512]{3,2,1,0:T(8,128)S(1)}, f32[2,64,512]{2,1,0:T(8,128)S(1)}) custom-call(bf16[2,32,16,512]{3,2,1,0:T(8,128)(2,1)S(1)} %copy-done.4, bf16[192,512]{1,0:T(8,128)(2,1)S(1)} %collective-permute-done.got_ref, bf16[3,3,512,512]{3,2,1,0:T(8,128)(2,1)S(1)} %copy-done.1), custom_call_target="tpu_custom_call" | custom-call | flops 4831838208 | bytes 8323072 | tf_op jit(solution)/shard_map/pallas_call | solution.py:22
  12.4 0.0 collective-permute-done.1.mine_ref
  12.4 0.2 collective-permute-start.2
  12.6 1.5 %collective-permute-done.2.theirs_ref = bf16[5,64,512]{2,1,0:T(8,128)(2,1)S(1)} collective-permute-done((bf16[5,64,512]{2,1,0:T(8,128)(2,1)S(1)}, bf16[5,64,512]{2,1,0:T(8,128)(2,1)S(1)}, u32[]{:S(2)}, u32[]{:S(2)}) %collective-permute-start.2) | collective-permute-done | bytes 327712 | tf_op jit(solution)/shard_map/ppermute | solution.py:52
  14.1 0.0 copy-done.2
  14.1 1.3 %shard_map.67 = (f32[2,32,16,512]{3,2,1,0:T(8,128)S(1)}, f32[2,64,512]{2,1,0:T(8,128)S(1)}, f32[64,512]{1,0:T(8,128)S(1)}, bf16[576,256]{1,0:T(8,128)(2,1)S(1)}, bf16[576,256]{1,0:T(8,128)(2,1)S(1)}) custom-call(bf16[5,64,512]{2,1,0:T(8,128)(2,1)S(1)} %collective-permute-done.1.mine_ref, bf16[5,64,512]{2,1,0:T(8,128)(2,1)S(1)} %collective-permute-done.2.theirs_ref, ...), custom_call_target="tpu_custom_call" | custom-call | flops 603979776 | bytes 10815488 | tf_op jit(solution)/shard_map/pallas_call | solution.py:22
  15.4 0.0 copy-start.3
  15.4 1.3 %collective-permute-start.3 = (bf16[576,256]{1,0:T(8,128)(2,1)S(1)}, bf16[576,256]{1,0:T(8,128)(2,1)S(1)}, u32[]{:S(2)}, u32[]{:S(2)}) collective-permute-start(bf16[576,256]{1,0:T(8,128)(2,1)S(1)} %get-tuple-element.31.end_ref), channel_id=1, source_target_pairs={{0,8},{8,0},{16,24},{4,20},{12,28},{1,9},{9,1},{17,25},{5,21},{13,... | collective-permute-start | bytes 884744 | tf_op jit(solution)/shard_map/ppermute | solution.py:264
  16.7 1.3 %collective-permute-start.4 = (bf16[576,256]{1,0:T(8,128)(2,1)S(1)}, bf16[576,256]{1,0:T(8,128)(2,1)S(1)}, u32[]{:S(2)}, u32[]{:S(2)}) collective-permute-start(bf16[576,256]{1,0:T(8,128)(2,1)S(1)} %get-tuple-element.32.end_ref), channel_id=1, source_target_pairs={{0,8},{8,0},{16,24},{4,20},{12,28},{1,9},{9,1},{17,25},{5,21},{13,... | collective-permute-start | bytes 884744 | tf_op jit(solution)/shard_map/ppermute | solution.py:264
  18.0 5.2 %collective-permute-done.3.got_ref.refs_0_ = bf16[576,256]{1,0:T(8,128)(2,1)S(1)} collective-permute-done((bf16[576,256]{1,0:T(8,128)(2,1)S(1)}, bf16[576,256]{1,0:T(8,128)(2,1)S(1)}, u32[]{:S(2)}, u32[]{:S(2)}) %collective-permute-start.3) | collective-permute-done | bytes 294944 | tf_op jit(solution)/shard_map/ppermute | solution.py:264
  23.1 0.1 shard_map.68
  23.3 1.9 %collective-permute-start.5 = (bf16[576,256]{1,0:T(8,128)(2,1)S(1)}, bf16[576,256]{1,0:T(8,128)(2,1)S(1)}, u32[]{:S(2)}, u32[]{:S(2)}) collective-permute-start(bf16[576,256]{1,0:T(8,128)(2,1)S(1)} %shard_map.68), channel_id=1, source_target_pairs={{0,16},{8,24},{4,12},{20,28},{28,20},{1,17},{9,25},{5,13},{21,29},... | collective-permute-start | bytes 884744 | tf_op jit(solution)/shard_map/ppermute | solution.py:275
  25.2 1.1 %collective-permute-done.4.got_ref.refs_1_ = bf16[576,256]{1,0:T(8,128)(2,1)S(1)} collective-permute-done((bf16[576,256]{1,0:T(8,128)(2,1)S(1)}, bf16[576,256]{1,0:T(8,128)(2,1)S(1)}, u32[]{:S(2)}, u32[]{:S(2)}) %collective-permute-start.4) | collective-permute-done | bytes 294944 | tf_op jit(solution)/shard_map/ppermute | solution.py:264
  26.3 0.1 shard_map.69
  26.4 2.3 %collective-permute-start.6 = (bf16[576,256]{1,0:T(8,128)(2,1)S(1)}, bf16[576,256]{1,0:T(8,128)(2,1)S(1)}, u32[]{:S(2)}, u32[]{:S(2)}) collective-permute-start(bf16[576,256]{1,0:T(8,128)(2,1)S(1)} %shard_map.69), channel_id=1, source_target_pairs={{0,16},{8,24},{4,12},{20,28},{28,20},{1,17},{9,25},{5,13},{21,29},... | collective-permute-start | bytes 884744 | tf_op jit(solution)/shard_map/ppermute | solution.py:275
  28.7 2.3 %collective-permute-done.5.refs_2_ = bf16[576,256]{1,0:T(8,128)(2,1)S(1)} collective-permute-done((bf16[576,256]{1,0:T(8,128)(2,1)S(1)}, bf16[576,256]{1,0:T(8,128)(2,1)S(1)}, u32[]{:S(2)}, u32[]{:S(2)}) %collective-permute-start.5) | collective-permute-done | bytes 294944 | tf_op jit(solution)/shard_map/ppermute | solution.py:275
  31.0 3.2 %collective-permute-done.6.refs_3_ = bf16[576,256]{1,0:T(8,128)(2,1)S(1)} collective-permute-done((bf16[576,256]{1,0:T(8,128)(2,1)S(1)}, bf16[576,256]{1,0:T(8,128)(2,1)S(1)}, u32[]{:S(2)}, u32[]{:S(2)}) %collective-permute-start.6) | collective-permute-done | bytes 294944 | tf_op jit(solution)/shard_map/ppermute | solution.py:275
  34.2 0.0 slice-start
  34.2 0.2 shard_map.70.entry_ref
  34.4 0.0 copy-done.3
  34.4 0.0 slice-start.1
  34.4 0.2 shard_map.72
  34.7 1.9 %collective-permute-start.7 = (bf16[2,32,512]{2,1,0:T(8,128)(2,1)S(1)}, bf16[2,32,512]{2,1,0:T(8,128)(2,1)S(1)}, u32[]{:S(2)}, u32[]{:S(2)}) collective-permute-start(bf16[2,32,512]{2,1,0:T(8,128)(2,1)S(1)} %get-tuple-element.35), channel_id=1, source_target_pairs={{0,4},{4,0},{1,5},{5,1},{2,6},{6,2},{3,7},{7,3},{8,12},{12,8},{9,1... | collective-permute-start | bytes 196616 | tf_op jit(solution)/shard_map/ppermute | solution.py:52
  36.6 1.0 %shard_map.71.cells_ref = bf16[2,32,16,512]{3,2,1,0:T(8,128)(2,1)S(1)} custom-call(f32[2,32,16,512]{3,2,1,0:T(8,128)S(1)} %get-tuple-element.30.drive_ref, f32[576,512]{1,0:T(8,128)S(1)} %shard_map.70.entry_ref, f32[32,16,512]{2,1,0:T(8,128)S(1)} %copy-done, s32[1,512]{1,0:T(1,128)S(1)} %bitcast.8, f32[1,512]{1,0:T(1,128)S(1)} %bitcast.10), custom_call_target="tpu_custom_call" | custom-call | bytes 5378048 | tf_op jit(solution)/shard_map/pallas_call | solution.py:22
  37.6 0.0 collective-permute-done.7.got_ref
  37.6 0.0 slice-done
  37.6 0.0 slice-done.1
  37.6 6.2 %shard_map.73 = bf16[2,32,16,512]{3,2,1,0:T(8,128)(2,1)} custom-call(bf16[2,32,16,512]{3,2,1,0:T(8,128)(2,1)S(1)} %shard_map.71.cells_ref, bf16[2,32,512]{2,1,0:T(8,128)(2,1)S(1)} %collective-permute-done.7.got_ref, bf16[2,64,512]{2,1,0:T(8,128)(2,1)S(1)} %get-tuple-element.36.beside_ref, bf16[3,3,512,512]{3,2,1,0:T(8,128)(2,1)S(1)} %bitcast.12), custom_call_target="tpu_custom_call" | custom-call | flops 4831838208 | bytes 7012352 | tf_op jit(solution)/shard_map/pallas_call | solution.py:22
  (3 shorter events, 0.0 us)
Async XLA Ops:
  0.0 1.7 %copy-start = (f32[32,16,512]{2,1,0:T(8,128)S(1)}, f32[32,16,512]{2,1,0:T(8,128)}, u32[]{:S(2)}) copy-start(f32[32,16,512]{2,1,0:T(8,128)} %start_ref.5) | copy-start | bytes 3145732
  0.0 1.3 %copy-start.4 = (bf16[2,32,16,512]{3,2,1,0:T(8,128)(2,1)S(1)}, bf16[2,32,16,512]{3,2,1,0:T(8,128)(2,1)}, u32[]{:S(2)}) copy-start(bf16[2,32,16,512]{3,2,1,0:T(8,128)(2,1)} %cells_ref.3) | copy-start | bytes 3145732
  1.3 6.0 %copy-start.1 = (bf16[3,3,512,512]{3,2,1,0:T(8,128)(2,1)S(1)}, bf16[3,3,512,512]{3,2,1,0:T(8,128)(2,1)}, u32[]{:S(2)}) copy-start(bf16[3,3,512,512]{3,2,1,0:T(8,128)(2,1)} %weight_ref.4) | copy-start | bytes 14155780
  1.9 1.8 %collective-permute-start = (bf16[192,512]{1,0:T(8,128)(2,1)S(1)}, bf16[192,512]{1,0:T(8,128)(2,1)S(1)}, u32[]{:S(2)}, u32[]{:S(2)}) collective-permute-start(bf16[192,512]{1,0:T(8,128)(2,1)S(1)} %get-tuple-element.24), channel_id=1, source_target_pairs={{0,4},{4,0},{1,5},{5,1},{2,6},{6,2},{3,7},{7,3},{8,12},{12,8},{9,1... | collective-permute-start | bytes 589832 | tf_op jit(solution)/shard_map/ppermute | solution.py:52
  3.8 10.3 %copy-start.2 = (s32[512]{0:T(512)S(1)}, s32[512]{0:T(512)}, u32[]{:S(2)}) copy-start(s32[512]{0:T(512)} %param.9) | copy-start | bytes 6148
  3.8 8.6 %collective-permute-start.1 = (bf16[5,64,512]{2,1,0:T(8,128)(2,1)S(1)}, bf16[5,64,512]{2,1,0:T(8,128)(2,1)S(1)}, u32[]{:S(2)}, u32[]{:S(2)}) collective-permute-start(bf16[5,64,512]{2,1,0:T(8,128)(2,1)S(1)} %pad_maximum_fusion), channel_id=1, source_target_pairs={{1,4},{2,5},{3,6},{4,1},{5,2},{6,3},{9,12},{10,13},{11,14},{12,9},... | collective-permute-start | bytes 983048 | tf_op jit(solution)/shard_map/ppermute | solution.py:96
  12.4 1.7 %collective-permute-start.2 = (bf16[5,64,512]{2,1,0:T(8,128)(2,1)S(1)}, bf16[5,64,512]{2,1,0:T(8,128)(2,1)S(1)}, u32[]{:S(2)}, u32[]{:S(2)}) collective-permute-start(bf16[5,64,512]{2,1,0:T(8,128)(2,1)S(1)} %collective-permute-done.1.mine_ref), channel_id=1, source_target_pairs={{0,4},{4,0},{1,5},{5,1},{2,6},{6,2},{3,7},{7,3},{8,12},{12,8},{9,1... | collective-permute-start | bytes 983048 | tf_op jit(solution)/shard_map/ppermute | solution.py:52
  15.4 19.1 %copy-start.3 = (f32[512]{0:T(512)S(1)}, f32[512]{0:T(512)}, u32[]{:S(2)}) copy-start(f32[512]{0:T(512)} %param.10) | copy-start | bytes 6148
  15.4 7.8 %collective-permute-start.3 = (bf16[576,256]{1,0:T(8,128)(2,1)S(1)}, bf16[576,256]{1,0:T(8,128)(2,1)S(1)}, u32[]{:S(2)}, u32[]{:S(2)}) collective-permute-start(bf16[576,256]{1,0:T(8,128)(2,1)S(1)} %get-tuple-element.31.end_ref), channel_id=1, source_target_pairs={{0,8},{8,0},{16,24},{4,20},{12,28},{1,9},{9,1},{17,25},{5,21},{13,... | collective-permute-start | bytes 884744 | tf_op jit(solution)/shard_map/ppermute | solution.py:264
  16.7 9.6 %collective-permute-start.4 = (bf16[576,256]{1,0:T(8,128)(2,1)S(1)}, bf16[576,256]{1,0:T(8,128)(2,1)S(1)}, u32[]{:S(2)}, u32[]{:S(2)}) collective-permute-start(bf16[576,256]{1,0:T(8,128)(2,1)S(1)} %get-tuple-element.32.end_ref), channel_id=1, source_target_pairs={{0,8},{8,0},{16,24},{4,20},{12,28},{1,9},{9,1},{17,25},{5,21},{13,... | collective-permute-start | bytes 884744 | tf_op jit(solution)/shard_map/ppermute | solution.py:264
  23.3 7.8 %collective-permute-start.5 = (bf16[576,256]{1,0:T(8,128)(2,1)S(1)}, bf16[576,256]{1,0:T(8,128)(2,1)S(1)}, u32[]{:S(2)}, u32[]{:S(2)}) collective-permute-start(bf16[576,256]{1,0:T(8,128)(2,1)S(1)} %shard_map.68), channel_id=1, source_target_pairs={{0,16},{8,24},{4,12},{20,28},{28,20},{1,17},{9,25},{5,13},{21,29},... | collective-permute-start | bytes 884744 | tf_op jit(solution)/shard_map/ppermute | solution.py:275
  26.4 7.8 %collective-permute-start.6 = (bf16[576,256]{1,0:T(8,128)(2,1)S(1)}, bf16[576,256]{1,0:T(8,128)(2,1)S(1)}, u32[]{:S(2)}, u32[]{:S(2)}) collective-permute-start(bf16[576,256]{1,0:T(8,128)(2,1)S(1)} %shard_map.69), channel_id=1, source_target_pairs={{0,16},{8,24},{4,12},{20,28},{28,20},{1,17},{9,25},{5,13},{21,29},... | collective-permute-start | bytes 884744 | tf_op jit(solution)/shard_map/ppermute | solution.py:275
  34.2 3.4 %slice-start = ((s8[4718592]{0:T(1024)(128)(4,1)}), s8[4194304]{0:T(1024)(128)(4,1)S(1)}, s32[]{:S(2)}) async-start(s8[4718592]{0:T(1024)(128)(4,1)} %bitcast.11), calls=%async_computation | async-start | bytes 8388608
  34.4 3.2 %slice-start.1 = ((s8[4718592]{0:T(1024)(128)(4,1)}), s8[524288]{0:T(1024)(128)(4,1)S(1)}, s32[]{:S(2)}) async-start(s8[4718592]{0:T(1024)(128)(4,1)} %bitcast.11), calls=%async_computation.1 | async-start | bytes 1048576
  34.7 2.9 %collective-permute-start.7 = (bf16[2,32,512]{2,1,0:T(8,128)(2,1)S(1)}, bf16[2,32,512]{2,1,0:T(8,128)(2,1)S(1)}, u32[]{:S(2)}, u32[]{:S(2)}) collective-permute-start(bf16[2,32,512]{2,1,0:T(8,128)(2,1)S(1)} %get-tuple-element.35), channel_id=1, source_target_pairs={{0,4},{4,0},{1,5},{5,1},{2,6},{6,2},{3,7},{7,3},{8,12},{12,8},{9,1... | collective-permute-start | bytes 196616 | tf_op jit(solution)/shard_map/ppermute | solution.py:52

commit v7 on v6

--- a/solution.py
+++ b/solution.py
@@ -117,8 +117,8 @@
     return jnp.concatenate([up, column, down], axis=1)
 
 
-def dot(lhs, weight_ref, column, lanes):
-    weight = weight_ref[:, column, :, lanes].reshape(lhs.shape[1], -1)
+def dot(lhs, weight_ref, column, lanes, inputs=slice(None)):
+    weight = weight_ref[:, column, inputs, lanes].reshape(lhs.shape[1], -1)
     return jnp.dot(lhs, weight, preferred_element_type=jnp.float32)
 
 
@@ -142,13 +142,10 @@
         )
 
 
-def drive_kernel(
-    mine_ref, theirs_ref, weight_ref, total_ref, spill_ref, pole_ref,
-    drive_ref, beside_ref, start_ref, *more_refs,
-):
-    count, rows, cols, _ = total_ref.shape
+def halo_kernel(mine_ref, theirs_ref, lhs_ref, start_ref):
+    rows = mine_ref.shape[1] // 2
+    count = mine_ref.shape[0] // 2
     room = count * rows
-    *end_refs, lhs_ref = more_refs
     zero, one = is_core(0), is_core(1)
     core = lax.axis_index("sx")
     slots = ((1, 0), (2, 3))
@@ -167,33 +164,34 @@
     start_ref[:rows] = zero * own + one * other
     start_ref[rows:] = zero * other + one * own
 
-    decay = jnp.exp(rate_of(pole_ref))
-    tile = (count, rows, cols, LANES)
-    col = lax.broadcasted_iota(jnp.int32, tile, 2)
-    for lane in range(0, weight_ref.shape[-1], LANES):
-        lanes = slice(lane, lane + LANES)
-        first = dot(lhs_ref[: 2 * room], weight_ref, 0, lanes)
-        middle = dot(lhs_ref[room : 3 * room], weight_ref, 1, lanes)
-        last = dot(lhs_ref[2 * room :], weight_ref, 2, lanes)
-        left = (spill_ref[0, :, lanes] + first[:room] + middle[:room]).reshape(count, rows, LANES)
-        right = (spill_ref[1, :, lanes] + middle[room:] + last[room:]).reshape(count, rows, LANES)
-        near = first[room:].reshape(count, rows, 1, LANES)
-        total = total_ref[:, :, :, lanes] + jnp.where(col == 0, near, 0.0)
-        near = last[:room].reshape(count, rows, 1, LANES)
-        total += jnp.where(col == cols - 1, near, 0.0)
-        drive_ref[:, :, :, lanes] = total
-        beside_ref[:, :rows, lanes] = left
-        beside_ref[:, rows:, lanes] = right
-        state, left_state, right_state = total[0], left[0], right[0]
-        for frame in range(1, count):
-            state = decay[:, lanes] * state + total[frame]
-            left_state = decay[:, lanes] * left_state + left[frame]
-            right_state = decay[:, lanes] * right_state + right[frame]
-        size = rows * cols
-        end_ref = end_refs[lane // LANES]
-        end_ref[:size] = state.reshape(size, LANES).astype(end_ref.dtype)
-        end_ref[size : size + rows] = left_state.astype(end_ref.dtype)
-        end_ref[size + rows :] = right_state.astype(end_ref.dtype)
+
+def drive_kernel(
+    lanes, lhs_ref, weight_ref, total_ref, spill_ref, pole_ref, drive_ref, beside_ref, end_ref
+):
+    count, rows, cols, wide = drive_ref.shape
+    room, size = count * rows, rows * cols
+    decay = jnp.exp(rate_of(pole_ref))[:, lanes]
+    col = lax.broadcasted_iota(jnp.int32, drive_ref.shape, 2)
+    first = dot(lhs_ref[: 2 * room], weight_ref, 0, lanes)
+    middle = dot(lhs_ref[room : 3 * room], weight_ref, 1, lanes)
+    last = dot(lhs_ref[2 * room :], weight_ref, 2, lanes)
+    left = (spill_ref[0, :, lanes] + first[:room] + middle[:room]).reshape(count, rows, wide)
+    right = (spill_ref[1, :, lanes] + middle[room:] + last[room:]).reshape(count, rows, wide)
+    near = first[room:].reshape(count, rows, 1, wide)
+    total = total_ref[:, :, :, lanes] + jnp.where(col == 0, near, 0.0)
+    near = last[:room].reshape(count, rows, 1, wide)
+    total += jnp.where(col == cols - 1, near, 0.0)
+    drive_ref[...] = total
+    beside_ref[:, :rows] = left
+    beside_ref[:, rows:] = right
+    state, left_state, right_state = total[0], left[0], right[0]
+    for frame in range(1, count):
+        state = decay * state + total[frame]
+        left_state = decay * left_state + left[frame]
+        right_state = decay * right_state + right[frame]
+    end_ref[:size] = state.reshape(size, wide).astype(end_ref.dtype)
+    end_ref[size : size + rows] = left_state.astype(end_ref.dtype)
+    end_ref[size + rows :] = right_state.astype(end_ref.dtype)
 
 
 def entry_kernel(frames, ends_ref, pole_ref, out_ref):
@@ -212,7 +210,8 @@
     entries = call(
         functools.partial(entry_kernel, frames), of(shares.shape, end.dtype), shares, pole
     )
-    return lax.all_to_all(entries, "tm", 0, 0).reshape(end.shape)
+    entry = lax.all_to_all(entries, "tm", 0, 0).reshape(end.shape)
+    return [(part,) for part in jnp.split(entry, len(ends), axis=1)]
 
 
 def pick(values):
@@ -238,19 +237,6 @@
     own = on_core(pick([carried, same, same, same]), pick([same, same, same, none]))
     got = on_core(pick([same, carried, carried, carried]), pick([none, none, twice, same]))
     out_ref[...] = weigh(end_ref, own, got_ref, got).astype(out_ref.dtype)
-
-
-def arrived_kernel(frames, parts, *refs):
-    *got_refs, pole_ref, out_ref = refs
-    rate = rate_of(pole_ref)
-    carried = jnp.exp(frames * rate)
-    none, same = jnp.zeros_like(rate), jnp.ones_like(rate)
-    early = on_core(pick([none, same, none, same]), pick([none, none, carried, carried]))
-    late = on_core(pick([none, none, same, carried]), pick([none, same, same, same]))
-    for part in range(parts):
-        lanes = slice(part * LANES, (part + 1) * LANES)
-        first, second = got_refs[part], got_refs[parts + part]
-        out_ref[:, lanes] = weigh(first, early[:, lanes], second, late[:, lanes])
 
 
 def exchange_four(ends, pole, frames):
@@ -272,49 +258,51 @@
         )
         for part, (end, here) in enumerate(zip(ends, got))
     ]
-    last = [lax.ppermute(end, axes, second_round) for end in relayed]
-    return call(
-        functools.partial(arrived_kernel, frames, len(ends)),
-        of((ends[0].shape[0], pole.shape[1]), jnp.float32),
-        *got,
-        *last,
-        pole,
-    )
-
-
-def activated(drives, entry, start, pole_ref, scale_ref):
-    rate = rate_of(pole_ref)
-    decay = jnp.exp(rate)
-    reach = jnp.exp((len(drives) * lax.axis_index("tm")).astype(jnp.float32) * rate)
-    state = reach * start + entry.astype(jnp.float32)
-    for drive in drives:
-        state = decay * state + drive
-        yield jax.nn.gelu(scale_ref[...] * state)
-
-
-def beside_kernel(
-    drive_ref, beside_ref, entry_ref, start_ref, sides_ref, pole_ref, scale_ref, give_ref, out_ref
-):
-    count, rows, cols, channels = drive_ref.shape
+    return [(here, lax.ppermute(end, axes, second_round)) for here, end in zip(got, relayed)]
+
+
+class Mix:
+    def __init__(self, lanes, count, arrived_refs, pole_ref, scale_ref):
+        self.rate = rate_of(pole_ref)[:, lanes]
+        self.scale = scale_ref[:, lanes]
+        self.count = count
+        self.arrived_refs = arrived_refs
+
+    def entry(self, rows):
+        parts = [ref[rows].astype(jnp.float32) for ref in self.arrived_refs]
+        if len(parts) == 1:
+            return parts[0]
+        carried = jnp.exp(self.count * self.rate)
+        none, same = jnp.zeros_like(self.rate), jnp.ones_like(self.rate)
+        early = on_core(pick([none, same, none, same]), pick([none, none, carried, carried]))
+        late = on_core(pick([none, none, same, carried]), pick([none, same, same, same]))
+        return early * parts[0] + late * parts[1]
+
+    def __call__(self, drives, rows, start):
+        decay = jnp.exp(self.rate)
+        reach = jnp.exp((self.count * lax.axis_index("tm")).astype(jnp.float32) * self.rate)
+        state = reach * start + self.entry(rows).reshape(start.shape)
+        for drive in drives:
+            state = decay * state + drive
+            yield jax.nn.gelu(self.scale * state)
+
+
+def beside_kernel(lanes, *refs):
+    drive_ref, beside_ref, start_ref, sides_ref, pole_ref, scale_ref, *arrived_refs = refs[:-2]
+    give_ref, out_ref = refs[-2:]
+    count, rows, cols, wide = drive_ref.shape
     size = rows * cols
     inner = inner_row(rows)
-    at = pl.multiple_of(inner * cols, cols)
+    mix = Mix(lanes, count, arrived_refs, pole_ref, scale_ref)
     chip, chips = lax.axis_index("sy"), lax.axis_size("sy")
-    row = lax.broadcasted_iota(jnp.int32, (2 * rows, channels), 0)
+    row = lax.broadcasted_iota(jnp.int32, (2 * rows, wide), 0)
     side = jnp.where(row < rows, (chip > 0).astype(jnp.float32), (chip < chips - 1).astype(jnp.float32))
-    beside = activated(
-        [beside_ref[frame] for frame in range(count)],
-        entry_ref[size:],
-        sides_ref[...],
-        pole_ref,
-        scale_ref,
-    )
-    tile = activated(
-        [drive_ref[frame, inner] for frame in range(count)],
-        entry_ref[pl.ds(at, cols)],
-        start_ref[inner],
-        pole_ref,
-        scale_ref,
+    beside = mix(
+        [beside_ref[frame] for frame in range(count)], slice(size, None), sides_ref[:, lanes]
+    )
+    here = pl.ds(pl.multiple_of(inner * cols, cols), cols)
+    tile = mix(
+        [drive_ref[frame, inner] for frame in range(count)], here, start_ref[inner, :, lanes]
     )
     zero, one = is_core(0), is_core(1)
     for frame, (cells, mixed) in enumerate(zip(tile, beside)):
@@ -323,24 +311,25 @@
         give_ref[frame, :cols] = cells.astype(give_ref.dtype)
         left = zero * mixed[rows - 1 : rows] + one * mixed[:1]
         right = zero * mixed[2 * rows - 1 :] + one * mixed[rows : rows + 1]
-        which = lax.broadcasted_iota(jnp.int32, (cols, channels), 0)
+        which = lax.broadcasted_iota(jnp.int32, (cols, wide), 0)
         ends = jnp.where(which == 0, left, right)
         give_ref[frame, cols:] = ends.astype(give_ref.dtype)
 
 
-def mixed_kernel(drive_ref, entry_ref, start_ref, pole_ref, scale_ref, out_ref):
-    count, rows, cols, channels = drive_ref.shape
+def mixed_kernel(lanes, *refs):
+    drive_ref, start_ref, pole_ref, scale_ref, *arrived_refs, out_ref = refs
+    count, rows, cols, _ = drive_ref.shape
+    mix = Mix(lanes, count, arrived_refs, pole_ref, scale_ref)
     block = 8
     for row in range(0, rows, block):
         here = slice(row, row + block)
         drives = [drive_ref[frame, here] for frame in range(count)]
-        entry = entry_ref[row * cols : (row + block) * cols].reshape(block, cols, channels)
-        mixed = activated(drives, entry, start_ref[here], pole_ref, scale_ref)
-        for frame, tile in enumerate(mixed):
+        cells = slice(row * cols, (row + block) * cols)
+        for frame, tile in enumerate(mix(drives, cells, start_ref[here, :, lanes])):
             out_ref[frame, here] = tile.astype(out_ref.dtype)
 
 
-def result_kernel(cells_ref, got_ref, beside_ref, weight_ref, out_ref, lhs_ref, held_ref, sems):
+def fill_tile(lhs_ref, cells_ref, got_ref, beside_ref):
     count, rows, cols, _ = cells_ref.shape
     size, room = rows * cols, count * rows
     for frame in range(count):
@@ -352,33 +341,56 @@
             here = slice(at + frame * rows, at + (frame + 1) * rows)
             lhs_ref[here] = row_taps(column, end, end).astype(lhs_ref.dtype)
 
-    def store(frame, lanes):
-        return pltpu.make_async_copy(
-            held_ref.at[frame, :, :, lanes],
-            out_ref.at[frame, :, :, lanes],
-            sems.at[frame, lanes.start // LANES],
-        )
-
-    inner = count * size
-    tile = (count, rows, cols, LANES)
+
+def tile_sum(tile, inputs, lanes, lhs_ref, weight_ref, before_ref):
+    count, rows, cols, _ = tile
+    inner, room = count * rows * cols, count * rows
     col = lax.broadcasted_iota(jnp.int32, tile, 2)
-    for lane in range(0, weight_ref.shape[-1], LANES):
-        lanes = slice(lane, lane + LANES)
-        total = dot(lhs_ref[room : room + inner], weight_ref, 1, lanes).reshape(tile)
-        first = dot(lhs_ref[: room + inner], weight_ref, 0, lanes)
-        halo = first[:room].reshape(count, rows, 1, LANES)
-        total += jnp.where(col == 0, halo, pltpu.roll(first[room:].reshape(tile), 1, 2))
-        last = dot(lhs_ref[room:], weight_ref, 2, lanes)
-        halo = last[inner:].reshape(count, rows, 1, LANES)
-        total += jnp.where(
-            col == cols - 1, halo, pltpu.roll(last[:inner].reshape(tile), cols - 1, 2)
-        )
+    total = dot(lhs_ref[room : room + inner], weight_ref, 1, lanes, inputs).reshape(tile)
+    if before_ref is not None:
+        total += before_ref[...]
+    first = dot(lhs_ref[: room + inner], weight_ref, 0, lanes, inputs)
+    halo = first[:room].reshape(count, rows, 1, LANES)
+    total += jnp.where(col == 0, halo, pltpu.roll(first[room:].reshape(tile), 1, 2))
+    last = dot(lhs_ref[room:], weight_ref, 2, lanes, inputs)
+    halo = last[inner:].reshape(count, rows, 1, LANES)
+    return total + jnp.where(
+        col == cols - 1, halo, pltpu.roll(last[:inner].reshape(tile), cols - 1, 2)
+    )
+
+
+def opening_kernel(inputs, lanes, has_before, cells_ref, got_ref, beside_ref, weight_ref, *refs):
+    *before_refs, out_ref, lhs_ref = refs
+    fill_tile(lhs_ref, cells_ref, got_ref, beside_ref)
+    before_ref = before_refs[0] if has_before else None
+    out_ref[...] = tile_sum(out_ref.shape, inputs, lanes, lhs_ref, weight_ref, before_ref)
+
+
+def further_kernel(inputs, lanes, has_before, lhs_ref, weight_ref, *refs):
+    *before_refs, out_ref = refs
+    before_ref = before_refs[0] if has_before else None
+    out_ref[...] = tile_sum(out_ref.shape, inputs, lanes, lhs_ref, weight_ref, before_ref)
+
+
+def result_kernel(inputs, outputs, cells_ref, got_ref, beside_ref, weight_ref, *refs):
+    *before_refs, out_ref, lhs_ref, held_ref, sems = refs
+    count, rows, cols, _ = cells_ref.shape
+    fill_tile(lhs_ref, cells_ref, got_ref, beside_ref)
+
+    def store(frame, part):
+        here = (frame, slice(None), slice(None), outputs[part])
+        return pltpu.make_async_copy(held_ref.at[here], out_ref.at[here], sems.at[frame, part])
+
+    for part, lanes in enumerate(outputs):
+        before_ref = before_refs[part] if before_refs else None
+        tile = (count, rows, cols, LANES)
+        total = tile_sum(tile, inputs, lanes, lhs_ref, weight_ref, before_ref)
         for frame in range(count):
             held_ref[frame, :, :, lanes] = total[frame].astype(held_ref.dtype)
-            store(frame, lanes).start()
-    for lane in range(0, weight_ref.shape[-1], LANES):
+            store(frame, part).start()
+    for part in range(len(outputs)):
         for frame in range(count):
-            store(frame, slice(lane, lane + LANES)).wait()
+            store(frame, part).wait()
 
 
 def on_device(frames, input_weight, output_weight, pole_index, gelu_scale, start_state):
@@ -418,53 +430,99 @@
         flops=18 * frames.size * channels,
     )
     mine, (total, spill) = lax.optimization_barrier((mine, main))
-    parts = channels // LANES
-    drive, beside, sides, *ends = call(
-        drive_kernel,
-        (
-            of(frames.shape, jnp.float32),
-            of((count, 2 * rows, channels), jnp.float32),
-            of((2 * rows, channels), jnp.float32),
-            *[of((size + 2 * rows, LANES), narrow)] * parts,
-        ),
+    halo, sides = call(
+        halo_kernel,
+        (of((4 * room, wide), narrow), of((2 * rows, channels), jnp.float32)),
         mine,
         swap_cores(mine),
-        input_weight,
-        total,
-        spill,
-        pole,
-        scratch=[pltpu.VMEM((4 * room, wide), narrow)],
-        flops=36 * room * channels * channels,
-    )
-    entry = (exchange_four if lax.axis_size("tm") == 4 else exchange)(ends, pole, count)
-
-    give, beside = call(
-        beside_kernel,
-        (of((count, 2 * cols, channels), narrow), of(beside.shape, narrow)),
-        drive,
-        beside,
-        entry,
-        start_state,
-        sides,
-        pole,
-        scale,
-    )
-    got = swap_cores(give)
-    mixed = call(mixed_kernel, of(frames.shape, narrow), drive, entry, start_state, pole, scale)
+    )
+    parts = [slice(lane, lane + LANES) for lane in range(0, channels, LANES)]
+    drives, besides, ends = zip(
+        *(
+            call(
+                functools.partial(drive_kernel, lanes),
+                (
+                    of((count, rows, cols, LANES), jnp.float32),
+                    of((count, 2 * rows, LANES), jnp.float32),
+                    of((size + 2 * rows, LANES), narrow),
+                ),
+                halo,
+                input_weight,
+                total,
+                spill,
+                pole,
+                flops=36 * room * channels * LANES,
+            )
+            for lanes in parts
+        )
+    )
+    arrivals = (exchange_four if lax.axis_size("tm") == 4 else exchange)(ends, pole, count)
+
+    sums, lhs = [None] * len(parts), None
+    inner = of((count, rows, cols, LANES), jnp.float32)
+    taps = (count * size + 2 * room, 3 * LANES)
+    for lanes, drive, beside, arrived in zip(parts, drives, besides, arrivals):
+        if lhs is not None:
+            *arrived, sums[0] = lax.optimization_barrier((*arrived, sums[0]))
+        give, edge = call(
+            functools.partial(beside_kernel, lanes),
+            (of((count, 2 * cols, LANES), narrow), of(beside.shape, narrow)),
+            drive,
+            beside,
+            start_state,
+            sides,
+            pole,
+            scale,
+            *arrived,
+        )
+        if lhs is not None:
+            give, lhs = lax.optimization_barrier((give, lhs))
+            for index in range(1, len(parts)):
+                sums[index] = call(
+                    functools.partial(further_kernel, before, parts[index], sums[index] is not None),
+                    inner,
+                    lhs,
+                    output_weight,
+                    *([] if sums[index] is None else [sums[index]]),
+                    flops=18 * drive.size * LANES,
+                )
+        got = swap_cores(give)
+        mixed = call(
+            functools.partial(mixed_kernel, lanes),
+            of(drive.shape, narrow),
+            drive,
+            start_state,
+            pole,
+            scale,
+            *arrived,
+        )
+        if lanes != parts[-1]:
+            sums[0], lhs = call(
+                functools.partial(opening_kernel, lanes, parts[0], sums[0] is not None),
+                (inner, of(taps, narrow)),
+                mixed,
+                got,
+                edge,
+                output_weight,
+                *([] if sums[0] is None else [sums[0]]),
+                flops=18 * drive.size * LANES,
+            )
+            before = lanes
     return call(
-        result_kernel,
+        functools.partial(result_kernel, parts[-1], parts),
         of(frames.shape, narrow),
         mixed,
         got,
-        beside,
+        edge,
         output_weight,
+        *([] if sums[0] is None else sums),
         out_specs=HBM,
         scratch=[
-            pltpu.VMEM((count * size + 2 * room, wide), narrow),
+            pltpu.VMEM(taps, narrow),
             pltpu.VMEM(frames.shape, narrow),
-            pltpu.SemaphoreType.DMA((count, parts)),
+            pltpu.SemaphoreType.DMA((count, len(parts))),
         ],
-        flops=18 * frames.size * channels,
+        flops=18 * mixed.size * channels,
     )
 
 

time: 44.2 us -> 42 us (0.950)
  waiting for transfers between devices: 14.3 us -> 10.3 us
  starting transfers between devices: 13.1 us -> 14.1 us
  Pallas kernels: 14.8 us -> 15.5 us
    ppermute x2, waiting for transfers between devices: 5.48 us -> 2.14 us  [exchange_four(): lax.ppermute(end, axes, second_round)]
    ppermute x2, waiting for transfers between devices: 6.25 us -> 5.35 us  [exchange_four(): got = [lax.ppermute(end, axes, first_round) for end in ends]]
    pallas_call x10 -> x15, Pallas kernels: 14.8 us -> 15.5 us  [call(): pl.pallas_call(kernel, in_specs=[WHOLE] * len(args), out_specs=out_specs...]
    ppermute x3 -> x4, starting transfers between devices: 2.85 us -> 3.42 us  [swap_cores(): return lax.ppermute(array, 'sx', [(0, 1), (1, 0)])]
    ppermute x3 -> x4, waiting for transfers between devices: 2.57 us -> 2.85 us  [swap_cores(): return lax.ppermute(array, 'sx', [(0, 1), (1, 0)])]
  transfers between devices with their start and end apart: 8 -> 9, of which waited for: 6 -> 6; matrix products, arithmetic and copies ran while one was open for 0% -> 0% of each run, Pallas kernels for 14% -> 25%
where the time goes in v7:
time: 42 us; the launch traced here: 41.8 us
  Pallas kernels  15.5 us (37%)
  starting transfers between devices  14.1 us (34%)
  waiting for transfers between devices  10.3 us (25%)
  local copies, waits for them, and re-layouts  1.42 us (3%)
    pallas_call x15, Pallas kernels, call(): pl.pallas_call(kernel, in_specs=[WHOLE] * len(args), out_specs=out_specs...  15.5 us
    ppermute x2, waiting for transfers between devices, exchange_four(): got = [lax.ppermute(end, axes, first_round) for end in ends]  5.35 us
    ppermute x2, starting transfers between devices, exchange_four(): lax.ppermute(end, axes, second_round)  4.38 us
    ppermute x1, starting transfers between devices, trade_columns(): return (got, lax.ppermute(columns, ('sx', 'sy'), pairs))  3.46 us
    ppermute x4, starting transfers between devices, swap_cores(): return lax.ppermute(array, 'sx', [(0, 1), (1, 0)])  3.42 us
    ppermute x2, starting transfers between devices, exchange_four(): got = [lax.ppermute(end, axes, first_round) for end in ends]  2.85 us
    ppermute x4, waiting for transfers between devices, swap_cores(): return lax.ppermute(array, 'sx', [(0, 1), (1, 0)])  2.85 us
    ppermute x2, waiting for transfers between devices, exchange_four(): lax.ppermute(end, axes, second_round)  2.14 us
  transfers between devices with their start and end apart: 9, of which 6 were waited for; matrix products, arithmetic and copies ran while one was open for 0% of the time, Pallas kernels for 25%

profile of v7, /device:TPU:23, one launch (start us, length us, event | category | flops | bytes accessed | tf_op | source)
XLA Modules:
  0.0 41.8 jit_solution(15728511579452932710)
XLA Ops:
  0.0 0.0 copy-start
  0.0 0.0 copy-start.1
  0.0 0.0 copy-start.4
  0.0 1.4 %copy-done.4 = bf16[2,32,16,512]{3,2,1,0:T(8,128)(2,1)S(1)} copy-done((bf16[2,32,16,512]{3,2,1,0:T(8,128)(2,1)S(1)}, bf16[2,32,16,512]{3,2,1,0:T(8,128)(2,1)}, u32[]{:S(2)}) %copy-start.4) | copy-done | bytes 1048600
  1.4 0.3 shard_map.64
  1.7 0.0 copy-done
  1.7 0.3 shard_map.65
  2.0 0.7 %collective-permute-start = (bf16[192,512]{1,0:T(8,128)(2,1)S(1)}, bf16[192,512]{1,0:T(8,128)(2,1)S(1)}, u32[]{:S(2)}, u32[]{:S(2)}) collective-permute-start(bf16[192,512]{1,0:T(8,128)(2,1)S(1)} %get-tuple-element.36), channel_id=1, source_target_pairs={{0,4},{4,0},{1,5},{5,1},{2,6},{6,2},{3,7},{7,3},{8,12},{12,8},{9,1... | collective-permute-start | bytes 589832 | tf_op jit(solution)/shard_map/ppermute | solution.py:52
  2.8 1.1 %collective-permute-done.got_ref = bf16[192,512]{1,0:T(8,128)(2,1)S(1)} collective-permute-done((bf16[192,512]{1,0:T(8,128)(2,1)S(1)}, bf16[192,512]{1,0:T(8,128)(2,1)S(1)}, u32[]{:S(2)}, u32[]{:S(2)}) %collective-permute-start) | collective-permute-done | bytes 196640 | tf_op jit(solution)/shard_map/ppermute | solution.py:52
  3.9 0.0 copy-start.2
  3.9 3.5 %collective-permute-start.1 = (bf16[5,64,512]{2,1,0:T(8,128)(2,1)S(1)}, bf16[5,64,512]{2,1,0:T(8,128)(2,1)S(1)}, u32[]{:S(2)}, u32[]{:S(2)}) collective-permute-start(bf16[5,64,512]{2,1,0:T(8,128)(2,1)S(1)} %pad_maximum_fusion), channel_id=1, source_target_pairs={{1,4},{2,5},{3,6},{4,1},{5,2},{6,3},{9,12},{10,13},{11,14},{12,9},... | collective-permute-start | bytes 983048 | tf_op jit(solution)/shard_map/ppermute | solution.py:96
  7.3 0.0 copy-done.1
  7.4 5.1 %shard_map.66 = (f32[2,32,16,512]{3,2,1,0:T(8,128)S(1)}, f32[2,64,512]{2,1,0:T(8,128)S(1)}) custom-call(bf16[2,32,16,512]{3,2,1,0:T(8,128)(2,1)S(1)} %copy-done.4, bf16[192,512]{1,0:T(8,128)(2,1)S(1)} %collective-permute-done.got_ref, bf16[3,3,512,512]{3,2,1,0:T(8,128)(2,1)S(1)} %copy-done.1), custom_call_target="tpu_custom_call" | custom-call | flops 4831838208 | bytes 8323072 | tf_op jit(solution)/shard_map/pallas_call | solution.py:22
  12.4 0.0 collective-permute-done.1.mine_ref
  12.4 0.2 collective-permute-start.2
  12.6 1.5 %collective-permute-done.2.theirs_ref = bf16[5,64,512]{2,1,0:T(8,128)(2,1)S(1)} collective-permute-done((bf16[5,64,512]{2,1,0:T(8,128)(2,1)S(1)}, bf16[5,64,512]{2,1,0:T(8,128)(2,1)S(1)}, u32[]{:S(2)}, u32[]{:S(2)}) %collective-permute-start.2) | collective-permute-done | bytes 327712 | tf_op jit(solution)/shard_map/ppermute | solution.py:52
  14.1 0.2 shard_map.67
  14.3 0.0 copy-done.2
  14.3 0.6 %shard_map.70 = (f32[2,32,16,256]{3,2,1,0:T(8,128)S(1)}, f32[2,64,256]{2,1,0:T(8,128)S(1)}, bf16[576,256]{1,0:T(8,128)(2,1)S(1)}) custom-call(bf16[256,1536]{1,0:T(8,128)(2,1)S(1)} %get-tuple-element.40.lhs_ref, bf16[3,3,512,512]{3,2,1,0:T(8,128)(2,1)S(1)} %copy-done.1, f32[2,32,16,512]{3,2,1,0:T(8,128)S(1)} %get-tuple-element.41.total_ref, ...), custom_call_target="tpu_custom_call" | custom-call | flops 301989888 | bytes 9340928 | tf_op jit(solution)/shard_map/pallas_call | solution.py:22
  15.0 0.0 copy-start.3
  15.0 1.3 %collective-permute-start.5 = (bf16[576,256]{1,0:T(8,128)(2,1)S(1)}, bf16[576,256]{1,0:T(8,128)(2,1)S(1)}, u32[]{:S(2)}, u32[]{:S(2)}) collective-permute-start(bf16[576,256]{1,0:T(8,128)(2,1)S(1)} %get-tuple-element.46.end_ref), channel_id=1, source_target_pairs={{0,8},{8,0},{16,24},{4,20},{12,28},{1,9},{9,1},{17,25},{5,21},{13,... | collective-permute-start | bytes 884744 | tf_op jit(solution)/shard_map/ppermute | solution.py:250
  16.3 0.0 slice-start
  16.3 0.6 %shard_map.68 = (f32[2,32,16,256]{3,2,1,0:T(8,128)S(1)}, f32[2,64,256]{2,1,0:T(8,128)S(1)}, bf16[576,256]{1,0:T(8,128)(2,1)S(1)}) custom-call(bf16[256,1536]{1,0:T(8,128)(2,1)S(1)} %get-tuple-element.40.lhs_ref, bf16[3,3,512,512]{3,2,1,0:T(8,128)(2,1)S(1)} %copy-done.1, f32[2,32,16,512]{3,2,1,0:T(8,128)S(1)} %get-tuple-element.41.total_ref, ...), custom_call_target="tpu_custom_call" | custom-call | flops 301989888 | bytes 9340928 | tf_op jit(solution)/shard_map/pallas_call | solution.py:22
  16.9 0.0 slice-start.1
  16.9 1.6 %collective-permute-start.3 = (bf16[576,256]{1,0:T(8,128)(2,1)S(1)}, bf16[576,256]{1,0:T(8,128)(2,1)S(1)}, u32[]{:S(2)}, u32[]{:S(2)}) collective-permute-start(bf16[576,256]{1,0:T(8,128)(2,1)S(1)} %get-tuple-element.44.end_ref), channel_id=1, source_target_pairs={{0,8},{8,0},{16,24},{4,20},{12,28},{1,9},{9,1},{17,25},{5,21},{13,... | collective-permute-start | bytes 884744 | tf_op jit(solution)/shard_map/ppermute | solution.py:250
  18.5 4.3 %collective-permute-done.5.got_ref.refs_4_.refs_6_ = bf16[576,256]{1,0:T(8,128)(2,1)S(1)} collective-permute-done((bf16[576,256]{1,0:T(8,128)(2,1)S(1)}, bf16[576,256]{1,0:T(8,128)(2,1)S(1)}, u32[]{:S(2)}, u32[]{:S(2)}) %collective-permute-start.5) | collective-permute-done | bytes 294944 | tf_op jit(solution)/shard_map/ppermute | solution.py:250
  22.7 0.1 shard_map.71
  22.9 1.9 %collective-permute-start.6 = (bf16[576,256]{1,0:T(8,128)(2,1)S(1)}, bf16[576,256]{1,0:T(8,128)(2,1)S(1)}, u32[]{:S(2)}, u32[]{:S(2)}) collective-permute-start(bf16[576,256]{1,0:T(8,128)(2,1)S(1)} %shard_map.71), channel_id=1, source_target_pairs={{0,16},{8,24},{4,12},{20,28},{28,20},{1,17},{9,25},{5,13},{21,29},... | collective-permute-start | bytes 884744 | tf_op jit(solution)/shard_map/ppermute | solution.py:261
  24.8 1.1 %collective-permute-done.3.got_ref.refs_4_.refs_6_ = bf16[576,256]{1,0:T(8,128)(2,1)S(1)} collective-permute-done((bf16[576,256]{1,0:T(8,128)(2,1)S(1)}, bf16[576,256]{1,0:T(8,128)(2,1)S(1)}, u32[]{:S(2)}, u32[]{:S(2)}) %collective-permute-start.3) | collective-permute-done | bytes 294944 | tf_op jit(solution)/shard_map/ppermute | solution.py:250
  25.9 0.1 shard_map.69
  26.0 2.5 %collective-permute-start.4 = (bf16[576,256]{1,0:T(8,128)(2,1)S(1)}, bf16[576,256]{1,0:T(8,128)(2,1)S(1)}, u32[]{:S(2)}, u32[]{:S(2)}) collective-permute-start(bf16[576,256]{1,0:T(8,128)(2,1)S(1)} %shard_map.69), channel_id=1, source_target_pairs={{0,16},{8,24},{4,12},{20,28},{28,20},{1,17},{9,25},{5,13},{21,29},... | collective-permute-start | bytes 884744 | tf_op jit(solution)/shard_map/ppermute | solution.py:261
  28.5 2.1 %collective-permute-done.6.refs_5_.refs_7_ = bf16[576,256]{1,0:T(8,128)(2,1)S(1)} collective-permute-done((bf16[576,256]{1,0:T(8,128)(2,1)S(1)}, bf16[576,256]{1,0:T(8,128)(2,1)S(1)}, u32[]{:S(2)}, u32[]{:S(2)}) %collective-permute-start.6) | collective-permute-done | bytes 294944 | tf_op jit(solution)/shard_map/ppermute | solution.py:261
  30.6 0.0 copy-done.3
  30.6 0.1 shard_map.73
  30.8 1.9 %collective-permute-start.7 = (bf16[2,32,256]{2,1,0:T(8,128)(2,1)S(1)}, bf16[2,32,256]{2,1,0:T(8,128)(2,1)S(1)}, u32[]{:S(2)}, u32[]{:S(2)}) collective-permute-start(bf16[2,32,256]{2,1,0:T(8,128)(2,1)S(1)} %get-tuple-element.49), channel_id=1, source_target_pairs={{0,4},{4,0},{1,5},{5,1},{2,6},{6,2},{3,7},{7,3},{8,12},{12,8},{9,1... | collective-permute-start | bytes 98312 | tf_op jit(solution)/shard_map/ppermute | solution.py:52
  32.7 0.6 %shard_map.72.cells_ref = bf16[2,32,16,256]{3,2,1,0:T(8,128)(2,1)S(1)} custom-call(f32[2,32,16,256]{3,2,1,0:T(8,128)S(1)} %get-tuple-element.45.refs_0_, f32[32,16,512]{2,1,0:T(8,128)S(1)} %copy-done, s32[1,512]{1,0:T(1,128)S(1)} %bitcast.10, f32[1,512]{1,0:T(1,128)S(1)} %bitcast.14, bf16[576,256]{1,0:T(8,128)(2,1)S(1)} %collective-permute-done.5.got_ref.refs_4_.refs_6_, ...), custom_call_target="tpu_custom_call" | custom-call | bytes 3215360 | tf_op jit(solution)/shard_map/pallas_call | solution.py:22
  33.3 0.3 collective-permute-done.7.got_ref
  33.5 0.0 slice-done
  33.5 0.0 slice-done.1
  33.5 1.6 %shard_map.74 = (f32[2,32,16,256]{3,2,1,0:T(8,128)S(1)}, bf16[1152,768]{1,0:T(8,128)(2,1)S(1)}) custom-call(bf16[2,32,16,256]{3,2,1,0:T(8,128)(2,1)S(1)} %shard_map.72.cells_ref, bf16[2,32,256]{2,1,0:T(8,128)(2,1)S(1)} %collective-permute-done.7.got_ref, bf16[2,64,256]{2,1,0:T(8,128)(2,1)S(1)} %get-tuple-element.50.beside_ref, ...), custom_call_target="tpu_custom_call" | custom-call | flops 1207959552 | bytes 8159232 | tf_op jit(solution)/shard_map/pallas_call | solution.py:22
  35.1 0.0 collective-permute-done.4.refs_5_.refs_7_
  35.1 0.1 shard_map.76
  35.3 0.6 %collective-permute-start.8 = (bf16[2,32,256]{2,1,0:T(8,128)(2,1)S(1)}, bf16[2,32,256]{2,1,0:T(8,128)(2,1)S(1)}, u32[]{:S(2)}, u32[]{:S(2)}) collective-permute-start(bf16[2,32,256]{2,1,0:T(8,128)(2,1)S(1)} %get-tuple-element.57), channel_id=1, source_target_pairs={{0,4},{4,0},{1,5},{5,1},{2,6},{6,2},{3,7},{7,3},{8,12},{12,8},{9,1... | collective-permute-start | bytes 98312 | tf_op jit(solution)/shard_map/ppermute | solution.py:52
  35.8 1.5 %shard_map.77.refs_1_ = f32[2,32,16,256]{3,2,1,0:T(8,128)S(1)} custom-call(bf16[1152,768]{1,0:T(8,128)(2,1)S(1)} %get-tuple-element.60.lhs_ref, bf16[3,3,512,512]{3,2,1,0:T(8,128)(2,1)S(1)} %bitcast.4), custom_call_target="tpu_custom_call" | custom-call | flops 1207959552 | bytes 7536640 | tf_op jit(solution)/shard_map/pallas_call | solution.py:22
  37.4 0.6 %shard_map.75.cells_ref = bf16[2,32,16,256]{3,2,1,0:T(8,128)(2,1)S(1)} custom-call(f32[2,32,16,256]{3,2,1,0:T(8,128)S(1)} %get-tuple-element.43.refs_0_, f32[32,16,512]{2,1,0:T(8,128)S(1)} %copy-done, s32[1,512]{1,0:T(1,128)S(1)} %bitcast.12, f32[1,512]{1,0:T(1,128)S(1)} %bitcast.16, bf16[576,256]{1,0:T(8,128)(2,1)S(1)} %collective-permute-done.3.got_ref.refs_4_.refs_6_, ...), custom_call_target="tpu_custom_call" | custom-call | bytes 3215360 | tf_op jit(solution)/shard_map/pallas_call | solution.py:22
  37.9 0.0 collective-permute-done.8.got_ref
  37.9 3.7 %shard_map.78 = bf16[2,32,16,512]{3,2,1,0:T(8,128)(2,1)} custom-call(bf16[2,32,16,256]{3,2,1,0:T(8,128)(2,1)S(1)} %shard_map.75.cells_ref, bf16[2,32,256]{2,1,0:T(8,128)(2,1)S(1)} %collective-permute-done.8.got_ref, bf16[2,64,256]{2,1,0:T(8,128)(2,1)S(1)} %get-tuple-element.58.beside_ref, bf16[3,3,512,512]{3,2,1,0:T(8,128)(2,1)S(1)} %bitcast.4, ...), custom_call_target="tpu_custom_call" | custom-call | flops 2415919104 | bytes 8486912 | tf_op jit(solution)/shard_map/pallas_call | solution.py:22
  (3 shorter events, 0.0 us)
Async XLA Ops:
  0.0 1.7 %copy-start = (f32[32,16,512]{2,1,0:T(8,128)S(1)}, f32[32,16,512]{2,1,0:T(8,128)}, u32[]{:S(2)}) copy-start(f32[32,16,512]{2,1,0:T(8,128)} %refs_2_.3) | copy-start | bytes 3145732
  0.0 7.3 %copy-start.1 = (bf16[3,3,512,512]{3,2,1,0:T(8,128)(2,1)S(1)}, bf16[3,3,512,512]{3,2,1,0:T(8,128)(2,1)}, u32[]{:S(2)}) copy-start(bf16[3,3,512,512]{3,2,1,0:T(8,128)(2,1)} %weight_ref.8) | copy-start | bytes 14155780
  0.0 1.4 %copy-start.4 = (bf16[2,32,16,512]{3,2,1,0:T(8,128)(2,1)S(1)}, bf16[2,32,16,512]{3,2,1,0:T(8,128)(2,1)}, u32[]{:S(2)}) copy-start(bf16[2,32,16,512]{3,2,1,0:T(8,128)(2,1)} %cells_ref.3) | copy-start | bytes 3145732
  2.0 1.8 %collective-permute-start = (bf16[192,512]{1,0:T(8,128)(2,1)S(1)}, bf16[192,512]{1,0:T(8,128)(2,1)S(1)}, u32[]{:S(2)}, u32[]{:S(2)}) collective-permute-start(bf16[192,512]{1,0:T(8,128)(2,1)S(1)} %get-tuple-element.36), channel_id=1, source_target_pairs={{0,4},{4,0},{1,5},{5,1},{2,6},{6,2},{3,7},{7,3},{8,12},{12,8},{9,1... | collective-permute-start | bytes 589832 | tf_op jit(solution)/shard_map/ppermute | solution.py:52
  3.9 10.5 %copy-start.2 = (s32[512]{0:T(512)S(1)}, s32[512]{0:T(512)}, u32[]{:S(2)}) copy-start(s32[512]{0:T(512)} %param.9) | copy-start | bytes 6148
  3.9 8.6 %collective-permute-start.1 = (bf16[5,64,512]{2,1,0:T(8,128)(2,1)S(1)}, bf16[5,64,512]{2,1,0:T(8,128)(2,1)S(1)}, u32[]{:S(2)}, u32[]{:S(2)}) collective-permute-start(bf16[5,64,512]{2,1,0:T(8,128)(2,1)S(1)} %pad_maximum_fusion), channel_id=1, source_target_pairs={{1,4},{2,5},{3,6},{4,1},{5,2},{6,3},{9,12},{10,13},{11,14},{12,9},... | collective-permute-start | bytes 983048 | tf_op jit(solution)/shard_map/ppermute | solution.py:96
  12.4 1.7 %collective-permute-start.2 = (bf16[5,64,512]{2,1,0:T(8,128)(2,1)S(1)}, bf16[5,64,512]{2,1,0:T(8,128)(2,1)S(1)}, u32[]{:S(2)}, u32[]{:S(2)}) collective-permute-start(bf16[5,64,512]{2,1,0:T(8,128)(2,1)S(1)} %collective-permute-done.1.mine_ref), channel_id=1, source_target_pairs={{0,4},{4,0},{1,5},{5,1},{2,6},{6,2},{3,7},{7,3},{8,12},{12,8},{9,1... | collective-permute-start | bytes 983048 | tf_op jit(solution)/shard_map/ppermute | solution.py:52
  15.0 15.7 %copy-start.3 = (f32[512]{0:T(512)S(1)}, f32[512]{0:T(512)}, u32[]{:S(2)}) copy-start(f32[512]{0:T(512)} %param.10) | copy-start | bytes 6148
  15.0 7.8 %collective-permute-start.5 = (bf16[576,256]{1,0:T(8,128)(2,1)S(1)}, bf16[576,256]{1,0:T(8,128)(2,1)S(1)}, u32[]{:S(2)}, u32[]{:S(2)}) collective-permute-start(bf16[576,256]{1,0:T(8,128)(2,1)S(1)} %get-tuple-element.46.end_ref), channel_id=1, source_target_pairs={{0,8},{8,0},{16,24},{4,20},{12,28},{1,9},{9,1},{17,25},{5,21},{13,... | collective-permute-start | bytes 884744 | tf_op jit(solution)/shard_map/ppermute | solution.py:250
  16.3 17.3 %slice-start = ((s8[4718592]{0:T(1024)(128)(4,1)}), s8[524288]{0:T(1024)(128)(4,1)S(1)}, s32[]{:S(2)}) async-start(s8[4718592]{0:T(1024)(128)(4,1)} %bitcast.3), calls=%async_computation | async-start | bytes 1048576
  16.9 16.6 %slice-start.1 = ((s8[4718592]{0:T(1024)(128)(4,1)}), s8[4194304]{0:T(1024)(128)(4,1)S(1)}, s32[]{:S(2)}) async-start(s8[4718592]{0:T(1024)(128)(4,1)} %bitcast.3), calls=%async_computation.1 | async-start | bytes 8388608
  16.9 9.0 %collective-permute-start.3 = (bf16[576,256]{1,0:T(8,128)(2,1)S(1)}, bf16[576,256]{1,0:T(8,128)(2,1)S(1)}, u32[]{:S(2)}, u32[]{:S(2)}) collective-permute-start(bf16[576,256]{1,0:T(8,128)(2,1)S(1)} %get-tuple-element.44.end_ref), channel_id=1, source_target_pairs={{0,8},{8,0},{16,24},{4,20},{12,28},{1,9},{9,1},{17,25},{5,21},{13,... | collective-permute-start | bytes 884744 | tf_op jit(solution)/shard_map/ppermute | solution.py:250
  22.9 7.8 %collective-permute-start.6 = (bf16[576,256]{1,0:T(8,128)(2,1)S(1)}, bf16[576,256]{1,0:T(8,128)(2,1)S(1)}, u32[]{:S(2)}, u32[]{:S(2)}) collective-permute-start(bf16[576,256]{1,0:T(8,128)(2,1)S(1)} %shard_map.71), channel_id=1, source_target_pairs={{0,16},{8,24},{4,12},{20,28},{28,20},{1,17},{9,25},{5,13},{21,29},... | collective-permute-start | bytes 884744 | tf_op jit(solution)/shard_map/ppermute | solution.py:261
  26.0 9.1 %collective-permute-start.4 = (bf16[576,256]{1,0:T(8,128)(2,1)S(1)}, bf16[576,256]{1,0:T(8,128)(2,1)S(1)}, u32[]{:S(2)}, u32[]{:S(2)}) collective-permute-start(bf16[576,256]{1,0:T(8,128)(2,1)S(1)} %shard_map.69), channel_id=1, source_target_pairs={{0,16},{8,24},{4,12},{20,28},{28,20},{1,17},{9,25},{5,13},{21,29},... | collective-permute-start | bytes 884744 | tf_op jit(solution)/shard_map/ppermute | solution.py:261
  30.8 2.8 %collective-permute-start.7 = (bf16[2,32,256]{2,1,0:T(8,128)(2,1)S(1)}, bf16[2,32,256]{2,1,0:T(8,128)(2,1)S(1)}, u32[]{:S(2)}, u32[]{:S(2)}) collective-permute-start(bf16[2,32,256]{2,1,0:T(8,128)(2,1)S(1)} %get-tuple-element.49), channel_id=1, source_target_pairs={{0,4},{4,0},{1,5},{5,1},{2,6},{6,2},{3,7},{7,3},{8,12},{12,8},{9,1... | collective-permute-start | bytes 98312 | tf_op jit(solution)/shard_map/ppermute | solution.py:52
  35.3 2.7 %collective-permute-start.8 = (bf16[2,32,256]{2,1,0:T(8,128)(2,1)S(1)}, bf16[2,32,256]{2,1,0:T(8,128)(2,1)S(1)}, u32[]{:S(2)}, u32[]{:S(2)}) collective-permute-start(bf16[2,32,256]{2,1,0:T(8,128)(2,1)S(1)} %get-tuple-element.57), channel_id=1, source_target_pairs={{0,4},{4,0},{1,5},{5,1},{2,6},{6,2},{3,7},{7,3},{8,12},{12,8},{9,1... | collective-permute-start | bytes 98312 | tf_op jit(solution)/shard_map/ppermute | solution.py:52

commit v8 on v7

--- a/solution.py
+++ b/solution.py
@@ -14,6 +14,7 @@
 HBM = pl.BlockSpec(memory_space=pltpu.HBM)
 LANES = 256
 EDGES_COST = 2_000_000_000
+RELAY_COST = 3_000_000_000
 
 
 def call(kernel, out_shape, *args, scratch=(), flops=0, out_specs=None, aliases=None):
@@ -166,7 +167,7 @@
 
 
 def drive_kernel(
-    lanes, lhs_ref, weight_ref, total_ref, spill_ref, pole_ref, drive_ref, beside_ref, end_ref
+    lanes, lhs_ref, weight_ref, total_ref, spill_ref, pole_ref, drive_ref, beside_ref, *end_refs
 ):
     count, rows, cols, wide = drive_ref.shape
     room, size = count * rows, rows * cols
@@ -189,9 +190,13 @@
         state = decay * state + total[frame]
         left_state = decay * left_state + left[frame]
         right_state = decay * right_state + right[frame]
-    end_ref[:size] = state.reshape(size, wide).astype(end_ref.dtype)
-    end_ref[size : size + rows] = left_state.astype(end_ref.dtype)
-    end_ref[size + rows :] = right_state.astype(end_ref.dtype)
+    at = 0
+    for end_ref in end_refs:
+        piece = slice(at, at + end_ref.shape[1])
+        at = piece.stop
+        end_ref[:size] = state.reshape(size, wide)[:, piece].astype(end_ref.dtype)
+        end_ref[size : size + rows] = left_state[:, piece].astype(end_ref.dtype)
+        end_ref[size + rows :] = right_state[:, piece].astype(end_ref.dtype)
 
 
 def entry_kernel(frames, ends_ref, pole_ref, out_ref):
@@ -211,7 +216,14 @@
         functools.partial(entry_kernel, frames), of(shares.shape, end.dtype), shares, pole
     )
     entry = lax.all_to_all(entries, "tm", 0, 0).reshape(end.shape)
-    return [(part,) for part in jnp.split(entry, len(ends), axis=1)]
+    return [(part,) for part in jnp.split(entry, pieces_at(ends), axis=1)]
+
+
+def pieces_at(ends):
+    at = [0]
+    for end in ends:
+        at.append(at[-1] + end.shape[1])
+    return at[1:-1]
 
 
 def pick(values):
@@ -230,8 +242,8 @@
     return by_one * one[...].astype(jnp.float32) + by_other * other[...].astype(jnp.float32)
 
 
-def relay_kernel(frames, part, end_ref, got_ref, pole_ref, out_ref):
-    rate = rate_of(pole_ref)[:, part * LANES : (part + 1) * LANES]
+def relay_kernel(frames, lanes, end_ref, got_ref, pole_ref, out_ref):
+    rate = rate_of(pole_ref)[:, lanes]
     carried, twice = jnp.exp(frames * rate), jnp.exp(2 * frames * rate)
     none, same = jnp.zeros_like(rate), jnp.ones_like(rate)
     own = on_core(pick([carried, same, same, same]), pick([same, same, same, none]))
@@ -250,27 +262,35 @@
     got = [lax.ppermute(end, axes, first_round) for end in ends]
     relayed = [
         call(
-            functools.partial(relay_kernel, frames, part),
+            functools.partial(relay_kernel, frames, slice(at, at + end.shape[1])),
             of(end.shape, end.dtype),
             end,
             here,
             pole,
+            flops=RELAY_COST,
         )
-        for part, (end, here) in enumerate(zip(ends, got))
+        for at, end, here in zip([0, *pieces_at(ends)], ends, got)
     ]
     return [(here, lax.ppermute(end, axes, second_round)) for here, end in zip(got, relayed)]
 
 
 class Mix:
-    def __init__(self, lanes, count, arrived_refs, pole_ref, scale_ref):
+    def __init__(self, lanes, rounds, count, arrived_refs, pole_ref, scale_ref):
+        self.rounds = rounds
         self.rate = rate_of(pole_ref)[:, lanes]
         self.scale = scale_ref[:, lanes]
         self.count = count
         self.arrived_refs = arrived_refs
 
     def entry(self, rows):
-        parts = [ref[rows].astype(jnp.float32) for ref in self.arrived_refs]
-        if len(parts) == 1:
+        parts = [
+            jnp.concatenate(
+                [ref[rows].astype(jnp.float32) for ref in self.arrived_refs[start :: self.rounds]],
+                axis=1,
+            )
+            for start in range(self.rounds)
+        ]
+        if self.rounds == 1:
             return parts[0]
         carried = jnp.exp(self.count * self.rate)
         none, same = jnp.zeros_like(self.rate), jnp.ones_like(self.rate)
@@ -287,13 +307,13 @@
             yield jax.nn.gelu(self.scale * state)
 
 
-def beside_kernel(lanes, *refs):
+def beside_kernel(lanes, rounds, *refs):
     drive_ref, beside_ref, start_ref, sides_ref, pole_ref, scale_ref, *arrived_refs = refs[:-2]
     give_ref, out_ref = refs[-2:]
     count, rows, cols, wide = drive_ref.shape
     size = rows * cols
     inner = inner_row(rows)
-    mix = Mix(lanes, count, arrived_refs, pole_ref, scale_ref)
+    mix = Mix(lanes, rounds, count, arrived_refs, pole_ref, scale_ref)
     chip, chips = lax.axis_index("sy"), lax.axis_size("sy")
     row = lax.broadcasted_iota(jnp.int32, (2 * rows, wide), 0)
     side = jnp.where(row < rows, (chip > 0).astype(jnp.float32), (chip < chips - 1).astype(jnp.float32))
@@ -316,10 +336,10 @@
         give_ref[frame, cols:] = ends.astype(give_ref.dtype)
 
 
-def mixed_kernel(lanes, *refs):
+def mixed_kernel(lanes, rounds, *refs):
     drive_ref, start_ref, pole_ref, scale_ref, *arrived_refs, out_ref = refs
     count, rows, cols, _ = drive_ref.shape
-    mix = Mix(lanes, count, arrived_refs, pole_ref, scale_ref)
+    mix = Mix(lanes, rounds, count, arrived_refs, pole_ref, scale_ref)
     block = 8
     for row in range(0, rows, block):
         here = slice(row, row + block)
@@ -437,26 +457,30 @@
         swap_cores(mine),
     )
     parts = [slice(lane, lane + LANES) for lane in range(0, channels, LANES)]
-    drives, besides, ends = zip(
-        *(
-            call(
-                functools.partial(drive_kernel, lanes),
-                (
-                    of((count, rows, cols, LANES), jnp.float32),
-                    of((count, 2 * rows, LANES), jnp.float32),
-                    of((size + 2 * rows, LANES), narrow),
-                ),
-                halo,
-                input_weight,
-                total,
-                spill,
-                pole,
-                flops=36 * room * channels * LANES,
-            )
-            for lanes in parts
+    pieces = [[LANES // 2] * 2, *[[LANES]] * (len(parts) - 1)]
+    drives, besides, ends = [], [], []
+    for lanes, widths in zip(parts, pieces):
+        drive, beside, *end = call(
+            functools.partial(drive_kernel, lanes),
+            (
+                of((count, rows, cols, LANES), jnp.float32),
+                of((count, 2 * rows, LANES), jnp.float32),
+                *[of((size + 2 * rows, width), narrow) for width in widths],
+            ),
+            halo,
+            input_weight,
+            total,
+            spill,
+            pole,
+            flops=36 * room * channels * LANES,
         )
-    )
-    arrivals = (exchange_four if lax.axis_size("tm") == 4 else exchange)(ends, pole, count)
+        drives.append(drive)
+        besides.append(beside)
+        ends += end
+    pairs = (exchange_four if lax.axis_size("tm") == 4 else exchange)(ends, pole, count)
+    rounds = len(pairs[0])
+    pairs = iter(pairs)
+    arrivals = [[each for _ in widths for each in next(pairs)] for widths in pieces]
 
     sums, lhs = [None] * len(parts), None
     inner = of((count, rows, cols, LANES), jnp.float32)
@@ -465,7 +489,7 @@
         if lhs is not None:
             *arrived, sums[0] = lax.optimization_barrier((*arrived, sums[0]))
         give, edge = call(
-            functools.partial(beside_kernel, lanes),
+            functools.partial(beside_kernel, lanes, rounds),
             (of((count, 2 * cols, LANES), narrow), of(beside.shape, narrow)),
             drive,
             beside,
@@ -488,7 +512,7 @@
                 )
         got = swap_cores(give)
         mixed = call(
-            functools.partial(mixed_kernel, lanes),
+            functools.partial(mixed_kernel, lanes, rounds),
             of(drive.shape, narrow),
             drive,
             start_state,
@@ -505,7 +529,7 @@
                 edge,
                 output_weight,
                 *([] if sums[0] is None else [sums[0]]),
-                flops=18 * drive.size * LANES,
+                flops=36 * drive.size * LANES,
             )
             before = lanes
     return call(

time: 42 us -> 46.4 us (1.10)
  starting transfers between devices: 14.1 us -> 23 us
  waiting for transfers between devices: 10.3 us -> 5.71 us
    ppermute x4, starting transfers between devices: 3.42 us -> 8.01 us  [swap_cores(): return lax.ppermute(array, 'sx', [(0, 1), (1, 0)])]
    ppermute x2 -> x3, waiting for transfers between devices: 5.35 us -> 1.66 us  [exchange_four(): got = [lax.ppermute(end, axes, first_round) for end in ends]]
    ppermute x2 -> x3, starting transfers between devices: 4.38 us -> 7.65 us  [exchange_four(): lax.ppermute(end, axes, second_round)]
    ppermute x2 -> x3, starting transfers between devices: 2.85 us -> 3.88 us  [exchange_four(): got = [lax.ppermute(end, axes, first_round) for end in ends]]
    ppermute x2 -> x3, waiting for transfers between devices: 2.14 us -> 1.2 us  [exchange_four(): lax.ppermute(end, axes, second_round)]
    pallas_call x15 -> x16, Pallas kernels: 15.5 us -> 15.6 us  [call(): pl.pallas_call(kernel, in_specs=[WHOLE] * len(args), out_specs=out_specs...]
  transfers between devices with their start and end apart: 9 -> 11, of which waited for: 6 -> 6; matrix products, arithmetic and copies ran while one was open for 0% -> 0% of each run, Pallas kernels for 25% -> 22%
where the time goes in v8:
time: 46.4 us; the launch traced here: 46.1 us
  starting transfers between devices  23 us (50%)
  Pallas kernels  15.6 us (34%)
  waiting for transfers between devices  5.71 us (12%)
  local copies, waits for them, and re-layouts  1.42 us (3%)
    pallas_call x16, Pallas kernels, call(): pl.pallas_call(kernel, in_specs=[WHOLE] * len(args), out_specs=out_specs...  15.6 us
    ppermute x4, starting transfers between devices, swap_cores(): return lax.ppermute(array, 'sx', [(0, 1), (1, 0)])  8.01 us
    ppermute x3, starting transfers between devices, exchange_four(): lax.ppermute(end, axes, second_round)  7.65 us
    ppermute x3, starting transfers between devices, exchange_four(): got = [lax.ppermute(end, axes, first_round) for end in ends]  3.88 us
    ppermute x1, starting transfers between devices, trade_columns(): return (got, lax.ppermute(columns, ('sx', 'sy'), pairs))  3.46 us
    ppermute x4, waiting for transfers between devices, swap_cores(): return lax.ppermute(array, 'sx', [(0, 1), (1, 0)])  2.85 us
    ppermute x3, waiting for transfers between devices, exchange_four(): got = [lax.ppermute(end, axes, first_round) for end in ends]  1.66 us
    unnamed x14, local copies, waits for them, and re-layouts  1.41 us
  transfers between devices with their start and end apart: 11, of which 6 were waited for; matrix products, arithmetic and copies ran while one was open for 0% of the time, Pallas kernels for 22%

profile of v8, /device:TPU:23, one launch (start us, length us, event | category | flops | bytes accessed | tf_op | source)
XLA Modules:
  0.0 46.1 jit_solution(9880690732163398370)
XLA Ops:
  0.0 0.0 copy-start
  0.0 0.0 copy-start.1
  0.0 0.0 copy-start.4
  0.0 1.4 %copy-done.4 = bf16[2,32,16,512]{3,2,1,0:T(8,128)(2,1)S(1)} copy-done((bf16[2,32,16,512]{3,2,1,0:T(8,128)(2,1)S(1)}, bf16[2,32,16,512]{3,2,1,0:T(8,128)(2,1)}, u32[]{:S(2)}) %copy-start.4) | copy-done | bytes 1048600
  1.4 0.3 shard_map.64
  1.7 0.0 copy-done
  1.7 0.3 shard_map.65
  2.0 0.7 %collective-permute-start = (bf16[192,512]{1,0:T(8,128)(2,1)S(1)}, bf16[192,512]{1,0:T(8,128)(2,1)S(1)}, u32[]{:S(2)}, u32[]{:S(2)}) collective-permute-start(bf16[192,512]{1,0:T(8,128)(2,1)S(1)} %get-tuple-element.37), channel_id=1, source_target_pairs={{0,4},{4,0},{1,5},{5,1},{2,6},{6,2},{3,7},{7,3},{8,12},{12,8},{9,1... | collective-permute-start | bytes 589832 | tf_op jit(solution)/shard_map/ppermute | solution.py:53
  2.8 1.1 %collective-permute-done.got_ref = bf16[192,512]{1,0:T(8,128)(2,1)S(1)} collective-permute-done((bf16[192,512]{1,0:T(8,128)(2,1)S(1)}, bf16[192,512]{1,0:T(8,128)(2,1)S(1)}, u32[]{:S(2)}, u32[]{:S(2)}) %collective-permute-start) | collective-permute-done | bytes 196640 | tf_op jit(solution)/shard_map/ppermute | solution.py:53
  3.9 0.0 copy-start.2
  3.9 3.5 %collective-permute-start.1 = (bf16[5,64,512]{2,1,0:T(8,128)(2,1)S(1)}, bf16[5,64,512]{2,1,0:T(8,128)(2,1)S(1)}, u32[]{:S(2)}, u32[]{:S(2)}) collective-permute-start(bf16[5,64,512]{2,1,0:T(8,128)(2,1)S(1)} %pad_maximum_fusion), channel_id=1, source_target_pairs={{1,4},{2,5},{3,6},{4,1},{5,2},{6,3},{9,12},{10,13},{11,14},{12,9},... | collective-permute-start | bytes 983048 | tf_op jit(solution)/shard_map/ppermute | solution.py:97
  7.3 0.0 copy-done.1
  7.4 5.1 %shard_map.66 = (f32[2,32,16,512]{3,2,1,0:T(8,128)S(1)}, f32[2,64,512]{2,1,0:T(8,128)S(1)}) custom-call(bf16[2,32,16,512]{3,2,1,0:T(8,128)(2,1)S(1)} %copy-done.4, bf16[192,512]{1,0:T(8,128)(2,1)S(1)} %collective-permute-done.got_ref, bf16[3,3,512,512]{3,2,1,0:T(8,128)(2,1)S(1)} %copy-done.1), custom_call_target="tpu_custom_call" | custom-call | flops 4831838208 | bytes 8323072 | tf_op jit(solution)/shard_map/pallas_call | solution.py:23
  12.4 0.0 collective-permute-done.1.mine_ref
  12.4 0.2 collective-permute-start.2
  12.6 1.5 %collective-permute-done.2.theirs_ref = bf16[5,64,512]{2,1,0:T(8,128)(2,1)S(1)} collective-permute-done((bf16[5,64,512]{2,1,0:T(8,128)(2,1)S(1)}, bf16[5,64,512]{2,1,0:T(8,128)(2,1)S(1)}, u32[]{:S(2)}, u32[]{:S(2)}) %collective-permute-start.2) | collective-permute-done | bytes 327712 | tf_op jit(solution)/shard_map/ppermute | solution.py:53
  14.1 0.2 shard_map.67
  14.3 0.0 copy-done.2
  14.3 0.6 %shard_map.70 = (f32[2,32,16,256]{3,2,1,0:T(8,128)S(1)}, f32[2,64,256]{2,1,0:T(8,128)S(1)}, bf16[576,128]{1,0:T(8,128)(2,1)S(1)}, bf16[576,128]{1,0:T(8,128)(2,1)S(1)}) custom-call(bf16[256,1536]{1,0:T(8,128)(2,1)S(1)} %get-tuple-element.41.lhs_ref, bf16[3,3,512,512]{3,2,1,0:T(8,128)(2,1)S(1)} %copy-done.1, ...), custom_call_target="tpu_custom_call" | custom-call | flops 301989888 | bytes 9340928 | tf_op jit(solution)/shard_map/pallas_call | solution.py:23
  15.0 1.3 %collective-permute-start.5 = (bf16[576,128]{1,0:T(8,128)(2,1)S(1)}, bf16[576,128]{1,0:T(8,128)(2,1)S(1)}, u32[]{:S(2)}, u32[]{:S(2)}) collective-permute-start(bf16[576,128]{1,0:T(8,128)(2,1)S(1)} %get-tuple-element.47.end_ref), channel_id=1, source_target_pairs={{0,8},{8,0},{16,24},{4,20},{12,28},{1,9},{9,1},{17,25},{5,21},{13,... | collective-permute-start | bytes 442376 | tf_op jit(solution)/shard_map/ppermute | solution.py:262
  16.3 1.3 %collective-permute-start.7 = (bf16[576,128]{1,0:T(8,128)(2,1)S(1)}, bf16[576,128]{1,0:T(8,128)(2,1)S(1)}, u32[]{:S(2)}, u32[]{:S(2)}) collective-permute-start(bf16[576,128]{1,0:T(8,128)(2,1)S(1)} %get-tuple-element.48.end_ref), channel_id=1, source_target_pairs={{0,8},{8,0},{16,24},{4,20},{12,28},{1,9},{9,1},{17,25},{5,21},{13,... | collective-permute-start | bytes 442376 | tf_op jit(solution)/shard_map/ppermute | solution.py:262
  17.6 0.6 %shard_map.68 = (f32[2,32,16,256]{3,2,1,0:T(8,128)S(1)}, f32[2,64,256]{2,1,0:T(8,128)S(1)}, bf16[576,256]{1,0:T(8,128)(2,1)S(1)}) custom-call(bf16[256,1536]{1,0:T(8,128)(2,1)S(1)} %get-tuple-element.41.lhs_ref, bf16[3,3,512,512]{3,2,1,0:T(8,128)(2,1)S(1)} %copy-done.1, f32[2,32,16,512]{3,2,1,0:T(8,128)S(1)} %get-tuple-element.42.total_ref, ...), custom_call_target="tpu_custom_call" | custom-call | flops 301989888 | bytes 9340928 | tf_op jit(solution)/shard_map/pallas_call | solution.py:23
  18.2 1.3 %collective-permute-start.3 = (bf16[576,256]{1,0:T(8,128)(2,1)S(1)}, bf16[576,256]{1,0:T(8,128)(2,1)S(1)}, u32[]{:S(2)}, u32[]{:S(2)}) collective-permute-start(bf16[576,256]{1,0:T(8,128)(2,1)S(1)} %get-tuple-element.45.end_ref), channel_id=1, source_target_pairs={{0,8},{8,0},{16,24},{4,20},{12,28},{1,9},{9,1},{17,25},{5,21},{13,... | collective-permute-start | bytes 884744 | tf_op jit(solution)/shard_map/ppermute | solution.py:262
  19.5 1.7 %collective-permute-done.5.got_ref.refs_4_.refs_6_ = bf16[576,128]{1,0:T(8,128)(2,1)S(1)} collective-permute-done((bf16[576,128]{1,0:T(8,128)(2,1)S(1)}, bf16[576,128]{1,0:T(8,128)(2,1)S(1)}, u32[]{:S(2)}, u32[]{:S(2)}) %collective-permute-start.5) | collective-permute-done | bytes 147488 | tf_op jit(solution)/shard_map/ppermute | solution.py:262
  21.1 0.1 shard_map.71
  21.2 1.9 %collective-permute-start.6 = (bf16[576,128]{1,0:T(8,128)(2,1)S(1)}, bf16[576,128]{1,0:T(8,128)(2,1)S(1)}, u32[]{:S(2)}, u32[]{:S(2)}) collective-permute-start(bf16[576,128]{1,0:T(8,128)(2,1)S(1)} %shard_map.71), channel_id=1, source_target_pairs={{0,16},{8,24},{4,12},{20,28},{28,20},{1,17},{9,25},{5,13},{21,29},... | collective-permute-start | bytes 442376 | tf_op jit(solution)/shard_map/ppermute | solution.py:274
  23.2 0.0 collective-permute-done.7.got_ref.refs_6_.refs_8_
  23.2 0.0 slice-start
  23.2 0.1 shard_map.72
  23.3 0.0 copy-start.3
  23.3 0.0 slice-start.1
  23.3 3.6 %collective-permute-start.8 = (bf16[576,128]{1,0:T(8,128)(2,1)S(1)}, bf16[576,128]{1,0:T(8,128)(2,1)S(1)}, u32[]{:S(2)}, u32[]{:S(2)}) collective-permute-start(bf16[576,128]{1,0:T(8,128)(2,1)S(1)} %shard_map.72), channel_id=1, source_target_pairs={{0,16},{8,24},{4,12},{20,28},{28,20},{1,17},{9,25},{5,13},{21,29},... | collective-permute-start | bytes 442376 | tf_op jit(solution)/shard_map/ppermute | solution.py:274
  26.9 0.0 collective-permute-done.3.got_ref.refs_4_.refs_6_
  26.9 0.1 shard_map.69
  27.1 2.1 %collective-permute-start.4 = (bf16[576,256]{1,0:T(8,128)(2,1)S(1)}, bf16[576,256]{1,0:T(8,128)(2,1)S(1)}, u32[]{:S(2)}, u32[]{:S(2)}) collective-permute-start(bf16[576,256]{1,0:T(8,128)(2,1)S(1)} %shard_map.69), channel_id=1, source_target_pairs={{0,16},{8,24},{4,12},{20,28},{28,20},{1,17},{9,25},{5,13},{21,29},... | collective-permute-start | bytes 884744 | tf_op jit(solution)/shard_map/ppermute | solution.py:274
  29.2 0.0 collective-permute-done.6.refs_5_.refs_7_
  29.2 0.5 %collective-permute-done.8.refs_7_.refs_9_ = bf16[576,128]{1,0:T(8,128)(2,1)S(1)} collective-permute-done((bf16[576,128]{1,0:T(8,128)(2,1)S(1)}, bf16[576,128]{1,0:T(8,128)(2,1)S(1)}, u32[]{:S(2)}, u32[]{:S(2)}) %collective-permute-start.8) | collective-permute-done | bytes 147488 | tf_op jit(solution)/shard_map/ppermute | solution.py:274
  29.7 0.0 copy-done.3
  29.7 0.1 shard_map.74
  29.9 1.6 %collective-permute-start.9 = (bf16[2,32,256]{2,1,0:T(8,128)(2,1)S(1)}, bf16[2,32,256]{2,1,0:T(8,128)(2,1)S(1)}, u32[]{:S(2)}, u32[]{:S(2)}) collective-permute-start(bf16[2,32,256]{2,1,0:T(8,128)(2,1)S(1)} %get-tuple-element.51), channel_id=1, source_target_pairs={{0,4},{4,0},{1,5},{5,1},{2,6},{6,2},{3,7},{7,3},{8,12},{12,8},{9,1... | collective-permute-start | bytes 98312 | tf_op jit(solution)/shard_map/ppermute | solution.py:53
  31.5 0.6 %shard_map.73.cells_ref = bf16[2,32,16,256]{3,2,1,0:T(8,128)(2,1)S(1)} custom-call(f32[2,32,16,256]{3,2,1,0:T(8,128)S(1)} %get-tuple-element.46.refs_0_, f32[32,16,512]{2,1,0:T(8,128)S(1)} %copy-done, s32[1,512]{1,0:T(1,128)S(1)} %bitcast.11, f32[1,512]{1,0:T(1,128)S(1)} %bitcast.15, bf16[576,128]{1,0:T(8,128)(2,1)S(1)} %collective-permute-done.5.got_ref.refs_4_.refs_6_, ...), custom_call_target="tpu_custom_call" | custom-call | bytes 3215360 | tf_op jit(solution)/shard_map/pallas_call | solution.py:23
  32.0 0.3 collective-permute-done.9.got_ref
  32.3 0.0 slice-done
  32.3 0.0 slice-done.1
  32.3 1.6 %shard_map.75 = (f32[2,32,16,256]{3,2,1,0:T(8,128)S(1)}, bf16[1152,768]{1,0:T(8,128)(2,1)S(1)}) custom-call(bf16[2,32,16,256]{3,2,1,0:T(8,128)(2,1)S(1)} %shard_map.73.cells_ref, bf16[2,32,256]{2,1,0:T(8,128)(2,1)S(1)} %collective-permute-done.9.got_ref, bf16[2,64,256]{2,1,0:T(8,128)(2,1)S(1)} %get-tuple-element.52.beside_ref, ...), custom_call_target="tpu_custom_call" | custom-call | flops 2415919104 | bytes 8159232 | tf_op jit(solution)/shard_map/pallas_call | solution.py:23
  33.9 0.7 %collective-permute-done.4.refs_5_.refs_7_ = bf16[576,256]{1,0:T(8,128)(2,1)S(1)} collective-permute-done((bf16[576,256]{1,0:T(8,128)(2,1)S(1)}, bf16[576,256]{1,0:T(8,128)(2,1)S(1)}, u32[]{:S(2)}, u32[]{:S(2)}) %collective-permute-start.4) | collective-permute-done | bytes 294944 | tf_op jit(solution)/shard_map/ppermute | solution.py:274
  34.5 0.1 shard_map.77
  34.7 5.5 %collective-permute-start.10 = (bf16[2,32,256]{2,1,0:T(8,128)(2,1)S(1)}, bf16[2,32,256]{2,1,0:T(8,128)(2,1)S(1)}, u32[]{:S(2)}, u32[]{:S(2)}) collective-permute-start(bf16[2,32,256]{2,1,0:T(8,128)(2,1)S(1)} %get-tuple-element.59), channel_id=1, source_target_pairs={{0,4},{4,0},{1,5},{5,1},{2,6},{6,2},{3,7},{7,3},{8,12},{12,8},{9,1... | collective-permute-start | bytes 98312 | tf_op jit(solution)/shard_map/ppermute | solution.py:53
  40.2 1.5 %shard_map.78.refs_1_ = f32[2,32,16,256]{3,2,1,0:T(8,128)S(1)} custom-call(bf16[1152,768]{1,0:T(8,128)(2,1)S(1)} %get-tuple-element.62.lhs_ref, bf16[3,3,512,512]{3,2,1,0:T(8,128)(2,1)S(1)} %bitcast.4), custom_call_target="tpu_custom_call" | custom-call | flops 1207959552 | bytes 7536640 | tf_op jit(solution)/shard_map/pallas_call | solution.py:23
  41.7 0.6 %shard_map.76.cells_ref = bf16[2,32,16,256]{3,2,1,0:T(8,128)(2,1)S(1)} custom-call(f32[2,32,16,256]{3,2,1,0:T(8,128)S(1)} %get-tuple-element.44.refs_0_, f32[32,16,512]{2,1,0:T(8,128)S(1)} %copy-done, s32[1,512]{1,0:T(1,128)S(1)} %bitcast.13, f32[1,512]{1,0:T(1,128)S(1)} %bitcast.17, bf16[576,256]{1,0:T(8,128)(2,1)S(1)} %collective-permute-done.3.got_ref.refs_4_.refs_6_, ...), custom_call_target="tpu_custom_call" | custom-call | bytes 3215360 | tf_op jit(solution)/shard_map/pallas_call | solution.py:23
  42.3 0.0 collective-permute-done.10.got_ref
  42.3 3.7 %shard_map.79 = bf16[2,32,16,512]{3,2,1,0:T(8,128)(2,1)} custom-call(bf16[2,32,16,256]{3,2,1,0:T(8,128)(2,1)S(1)} %shard_map.76.cells_ref, bf16[2,32,256]{2,1,0:T(8,128)(2,1)S(1)} %collective-permute-done.10.got_ref, bf16[2,64,256]{2,1,0:T(8,128)(2,1)S(1)} %get-tuple-element.60.beside_ref, bf16[3,3,512,512]{3,2,1,0:T(8,128)(2,1)S(1)} %bitcast.4, ...), custom_call_target="tpu_custom_call" | custom-call | flops 2415919104 | bytes 8486912 | tf_op jit(solution)/shard_map/pallas_call | solution.py:23
  (3 shorter events, 0.0 us)
Async XLA Ops:
  0.0 1.7 %copy-start = (f32[32,16,512]{2,1,0:T(8,128)S(1)}, f32[32,16,512]{2,1,0:T(8,128)}, u32[]{:S(2)}) copy-start(f32[32,16,512]{2,1,0:T(8,128)} %refs_2_.3) | copy-start | bytes 3145732
  0.0 7.3 %copy-start.1 = (bf16[3,3,512,512]{3,2,1,0:T(8,128)(2,1)S(1)}, bf16[3,3,512,512]{3,2,1,0:T(8,128)(2,1)}, u32[]{:S(2)}) copy-start(bf16[3,3,512,512]{3,2,1,0:T(8,128)(2,1)} %weight_ref.8) | copy-start | bytes 14155780
  0.0 1.4 %copy-start.4 = (bf16[2,32,16,512]{3,2,1,0:T(8,128)(2,1)S(1)}, bf16[2,32,16,512]{3,2,1,0:T(8,128)(2,1)}, u32[]{:S(2)}) copy-start(bf16[2,32,16,512]{3,2,1,0:T(8,128)(2,1)} %cells_ref.3) | copy-start | bytes 3145732
  2.0 1.8 %collective-permute-start = (bf16[192,512]{1,0:T(8,128)(2,1)S(1)}, bf16[192,512]{1,0:T(8,128)(2,1)S(1)}, u32[]{:S(2)}, u32[]{:S(2)}) collective-permute-start(bf16[192,512]{1,0:T(8,128)(2,1)S(1)} %get-tuple-element.37), channel_id=1, source_target_pairs={{0,4},{4,0},{1,5},{5,1},{2,6},{6,2},{3,7},{7,3},{8,12},{12,8},{9,1... | collective-permute-start | bytes 589832 | tf_op jit(solution)/shard_map/ppermute | solution.py:53
  3.9 10.5 %copy-start.2 = (s32[512]{0:T(512)S(1)}, s32[512]{0:T(512)}, u32[]{:S(2)}) copy-start(s32[512]{0:T(512)} %param.9) | copy-start | bytes 6148
  3.9 8.6 %collective-permute-start.1 = (bf16[5,64,512]{2,1,0:T(8,128)(2,1)S(1)}, bf16[5,64,512]{2,1,0:T(8,128)(2,1)S(1)}, u32[]{:S(2)}, u32[]{:S(2)}) collective-permute-start(bf16[5,64,512]{2,1,0:T(8,128)(2,1)S(1)} %pad_maximum_fusion), channel_id=1, source_target_pairs={{1,4},{2,5},{3,6},{4,1},{5,2},{6,3},{9,12},{10,13},{11,14},{12,9},... | collective-permute-start | bytes 983048 | tf_op jit(solution)/shard_map/ppermute | solution.py:97
  12.4 1.7 %collective-permute-start.2 = (bf16[5,64,512]{2,1,0:T(8,128)(2,1)S(1)}, bf16[5,64,512]{2,1,0:T(8,128)(2,1)S(1)}, u32[]{:S(2)}, u32[]{:S(2)}) collective-permute-start(bf16[5,64,512]{2,1,0:T(8,128)(2,1)S(1)} %collective-permute-done.1.mine_ref), channel_id=1, source_target_pairs={{0,4},{4,0},{1,5},{5,1},{2,6},{6,2},{3,7},{7,3},{8,12},{12,8},{9,1... | collective-permute-start | bytes 983048 | tf_op jit(solution)/shard_map/ppermute | solution.py:53
  15.0 6.2 %collective-permute-start.5 = (bf16[576,128]{1,0:T(8,128)(2,1)S(1)}, bf16[576,128]{1,0:T(8,128)(2,1)S(1)}, u32[]{:S(2)}, u32[]{:S(2)}) collective-permute-start(bf16[576,128]{1,0:T(8,128)(2,1)S(1)} %get-tuple-element.47.end_ref), channel_id=1, source_target_pairs={{0,8},{8,0},{16,24},{4,20},{12,28},{1,9},{9,1},{17,25},{5,21},{13,... | collective-permute-start | bytes 442376 | tf_op jit(solution)/shard_map/ppermute | solution.py:262
  16.3 6.9 %collective-permute-start.7 = (bf16[576,128]{1,0:T(8,128)(2,1)S(1)}, bf16[576,128]{1,0:T(8,128)(2,1)S(1)}, u32[]{:S(2)}, u32[]{:S(2)}) collective-permute-start(bf16[576,128]{1,0:T(8,128)(2,1)S(1)} %get-tuple-element.48.end_ref), channel_id=1, source_target_pairs={{0,8},{8,0},{16,24},{4,20},{12,28},{1,9},{9,1},{17,25},{5,21},{13,... | collective-permute-start | bytes 442376 | tf_op jit(solution)/shard_map/ppermute | solution.py:262
  18.2 8.7 %collective-permute-start.3 = (bf16[576,256]{1,0:T(8,128)(2,1)S(1)}, bf16[576,256]{1,0:T(8,128)(2,1)S(1)}, u32[]{:S(2)}, u32[]{:S(2)}) collective-permute-start(bf16[576,256]{1,0:T(8,128)(2,1)S(1)} %get-tuple-element.45.end_ref), channel_id=1, source_target_pairs={{0,8},{8,0},{16,24},{4,20},{12,28},{1,9},{9,1},{17,25},{5,21},{13,... | collective-permute-start | bytes 884744 | tf_op jit(solution)/shard_map/ppermute | solution.py:262
  21.2 8.0 %collective-permute-start.6 = (bf16[576,128]{1,0:T(8,128)(2,1)S(1)}, bf16[576,128]{1,0:T(8,128)(2,1)S(1)}, u32[]{:S(2)}, u32[]{:S(2)}) collective-permute-start(bf16[576,128]{1,0:T(8,128)(2,1)S(1)} %shard_map.71), channel_id=1, source_target_pairs={{0,16},{8,24},{4,12},{20,28},{28,20},{1,17},{9,25},{5,13},{21,29},... | collective-permute-start | bytes 442376 | tf_op jit(solution)/shard_map/ppermute | solution.py:274
  23.2 9.2 %slice-start = ((s8[4718592]{0:T(1024)(128)(4,1)}), s8[4194304]{0:T(1024)(128)(4,1)S(1)}, s32[]{:S(2)}) async-start(s8[4718592]{0:T(1024)(128)(4,1)} %bitcast.3), calls=%async_computation | async-start | bytes 8388608
  23.3 6.5 %copy-start.3 = (f32[512]{0:T(512)S(1)}, f32[512]{0:T(512)}, u32[]{:S(2)}) copy-start(f32[512]{0:T(512)} %param.10) | copy-start | bytes 6148
  23.3 9.0 %slice-start.1 = ((s8[4718592]{0:T(1024)(128)(4,1)}), s8[524288]{0:T(1024)(128)(4,1)S(1)}, s32[]{:S(2)}) async-start(s8[4718592]{0:T(1024)(128)(4,1)} %bitcast.3), calls=%async_computation.1 | async-start | bytes 1048576
  23.3 6.4 %collective-permute-start.8 = (bf16[576,128]{1,0:T(8,128)(2,1)S(1)}, bf16[576,128]{1,0:T(8,128)(2,1)S(1)}, u32[]{:S(2)}, u32[]{:S(2)}) collective-permute-start(bf16[576,128]{1,0:T(8,128)(2,1)S(1)} %shard_map.72), channel_id=1, source_target_pairs={{0,16},{8,24},{4,12},{20,28},{28,20},{1,17},{9,25},{5,13},{21,29},... | collective-permute-start | bytes 442376 | tf_op jit(solution)/shard_map/ppermute | solution.py:274
  27.1 7.5 %collective-permute-start.4 = (bf16[576,256]{1,0:T(8,128)(2,1)S(1)}, bf16[576,256]{1,0:T(8,128)(2,1)S(1)}, u32[]{:S(2)}, u32[]{:S(2)}) collective-permute-start(bf16[576,256]{1,0:T(8,128)(2,1)S(1)} %shard_map.69), channel_id=1, source_target_pairs={{0,16},{8,24},{4,12},{20,28},{28,20},{1,17},{9,25},{5,13},{21,29},... | collective-permute-start | bytes 884744 | tf_op jit(solution)/shard_map/ppermute | solution.py:274
  29.9 2.5 %collective-permute-start.9 = (bf16[2,32,256]{2,1,0:T(8,128)(2,1)S(1)}, bf16[2,32,256]{2,1,0:T(8,128)(2,1)S(1)}, u32[]{:S(2)}, u32[]{:S(2)}) collective-permute-start(bf16[2,32,256]{2,1,0:T(8,128)(2,1)S(1)} %get-tuple-element.51), channel_id=1, source_target_pairs={{0,4},{4,0},{1,5},{5,1},{2,6},{6,2},{3,7},{7,3},{8,12},{12,8},{9,1... | collective-permute-start | bytes 98312 | tf_op jit(solution)/shard_map/ppermute | solution.py:53
  34.7 7.6 %collective-permute-start.10 = (bf16[2,32,256]{2,1,0:T(8,128)(2,1)S(1)}, bf16[2,32,256]{2,1,0:T(8,128)(2,1)S(1)}, u32[]{:S(2)}, u32[]{:S(2)}) collective-permute-start(bf16[2,32,256]{2,1,0:T(8,128)(2,1)S(1)} %get-tuple-element.59), channel_id=1, source_target_pairs={{0,4},{4,0},{1,5},{5,1},{2,6},{6,2},{3,7},{7,3},{8,12},{12,8},{9,1... | collective-permute-start | bytes 98312 | tf_op jit(solution)/shard_map/ppermute | solution.py:53

commit v9 on v7

--- a/solution.py
+++ b/solution.py
@@ -96,17 +96,28 @@
     return got, lax.ppermute(columns, ("sx", "sy"), pairs)
 
 
-def fill(lhs_ref, at, cells_ref, frame, row):
-    _, rows, cols, channels = cells_ref.shape
+def put_cells(lhs_ref, at, size, cols, first, cells):
+    count, channels = cells.shape
+    upper, lower = min(count, size - cols - first), max(0, cols - first)
+    here = at + first
+    lhs_ref[here : here + count, channels : 2 * channels] = cells
+    lhs_ref[here + cols : here + cols + upper, :channels] = cells[:upper]
+    lhs_ref[here + lower - cols : here + count - cols, 2 * channels :] = cells[lower:]
+
+
+def put_row(lhs_ref, at, size, row):
+    cols, channels = row.shape
+    row = row.astype(jnp.float32)
+    last = slice(at + size - cols, at + size)
+    lhs_ref[at : at + cols, :channels] = (is_core(1) * row).astype(lhs_ref.dtype)
+    lhs_ref[last, 2 * channels :] = (is_core(0) * row).astype(lhs_ref.dtype)
+
+
+def taps_kernel(cells_ref, lhs_ref):
+    count, rows, cols, channels = cells_ref.shape
     size = rows * cols
-    row = row.astype(jnp.float32)
-    cells = cells_ref[frame].reshape(size, channels)
-    mid, low = slice(channels, 2 * channels), slice(2 * channels, 3 * channels)
-    lhs_ref[at : at + cols, :channels] = (is_core(1) * row).astype(lhs_ref.dtype)
-    lhs_ref[at + cols : at + size, :channels] = cells[: size - cols]
-    lhs_ref[at : at + size, mid] = cells
-    lhs_ref[at : at + size - cols, low] = cells[cols:]
-    lhs_ref[at + size - cols : at + size, low] = (is_core(0) * row).astype(lhs_ref.dtype)
+    for frame in range(count):
+        put_cells(lhs_ref, frame * size, size, cols, 0, cells_ref[frame].reshape(size, channels))
 
 
 def row_taps(column, above, below):
@@ -122,11 +133,11 @@
     return jnp.dot(lhs, weight, preferred_element_type=jnp.float32)
 
 
-def main_kernel(cells_ref, got_ref, weight_ref, total_ref, spill_ref, lhs_ref):
-    count, rows, cols, _ = cells_ref.shape
+def main_kernel(_, got_ref, weight_ref, total_ref, spill_ref, lhs_ref):
+    count, rows, cols, _ = total_ref.shape
     size = rows * cols
     for frame in range(count):
-        fill(lhs_ref, frame * size, cells_ref, frame, got_ref[frame * cols : (frame + 1) * cols])
+        put_row(lhs_ref, frame * size, size, got_ref[frame * cols : (frame + 1) * cols])
     tile = (count, rows, cols, LANES)
     col = lax.broadcasted_iota(jnp.int32, tile, 2)
     for lane in range(0, weight_ref.shape[-1], LANES):
@@ -317,8 +328,9 @@
 
 
 def mixed_kernel(lanes, *refs):
-    drive_ref, start_ref, pole_ref, scale_ref, *arrived_refs, out_ref = refs
-    count, rows, cols, _ = drive_ref.shape
+    drive_ref, start_ref, pole_ref, scale_ref, *arrived_refs, lhs_ref = refs
+    count, rows, cols, wide = drive_ref.shape
+    size, room = rows * cols, count * rows
     mix = Mix(lanes, count, arrived_refs, pole_ref, scale_ref)
     block = 8
     for row in range(0, rows, block):
@@ -326,14 +338,15 @@
         drives = [drive_ref[frame, here] for frame in range(count)]
         cells = slice(row * cols, (row + block) * cols)
         for frame, tile in enumerate(mix(drives, cells, start_ref[here, :, lanes])):
-            out_ref[frame, here] = tile.astype(out_ref.dtype)
-
-
-def fill_tile(lhs_ref, cells_ref, got_ref, beside_ref):
-    count, rows, cols, _ = cells_ref.shape
+            tile = tile.reshape(block * cols, wide).astype(lhs_ref.dtype)
+            put_cells(lhs_ref, room + frame * size, size, cols, row * cols, tile)
+
+
+def put_edges(lhs_ref, tile, got_ref, beside_ref):
+    count, rows, cols, _ = tile
     size, room = rows * cols, count * rows
     for frame in range(count):
-        fill(lhs_ref, room + frame * size, cells_ref, frame, got_ref[frame, :cols])
+        put_row(lhs_ref, room + frame * size, size, got_ref[frame, :cols])
         ends = got_ref[frame, cols:].astype(jnp.float32)
         beside = beside_ref[frame].astype(jnp.float32)
         for side, at in enumerate((0, room + count * size)):
@@ -359,9 +372,9 @@
     )
 
 
-def opening_kernel(inputs, lanes, has_before, cells_ref, got_ref, beside_ref, weight_ref, *refs):
+def opening_kernel(inputs, lanes, has_before, _, got_ref, beside_ref, weight_ref, *refs):
     *before_refs, out_ref, lhs_ref = refs
-    fill_tile(lhs_ref, cells_ref, got_ref, beside_ref)
+    put_edges(lhs_ref, out_ref.shape, got_ref, beside_ref)
     before_ref = before_refs[0] if has_before else None
     out_ref[...] = tile_sum(out_ref.shape, inputs, lanes, lhs_ref, weight_ref, before_ref)
 
@@ -372,10 +385,10 @@
     out_ref[...] = tile_sum(out_ref.shape, inputs, lanes, lhs_ref, weight_ref, before_ref)
 
 
-def result_kernel(inputs, outputs, cells_ref, got_ref, beside_ref, weight_ref, *refs):
+def result_kernel(inputs, outputs, _, got_ref, beside_ref, weight_ref, *refs):
     *before_refs, out_ref, lhs_ref, held_ref, sems = refs
-    count, rows, cols, _ = cells_ref.shape
-    fill_tile(lhs_ref, cells_ref, got_ref, beside_ref)
+    count, rows, cols, _ = held_ref.shape
+    put_edges(lhs_ref, held_ref.shape, got_ref, beside_ref)
 
     def store(frame, part):
         here = (frame, slice(None), slice(None), outputs[part])
@@ -420,16 +433,17 @@
         aliases={1: 0, 2: 1},
     )
     got, mine = trade_columns(give, keep, count * cols)
-    main = call(
+    taps = of((count * size, wide), narrow)
+    *main, _ = call(
         main_kernel,
-        (of(frames.shape, jnp.float32), of((2, room, channels), jnp.float32)),
-        frames,
+        (of(frames.shape, jnp.float32), of((2, room, channels), jnp.float32), taps),
+        call(taps_kernel, taps, frames),
         got,
         input_weight,
-        scratch=[pltpu.VMEM((count * size, wide), narrow)],
+        aliases={0: 2},
         flops=18 * frames.size * channels,
     )
-    mine, (total, spill) = lax.optimization_barrier((mine, main))
+    mine, total, spill = lax.optimization_barrier((mine, *main))
     halo, sides = call(
         halo_kernel,
         (of((4 * room, wide), narrow), of((2 * rows, channels), jnp.float32)),
@@ -460,7 +474,7 @@
 
     sums, lhs = [None] * len(parts), None
     inner = of((count, rows, cols, LANES), jnp.float32)
-    taps = (count * size + 2 * room, 3 * LANES)
+    taps = of((count * size + 2 * room, 3 * LANES), narrow)
     for lanes, drive, beside, arrived in zip(parts, drives, besides, arrivals):
         if lhs is not None:
             *arrived, sums[0] = lax.optimization_barrier((*arrived, sums[0]))
@@ -489,7 +503,7 @@
         got = swap_cores(give)
         mixed = call(
             functools.partial(mixed_kernel, lanes),
-            of(drive.shape, narrow),
+            taps,
             drive,
             start_state,
             pole,
@@ -499,31 +513,33 @@
         if lanes != parts[-1]:
             sums[0], lhs = call(
                 functools.partial(opening_kernel, lanes, parts[0], sums[0] is not None),
-                (inner, of(taps, narrow)),
+                (inner, taps),
                 mixed,
                 got,
                 edge,
                 output_weight,
                 *([] if sums[0] is None else [sums[0]]),
+                aliases={0: 1},
                 flops=18 * drive.size * LANES,
             )
             before = lanes
-    return call(
+    result, _ = call(
         functools.partial(result_kernel, parts[-1], parts),
-        of(frames.shape, narrow),
+        (of(frames.shape, narrow), taps),
         mixed,
         got,
         edge,
         output_weight,
         *([] if sums[0] is None else sums),
-        out_specs=HBM,
+        out_specs=(HBM, WHOLE),
+        aliases={0: 1},
         scratch=[
-            pltpu.VMEM(taps, narrow),
             pltpu.VMEM(frames.shape, narrow),
             pltpu.SemaphoreType.DMA((count, len(parts))),
         ],
-        flops=18 * mixed.size * channels,
-    )
+        flops=18 * drive.size * channels,
+    )
+    return result
 
 
 def solution(mesh):

time: 42 us -> 42.1 us (level)
    pallas_call x15 -> x16, Pallas kernels: 15.5 us -> 15.8 us  [call(): pl.pallas_call(kernel, in_specs=[WHOLE] * len(args), out_specs=out_specs...]
    unnamed x14 -> x16, local copies, waits for them, and re-layouts: 1.41 us -> 1.52 us
where the time goes in v9:
time: 42.1 us; the launch traced here: 41.9 us
  Pallas kernels  15.8 us (38%)
  starting transfers between devices  14.1 us (33%)
  waiting for transfers between devices  10.1 us (24%)
  local copies, waits for them, and re-layouts  1.53 us (4%)
    pallas_call x16, Pallas kernels, call(): pl.pallas_call(kernel, in_specs=[WHOLE] * len(args), out_specs=out_specs...  15.8 us
    ppermute x2, waiting for transfers between devices, exchange_four(): got = [lax.ppermute(end, axes, first_round) for end in ends]  5.46 us
    ppermute x2, starting transfers between devices, exchange_four(): lax.ppermute(end, axes, second_round)  4.39 us
    ppermute x4, starting transfers between devices, swap_cores(): return lax.ppermute(array, 'sx', [(0, 1), (1, 0)])  3.5 us
    ppermute x1, starting transfers between devices, trade_columns(): return (got, lax.ppermute(columns, ('sx', 'sy'), pairs))  3.46 us
    ppermute x2, starting transfers between devices, exchange_four(): got = [lax.ppermute(end, axes, first_round) for end in ends]  2.72 us
    ppermute x4, waiting for transfers between devices, swap_cores(): return lax.ppermute(array, 'sx', [(0, 1), (1, 0)])  2.47 us
    ppermute x2, waiting for transfers between devices, exchange_four(): lax.ppermute(end, axes, second_round)  2.13 us
  transfers between devices with their start and end apart: 9, of which 6 were waited for; matrix products, arithmetic and copies ran while one was open for 0% of the time, Pallas kernels for 25%

profile of v9, /device:TPU:23, one launch (start us, length us, event | category | flops | bytes accessed | tf_op | source)
XLA Modules:
  0.0 41.9 jit_solution(2613776710629066072)
XLA Ops:
  0.0 0.0 copy-start
  0.0 0.0 copy-start.2
  0.0 1.3 %copy-done.2 = bf16[2,32,16,512]{3,2,1,0:T(8,128)(2,1)S(1)} copy-done((bf16[2,32,16,512]{3,2,1,0:T(8,128)(2,1)S(1)}, bf16[2,32,16,512]{3,2,1,0:T(8,128)(2,1)}, u32[]{:S(2)}) %copy-start.2) | copy-done | bytes 1048600
  1.3 0.3 shard_map.64
  1.6 0.0 copy-start.3
  1.7 0.0 copy-done
  1.7 0.3 shard_map.65
  2.0 0.0 copy-start.1
  2.0 0.7 %collective-permute-start = (bf16[192,512]{1,0:T(8,128)(2,1)S(1)}, bf16[192,512]{1,0:T(8,128)(2,1)S(1)}, u32[]{:S(2)}, u32[]{:S(2)}) collective-permute-start(bf16[192,512]{1,0:T(8,128)(2,1)S(1)} %get-tuple-element.37), channel_id=1, source_target_pairs={{0,4},{4,0},{1,5},{5,1},{2,6},{6,2},{3,7},{7,3},{8,12},{12,8},{9,1... | collective-permute-start | bytes 589832 | tf_op jit(solution)/shard_map/ppermute | solution.py:52
  2.7 0.2 copy-done.3
  2.9 0.2 shard_map.66._
  3.1 0.7 %collective-permute-done.got_ref = bf16[192,512]{1,0:T(8,128)(2,1)S(1)} collective-permute-done((bf16[192,512]{1,0:T(8,128)(2,1)S(1)}, bf16[192,512]{1,0:T(8,128)(2,1)S(1)}, u32[]{:S(2)}, u32[]{:S(2)}) %collective-permute-start) | collective-permute-done | bytes 196640 | tf_op jit(solution)/shard_map/ppermute | solution.py:52
  3.8 0.0 copy-start.4
  3.8 3.5 %collective-permute-start.1 = (bf16[5,64,512]{2,1,0:T(8,128)(2,1)S(1)}, bf16[5,64,512]{2,1,0:T(8,128)(2,1)S(1)}, u32[]{:S(2)}, u32[]{:S(2)}) collective-permute-start(bf16[5,64,512]{2,1,0:T(8,128)(2,1)S(1)} %pad_maximum_fusion), channel_id=1, source_target_pairs={{1,4},{2,5},{3,6},{4,1},{5,2},{6,3},{9,12},{10,13},{11,14},{12,9},... | collective-permute-start | bytes 983048 | tf_op jit(solution)/shard_map/ppermute | solution.py:96
  7.3 0.0 copy-done.1
  7.3 5.1 %shard_map.67 = (f32[2,32,16,512]{3,2,1,0:T(8,128)S(1)}, f32[2,64,512]{2,1,0:T(8,128)S(1)}, bf16[1024,1536]{1,0:T(8,128)(2,1)S(1)}) custom-call(bf16[1024,1536]{1,0:T(8,128)(2,1)S(1)} %shard_map.66._, bf16[192,512]{1,0:T(8,128)(2,1)S(1)} %collective-permute-done.got_ref, bf16[3,3,512,512]{3,2,1,0:T(8,128)(2,1)S(1)} %copy-done.1), custom_call_target="tpu_custom_call", output_to_operand_aliasing={{2}: (0, {})} | custom-call | flops 4831838208 | bytes 13565952 | tf_op jit(solution)/shard_map/pallas_call | solution.py:22
  12.4 0.0 collective-permute-done.1.mine_ref
  12.4 0.2 collective-permute-start.2
  12.6 1.5 %collective-permute-done.2.theirs_ref = bf16[5,64,512]{2,1,0:T(8,128)(2,1)S(1)} collective-permute-done((bf16[5,64,512]{2,1,0:T(8,128)(2,1)S(1)}, bf16[5,64,512]{2,1,0:T(8,128)(2,1)S(1)}, u32[]{:S(2)}, u32[]{:S(2)}) %collective-permute-start.2) | collective-permute-done | bytes 327712 | tf_op jit(solution)/shard_map/ppermute | solution.py:52
  14.1 0.2 shard_map.68
  14.3 0.0 copy-done.4
  14.3 0.6 %shard_map.71 = (f32[2,32,16,256]{3,2,1,0:T(8,128)S(1)}, f32[2,64,256]{2,1,0:T(8,128)S(1)}, bf16[576,256]{1,0:T(8,128)(2,1)S(1)}) custom-call(bf16[256,1536]{1,0:T(8,128)(2,1)S(1)} %get-tuple-element.41.lhs_ref, bf16[3,3,512,512]{3,2,1,0:T(8,128)(2,1)S(1)} %copy-done.1, f32[2,32,16,512]{3,2,1,0:T(8,128)S(1)} %get-tuple-element.42.total_ref, ...), custom_call_target="tpu_custom_call" | custom-call | flops 301989888 | bytes 9340928 | tf_op jit(solution)/shard_map/pallas_call | solution.py:22
  14.9 0.0 copy-start.5
  14.9 1.3 %collective-permute-start.5 = (bf16[576,256]{1,0:T(8,128)(2,1)S(1)}, bf16[576,256]{1,0:T(8,128)(2,1)S(1)}, u32[]{:S(2)}, u32[]{:S(2)}) collective-permute-start(bf16[576,256]{1,0:T(8,128)(2,1)S(1)} %get-tuple-element.47.end_ref), channel_id=1, source_target_pairs={{0,8},{8,0},{16,24},{4,20},{12,28},{1,9},{9,1},{17,25},{5,21},{13,... | collective-permute-start | bytes 884744 | tf_op jit(solution)/shard_map/ppermute | solution.py:261
  16.2 0.0 slice-start
  16.2 0.6 %shard_map.69 = (f32[2,32,16,256]{3,2,1,0:T(8,128)S(1)}, f32[2,64,256]{2,1,0:T(8,128)S(1)}, bf16[576,256]{1,0:T(8,128)(2,1)S(1)}) custom-call(bf16[256,1536]{1,0:T(8,128)(2,1)S(1)} %get-tuple-element.41.lhs_ref, bf16[3,3,512,512]{3,2,1,0:T(8,128)(2,1)S(1)} %copy-done.1, f32[2,32,16,512]{3,2,1,0:T(8,128)S(1)} %get-tuple-element.42.total_ref, ...), custom_call_target="tpu_custom_call" | custom-call | flops 301989888 | bytes 9340928 | tf_op jit(solution)/shard_map/pallas_call | solution.py:22
  16.9 0.0 slice-start.1
  16.9 1.4 %collective-permute-start.3 = (bf16[576,256]{1,0:T(8,128)(2,1)S(1)}, bf16[576,256]{1,0:T(8,128)(2,1)S(1)}, u32[]{:S(2)}, u32[]{:S(2)}) collective-permute-start(bf16[576,256]{1,0:T(8,128)(2,1)S(1)} %get-tuple-element.45.end_ref), channel_id=1, source_target_pairs={{0,8},{8,0},{16,24},{4,20},{12,28},{1,9},{9,1},{17,25},{5,21},{13,... | collective-permute-start | bytes 884744 | tf_op jit(solution)/shard_map/ppermute | solution.py:261
  18.3 4.4 %collective-permute-done.5.got_ref.refs_4_.refs_6_ = bf16[576,256]{1,0:T(8,128)(2,1)S(1)} collective-permute-done((bf16[576,256]{1,0:T(8,128)(2,1)S(1)}, bf16[576,256]{1,0:T(8,128)(2,1)S(1)}, u32[]{:S(2)}, u32[]{:S(2)}) %collective-permute-start.5) | collective-permute-done | bytes 294944 | tf_op jit(solution)/shard_map/ppermute | solution.py:261
  22.7 0.1 shard_map.72
  22.8 1.9 %collective-permute-start.6 = (bf16[576,256]{1,0:T(8,128)(2,1)S(1)}, bf16[576,256]{1,0:T(8,128)(2,1)S(1)}, u32[]{:S(2)}, u32[]{:S(2)}) collective-permute-start(bf16[576,256]{1,0:T(8,128)(2,1)S(1)} %shard_map.72), channel_id=1, source_target_pairs={{0,16},{8,24},{4,12},{20,28},{28,20},{1,17},{9,25},{5,13},{21,29},... | collective-permute-start | bytes 884744 | tf_op jit(solution)/shard_map/ppermute | solution.py:272
  24.8 1.1 %collective-permute-done.3.got_ref.refs_4_.refs_6_ = bf16[576,256]{1,0:T(8,128)(2,1)S(1)} collective-permute-done((bf16[576,256]{1,0:T(8,128)(2,1)S(1)}, bf16[576,256]{1,0:T(8,128)(2,1)S(1)}, u32[]{:S(2)}, u32[]{:S(2)}) %collective-permute-start.3) | collective-permute-done | bytes 294944 | tf_op jit(solution)/shard_map/ppermute | solution.py:261
  25.8 0.1 shard_map.70
  26.0 2.5 %collective-permute-start.4 = (bf16[576,256]{1,0:T(8,128)(2,1)S(1)}, bf16[576,256]{1,0:T(8,128)(2,1)S(1)}, u32[]{:S(2)}, u32[]{:S(2)}) collective-permute-start(bf16[576,256]{1,0:T(8,128)(2,1)S(1)} %shard_map.70), channel_id=1, source_target_pairs={{0,16},{8,24},{4,12},{20,28},{28,20},{1,17},{9,25},{5,13},{21,29},... | collective-permute-start | bytes 884744 | tf_op jit(solution)/shard_map/ppermute | solution.py:272
  28.5 2.1 %collective-permute-done.6.refs_5_.refs_7_ = bf16[576,256]{1,0:T(8,128)(2,1)S(1)} collective-permute-done((bf16[576,256]{1,0:T(8,128)(2,1)S(1)}, bf16[576,256]{1,0:T(8,128)(2,1)S(1)}, u32[]{:S(2)}, u32[]{:S(2)}) %collective-permute-start.6) | collective-permute-done | bytes 294944 | tf_op jit(solution)/shard_map/ppermute | solution.py:272
  30.6 0.0 copy-done.5
  30.6 0.1 shard_map.74
  30.7 1.9 %collective-permute-start.7 = (bf16[2,32,256]{2,1,0:T(8,128)(2,1)S(1)}, bf16[2,32,256]{2,1,0:T(8,128)(2,1)S(1)}, u32[]{:S(2)}, u32[]{:S(2)}) collective-permute-start(bf16[2,32,256]{2,1,0:T(8,128)(2,1)S(1)} %get-tuple-element.50), channel_id=1, source_target_pairs={{0,4},{4,0},{1,5},{5,1},{2,6},{6,2},{3,7},{7,3},{8,12},{12,8},{9,1... | collective-permute-start | bytes 98312 | tf_op jit(solution)/shard_map/ppermute | solution.py:52
  32.6 0.6 %shard_map.73._ = bf16[1152,768]{1,0:T(8,128)(2,1)S(1)} custom-call(f32[2,32,16,256]{3,2,1,0:T(8,128)S(1)} %get-tuple-element.46.refs_0_, f32[32,16,512]{2,1,0:T(8,128)S(1)} %copy-done, s32[1,512]{1,0:T(1,128)S(1)} %bitcast.10, f32[1,512]{1,0:T(1,128)S(1)} %bitcast.14, bf16[576,256]{1,0:T(8,128)(2,1)S(1)} %collective-permute-done.5.got_ref.refs_4_.refs_6_, ...), custom_call_target="tpu_custom_call" | custom-call | bytes 4460544 | tf_op jit(solution)/shard_map/pallas_call | solution.py:22
  33.2 0.3 collective-permute-done.7.got_ref
  33.5 0.0 slice-done
  33.5 0.0 slice-done.1
  33.5 1.5 %shard_map.75 = (f32[2,32,16,256]{3,2,1,0:T(8,128)S(1)}, bf16[1152,768]{1,0:T(8,128)(2,1)S(1)}) custom-call(bf16[1152,768]{1,0:T(8,128)(2,1)S(1)} %shard_map.73._, bf16[2,32,256]{2,1,0:T(8,128)(2,1)S(1)} %collective-permute-done.7.got_ref, bf16[2,64,256]{2,1,0:T(8,128)(2,1)S(1)} %get-tuple-element.51.beside_ref, ...), custom_call_target="tpu_custom_call", output_to_operand_aliasing={{1}: (0, {})} | custom-call | flops 1207959552 | bytes 9404416 | tf_op jit(solution)/shard_map/pallas_call | solution.py:22
  35.0 0.0 collective-permute-done.4.refs_5_.refs_7_
  35.0 0.1 shard_map.77
  35.2 0.6 %collective-permute-start.8 = (bf16[2,32,256]{2,1,0:T(8,128)(2,1)S(1)}, bf16[2,32,256]{2,1,0:T(8,128)(2,1)S(1)}, u32[]{:S(2)}, u32[]{:S(2)}) collective-permute-start(bf16[2,32,256]{2,1,0:T(8,128)(2,1)S(1)} %get-tuple-element.58), channel_id=1, source_target_pairs={{0,4},{4,0},{1,5},{5,1},{2,6},{6,2},{3,7},{7,3},{8,12},{12,8},{9,1... | collective-permute-start | bytes 98312 | tf_op jit(solution)/shard_map/ppermute | solution.py:52
  35.8 1.5 %shard_map.78.refs_1_ = f32[2,32,16,256]{3,2,1,0:T(8,128)S(1)} custom-call(bf16[1152,768]{1,0:T(8,128)(2,1)S(1)} %get-tuple-element.61.lhs_ref, bf16[3,3,512,512]{3,2,1,0:T(8,128)(2,1)S(1)} %bitcast.4), custom_call_target="tpu_custom_call" | custom-call | flops 1207959552 | bytes 7536640 | tf_op jit(solution)/shard_map/pallas_call | solution.py:22
  37.3 0.6 %shard_map.76._ = bf16[1152,768]{1,0:T(8,128)(2,1)S(1)} custom-call(f32[2,32,16,256]{3,2,1,0:T(8,128)S(1)} %get-tuple-element.44.refs_0_, f32[32,16,512]{2,1,0:T(8,128)S(1)} %copy-done, s32[1,512]{1,0:T(1,128)S(1)} %bitcast.12, f32[1,512]{1,0:T(1,128)S(1)} %bitcast.16, bf16[576,256]{1,0:T(8,128)(2,1)S(1)} %collective-permute-done.3.got_ref.refs_4_.refs_6_, ...), custom_call_target="tpu_custom_call" | custom-call | bytes 4460544 | tf_op jit(solution)/shard_map/pallas_call | solution.py:22
  37.9 0.0 collective-permute-done.8.got_ref
  37.9 3.8 %shard_map.79 = (bf16[2,32,16,512]{3,2,1,0:T(8,128)(2,1)}, bf16[1152,768]{1,0:T(8,128)(2,1)S(1)}) custom-call(bf16[1152,768]{1,0:T(8,128)(2,1)S(1)} %shard_map.76._, bf16[2,32,256]{2,1,0:T(8,128)(2,1)S(1)} %collective-permute-done.8.got_ref, bf16[2,64,256]{2,1,0:T(8,128)(2,1)S(1)} %get-tuple-element.59.beside_ref, ...), custom_call_target="tpu_custom_call", output_to_operand_aliasing={{1}: (0, {})} | custom-call | flops 2415919104 | bytes 11501568 | tf_op jit(solution)/shard_map/pallas_call | solution.py:22
  (3 shorter events, 0.0 us)
Async XLA Ops:
  0.0 1.7 %copy-start = (f32[32,16,512]{2,1,0:T(8,128)S(1)}, f32[32,16,512]{2,1,0:T(8,128)}, u32[]{:S(2)}) copy-start(f32[32,16,512]{2,1,0:T(8,128)} %refs_2_.3) | copy-start | bytes 3145732
  0.0 1.3 %copy-start.2 = (bf16[2,32,16,512]{3,2,1,0:T(8,128)(2,1)S(1)}, bf16[2,32,16,512]{3,2,1,0:T(8,128)(2,1)}, u32[]{:S(2)}) copy-start(bf16[2,32,16,512]{3,2,1,0:T(8,128)(2,1)} %cells_ref.3) | copy-start | bytes 3145732
  1.6 1.2 %copy-start.3 = (bf16[2,32,16,512]{3,2,1,0:T(8,128)(2,1)S(1)}, bf16[2,32,16,512]{3,2,1,0:T(8,128)(2,1)}, u32[]{:S(2)}) copy-start(bf16[2,32,16,512]{3,2,1,0:T(8,128)(2,1)} %cells_ref.3) | copy-start | bytes 3145732
  2.0 5.4 %copy-start.1 = (bf16[3,3,512,512]{3,2,1,0:T(8,128)(2,1)S(1)}, bf16[3,3,512,512]{3,2,1,0:T(8,128)(2,1)}, u32[]{:S(2)}) copy-start(bf16[3,3,512,512]{3,2,1,0:T(8,128)(2,1)} %weight_ref.8) | copy-start | bytes 14155780
  2.0 1.8 %collective-permute-start = (bf16[192,512]{1,0:T(8,128)(2,1)S(1)}, bf16[192,512]{1,0:T(8,128)(2,1)S(1)}, u32[]{:S(2)}, u32[]{:S(2)}) collective-permute-start(bf16[192,512]{1,0:T(8,128)(2,1)S(1)} %get-tuple-element.37), channel_id=1, source_target_pairs={{0,4},{4,0},{1,5},{5,1},{2,6},{6,2},{3,7},{7,3},{8,12},{12,8},{9,1... | collective-permute-start | bytes 589832 | tf_op jit(solution)/shard_map/ppermute | solution.py:52
  3.8 10.4 %copy-start.4 = (s32[512]{0:T(512)S(1)}, s32[512]{0:T(512)}, u32[]{:S(2)}) copy-start(s32[512]{0:T(512)} %param.9) | copy-start | bytes 6148
  3.8 8.5 %collective-permute-start.1 = (bf16[5,64,512]{2,1,0:T(8,128)(2,1)S(1)}, bf16[5,64,512]{2,1,0:T(8,128)(2,1)S(1)}, u32[]{:S(2)}, u32[]{:S(2)}) collective-permute-start(bf16[5,64,512]{2,1,0:T(8,128)(2,1)S(1)} %pad_maximum_fusion), channel_id=1, source_target_pairs={{1,4},{2,5},{3,6},{4,1},{5,2},{6,3},{9,12},{10,13},{11,14},{12,9},... | collective-permute-start | bytes 983048 | tf_op jit(solution)/shard_map/ppermute | solution.py:96
  12.4 1.7 %collective-permute-start.2 = (bf16[5,64,512]{2,1,0:T(8,128)(2,1)S(1)}, bf16[5,64,512]{2,1,0:T(8,128)(2,1)S(1)}, u32[]{:S(2)}, u32[]{:S(2)}) collective-permute-start(bf16[5,64,512]{2,1,0:T(8,128)(2,1)S(1)} %collective-permute-done.1.mine_ref), channel_id=1, source_target_pairs={{0,4},{4,0},{1,5},{5,1},{2,6},{6,2},{3,7},{7,3},{8,12},{12,8},{9,1... | collective-permute-start | bytes 983048 | tf_op jit(solution)/shard_map/ppermute | solution.py:52
  14.9 15.7 %copy-start.5 = (f32[512]{0:T(512)S(1)}, f32[512]{0:T(512)}, u32[]{:S(2)}) copy-start(f32[512]{0:T(512)} %param.10) | copy-start | bytes 6148
  14.9 7.8 %collective-permute-start.5 = (bf16[576,256]{1,0:T(8,128)(2,1)S(1)}, bf16[576,256]{1,0:T(8,128)(2,1)S(1)}, u32[]{:S(2)}, u32[]{:S(2)}) collective-permute-start(bf16[576,256]{1,0:T(8,128)(2,1)S(1)} %get-tuple-element.47.end_ref), channel_id=1, source_target_pairs={{0,8},{8,0},{16,24},{4,20},{12,28},{1,9},{9,1},{17,25},{5,21},{13,... | collective-permute-start | bytes 884744 | tf_op jit(solution)/shard_map/ppermute | solution.py:261
  16.2 17.3 %slice-start = ((s8[4718592]{0:T(1024)(128)(4,1)}), s8[4194304]{0:T(1024)(128)(4,1)S(1)}, s32[]{:S(2)}) async-start(s8[4718592]{0:T(1024)(128)(4,1)} %bitcast.3), calls=%async_computation | async-start | bytes 8388608
  16.9 16.6 %slice-start.1 = ((s8[4718592]{0:T(1024)(128)(4,1)}), s8[524288]{0:T(1024)(128)(4,1)S(1)}, s32[]{:S(2)}) async-start(s8[4718592]{0:T(1024)(128)(4,1)} %bitcast.3), calls=%async_computation.1 | async-start | bytes 1048576
  16.9 9.0 %collective-permute-start.3 = (bf16[576,256]{1,0:T(8,128)(2,1)S(1)}, bf16[576,256]{1,0:T(8,128)(2,1)S(1)}, u32[]{:S(2)}, u32[]{:S(2)}) collective-permute-start(bf16[576,256]{1,0:T(8,128)(2,1)S(1)} %get-tuple-element.45.end_ref), channel_id=1, source_target_pairs={{0,8},{8,0},{16,24},{4,20},{12,28},{1,9},{9,1},{17,25},{5,21},{13,... | collective-permute-start | bytes 884744 | tf_op jit(solution)/shard_map/ppermute | solution.py:261
  22.8 7.8 %collective-permute-start.6 = (bf16[576,256]{1,0:T(8,128)(2,1)S(1)}, bf16[576,256]{1,0:T(8,128)(2,1)S(1)}, u32[]{:S(2)}, u32[]{:S(2)}) collective-permute-start(bf16[576,256]{1,0:T(8,128)(2,1)S(1)} %shard_map.72), channel_id=1, source_target_pairs={{0,16},{8,24},{4,12},{20,28},{28,20},{1,17},{9,25},{5,13},{21,29},... | collective-permute-start | bytes 884744 | tf_op jit(solution)/shard_map/ppermute | solution.py:272
  26.0 9.1 %collective-permute-start.4 = (bf16[576,256]{1,0:T(8,128)(2,1)S(1)}, bf16[576,256]{1,0:T(8,128)(2,1)S(1)}, u32[]{:S(2)}, u32[]{:S(2)}) collective-permute-start(bf16[576,256]{1,0:T(8,128)(2,1)S(1)} %shard_map.70), channel_id=1, source_target_pairs={{0,16},{8,24},{4,12},{20,28},{28,20},{1,17},{9,25},{5,13},{21,29},... | collective-permute-start | bytes 884744 | tf_op jit(solution)/shard_map/ppermute | solution.py:272
  30.7 2.8 %collective-permute-start.7 = (bf16[2,32,256]{2,1,0:T(8,128)(2,1)S(1)}, bf16[2,32,256]{2,1,0:T(8,128)(2,1)S(1)}, u32[]{:S(2)}, u32[]{:S(2)}) collective-permute-start(bf16[2,32,256]{2,1,0:T(8,128)(2,1)S(1)} %get-tuple-element.50), channel_id=1, source_target_pairs={{0,4},{4,0},{1,5},{5,1},{2,6},{6,2},{3,7},{7,3},{8,12},{12,8},{9,1... | collective-permute-start | bytes 98312 | tf_op jit(solution)/shard_map/ppermute | solution.py:52
  35.2 2.7 %collective-permute-start.8 = (bf16[2,32,256]{2,1,0:T(8,128)(2,1)S(1)}, bf16[2,32,256]{2,1,0:T(8,128)(2,1)S(1)}, u32[]{:S(2)}, u32[]{:S(2)}) collective-permute-start(bf16[2,32,256]{2,1,0:T(8,128)(2,1)S(1)} %get-tuple-element.58), channel_id=1, source_target_pairs={{0,4},{4,0},{1,5},{5,1},{2,6},{6,2},{3,7},{7,3},{8,12},{12,8},{9,1... | collective-permute-start | bytes 98312 | tf_op jit(solution)/shard_map/ppermute | solution.py:52

commit v10 on v9

v10 whole, which is shorter than its diff:
```python
import functools
import math

import jax
import jax.numpy as jnp
from jax import lax
from jax.experimental import pallas as pl
from jax.experimental.pallas import tpu as pltpu
from jax.sharding import PartitionSpec as P

NPOLES = 16
VMEM_LIMIT = 24 * 1024 * 1024
WHOLE = pl.BlockSpec(memory_space=pltpu.VMEM)
HBM = pl.BlockSpec(memory_space=pltpu.HBM)
EDGES_COST = 2_000_000_000


def call(kernel, out_shape, *args, scratch=(), flops=0, out_specs=None, aliases=None):
    outs = jax.tree.leaves(out_shape)
    moved = sum(leaf.size * leaf.dtype.itemsize for leaf in (*args, *outs))
    return pl.pallas_call(
        kernel,
        in_specs=[WHOLE] * len(args),
        out_specs=out_specs or jax.tree.map(lambda _: WHOLE, out_shape),
        out_shape=out_shape,
        scratch_shapes=scratch,
        input_output_aliases=aliases or {},
        compiler_params=pltpu.CompilerParams(vmem_limit_bytes=VMEM_LIMIT),
        cost_estimate=pl.CostEstimate(flops=flops, bytes_accessed=moved, transcendentals=0),
    )(*args)


def of(shape, dtype):
    return jax.ShapeDtypeStruct(shape, dtype)


def is_core(which):
    return (lax.axis_index("sx") == which).astype(jnp.float32)


def rate_of(pole_ref):
    pole = pole_ref[...].astype(jnp.float32)
    return -0.001 * jnp.exp(pole * (math.log(300.0) / (NPOLES - 1)))


def inner_row(rows):
    return jnp.where(lax.axis_index("sx") == 0, rows - 1, 0)


def swap_cores(array):
    return lax.ppermute(array, "sx", [(0, 1), (1, 0)])


def put_columns(index, left, right, give_ref, keep_ref):
    zero, one = is_core(0), is_core(1)
    count, rows, _ = keep_ref.shape
    at = give_ref.shape[0] - (count - index) * rows
    give_ref[at : at + rows] = (zero * right + one * left).astype(give_ref.dtype)
    keep_ref[index] = (zero * left + one * right).astype(keep_ref.dtype)


def edges_kernel(cells_ref, give_ref, keep_ref, wide_ref):
    count, rows, cols, channels = cells_ref.shape
    for frame in range(count):
        give_ref[frame * cols : (frame + 1) * cols] = cells_ref[frame, inner_row(rows)]
        tile = cells_ref[frame].reshape(rows * cols, channels).astype(jnp.float32)
        lanes = wide_ref.shape[-1]
        for part in range(channels // lanes):
            wide_ref[frame, part] = tile[:, part * lanes : (part + 1) * lanes]

        def column(col):
            parts = [
                wide_ref[frame, part, pl.ds(col, rows, stride=cols), :]
                for part in range(channels // lanes)
            ]
            return jnp.concatenate(parts, axis=1)

        for depth in range(2):
            left, right = column(depth), column(cols - 1 - depth)
            put_columns(2 * frame + depth, left, right, give_ref, keep_ref)


def start_edges_kernel(start_ref, _, __, give_ref, keep_ref):
    tile, cols = start_ref[...], start_ref.shape[1]
    index = keep_ref.shape[0] - 1
    put_columns(index, tile[:, 0, :], tile[:, cols - 1, :], give_ref, keep_ref)


def trade_columns(give, keep, at):
    chips = lax.axis_size("sy")
    got = swap_cores(give)
    pairs = [(chip, chips + chip - 1) for chip in range(1, chips)]
    pairs += [(after, before) for before, after in pairs]
    columns = jnp.concatenate([keep, got[at:].reshape(keep.shape)], axis=1)
    return got, lax.ppermute(columns, ("sx", "sy"), pairs)


def put_cells(lhs_ref, at, size, cols, first, cells):
    count, channels = cells.shape
    upper, lower = min(count, size - cols - first), max(0, cols - first)
    here = at + first
    lhs_ref[here : here + count, channels : 2 * channels] = cells
    lhs_ref[here + cols : here + cols + upper, :channels] = cells[:upper]
    lhs_ref[here + lower - cols : here + count - cols, 2 * channels :] = cells[lower:]


def put_row(lhs_ref, at, size, row):
    cols, channels = row.shape
    row = row.astype(jnp.float32)
    last = slice(at + size - cols, at + size)
    lhs_ref[at : at + cols, :channels] = (is_core(1) * row).astype(lhs_ref.dtype)
    lhs_ref[last, 2 * channels :] = (is_core(0) * row).astype(lhs_ref.dtype)


def taps_kernel(cells_ref, lhs_ref):
    count, rows, cols, channels = cells_ref.shape
    size = rows * cols
    for frame in range(count):
        put_cells(lhs_ref, frame * size, size, cols, 0, cells_ref[frame].reshape(size, channels))


def row_taps(column, above, below):
    rows = column.shape[0]
    row = lax.broadcasted_iota(jnp.int32, column.shape, 0)
    up = jnp.where(row == 0, is_core(1) * above, pltpu.roll(column, 1, 0))
    down = jnp.where(row == rows - 1, is_core(0) * below, pltpu.roll(column, rows - 1, 0))
    return jnp.concatenate([up, column, down], axis=1)


def halves(channels):
    return slice(0, channels // 2), slice(channels // 2, channels)


def end_state(frames, pole_ref, lanes):
    decay = jnp.exp(rate_of(pole_ref))[:, lanes]
    state = frames[0]
    for frame in frames[1:]:
        state = decay * state + frame
    return state


def dot(lhs, weight_ref, column, lanes, inputs=slice(None)):
    weight = weight_ref[:, column, inputs, lanes].reshape(lhs.shape[1], -1)
    return jnp.dot(lhs, weight, preferred_element_type=jnp.float32)


def main_kernel(_, got_ref, weight_ref, pole_ref, total_ref, spill_ref, end_ref, lhs_ref):
    count, rows, cols, _ = total_ref.shape
    size = rows * cols
    for frame in range(count):
        put_row(lhs_ref, frame * size, size, got_ref[frame * cols : (frame + 1) * cols])
    for lanes in halves(weight_ref.shape[-1]):
        tile = (count, rows, cols, lanes.stop - lanes.start)
        col = lax.broadcasted_iota(jnp.int32, tile, 2)
        total = dot(lhs_ref[...], weight_ref, 1, lanes).reshape(tile)
        first = dot(lhs_ref[...], weight_ref, 0, lanes).reshape(tile)
        spill_ref[1, :, lanes] = first[:, :, cols - 1, :].reshape(count * rows, -1)
        total += jnp.where(col == 0, 0.0, pltpu.roll(first, 1, 2))
        last = dot(lhs_ref[...], weight_ref, 2, lanes).reshape(tile)
        spill_ref[0, :, lanes] = last[:, :, 0, :].reshape(count * rows, -1)
        total += jnp.where(col == cols - 1, 0.0, pltpu.roll(last, cols - 1, 2))
        total_ref[:, :, :, lanes] = total
        if lanes.start == 0:
            state = end_state([total[frame] for frame in range(count)], pole_ref, lanes)
            end_ref[...] = state.reshape(end_ref.shape).astype(end_ref.dtype)


def halo_kernel(mine_ref, theirs_ref, lhs_ref, start_ref):
    rows = mine_ref.shape[1] // 2
    count = mine_ref.shape[0] // 2
    room = count * rows
    zero, one = is_core(0), is_core(1)
    core = lax.axis_index("sx")
    slots = ((1, 0), (2, 3))
    for frame in range(count):
        for depth in range(2):
            own = mine_ref[2 * frame + depth].astype(jnp.float32)
            other = theirs_ref[2 * frame + depth].astype(jnp.float32)
            own = row_taps(own[rows:], own[rows - 1 : rows], own[:1])
            other = row_taps(other[:rows], other[2 * rows - 1 :], other[rows : rows + 1])
            for swapped, taps in enumerate((own, other)):
                slot = jnp.where(core == swapped, slots[0][depth], slots[1][depth])
                at = pl.multiple_of(slot * room + frame * rows, rows)
                lhs_ref[pl.ds(at, rows)] = taps.astype(lhs_ref.dtype)
    own = mine_ref[2 * count, rows:].astype(jnp.float32)
    other = theirs_ref[2 * count, :rows].astype(jnp.float32)
    start_ref[:rows] = zero * own + one * other
    start_ref[rows:] = zero * other + one * own


def drive_kernel(
    lhs_ref, weight_ref, total_ref, spill_ref, pole_ref, drive_ref, beside_ref, strips_ref, end_ref
):
    count, rows, cols, wide = drive_ref.shape
    room, size = count * rows, rows * cols
    at = size + 2 * rows
    for lanes in halves(weight_ref.shape[-1]):
        first = dot(lhs_ref[: 2 * room], weight_ref, 0, lanes)
        middle = dot(lhs_ref[room : 3 * room], weight_ref, 1, lanes)
        last = dot(lhs_ref[2 * room :], weight_ref, 2, lanes)
        left = (spill_ref[0, :, lanes] + first[:room] + middle[:room]).reshape(count, rows, wide)
        right = (spill_ref[1, :, lanes] + middle[room:] + last[room:]).reshape(count, rows, wide)
        total = total_ref[:, :, :, lanes]
        if lanes.start == 0:
            near = total[:, :, 0, :] + first[room:].reshape(count, rows, wide)
            far = total[:, :, cols - 1, :] + last[:room].reshape(count, rows, wide)
            strips = jnp.concatenate([left, near, far, right], axis=1)
            strips_ref[...] = strips
            state = end_state([strips[frame] for frame in range(count)], pole_ref, lanes)
            end_ref[at:] = state.astype(end_ref.dtype)
            continue
        col = lax.broadcasted_iota(jnp.int32, drive_ref.shape, 2)
        total += jnp.where(col == 0, first[room:].reshape(count, rows, 1, wide), 0.0)
        total += jnp.where(col == cols - 1, last[:room].reshape(count, rows, 1, wide), 0.0)
        drive_ref[...] = total
        state = end_state([total[frame] for frame in range(count)], pole_ref, lanes)
        end_ref[:size] = state.reshape(size, wide).astype(end_ref.dtype)
        beside = jnp.concatenate([left, right], axis=1)
        beside_ref[...] = beside
        state = end_state([beside[frame] for frame in range(count)], pole_ref, lanes)
        end_ref[size:at] = state.astype(end_ref.dtype)


def entry_kernel(frames, ends_ref, pole_ref, out_ref):
    carried = jnp.exp(frames * rate_of(pole_ref))
    entry = jnp.zeros(ends_ref.shape[1:], jnp.float32)
    out_ref[0] = entry.astype(out_ref.dtype)
    for index in range(ends_ref.shape[0] - 1):
        entry = carried * entry + ends_ref[index].astype(jnp.float32)
        out_ref[index + 1] = entry.astype(out_ref.dtype)


def exchange(pieces, pole, frames):
    groups = lax.axis_size("tm")
    arrivals = []
    for end, blocks in pieces:
        entries = []
        for rows, lanes in blocks:
            shares = end[rows].reshape(groups, -1, end.shape[1])
            shares = lax.all_to_all(shares, "tm", 0, 0)
            kernel = functools.partial(entry_kernel, frames)
            entry = call(kernel, of(shares.shape, end.dtype), shares, pole[:, lanes])
            entries.append(lax.all_to_all(entry, "tm", 0, 0).reshape(-1, end.shape[1]))
        arrivals.append((jnp.concatenate(entries, axis=0),))
    return arrivals


def pick(values):
    group = lax.axis_index("tm")
    picked = values[-1]
    for index, value in enumerate(values[:-1]):
        picked = jnp.where(group == index, value, picked)
    return picked


def on_core(first, second):
    return jnp.where(lax.axis_index("sx") == 0, first, second)


def weigh(one, by_one, other, by_other):
    return by_one * one.astype(jnp.float32) + by_other * other.astype(jnp.float32)


def relay_kernel(frames, blocks, end_ref, got_ref, pole_ref, out_ref):
    for rows, lanes in blocks:
        rate = rate_of(pole_ref)[:, lanes]
        carried, twice = jnp.exp(frames * rate), jnp.exp(2 * frames * rate)
        none, same = jnp.zeros_like(rate), jnp.ones_like(rate)
        own = on_core(pick([carried, same, same, same]), pick([same, same, same, none]))
        got = on_core(pick([same, carried, carried, carried]), pick([none, none, twice, same]))
        out_ref[rows] = weigh(end_ref[rows], own, got_ref[rows], got).astype(out_ref.dtype)


def exchange_four(pieces, pole, frames):
    def along(pairs, core):
        return [(2 * source + core, 2 * target + core) for source, target in pairs]

    axes = ("tm", "sx")
    down = [(0, 2), (1, 3)]
    first_round = along([(0, 1), (1, 0), (2, 3)], 0) + along(down, 1)
    second_round = along(down, 0) + along([(0, 1), (2, 3), (3, 2)], 1)
    arrivals = []
    for end, blocks in pieces:
        got = lax.ppermute(end, axes, first_round)
        kernel = functools.partial(relay_kernel, frames, blocks)
        relayed = call(kernel, of(end.shape, end.dtype), end, got, pole)
        arrivals.append((got, lax.ppermute(relayed, axes, second_round)))
    return arrivals


class Mix:
    def __init__(self, lanes, count, arrived_refs, pole_ref, scale_ref):
        self.rate = rate_of(pole_ref)[:, lanes]
        self.scale = scale_ref[:, lanes]
        self.count = count
        self.arrived_refs = arrived_refs

    def entry(self, rows):
        parts = [ref[rows] for ref in self.arrived_refs]
        if len(parts) == 1:
            return parts[0].astype(jnp.float32)
        carried = jnp.exp(self.count * self.rate)
        none, same = jnp.zeros_like(self.rate), jnp.ones_like(self.rate)
        early = on_core(pick([none, same, none, same]), pick([none, none, carried, carried]))
        late = on_core(pick([none, none, same, carried]), pick([none, same, same, same]))
        return weigh(parts[0], early, parts[1], late)

    def __call__(self, drives, rows, start):
        decay = jnp.exp(self.rate)
        reach = jnp.exp((self.count * lax.axis_index("tm")).astype(jnp.float32) * self.rate)
        state = reach * start + self.entry(rows).reshape(start.shape)
        for drive in drives:
            state = decay * state + drive
            yield jax.nn.gelu(self.scale * state)


def middle_kernel(lanes, *refs):
    total_ref, start_ref, pole_ref, scale_ref, *arrived_refs, give_ref = refs
    count, rows, cols, _ = total_ref.shape
    mix = Mix(lanes, count, arrived_refs, pole_ref, scale_ref)
    inner = inner_row(rows)
    drives = [total_ref[frame, inner, :, lanes] for frame in range(count)]
    here = pl.ds(pl.multiple_of(inner * cols, cols), cols)
    col = lax.broadcasted_iota(jnp.int32, give_ref.shape[1:], 0)
    for frame, cells in enumerate(mix(drives, here, start_ref[inner, :, lanes])):
        cells = jnp.where((col == 0) | (col == cols - 1), 0.0, cells)
        give_ref[frame] = cells.astype(give_ref.dtype)


def mixed_kernel(lanes, inner_only, *refs):
    drive_ref, start_ref, pole_ref, scale_ref, *arrived_refs, lhs_ref = refs
    count, rows, cols, _ = drive_ref.shape
    wide = lanes.stop - lanes.start
    size = rows * cols
    room = (lhs_ref.shape[0] - count * size) // 2
    mix = Mix(lanes, count, arrived_refs, pole_ref, scale_ref)
    held = lanes if inner_only else slice(None)
    block = 8
    col = lax.broadcasted_iota(jnp.int32, (block, cols, wide), 1)
    for row in range(0, rows, block):
        here = slice(row, row + block)
        drives = [drive_ref[frame, here, :, held] for frame in range(count)]
        cells = slice(row * cols, (row + block) * cols)
        for frame, tile in enumerate(mix(drives, cells, start_ref[here, :, lanes])):
            if inner_only:
                tile = jnp.where((col == 0) | (col == cols - 1), 0.0, tile)
            tile = tile.reshape(block * cols, wide).astype(lhs_ref.dtype)
            put_cells(lhs_ref, room + frame * size, size, cols, row * cols, tile)


def strip_start_kernel(start_ref, sides_ref, out_ref):
    rows, cols, _ = start_ref.shape
    start = start_ref[...]
    out_ref[:rows] = sides_ref[:rows]
    out_ref[rows : 2 * rows] = start[:, 0, :]
    out_ref[2 * rows : 3 * rows] = start[:, cols - 1, :]
    out_ref[3 * rows :] = sides_ref[rows:]


def late_kernel(parts, *refs):
    drive_ref, beside_ref, strips_ref, start_ref, strip_start_ref, pole_ref, scale_ref, *refs = refs
    *arrived_refs, give_ref, beside_out_ref, strips_out_ref = refs
    count, rows, cols, wide = drive_ref.shape
    size = rows * cols
    inner = inner_row(rows)
    zero, one = is_core(0), is_core(1)
    chip, chips = lax.axis_index("sy"), lax.axis_size("sy")
    inside = [(chip > 0).astype(jnp.float32), (chip < chips - 1).astype(jnp.float32)]
    early, late = (Mix(lanes, count, arrived_refs, pole_ref, scale_ref) for lanes in parts)

    def columns_of(cells, count):
        return [cells[index * rows : (index + 1) * rows] for index in range(count)]

    starts = columns_of(strip_start_ref, 4)
    starts = jnp.concatenate([starts[0][:, parts[1]], starts[3][:, parts[1]]], axis=0)
    at = size + 2 * rows
    beside = late([beside_ref[frame] for frame in range(count)], slice(size, at), starts)
    strips = early(
        [strips_ref[frame] for frame in range(count)],
        slice(at, at + 4 * rows),
        strip_start_ref[:, parts[0]],
    )
    here = pl.ds(pl.multiple_of(inner * cols, cols), cols)
    drives = [drive_ref[frame, inner] for frame in range(count)]
    tile = late(drives, here, start_ref[inner, :, parts[1]])
    which = lax.broadcasted_iota(jnp.int32, (cols, wide), 0)
    for frame, (cells, sides, strip) in enumerate(zip(tile, beside, strips)):
        sides, strip = columns_of(sides, 2), columns_of(strip, 4)
        sides = [sides[0] * inside[0], sides[1] * inside[1]]
        strip = [strip[0] * inside[0], strip[1], strip[2], strip[3] * inside[1]]
        give_ref[frame, :cols] = cells.astype(give_ref.dtype)
        ends = jnp.zeros(which.shape, jnp.float32)
        for index, column in enumerate((*sides, *strip)):
            end = zero * column[rows - 1 :] + one * column[:1]
            ends = jnp.where(which == index, end, ends)
        give_ref[frame, cols:] = ends.astype(give_ref.dtype)
        beside_out_ref[frame] = jnp.concatenate(sides, axis=0).astype(give_ref.dtype)
        strips_out_ref[frame] = jnp.concatenate(strip, axis=0).astype(give_ref.dtype)


def put_columns_taps(lhs_ref, slots, frame, count, columns, ends):
    rows = columns.shape[0] // len(slots)
    columns, ends = columns.astype(jnp.float32), ends.astype(jnp.float32)
    for index, slot in enumerate(slots):
        column, end = columns[index * rows : (index + 1) * rows], ends[index : index + 1]
        at = slot + frame * rows
        lhs_ref[at : at + rows] = row_taps(column, end, end).astype(lhs_ref.dtype)


def tile_sum(tile, inputs, lanes, room, lhs_ref, weight_ref):
    count, rows, cols, wide = tile
    inner = count * rows * cols
    col = lax.broadcasted_iota(jnp.int32, tile, 2)

    def beside(cells):
        return cells.reshape(count, rows, 1, wide) if room else 0.0

    total = dot(lhs_ref[room : room + inner], weight_ref, 1, lanes, inputs).reshape(tile)
    first = dot(lhs_ref[: room + inner], weight_ref, 0, lanes, inputs)
    halo = beside(first[:room])
    total += jnp.where(col == 0, halo, pltpu.roll(first[room:].reshape(tile), 1, 2))
    last = dot(lhs_ref[room:], weight_ref, 2, lanes, inputs)
    halo = beside(last[inner:])
    return total + jnp.where(
        col == cols - 1, halo, pltpu.roll(last[:inner].reshape(tile), cols - 1, 2)
    )


def strip_sum(tile, inputs, lanes, lhs_ref, weight_ref):
    count, rows, cols, wide = tile
    room = count * rows
    col = lax.broadcasted_iota(jnp.int32, tile, 2)
    first = dot(lhs_ref[: 2 * room], weight_ref, 0, lanes, inputs)
    middle = dot(lhs_ref[room : 3 * room], weight_ref, 1, lanes, inputs)
    last = dot(lhs_ref[2 * room :], weight_ref, 2, lanes, inputs)
    total = 0.0
    for at, cells in (
        (0, first[:room] + middle[:room]),
        (1, first[room:]),
        (cols - 2, last[:room]),
        (cols - 1, middle[room:] + last[room:]),
    ):
        total = jnp.where(col == at, cells.reshape(count, rows, 1, wide), total)
    return total


def opening_kernel(inputs, lanes, _, got_ref, weight_ref, out_ref, lhs_ref):
    count, rows, cols, _ = out_ref.shape
    size = rows * cols
    for frame in range(count):
        put_row(lhs_ref, frame * size, size, got_ref[frame])
    out_ref[...] = tile_sum(out_ref.shape, inputs, lanes, 0, lhs_ref, weight_ref)


def further_kernel(inputs, lanes, lhs_ref, weight_ref, out_ref):
    out_ref[...] = tile_sum(out_ref.shape, inputs, lanes, 0, lhs_ref, weight_ref)


def result_kernel(
    parts, _, got_ref, beside_ref, strips_ref, weight_ref, *refs
):
    *before_refs, out_ref, lhs_ref, held_ref, strip_lhs_ref, sems = refs
    count, rows, cols, _ = held_ref.shape
    size, room = rows * cols, count * rows
    for frame in range(count):
        put_row(lhs_ref, room + frame * size, size, got_ref[frame, :cols])
        ends = got_ref[frame, cols:]
        put_columns_taps(
            lhs_ref, (0, room + count * size), frame, count, beside_ref[frame], ends
        )
        slots = [slot * room for slot in range(4)]
        put_columns_taps(
            strip_lhs_ref, slots, frame, count, strips_ref[frame], ends.astype(jnp.float32)[2:]
        )

    def store(frame, part):
        here = (frame, slice(None), slice(None), parts[part])
        return pltpu.make_async_copy(held_ref.at[here], out_ref.at[here], sems.at[frame, part])

    for part, lanes in enumerate(parts):
        tile = (count, rows, cols, lanes.stop - lanes.start)
        total = before_refs[part][...]
        total += strip_sum(tile, parts[0], lanes, strip_lhs_ref, weight_ref)
        total += tile_sum(tile, parts[1], lanes, room, lhs_ref, weight_ref)
        for frame in range(count):
            held_ref[frame, :, :, lanes] = total[frame].astype(held_ref.dtype)
            store(frame, part).start()
    for part in range(len(parts)):
        for frame in range(count):
            store(frame, part).wait()


def on_device(frames, input_weight, output_weight, pole_index, gelu_scale, start_state):
    count, rows, cols, channels = frames.shape
    size, room = rows * cols, count * rows
    wide = 3 * channels
    assert lax.axis_size("sx") == 2
    narrow = frames.dtype
    pole, scale = pole_index[None], gelu_scale[None]

    shapes = (
        of((count * cols + (2 * count + 1) * rows, channels), narrow),
        of((2 * count + 1, rows, channels), narrow),
    )
    edges = call(
        edges_kernel,
        shapes,
        frames,
        scratch=[pltpu.VMEM((count, channels // 128, size, 128), jnp.float32)],
        flops=EDGES_COST,
    )
    give, keep = call(
        start_edges_kernel,
        shapes,
        start_state,
        *edges,
        aliases={1: 0, 2: 1},
    )
    got, mine = trade_columns(give, keep, count * cols)
    taps = of((count * size, wide), narrow)
    parts = halves(channels)
    half = channels // 2
    inner = of((count, rows, cols, half), jnp.float32)
    *main, early, _ = call(
        main_kernel,
        (
            of(frames.shape, jnp.float32),
            of((2, room, channels), jnp.float32),
            of((size, half), narrow),
            taps,
        ),
        call(taps_kernel, taps, frames),
        got,
        input_weight,
        pole,
        aliases={0: 3},
        flops=18 * frames.size * channels,
    )
    mine, total, spill = lax.optimization_barrier((mine, *main))
    halo, sides = call(
        halo_kernel,
        (of((4 * room, wide), narrow), of((2 * rows, channels), jnp.float32)),
        mine,
        swap_cores(mine),
    )
    drive, beside, strips, late = call(
        drive_kernel,
        (
            inner,
            of((count, 2 * rows, half), jnp.float32),
            of((count, 4 * rows, half), jnp.float32),
            of((size + 6 * rows, half), narrow),
        ),
        halo,
        input_weight,
        total,
        spill,
        pole,
        flops=36 * room * channels * channels,
    )
    at = size + 2 * rows
    pieces = [
        (early, [(slice(0, size), parts[0])]),
        (late, [(slice(0, at), parts[1]), (slice(at, at + 4 * rows), parts[0])]),
    ]
    exchanged = (exchange_four if lax.axis_size("tm") == 4 else exchange)(pieces, pole, count)
    early, late = exchanged

    mixing = (start_state, pole, scale)
    give = call(
        functools.partial(middle_kernel, parts[0]),
        of((count, cols, half), narrow),
        total,
        *mixing,
        *early,
    )
    taps = of((count * size, 3 * half), narrow)
    lhs = call(
        functools.partial(mixed_kernel, parts[0], True), taps, total, *mixing, *early
    )
    strip_start = call(strip_start_kernel, of((4 * rows, channels), jnp.float32), start_state, sides)
    flops = 18 * inner.size * half
    first_sum, lhs = call(
        functools.partial(opening_kernel, parts[0], parts[0]),
        (inner, taps),
        lhs,
        swap_cores(give),
        output_weight,
        aliases={0: 1},
        flops=flops,
    )
    second_sum = call(
        functools.partial(further_kernel, parts[0], parts[1]),
        inner,
        lhs,
        output_weight,
        flops=flops,
    )
    *late, first_sum, second_sum = lax.optimization_barrier((*late, first_sum, second_sum))
    give, beside, strips = call(
        functools.partial(late_kernel, parts),
        (
            of((count, 2 * cols, half), narrow),
            of(beside.shape, narrow),
            of(strips.shape, narrow),
        ),
        drive,
        beside,
        strips,
        start_state,
        strip_start,
        pole,
        scale,
        *late,
    )
    taps = of((count * size + 2 * room, 3 * half), narrow)
    lhs = call(functools.partial(mixed_kernel, parts[1], False), taps, drive, *mixing, *late)
    result, _ = call(
        functools.partial(result_kernel, parts),
        (of(frames.shape, narrow), taps),
        lhs,
        swap_cores(give),
        beside,
        strips,
        output_weight,
        first_sum,
        second_sum,
        out_specs=(HBM, WHOLE),
        aliases={0: 1},
        scratch=[
            pltpu.VMEM(frames.shape, narrow),
            pltpu.VMEM((4 * room, 3 * half), narrow),
            pltpu.SemaphoreType.DMA((count, len(parts))),
        ],
        flops=2 * flops,
    )
    return result


def solution(mesh):
    return jax.shard_map(
        on_device,
        mesh=mesh,
        in_specs=(P("tm", "sx", "sy", None), P(), P(), P(), P(), P("sx", "sy", None)),
        out_specs=P("tm", "sx", "sy", None),
        check_vma=False,
    )
```

time: 42.1 us -> 40.9 us (0.971)
  waiting for transfers between devices: 10.1 us -> 8.06 us
    ppermute x4, waiting for transfers between devices: 2.47 us -> 1.46 us  [swap_cores(): return lax.ppermute(array, 'sx', [(0, 1), (1, 0)])]
    ppermute x4, waiting for transfers between devices: 7.59 us -> 6.59 us  [the longest x2 4.94 us: exchange_four(): got = lax.ppermute(end, axes, first_round)]
    ppermute x4, starting transfers between devices: 3.5 us -> 4.14 us  [swap_cores(): return lax.ppermute(array, 'sx', [(0, 1), (1, 0)])]
  transfers between devices with their start and end apart: 9 -> 9, of which waited for: 6 -> 7; matrix products, arithmetic and copies ran while one was open for 0% -> 0% of each run, Pallas kernels for 25% -> 27%
where the time goes in v10:
time: 40.9 us; the launch traced here: 40.6 us
  Pallas kernels  16.1 us (39%)
  starting transfers between devices  14.5 us (35%)
  waiting for transfers between devices  8.06 us (20%)
  local copies, waits for them, and re-layouts  1.51 us (4%)
    pallas_call x16, Pallas kernels, call(): pl.pallas_call(kernel, in_specs=[WHOLE] * len(args), out_specs=out_specs...  16.1 us
    ppermute x2, waiting for transfers between devices, exchange_four(): got = lax.ppermute(end, axes, first_round)  4.94 us
    ppermute x2, starting transfers between devices, exchange_four(): arrivals.append((got, lax.ppermute(relayed, axes, second_round)))  4.28 us
    ppermute x4, starting transfers between devices, swap_cores(): return lax.ppermute(array, 'sx', [(0, 1), (1, 0)])  4.14 us
    ppermute x1, starting transfers between devices, trade_columns(): return (got, lax.ppermute(columns, ('sx', 'sy'), pairs))  3.46 us
    ppermute x2, starting transfers between devices, exchange_four(): got = lax.ppermute(end, axes, first_round)  2.57 us
    ppermute x2, waiting for transfers between devices, exchange_four(): arrivals.append((got, lax.ppermute(relayed, axes, second_round)))  1.65 us
    unnamed x16, local copies, waits for them, and re-layouts  1.5 us
  transfers between devices with their start and end apart: 9, of which 7 were waited for; matrix products, arithmetic and copies ran while one was open for 0% of the time, Pallas kernels for 27%

profile of v10, /device:TPU:23, one launch (start us, length us, event | category | flops | bytes accessed | tf_op | source)
XLA Modules:
  0.0 40.6 jit_solution(4110213499240701395)
XLA Ops:
  0.0 0.0 copy-start
  0.0 0.0 copy-start.2
  0.0 1.3 %copy-done.2 = bf16[2,32,16,512]{3,2,1,0:T(8,128)(2,1)S(1)} copy-done((bf16[2,32,16,512]{3,2,1,0:T(8,128)(2,1)S(1)}, bf16[2,32,16,512]{3,2,1,0:T(8,128)(2,1)}, u32[]{:S(2)}) %copy-start.2) | copy-done | bytes 1048600
  1.3 0.3 shard_map.64
  1.6 0.0 copy-start.3
  1.7 0.0 copy-done
  1.7 0.3 shard_map.65
  2.0 0.0 copy-start.1
  2.0 0.0 copy-start.4
  2.0 0.7 %collective-permute-start = (bf16[192,512]{1,0:T(8,128)(2,1)S(1)}, bf16[192,512]{1,0:T(8,128)(2,1)S(1)}, u32[]{:S(2)}, u32[]{:S(2)}) collective-permute-start(bf16[192,512]{1,0:T(8,128)(2,1)S(1)} %get-tuple-element.34), channel_id=1, source_target_pairs={{0,4},{4,0},{1,5},{5,1},{2,6},{6,2},{3,7},{7,3},{8,12},{12,8},{9,1... | collective-permute-start | bytes 589832 | tf_op jit(solution)/shard_map/ppermute | solution.py:51
  2.7 0.2 copy-done.3
  2.9 0.2 shard_map.66._
  3.1 0.7 %collective-permute-done.got_ref = bf16[192,512]{1,0:T(8,128)(2,1)S(1)} collective-permute-done((bf16[192,512]{1,0:T(8,128)(2,1)S(1)}, bf16[192,512]{1,0:T(8,128)(2,1)S(1)}, u32[]{:S(2)}, u32[]{:S(2)}) %collective-permute-start) | collective-permute-done | bytes 196640 | tf_op jit(solution)/shard_map/ppermute | solution.py:51
  3.8 3.5 %collective-permute-start.1 = (bf16[5,64,512]{2,1,0:T(8,128)(2,1)S(1)}, bf16[5,64,512]{2,1,0:T(8,128)(2,1)S(1)}, u32[]{:S(2)}, u32[]{:S(2)}) collective-permute-start(bf16[5,64,512]{2,1,0:T(8,128)(2,1)S(1)} %pad_maximum_fusion), channel_id=1, source_target_pairs={{1,4},{2,5},{3,6},{4,1},{5,2},{6,3},{9,12},{10,13},{11,14},{12,9},... | collective-permute-start | bytes 983048 | tf_op jit(solution)/shard_map/ppermute | solution.py:95
  7.3 0.0 copy-done.1
  7.3 0.0 copy-done.4
  7.3 5.1 %shard_map.67 = (f32[2,32,16,512]{3,2,1,0:T(8,128)S(1)}, f32[2,64,512]{2,1,0:T(8,128)S(1)}, bf16[512,256]{1,0:T(8,128)(2,1)S(1)}, bf16[1024,1536]{1,0:T(8,128)(2,1)S(1)}) custom-call(bf16[1024,1536]{1,0:T(8,128)(2,1)S(1)} %shard_map.66._, bf16[192,512]{1,0:T(8,128)(2,1)S(1)} %collective-permute-done.got_ref, ...), custom_call_target="tpu_custom_call", output_to_operand_aliasing={{3}: (0, {})} | custom-call | flops 4831838208 | bytes 13830144 | tf_op jit(solution)/shard_map/pallas_call | solution.py:21
  12.4 0.0 collective-permute-done.1.mine_ref
  12.4 0.2 collective-permute-start.2
  12.6 1.3 %collective-permute-start.5 = (bf16[512,256]{1,0:T(8,128)(2,1)S(1)}, bf16[512,256]{1,0:T(8,128)(2,1)S(1)}, u32[]{:S(2)}, u32[]{:S(2)}) collective-permute-start(bf16[512,256]{1,0:T(8,128)(2,1)S(1)} %get-tuple-element.43.end_ref), channel_id=1, source_target_pairs={{0,8},{8,0},{16,24},{4,20},{12,28},{1,9},{9,1},{17,25},{5,21},{13,... | collective-permute-start | bytes 786440 | tf_op jit(solution)/shard_map/ppermute | solution.py:284
  13.9 0.2 collective-permute-done.2.theirs_ref
  14.1 0.2 shard_map.68
  14.3 0.0 copy-start.5
  14.3 1.0 %shard_map.69 = (f32[2,32,16,256]{3,2,1,0:T(8,128)S(1)}, f32[2,64,256]{2,1,0:T(8,128)S(1)}, f32[2,128,256]{2,1,0:T(8,128)S(1)}, bf16[704,256]{1,0:T(8,128)(2,1)S(1)}) custom-call(bf16[256,1536]{1,0:T(8,128)(2,1)S(1)} %get-tuple-element.38.lhs_ref, bf16[3,3,512,512]{3,2,1,0:T(8,128)(2,1)S(1)} %copy-done.1, ...), custom_call_target="tpu_custom_call" | custom-call | flops 603979776 | bytes 9668608 | tf_op jit(solution)/shard_map/pallas_call | solution.py:21
  15.3 1.3 %collective-permute-start.3 = (bf16[704,256]{1,0:T(8,128)(2,1)S(1)}, bf16[704,256]{1,0:T(8,128)(2,1)S(1)}, u32[]{:S(2)}, u32[]{:S(2)}) collective-permute-start(bf16[704,256]{1,0:T(8,128)(2,1)S(1)} %get-tuple-element.42.end_ref), channel_id=1, source_target_pairs={{0,8},{8,0},{16,24},{4,20},{12,28},{1,9},{9,1},{17,25},{5,21},{13,... | collective-permute-start | bytes 1081352 | tf_op jit(solution)/shard_map/ppermute | solution.py:284
  16.6 3.4 %collective-permute-done.5.got_ref.refs_4_ = bf16[512,256]{1,0:T(8,128)(2,1)S(1)} collective-permute-done((bf16[512,256]{1,0:T(8,128)(2,1)S(1)}, bf16[512,256]{1,0:T(8,128)(2,1)S(1)}, u32[]{:S(2)}, u32[]{:S(2)}) %collective-permute-start.5) | collective-permute-done | bytes 262176 | tf_op jit(solution)/shard_map/ppermute | solution.py:284
  20.0 0.0 slice-start
  20.0 0.1 shard_map.71
  20.1 2.2 %collective-permute-start.6 = (bf16[512,256]{1,0:T(8,128)(2,1)S(1)}, bf16[512,256]{1,0:T(8,128)(2,1)S(1)}, u32[]{:S(2)}, u32[]{:S(2)}) collective-permute-start(bf16[512,256]{1,0:T(8,128)(2,1)S(1)} %shard_map.71), channel_id=1, source_target_pairs={{0,16},{8,24},{4,12},{20,28},{28,20},{1,17},{9,25},{5,13},{21,29},... | collective-permute-start | bytes 786440 | tf_op jit(solution)/shard_map/ppermute | solution.py:287
  22.3 1.5 %collective-permute-done.3.got_ref.refs_4_.refs_7_ = bf16[704,256]{1,0:T(8,128)(2,1)S(1)} collective-permute-done((bf16[704,256]{1,0:T(8,128)(2,1)S(1)}, bf16[704,256]{1,0:T(8,128)(2,1)S(1)}, u32[]{:S(2)}, u32[]{:S(2)}) %collective-permute-start.3) | collective-permute-done | bytes 360480 | tf_op jit(solution)/shard_map/ppermute | solution.py:284
  23.9 0.2 shard_map.70
  24.0 2.1 %collective-permute-start.4 = (bf16[704,256]{1,0:T(8,128)(2,1)S(1)}, bf16[704,256]{1,0:T(8,128)(2,1)S(1)}, u32[]{:S(2)}, u32[]{:S(2)}) collective-permute-start(bf16[704,256]{1,0:T(8,128)(2,1)S(1)} %shard_map.70), channel_id=1, source_target_pairs={{0,16},{8,24},{4,12},{20,28},{28,20},{1,17},{9,25},{5,13},{21,29},... | collective-permute-start | bytes 1081352 | tf_op jit(solution)/shard_map/ppermute | solution.py:287
  26.2 1.6 %collective-permute-done.6.refs_5_ = bf16[512,256]{1,0:T(8,128)(2,1)S(1)} collective-permute-done((bf16[512,256]{1,0:T(8,128)(2,1)S(1)}, bf16[512,256]{1,0:T(8,128)(2,1)S(1)}, u32[]{:S(2)}, u32[]{:S(2)}) %collective-permute-start.6) | collective-permute-done | bytes 262176 | tf_op jit(solution)/shard_map/ppermute | solution.py:287
  27.8 0.0 copy-done.5
  27.8 0.0 slice-start.1
  27.9 2.2 %collective-permute-start.7 = (bf16[2,16,256]{2,1,0:T(8,128)(2,1)S(1)}, bf16[2,16,256]{2,1,0:T(8,128)(2,1)S(1)}, u32[]{:S(2)}, u32[]{:S(2)}) collective-permute-start(bf16[2,16,256]{2,1,0:T(8,128)(2,1)S(1)} %shard_map.73), channel_id=1, source_target_pairs={{0,4},{4,0},{1,5},{5,1},{2,6},{6,2},{3,7},{7,3},{8,12},{12,8},{9,1... | collective-permute-start | bytes 49160 | tf_op jit(solution)/shard_map/ppermute | solution.py:51
  30.0 0.6 %shard_map.72._ = bf16[1024,768]{1,0:T(8,128)(2,1)S(1)} custom-call(f32[2,32,16,512]{3,2,1,0:T(8,128)S(1)} %get-tuple-element.39.total_ref.refs_0_, f32[32,16,512]{2,1,0:T(8,128)S(1)} %copy-done, s32[1,512]{1,0:T(1,128)S(1)} %bitcast.10, f32[1,512]{1,0:T(1,128)S(1)} %bitcast.14, bf16[512,256]{1,0:T(8,128)(2,1)S(1)} %collective-permute-done.5.got_ref.refs_4_, ...), custom_call_target="tpu_custom_call" | custom-call | bytes 5246976 | tf_op jit(solution)/shard_map/pallas_call | solution.py:21
  30.7 0.2 collective-permute-done.7.got_ref
  30.9 0.0 slice-done
  30.9 0.0 slice-done.1
  30.9 1.4 %shard_map.74 = (f32[2,32,16,256]{3,2,1,0:T(8,128)S(1)}, bf16[1024,768]{1,0:T(8,128)(2,1)S(1)}) custom-call(bf16[1024,768]{1,0:T(8,128)(2,1)S(1)} %shard_map.72._, bf16[2,16,256]{2,1,0:T(8,128)(2,1)S(1)} %collective-permute-done.7.got_ref, bf16[3,3,512,512]{3,2,1,0:T(8,128)(2,1)S(1)} %bitcast.4), custom_call_target="tpu_custom_call", output_to_operand_aliasing={{1}: (0, {})} | custom-call | flops 1207959552 | bytes 8929280 | tf_op jit(solution)/shard_map/pallas_call | solution.py:21
  32.3 1.4 %shard_map.75.refs_1_ = f32[2,32,16,256]{3,2,1,0:T(8,128)S(1)} custom-call(bf16[1024,768]{1,0:T(8,128)(2,1)S(1)} %get-tuple-element.45.lhs_ref, bf16[3,3,512,512]{3,2,1,0:T(8,128)(2,1)S(1)} %bitcast.4), custom_call_target="tpu_custom_call" | custom-call | flops 1207959552 | bytes 7340032 | tf_op jit(solution)/shard_map/pallas_call | solution.py:21
  33.7 0.1 shard_map.77.refs_4_
  33.8 0.0 collective-permute-done.4.refs_5_.refs_8_
  33.8 0.3 shard_map.78
  34.1 1.0 %collective-permute-start.8 = (bf16[2,32,256]{2,1,0:T(8,128)(2,1)S(1)}, bf16[2,32,256]{2,1,0:T(8,128)(2,1)S(1)}, u32[]{:S(2)}, u32[]{:S(2)}) collective-permute-start(bf16[2,32,256]{2,1,0:T(8,128)(2,1)S(1)} %get-tuple-element.51), channel_id=1, source_target_pairs={{0,4},{4,0},{1,5},{5,1},{2,6},{6,2},{3,7},{7,3},{8,12},{12,8},{9,1... | collective-permute-start | bytes 98312 | tf_op jit(solution)/shard_map/ppermute | solution.py:51
  35.2 0.6 %shard_map.76._ = bf16[1152,768]{1,0:T(8,128)(2,1)S(1)} custom-call(f32[2,32,16,256]{3,2,1,0:T(8,128)S(1)} %get-tuple-element.41.refs_0_, f32[32,16,512]{2,1,0:T(8,128)S(1)} %copy-done, s32[1,512]{1,0:T(1,128)S(1)} %bitcast.12, f32[1,512]{1,0:T(1,128)S(1)} %bitcast.16, bf16[704,256]{1,0:T(8,128)(2,1)S(1)} %collective-permute-done.3.got_ref.refs_4_.refs_7_, ...), custom_call_target="tpu_custom_call" | custom-call | bytes 4591616 | tf_op jit(solution)/shard_map/pallas_call | solution.py:21
  35.7 0.3 collective-permute-done.8.got_ref
  36.0 4.4 %shard_map.79 = (bf16[2,32,16,512]{3,2,1,0:T(8,128)(2,1)}, bf16[1152,768]{1,0:T(8,128)(2,1)S(1)}) custom-call(bf16[1152,768]{1,0:T(8,128)(2,1)S(1)} %shard_map.76._, bf16[2,32,256]{2,1,0:T(8,128)(2,1)S(1)} %collective-permute-done.8.got_ref, bf16[2,64,256]{2,1,0:T(8,128)(2,1)S(1)} %get-tuple-element.52.beside_ref, ...), custom_call_target="tpu_custom_call", output_to_operand_aliasing={{1}: (0, {})} | custom-call | flops 2415919104 | bytes 11632640 | tf_op jit(solution)/shard_map/pallas_call | solution.py:21
  (4 shorter events, 0.1 us)
Async XLA Ops:
  0.0 1.7 %copy-start = (f32[32,16,512]{2,1,0:T(8,128)S(1)}, f32[32,16,512]{2,1,0:T(8,128)}, u32[]{:S(2)}) copy-start(f32[32,16,512]{2,1,0:T(8,128)} %refs_3_.1) | copy-start | bytes 3145732
  0.0 1.3 %copy-start.2 = (bf16[2,32,16,512]{3,2,1,0:T(8,128)(2,1)S(1)}, bf16[2,32,16,512]{3,2,1,0:T(8,128)(2,1)}, u32[]{:S(2)}) copy-start(bf16[2,32,16,512]{3,2,1,0:T(8,128)(2,1)} %cells_ref.3) | copy-start | bytes 3145732
  1.6 1.2 %copy-start.3 = (bf16[2,32,16,512]{3,2,1,0:T(8,128)(2,1)S(1)}, bf16[2,32,16,512]{3,2,1,0:T(8,128)(2,1)}, u32[]{:S(2)}) copy-start(bf16[2,32,16,512]{3,2,1,0:T(8,128)(2,1)} %cells_ref.3) | copy-start | bytes 3145732
  2.0 5.4 %copy-start.1 = (bf16[3,3,512,512]{3,2,1,0:T(8,128)(2,1)S(1)}, bf16[3,3,512,512]{3,2,1,0:T(8,128)(2,1)}, u32[]{:S(2)}) copy-start(bf16[3,3,512,512]{3,2,1,0:T(8,128)(2,1)} %weight_ref.6) | copy-start | bytes 14155780
  2.0 5.4 %copy-start.4 = (s32[512]{0:T(512)S(1)}, s32[512]{0:T(512)}, u32[]{:S(2)}) copy-start(s32[512]{0:T(512)} %param.9) | copy-start | bytes 6148
  2.0 1.8 %collective-permute-start = (bf16[192,512]{1,0:T(8,128)(2,1)S(1)}, bf16[192,512]{1,0:T(8,128)(2,1)S(1)}, u32[]{:S(2)}, u32[]{:S(2)}) collective-permute-start(bf16[192,512]{1,0:T(8,128)(2,1)S(1)} %get-tuple-element.34), channel_id=1, source_target_pairs={{0,4},{4,0},{1,5},{5,1},{2,6},{6,2},{3,7},{7,3},{8,12},{12,8},{9,1... | collective-permute-start | bytes 589832 | tf_op jit(solution)/shard_map/ppermute | solution.py:51
  3.8 8.6 %collective-permute-start.1 = (bf16[5,64,512]{2,1,0:T(8,128)(2,1)S(1)}, bf16[5,64,512]{2,1,0:T(8,128)(2,1)S(1)}, u32[]{:S(2)}, u32[]{:S(2)}) collective-permute-start(bf16[5,64,512]{2,1,0:T(8,128)(2,1)S(1)} %pad_maximum_fusion), channel_id=1, source_target_pairs={{1,4},{2,5},{3,6},{4,1},{5,2},{6,3},{9,12},{10,13},{11,14},{12,9},... | collective-permute-start | bytes 983048 | tf_op jit(solution)/shard_map/ppermute | solution.py:95
  12.4 1.7 %collective-permute-start.2 = (bf16[5,64,512]{2,1,0:T(8,128)(2,1)S(1)}, bf16[5,64,512]{2,1,0:T(8,128)(2,1)S(1)}, u32[]{:S(2)}, u32[]{:S(2)}) collective-permute-start(bf16[5,64,512]{2,1,0:T(8,128)(2,1)S(1)} %collective-permute-done.1.mine_ref), channel_id=1, source_target_pairs={{0,4},{4,0},{1,5},{5,1},{2,6},{6,2},{3,7},{7,3},{8,12},{12,8},{9,1... | collective-permute-start | bytes 983048 | tf_op jit(solution)/shard_map/ppermute | solution.py:51
  12.6 7.4 %collective-permute-start.5 = (bf16[512,256]{1,0:T(8,128)(2,1)S(1)}, bf16[512,256]{1,0:T(8,128)(2,1)S(1)}, u32[]{:S(2)}, u32[]{:S(2)}) collective-permute-start(bf16[512,256]{1,0:T(8,128)(2,1)S(1)} %get-tuple-element.43.end_ref), channel_id=1, source_target_pairs={{0,8},{8,0},{16,24},{4,20},{12,28},{1,9},{9,1},{17,25},{5,21},{13,... | collective-permute-start | bytes 786440 | tf_op jit(solution)/shard_map/ppermute | solution.py:284
  14.3 13.5 %copy-start.5 = (f32[512]{0:T(512)S(1)}, f32[512]{0:T(512)}, u32[]{:S(2)}) copy-start(f32[512]{0:T(512)} %param.10) | copy-start | bytes 6148
  15.3 8.6 %collective-permute-start.3 = (bf16[704,256]{1,0:T(8,128)(2,1)S(1)}, bf16[704,256]{1,0:T(8,128)(2,1)S(1)}, u32[]{:S(2)}, u32[]{:S(2)}) collective-permute-start(bf16[704,256]{1,0:T(8,128)(2,1)S(1)} %get-tuple-element.42.end_ref), channel_id=1, source_target_pairs={{0,8},{8,0},{16,24},{4,20},{12,28},{1,9},{9,1},{17,25},{5,21},{13,... | collective-permute-start | bytes 1081352 | tf_op jit(solution)/shard_map/ppermute | solution.py:284
  20.0 10.9 %slice-start = ((s8[4718592]{0:T(1024)(128)(4,1)}), s8[4194304]{0:T(1024)(128)(4,1)S(1)}, s32[]{:S(2)}) async-start(s8[4718592]{0:T(1024)(128)(4,1)} %bitcast.3), calls=%async_computation | async-start | bytes 8388608
  20.1 7.7 %collective-permute-start.6 = (bf16[512,256]{1,0:T(8,128)(2,1)S(1)}, bf16[512,256]{1,0:T(8,128)(2,1)S(1)}, u32[]{:S(2)}, u32[]{:S(2)}) collective-permute-start(bf16[512,256]{1,0:T(8,128)(2,1)S(1)} %shard_map.71), channel_id=1, source_target_pairs={{0,16},{8,24},{4,12},{20,28},{28,20},{1,17},{9,25},{5,13},{21,29},... | collective-permute-start | bytes 786440 | tf_op jit(solution)/shard_map/ppermute | solution.py:287
  24.0 9.8 %collective-permute-start.4 = (bf16[704,256]{1,0:T(8,128)(2,1)S(1)}, bf16[704,256]{1,0:T(8,128)(2,1)S(1)}, u32[]{:S(2)}, u32[]{:S(2)}) collective-permute-start(bf16[704,256]{1,0:T(8,128)(2,1)S(1)} %shard_map.70), channel_id=1, source_target_pairs={{0,16},{8,24},{4,12},{20,28},{28,20},{1,17},{9,25},{5,13},{21,29},... | collective-permute-start | bytes 1081352 | tf_op jit(solution)/shard_map/ppermute | solution.py:287
  27.8 3.1 %slice-start.1 = ((s8[4718592]{0:T(1024)(128)(4,1)}), s8[524288]{0:T(1024)(128)(4,1)S(1)}, s32[]{:S(2)}) async-start(s8[4718592]{0:T(1024)(128)(4,1)} %bitcast.3), calls=%async_computation.1 | async-start | bytes 1048576
  27.9 3.0 %collective-permute-start.7 = (bf16[2,16,256]{2,1,0:T(8,128)(2,1)S(1)}, bf16[2,16,256]{2,1,0:T(8,128)(2,1)S(1)}, u32[]{:S(2)}, u32[]{:S(2)}) collective-permute-start(bf16[2,16,256]{2,1,0:T(8,128)(2,1)S(1)} %shard_map.73), channel_id=1, source_target_pairs={{0,4},{4,0},{1,5},{5,1},{2,6},{6,2},{3,7},{7,3},{8,12},{12,8},{9,1... | collective-permute-start | bytes 49160 | tf_op jit(solution)/shard_map/ppermute | solution.py:51
  34.1 1.9 %collective-permute-start.8 = (bf16[2,32,256]{2,1,0:T(8,128)(2,1)S(1)}, bf16[2,32,256]{2,1,0:T(8,128)(2,1)S(1)}, u32[]{:S(2)}, u32[]{:S(2)}) collective-permute-start(bf16[2,32,256]{2,1,0:T(8,128)(2,1)S(1)} %get-tuple-element.51), channel_id=1, source_target_pairs={{0,4},{4,0},{1,5},{5,1},{2,6},{6,2},{3,7},{7,3},{8,12},{12,8},{9,1... | collective-permute-start | bytes 98312 | tf_op jit(solution)/shard_map/ppermute | solution.py:51

commit v11 on v10

--- a/solution.py
+++ b/solution.py
@@ -55,8 +55,8 @@
     zero, one = is_core(0), is_core(1)
     count, rows, _ = keep_ref.shape
     at = give_ref.shape[0] - (count - index) * rows
-    give_ref[at : at + rows] = (zero * right + one * left).astype(give_ref.dtype)
-    keep_ref[index] = (zero * left + one * right).astype(keep_ref.dtype)
+    give_ref[at : at + rows] = (zero * left + one * right).astype(give_ref.dtype)
+    keep_ref[index] = (zero * right + one * left).astype(keep_ref.dtype)
 
 
 def edges_kernel(cells_ref, give_ref, keep_ref, wide_ref):
@@ -89,7 +89,7 @@
 def trade_columns(give, keep, at):
     chips = lax.axis_size("sy")
     got = swap_cores(give)
-    pairs = [(chip, chips + chip - 1) for chip in range(1, chips)]
+    pairs = [(chip, chips + chip + 1) for chip in range(chips - 1)]
     pairs += [(after, before) for before, after in pairs]
     columns = jnp.concatenate([keep, got[at:].reshape(keep.shape)], axis=1)
     return got, lax.ppermute(columns, ("sx", "sy"), pairs)
@@ -179,13 +179,13 @@
             own = row_taps(own[rows:], own[rows - 1 : rows], own[:1])
             other = row_taps(other[:rows], other[2 * rows - 1 :], other[rows : rows + 1])
             for swapped, taps in enumerate((own, other)):
-                slot = jnp.where(core == swapped, slots[0][depth], slots[1][depth])
+                slot = jnp.where(core == swapped, slots[1][depth], slots[0][depth])
                 at = pl.multiple_of(slot * room + frame * rows, rows)
                 lhs_ref[pl.ds(at, rows)] = taps.astype(lhs_ref.dtype)
     own = mine_ref[2 * count, rows:].astype(jnp.float32)
     other = theirs_ref[2 * count, :rows].astype(jnp.float32)
-    start_ref[:rows] = zero * own + one * other
-    start_ref[rows:] = zero * other + one * own
+    start_ref[:rows] = zero * other + one * own
+    start_ref[rows:] = zero * own + one * other
 
 
 def drive_kernel(

time: 40.9 us -> 40.7 us (level)
  starting transfers between devices: 14.5 us -> 13.1 us
  waiting for transfers between devices: 8.06 us -> 8.97 us
    ppermute x1, starting transfers between devices: 3.46 us -> 2.33 us  [trade_columns(): return (got, lax.ppermute(columns, ('sx', 'sy'), pairs))]
    ppermute x1, waiting for transfers between devices: 0.01 us -> 0.93 us  [trade_columns(): return (got, lax.ppermute(columns, ('sx', 'sy'), pairs))]
where the time goes in v11:
time: 40.7 us; the launch traced here: 40.2 us
  Pallas kernels  16.2 us (40%)
  starting transfers between devices  13.1 us (32%)
  waiting for transfers between devices  8.97 us (22%)
  local copies, waits for them, and re-layouts  1.51 us (4%)
    pallas_call x16, Pallas kernels, call(): pl.pallas_call(kernel, in_specs=[WHOLE] * len(args), out_specs=out_specs...  16.2 us
    ppermute x2, waiting for transfers between devices, exchange_four(): got = lax.ppermute(end, axes, first_round)  5.16 us
    ppermute x2, starting transfers between devices, exchange_four(): arrivals.append((got, lax.ppermute(relayed, axes, second_round)))  4.28 us
    ppermute x4, starting transfers between devices, swap_cores(): return lax.ppermute(array, 'sx', [(0, 1), (1, 0)])  3.91 us
    ppermute x2, starting transfers between devices, exchange_four(): got = lax.ppermute(end, axes, first_round)  2.57 us
    ppermute x1, starting transfers between devices, trade_columns(): return (got, lax.ppermute(columns, ('sx', 'sy'), pairs))  2.33 us
    ppermute x2, waiting for transfers between devices, exchange_four(): arrivals.append((got, lax.ppermute(relayed, axes, second_round)))  1.65 us
    unnamed x16, local copies, waits for them, and re-layouts  1.5 us
  transfers between devices with their start and end apart: 9, of which 7 were waited for; matrix products, arithmetic and copies ran while one was open for 0% of the time, Pallas kernels for 27%

profile of v11, /device:TPU:23, one launch (start us, length us, event | category | flops | bytes accessed | tf_op | source)
XLA Modules:
  0.0 40.2 jit_solution(10347663925049504981)
XLA Ops:
  0.0 0.0 copy-start
  0.0 0.0 copy-start.2
  0.0 1.3 %copy-done.2 = bf16[2,32,16,512]{3,2,1,0:T(8,128)(2,1)S(1)} copy-done((bf16[2,32,16,512]{3,2,1,0:T(8,128)(2,1)S(1)}, bf16[2,32,16,512]{3,2,1,0:T(8,128)(2,1)}, u32[]{:S(2)}) %copy-start.2) | copy-done | bytes 1048600
  1.3 0.3 shard_map.64
  1.7 0.0 copy-start.3
  1.7 0.0 copy-done
  1.7 0.3 shard_map.65
  2.0 0.0 copy-start.1
  2.0 0.0 copy-start.4
  2.0 0.7 %collective-permute-start = (bf16[192,512]{1,0:T(8,128)(2,1)S(1)}, bf16[192,512]{1,0:T(8,128)(2,1)S(1)}, u32[]{:S(2)}, u32[]{:S(2)}) collective-permute-start(bf16[192,512]{1,0:T(8,128)(2,1)S(1)} %get-tuple-element.34), channel_id=1, source_target_pairs={{0,4},{4,0},{1,5},{5,1},{2,6},{6,2},{3,7},{7,3},{8,12},{12,8},{9,1... | collective-permute-start | bytes 589832 | tf_op jit(solution)/shard_map/ppermute | solution.py:51
  2.7 0.2 copy-done.3
  2.9 0.2 shard_map.66._
  3.1 0.7 %collective-permute-done.got_ref = bf16[192,512]{1,0:T(8,128)(2,1)S(1)} collective-permute-done((bf16[192,512]{1,0:T(8,128)(2,1)S(1)}, bf16[192,512]{1,0:T(8,128)(2,1)S(1)}, u32[]{:S(2)}, u32[]{:S(2)}) %collective-permute-start) | collective-permute-done | bytes 196640 | tf_op jit(solution)/shard_map/ppermute | solution.py:51
  3.8 2.3 %collective-permute-start.1 = (bf16[5,64,512]{2,1,0:T(8,128)(2,1)S(1)}, bf16[5,64,512]{2,1,0:T(8,128)(2,1)S(1)}, u32[]{:S(2)}, u32[]{:S(2)}) collective-permute-start(bf16[5,64,512]{2,1,0:T(8,128)(2,1)S(1)} %pad_maximum_fusion), channel_id=1, source_target_pairs={{0,5},{1,6},{2,7},{5,0},{6,1},{7,2},{8,13},{9,14},{10,15},{13,8},{... | collective-permute-start | bytes 983048 | tf_op jit(solution)/shard_map/ppermute | solution.py:95
  6.2 0.0 copy-done.1
  6.2 0.0 copy-done.4
  6.2 5.1 %shard_map.67 = (f32[2,32,16,512]{3,2,1,0:T(8,128)S(1)}, f32[2,64,512]{2,1,0:T(8,128)S(1)}, bf16[512,256]{1,0:T(8,128)(2,1)S(1)}, bf16[1024,1536]{1,0:T(8,128)(2,1)S(1)}) custom-call(bf16[1024,1536]{1,0:T(8,128)(2,1)S(1)} %shard_map.66._, bf16[192,512]{1,0:T(8,128)(2,1)S(1)} %collective-permute-done.got_ref, ...), custom_call_target="tpu_custom_call", output_to_operand_aliasing={{3}: (0, {})} | custom-call | flops 4831838208 | bytes 13830144 | tf_op jit(solution)/shard_map/pallas_call | solution.py:21
  11.3 0.9 %collective-permute-done.1.mine_ref = bf16[5,64,512]{2,1,0:T(8,128)(2,1)S(1)} collective-permute-done((bf16[5,64,512]{2,1,0:T(8,128)(2,1)S(1)}, bf16[5,64,512]{2,1,0:T(8,128)(2,1)S(1)}, u32[]{:S(2)}, u32[]{:S(2)}) %collective-permute-start.1) | collective-permute-done | bytes 327712 | tf_op jit(solution)/shard_map/ppermute | solution.py:95
  12.2 0.4 %collective-permute-start.2 = (bf16[5,64,512]{2,1,0:T(8,128)(2,1)S(1)}, bf16[5,64,512]{2,1,0:T(8,128)(2,1)S(1)}, u32[]{:S(2)}, u32[]{:S(2)}) collective-permute-start(bf16[5,64,512]{2,1,0:T(8,128)(2,1)S(1)} %collective-permute-done.1.mine_ref), channel_id=1, source_target_pairs={{0,4},{4,0},{1,5},{5,1},{2,6},{6,2},{3,7},{7,3},{8,12},{12,8},{9,1... | collective-permute-start | bytes 983048 | tf_op jit(solution)/shard_map/ppermute | solution.py:51
  12.6 1.3 %collective-permute-start.5 = (bf16[512,256]{1,0:T(8,128)(2,1)S(1)}, bf16[512,256]{1,0:T(8,128)(2,1)S(1)}, u32[]{:S(2)}, u32[]{:S(2)}) collective-permute-start(bf16[512,256]{1,0:T(8,128)(2,1)S(1)} %get-tuple-element.43.end_ref), channel_id=1, source_target_pairs={{0,8},{8,0},{16,24},{4,20},{12,28},{1,9},{9,1},{17,25},{5,21},{13,... | collective-permute-start | bytes 786440 | tf_op jit(solution)/shard_map/ppermute | solution.py:284
  13.9 0.0 collective-permute-done.2.theirs_ref
  13.9 0.2 shard_map.68
  14.1 0.0 copy-start.5
  14.1 1.0 %shard_map.69 = (f32[2,32,16,256]{3,2,1,0:T(8,128)S(1)}, f32[2,64,256]{2,1,0:T(8,128)S(1)}, f32[2,128,256]{2,1,0:T(8,128)S(1)}, bf16[704,256]{1,0:T(8,128)(2,1)S(1)}) custom-call(bf16[256,1536]{1,0:T(8,128)(2,1)S(1)} %get-tuple-element.38.lhs_ref, bf16[3,3,512,512]{3,2,1,0:T(8,128)(2,1)S(1)} %copy-done.1, ...), custom_call_target="tpu_custom_call" | custom-call | flops 603979776 | bytes 9668608 | tf_op jit(solution)/shard_map/pallas_call | solution.py:21
  15.1 1.3 %collective-permute-start.3 = (bf16[704,256]{1,0:T(8,128)(2,1)S(1)}, bf16[704,256]{1,0:T(8,128)(2,1)S(1)}, u32[]{:S(2)}, u32[]{:S(2)}) collective-permute-start(bf16[704,256]{1,0:T(8,128)(2,1)S(1)} %get-tuple-element.42.end_ref), channel_id=1, source_target_pairs={{0,8},{8,0},{16,24},{4,20},{12,28},{1,9},{9,1},{17,25},{5,21},{13,... | collective-permute-start | bytes 1081352 | tf_op jit(solution)/shard_map/ppermute | solution.py:284
  16.4 3.6 %collective-permute-done.5.got_ref.refs_4_ = bf16[512,256]{1,0:T(8,128)(2,1)S(1)} collective-permute-done((bf16[512,256]{1,0:T(8,128)(2,1)S(1)}, bf16[512,256]{1,0:T(8,128)(2,1)S(1)}, u32[]{:S(2)}, u32[]{:S(2)}) %collective-permute-start.5) | collective-permute-done | bytes 262176 | tf_op jit(solution)/shard_map/ppermute | solution.py:284
  20.0 0.0 slice-start
  20.0 0.1 shard_map.71
  20.2 2.2 %collective-permute-start.6 = (bf16[512,256]{1,0:T(8,128)(2,1)S(1)}, bf16[512,256]{1,0:T(8,128)(2,1)S(1)}, u32[]{:S(2)}, u32[]{:S(2)}) collective-permute-start(bf16[512,256]{1,0:T(8,128)(2,1)S(1)} %shard_map.71), channel_id=1, source_target_pairs={{0,16},{8,24},{4,12},{20,28},{28,20},{1,17},{9,25},{5,13},{21,29},... | collective-permute-start | bytes 786440 | tf_op jit(solution)/shard_map/ppermute | solution.py:287
  22.4 1.5 %collective-permute-done.3.got_ref.refs_4_.refs_7_ = bf16[704,256]{1,0:T(8,128)(2,1)S(1)} collective-permute-done((bf16[704,256]{1,0:T(8,128)(2,1)S(1)}, bf16[704,256]{1,0:T(8,128)(2,1)S(1)}, u32[]{:S(2)}, u32[]{:S(2)}) %collective-permute-start.3) | collective-permute-done | bytes 360480 | tf_op jit(solution)/shard_map/ppermute | solution.py:284
  23.9 0.2 shard_map.70
  24.1 2.1 %collective-permute-start.4 = (bf16[704,256]{1,0:T(8,128)(2,1)S(1)}, bf16[704,256]{1,0:T(8,128)(2,1)S(1)}, u32[]{:S(2)}, u32[]{:S(2)}) collective-permute-start(bf16[704,256]{1,0:T(8,128)(2,1)S(1)} %shard_map.70), channel_id=1, source_target_pairs={{0,16},{8,24},{4,12},{20,28},{28,20},{1,17},{9,25},{5,13},{21,29},... | collective-permute-start | bytes 1081352 | tf_op jit(solution)/shard_map/ppermute | solution.py:287
  26.2 1.6 %collective-permute-done.6.refs_5_ = bf16[512,256]{1,0:T(8,128)(2,1)S(1)} collective-permute-done((bf16[512,256]{1,0:T(8,128)(2,1)S(1)}, bf16[512,256]{1,0:T(8,128)(2,1)S(1)}, u32[]{:S(2)}, u32[]{:S(2)}) %collective-permute-start.6) | collective-permute-done | bytes 262176 | tf_op jit(solution)/shard_map/ppermute | solution.py:287
  27.8 0.0 copy-done.5
  27.8 0.0 slice-start.1
  27.9 1.9 %collective-permute-start.7 = (bf16[2,16,256]{2,1,0:T(8,128)(2,1)S(1)}, bf16[2,16,256]{2,1,0:T(8,128)(2,1)S(1)}, u32[]{:S(2)}, u32[]{:S(2)}) collective-permute-start(bf16[2,16,256]{2,1,0:T(8,128)(2,1)S(1)} %shard_map.73), channel_id=1, source_target_pairs={{0,4},{4,0},{1,5},{5,1},{2,6},{6,2},{3,7},{7,3},{8,12},{12,8},{9,1... | collective-permute-start | bytes 49160 | tf_op jit(solution)/shard_map/ppermute | solution.py:51
  29.8 0.6 %shard_map.72._ = bf16[1024,768]{1,0:T(8,128)(2,1)S(1)} custom-call(f32[2,32,16,512]{3,2,1,0:T(8,128)S(1)} %get-tuple-element.39.total_ref.refs_0_, f32[32,16,512]{2,1,0:T(8,128)S(1)} %copy-done, s32[1,512]{1,0:T(1,128)S(1)} %bitcast.10, f32[1,512]{1,0:T(1,128)S(1)} %bitcast.14, bf16[512,256]{1,0:T(8,128)(2,1)S(1)} %collective-permute-done.5.got_ref.refs_4_, ...), custom_call_target="tpu_custom_call" | custom-call | bytes 5246976 | tf_op jit(solution)/shard_map/pallas_call | solution.py:21
  30.4 0.2 collective-permute-done.7.got_ref
  30.6 0.0 slice-done
  30.6 0.0 slice-done.1
  30.6 1.4 %shard_map.74 = (f32[2,32,16,256]{3,2,1,0:T(8,128)S(1)}, bf16[1024,768]{1,0:T(8,128)(2,1)S(1)}) custom-call(bf16[1024,768]{1,0:T(8,128)(2,1)S(1)} %shard_map.72._, bf16[2,16,256]{2,1,0:T(8,128)(2,1)S(1)} %collective-permute-done.7.got_ref, bf16[3,3,512,512]{3,2,1,0:T(8,128)(2,1)S(1)} %bitcast.4), custom_call_target="tpu_custom_call", output_to_operand_aliasing={{1}: (0, {})} | custom-call | flops 1207959552 | bytes 8929280 | tf_op jit(solution)/shard_map/pallas_call | solution.py:21
  32.0 1.4 %shard_map.75.refs_1_ = f32[2,32,16,256]{3,2,1,0:T(8,128)S(1)} custom-call(bf16[1024,768]{1,0:T(8,128)(2,1)S(1)} %get-tuple-element.45.lhs_ref, bf16[3,3,512,512]{3,2,1,0:T(8,128)(2,1)S(1)} %bitcast.4), custom_call_target="tpu_custom_call" | custom-call | flops 1207959552 | bytes 7340032 | tf_op jit(solution)/shard_map/pallas_call | solution.py:21
  33.4 0.1 shard_map.77.refs_4_
  33.5 0.0 collective-permute-done.4.refs_5_.refs_8_
  33.5 0.3 shard_map.78
  33.8 0.9 %collective-permute-start.8 = (bf16[2,32,256]{2,1,0:T(8,128)(2,1)S(1)}, bf16[2,32,256]{2,1,0:T(8,128)(2,1)S(1)}, u32[]{:S(2)}, u32[]{:S(2)}) collective-permute-start(bf16[2,32,256]{2,1,0:T(8,128)(2,1)S(1)} %get-tuple-element.51), channel_id=1, source_target_pairs={{0,4},{4,0},{1,5},{5,1},{2,6},{6,2},{3,7},{7,3},{8,12},{12,8},{9,1... | collective-permute-start | bytes 98312 | tf_op jit(solution)/shard_map/ppermute | solution.py:51
  34.7 0.6 %shard_map.76._ = bf16[1152,768]{1,0:T(8,128)(2,1)S(1)} custom-call(f32[2,32,16,256]{3,2,1,0:T(8,128)S(1)} %get-tuple-element.41.refs_0_, f32[32,16,512]{2,1,0:T(8,128)S(1)} %copy-done, s32[1,512]{1,0:T(1,128)S(1)} %bitcast.12, f32[1,512]{1,0:T(1,128)S(1)} %bitcast.16, bf16[704,256]{1,0:T(8,128)(2,1)S(1)} %collective-permute-done.3.got_ref.refs_4_.refs_7_, ...), custom_call_target="tpu_custom_call" | custom-call | bytes 4591616 | tf_op jit(solution)/shard_map/pallas_call | solution.py:21
  35.3 0.3 collective-permute-done.8.got_ref
  35.6 4.4 %shard_map.79 = (bf16[2,32,16,512]{3,2,1,0:T(8,128)(2,1)}, bf16[1152,768]{1,0:T(8,128)(2,1)S(1)}) custom-call(bf16[1152,768]{1,0:T(8,128)(2,1)S(1)} %shard_map.76._, bf16[2,32,256]{2,1,0:T(8,128)(2,1)S(1)} %collective-permute-done.8.got_ref, bf16[2,64,256]{2,1,0:T(8,128)(2,1)S(1)} %get-tuple-element.52.beside_ref, ...), custom_call_target="tpu_custom_call", output_to_operand_aliasing={{1}: (0, {})} | custom-call | flops 2415919104 | bytes 11632640 | tf_op jit(solution)/shard_map/pallas_call | solution.py:21
  (4 shorter events, 0.1 us)
Async XLA Ops:
  0.0 1.7 %copy-start = (f32[32,16,512]{2,1,0:T(8,128)S(1)}, f32[32,16,512]{2,1,0:T(8,128)}, u32[]{:S(2)}) copy-start(f32[32,16,512]{2,1,0:T(8,128)} %refs_3_.1) | copy-start | bytes 3145732
  0.0 1.3 %copy-start.2 = (bf16[2,32,16,512]{3,2,1,0:T(8,128)(2,1)S(1)}, bf16[2,32,16,512]{3,2,1,0:T(8,128)(2,1)}, u32[]{:S(2)}) copy-start(bf16[2,32,16,512]{3,2,1,0:T(8,128)(2,1)} %cells_ref.3) | copy-start | bytes 3145732
  1.7 1.2 %copy-start.3 = (bf16[2,32,16,512]{3,2,1,0:T(8,128)(2,1)S(1)}, bf16[2,32,16,512]{3,2,1,0:T(8,128)(2,1)}, u32[]{:S(2)}) copy-start(bf16[2,32,16,512]{3,2,1,0:T(8,128)(2,1)} %cells_ref.3) | copy-start | bytes 3145732
  2.0 4.2 %copy-start.1 = (bf16[3,3,512,512]{3,2,1,0:T(8,128)(2,1)S(1)}, bf16[3,3,512,512]{3,2,1,0:T(8,128)(2,1)}, u32[]{:S(2)}) copy-start(bf16[3,3,512,512]{3,2,1,0:T(8,128)(2,1)} %weight_ref.6) | copy-start | bytes 14155780
  2.0 4.2 %copy-start.4 = (s32[512]{0:T(512)S(1)}, s32[512]{0:T(512)}, u32[]{:S(2)}) copy-start(s32[512]{0:T(512)} %param.9) | copy-start | bytes 6148
  2.0 1.8 %collective-permute-start = (bf16[192,512]{1,0:T(8,128)(2,1)S(1)}, bf16[192,512]{1,0:T(8,128)(2,1)S(1)}, u32[]{:S(2)}, u32[]{:S(2)}) collective-permute-start(bf16[192,512]{1,0:T(8,128)(2,1)S(1)} %get-tuple-element.34), channel_id=1, source_target_pairs={{0,4},{4,0},{1,5},{5,1},{2,6},{6,2},{3,7},{7,3},{8,12},{12,8},{9,1... | collective-permute-start | bytes 589832 | tf_op jit(solution)/shard_map/ppermute | solution.py:51
  3.8 8.4 %collective-permute-start.1 = (bf16[5,64,512]{2,1,0:T(8,128)(2,1)S(1)}, bf16[5,64,512]{2,1,0:T(8,128)(2,1)S(1)}, u32[]{:S(2)}, u32[]{:S(2)}) collective-permute-start(bf16[5,64,512]{2,1,0:T(8,128)(2,1)S(1)} %pad_maximum_fusion), channel_id=1, source_target_pairs={{0,5},{1,6},{2,7},{5,0},{6,1},{7,2},{8,13},{9,14},{10,15},{13,8},{... | collective-permute-start | bytes 983048 | tf_op jit(solution)/shard_map/ppermute | solution.py:95
  12.2 1.7 %collective-permute-start.2 = (bf16[5,64,512]{2,1,0:T(8,128)(2,1)S(1)}, bf16[5,64,512]{2,1,0:T(8,128)(2,1)S(1)}, u32[]{:S(2)}, u32[]{:S(2)}) collective-permute-start(bf16[5,64,512]{2,1,0:T(8,128)(2,1)S(1)} %collective-permute-done.1.mine_ref), channel_id=1, source_target_pairs={{0,4},{4,0},{1,5},{5,1},{2,6},{6,2},{3,7},{7,3},{8,12},{12,8},{9,1... | collective-permute-start | bytes 983048 | tf_op jit(solution)/shard_map/ppermute | solution.py:51
  12.6 7.4 %collective-permute-start.5 = (bf16[512,256]{1,0:T(8,128)(2,1)S(1)}, bf16[512,256]{1,0:T(8,128)(2,1)S(1)}, u32[]{:S(2)}, u32[]{:S(2)}) collective-permute-start(bf16[512,256]{1,0:T(8,128)(2,1)S(1)} %get-tuple-element.43.end_ref), channel_id=1, source_target_pairs={{0,8},{8,0},{16,24},{4,20},{12,28},{1,9},{9,1},{17,25},{5,21},{13,... | collective-permute-start | bytes 786440 | tf_op jit(solution)/shard_map/ppermute | solution.py:284
  14.1 13.7 %copy-start.5 = (f32[512]{0:T(512)S(1)}, f32[512]{0:T(512)}, u32[]{:S(2)}) copy-start(f32[512]{0:T(512)} %param.10) | copy-start | bytes 6148
  15.1 8.8 %collective-permute-start.3 = (bf16[704,256]{1,0:T(8,128)(2,1)S(1)}, bf16[704,256]{1,0:T(8,128)(2,1)S(1)}, u32[]{:S(2)}, u32[]{:S(2)}) collective-permute-start(bf16[704,256]{1,0:T(8,128)(2,1)S(1)} %get-tuple-element.42.end_ref), channel_id=1, source_target_pairs={{0,8},{8,0},{16,24},{4,20},{12,28},{1,9},{9,1},{17,25},{5,21},{13,... | collective-permute-start | bytes 1081352 | tf_op jit(solution)/shard_map/ppermute | solution.py:284
  20.0 10.6 %slice-start = ((s8[4718592]{0:T(1024)(128)(4,1)}), s8[4194304]{0:T(1024)(128)(4,1)S(1)}, s32[]{:S(2)}) async-start(s8[4718592]{0:T(1024)(128)(4,1)} %bitcast.3), calls=%async_computation | async-start | bytes 8388608
  20.2 7.7 %collective-permute-start.6 = (bf16[512,256]{1,0:T(8,128)(2,1)S(1)}, bf16[512,256]{1,0:T(8,128)(2,1)S(1)}, u32[]{:S(2)}, u32[]{:S(2)}) collective-permute-start(bf16[512,256]{1,0:T(8,128)(2,1)S(1)} %shard_map.71), channel_id=1, source_target_pairs={{0,16},{8,24},{4,12},{20,28},{28,20},{1,17},{9,25},{5,13},{21,29},... | collective-permute-start | bytes 786440 | tf_op jit(solution)/shard_map/ppermute | solution.py:287
  24.1 9.4 %collective-permute-start.4 = (bf16[704,256]{1,0:T(8,128)(2,1)S(1)}, bf16[704,256]{1,0:T(8,128)(2,1)S(1)}, u32[]{:S(2)}, u32[]{:S(2)}) collective-permute-start(bf16[704,256]{1,0:T(8,128)(2,1)S(1)} %shard_map.70), channel_id=1, source_target_pairs={{0,16},{8,24},{4,12},{20,28},{28,20},{1,17},{9,25},{5,13},{21,29},... | collective-permute-start | bytes 1081352 | tf_op jit(solution)/shard_map/ppermute | solution.py:287
  27.8 2.8 %slice-start.1 = ((s8[4718592]{0:T(1024)(128)(4,1)}), s8[524288]{0:T(1024)(128)(4,1)S(1)}, s32[]{:S(2)}) async-start(s8[4718592]{0:T(1024)(128)(4,1)} %bitcast.3), calls=%async_computation.1 | async-start | bytes 1048576
  27.9 2.7 %collective-permute-start.7 = (bf16[2,16,256]{2,1,0:T(8,128)(2,1)S(1)}, bf16[2,16,256]{2,1,0:T(8,128)(2,1)S(1)}, u32[]{:S(2)}, u32[]{:S(2)}) collective-permute-start(bf16[2,16,256]{2,1,0:T(8,128)(2,1)S(1)} %shard_map.73), channel_id=1, source_target_pairs={{0,4},{4,0},{1,5},{5,1},{2,6},{6,2},{3,7},{7,3},{8,12},{12,8},{9,1... | collective-permute-start | bytes 49160 | tf_op jit(solution)/shard_map/ppermute | solution.py:51
  33.8 1.7 %collective-permute-start.8 = (bf16[2,32,256]{2,1,0:T(8,128)(2,1)S(1)}, bf16[2,32,256]{2,1,0:T(8,128)(2,1)S(1)}, u32[]{:S(2)}, u32[]{:S(2)}) collective-permute-start(bf16[2,32,256]{2,1,0:T(8,128)(2,1)S(1)} %get-tuple-element.51), channel_id=1, source_target_pairs={{0,4},{4,0},{1,5},{5,1},{2,6},{6,2},{3,7},{7,3},{8,12},{12,8},{9,1... | collective-permute-start | bytes 98312 | tf_op jit(solution)/shard_map/ppermute | solution.py:51

commit v12 on v11

--- a/solution.py
+++ b/solution.py
@@ -144,7 +144,13 @@
     return jnp.dot(lhs, weight, preferred_element_type=jnp.float32)
 
 
-def main_kernel(_, got_ref, weight_ref, pole_ref, total_ref, spill_ref, end_ref, lhs_ref):
+def first_rows(rows):
+    return rows // 4
+
+
+def main_kernel(
+    _, got_ref, weight_ref, pole_ref, total_ref, spill_ref, early_ref, late_ref, lhs_ref
+):
     count, rows, cols, _ = total_ref.shape
     size = rows * cols
     for frame in range(count):
@@ -160,9 +166,14 @@
         spill_ref[0, :, lanes] = last[:, :, 0, :].reshape(count * rows, -1)
         total += jnp.where(col == cols - 1, 0.0, pltpu.roll(last, cols - 1, 2))
         total_ref[:, :, :, lanes] = total
+        state = end_state([total[frame] for frame in range(count)], pole_ref, lanes)
+        state = state.reshape(size, -1).astype(early_ref.dtype)
         if lanes.start == 0:
-            state = end_state([total[frame] for frame in range(count)], pole_ref, lanes)
-            end_ref[...] = state.reshape(end_ref.shape).astype(end_ref.dtype)
+            early_ref[:size] = state
+        else:
+            cut = first_rows(rows) * cols
+            early_ref[size:] = state[:cut]
+            late_ref[: size - cut] = state[cut:]
 
 
 def halo_kernel(mine_ref, theirs_ref, lhs_ref, start_ref):
@@ -188,37 +199,29 @@
     start_ref[rows:] = zero * own + one * other
 
 
-def drive_kernel(
-    lhs_ref, weight_ref, total_ref, spill_ref, pole_ref, drive_ref, beside_ref, strips_ref, end_ref
+def strips_kernel(
+    lhs_ref, weight_ref, total_ref, spill_ref, pole_ref, _, strips_ref, late_ref
 ):
-    count, rows, cols, wide = drive_ref.shape
-    room, size = count * rows, rows * cols
-    at = size + 2 * rows
-    for lanes in halves(weight_ref.shape[-1]):
+    count, rows, cols, channels = total_ref.shape
+    room = count * rows
+    at = late_ref.shape[0] - 8 * rows
+    for lanes in halves(channels):
+        wide = lanes.stop - lanes.start
         first = dot(lhs_ref[: 2 * room], weight_ref, 0, lanes)
         middle = dot(lhs_ref[room : 3 * room], weight_ref, 1, lanes)
         last = dot(lhs_ref[2 * room :], weight_ref, 2, lanes)
-        left = (spill_ref[0, :, lanes] + first[:room] + middle[:room]).reshape(count, rows, wide)
-        right = (spill_ref[1, :, lanes] + middle[room:] + last[room:]).reshape(count, rows, wide)
         total = total_ref[:, :, :, lanes]
-        if lanes.start == 0:
-            near = total[:, :, 0, :] + first[room:].reshape(count, rows, wide)
-            far = total[:, :, cols - 1, :] + last[:room].reshape(count, rows, wide)
-            strips = jnp.concatenate([left, near, far, right], axis=1)
-            strips_ref[...] = strips
-            state = end_state([strips[frame] for frame in range(count)], pole_ref, lanes)
-            end_ref[at:] = state.astype(end_ref.dtype)
-            continue
-        col = lax.broadcasted_iota(jnp.int32, drive_ref.shape, 2)
-        total += jnp.where(col == 0, first[room:].reshape(count, rows, 1, wide), 0.0)
-        total += jnp.where(col == cols - 1, last[:room].reshape(count, rows, 1, wide), 0.0)
-        drive_ref[...] = total
-        state = end_state([total[frame] for frame in range(count)], pole_ref, lanes)
-        end_ref[:size] = state.reshape(size, wide).astype(end_ref.dtype)
-        beside = jnp.concatenate([left, right], axis=1)
-        beside_ref[...] = beside
-        state = end_state([beside[frame] for frame in range(count)], pole_ref, lanes)
-        end_ref[size:at] = state.astype(end_ref.dtype)
+        strips = [
+            (spill_ref[0, :, lanes] + first[:room] + middle[:room]).reshape(count, rows, wide),
+            total[:, :, 0, :] + first[room:].reshape(count, rows, wide),
+            total[:, :, cols - 1, :] + last[:room].reshape(count, rows, wide),
+            (spill_ref[1, :, lanes] + middle[room:] + last[room:]).reshape(count, rows, wide),
+        ]
+        strips = jnp.concatenate(strips, axis=1)
+        strips_ref[:, :, lanes] = strips
+        state = end_state([strips[frame] for frame in range(count)], pole_ref, lanes)
+        late_ref[at : at + 4 * rows] = state.astype(late_ref.dtype)
+        at += 4 * rows
 
 
 def entry_kernel(frames, ends_ref, pole_ref, out_ref):
@@ -289,14 +292,13 @@
 
 
 class Mix:
-    def __init__(self, lanes, count, arrived_refs, pole_ref, scale_ref):
+    def __init__(self, lanes, count, pole_ref, scale_ref):
         self.rate = rate_of(pole_ref)[:, lanes]
         self.scale = scale_ref[:, lanes]
         self.count = count
-        self.arrived_refs = arrived_refs
-
-    def entry(self, rows):
-        parts = [ref[rows] for ref in self.arrived_refs]
+
+    def entry(self, arrived_refs, rows):
+        parts = [ref[rows] for ref in arrived_refs]
         if len(parts) == 1:
             return parts[0].astype(jnp.float32)
         carried = jnp.exp(self.count * self.rate)
@@ -305,47 +307,40 @@
         late = on_core(pick([none, none, same, carried]), pick([none, same, same, same]))
         return weigh(parts[0], early, parts[1], late)
 
-    def __call__(self, drives, rows, start):
+    def __call__(self, drives, entry, start):
         decay = jnp.exp(self.rate)
         reach = jnp.exp((self.count * lax.axis_index("tm")).astype(jnp.float32) * self.rate)
-        state = reach * start + self.entry(rows).reshape(start.shape)
+        state = reach * start + entry.reshape(start.shape)
         for drive in drives:
             state = decay * state + drive
             yield jax.nn.gelu(self.scale * state)
 
 
-def middle_kernel(lanes, *refs):
-    total_ref, start_ref, pole_ref, scale_ref, *arrived_refs, give_ref = refs
+def no_border(cells, axis):
+    col = lax.broadcasted_iota(jnp.int32, cells.shape, axis)
+    return jnp.where((col == 0) | (col == cells.shape[axis] - 1), 0.0, cells)
+
+
+def mixed_kernel(lanes, rounds, *refs):
+    total_ref, start_ref, pole_ref, scale_ref, *arrived_refs, lhs_ref = refs
     count, rows, cols, _ = total_ref.shape
-    mix = Mix(lanes, count, arrived_refs, pole_ref, scale_ref)
-    inner = inner_row(rows)
-    drives = [total_ref[frame, inner, :, lanes] for frame in range(count)]
-    here = pl.ds(pl.multiple_of(inner * cols, cols), cols)
-    col = lax.broadcasted_iota(jnp.int32, give_ref.shape[1:], 0)
-    for frame, cells in enumerate(mix(drives, here, start_ref[inner, :, lanes])):
-        cells = jnp.where((col == 0) | (col == cols - 1), 0.0, cells)
-        give_ref[frame] = cells.astype(give_ref.dtype)
-
-
-def mixed_kernel(lanes, inner_only, *refs):
-    drive_ref, start_ref, pole_ref, scale_ref, *arrived_refs, lhs_ref = refs
-    count, rows, cols, _ = drive_ref.shape
-    wide = lanes.stop - lanes.start
     size = rows * cols
-    room = (lhs_ref.shape[0] - count * size) // 2
-    mix = Mix(lanes, count, arrived_refs, pole_ref, scale_ref)
-    held = lanes if inner_only else slice(None)
-    block = 8
-    col = lax.broadcasted_iota(jnp.int32, (block, cols, wide), 1)
+    early_refs, late_refs = arrived_refs[:rounds], arrived_refs[rounds:]
+    mix = Mix(lanes, count, pole_ref, scale_ref)
+    block = first_rows(rows)
     for row in range(0, rows, block):
         here = slice(row, row + block)
-        drives = [drive_ref[frame, here, :, held] for frame in range(count)]
-        cells = slice(row * cols, (row + block) * cols)
-        for frame, tile in enumerate(mix(drives, cells, start_ref[here, :, lanes])):
-            if inner_only:
-                tile = jnp.where((col == 0) | (col == cols - 1), 0.0, tile)
-            tile = tile.reshape(block * cols, wide).astype(lhs_ref.dtype)
-            put_cells(lhs_ref, room + frame * size, size, cols, row * cols, tile)
+        if lanes.start == 0:
+            source, at = early_refs, row * cols
+        elif row < block:
+            source, at = early_refs, size
+        else:
+            source, at = late_refs, (row - block) * cols
+        entry = mix.entry(source, slice(at, at + block * cols))
+        drives = [total_ref[frame, here, :, lanes] for frame in range(count)]
+        for frame, tile in enumerate(mix(drives, entry, start_ref[here, :, lanes])):
+            tile = no_border(tile, 1).reshape(block * cols, -1).astype(lhs_ref.dtype)
+            put_cells(lhs_ref, frame * size, size, cols, row * cols, tile)
 
 
 def strip_start_kernel(start_ref, sides_ref, out_ref):
@@ -357,48 +352,45 @@
     out_ref[3 * rows :] = sides_ref[rows:]
 
 
-def late_kernel(parts, *refs):
-    drive_ref, beside_ref, strips_ref, start_ref, strip_start_ref, pole_ref, scale_ref, *refs = refs
-    *arrived_refs, give_ref, beside_out_ref, strips_out_ref = refs
-    count, rows, cols, wide = drive_ref.shape
+def late_kernel(rounds, *refs):
+    total_ref, strips_ref, start_ref, strip_start_ref, pole_ref, scale_ref, *refs = refs
+    *arrived_refs, give_ref, out_ref = refs
+    early_refs, late_refs = arrived_refs[:rounds], arrived_refs[rounds:]
+    count, rows, cols, channels = total_ref.shape
     size = rows * cols
     inner = inner_row(rows)
     zero, one = is_core(0), is_core(1)
     chip, chips = lax.axis_index("sy"), lax.axis_size("sy")
-    inside = [(chip > 0).astype(jnp.float32), (chip < chips - 1).astype(jnp.float32)]
-    early, late = (Mix(lanes, count, arrived_refs, pole_ref, scale_ref) for lanes in parts)
-
-    def columns_of(cells, count):
-        return [cells[index * rows : (index + 1) * rows] for index in range(count)]
-
-    starts = columns_of(strip_start_ref, 4)
-    starts = jnp.concatenate([starts[0][:, parts[1]], starts[3][:, parts[1]]], axis=0)
-    at = size + 2 * rows
-    beside = late([beside_ref[frame] for frame in range(count)], slice(size, at), starts)
-    strips = early(
-        [strips_ref[frame] for frame in range(count)],
-        slice(at, at + 4 * rows),
-        strip_start_ref[:, parts[0]],
-    )
-    here = pl.ds(pl.multiple_of(inner * cols, cols), cols)
-    drives = [drive_ref[frame, inner] for frame in range(count)]
-    tile = late(drives, here, start_ref[inner, :, parts[1]])
-    which = lax.broadcasted_iota(jnp.int32, (cols, wide), 0)
-    for frame, (cells, sides, strip) in enumerate(zip(tile, beside, strips)):
-        sides, strip = columns_of(sides, 2), columns_of(strip, 4)
-        sides = [sides[0] * inside[0], sides[1] * inside[1]]
-        strip = [strip[0] * inside[0], strip[1], strip[2], strip[3] * inside[1]]
-        give_ref[frame, :cols] = cells.astype(give_ref.dtype)
-        ends = jnp.zeros(which.shape, jnp.float32)
-        for index, column in enumerate((*sides, *strip)):
-            end = zero * column[rows - 1 :] + one * column[:1]
-            ends = jnp.where(which == index, end, ends)
-        give_ref[frame, cols:] = ends.astype(give_ref.dtype)
-        beside_out_ref[frame] = jnp.concatenate(sides, axis=0).astype(give_ref.dtype)
-        strips_out_ref[frame] = jnp.concatenate(strip, axis=0).astype(give_ref.dtype)
-
-
-def put_columns_taps(lhs_ref, slots, frame, count, columns, ends):
+    inside = [(chip > 0).astype(jnp.float32), 1.0, 1.0, (chip < chips - 1).astype(jnp.float32)]
+    cut = size - first_rows(rows) * cols
+    for index, lanes in enumerate(halves(channels)):
+        mix = Mix(lanes, count, pole_ref, scale_ref)
+        here = slice(cut + 4 * rows * index, cut + 4 * rows * (index + 1))
+        drives = [strips_ref[frame, :, lanes] for frame in range(count)]
+        strips = mix(drives, mix.entry(late_refs, here), strip_start_ref[:, lanes])
+        if index == 0:
+            here = pl.ds(pl.multiple_of(inner * cols, cols), cols)
+            entry = mix.entry(early_refs, here)
+        else:
+            entry = zero * mix.entry(late_refs, slice(cut - cols, cut))
+            entry += one * mix.entry(early_refs, slice(size, size + cols))
+        drives = [total_ref[frame, inner, :, lanes] for frame in range(count)]
+        tile = mix(drives, entry, start_ref[inner, :, lanes])
+        for frame, (cells, strip) in enumerate(zip(tile, strips)):
+            give_ref[frame, :cols, lanes] = no_border(cells, 0).astype(give_ref.dtype)
+            which = lax.broadcasted_iota(jnp.int32, cells.shape, 0)
+            ends = jnp.zeros(cells.shape, jnp.float32)
+            columns = []
+            for slot, factor in enumerate(inside):
+                column = factor * strip[slot * rows : (slot + 1) * rows]
+                end = zero * column[rows - 1 :] + one * column[:1]
+                ends = jnp.where(which == slot, end, ends)
+                columns.append(column)
+            give_ref[frame, cols:, lanes] = ends.astype(give_ref.dtype)
+            out_ref[frame, :, lanes] = jnp.concatenate(columns, axis=0).astype(out_ref.dtype)
+
+
+def put_columns_taps(lhs_ref, slots, frame, columns, ends):
     rows = columns.shape[0] // len(slots)
     columns, ends = columns.astype(jnp.float32), ends.astype(jnp.float32)
     for index, slot in enumerate(slots):
@@ -407,32 +399,23 @@
         lhs_ref[at : at + rows] = row_taps(column, end, end).astype(lhs_ref.dtype)
 
 
-def tile_sum(tile, inputs, lanes, room, lhs_ref, weight_ref):
-    count, rows, cols, wide = tile
-    inner = count * rows * cols
+def tile_sum(tile, inputs, lanes, lhs_ref, weight_ref):
+    cols = tile[2]
     col = lax.broadcasted_iota(jnp.int32, tile, 2)
-
-    def beside(cells):
-        return cells.reshape(count, rows, 1, wide) if room else 0.0
-
-    total = dot(lhs_ref[room : room + inner], weight_ref, 1, lanes, inputs).reshape(tile)
-    first = dot(lhs_ref[: room + inner], weight_ref, 0, lanes, inputs)
-    halo = beside(first[:room])
-    total += jnp.where(col == 0, halo, pltpu.roll(first[room:].reshape(tile), 1, 2))
-    last = dot(lhs_ref[room:], weight_ref, 2, lanes, inputs)
-    halo = beside(last[inner:])
-    return total + jnp.where(
-        col == cols - 1, halo, pltpu.roll(last[:inner].reshape(tile), cols - 1, 2)
-    )
-
-
-def strip_sum(tile, inputs, lanes, lhs_ref, weight_ref):
+    total = dot(lhs_ref[...], weight_ref, 1, lanes, inputs).reshape(tile)
+    first = dot(lhs_ref[...], weight_ref, 0, lanes, inputs).reshape(tile)
+    total += jnp.where(col == 0, 0.0, pltpu.roll(first, 1, 2))
+    last = dot(lhs_ref[...], weight_ref, 2, lanes, inputs).reshape(tile)
+    return total + jnp.where(col == cols - 1, 0.0, pltpu.roll(last, cols - 1, 2))
+
+
+def strip_sum(tile, lanes, lhs_ref, weight_ref):
     count, rows, cols, wide = tile
     room = count * rows
     col = lax.broadcasted_iota(jnp.int32, tile, 2)
-    first = dot(lhs_ref[: 2 * room], weight_ref, 0, lanes, inputs)
-    middle = dot(lhs_ref[room : 3 * room], weight_ref, 1, lanes, inputs)
-    last = dot(lhs_ref[2 * room :], weight_ref, 2, lanes, inputs)
+    first = dot(lhs_ref[: 2 * room], weight_ref, 0, lanes)
+    middle = dot(lhs_ref[room : 3 * room], weight_ref, 1, lanes)
+    last = dot(lhs_ref[2 * room :], weight_ref, 2, lanes)
     total = 0.0
     for at, cells in (
         (0, first[:room] + middle[:room]),
@@ -444,34 +427,36 @@
     return total
 
 
-def opening_kernel(inputs, lanes, _, got_ref, weight_ref, out_ref, lhs_ref):
-    count, rows, cols, _ = out_ref.shape
-    size = rows * cols
-    for frame in range(count):
-        put_row(lhs_ref, frame * size, size, got_ref[frame])
-    out_ref[...] = tile_sum(out_ref.shape, inputs, lanes, 0, lhs_ref, weight_ref)
-
-
-def further_kernel(inputs, lanes, lhs_ref, weight_ref, out_ref):
-    out_ref[...] = tile_sum(out_ref.shape, inputs, lanes, 0, lhs_ref, weight_ref)
-
-
-def result_kernel(
-    parts, _, got_ref, beside_ref, strips_ref, weight_ref, *refs
-):
+def row_sum(tile, inputs, lanes, got_ref, weight_ref):
+    count, rows, cols, wide = tile
+    given = jnp.concatenate([got_ref[frame, :cols, inputs] for frame in range(count)], axis=0)
+    tap = jnp.where(lax.axis_index("sx") == 0, weight_ref.shape[0] - 1, 0)
+    col = lax.broadcasted_iota(jnp.int32, (count, cols, wide), 1)
+
+    def product(column):
+        weight = weight_ref[pl.ds(tap, 1), column, inputs, lanes].reshape(given.shape[1], wide)
+        total = jnp.dot(given, weight, preferred_element_type=jnp.float32)
+        return total.reshape(count, cols, wide)
+
+    total = product(1)
+    total += jnp.where(col == 0, 0.0, pltpu.roll(product(0), 1, 1))
+    total += jnp.where(col == cols - 1, 0.0, pltpu.roll(product(2), cols - 1, 1))
+    row = lax.broadcasted_iota(jnp.int32, tile, 1)
+    return jnp.where(row == inner_row(rows), total.reshape(count, 1, cols, wide), 0.0)
+
+
+def opening_kernel(inputs, lanes, lhs_ref, weight_ref, out_ref):
+    out_ref[...] = tile_sum(out_ref.shape, inputs, lanes, lhs_ref, weight_ref)
+
+
+def result_kernel(parts, _, got_ref, strips_ref, weight_ref, *refs):
     *before_refs, out_ref, lhs_ref, held_ref, strip_lhs_ref, sems = refs
     count, rows, cols, _ = held_ref.shape
     size, room = rows * cols, count * rows
+    slots = [slot * room for slot in range(4)]
     for frame in range(count):
-        put_row(lhs_ref, room + frame * size, size, got_ref[frame, :cols])
-        ends = got_ref[frame, cols:]
-        put_columns_taps(
-            lhs_ref, (0, room + count * size), frame, count, beside_ref[frame], ends
-        )
-        slots = [slot * room for slot in range(4)]
-        put_columns_taps(
-            strip_lhs_ref, slots, frame, count, strips_ref[frame], ends.astype(jnp.float32)[2:]
-        )
+        put_row(lhs_ref, frame * size, size, got_ref[frame, :cols, parts[1]])
+        put_columns_taps(strip_lhs_ref, slots, frame, strips_ref[frame], got_ref[frame, cols:])
 
     def store(frame, part):
         here = (frame, slice(None), slice(None), parts[part])
@@ -480,8 +465,9 @@
     for part, lanes in enumerate(parts):
         tile = (count, rows, cols, lanes.stop - lanes.start)
         total = before_refs[part][...]
-        total += strip_sum(tile, parts[0], lanes, strip_lhs_ref, weight_ref)
-        total += tile_sum(tile, parts[1], lanes, room, lhs_ref, weight_ref)
+        total += row_sum(tile, parts[0], lanes, got_ref, weight_ref)
+        total += strip_sum(tile, lanes, strip_lhs_ref, weight_ref)
+        total += tile_sum(tile, parts[1], lanes, lhs_ref, weight_ref)
         for frame in range(count):
             held_ref[frame, :, :, lanes] = total[frame].astype(held_ref.dtype)
             store(frame, part).start()
@@ -521,106 +507,100 @@
     parts = halves(channels)
     half = channels // 2
     inner = of((count, rows, cols, half), jnp.float32)
-    *main, early, _ = call(
+    cut = first_rows(rows) * cols
+    *main, early, late, _ = call(
         main_kernel,
         (
             of(frames.shape, jnp.float32),
             of((2, room, channels), jnp.float32),
-            of((size, half), narrow),
+            of((size + cut, half), narrow),
+            of((size - cut + 8 * rows, half), narrow),
             taps,
         ),
         call(taps_kernel, taps, frames),
         got,
         input_weight,
         pole,
-        aliases={0: 3},
+        aliases={0: 4},
         flops=18 * frames.size * channels,
     )
-    mine, total, spill = lax.optimization_barrier((mine, *main))
+    mine, total, spill, late = lax.optimization_barrier((mine, *main, late))
     halo, sides = call(
         halo_kernel,
         (of((4 * room, wide), narrow), of((2 * rows, channels), jnp.float32)),
         mine,
         swap_cores(mine),
     )
-    drive, beside, strips, late = call(
-        drive_kernel,
-        (
-            inner,
-            of((count, 2 * rows, half), jnp.float32),
-            of((count, 4 * rows, half), jnp.float32),
-            of((size + 6 * rows, half), narrow),
-        ),
+    strips, late = call(
+        strips_kernel,
+        (of((count, 4 * rows, channels), jnp.float32), of(late.shape, narrow)),
         halo,
         input_weight,
         total,
         spill,
         pole,
+        late,
+        aliases={5: 1},
         flops=36 * room * channels * channels,
     )
-    at = size + 2 * rows
+    at = size - cut
     pieces = [
-        (early, [(slice(0, size), parts[0])]),
-        (late, [(slice(0, at), parts[1]), (slice(at, at + 4 * rows), parts[0])]),
+        (early, [(slice(0, size), parts[0]), (slice(size, size + cut), parts[1])]),
+        (
+            late,
+            [
+                (slice(0, at), parts[1]),
+                (slice(at, at + 4 * rows), parts[0]),
+                (slice(at + 4 * rows, at + 8 * rows), parts[1]),
+            ],
+        ),
     ]
-    exchanged = (exchange_four if lax.axis_size("tm") == 4 else exchange)(pieces, pole, count)
-    early, late = exchanged
+    early, late = (exchange_four if lax.axis_size("tm") == 4 else exchange)(pieces, pole, count)
+    rounds = len(early)
 
     mixing = (start_state, pole, scale)
-    give = call(
-        functools.partial(middle_kernel, parts[0]),
-        of((count, cols, half), narrow),
-        total,
-        *mixing,
-        *early,
-    )
     taps = of((count * size, 3 * half), narrow)
     lhs = call(
-        functools.partial(mixed_kernel, parts[0], True), taps, total, *mixing, *early
+        functools.partial(mixed_kernel, parts[0], rounds), taps, total, *mixing, *early
     )
     strip_start = call(strip_start_kernel, of((4 * rows, channels), jnp.float32), start_state, sides)
     flops = 18 * inner.size * half
-    first_sum, lhs = call(
+    first_sum = call(
         functools.partial(opening_kernel, parts[0], parts[0]),
-        (inner, taps),
-        lhs,
-        swap_cores(give),
-        output_weight,
-        aliases={0: 1},
-        flops=flops,
-    )
-    second_sum = call(
-        functools.partial(further_kernel, parts[0], parts[1]),
         inner,
         lhs,
         output_weight,
         flops=flops,
     )
-    *late, first_sum, second_sum = lax.optimization_barrier((*late, first_sum, second_sum))
-    give, beside, strips = call(
-        functools.partial(late_kernel, parts),
-        (
-            of((count, 2 * cols, half), narrow),
-            of(beside.shape, narrow),
-            of(strips.shape, narrow),
-        ),
-        drive,
-        beside,
+    *late, first_sum = lax.optimization_barrier((*late, first_sum))
+    give, strips = call(
+        functools.partial(late_kernel, rounds),
+        (of((count, 2 * cols, channels), narrow), of(strips.shape, narrow)),
+        total,
         strips,
         start_state,
         strip_start,
         pole,
         scale,
+        *early,
         *late,
     )
-    taps = of((count * size + 2 * room, 3 * half), narrow)
-    lhs = call(functools.partial(mixed_kernel, parts[1], False), taps, drive, *mixing, *late)
+    give, lhs = lax.optimization_barrier((give, lhs))
+    second_sum = call(
+        functools.partial(opening_kernel, parts[0], parts[1]),
+        inner,
+        lhs,
+        output_weight,
+        flops=flops,
+    )
+    lhs = call(
+        functools.partial(mixed_kernel, parts[1], rounds), taps, total, *mixing, *early, *late
+    )
     result, _ = call(
         functools.partial(result_kernel, parts),
         (of(frames.shape, narrow), taps),
         lhs,
         swap_cores(give),
-        beside,
         strips,
         output_weight,
         first_sum,
@@ -629,7 +609,7 @@
         aliases={0: 1},
         scratch=[
             pltpu.VMEM(frames.shape, narrow),
-            pltpu.VMEM((4 * room, 3 * half), narrow),
+            pltpu.VMEM((4 * room, wide), narrow),
             pltpu.SemaphoreType.DMA((count, len(parts))),
         ],
         flops=2 * flops,

time: 40.7 us -> 41.9 us (1.029)
  waiting for transfers between devices: 8.97 us -> 11.3 us
  starting transfers between devices: 13.1 us -> 12.1 us
    ppermute x2, waiting for transfers between devices: 1.65 us -> 3.84 us  [exchange_four(): arrivals.append((got, lax.ppermute(relayed, axes, second_round)))]
    ppermute x4 -> x3, starting transfers between devices: 3.91 us -> 3.03 us  [swap_cores(): return lax.ppermute(array, 'sx', [(0, 1), (1, 0)])]
    ppermute x2, waiting for transfers between devices: 5.16 us -> 5.74 us  [exchange_four(): got = lax.ppermute(end, axes, first_round)]
    ppermute x4 -> x3, waiting for transfers between devices: 1.22 us -> 0.87 us  [swap_cores(): return lax.ppermute(array, 'sx', [(0, 1), (1, 0)])]
    pallas_call x16 -> x15, Pallas kernels: 16.2 us -> 16.4 us  [call(): pl.pallas_call(kernel, in_specs=[WHOLE] * len(args), out_specs=out_specs...]
  transfers between devices with their start and end apart: 9 -> 8, of which waited for: 7 -> 6; matrix products, arithmetic and copies ran while one was open for 0% -> 0% of each run, Pallas kernels for 27% -> 26%
where the time goes in v12:
time: 41.9 us; the launch traced here: 41.7 us
  Pallas kernels  16.4 us (39%)
  starting transfers between devices  12.1 us (29%)
  waiting for transfers between devices  11.3 us (27%)
  local copies, waits for them, and re-layouts  1.37 us (3%)
  between operations  0.42 us (1%)
    pallas_call x15, Pallas kernels, call(): pl.pallas_call(kernel, in_specs=[WHOLE] * len(args), out_specs=out_specs...  16.4 us
    ppermute x2, waiting for transfers between devices, exchange_four(): got = lax.ppermute(end, axes, first_round)  5.74 us
    ppermute x2, starting transfers between devices, exchange_four(): arrivals.append((got, lax.ppermute(relayed, axes, second_round)))  4.05 us
    ppermute x2, waiting for transfers between devices, exchange_four(): arrivals.append((got, lax.ppermute(relayed, axes, second_round)))  3.84 us
    ppermute x3, starting transfers between devices, swap_cores(): return lax.ppermute(array, 'sx', [(0, 1), (1, 0)])  3.03 us
    ppermute x2, starting transfers between devices, exchange_four(): got = lax.ppermute(end, axes, first_round)  2.7 us
    ppermute x1, starting transfers between devices, trade_columns(): return (got, lax.ppermute(columns, ('sx', 'sy'), pairs))  2.33 us
    unnamed x16, local copies, waits for them, and re-layouts  1.35 us
  transfers between devices with their start and end apart: 8, of which 6 were waited for; matrix products, arithmetic and copies ran while one was open for 0% of the time, Pallas kernels for 26%

profile of v12, /device:TPU:23, one launch (start us, length us, event | category | flops | bytes accessed | tf_op | source)
XLA Modules:
  0.0 41.7 jit_solution(11985282718455123994)
XLA Ops:
  0.0 0.0 copy-start
  0.0 0.0 copy-start.2
  0.0 1.3 %copy-done.2 = bf16[2,32,16,512]{3,2,1,0:T(8,128)(2,1)S(1)} copy-done((bf16[2,32,16,512]{3,2,1,0:T(8,128)(2,1)S(1)}, bf16[2,32,16,512]{3,2,1,0:T(8,128)(2,1)}, u32[]{:S(2)}) %copy-start.2) | copy-done | bytes 1048600
  1.3 0.0 copy-start.3
  1.3 0.3 shard_map.64
  1.7 0.0 copy-done
  1.7 0.0 copy-start.1
  1.7 0.0 copy-start.4
  1.7 0.3 shard_map.65
  2.0 0.7 %collective-permute-start = (bf16[192,512]{1,0:T(8,128)(2,1)S(1)}, bf16[192,512]{1,0:T(8,128)(2,1)S(1)}, u32[]{:S(2)}, u32[]{:S(2)}) collective-permute-start(bf16[192,512]{1,0:T(8,128)(2,1)S(1)} %get-tuple-element.32), channel_id=1, source_target_pairs={{0,4},{4,0},{1,5},{5,1},{2,6},{6,2},{3,7},{7,3},{8,12},{12,8},{9,1... | collective-permute-start | bytes 589832 | tf_op jit(solution)/shard_map/ppermute | solution.py:51
  2.7 0.0 copy-done.3
  2.7 0.2 shard_map.66._
  2.9 0.9 %collective-permute-done.got_ref = bf16[192,512]{1,0:T(8,128)(2,1)S(1)} collective-permute-done((bf16[192,512]{1,0:T(8,128)(2,1)S(1)}, bf16[192,512]{1,0:T(8,128)(2,1)S(1)}, u32[]{:S(2)}, u32[]{:S(2)}) %collective-permute-start) | collective-permute-done | bytes 196640 | tf_op jit(solution)/shard_map/ppermute | solution.py:51
  3.8 2.3 %collective-permute-start.1 = (bf16[5,64,512]{2,1,0:T(8,128)(2,1)S(1)}, bf16[5,64,512]{2,1,0:T(8,128)(2,1)S(1)}, u32[]{:S(2)}, u32[]{:S(2)}) collective-permute-start(bf16[5,64,512]{2,1,0:T(8,128)(2,1)S(1)} %pad_maximum_fusion), channel_id=1, source_target_pairs={{0,5},{1,6},{2,7},{5,0},{6,1},{7,2},{8,13},{9,14},{10,15},{13,8},{... | collective-permute-start | bytes 983048 | tf_op jit(solution)/shard_map/ppermute | solution.py:95
  6.2 0.0 copy-done.1
  6.2 0.0 copy-done.4
  6.2 5.1 %shard_map.67 = (f32[2,32,16,512]{3,2,1,0:T(8,128)S(1)}, f32[2,64,512]{2,1,0:T(8,128)S(1)}, bf16[640,256]{1,0:T(8,128)(2,1)S(1)}, bf16[640,256]{1,0:T(8,128)(2,1)S(1)}, bf16[1024,1536]{1,0:T(8,128)(2,1)S(1)}) custom-call(bf16[1024,1536]{1,0:T(8,128)(2,1)S(1)} %shard_map.66._, ...), custom_call_target="tpu_custom_call", output_to_operand_aliasing={{4}: (0, {})} | custom-call | flops 4831838208 | bytes 14223360 | tf_op jit(solution)/shard_map/pallas_call | solution.py:21
  11.3 0.9 %collective-permute-done.1.mine_ref = bf16[5,64,512]{2,1,0:T(8,128)(2,1)S(1)} collective-permute-done((bf16[5,64,512]{2,1,0:T(8,128)(2,1)S(1)}, bf16[5,64,512]{2,1,0:T(8,128)(2,1)S(1)}, u32[]{:S(2)}, u32[]{:S(2)}) %collective-permute-start.1) | collective-permute-done | bytes 327712 | tf_op jit(solution)/shard_map/ppermute | solution.py:95
  12.2 0.4 %collective-permute-start.4 = (bf16[5,64,512]{2,1,0:T(8,128)(2,1)S(1)}, bf16[5,64,512]{2,1,0:T(8,128)(2,1)S(1)}, u32[]{:S(2)}, u32[]{:S(2)}) collective-permute-start(bf16[5,64,512]{2,1,0:T(8,128)(2,1)S(1)} %collective-permute-done.1.mine_ref), channel_id=1, source_target_pairs={{0,4},{4,0},{1,5},{5,1},{2,6},{6,2},{3,7},{7,3},{8,12},{12,8},{9,1... | collective-permute-start | bytes 983048 | tf_op jit(solution)/shard_map/ppermute | solution.py:51
  12.7 1.3 %collective-permute-start.2 = (bf16[640,256]{1,0:T(8,128)(2,1)S(1)}, bf16[640,256]{1,0:T(8,128)(2,1)S(1)}, u32[]{:S(2)}, u32[]{:S(2)}) collective-permute-start(bf16[640,256]{1,0:T(8,128)(2,1)S(1)} %get-tuple-element.37.end_ref), channel_id=1, source_target_pairs={{0,8},{8,0},{16,24},{4,20},{12,28},{1,9},{9,1},{17,25},{5,21},{13,... | collective-permute-start | bytes 983048 | tf_op jit(solution)/shard_map/ppermute | solution.py:287
  14.0 0.0 collective-permute-done.4.theirs_ref
  14.0 0.2 shard_map.69
  14.2 0.0 slice-start
  14.2 0.8 %shard_map.70 = (f32[2,128,512]{2,1,0:T(8,128)S(1)}, bf16[640,256]{1,0:T(8,128)(2,1)S(1)}) custom-call(bf16[256,1536]{1,0:T(8,128)(2,1)S(1)} %get-tuple-element.39.lhs_ref, bf16[3,3,512,512]{3,2,1,0:T(8,128)(2,1)S(1)} %copy-done.1, f32[2,32,16,512]{3,2,1,0:T(8,128)S(1)} %get-tuple-element.36.total_ref.refs_0_, ...), custom_call_target="tpu_custom_call", output_to_operand_aliasing={{1}: (5, {})} | custom-call | flops 603979776 | bytes 9046016 | tf_op jit(solution)/shard_map/pallas_call | solution.py:21
  15.0 0.0 copy-start.5
  15.0 0.0 slice-start.1
  15.0 1.4 %collective-permute-start.5 = (bf16[640,256]{1,0:T(8,128)(2,1)S(1)}, bf16[640,256]{1,0:T(8,128)(2,1)S(1)}, u32[]{:S(2)}, u32[]{:S(2)}) collective-permute-start(bf16[640,256]{1,0:T(8,128)(2,1)S(1)} %get-tuple-element.42.end_ref), channel_id=1, source_target_pairs={{0,8},{8,0},{16,24},{4,20},{12,28},{1,9},{9,1},{17,25},{5,21},{13,... | collective-permute-start | bytes 983048 | tf_op jit(solution)/shard_map/ppermute | solution.py:287
  16.5 4.3 %collective-permute-done.2.got_ref.refs_4_.refs_6_ = bf16[640,256]{1,0:T(8,128)(2,1)S(1)} collective-permute-done((bf16[640,256]{1,0:T(8,128)(2,1)S(1)}, bf16[640,256]{1,0:T(8,128)(2,1)S(1)}, u32[]{:S(2)}, u32[]{:S(2)}) %collective-permute-start.2) | collective-permute-done | bytes 327712 | tf_op jit(solution)/shard_map/ppermute | solution.py:287
  20.8 0.2 shard_map.68
  20.9 1.9 %collective-permute-start.3 = (bf16[640,256]{1,0:T(8,128)(2,1)S(1)}, bf16[640,256]{1,0:T(8,128)(2,1)S(1)}, u32[]{:S(2)}, u32[]{:S(2)}) collective-permute-start(bf16[640,256]{1,0:T(8,128)(2,1)S(1)} %shard_map.68), channel_id=1, source_target_pairs={{0,16},{8,24},{4,12},{20,28},{28,20},{1,17},{9,25},{5,13},{21,29},... | collective-permute-start | bytes 983048 | tf_op jit(solution)/shard_map/ppermute | solution.py:290
  22.9 1.4 %collective-permute-done.5.got_ref.refs_6_.refs_8_ = bf16[640,256]{1,0:T(8,128)(2,1)S(1)} collective-permute-done((bf16[640,256]{1,0:T(8,128)(2,1)S(1)}, bf16[640,256]{1,0:T(8,128)(2,1)S(1)}, u32[]{:S(2)}, u32[]{:S(2)}) %collective-permute-start.5) | collective-permute-done | bytes 327712 | tf_op jit(solution)/shard_map/ppermute | solution.py:287
  24.3 0.2 shard_map.71
  24.4 2.1 %collective-permute-start.6 = (bf16[640,256]{1,0:T(8,128)(2,1)S(1)}, bf16[640,256]{1,0:T(8,128)(2,1)S(1)}, u32[]{:S(2)}, u32[]{:S(2)}) collective-permute-start(bf16[640,256]{1,0:T(8,128)(2,1)S(1)} %shard_map.71), channel_id=1, source_target_pairs={{0,16},{8,24},{4,12},{20,28},{28,20},{1,17},{9,25},{5,13},{21,29},... | collective-permute-start | bytes 983048 | tf_op jit(solution)/shard_map/ppermute | solution.py:290
  26.6 0.1 shard_map.75.refs_3_
  26.7 2.4 %collective-permute-done.3.refs_5_.refs_7_ = bf16[640,256]{1,0:T(8,128)(2,1)S(1)} collective-permute-done((bf16[640,256]{1,0:T(8,128)(2,1)S(1)}, bf16[640,256]{1,0:T(8,128)(2,1)S(1)}, u32[]{:S(2)}, u32[]{:S(2)}) %collective-permute-start.3) | collective-permute-done | bytes 327712 | tf_op jit(solution)/shard_map/ppermute | solution.py:290
  29.0 0.0 copy-done.5
  29.1 0.6 %shard_map.72.lhs_ref = bf16[1024,768]{1,0:T(8,128)(2,1)S(1)} custom-call(f32[2,32,16,512]{3,2,1,0:T(8,128)S(1)} %get-tuple-element.36.total_ref.refs_0_, f32[32,16,512]{2,1,0:T(8,128)S(1)} %copy-done, s32[1,512]{1,0:T(1,128)S(1)} %bitcast.9, f32[1,512]{1,0:T(1,128)S(1)} %bitcast.12, bf16[640,256]{1,0:T(8,128)(2,1)S(1)} %collective-permute-done.2.got_ref.refs_4_.refs_6_, ...), custom_call_target="tpu_custom_call" | custom-call | bytes 5378048 | tf_op jit(solution)/shard_map/pallas_call | solution.py:21
  29.7 0.0 slice-done
  29.7 0.0 slice-done.1
  29.7 1.4 %shard_map.73.refs_0_ = f32[2,32,16,256]{3,2,1,0:T(8,128)S(1)} custom-call(bf16[1024,768]{1,0:T(8,128)(2,1)S(1)} %shard_map.72.lhs_ref, bf16[3,3,512,512]{3,2,1,0:T(8,128)(2,1)S(1)} %bitcast.4), custom_call_target="tpu_custom_call" | custom-call | flops 1207959552 | bytes 7340032 | tf_op jit(solution)/shard_map/pallas_call | solution.py:21
  31.1 1.5 %collective-permute-done.6.refs_7_.refs_9_ = bf16[640,256]{1,0:T(8,128)(2,1)S(1)} collective-permute-done((bf16[640,256]{1,0:T(8,128)(2,1)S(1)}, bf16[640,256]{1,0:T(8,128)(2,1)S(1)}, u32[]{:S(2)}, u32[]{:S(2)}) %collective-permute-start.6) | collective-permute-done | bytes 327712 | tf_op jit(solution)/shard_map/ppermute | solution.py:290
  32.6 0.4 shard_map.76
  32.9 1.8 %collective-permute-start.7 = (bf16[2,32,512]{2,1,0:T(8,128)(2,1)S(1)}, bf16[2,32,512]{2,1,0:T(8,128)(2,1)S(1)}, u32[]{:S(2)}, u32[]{:S(2)}) collective-permute-start(bf16[2,32,512]{2,1,0:T(8,128)(2,1)S(1)} %get-tuple-element.48), channel_id=1, source_target_pairs={{0,4},{4,0},{1,5},{5,1},{2,6},{6,2},{3,7},{7,3},{8,12},{12,8},{9,1... | collective-permute-start | bytes 196616 | tf_op jit(solution)/shard_map/ppermute | solution.py:51
  34.8 0.6 %shard_map.74._ = bf16[1024,768]{1,0:T(8,128)(2,1)S(1)} custom-call(f32[2,32,16,512]{3,2,1,0:T(8,128)S(1)} %get-tuple-element.36.total_ref.refs_0_, f32[32,16,512]{2,1,0:T(8,128)S(1)} %copy-done, s32[1,512]{1,0:T(1,128)S(1)} %bitcast.11, f32[1,512]{1,0:T(1,128)S(1)} %bitcast.14, bf16[640,256]{1,0:T(8,128)(2,1)S(1)} %collective-permute-done.2.got_ref.refs_4_.refs_6_, ...), custom_call_target="tpu_custom_call" | custom-call | bytes 6033408 | tf_op jit(solution)/shard_map/pallas_call | solution.py:21
  35.4 1.4 %shard_map.77.refs_1_ = f32[2,32,16,256]{3,2,1,0:T(8,128)S(1)} custom-call(bf16[1024,768]{1,0:T(8,128)(2,1)S(1)} %shard_map.72.lhs_ref, bf16[3,3,512,512]{3,2,1,0:T(8,128)(2,1)S(1)} %bitcast.4), custom_call_target="tpu_custom_call" | custom-call | flops 1207959552 | bytes 7340032 | tf_op jit(solution)/shard_map/pallas_call | solution.py:21
  36.8 0.0 collective-permute-done.7.got_ref
  36.8 4.7 %shard_map.78 = (bf16[2,32,16,512]{3,2,1,0:T(8,128)(2,1)}, bf16[1024,768]{1,0:T(8,128)(2,1)S(1)}) custom-call(bf16[1024,768]{1,0:T(8,128)(2,1)S(1)} %shard_map.74._, bf16[2,32,512]{2,1,0:T(8,128)(2,1)S(1)} %collective-permute-done.7.got_ref, bf16[2,128,512]{2,1,0:T(8,128)(2,1)S(1)} %get-tuple-element.49.strips_ref, ...), custom_call_target="tpu_custom_call", output_to_operand_aliasing={{1}: (0, {})} | custom-call | flops 2415919104 | bytes 11337728 | tf_op jit(solution)/shard_map/pallas_call | solution.py:21
  (3 shorter events, 0.0 us)
Async XLA Ops:
  0.0 1.7 %copy-start = (f32[32,16,512]{2,1,0:T(8,128)S(1)}, f32[32,16,512]{2,1,0:T(8,128)}, u32[]{:S(2)}) copy-start(f32[32,16,512]{2,1,0:T(8,128)} %refs_2_.1) | copy-start | bytes 3145732
  0.0 1.3 %copy-start.2 = (bf16[2,32,16,512]{3,2,1,0:T(8,128)(2,1)S(1)}, bf16[2,32,16,512]{3,2,1,0:T(8,128)(2,1)}, u32[]{:S(2)}) copy-start(bf16[2,32,16,512]{3,2,1,0:T(8,128)(2,1)} %cells_ref.3) | copy-start | bytes 3145732
  1.3 1.4 %copy-start.3 = (bf16[2,32,16,512]{3,2,1,0:T(8,128)(2,1)S(1)}, bf16[2,32,16,512]{3,2,1,0:T(8,128)(2,1)}, u32[]{:S(2)}) copy-start(bf16[2,32,16,512]{3,2,1,0:T(8,128)(2,1)} %cells_ref.3) | copy-start | bytes 3145732
  1.7 4.5 %copy-start.1 = (bf16[3,3,512,512]{3,2,1,0:T(8,128)(2,1)S(1)}, bf16[3,3,512,512]{3,2,1,0:T(8,128)(2,1)}, u32[]{:S(2)}) copy-start(bf16[3,3,512,512]{3,2,1,0:T(8,128)(2,1)} %weight_ref.6) | copy-start | bytes 14155780
  1.7 4.5 %copy-start.4 = (s32[512]{0:T(512)S(1)}, s32[512]{0:T(512)}, u32[]{:S(2)}) copy-start(s32[512]{0:T(512)} %param.9) | copy-start | bytes 6148
  2.0 1.8 %collective-permute-start = (bf16[192,512]{1,0:T(8,128)(2,1)S(1)}, bf16[192,512]{1,0:T(8,128)(2,1)S(1)}, u32[]{:S(2)}, u32[]{:S(2)}) collective-permute-start(bf16[192,512]{1,0:T(8,128)(2,1)S(1)} %get-tuple-element.32), channel_id=1, source_target_pairs={{0,4},{4,0},{1,5},{5,1},{2,6},{6,2},{3,7},{7,3},{8,12},{12,8},{9,1... | collective-permute-start | bytes 589832 | tf_op jit(solution)/shard_map/ppermute | solution.py:51
  3.8 8.4 %collective-permute-start.1 = (bf16[5,64,512]{2,1,0:T(8,128)(2,1)S(1)}, bf16[5,64,512]{2,1,0:T(8,128)(2,1)S(1)}, u32[]{:S(2)}, u32[]{:S(2)}) collective-permute-start(bf16[5,64,512]{2,1,0:T(8,128)(2,1)S(1)} %pad_maximum_fusion), channel_id=1, source_target_pairs={{0,5},{1,6},{2,7},{5,0},{6,1},{7,2},{8,13},{9,14},{10,15},{13,8},{... | collective-permute-start | bytes 983048 | tf_op jit(solution)/shard_map/ppermute | solution.py:95
  12.2 1.7 %collective-permute-start.4 = (bf16[5,64,512]{2,1,0:T(8,128)(2,1)S(1)}, bf16[5,64,512]{2,1,0:T(8,128)(2,1)S(1)}, u32[]{:S(2)}, u32[]{:S(2)}) collective-permute-start(bf16[5,64,512]{2,1,0:T(8,128)(2,1)S(1)} %collective-permute-done.1.mine_ref), channel_id=1, source_target_pairs={{0,4},{4,0},{1,5},{5,1},{2,6},{6,2},{3,7},{7,3},{8,12},{12,8},{9,1... | collective-permute-start | bytes 983048 | tf_op jit(solution)/shard_map/ppermute | solution.py:51
  12.7 8.1 %collective-permute-start.2 = (bf16[640,256]{1,0:T(8,128)(2,1)S(1)}, bf16[640,256]{1,0:T(8,128)(2,1)S(1)}, u32[]{:S(2)}, u32[]{:S(2)}) collective-permute-start(bf16[640,256]{1,0:T(8,128)(2,1)S(1)} %get-tuple-element.37.end_ref), channel_id=1, source_target_pairs={{0,8},{8,0},{16,24},{4,20},{12,28},{1,9},{9,1},{17,25},{5,21},{13,... | collective-permute-start | bytes 983048 | tf_op jit(solution)/shard_map/ppermute | solution.py:287
  14.2 15.5 %slice-start = ((s8[4718592]{0:T(1024)(128)(4,1)}), s8[4194304]{0:T(1024)(128)(4,1)S(1)}, s32[]{:S(2)}) async-start(s8[4718592]{0:T(1024)(128)(4,1)} %bitcast.3), calls=%async_computation | async-start | bytes 8388608
  15.0 14.1 %copy-start.5 = (f32[512]{0:T(512)S(1)}, f32[512]{0:T(512)}, u32[]{:S(2)}) copy-start(f32[512]{0:T(512)} %param.10) | copy-start | bytes 6148
  15.0 14.7 %slice-start.1 = ((s8[4718592]{0:T(1024)(128)(4,1)}), s8[524288]{0:T(1024)(128)(4,1)S(1)}, s32[]{:S(2)}) async-start(s8[4718592]{0:T(1024)(128)(4,1)} %bitcast.3), calls=%async_computation.1 | async-start | bytes 1048576
  15.0 9.3 %collective-permute-start.5 = (bf16[640,256]{1,0:T(8,128)(2,1)S(1)}, bf16[640,256]{1,0:T(8,128)(2,1)S(1)}, u32[]{:S(2)}, u32[]{:S(2)}) collective-permute-start(bf16[640,256]{1,0:T(8,128)(2,1)S(1)} %get-tuple-element.42.end_ref), channel_id=1, source_target_pairs={{0,8},{8,0},{16,24},{4,20},{12,28},{1,9},{9,1},{17,25},{5,21},{13,... | collective-permute-start | bytes 983048 | tf_op jit(solution)/shard_map/ppermute | solution.py:287
  20.9 8.1 %collective-permute-start.3 = (bf16[640,256]{1,0:T(8,128)(2,1)S(1)}, bf16[640,256]{1,0:T(8,128)(2,1)S(1)}, u32[]{:S(2)}, u32[]{:S(2)}) collective-permute-start(bf16[640,256]{1,0:T(8,128)(2,1)S(1)} %shard_map.68), channel_id=1, source_target_pairs={{0,16},{8,24},{4,12},{20,28},{28,20},{1,17},{9,25},{5,13},{21,29},... | collective-permute-start | bytes 983048 | tf_op jit(solution)/shard_map/ppermute | solution.py:290
  24.4 8.1 %collective-permute-start.6 = (bf16[640,256]{1,0:T(8,128)(2,1)S(1)}, bf16[640,256]{1,0:T(8,128)(2,1)S(1)}, u32[]{:S(2)}, u32[]{:S(2)}) collective-permute-start(bf16[640,256]{1,0:T(8,128)(2,1)S(1)} %shard_map.71), channel_id=1, source_target_pairs={{0,16},{8,24},{4,12},{20,28},{28,20},{1,17},{9,25},{5,13},{21,29},... | collective-permute-start | bytes 983048 | tf_op jit(solution)/shard_map/ppermute | solution.py:290
  32.9 3.9 %collective-permute-start.7 = (bf16[2,32,512]{2,1,0:T(8,128)(2,1)S(1)}, bf16[2,32,512]{2,1,0:T(8,128)(2,1)S(1)}, u32[]{:S(2)}, u32[]{:S(2)}) collective-permute-start(bf16[2,32,512]{2,1,0:T(8,128)(2,1)S(1)} %get-tuple-element.48), channel_id=1, source_target_pairs={{0,4},{4,0},{1,5},{5,1},{2,6},{6,2},{3,7},{7,3},{8,12},{12,8},{9,1... | collective-permute-start | bytes 196616 | tf_op jit(solution)/shard_map/ppermute | solution.py:51

commit v13 on v11

--- a/solution.py
+++ b/solution.py
@@ -150,18 +150,23 @@
     for frame in range(count):
         put_row(lhs_ref, frame * size, size, got_ref[frame * cols : (frame + 1) * cols])
     for lanes in halves(weight_ref.shape[-1]):
-        tile = (count, rows, cols, lanes.stop - lanes.start)
-        col = lax.broadcasted_iota(jnp.int32, tile, 2)
-        total = dot(lhs_ref[...], weight_ref, 1, lanes).reshape(tile)
-        first = dot(lhs_ref[...], weight_ref, 0, lanes).reshape(tile)
-        spill_ref[1, :, lanes] = first[:, :, cols - 1, :].reshape(count * rows, -1)
-        total += jnp.where(col == 0, 0.0, pltpu.roll(first, 1, 2))
-        last = dot(lhs_ref[...], weight_ref, 2, lanes).reshape(tile)
-        spill_ref[0, :, lanes] = last[:, :, 0, :].reshape(count * rows, -1)
-        total += jnp.where(col == cols - 1, 0.0, pltpu.roll(last, cols - 1, 2))
-        total_ref[:, :, :, lanes] = total
+        tile = (rows, cols, lanes.stop - lanes.start)
+        col = lax.broadcasted_iota(jnp.int32, tile, 1)
+        totals = []
+        for frame in range(count):
+            cells = lhs_ref[frame * size : (frame + 1) * size]
+            here = slice(frame * rows, (frame + 1) * rows)
+            total = dot(cells, weight_ref, 1, lanes).reshape(tile)
+            first = dot(cells, weight_ref, 0, lanes).reshape(tile)
+            spill_ref[1, here, lanes] = first[:, cols - 1, :]
+            total += jnp.where(col == 0, 0.0, pltpu.roll(first, 1, 1))
+            last = dot(cells, weight_ref, 2, lanes).reshape(tile)
+            spill_ref[0, here, lanes] = last[:, 0, :]
+            total += jnp.where(col == cols - 1, 0.0, pltpu.roll(last, cols - 1, 1))
+            total_ref[frame, :, :, lanes] = total
+            totals.append(total)
         if lanes.start == 0:
-            state = end_state([total[frame] for frame in range(count)], pole_ref, lanes)
+            state = end_state(totals, pole_ref, lanes)
             end_ref[...] = state.reshape(end_ref.shape).astype(end_ref.dtype)
 
 
@@ -332,7 +337,8 @@
     count, rows, cols, _ = drive_ref.shape
     wide = lanes.stop - lanes.start
     size = rows * cols
-    room = (lhs_ref.shape[0] - count * size) // 2
+    stride = lhs_ref.shape[0] // count
+    room = (stride - size) // 2
     mix = Mix(lanes, count, arrived_refs, pole_ref, scale_ref)
     held = lanes if inner_only else slice(None)
     block = 8
@@ -345,7 +351,7 @@
             if inner_only:
                 tile = jnp.where((col == 0) | (col == cols - 1), 0.0, tile)
             tile = tile.reshape(block * cols, wide).astype(lhs_ref.dtype)
-            put_cells(lhs_ref, room + frame * size, size, cols, row * cols, tile)
+            put_cells(lhs_ref, frame * stride + room, size, cols, row * cols, tile)
 
 
 def strip_start_kernel(start_ref, sides_ref, out_ref):
@@ -398,32 +404,32 @@
         strips_out_ref[frame] = jnp.concatenate(strip, axis=0).astype(give_ref.dtype)
 
 
-def put_columns_taps(lhs_ref, slots, frame, count, columns, ends):
+def put_columns_taps(lhs_ref, slots, columns, ends):
     rows = columns.shape[0] // len(slots)
     columns, ends = columns.astype(jnp.float32), ends.astype(jnp.float32)
-    for index, slot in enumerate(slots):
+    for index, at in enumerate(slots):
         column, end = columns[index * rows : (index + 1) * rows], ends[index : index + 1]
-        at = slot + frame * rows
         lhs_ref[at : at + rows] = row_taps(column, end, end).astype(lhs_ref.dtype)
 
 
 def tile_sum(tile, inputs, lanes, room, lhs_ref, weight_ref):
     count, rows, cols, wide = tile
-    inner = count * rows * cols
-    col = lax.broadcasted_iota(jnp.int32, tile, 2)
+    size = rows * cols
+    col = lax.broadcasted_iota(jnp.int32, tile[1:], 1)
 
     def beside(cells):
-        return cells.reshape(count, rows, 1, wide) if room else 0.0
-
-    total = dot(lhs_ref[room : room + inner], weight_ref, 1, lanes, inputs).reshape(tile)
-    first = dot(lhs_ref[: room + inner], weight_ref, 0, lanes, inputs)
-    halo = beside(first[:room])
-    total += jnp.where(col == 0, halo, pltpu.roll(first[room:].reshape(tile), 1, 2))
-    last = dot(lhs_ref[room:], weight_ref, 2, lanes, inputs)
-    halo = beside(last[inner:])
-    return total + jnp.where(
-        col == cols - 1, halo, pltpu.roll(last[:inner].reshape(tile), cols - 1, 2)
-    )
+        return cells.reshape(rows, 1, wide) if room else 0.0
+
+    for frame in range(count):
+        at = frame * (size + 2 * room)
+        end = at + room + size
+        total = dot(lhs_ref[at + room : end], weight_ref, 1, lanes, inputs).reshape(tile[1:])
+        first = dot(lhs_ref[at:end], weight_ref, 0, lanes, inputs)
+        shifted = pltpu.roll(first[room:].reshape(tile[1:]), 1, 1)
+        total += jnp.where(col == 0, beside(first[:room]), shifted)
+        last = dot(lhs_ref[at + room : end + room], weight_ref, 2, lanes, inputs)
+        shifted = pltpu.roll(last[:size].reshape(tile[1:]), cols - 1, 1)
+        yield total + jnp.where(col == cols - 1, beside(last[size:]), shifted)
 
 
 def strip_sum(tile, inputs, lanes, lhs_ref, weight_ref):
@@ -449,11 +455,13 @@
     size = rows * cols
     for frame in range(count):
         put_row(lhs_ref, frame * size, size, got_ref[frame])
-    out_ref[...] = tile_sum(out_ref.shape, inputs, lanes, 0, lhs_ref, weight_ref)
+    further_kernel(inputs, lanes, lhs_ref, weight_ref, out_ref)
 
 
 def further_kernel(inputs, lanes, lhs_ref, weight_ref, out_ref):
-    out_ref[...] = tile_sum(out_ref.shape, inputs, lanes, 0, lhs_ref, weight_ref)
+    tiles = tile_sum(out_ref.shape, inputs, lanes, 0, lhs_ref, weight_ref)
+    for frame, total in enumerate(tiles):
+        out_ref[frame] = total
 
 
 def result_kernel(
@@ -462,16 +470,14 @@
     *before_refs, out_ref, lhs_ref, held_ref, strip_lhs_ref, sems = refs
     count, rows, cols, _ = held_ref.shape
     size, room = rows * cols, count * rows
+    stride = size + 2 * rows
     for frame in range(count):
-        put_row(lhs_ref, room + frame * size, size, got_ref[frame, :cols])
+        at = frame * stride
+        put_row(lhs_ref, at + rows, size, got_ref[frame, :cols])
         ends = got_ref[frame, cols:]
-        put_columns_taps(
-            lhs_ref, (0, room + count * size), frame, count, beside_ref[frame], ends
-        )
-        slots = [slot * room for slot in range(4)]
-        put_columns_taps(
-            strip_lhs_ref, slots, frame, count, strips_ref[frame], ends.astype(jnp.float32)[2:]
-        )
+        put_columns_taps(lhs_ref, (at, at + rows + size), beside_ref[frame], ends)
+        slots = [slot * room + frame * rows for slot in range(4)]
+        put_columns_taps(strip_lhs_ref, slots, strips_ref[frame], ends.astype(jnp.float32)[2:])
 
     def store(frame, part):
         here = (frame, slice(None), slice(None), parts[part])
@@ -479,11 +485,11 @@
 
     for part, lanes in enumerate(parts):
         tile = (count, rows, cols, lanes.stop - lanes.start)
-        total = before_refs[part][...]
-        total += strip_sum(tile, parts[0], lanes, strip_lhs_ref, weight_ref)
-        total += tile_sum(tile, parts[1], lanes, room, lhs_ref, weight_ref)
-        for frame in range(count):
-            held_ref[frame, :, :, lanes] = total[frame].astype(held_ref.dtype)
+        strips = strip_sum(tile, parts[0], lanes, strip_lhs_ref, weight_ref)
+        tiles = tile_sum(tile, parts[1], lanes, rows, lhs_ref, weight_ref)
+        for frame, total in enumerate(tiles):
+            total += before_refs[part][frame] + strips[frame]
+            held_ref[frame, :, :, lanes] = total.astype(held_ref.dtype)
             store(frame, part).start()
     for part in range(len(parts)):
         for frame in range(count):

time: 40.7 us -> 40.5 us (level)
  no operation moved by 1% of the time
where the time goes in v13:
time: 40.5 us; the launch traced here: 40 us
  Pallas kernels  16 us (40%)
  starting transfers between devices  13.1 us (32%)
  waiting for transfers between devices  8.92 us (22%)
  local copies, waits for them, and re-layouts  1.51 us (4%)
    pallas_call x16, Pallas kernels, call(): pl.pallas_call(kernel, in_specs=[WHOLE] * len(args), out_specs=out_specs...  16 us
    ppermute x2, waiting for transfers between devices, exchange_four(): got = lax.ppermute(end, axes, first_round)  5.17 us
    ppermute x2, starting transfers between devices, exchange_four(): arrivals.append((got, lax.ppermute(relayed, axes, second_round)))  4.28 us
    ppermute x4, starting transfers between devices, swap_cores(): return lax.ppermute(array, 'sx', [(0, 1), (1, 0)])  3.93 us
    ppermute x2, starting transfers between devices, exchange_four(): got = lax.ppermute(end, axes, first_round)  2.57 us
    ppermute x1, starting transfers between devices, trade_columns(): return (got, lax.ppermute(columns, ('sx', 'sy'), pairs))  2.33 us
    ppermute x2, waiting for transfers between devices, exchange_four(): arrivals.append((got, lax.ppermute(relayed, axes, second_round)))  1.65 us
    unnamed x16, local copies, waits for them, and re-layouts  1.5 us
  transfers between devices with their start and end apart: 9, of which 7 were waited for; matrix products, arithmetic and copies ran while one was open for 0% of the time, Pallas kernels for 27%

profile of v13, /device:TPU:23, one launch (start us, length us, event | category | flops | bytes accessed | tf_op | source)
XLA Modules:
  0.0 40.0 jit_solution(405081884423634493)
XLA Ops:
  0.0 0.0 copy-start
  0.0 0.0 copy-start.2
  0.0 1.3 %copy-done.2 = bf16[2,32,16,512]{3,2,1,0:T(8,128)(2,1)S(1)} copy-done((bf16[2,32,16,512]{3,2,1,0:T(8,128)(2,1)S(1)}, bf16[2,32,16,512]{3,2,1,0:T(8,128)(2,1)}, u32[]{:S(2)}) %copy-start.2) | copy-done | bytes 1048600
  1.3 0.3 shard_map.64
  1.7 0.0 copy-start.3
  1.7 0.0 copy-done
  1.7 0.3 shard_map.65
  2.0 0.0 copy-start.1
  2.0 0.0 copy-start.4
  2.0 0.7 %collective-permute-start = (bf16[192,512]{1,0:T(8,128)(2,1)S(1)}, bf16[192,512]{1,0:T(8,128)(2,1)S(1)}, u32[]{:S(2)}, u32[]{:S(2)}) collective-permute-start(bf16[192,512]{1,0:T(8,128)(2,1)S(1)} %get-tuple-element.34), channel_id=1, source_target_pairs={{0,4},{4,0},{1,5},{5,1},{2,6},{6,2},{3,7},{7,3},{8,12},{12,8},{9,1... | collective-permute-start | bytes 589832 | tf_op jit(solution)/shard_map/ppermute | solution.py:51
  2.7 0.2 copy-done.3
  2.9 0.2 shard_map.66._
  3.1 0.7 %collective-permute-done.got_ref = bf16[192,512]{1,0:T(8,128)(2,1)S(1)} collective-permute-done((bf16[192,512]{1,0:T(8,128)(2,1)S(1)}, bf16[192,512]{1,0:T(8,128)(2,1)S(1)}, u32[]{:S(2)}, u32[]{:S(2)}) %collective-permute-start) | collective-permute-done | bytes 196640 | tf_op jit(solution)/shard_map/ppermute | solution.py:51
  3.8 2.3 %collective-permute-start.1 = (bf16[5,64,512]{2,1,0:T(8,128)(2,1)S(1)}, bf16[5,64,512]{2,1,0:T(8,128)(2,1)S(1)}, u32[]{:S(2)}, u32[]{:S(2)}) collective-permute-start(bf16[5,64,512]{2,1,0:T(8,128)(2,1)S(1)} %pad_maximum_fusion), channel_id=1, source_target_pairs={{0,5},{1,6},{2,7},{5,0},{6,1},{7,2},{8,13},{9,14},{10,15},{13,8},{... | collective-permute-start | bytes 983048 | tf_op jit(solution)/shard_map/ppermute | solution.py:95
  6.2 0.0 copy-done.1
  6.2 0.0 copy-done.4
  6.2 5.2 %shard_map.67 = (f32[2,32,16,512]{3,2,1,0:T(8,128)S(1)}, f32[2,64,512]{2,1,0:T(8,128)S(1)}, bf16[512,256]{1,0:T(8,128)(2,1)S(1)}, bf16[1024,1536]{1,0:T(8,128)(2,1)S(1)}) custom-call(bf16[1024,1536]{1,0:T(8,128)(2,1)S(1)} %shard_map.66._, bf16[192,512]{1,0:T(8,128)(2,1)S(1)} %collective-permute-done.got_ref, ...), custom_call_target="tpu_custom_call", output_to_operand_aliasing={{3}: (0, {})} | custom-call | flops 4831838208 | bytes 13830144 | tf_op jit(solution)/shard_map/pallas_call | solution.py:21
  11.4 0.9 %collective-permute-done.1.mine_ref = bf16[5,64,512]{2,1,0:T(8,128)(2,1)S(1)} collective-permute-done((bf16[5,64,512]{2,1,0:T(8,128)(2,1)S(1)}, bf16[5,64,512]{2,1,0:T(8,128)(2,1)S(1)}, u32[]{:S(2)}, u32[]{:S(2)}) %collective-permute-start.1) | collective-permute-done | bytes 327712 | tf_op jit(solution)/shard_map/ppermute | solution.py:95
  12.2 0.5 %collective-permute-start.2 = (bf16[5,64,512]{2,1,0:T(8,128)(2,1)S(1)}, bf16[5,64,512]{2,1,0:T(8,128)(2,1)S(1)}, u32[]{:S(2)}, u32[]{:S(2)}) collective-permute-start(bf16[5,64,512]{2,1,0:T(8,128)(2,1)S(1)} %collective-permute-done.1.mine_ref), channel_id=1, source_target_pairs={{0,4},{4,0},{1,5},{5,1},{2,6},{6,2},{3,7},{7,3},{8,12},{12,8},{9,1... | collective-permute-start | bytes 983048 | tf_op jit(solution)/shard_map/ppermute | solution.py:51
  12.7 1.3 %collective-permute-start.5 = (bf16[512,256]{1,0:T(8,128)(2,1)S(1)}, bf16[512,256]{1,0:T(8,128)(2,1)S(1)}, u32[]{:S(2)}, u32[]{:S(2)}) collective-permute-start(bf16[512,256]{1,0:T(8,128)(2,1)S(1)} %get-tuple-element.43.end_ref), channel_id=1, source_target_pairs={{0,8},{8,0},{16,24},{4,20},{12,28},{1,9},{9,1},{17,25},{5,21},{13,... | collective-permute-start | bytes 786440 | tf_op jit(solution)/shard_map/ppermute | solution.py:289
  14.0 0.0 collective-permute-done.2.theirs_ref
  14.0 0.2 shard_map.68
  14.2 0.0 copy-start.5
  14.2 1.0 %shard_map.69 = (f32[2,32,16,256]{3,2,1,0:T(8,128)S(1)}, f32[2,64,256]{2,1,0:T(8,128)S(1)}, f32[2,128,256]{2,1,0:T(8,128)S(1)}, bf16[704,256]{1,0:T(8,128)(2,1)S(1)}) custom-call(bf16[256,1536]{1,0:T(8,128)(2,1)S(1)} %get-tuple-element.38.lhs_ref, bf16[3,3,512,512]{3,2,1,0:T(8,128)(2,1)S(1)} %copy-done.1, ...), custom_call_target="tpu_custom_call" | custom-call | flops 603979776 | bytes 9668608 | tf_op jit(solution)/shard_map/pallas_call | solution.py:21
  15.2 1.3 %collective-permute-start.3 = (bf16[704,256]{1,0:T(8,128)(2,1)S(1)}, bf16[704,256]{1,0:T(8,128)(2,1)S(1)}, u32[]{:S(2)}, u32[]{:S(2)}) collective-permute-start(bf16[704,256]{1,0:T(8,128)(2,1)S(1)} %get-tuple-element.42.end_ref), channel_id=1, source_target_pairs={{0,8},{8,0},{16,24},{4,20},{12,28},{1,9},{9,1},{17,25},{5,21},{13,... | collective-permute-start | bytes 1081352 | tf_op jit(solution)/shard_map/ppermute | solution.py:289
  16.5 3.6 %collective-permute-done.5.got_ref.refs_4_ = bf16[512,256]{1,0:T(8,128)(2,1)S(1)} collective-permute-done((bf16[512,256]{1,0:T(8,128)(2,1)S(1)}, bf16[512,256]{1,0:T(8,128)(2,1)S(1)}, u32[]{:S(2)}, u32[]{:S(2)}) %collective-permute-start.5) | collective-permute-done | bytes 262176 | tf_op jit(solution)/shard_map/ppermute | solution.py:289
  20.1 0.0 slice-start
  20.1 0.1 shard_map.71
  20.2 2.2 %collective-permute-start.6 = (bf16[512,256]{1,0:T(8,128)(2,1)S(1)}, bf16[512,256]{1,0:T(8,128)(2,1)S(1)}, u32[]{:S(2)}, u32[]{:S(2)}) collective-permute-start(bf16[512,256]{1,0:T(8,128)(2,1)S(1)} %shard_map.71), channel_id=1, source_target_pairs={{0,16},{8,24},{4,12},{20,28},{28,20},{1,17},{9,25},{5,13},{21,29},... | collective-permute-start | bytes 786440 | tf_op jit(solution)/shard_map/ppermute | solution.py:292
  22.4 1.5 %collective-permute-done.3.got_ref.refs_4_.refs_7_ = bf16[704,256]{1,0:T(8,128)(2,1)S(1)} collective-permute-done((bf16[704,256]{1,0:T(8,128)(2,1)S(1)}, bf16[704,256]{1,0:T(8,128)(2,1)S(1)}, u32[]{:S(2)}, u32[]{:S(2)}) %collective-permute-start.3) | collective-permute-done | bytes 360480 | tf_op jit(solution)/shard_map/ppermute | solution.py:289
  24.0 0.2 shard_map.70
  24.1 2.1 %collective-permute-start.4 = (bf16[704,256]{1,0:T(8,128)(2,1)S(1)}, bf16[704,256]{1,0:T(8,128)(2,1)S(1)}, u32[]{:S(2)}, u32[]{:S(2)}) collective-permute-start(bf16[704,256]{1,0:T(8,128)(2,1)S(1)} %shard_map.70), channel_id=1, source_target_pairs={{0,16},{8,24},{4,12},{20,28},{28,20},{1,17},{9,25},{5,13},{21,29},... | collective-permute-start | bytes 1081352 | tf_op jit(solution)/shard_map/ppermute | solution.py:292
  26.3 1.6 %collective-permute-done.6.refs_5_ = bf16[512,256]{1,0:T(8,128)(2,1)S(1)} collective-permute-done((bf16[512,256]{1,0:T(8,128)(2,1)S(1)}, bf16[512,256]{1,0:T(8,128)(2,1)S(1)}, u32[]{:S(2)}, u32[]{:S(2)}) %collective-permute-start.6) | collective-permute-done | bytes 262176 | tf_op jit(solution)/shard_map/ppermute | solution.py:292
  27.9 0.0 copy-done.5
  27.9 0.0 slice-start.1
  28.0 1.8 %collective-permute-start.7 = (bf16[2,16,256]{2,1,0:T(8,128)(2,1)S(1)}, bf16[2,16,256]{2,1,0:T(8,128)(2,1)S(1)}, u32[]{:S(2)}, u32[]{:S(2)}) collective-permute-start(bf16[2,16,256]{2,1,0:T(8,128)(2,1)S(1)} %shard_map.73), channel_id=1, source_target_pairs={{0,4},{4,0},{1,5},{5,1},{2,6},{6,2},{3,7},{7,3},{8,12},{12,8},{9,1... | collective-permute-start | bytes 49160 | tf_op jit(solution)/shard_map/ppermute | solution.py:51
  29.8 0.6 %shard_map.72._ = bf16[1024,768]{1,0:T(8,128)(2,1)S(1)} custom-call(f32[2,32,16,512]{3,2,1,0:T(8,128)S(1)} %get-tuple-element.39.total_ref.refs_0_, f32[32,16,512]{2,1,0:T(8,128)S(1)} %copy-done, s32[1,512]{1,0:T(1,128)S(1)} %bitcast.10, f32[1,512]{1,0:T(1,128)S(1)} %bitcast.14, bf16[512,256]{1,0:T(8,128)(2,1)S(1)} %collective-permute-done.5.got_ref.refs_4_, ...), custom_call_target="tpu_custom_call" | custom-call | bytes 5246976 | tf_op jit(solution)/shard_map/pallas_call | solution.py:21
  30.4 0.2 collective-permute-done.7.got_ref
  30.6 0.0 slice-done
  30.6 0.0 slice-done.1
  30.6 1.4 %shard_map.74 = (f32[2,32,16,256]{3,2,1,0:T(8,128)S(1)}, bf16[1024,768]{1,0:T(8,128)(2,1)S(1)}) custom-call(bf16[1024,768]{1,0:T(8,128)(2,1)S(1)} %shard_map.72._, bf16[2,16,256]{2,1,0:T(8,128)(2,1)S(1)} %collective-permute-done.7.got_ref, bf16[3,3,512,512]{3,2,1,0:T(8,128)(2,1)S(1)} %bitcast.4), custom_call_target="tpu_custom_call", output_to_operand_aliasing={{1}: (0, {})} | custom-call | flops 1207959552 | bytes 8929280 | tf_op jit(solution)/shard_map/pallas_call | solution.py:21
  32.0 1.4 %shard_map.75.refs_1_ = f32[2,32,16,256]{3,2,1,0:T(8,128)S(1)} custom-call(bf16[1024,768]{1,0:T(8,128)(2,1)S(1)} %get-tuple-element.45.lhs_ref, bf16[3,3,512,512]{3,2,1,0:T(8,128)(2,1)S(1)} %bitcast.4), custom_call_target="tpu_custom_call" | custom-call | flops 1207959552 | bytes 7340032 | tf_op jit(solution)/shard_map/pallas_call | solution.py:21
  33.4 0.1 shard_map.77.refs_4_
  33.5 0.0 collective-permute-done.4.refs_5_.refs_8_
  33.5 0.3 shard_map.78
  33.8 0.9 %collective-permute-start.8 = (bf16[2,32,256]{2,1,0:T(8,128)(2,1)S(1)}, bf16[2,32,256]{2,1,0:T(8,128)(2,1)S(1)}, u32[]{:S(2)}, u32[]{:S(2)}) collective-permute-start(bf16[2,32,256]{2,1,0:T(8,128)(2,1)S(1)} %get-tuple-element.51), channel_id=1, source_target_pairs={{0,4},{4,0},{1,5},{5,1},{2,6},{6,2},{3,7},{7,3},{8,12},{12,8},{9,1... | collective-permute-start | bytes 98312 | tf_op jit(solution)/shard_map/ppermute | solution.py:51
  34.7 0.6 %shard_map.76._ = bf16[1152,768]{1,0:T(8,128)(2,1)S(1)} custom-call(f32[2,32,16,256]{3,2,1,0:T(8,128)S(1)} %get-tuple-element.41.refs_0_, f32[32,16,512]{2,1,0:T(8,128)S(1)} %copy-done, s32[1,512]{1,0:T(1,128)S(1)} %bitcast.12, f32[1,512]{1,0:T(1,128)S(1)} %bitcast.16, bf16[704,256]{1,0:T(8,128)(2,1)S(1)} %collective-permute-done.3.got_ref.refs_4_.refs_7_, ...), custom_call_target="tpu_custom_call" | custom-call | bytes 4591616 | tf_op jit(solution)/shard_map/pallas_call | solution.py:21
  35.3 0.3 collective-permute-done.8.got_ref
  35.6 4.2 %shard_map.79 = (bf16[2,32,16,512]{3,2,1,0:T(8,128)(2,1)}, bf16[1152,768]{1,0:T(8,128)(2,1)S(1)}) custom-call(bf16[1152,768]{1,0:T(8,128)(2,1)S(1)} %shard_map.76._, bf16[2,32,256]{2,1,0:T(8,128)(2,1)S(1)} %collective-permute-done.8.got_ref, bf16[2,64,256]{2,1,0:T(8,128)(2,1)S(1)} %get-tuple-element.52.beside_ref, ...), custom_call_target="tpu_custom_call", output_to_operand_aliasing={{1}: (0, {})} | custom-call | flops 2415919104 | bytes 11632640 | tf_op jit(solution)/shard_map/pallas_call | solution.py:21
  (4 shorter events, 0.1 us)
Async XLA Ops:
  0.0 1.7 %copy-start = (f32[32,16,512]{2,1,0:T(8,128)S(1)}, f32[32,16,512]{2,1,0:T(8,128)}, u32[]{:S(2)}) copy-start(f32[32,16,512]{2,1,0:T(8,128)} %refs_3_.1) | copy-start | bytes 3145732
  0.0 1.3 %copy-start.2 = (bf16[2,32,16,512]{3,2,1,0:T(8,128)(2,1)S(1)}, bf16[2,32,16,512]{3,2,1,0:T(8,128)(2,1)}, u32[]{:S(2)}) copy-start(bf16[2,32,16,512]{3,2,1,0:T(8,128)(2,1)} %cells_ref.3) | copy-start | bytes 3145732
  1.7 1.2 %copy-start.3 = (bf16[2,32,16,512]{3,2,1,0:T(8,128)(2,1)S(1)}, bf16[2,32,16,512]{3,2,1,0:T(8,128)(2,1)}, u32[]{:S(2)}) copy-start(bf16[2,32,16,512]{3,2,1,0:T(8,128)(2,1)} %cells_ref.3) | copy-start | bytes 3145732
  2.0 4.2 %copy-start.1 = (bf16[3,3,512,512]{3,2,1,0:T(8,128)(2,1)S(1)}, bf16[3,3,512,512]{3,2,1,0:T(8,128)(2,1)}, u32[]{:S(2)}) copy-start(bf16[3,3,512,512]{3,2,1,0:T(8,128)(2,1)} %weight_ref.6) | copy-start | bytes 14155780
  2.0 4.2 %copy-start.4 = (s32[512]{0:T(512)S(1)}, s32[512]{0:T(512)}, u32[]{:S(2)}) copy-start(s32[512]{0:T(512)} %param.9) | copy-start | bytes 6148
  2.0 1.8 %collective-permute-start = (bf16[192,512]{1,0:T(8,128)(2,1)S(1)}, bf16[192,512]{1,0:T(8,128)(2,1)S(1)}, u32[]{:S(2)}, u32[]{:S(2)}) collective-permute-start(bf16[192,512]{1,0:T(8,128)(2,1)S(1)} %get-tuple-element.34), channel_id=1, source_target_pairs={{0,4},{4,0},{1,5},{5,1},{2,6},{6,2},{3,7},{7,3},{8,12},{12,8},{9,1... | collective-permute-start | bytes 589832 | tf_op jit(solution)/shard_map/ppermute | solution.py:51
  3.8 8.4 %collective-permute-start.1 = (bf16[5,64,512]{2,1,0:T(8,128)(2,1)S(1)}, bf16[5,64,512]{2,1,0:T(8,128)(2,1)S(1)}, u32[]{:S(2)}, u32[]{:S(2)}) collective-permute-start(bf16[5,64,512]{2,1,0:T(8,128)(2,1)S(1)} %pad_maximum_fusion), channel_id=1, source_target_pairs={{0,5},{1,6},{2,7},{5,0},{6,1},{7,2},{8,13},{9,14},{10,15},{13,8},{... | collective-permute-start | bytes 983048 | tf_op jit(solution)/shard_map/ppermute | solution.py:95
  12.2 1.8 %collective-permute-start.2 = (bf16[5,64,512]{2,1,0:T(8,128)(2,1)S(1)}, bf16[5,64,512]{2,1,0:T(8,128)(2,1)S(1)}, u32[]{:S(2)}, u32[]{:S(2)}) collective-permute-start(bf16[5,64,512]{2,1,0:T(8,128)(2,1)S(1)} %collective-permute-done.1.mine_ref), channel_id=1, source_target_pairs={{0,4},{4,0},{1,5},{5,1},{2,6},{6,2},{3,7},{7,3},{8,12},{12,8},{9,1... | collective-permute-start | bytes 983048 | tf_op jit(solution)/shard_map/ppermute | solution.py:51
  12.7 7.4 %collective-permute-start.5 = (bf16[512,256]{1,0:T(8,128)(2,1)S(1)}, bf16[512,256]{1,0:T(8,128)(2,1)S(1)}, u32[]{:S(2)}, u32[]{:S(2)}) collective-permute-start(bf16[512,256]{1,0:T(8,128)(2,1)S(1)} %get-tuple-element.43.end_ref), channel_id=1, source_target_pairs={{0,8},{8,0},{16,24},{4,20},{12,28},{1,9},{9,1},{17,25},{5,21},{13,... | collective-permute-start | bytes 786440 | tf_op jit(solution)/shard_map/ppermute | solution.py:289
  14.2 13.7 %copy-start.5 = (f32[512]{0:T(512)S(1)}, f32[512]{0:T(512)}, u32[]{:S(2)}) copy-start(f32[512]{0:T(512)} %param.10) | copy-start | bytes 6148
  15.2 8.8 %collective-permute-start.3 = (bf16[704,256]{1,0:T(8,128)(2,1)S(1)}, bf16[704,256]{1,0:T(8,128)(2,1)S(1)}, u32[]{:S(2)}, u32[]{:S(2)}) collective-permute-start(bf16[704,256]{1,0:T(8,128)(2,1)S(1)} %get-tuple-element.42.end_ref), channel_id=1, source_target_pairs={{0,8},{8,0},{16,24},{4,20},{12,28},{1,9},{9,1},{17,25},{5,21},{13,... | collective-permute-start | bytes 1081352 | tf_op jit(solution)/shard_map/ppermute | solution.py:289
  20.1 10.5 %slice-start = ((s8[4718592]{0:T(1024)(128)(4,1)}), s8[4194304]{0:T(1024)(128)(4,1)S(1)}, s32[]{:S(2)}) async-start(s8[4718592]{0:T(1024)(128)(4,1)} %bitcast.3), calls=%async_computation | async-start | bytes 8388608
  20.2 7.7 %collective-permute-start.6 = (bf16[512,256]{1,0:T(8,128)(2,1)S(1)}, bf16[512,256]{1,0:T(8,128)(2,1)S(1)}, u32[]{:S(2)}, u32[]{:S(2)}) collective-permute-start(bf16[512,256]{1,0:T(8,128)(2,1)S(1)} %shard_map.71), channel_id=1, source_target_pairs={{0,16},{8,24},{4,12},{20,28},{28,20},{1,17},{9,25},{5,13},{21,29},... | collective-permute-start | bytes 786440 | tf_op jit(solution)/shard_map/ppermute | solution.py:292
  24.1 9.4 %collective-permute-start.4 = (bf16[704,256]{1,0:T(8,128)(2,1)S(1)}, bf16[704,256]{1,0:T(8,128)(2,1)S(1)}, u32[]{:S(2)}, u32[]{:S(2)}) collective-permute-start(bf16[704,256]{1,0:T(8,128)(2,1)S(1)} %shard_map.70), channel_id=1, source_target_pairs={{0,16},{8,24},{4,12},{20,28},{28,20},{1,17},{9,25},{5,13},{21,29},... | collective-permute-start | bytes 1081352 | tf_op jit(solution)/shard_map/ppermute | solution.py:292
  27.9 2.7 %slice-start.1 = ((s8[4718592]{0:T(1024)(128)(4,1)}), s8[524288]{0:T(1024)(128)(4,1)S(1)}, s32[]{:S(2)}) async-start(s8[4718592]{0:T(1024)(128)(4,1)} %bitcast.3), calls=%async_computation.1 | async-start | bytes 1048576
  28.0 2.7 %collective-permute-start.7 = (bf16[2,16,256]{2,1,0:T(8,128)(2,1)S(1)}, bf16[2,16,256]{2,1,0:T(8,128)(2,1)S(1)}, u32[]{:S(2)}, u32[]{:S(2)}) collective-permute-start(bf16[2,16,256]{2,1,0:T(8,128)(2,1)S(1)} %shard_map.73), channel_id=1, source_target_pairs={{0,4},{4,0},{1,5},{5,1},{2,6},{6,2},{3,7},{7,3},{8,12},{12,8},{9,1... | collective-permute-start | bytes 49160 | tf_op jit(solution)/shard_map/ppermute | solution.py:51
  33.8 1.8 %collective-permute-start.8 = (bf16[2,32,256]{2,1,0:T(8,128)(2,1)S(1)}, bf16[2,32,256]{2,1,0:T(8,128)(2,1)S(1)}, u32[]{:S(2)}, u32[]{:S(2)}) collective-permute-start(bf16[2,32,256]{2,1,0:T(8,128)(2,1)S(1)} %get-tuple-element.51), channel_id=1, source_target_pairs={{0,4},{4,0},{1,5},{5,1},{2,6},{6,2},{3,7},{7,3},{8,12},{12,8},{9,1... | collective-permute-start | bytes 98312 | tf_op jit(solution)/shard_map/ppermute | solution.py:51

commit v14 on v13

--- a/solution.py
+++ b/solution.py
@@ -149,6 +149,7 @@
     size = rows * cols
     for frame in range(count):
         put_row(lhs_ref, frame * size, size, got_ref[frame * cols : (frame + 1) * cols])
+    states = []
     for lanes in halves(weight_ref.shape[-1]):
         tile = (rows, cols, lanes.stop - lanes.start)
         col = lax.broadcasted_iota(jnp.int32, tile, 1)
@@ -165,9 +166,10 @@
             total += jnp.where(col == cols - 1, 0.0, pltpu.roll(last, cols - 1, 1))
             total_ref[frame, :, :, lanes] = total
             totals.append(total)
-        if lanes.start == 0:
-            state = end_state(totals, pole_ref, lanes)
-            end_ref[...] = state.reshape(end_ref.shape).astype(end_ref.dtype)
+        states.append(end_state(totals, pole_ref, lanes))
+    state = jnp.where(col == 0, pltpu.roll(states[1], cols - 1, 1), states[0])
+    state = jnp.where(col == cols - 1, pltpu.roll(states[1], 1, 1), state)
+    end_ref[...] = state.reshape(end_ref.shape).astype(end_ref.dtype)
 
 
 def halo_kernel(mine_ref, theirs_ref, lhs_ref, start_ref):
@@ -199,6 +201,7 @@
     count, rows, cols, wide = drive_ref.shape
     room, size = count * rows, rows * cols
     at = size + 2 * rows
+    early = None
     for lanes in halves(weight_ref.shape[-1]):
         first = dot(lhs_ref[: 2 * room], weight_ref, 0, lanes)
         middle = dot(lhs_ref[room : 3 * room], weight_ref, 1, lanes)
@@ -211,14 +214,19 @@
             far = total[:, :, cols - 1, :] + last[:room].reshape(count, rows, wide)
             strips = jnp.concatenate([left, near, far, right], axis=1)
             strips_ref[...] = strips
-            state = end_state([strips[frame] for frame in range(count)], pole_ref, lanes)
-            end_ref[at:] = state.astype(end_ref.dtype)
+            early = end_state([strips[frame] for frame in range(count)], pole_ref, lanes)
+            end_ref[at : at + rows] = early[:rows].astype(end_ref.dtype)
+            end_ref[at + rows :] = early[3 * rows :].astype(end_ref.dtype)
             continue
         col = lax.broadcasted_iota(jnp.int32, drive_ref.shape, 2)
         total += jnp.where(col == 0, first[room:].reshape(count, rows, 1, wide), 0.0)
         total += jnp.where(col == cols - 1, last[:room].reshape(count, rows, 1, wide), 0.0)
         drive_ref[...] = total
         state = end_state([total[frame] for frame in range(count)], pole_ref, lanes)
+        col = lax.broadcasted_iota(jnp.int32, state.shape, 1)
+        state = jnp.where(col == 1, early[rows : 2 * rows].reshape(rows, 1, wide), state)
+        border = early[2 * rows : 3 * rows].reshape(rows, 1, wide)
+        state = jnp.where(col == cols - 2, border, state)
         end_ref[:size] = state.reshape(size, wide).astype(end_ref.dtype)
         beside = jnp.concatenate([left, right], axis=1)
         beside_ref[...] = beside
@@ -226,8 +234,22 @@
         end_ref[size:at] = state.astype(end_ref.dtype)
 
 
-def entry_kernel(frames, ends_ref, pole_ref, out_ref):
-    carried = jnp.exp(frames * rate_of(pole_ref))
+def spread(block, cols, count, of_lanes):
+    _, lanes, inset = block
+    value = of_lanes(lanes)
+    if inset is None:
+        return value
+    other, columns = inset
+    value, instead = jnp.broadcast_arrays(value, of_lanes(other))
+    shape = (count, value.shape[1])
+    col = lax.rem(lax.broadcasted_iota(jnp.int32, shape, 0), cols)
+    return jnp.where((col == columns[0]) | (col == columns[1]), instead, value)
+
+
+def entry_kernel(frames, cols, block, ends_ref, pole_ref, out_ref):
+    rate = rate_of(pole_ref)
+    count = ends_ref.shape[1]
+    carried = spread(block, cols, count, lambda lanes: jnp.exp(frames * rate[:, lanes]))
     entry = jnp.zeros(ends_ref.shape[1:], jnp.float32)
     out_ref[0] = entry.astype(out_ref.dtype)
     for index in range(ends_ref.shape[0] - 1):
@@ -235,16 +257,17 @@
         out_ref[index + 1] = entry.astype(out_ref.dtype)
 
 
-def exchange(pieces, pole, frames):
+def exchange(pieces, pole, frames, cols):
     groups = lax.axis_size("tm")
     arrivals = []
     for end, blocks in pieces:
         entries = []
-        for rows, lanes in blocks:
-            shares = end[rows].reshape(groups, -1, end.shape[1])
+        for block in blocks:
+            shares = end[block[0]].reshape(groups, -1, end.shape[1])
+            assert block[2] is None or shares.shape[1] % cols == 0
             shares = lax.all_to_all(shares, "tm", 0, 0)
-            kernel = functools.partial(entry_kernel, frames)
-            entry = call(kernel, of(shares.shape, end.dtype), shares, pole[:, lanes])
+            kernel = functools.partial(entry_kernel, frames, cols, block)
+            entry = call(kernel, of(shares.shape, end.dtype), shares, pole)
             entries.append(lax.all_to_all(entry, "tm", 0, 0).reshape(-1, end.shape[1]))
         arrivals.append((jnp.concatenate(entries, axis=0),))
     return arrivals
@@ -266,17 +289,21 @@
     return by_one * one.astype(jnp.float32) + by_other * other.astype(jnp.float32)
 
 
-def relay_kernel(frames, blocks, end_ref, got_ref, pole_ref, out_ref):
-    for rows, lanes in blocks:
-        rate = rate_of(pole_ref)[:, lanes]
-        carried, twice = jnp.exp(frames * rate), jnp.exp(2 * frames * rate)
-        none, same = jnp.zeros_like(rate), jnp.ones_like(rate)
-        own = on_core(pick([carried, same, same, same]), pick([same, same, same, none]))
-        got = on_core(pick([same, carried, carried, carried]), pick([none, none, twice, same]))
-        out_ref[rows] = weigh(end_ref[rows], own, got_ref[rows], got).astype(out_ref.dtype)
-
-
-def exchange_four(pieces, pole, frames):
+def relay_kernel(frames, cols, blocks, end_ref, got_ref, pole_ref, out_ref):
+    rate = rate_of(pole_ref)
+    carried, twice = jnp.exp(frames * rate), jnp.exp(2 * frames * rate)
+    none, same = jnp.zeros_like(rate), jnp.ones_like(rate)
+    own = on_core(pick([carried, same, same, same]), pick([same, same, same, none]))
+    got = on_core(pick([same, carried, carried, carried]), pick([none, none, twice, same]))
+    for block in blocks:
+        rows = block[0]
+        count = rows.stop - rows.start
+        by_own = spread(block, cols, count, lambda lanes: own[:, lanes])
+        by_got = spread(block, cols, count, lambda lanes: got[:, lanes])
+        out_ref[rows] = weigh(end_ref[rows], by_own, got_ref[rows], by_got).astype(out_ref.dtype)
+
+
+def exchange_four(pieces, pole, frames, cols):
     def along(pairs, core):
         return [(2 * source + core, 2 * target + core) for source, target in pairs]
 
@@ -287,69 +314,74 @@
     arrivals = []
     for end, blocks in pieces:
         got = lax.ppermute(end, axes, first_round)
-        kernel = functools.partial(relay_kernel, frames, blocks)
+        kernel = functools.partial(relay_kernel, frames, cols, blocks)
         relayed = call(kernel, of(end.shape, end.dtype), end, got, pole)
         arrivals.append((got, lax.ppermute(relayed, axes, second_round)))
     return arrivals
 
 
 class Mix:
-    def __init__(self, lanes, count, arrived_refs, pole_ref, scale_ref):
+    def __init__(self, lanes, count, pole_ref, scale_ref):
         self.rate = rate_of(pole_ref)[:, lanes]
         self.scale = scale_ref[:, lanes]
         self.count = count
-        self.arrived_refs = arrived_refs
-
-    def entry(self, rows):
-        parts = [ref[rows] for ref in self.arrived_refs]
+
+    def entry(self, arrived_refs, rows):
+        parts = [ref[rows].astype(jnp.float32) for ref in arrived_refs]
         if len(parts) == 1:
-            return parts[0].astype(jnp.float32)
+            return parts[0]
         carried = jnp.exp(self.count * self.rate)
         none, same = jnp.zeros_like(self.rate), jnp.ones_like(self.rate)
         early = on_core(pick([none, same, none, same]), pick([none, none, carried, carried]))
         late = on_core(pick([none, none, same, carried]), pick([none, same, same, same]))
         return weigh(parts[0], early, parts[1], late)
 
-    def __call__(self, drives, rows, start):
+    def __call__(self, drives, entry, start):
         decay = jnp.exp(self.rate)
         reach = jnp.exp((self.count * lax.axis_index("tm")).astype(jnp.float32) * self.rate)
-        state = reach * start + self.entry(rows).reshape(start.shape)
+        state = reach * start + entry.reshape(start.shape)
         for drive in drives:
             state = decay * state + drive
             yield jax.nn.gelu(self.scale * state)
 
 
-def middle_kernel(lanes, *refs):
-    total_ref, start_ref, pole_ref, scale_ref, *arrived_refs, give_ref = refs
-    count, rows, cols, _ = total_ref.shape
-    mix = Mix(lanes, count, arrived_refs, pole_ref, scale_ref)
-    inner = inner_row(rows)
-    drives = [total_ref[frame, inner, :, lanes] for frame in range(count)]
-    here = pl.ds(pl.multiple_of(inner * cols, cols), cols)
-    col = lax.broadcasted_iota(jnp.int32, give_ref.shape[1:], 0)
-    for frame, cells in enumerate(mix(drives, here, start_ref[inner, :, lanes])):
-        cells = jnp.where((col == 0) | (col == cols - 1), 0.0, cells)
-        give_ref[frame] = cells.astype(give_ref.dtype)
-
-
-def mixed_kernel(lanes, inner_only, *refs):
+def no_border(cells, axis):
+    col = lax.broadcasted_iota(jnp.int32, cells.shape, axis)
+    return jnp.where((col == 0) | (col == cells.shape[axis] - 1), 0.0, cells)
+
+
+def put_back(late, early, axis):
+    cols = late.shape[axis]
+    col = lax.broadcasted_iota(jnp.int32, late.shape, axis)
+    late = jnp.where(col == 1, pltpu.roll(early, 1, axis), late)
+    return jnp.where(col == cols - 2, pltpu.roll(early, cols - 1, axis), late)
+
+
+def mixed_kernel(lanes, rounds, *refs):
     drive_ref, start_ref, pole_ref, scale_ref, *arrived_refs, lhs_ref = refs
+    early_refs, late_refs = arrived_refs[:rounds], arrived_refs[rounds:]
     count, rows, cols, _ = drive_ref.shape
     wide = lanes.stop - lanes.start
     size = rows * cols
     stride = lhs_ref.shape[0] // count
     room = (stride - size) // 2
-    mix = Mix(lanes, count, arrived_refs, pole_ref, scale_ref)
-    held = lanes if inner_only else slice(None)
+    mix = Mix(lanes, count, pole_ref, scale_ref)
+    first = lanes.start == 0
+    held = lanes if first else slice(None)
     block = 8
-    col = lax.broadcasted_iota(jnp.int32, (block, cols, wide), 1)
+    if first:
+        for frame in range(count):
+            put_row(lhs_ref, frame * stride + room, size, jnp.zeros((cols, wide), lhs_ref.dtype))
     for row in range(0, rows, block):
         here = slice(row, row + block)
         drives = [drive_ref[frame, here, :, held] for frame in range(count)]
         cells = slice(row * cols, (row + block) * cols)
-        for frame, tile in enumerate(mix(drives, cells, start_ref[here, :, lanes])):
-            if inner_only:
-                tile = jnp.where((col == 0) | (col == cols - 1), 0.0, tile)
+        entry = mix.entry(early_refs, cells).reshape(block, cols, wide)
+        if not first:
+            entry = put_back(mix.entry(late_refs, cells).reshape(entry.shape), entry, 1)
+        for frame, tile in enumerate(mix(drives, entry, start_ref[here, :, lanes])):
+            if first:
+                tile = no_border(tile, 1)
             tile = tile.reshape(block * cols, wide).astype(lhs_ref.dtype)
             put_cells(lhs_ref, frame * stride + room, size, cols, row * cols, tile)
 
@@ -363,45 +395,102 @@
     out_ref[3 * rows :] = sides_ref[rows:]
 
 
-def late_kernel(parts, *refs):
-    drive_ref, beside_ref, strips_ref, start_ref, strip_start_ref, pole_ref, scale_ref, *refs = refs
-    *arrived_refs, give_ref, beside_out_ref, strips_out_ref = refs
+def inside(slot):
+    chip, chips = lax.axis_index("sy"), lax.axis_size("sy")
+    return {0: (chip > 0).astype(jnp.float32), 3: (chip < chips - 1).astype(jnp.float32)}.get(slot, 1.0)
+
+
+def give_kernel(parts, rounds, *refs):
+    total_ref, drive_ref, beside_ref, strips_ref, *refs = refs
+    start_ref, strip_start_ref, pole_ref, scale_ref, *arrived_refs, give_ref = refs
+    early_refs, late_refs = arrived_refs[:rounds], arrived_refs[rounds:]
     count, rows, cols, wide = drive_ref.shape
     size = rows * cols
     inner = inner_row(rows)
     zero, one = is_core(0), is_core(1)
-    chip, chips = lax.axis_index("sy"), lax.axis_size("sy")
-    inside = [(chip > 0).astype(jnp.float32), (chip < chips - 1).astype(jnp.float32)]
-    early, late = (Mix(lanes, count, arrived_refs, pole_ref, scale_ref) for lanes in parts)
-
-    def columns_of(cells, count):
-        return [cells[index * rows : (index + 1) * rows] for index in range(count)]
-
-    starts = columns_of(strip_start_ref, 4)
-    starts = jnp.concatenate([starts[0][:, parts[1]], starts[3][:, parts[1]]], axis=0)
+    early, late = (Mix(lanes, count, pole_ref, scale_ref) for lanes in parts)
+    row = pl.ds(pl.multiple_of(inner * cols, cols), cols)
+    which = lax.broadcasted_iota(jnp.int32, (cols, wide), 0)
+
+    def near(at):
+        return pl.ds(pl.multiple_of(at + jnp.where(inner == 0, 0, rows - cols), cols), cols)
+
+    def end(cells):
+        return zero * cells[cols - 1 :] + one * cells[:1]
+
+    def rows_of(cells):
+        table = jnp.zeros(which.shape, jnp.float32)
+        for index, cell in cells:
+            table = jnp.where(which == index, cell, table)
+        return table
+
+    entry = put_back(late.entry(late_refs, row), late.entry(early_refs, row), 0)
+    drives = [drive_ref[frame, inner] for frame in range(count)]
+    tile = late(drives, entry, start_ref[inner, :, parts[1]])
+    drives = [total_ref[frame, inner, :, parts[0]] for frame in range(count)]
+    first = early(drives, early.entry(early_refs, row), start_ref[inner, :, parts[0]])
+
+    slots = [(0, 0), (1, 3)]
+    entry = rows_of([(i, end(late.entry(late_refs, near(size + i * rows)))) for i, _ in slots])
+    start = rows_of([(i, end(strip_start_ref[near(slot * rows), parts[1]])) for i, slot in slots])
+    drives = [
+        rows_of([(i, end(beside_ref[frame, near(i * rows)])) for i, _ in slots])
+        for frame in range(count)
+    ]
+    beside = late(drives, entry, start)
+
+    slots = [(2 + slot, slot) for slot in range(4)]
+    grid = early.entry(late_refs, row)
     at = size + 2 * rows
-    beside = late([beside_ref[frame] for frame in range(count)], slice(size, at), starts)
-    strips = early(
-        [strips_ref[frame] for frame in range(count)],
-        slice(at, at + 4 * rows),
-        strip_start_ref[:, parts[0]],
-    )
-    here = pl.ds(pl.multiple_of(inner * cols, cols), cols)
-    drives = [drive_ref[frame, inner] for frame in range(count)]
-    tile = late(drives, here, start_ref[inner, :, parts[1]])
-    which = lax.broadcasted_iota(jnp.int32, (cols, wide), 0)
-    for frame, (cells, sides, strip) in enumerate(zip(tile, beside, strips)):
-        sides, strip = columns_of(sides, 2), columns_of(strip, 4)
-        sides = [sides[0] * inside[0], sides[1] * inside[1]]
-        strip = [strip[0] * inside[0], strip[1], strip[2], strip[3] * inside[1]]
-        give_ref[frame, :cols] = cells.astype(give_ref.dtype)
-        ends = jnp.zeros(which.shape, jnp.float32)
-        for index, column in enumerate((*sides, *strip)):
-            end = zero * column[rows - 1 :] + one * column[:1]
-            ends = jnp.where(which == index, end, ends)
-        give_ref[frame, cols:] = ends.astype(give_ref.dtype)
-        beside_out_ref[frame] = jnp.concatenate(sides, axis=0).astype(give_ref.dtype)
-        strips_out_ref[frame] = jnp.concatenate(strip, axis=0).astype(give_ref.dtype)
+    entry = rows_of(
+        [
+            (2, end(early.entry(late_refs, near(at)))),
+            (3, grid[1:2]),
+            (4, grid[cols - 2 : cols - 1]),
+            (5, end(early.entry(late_refs, near(at + rows)))),
+        ]
+    )
+    start = rows_of([(i, end(strip_start_ref[near(slot * rows), parts[0]])) for i, slot in slots])
+    drives = [
+        rows_of([(i, end(strips_ref[frame, near(slot * rows)])) for i, slot in slots])
+        for frame in range(count)
+    ]
+    strips = early(drives, entry, start)
+    for frame, cells in enumerate(zip(tile, first, beside, strips)):
+        give_ref[frame, :cols] = cells[0].astype(give_ref.dtype)
+        ends = jnp.where(which < 2, cells[2], cells[3])
+        ends = jnp.where((which == 0) | (which == 2), inside(0) * ends, ends)
+        ends = jnp.where((which == 1) | (which == 5), inside(3) * ends, ends)
+        give_ref[frame, cols : 2 * cols] = ends.astype(give_ref.dtype)
+        give_ref[frame, 2 * cols :] = no_border(cells[1], 0).astype(give_ref.dtype)
+
+
+def late_kernel(parts, rounds, *refs):
+    beside_ref, strips_ref, strip_start_ref, pole_ref, scale_ref, *refs = refs
+    *late_refs, beside_out_ref, strips_out_ref = refs
+    count, room, wide = beside_ref.shape
+    rows = room // 2
+    size = late_refs[0].shape[0] - 4 * rows
+    cols = size // rows
+    early, late = (Mix(lanes, count, pole_ref, scale_ref) for lanes in parts)
+
+    def column(cells, index):
+        return cells[index * rows : (index + 1) * rows]
+
+    starts = [strip_start_ref[slot * rows : (slot + 1) * rows, parts[1]] for slot in (0, 3)]
+    entry = late.entry(late_refs, slice(size, size + 2 * rows))
+    drives = [beside_ref[frame] for frame in range(count)]
+    beside = late(drives, entry, jnp.concatenate(starts, axis=0))
+    grid = early.entry(late_refs, slice(0, size)).reshape(rows, cols, wide)
+    sides = early.entry(late_refs, slice(size + 2 * rows, size + 4 * rows))
+    entry = [sides[:rows], grid[:, 1, :], grid[:, cols - 2, :], sides[rows:]]
+    drives = [strips_ref[frame] for frame in range(count)]
+    strips = early(drives, jnp.concatenate(entry, axis=0), strip_start_ref[:, parts[0]])
+    for frame, (sides, strip) in enumerate(zip(beside, strips)):
+        sides = [column(sides, 0) * inside(0), column(sides, 1) * inside(3)]
+        strip = [column(strip, slot) * inside(slot) for slot in range(4)]
+        beside_out_ref[frame] = jnp.concatenate(sides, axis=0).astype(beside_out_ref.dtype)
+        strips_out_ref[frame] = jnp.concatenate(strip, axis=0).astype(strips_out_ref.dtype)
 
 
 def put_columns_taps(lhs_ref, slots, columns, ends):
@@ -450,12 +539,19 @@
     return total
 
 
-def opening_kernel(inputs, lanes, _, got_ref, weight_ref, out_ref, lhs_ref):
-    count, rows, cols, _ = out_ref.shape
-    size = rows * cols
-    for frame in range(count):
-        put_row(lhs_ref, frame * size, size, got_ref[frame])
-    further_kernel(inputs, lanes, lhs_ref, weight_ref, out_ref)
+def row_sum(tile, inputs, lanes, given, weight_ref):
+    count, rows, cols, wide = tile
+    tap = jnp.where(lax.axis_index("sx") == 0, weight_ref.shape[0] - 1, 0)
+    col = lax.broadcasted_iota(jnp.int32, (count, cols, wide), 1)
+
+    def product(column):
+        weight = weight_ref[pl.ds(tap, 1), column, inputs, lanes].reshape(given.shape[1], wide)
+        total = jnp.dot(given, weight, preferred_element_type=jnp.float32)
+        return total.reshape(count, cols, wide)
+
+    total = product(1)
+    total += jnp.where(col == 0, 0.0, pltpu.roll(product(0), 1, 1))
+    return total + jnp.where(col == cols - 1, 0.0, pltpu.roll(product(2), cols - 1, 1))
 
 
 def further_kernel(inputs, lanes, lhs_ref, weight_ref, out_ref):
@@ -474,7 +570,7 @@
     for frame in range(count):
         at = frame * stride
         put_row(lhs_ref, at + rows, size, got_ref[frame, :cols])
-        ends = got_ref[frame, cols:]
+        ends = got_ref[frame, cols : 2 * cols]
         put_columns_taps(lhs_ref, (at, at + rows + size), beside_ref[frame], ends)
         slots = [slot * room + frame * rows for slot in range(4)]
         put_columns_taps(strip_lhs_ref, slots, strips_ref[frame], ends.astype(jnp.float32)[2:])
@@ -483,12 +579,16 @@
         here = (frame, slice(None), slice(None), parts[part])
         return pltpu.make_async_copy(held_ref.at[here], out_ref.at[here], sems.at[frame, part])
 
+    given = jnp.concatenate([got_ref[frame, 2 * cols :] for frame in range(count)], axis=0)
     for part, lanes in enumerate(parts):
         tile = (count, rows, cols, lanes.stop - lanes.start)
+        row = lax.broadcasted_iota(jnp.int32, tile[1:], 0)
+        reached = row_sum(tile, parts[0], lanes, given, weight_ref)
         strips = strip_sum(tile, parts[0], lanes, strip_lhs_ref, weight_ref)
         tiles = tile_sum(tile, parts[1], lanes, rows, lhs_ref, weight_ref)
         for frame, total in enumerate(tiles):
             total += before_refs[part][frame] + strips[frame]
+            total += jnp.where(row == inner_row(rows), reached[frame][None], 0.0)
             held_ref[frame, :, :, lanes] = total.astype(held_ref.dtype)
             store(frame, part).start()
     for part in range(len(parts)):
@@ -555,7 +655,7 @@
             inner,
             of((count, 2 * rows, half), jnp.float32),
             of((count, 4 * rows, half), jnp.float32),
-            of((size + 6 * rows, half), narrow),
+            of((size + 4 * rows, half), narrow),
         ),
         halo,
         input_weight,
@@ -565,51 +665,38 @@
         flops=36 * room * channels * channels,
     )
     at = size + 2 * rows
+    tile = slice(0, size)
     pieces = [
-        (early, [(slice(0, size), parts[0])]),
-        (late, [(slice(0, at), parts[1]), (slice(at, at + 4 * rows), parts[0])]),
+        (early, [(tile, parts[0], (parts[1], (0, cols - 1)))]),
+        (
+            late,
+            [
+                (tile, parts[1], (parts[0], (1, cols - 2))),
+                (slice(size, at), parts[1], None),
+                (slice(at, at + 2 * rows), parts[0], None),
+            ],
+        ),
     ]
-    exchanged = (exchange_four if lax.axis_size("tm") == 4 else exchange)(pieces, pole, count)
-    early, late = exchanged
+    exchanged = exchange_four if lax.axis_size("tm") == 4 else exchange
+    early, late = exchanged(pieces, pole, count, cols)
+    rounds = len(early)
 
     mixing = (start_state, pole, scale)
-    give = call(
-        functools.partial(middle_kernel, parts[0]),
-        of((count, cols, half), narrow),
-        total,
-        *mixing,
-        *early,
-    )
     taps = of((count * size, 3 * half), narrow)
-    lhs = call(
-        functools.partial(mixed_kernel, parts[0], True), taps, total, *mixing, *early
-    )
+    lhs = call(functools.partial(mixed_kernel, parts[0], rounds), taps, total, *mixing, *early)
     strip_start = call(strip_start_kernel, of((4 * rows, channels), jnp.float32), start_state, sides)
     flops = 18 * inner.size * half
-    first_sum, lhs = call(
-        functools.partial(opening_kernel, parts[0], parts[0]),
-        (inner, taps),
-        lhs,
-        swap_cores(give),
-        output_weight,
-        aliases={0: 1},
-        flops=flops,
-    )
-    second_sum = call(
-        functools.partial(further_kernel, parts[0], parts[1]),
-        inner,
-        lhs,
-        output_weight,
-        flops=flops,
+    first_sum, second_sum = (
+        call(
+            functools.partial(further_kernel, parts[0], lanes), inner, lhs, output_weight, flops=flops
+        )
+        for lanes in parts
     )
     *late, first_sum, second_sum = lax.optimization_barrier((*late, first_sum, second_sum))
-    give, beside, strips = call(
-        functools.partial(late_kernel, parts),
-        (
-            of((count, 2 * cols, half), narrow),
-            of(beside.shape, narrow),
-            of(strips.shape, narrow),
-        ),
+    give = call(
+        functools.partial(give_kernel, parts, rounds),
+        of((count, 3 * cols, half), narrow),
+        total,
         drive,
         beside,
         strips,
@@ -617,10 +704,23 @@
         strip_start,
         pole,
         scale,
+        *early,
         *late,
     )
+    beside, strips = call(
+        functools.partial(late_kernel, parts, rounds),
+        (of(beside.shape, narrow), of(strips.shape, narrow)),
+        beside,
+        strips,
+        strip_start,
+        pole,
+        scale,
+        *late,
+    )
     taps = of((count * size + 2 * room, 3 * half), narrow)
-    lhs = call(functools.partial(mixed_kernel, parts[1], False), taps, drive, *mixing, *late)
+    lhs = call(
+        functools.partial(mixed_kernel, parts[1], rounds), taps, drive, *mixing, *early, *late
+    )
     result, _ = call(
         functools.partial(result_kernel, parts),
         (of(frames.shape, narrow), taps),

time: 40.5 us -> 40.6 us (level)
  Pallas kernels: 16 us -> 17 us
  starting transfers between devices: 13.1 us -> 12.5 us
    pallas_call x16, Pallas kernels: 16 us -> 17 us  [call(): pl.pallas_call(kernel, in_specs=[WHOLE] * len(args), out_specs=out_specs...]
    ppermute x2, waiting for transfers between devices: 1.65 us -> 2.43 us  [exchange_four(): arrivals.append((got, lax.ppermute(relayed, axes, second_round)))]
    ppermute x4 -> x3, starting transfers between devices: 3.93 us -> 3.35 us  [swap_cores(): return lax.ppermute(array, 'sx', [(0, 1), (1, 0)])]
    ppermute x4 -> x3, waiting for transfers between devices: 1.22 us -> 0.87 us  [swap_cores(): return lax.ppermute(array, 'sx', [(0, 1), (1, 0)])]
  transfers between devices with their start and end apart: 9 -> 8, of which waited for: 7 -> 6; matrix products, arithmetic and copies ran while one was open for 0% -> 0% of each run, Pallas kernels for 27% -> 29%
where the time goes in v14:
time: 40.6 us; the launch traced here: 40.1 us
  Pallas kernels  17 us (42%)
  starting transfers between devices  12.5 us (31%)
  waiting for transfers between devices  8.84 us (22%)
  local copies, waits for them, and re-layouts  1.36 us (3%)
  between operations  0.41 us (1%)
    pallas_call x16, Pallas kernels, call(): pl.pallas_call(kernel, in_specs=[WHOLE] * len(args), out_specs=out_specs...  17 us
    ppermute x2, waiting for transfers between devices, exchange_four(): got = lax.ppermute(end, axes, first_round)  4.82 us
    ppermute x2, starting transfers between devices, exchange_four(): arrivals.append((got, lax.ppermute(relayed, axes, second_round)))  4.07 us
    ppermute x3, starting transfers between devices, swap_cores(): return lax.ppermute(array, 'sx', [(0, 1), (1, 0)])  3.35 us
    ppermute x2, starting transfers between devices, exchange_four(): got = lax.ppermute(end, axes, first_round)  2.7 us
    ppermute x2, waiting for transfers between devices, exchange_four(): arrivals.append((got, lax.ppermute(relayed, axes, second_round)))  2.43 us
    ppermute x1, starting transfers between devices, trade_columns(): return (got, lax.ppermute(columns, ('sx', 'sy'), pairs))  2.33 us
    unnamed x16, local copies, waits for them, and re-layouts  1.35 us
  transfers between devices with their start and end apart: 8, of which 6 were waited for; matrix products, arithmetic and copies ran while one was open for 0% of the time, Pallas kernels for 29%

profile of v14, /device:TPU:23, one launch (start us, length us, event | category | flops | bytes accessed | tf_op | source)
XLA Modules:
  0.0 40.1 jit_solution(4618319168122388285)
XLA Ops:
  0.0 0.0 copy-start
  0.0 0.0 copy-start.2
  0.0 1.3 %copy-done.2 = bf16[2,32,16,512]{3,2,1,0:T(8,128)(2,1)S(1)} copy-done((bf16[2,32,16,512]{3,2,1,0:T(8,128)(2,1)S(1)}, bf16[2,32,16,512]{3,2,1,0:T(8,128)(2,1)}, u32[]{:S(2)}) %copy-start.2) | copy-done | bytes 1048600
  1.3 0.0 copy-start.3
  1.3 0.3 shard_map.64
  1.7 0.0 copy-done
  1.7 0.0 copy-start.1
  1.7 0.0 copy-start.4
  1.7 0.3 shard_map.65
  2.0 0.7 %collective-permute-start = (bf16[192,512]{1,0:T(8,128)(2,1)S(1)}, bf16[192,512]{1,0:T(8,128)(2,1)S(1)}, u32[]{:S(2)}, u32[]{:S(2)}) collective-permute-start(bf16[192,512]{1,0:T(8,128)(2,1)S(1)} %get-tuple-element.31), channel_id=1, source_target_pairs={{0,4},{4,0},{1,5},{5,1},{2,6},{6,2},{3,7},{7,3},{8,12},{12,8},{9,1... | collective-permute-start | bytes 589832 | tf_op jit(solution)/shard_map/ppermute | solution.py:51
  2.7 0.0 copy-done.3
  2.7 0.2 shard_map.66._
  2.9 0.9 %collective-permute-done.got_ref = bf16[192,512]{1,0:T(8,128)(2,1)S(1)} collective-permute-done((bf16[192,512]{1,0:T(8,128)(2,1)S(1)}, bf16[192,512]{1,0:T(8,128)(2,1)S(1)}, u32[]{:S(2)}, u32[]{:S(2)}) %collective-permute-start) | collective-permute-done | bytes 196640 | tf_op jit(solution)/shard_map/ppermute | solution.py:51
  3.8 2.3 %collective-permute-start.1 = (bf16[5,64,512]{2,1,0:T(8,128)(2,1)S(1)}, bf16[5,64,512]{2,1,0:T(8,128)(2,1)S(1)}, u32[]{:S(2)}, u32[]{:S(2)}) collective-permute-start(bf16[5,64,512]{2,1,0:T(8,128)(2,1)S(1)} %pad_maximum_fusion), channel_id=1, source_target_pairs={{0,5},{1,6},{2,7},{5,0},{6,1},{7,2},{8,13},{9,14},{10,15},{13,8},{... | collective-permute-start | bytes 983048 | tf_op jit(solution)/shard_map/ppermute | solution.py:95
  6.2 0.0 copy-done.1
  6.2 0.0 copy-done.4
  6.2 5.3 %shard_map.67 = (f32[2,32,16,512]{3,2,1,0:T(8,128)S(1)}, f32[2,64,512]{2,1,0:T(8,128)S(1)}, bf16[512,256]{1,0:T(8,128)(2,1)S(1)}, bf16[1024,1536]{1,0:T(8,128)(2,1)S(1)}) custom-call(bf16[1024,1536]{1,0:T(8,128)(2,1)S(1)} %shard_map.66._, bf16[192,512]{1,0:T(8,128)(2,1)S(1)} %collective-permute-done.got_ref, ...), custom_call_target="tpu_custom_call", output_to_operand_aliasing={{3}: (0, {})} | custom-call | flops 4831838208 | bytes 13830144 | tf_op jit(solution)/shard_map/pallas_call | solution.py:21
  11.5 0.7 %collective-permute-done.1.mine_ref = bf16[5,64,512]{2,1,0:T(8,128)(2,1)S(1)} collective-permute-done((bf16[5,64,512]{2,1,0:T(8,128)(2,1)S(1)}, bf16[5,64,512]{2,1,0:T(8,128)(2,1)S(1)}, u32[]{:S(2)}, u32[]{:S(2)}) %collective-permute-start.1) | collective-permute-done | bytes 327712 | tf_op jit(solution)/shard_map/ppermute | solution.py:95
  12.2 0.6 %collective-permute-start.2 = (bf16[5,64,512]{2,1,0:T(8,128)(2,1)S(1)}, bf16[5,64,512]{2,1,0:T(8,128)(2,1)S(1)}, u32[]{:S(2)}, u32[]{:S(2)}) collective-permute-start(bf16[5,64,512]{2,1,0:T(8,128)(2,1)S(1)} %collective-permute-done.1.mine_ref), channel_id=1, source_target_pairs={{0,4},{4,0},{1,5},{5,1},{2,6},{6,2},{3,7},{7,3},{8,12},{12,8},{9,1... | collective-permute-start | bytes 983048 | tf_op jit(solution)/shard_map/ppermute | solution.py:51
  12.9 1.3 %collective-permute-start.3 = (bf16[512,256]{1,0:T(8,128)(2,1)S(1)}, bf16[512,256]{1,0:T(8,128)(2,1)S(1)}, u32[]{:S(2)}, u32[]{:S(2)}) collective-permute-start(bf16[512,256]{1,0:T(8,128)(2,1)S(1)} %get-tuple-element.39.end_ref), channel_id=1, source_target_pairs={{0,8},{8,0},{16,24},{4,20},{12,28},{1,9},{9,1},{17,25},{5,21},{13,... | collective-permute-start | bytes 786440 | tf_op jit(solution)/shard_map/ppermute | solution.py:316
  14.1 0.0 collective-permute-done.2.theirs_ref
  14.1 0.2 shard_map.68
  14.3 0.0 slice-start
  14.3 0.0 copy-start.5
  14.4 0.0 slice-start.1
  14.4 1.0 %shard_map.69 = (f32[2,32,16,256]{3,2,1,0:T(8,128)S(1)}, f32[2,64,256]{2,1,0:T(8,128)S(1)}, f32[2,128,256]{2,1,0:T(8,128)S(1)}, bf16[640,256]{1,0:T(8,128)(2,1)S(1)}) custom-call(bf16[256,1536]{1,0:T(8,128)(2,1)S(1)} %get-tuple-element.35.lhs_ref, bf16[3,3,512,512]{3,2,1,0:T(8,128)(2,1)S(1)} %copy-done.1, ...), custom_call_target="tpu_custom_call" | custom-call | flops 603979776 | bytes 9635840 | tf_op jit(solution)/shard_map/pallas_call | solution.py:21
  15.4 1.4 %collective-permute-start.5 = (bf16[640,256]{1,0:T(8,128)(2,1)S(1)}, bf16[640,256]{1,0:T(8,128)(2,1)S(1)}, u32[]{:S(2)}, u32[]{:S(2)}) collective-permute-start(bf16[640,256]{1,0:T(8,128)(2,1)S(1)} %get-tuple-element.40.end_ref), channel_id=1, source_target_pairs={{0,8},{8,0},{16,24},{4,20},{12,28},{1,9},{9,1},{17,25},{5,21},{13,... | collective-permute-start | bytes 983048 | tf_op jit(solution)/shard_map/ppermute | solution.py:316
  16.8 3.4 %collective-permute-done.3.got_ref.refs_4_.refs_8_ = bf16[512,256]{1,0:T(8,128)(2,1)S(1)} collective-permute-done((bf16[512,256]{1,0:T(8,128)(2,1)S(1)}, bf16[512,256]{1,0:T(8,128)(2,1)S(1)}, u32[]{:S(2)}, u32[]{:S(2)}) %collective-permute-start.3) | collective-permute-done | bytes 262176 | tf_op jit(solution)/shard_map/ppermute | solution.py:316
  20.3 0.2 shard_map.70
  20.4 1.9 %collective-permute-start.4 = (bf16[512,256]{1,0:T(8,128)(2,1)S(1)}, bf16[512,256]{1,0:T(8,128)(2,1)S(1)}, u32[]{:S(2)}, u32[]{:S(2)}) collective-permute-start(bf16[512,256]{1,0:T(8,128)(2,1)S(1)} %shard_map.70), channel_id=1, source_target_pairs={{0,16},{8,24},{4,12},{20,28},{28,20},{1,17},{9,25},{5,13},{21,29},... | collective-permute-start | bytes 786440 | tf_op jit(solution)/shard_map/ppermute | solution.py:319
  22.4 1.4 %collective-permute-done.5.got_ref.refs_6_.refs_10_.refs_5_ = bf16[640,256]{1,0:T(8,128)(2,1)S(1)} collective-permute-done((bf16[640,256]{1,0:T(8,128)(2,1)S(1)}, bf16[640,256]{1,0:T(8,128)(2,1)S(1)}, u32[]{:S(2)}, u32[]{:S(2)}) %collective-permute-start.5) | collective-permute-done | bytes 327712 | tf_op jit(solution)/shard_map/ppermute | solution.py:316
  23.8 0.2 shard_map.71
  24.0 2.1 %collective-permute-start.6 = (bf16[640,256]{1,0:T(8,128)(2,1)S(1)}, bf16[640,256]{1,0:T(8,128)(2,1)S(1)}, u32[]{:S(2)}, u32[]{:S(2)}) collective-permute-start(bf16[640,256]{1,0:T(8,128)(2,1)S(1)} %shard_map.71), channel_id=1, source_target_pairs={{0,16},{8,24},{4,12},{20,28},{28,20},{1,17},{9,25},{5,13},{21,29},... | collective-permute-start | bytes 983048 | tf_op jit(solution)/shard_map/ppermute | solution.py:319
  26.1 1.7 %collective-permute-done.4.refs_5_.refs_9_ = bf16[512,256]{1,0:T(8,128)(2,1)S(1)} collective-permute-done((bf16[512,256]{1,0:T(8,128)(2,1)S(1)}, bf16[512,256]{1,0:T(8,128)(2,1)S(1)}, u32[]{:S(2)}, u32[]{:S(2)}) %collective-permute-start.4) | collective-permute-done | bytes 262176 | tf_op jit(solution)/shard_map/ppermute | solution.py:319
  27.8 0.0 copy-done.5
  27.8 0.6 %shard_map.72.lhs_ref = bf16[1024,768]{1,0:T(8,128)(2,1)S(1)} custom-call(f32[2,32,16,512]{3,2,1,0:T(8,128)S(1)} %get-tuple-element.36.total_ref.refs_0_, f32[32,16,512]{2,1,0:T(8,128)S(1)} %copy-done, s32[1,512]{1,0:T(1,128)S(1)} %bitcast.9, f32[1,512]{1,0:T(1,128)S(1)} %bitcast.13, bf16[512,256]{1,0:T(8,128)(2,1)S(1)} %collective-permute-done.3.got_ref.refs_4_.refs_8_, ...), custom_call_target="tpu_custom_call" | custom-call | bytes 5246976 | tf_op jit(solution)/shard_map/pallas_call | solution.py:21
  28.5 0.0 slice-done
  28.5 0.0 slice-done.1
  28.5 1.4 %shard_map.73.refs_0_ = f32[2,32,16,256]{3,2,1,0:T(8,128)S(1)} custom-call(bf16[1024,768]{1,0:T(8,128)(2,1)S(1)} %shard_map.72.lhs_ref, bf16[3,3,512,512]{3,2,1,0:T(8,128)(2,1)S(1)} %bitcast.4), custom_call_target="tpu_custom_call" | custom-call | flops 1207959552 | bytes 7340032 | tf_op jit(solution)/shard_map/pallas_call | solution.py:21
  29.9 1.4 %shard_map.74.refs_1_ = f32[2,32,16,256]{3,2,1,0:T(8,128)S(1)} custom-call(bf16[1024,768]{1,0:T(8,128)(2,1)S(1)} %shard_map.72.lhs_ref, bf16[3,3,512,512]{3,2,1,0:T(8,128)(2,1)S(1)} %bitcast.4), custom_call_target="tpu_custom_call" | custom-call | flops 1207959552 | bytes 7340032 | tf_op jit(solution)/shard_map/pallas_call | solution.py:21
  31.3 0.1 shard_map.76.refs_5_.refs_2_
  31.4 0.7 %collective-permute-done.6.refs_7_.refs_11_.refs_6_ = bf16[640,256]{1,0:T(8,128)(2,1)S(1)} collective-permute-done((bf16[640,256]{1,0:T(8,128)(2,1)S(1)}, bf16[640,256]{1,0:T(8,128)(2,1)S(1)}, u32[]{:S(2)}, u32[]{:S(2)}) %collective-permute-start.6) | collective-permute-done | bytes 327712 | tf_op jit(solution)/shard_map/ppermute | solution.py:319
  32.1 0.1 shard_map.77
  32.2 2.0 %collective-permute-start.7 = (bf16[2,48,256]{2,1,0:T(8,128)(2,1)S(1)}, bf16[2,48,256]{2,1,0:T(8,128)(2,1)S(1)}, u32[]{:S(2)}, u32[]{:S(2)}) collective-permute-start(bf16[2,48,256]{2,1,0:T(8,128)(2,1)S(1)} %shard_map.77), channel_id=1, source_target_pairs={{0,4},{4,0},{1,5},{5,1},{2,6},{6,2},{3,7},{7,3},{8,12},{12,8},{9,1... | collective-permute-start | bytes 147464 | tf_op jit(solution)/shard_map/ppermute | solution.py:51
  34.2 0.4 shard_map.78
  34.6 0.7 %shard_map.75._ = bf16[1152,768]{1,0:T(8,128)(2,1)S(1)} custom-call(f32[2,32,16,256]{3,2,1,0:T(8,128)S(1)} %get-tuple-element.38.refs_0_.refs_1_, f32[32,16,512]{2,1,0:T(8,128)S(1)} %copy-done, s32[1,512]{1,0:T(1,128)S(1)} %bitcast.12, f32[1,512]{1,0:T(1,128)S(1)} %bitcast.16, bf16[512,256]{1,0:T(8,128)(2,1)S(1)} %collective-permute-done.3.got_ref.refs_4_.refs_8_, ...), custom_call_target="tpu_custom_call" | custom-call | bytes 5050368 | tf_op jit(solution)/shard_map/pallas_call | solution.py:21
  35.3 0.0 collective-permute-done.7.got_ref
  35.3 4.7 %shard_map.79 = (bf16[2,32,16,512]{3,2,1,0:T(8,128)(2,1)}, bf16[1152,768]{1,0:T(8,128)(2,1)S(1)}) custom-call(bf16[1152,768]{1,0:T(8,128)(2,1)S(1)} %shard_map.75._, bf16[2,48,256]{2,1,0:T(8,128)(2,1)S(1)} %collective-permute-done.7.got_ref, bf16[2,64,256]{2,1,0:T(8,128)(2,1)S(1)} %get-tuple-element.46.beside_ref, ...), custom_call_target="tpu_custom_call", output_to_operand_aliasing={{1}: (0, {})} | custom-call | flops 2415919104 | bytes 11649024 | tf_op jit(solution)/shard_map/pallas_call | solution.py:21
  (3 shorter events, 0.0 us)
Async XLA Ops:
  0.0 1.7 %copy-start = (f32[32,16,512]{2,1,0:T(8,128)S(1)}, f32[32,16,512]{2,1,0:T(8,128)}, u32[]{:S(2)}) copy-start(f32[32,16,512]{2,1,0:T(8,128)} %refs_4_.1) | copy-start | bytes 3145732
  0.0 1.3 %copy-start.2 = (bf16[2,32,16,512]{3,2,1,0:T(8,128)(2,1)S(1)}, bf16[2,32,16,512]{3,2,1,0:T(8,128)(2,1)}, u32[]{:S(2)}) copy-start(bf16[2,32,16,512]{3,2,1,0:T(8,128)(2,1)} %cells_ref.3) | copy-start | bytes 3145732
  1.3 1.4 %copy-start.3 = (bf16[2,32,16,512]{3,2,1,0:T(8,128)(2,1)S(1)}, bf16[2,32,16,512]{3,2,1,0:T(8,128)(2,1)}, u32[]{:S(2)}) copy-start(bf16[2,32,16,512]{3,2,1,0:T(8,128)(2,1)} %cells_ref.3) | copy-start | bytes 3145732
  1.7 4.5 %copy-start.1 = (bf16[3,3,512,512]{3,2,1,0:T(8,128)(2,1)S(1)}, bf16[3,3,512,512]{3,2,1,0:T(8,128)(2,1)}, u32[]{:S(2)}) copy-start(bf16[3,3,512,512]{3,2,1,0:T(8,128)(2,1)} %weight_ref.6) | copy-start | bytes 14155780
  1.7 4.5 %copy-start.4 = (s32[512]{0:T(512)S(1)}, s32[512]{0:T(512)}, u32[]{:S(2)}) copy-start(s32[512]{0:T(512)} %param.9) | copy-start | bytes 6148
  2.0 1.8 %collective-permute-start = (bf16[192,512]{1,0:T(8,128)(2,1)S(1)}, bf16[192,512]{1,0:T(8,128)(2,1)S(1)}, u32[]{:S(2)}, u32[]{:S(2)}) collective-permute-start(bf16[192,512]{1,0:T(8,128)(2,1)S(1)} %get-tuple-element.31), channel_id=1, source_target_pairs={{0,4},{4,0},{1,5},{5,1},{2,6},{6,2},{3,7},{7,3},{8,12},{12,8},{9,1... | collective-permute-start | bytes 589832 | tf_op jit(solution)/shard_map/ppermute | solution.py:51
  3.8 8.4 %collective-permute-start.1 = (bf16[5,64,512]{2,1,0:T(8,128)(2,1)S(1)}, bf16[5,64,512]{2,1,0:T(8,128)(2,1)S(1)}, u32[]{:S(2)}, u32[]{:S(2)}) collective-permute-start(bf16[5,64,512]{2,1,0:T(8,128)(2,1)S(1)} %pad_maximum_fusion), channel_id=1, source_target_pairs={{0,5},{1,6},{2,7},{5,0},{6,1},{7,2},{8,13},{9,14},{10,15},{13,8},{... | collective-permute-start | bytes 983048 | tf_op jit(solution)/shard_map/ppermute | solution.py:95
  12.2 1.9 %collective-permute-start.2 = (bf16[5,64,512]{2,1,0:T(8,128)(2,1)S(1)}, bf16[5,64,512]{2,1,0:T(8,128)(2,1)S(1)}, u32[]{:S(2)}, u32[]{:S(2)}) collective-permute-start(bf16[5,64,512]{2,1,0:T(8,128)(2,1)S(1)} %collective-permute-done.1.mine_ref), channel_id=1, source_target_pairs={{0,4},{4,0},{1,5},{5,1},{2,6},{6,2},{3,7},{7,3},{8,12},{12,8},{9,1... | collective-permute-start | bytes 983048 | tf_op jit(solution)/shard_map/ppermute | solution.py:51
  12.9 7.4 %collective-permute-start.3 = (bf16[512,256]{1,0:T(8,128)(2,1)S(1)}, bf16[512,256]{1,0:T(8,128)(2,1)S(1)}, u32[]{:S(2)}, u32[]{:S(2)}) collective-permute-start(bf16[512,256]{1,0:T(8,128)(2,1)S(1)} %get-tuple-element.39.end_ref), channel_id=1, source_target_pairs={{0,8},{8,0},{16,24},{4,20},{12,28},{1,9},{9,1},{17,25},{5,21},{13,... | collective-permute-start | bytes 786440 | tf_op jit(solution)/shard_map/ppermute | solution.py:316
  14.3 14.1 %slice-start = ((s8[4718592]{0:T(1024)(128)(4,1)}), s8[4194304]{0:T(1024)(128)(4,1)S(1)}, s32[]{:S(2)}) async-start(s8[4718592]{0:T(1024)(128)(4,1)} %bitcast.3), calls=%async_computation | async-start | bytes 8388608
  14.3 13.5 %copy-start.5 = (f32[512]{0:T(512)S(1)}, f32[512]{0:T(512)}, u32[]{:S(2)}) copy-start(f32[512]{0:T(512)} %param.10) | copy-start | bytes 6148
  14.4 14.1 %slice-start.1 = ((s8[4718592]{0:T(1024)(128)(4,1)}), s8[524288]{0:T(1024)(128)(4,1)S(1)}, s32[]{:S(2)}) async-start(s8[4718592]{0:T(1024)(128)(4,1)} %bitcast.3), calls=%async_computation.1 | async-start | bytes 1048576
  15.4 8.4 %collective-permute-start.5 = (bf16[640,256]{1,0:T(8,128)(2,1)S(1)}, bf16[640,256]{1,0:T(8,128)(2,1)S(1)}, u32[]{:S(2)}, u32[]{:S(2)}) collective-permute-start(bf16[640,256]{1,0:T(8,128)(2,1)S(1)} %get-tuple-element.40.end_ref), channel_id=1, source_target_pairs={{0,8},{8,0},{16,24},{4,20},{12,28},{1,9},{9,1},{17,25},{5,21},{13,... | collective-permute-start | bytes 983048 | tf_op jit(solution)/shard_map/ppermute | solution.py:316
  20.4 7.4 %collective-permute-start.4 = (bf16[512,256]{1,0:T(8,128)(2,1)S(1)}, bf16[512,256]{1,0:T(8,128)(2,1)S(1)}, u32[]{:S(2)}, u32[]{:S(2)}) collective-permute-start(bf16[512,256]{1,0:T(8,128)(2,1)S(1)} %shard_map.70), channel_id=1, source_target_pairs={{0,16},{8,24},{4,12},{20,28},{28,20},{1,17},{9,25},{5,13},{21,29},... | collective-permute-start | bytes 786440 | tf_op jit(solution)/shard_map/ppermute | solution.py:319
  24.0 8.1 %collective-permute-start.6 = (bf16[640,256]{1,0:T(8,128)(2,1)S(1)}, bf16[640,256]{1,0:T(8,128)(2,1)S(1)}, u32[]{:S(2)}, u32[]{:S(2)}) collective-permute-start(bf16[640,256]{1,0:T(8,128)(2,1)S(1)} %shard_map.71), channel_id=1, source_target_pairs={{0,16},{8,24},{4,12},{20,28},{28,20},{1,17},{9,25},{5,13},{21,29},... | collective-permute-start | bytes 983048 | tf_op jit(solution)/shard_map/ppermute | solution.py:319
  32.2 3.1 %collective-permute-start.7 = (bf16[2,48,256]{2,1,0:T(8,128)(2,1)S(1)}, bf16[2,48,256]{2,1,0:T(8,128)(2,1)S(1)}, u32[]{:S(2)}, u32[]{:S(2)}) collective-permute-start(bf16[2,48,256]{2,1,0:T(8,128)(2,1)S(1)} %shard_map.77), channel_id=1, source_target_pairs={{0,4},{4,0},{1,5},{5,1},{2,6},{6,2},{3,7},{7,3},{8,12},{12,8},{9,1... | collective-permute-start | bytes 147464 | tf_op jit(solution)/shard_map/ppermute | solution.py:51

commit v15 on v14

--- a/solution.py
+++ b/solution.py
@@ -521,37 +521,38 @@
         yield total + jnp.where(col == cols - 1, beside(last[size:]), shifted)
 
 
+def strip_slots(count, rows, cols):
+    room, given = count * rows, count * cols
+    strips = [given, given + room, 2 * given + 2 * room, 2 * given + 3 * room]
+    return strips, [0, given + 2 * room, 2 * given + 4 * room]
+
+
 def strip_sum(tile, inputs, lanes, lhs_ref, weight_ref):
     count, rows, cols, wide = tile
-    room = count * rows
+    room, given = count * rows, count * cols
+    strips, _ = strip_slots(count, rows, cols)
+    first = dot(lhs_ref[: strips[1] + room], weight_ref, 0, lanes, inputs)
+    middle = dot(lhs_ref[strips[1] : strips[2] + room], weight_ref, 1, lanes, inputs)
+    last = dot(lhs_ref[strips[2] :], weight_ref, 2, lanes, inputs)
+    col = lax.broadcasted_iota(jnp.int32, (count, cols, wide), 1)
+
+    def row_of(cells):
+        return cells.reshape(count, cols, wide)
+
+    reached = row_of(middle[room : room + given])
+    reached += jnp.where(col == 0, 0.0, pltpu.roll(row_of(first[:given]), 1, 1))
+    reached += jnp.where(col == cols - 1, 0.0, pltpu.roll(row_of(last[2 * room :]), cols - 1, 1))
+    row = lax.broadcasted_iota(jnp.int32, tile, 1)
     col = lax.broadcasted_iota(jnp.int32, tile, 2)
-    first = dot(lhs_ref[: 2 * room], weight_ref, 0, lanes, inputs)
-    middle = dot(lhs_ref[room : 3 * room], weight_ref, 1, lanes, inputs)
-    last = dot(lhs_ref[2 * room :], weight_ref, 2, lanes, inputs)
-    total = 0.0
+    total = jnp.where(row == inner_row(rows), reached.reshape(count, 1, cols, wide), 0.0)
     for at, cells in (
-        (0, first[:room] + middle[:room]),
-        (1, first[room:]),
+        (0, first[given : given + room] + middle[:room]),
+        (1, first[given + room :]),
         (cols - 2, last[:room]),
-        (cols - 1, middle[room:] + last[room:]),
+        (cols - 1, middle[room + given :] + last[room : 2 * room]),
     ):
-        total = jnp.where(col == at, cells.reshape(count, rows, 1, wide), total)
+        total += jnp.where(col == at, cells.reshape(count, rows, 1, wide), 0.0)
     return total
-
-
-def row_sum(tile, inputs, lanes, given, weight_ref):
-    count, rows, cols, wide = tile
-    tap = jnp.where(lax.axis_index("sx") == 0, weight_ref.shape[0] - 1, 0)
-    col = lax.broadcasted_iota(jnp.int32, (count, cols, wide), 1)
-
-    def product(column):
-        weight = weight_ref[pl.ds(tap, 1), column, inputs, lanes].reshape(given.shape[1], wide)
-        total = jnp.dot(given, weight, preferred_element_type=jnp.float32)
-        return total.reshape(count, cols, wide)
-
-    total = product(1)
-    total += jnp.where(col == 0, 0.0, pltpu.roll(product(0), 1, 1))
-    return total + jnp.where(col == cols - 1, 0.0, pltpu.roll(product(2), cols - 1, 1))
 
 
 def further_kernel(inputs, lanes, lhs_ref, weight_ref, out_ref):
@@ -565,30 +566,32 @@
 ):
     *before_refs, out_ref, lhs_ref, held_ref, strip_lhs_ref, sems = refs
     count, rows, cols, _ = held_ref.shape
-    size, room = rows * cols, count * rows
+    size = rows * cols
     stride = size + 2 * rows
+    strips_at, given_at = strip_slots(count, rows, cols)
     for frame in range(count):
         at = frame * stride
         put_row(lhs_ref, at + rows, size, got_ref[frame, :cols])
         ends = got_ref[frame, cols : 2 * cols]
         put_columns_taps(lhs_ref, (at, at + rows + size), beside_ref[frame], ends)
-        slots = [slot * room + frame * rows for slot in range(4)]
+        slots = [slot + frame * rows for slot in strips_at]
         put_columns_taps(strip_lhs_ref, slots, strips_ref[frame], ends.astype(jnp.float32)[2:])
+        given = got_ref[frame, 2 * cols :].astype(jnp.float32)
+        given = [is_core(1) * given, jnp.zeros_like(given), is_core(0) * given]
+        given = jnp.concatenate(given, axis=1).astype(strip_lhs_ref.dtype)
+        for at in given_at:
+            strip_lhs_ref[at + frame * cols : at + (frame + 1) * cols] = given
 
     def store(frame, part):
         here = (frame, slice(None), slice(None), parts[part])
         return pltpu.make_async_copy(held_ref.at[here], out_ref.at[here], sems.at[frame, part])
 
-    given = jnp.concatenate([got_ref[frame, 2 * cols :] for frame in range(count)], axis=0)
     for part, lanes in enumerate(parts):
         tile = (count, rows, cols, lanes.stop - lanes.start)
-        row = lax.broadcasted_iota(jnp.int32, tile[1:], 0)
-        reached = row_sum(tile, parts[0], lanes, given, weight_ref)
         strips = strip_sum(tile, parts[0], lanes, strip_lhs_ref, weight_ref)
         tiles = tile_sum(tile, parts[1], lanes, rows, lhs_ref, weight_ref)
         for frame, total in enumerate(tiles):
             total += before_refs[part][frame] + strips[frame]
-            total += jnp.where(row == inner_row(rows), reached[frame][None], 0.0)
             held_ref[frame, :, :, lanes] = total.astype(held_ref.dtype)
             store(frame, part).start()
     for part in range(len(parts)):
@@ -735,7 +738,7 @@
         aliases={0: 1},
         scratch=[
             pltpu.VMEM(frames.shape, narrow),
-            pltpu.VMEM((4 * room, 3 * half), narrow),
+            pltpu.VMEM((4 * room + 3 * count * cols, 3 * half), narrow),
             pltpu.SemaphoreType.DMA((count, len(parts))),
         ],
         flops=2 * flops,

time: 40.6 us -> 40.7 us (level)
  no operation moved by 1% of the time
where the time goes in v15:
time: 40.7 us; the launch traced here: 40.3 us
  Pallas kernels  17.2 us (42%)
  starting transfers between devices  12.5 us (31%)
  waiting for transfers between devices  8.84 us (22%)
  local copies, waits for them, and re-layouts  1.36 us (3%)
  between operations  0.41 us (1%)
    pallas_call x16, Pallas kernels, call(): pl.pallas_call(kernel, in_specs=[WHOLE] * len(args), out_specs=out_specs...  17.2 us
    ppermute x2, waiting for transfers between devices, exchange_four(): got = lax.ppermute(end, axes, first_round)  4.82 us
    ppermute x2, starting transfers between devices, exchange_four(): arrivals.append((got, lax.ppermute(relayed, axes, second_round)))  4.07 us
    ppermute x3, starting transfers between devices, swap_cores(): return lax.ppermute(array, 'sx', [(0, 1), (1, 0)])  3.35 us
    ppermute x2, starting transfers between devices, exchange_four(): got = lax.ppermute(end, axes, first_round)  2.7 us
    ppermute x2, waiting for transfers between devices, exchange_four(): arrivals.append((got, lax.ppermute(relayed, axes, second_round)))  2.43 us
    ppermute x1, starting transfers between devices, trade_columns(): return (got, lax.ppermute(columns, ('sx', 'sy'), pairs))  2.33 us
    unnamed x16, local copies, waits for them, and re-layouts  1.35 us
  transfers between devices with their start and end apart: 8, of which 6 were waited for; matrix products, arithmetic and copies ran while one was open for 0% of the time, Pallas kernels for 29%

profile of v15, /device:TPU:23, one launch (start us, length us, event | category | flops | bytes accessed | tf_op | source)
XLA Modules:
  0.0 40.3 jit_solution(13323852399628526173)
XLA Ops:
  0.0 0.0 copy-start
  0.0 0.0 copy-start.2
  0.0 1.3 %copy-done.2 = bf16[2,32,16,512]{3,2,1,0:T(8,128)(2,1)S(1)} copy-done((bf16[2,32,16,512]{3,2,1,0:T(8,128)(2,1)S(1)}, bf16[2,32,16,512]{3,2,1,0:T(8,128)(2,1)}, u32[]{:S(2)}) %copy-start.2) | copy-done | bytes 1048600
  1.3 0.0 copy-start.3
  1.3 0.3 shard_map.64
  1.7 0.0 copy-done
  1.7 0.0 copy-start.1
  1.7 0.0 copy-start.4
  1.7 0.3 shard_map.65
  2.0 0.7 %collective-permute-start = (bf16[192,512]{1,0:T(8,128)(2,1)S(1)}, bf16[192,512]{1,0:T(8,128)(2,1)S(1)}, u32[]{:S(2)}, u32[]{:S(2)}) collective-permute-start(bf16[192,512]{1,0:T(8,128)(2,1)S(1)} %get-tuple-element.31), channel_id=1, source_target_pairs={{0,4},{4,0},{1,5},{5,1},{2,6},{6,2},{3,7},{7,3},{8,12},{12,8},{9,1... | collective-permute-start | bytes 589832 | tf_op jit(solution)/shard_map/ppermute | solution.py:51
  2.7 0.0 copy-done.3
  2.7 0.2 shard_map.66._
  2.9 0.9 %collective-permute-done.got_ref = bf16[192,512]{1,0:T(8,128)(2,1)S(1)} collective-permute-done((bf16[192,512]{1,0:T(8,128)(2,1)S(1)}, bf16[192,512]{1,0:T(8,128)(2,1)S(1)}, u32[]{:S(2)}, u32[]{:S(2)}) %collective-permute-start) | collective-permute-done | bytes 196640 | tf_op jit(solution)/shard_map/ppermute | solution.py:51
  3.8 2.3 %collective-permute-start.1 = (bf16[5,64,512]{2,1,0:T(8,128)(2,1)S(1)}, bf16[5,64,512]{2,1,0:T(8,128)(2,1)S(1)}, u32[]{:S(2)}, u32[]{:S(2)}) collective-permute-start(bf16[5,64,512]{2,1,0:T(8,128)(2,1)S(1)} %pad_maximum_fusion), channel_id=1, source_target_pairs={{0,5},{1,6},{2,7},{5,0},{6,1},{7,2},{8,13},{9,14},{10,15},{13,8},{... | collective-permute-start | bytes 983048 | tf_op jit(solution)/shard_map/ppermute | solution.py:95
  6.2 0.0 copy-done.1
  6.2 0.0 copy-done.4
  6.2 5.3 %shard_map.67 = (f32[2,32,16,512]{3,2,1,0:T(8,128)S(1)}, f32[2,64,512]{2,1,0:T(8,128)S(1)}, bf16[512,256]{1,0:T(8,128)(2,1)S(1)}, bf16[1024,1536]{1,0:T(8,128)(2,1)S(1)}) custom-call(bf16[1024,1536]{1,0:T(8,128)(2,1)S(1)} %shard_map.66._, bf16[192,512]{1,0:T(8,128)(2,1)S(1)} %collective-permute-done.got_ref, ...), custom_call_target="tpu_custom_call", output_to_operand_aliasing={{3}: (0, {})} | custom-call | flops 4831838208 | bytes 13830144 | tf_op jit(solution)/shard_map/pallas_call | solution.py:21
  11.5 0.7 %collective-permute-done.1.mine_ref = bf16[5,64,512]{2,1,0:T(8,128)(2,1)S(1)} collective-permute-done((bf16[5,64,512]{2,1,0:T(8,128)(2,1)S(1)}, bf16[5,64,512]{2,1,0:T(8,128)(2,1)S(1)}, u32[]{:S(2)}, u32[]{:S(2)}) %collective-permute-start.1) | collective-permute-done | bytes 327712 | tf_op jit(solution)/shard_map/ppermute | solution.py:95
  12.2 0.6 %collective-permute-start.2 = (bf16[5,64,512]{2,1,0:T(8,128)(2,1)S(1)}, bf16[5,64,512]{2,1,0:T(8,128)(2,1)S(1)}, u32[]{:S(2)}, u32[]{:S(2)}) collective-permute-start(bf16[5,64,512]{2,1,0:T(8,128)(2,1)S(1)} %collective-permute-done.1.mine_ref), channel_id=1, source_target_pairs={{0,4},{4,0},{1,5},{5,1},{2,6},{6,2},{3,7},{7,3},{8,12},{12,8},{9,1... | collective-permute-start | bytes 983048 | tf_op jit(solution)/shard_map/ppermute | solution.py:51
  12.9 1.3 %collective-permute-start.3 = (bf16[512,256]{1,0:T(8,128)(2,1)S(1)}, bf16[512,256]{1,0:T(8,128)(2,1)S(1)}, u32[]{:S(2)}, u32[]{:S(2)}) collective-permute-start(bf16[512,256]{1,0:T(8,128)(2,1)S(1)} %get-tuple-element.39.end_ref), channel_id=1, source_target_pairs={{0,8},{8,0},{16,24},{4,20},{12,28},{1,9},{9,1},{17,25},{5,21},{13,... | collective-permute-start | bytes 786440 | tf_op jit(solution)/shard_map/ppermute | solution.py:316
  14.1 0.0 collective-permute-done.2.theirs_ref
  14.1 0.2 shard_map.68
  14.3 0.0 slice-start
  14.3 0.0 copy-start.5
  14.4 0.0 slice-start.1
  14.4 1.0 %shard_map.69 = (f32[2,32,16,256]{3,2,1,0:T(8,128)S(1)}, f32[2,64,256]{2,1,0:T(8,128)S(1)}, f32[2,128,256]{2,1,0:T(8,128)S(1)}, bf16[640,256]{1,0:T(8,128)(2,1)S(1)}) custom-call(bf16[256,1536]{1,0:T(8,128)(2,1)S(1)} %get-tuple-element.35.lhs_ref, bf16[3,3,512,512]{3,2,1,0:T(8,128)(2,1)S(1)} %copy-done.1, ...), custom_call_target="tpu_custom_call" | custom-call | flops 603979776 | bytes 9635840 | tf_op jit(solution)/shard_map/pallas_call | solution.py:21
  15.4 1.4 %collective-permute-start.5 = (bf16[640,256]{1,0:T(8,128)(2,1)S(1)}, bf16[640,256]{1,0:T(8,128)(2,1)S(1)}, u32[]{:S(2)}, u32[]{:S(2)}) collective-permute-start(bf16[640,256]{1,0:T(8,128)(2,1)S(1)} %get-tuple-element.40.end_ref), channel_id=1, source_target_pairs={{0,8},{8,0},{16,24},{4,20},{12,28},{1,9},{9,1},{17,25},{5,21},{13,... | collective-permute-start | bytes 983048 | tf_op jit(solution)/shard_map/ppermute | solution.py:316
  16.8 3.4 %collective-permute-done.3.got_ref.refs_4_.refs_8_ = bf16[512,256]{1,0:T(8,128)(2,1)S(1)} collective-permute-done((bf16[512,256]{1,0:T(8,128)(2,1)S(1)}, bf16[512,256]{1,0:T(8,128)(2,1)S(1)}, u32[]{:S(2)}, u32[]{:S(2)}) %collective-permute-start.3) | collective-permute-done | bytes 262176 | tf_op jit(solution)/shard_map/ppermute | solution.py:316
  20.3 0.2 shard_map.70
  20.4 1.9 %collective-permute-start.4 = (bf16[512,256]{1,0:T(8,128)(2,1)S(1)}, bf16[512,256]{1,0:T(8,128)(2,1)S(1)}, u32[]{:S(2)}, u32[]{:S(2)}) collective-permute-start(bf16[512,256]{1,0:T(8,128)(2,1)S(1)} %shard_map.70), channel_id=1, source_target_pairs={{0,16},{8,24},{4,12},{20,28},{28,20},{1,17},{9,25},{5,13},{21,29},... | collective-permute-start | bytes 786440 | tf_op jit(solution)/shard_map/ppermute | solution.py:319
  22.4 1.4 %collective-permute-done.5.got_ref.refs_6_.refs_10_.refs_5_ = bf16[640,256]{1,0:T(8,128)(2,1)S(1)} collective-permute-done((bf16[640,256]{1,0:T(8,128)(2,1)S(1)}, bf16[640,256]{1,0:T(8,128)(2,1)S(1)}, u32[]{:S(2)}, u32[]{:S(2)}) %collective-permute-start.5) | collective-permute-done | bytes 327712 | tf_op jit(solution)/shard_map/ppermute | solution.py:316
  23.8 0.2 shard_map.71
  24.0 2.1 %collective-permute-start.6 = (bf16[640,256]{1,0:T(8,128)(2,1)S(1)}, bf16[640,256]{1,0:T(8,128)(2,1)S(1)}, u32[]{:S(2)}, u32[]{:S(2)}) collective-permute-start(bf16[640,256]{1,0:T(8,128)(2,1)S(1)} %shard_map.71), channel_id=1, source_target_pairs={{0,16},{8,24},{4,12},{20,28},{28,20},{1,17},{9,25},{5,13},{21,29},... | collective-permute-start | bytes 983048 | tf_op jit(solution)/shard_map/ppermute | solution.py:319
  26.1 1.7 %collective-permute-done.4.refs_5_.refs_9_ = bf16[512,256]{1,0:T(8,128)(2,1)S(1)} collective-permute-done((bf16[512,256]{1,0:T(8,128)(2,1)S(1)}, bf16[512,256]{1,0:T(8,128)(2,1)S(1)}, u32[]{:S(2)}, u32[]{:S(2)}) %collective-permute-start.4) | collective-permute-done | bytes 262176 | tf_op jit(solution)/shard_map/ppermute | solution.py:319
  27.8 0.0 copy-done.5
  27.8 0.6 %shard_map.72.lhs_ref = bf16[1024,768]{1,0:T(8,128)(2,1)S(1)} custom-call(f32[2,32,16,512]{3,2,1,0:T(8,128)S(1)} %get-tuple-element.36.total_ref.refs_0_, f32[32,16,512]{2,1,0:T(8,128)S(1)} %copy-done, s32[1,512]{1,0:T(1,128)S(1)} %bitcast.9, f32[1,512]{1,0:T(1,128)S(1)} %bitcast.13, bf16[512,256]{1,0:T(8,128)(2,1)S(1)} %collective-permute-done.3.got_ref.refs_4_.refs_8_, ...), custom_call_target="tpu_custom_call" | custom-call | bytes 5246976 | tf_op jit(solution)/shard_map/pallas_call | solution.py:21
  28.5 0.0 slice-done
  28.5 0.0 slice-done.1
  28.5 1.4 %shard_map.73.refs_0_ = f32[2,32,16,256]{3,2,1,0:T(8,128)S(1)} custom-call(bf16[1024,768]{1,0:T(8,128)(2,1)S(1)} %shard_map.72.lhs_ref, bf16[3,3,512,512]{3,2,1,0:T(8,128)(2,1)S(1)} %bitcast.4), custom_call_target="tpu_custom_call" | custom-call | flops 1207959552 | bytes 7340032 | tf_op jit(solution)/shard_map/pallas_call | solution.py:21
  29.9 1.4 %shard_map.74.refs_1_ = f32[2,32,16,256]{3,2,1,0:T(8,128)S(1)} custom-call(bf16[1024,768]{1,0:T(8,128)(2,1)S(1)} %shard_map.72.lhs_ref, bf16[3,3,512,512]{3,2,1,0:T(8,128)(2,1)S(1)} %bitcast.4), custom_call_target="tpu_custom_call" | custom-call | flops 1207959552 | bytes 7340032 | tf_op jit(solution)/shard_map/pallas_call | solution.py:21
  31.3 0.1 shard_map.76.refs_5_.refs_2_
  31.4 0.7 %collective-permute-done.6.refs_7_.refs_11_.refs_6_ = bf16[640,256]{1,0:T(8,128)(2,1)S(1)} collective-permute-done((bf16[640,256]{1,0:T(8,128)(2,1)S(1)}, bf16[640,256]{1,0:T(8,128)(2,1)S(1)}, u32[]{:S(2)}, u32[]{:S(2)}) %collective-permute-start.6) | collective-permute-done | bytes 327712 | tf_op jit(solution)/shard_map/ppermute | solution.py:319
  32.1 0.1 shard_map.77
  32.2 2.0 %collective-permute-start.7 = (bf16[2,48,256]{2,1,0:T(8,128)(2,1)S(1)}, bf16[2,48,256]{2,1,0:T(8,128)(2,1)S(1)}, u32[]{:S(2)}, u32[]{:S(2)}) collective-permute-start(bf16[2,48,256]{2,1,0:T(8,128)(2,1)S(1)} %shard_map.77), channel_id=1, source_target_pairs={{0,4},{4,0},{1,5},{5,1},{2,6},{6,2},{3,7},{7,3},{8,12},{12,8},{9,1... | collective-permute-start | bytes 147464 | tf_op jit(solution)/shard_map/ppermute | solution.py:51
  34.2 0.4 shard_map.78
  34.6 0.7 %shard_map.75._ = bf16[1152,768]{1,0:T(8,128)(2,1)S(1)} custom-call(f32[2,32,16,256]{3,2,1,0:T(8,128)S(1)} %get-tuple-element.38.refs_0_.refs_1_, f32[32,16,512]{2,1,0:T(8,128)S(1)} %copy-done, s32[1,512]{1,0:T(1,128)S(1)} %bitcast.12, f32[1,512]{1,0:T(1,128)S(1)} %bitcast.16, bf16[512,256]{1,0:T(8,128)(2,1)S(1)} %collective-permute-done.3.got_ref.refs_4_.refs_8_, ...), custom_call_target="tpu_custom_call" | custom-call | bytes 5050368 | tf_op jit(solution)/shard_map/pallas_call | solution.py:21
  35.3 0.0 collective-permute-done.7.got_ref
  35.3 4.8 %shard_map.79 = (bf16[2,32,16,512]{3,2,1,0:T(8,128)(2,1)}, bf16[1152,768]{1,0:T(8,128)(2,1)S(1)}) custom-call(bf16[1152,768]{1,0:T(8,128)(2,1)S(1)} %shard_map.75._, bf16[2,48,256]{2,1,0:T(8,128)(2,1)S(1)} %collective-permute-done.7.got_ref, bf16[2,64,256]{2,1,0:T(8,128)(2,1)S(1)} %get-tuple-element.46.beside_ref, ...), custom_call_target="tpu_custom_call", output_to_operand_aliasing={{1}: (0, {})} | custom-call | flops 2415919104 | bytes 11649024 | tf_op jit(solution)/shard_map/pallas_call | solution.py:21
  (3 shorter events, 0.0 us)
Async XLA Ops:
  0.0 1.7 %copy-start = (f32[32,16,512]{2,1,0:T(8,128)S(1)}, f32[32,16,512]{2,1,0:T(8,128)}, u32[]{:S(2)}) copy-start(f32[32,16,512]{2,1,0:T(8,128)} %refs_4_.1) | copy-start | bytes 3145732
  0.0 1.3 %copy-start.2 = (bf16[2,32,16,512]{3,2,1,0:T(8,128)(2,1)S(1)}, bf16[2,32,16,512]{3,2,1,0:T(8,128)(2,1)}, u32[]{:S(2)}) copy-start(bf16[2,32,16,512]{3,2,1,0:T(8,128)(2,1)} %cells_ref.3) | copy-start | bytes 3145732
  1.3 1.4 %copy-start.3 = (bf16[2,32,16,512]{3,2,1,0:T(8,128)(2,1)S(1)}, bf16[2,32,16,512]{3,2,1,0:T(8,128)(2,1)}, u32[]{:S(2)}) copy-start(bf16[2,32,16,512]{3,2,1,0:T(8,128)(2,1)} %cells_ref.3) | copy-start | bytes 3145732
  1.7 4.5 %copy-start.1 = (bf16[3,3,512,512]{3,2,1,0:T(8,128)(2,1)S(1)}, bf16[3,3,512,512]{3,2,1,0:T(8,128)(2,1)}, u32[]{:S(2)}) copy-start(bf16[3,3,512,512]{3,2,1,0:T(8,128)(2,1)} %weight_ref.6) | copy-start | bytes 14155780
  1.7 4.5 %copy-start.4 = (s32[512]{0:T(512)S(1)}, s32[512]{0:T(512)}, u32[]{:S(2)}) copy-start(s32[512]{0:T(512)} %param.9) | copy-start | bytes 6148
  2.0 1.8 %collective-permute-start = (bf16[192,512]{1,0:T(8,128)(2,1)S(1)}, bf16[192,512]{1,0:T(8,128)(2,1)S(1)}, u32[]{:S(2)}, u32[]{:S(2)}) collective-permute-start(bf16[192,512]{1,0:T(8,128)(2,1)S(1)} %get-tuple-element.31), channel_id=1, source_target_pairs={{0,4},{4,0},{1,5},{5,1},{2,6},{6,2},{3,7},{7,3},{8,12},{12,8},{9,1... | collective-permute-start | bytes 589832 | tf_op jit(solution)/shard_map/ppermute | solution.py:51
  3.8 8.4 %collective-permute-start.1 = (bf16[5,64,512]{2,1,0:T(8,128)(2,1)S(1)}, bf16[5,64,512]{2,1,0:T(8,128)(2,1)S(1)}, u32[]{:S(2)}, u32[]{:S(2)}) collective-permute-start(bf16[5,64,512]{2,1,0:T(8,128)(2,1)S(1)} %pad_maximum_fusion), channel_id=1, source_target_pairs={{0,5},{1,6},{2,7},{5,0},{6,1},{7,2},{8,13},{9,14},{10,15},{13,8},{... | collective-permute-start | bytes 983048 | tf_op jit(solution)/shard_map/ppermute | solution.py:95
  12.2 1.9 %collective-permute-start.2 = (bf16[5,64,512]{2,1,0:T(8,128)(2,1)S(1)}, bf16[5,64,512]{2,1,0:T(8,128)(2,1)S(1)}, u32[]{:S(2)}, u32[]{:S(2)}) collective-permute-start(bf16[5,64,512]{2,1,0:T(8,128)(2,1)S(1)} %collective-permute-done.1.mine_ref), channel_id=1, source_target_pairs={{0,4},{4,0},{1,5},{5,1},{2,6},{6,2},{3,7},{7,3},{8,12},{12,8},{9,1... | collective-permute-start | bytes 983048 | tf_op jit(solution)/shard_map/ppermute | solution.py:51
  12.9 7.4 %collective-permute-start.3 = (bf16[512,256]{1,0:T(8,128)(2,1)S(1)}, bf16[512,256]{1,0:T(8,128)(2,1)S(1)}, u32[]{:S(2)}, u32[]{:S(2)}) collective-permute-start(bf16[512,256]{1,0:T(8,128)(2,1)S(1)} %get-tuple-element.39.end_ref), channel_id=1, source_target_pairs={{0,8},{8,0},{16,24},{4,20},{12,28},{1,9},{9,1},{17,25},{5,21},{13,... | collective-permute-start | bytes 786440 | tf_op jit(solution)/shard_map/ppermute | solution.py:316
  14.3 14.1 %slice-start = ((s8[4718592]{0:T(1024)(128)(4,1)}), s8[4194304]{0:T(1024)(128)(4,1)S(1)}, s32[]{:S(2)}) async-start(s8[4718592]{0:T(1024)(128)(4,1)} %bitcast.3), calls=%async_computation | async-start | bytes 8388608
  14.3 13.5 %copy-start.5 = (f32[512]{0:T(512)S(1)}, f32[512]{0:T(512)}, u32[]{:S(2)}) copy-start(f32[512]{0:T(512)} %param.10) | copy-start | bytes 6148
  14.4 14.1 %slice-start.1 = ((s8[4718592]{0:T(1024)(128)(4,1)}), s8[524288]{0:T(1024)(128)(4,1)S(1)}, s32[]{:S(2)}) async-start(s8[4718592]{0:T(1024)(128)(4,1)} %bitcast.3), calls=%async_computation.1 | async-start | bytes 1048576
  15.4 8.4 %collective-permute-start.5 = (bf16[640,256]{1,0:T(8,128)(2,1)S(1)}, bf16[640,256]{1,0:T(8,128)(2,1)S(1)}, u32[]{:S(2)}, u32[]{:S(2)}) collective-permute-start(bf16[640,256]{1,0:T(8,128)(2,1)S(1)} %get-tuple-element.40.end_ref), channel_id=1, source_target_pairs={{0,8},{8,0},{16,24},{4,20},{12,28},{1,9},{9,1},{17,25},{5,21},{13,... | collective-permute-start | bytes 983048 | tf_op jit(solution)/shard_map/ppermute | solution.py:316
  20.4 7.4 %collective-permute-start.4 = (bf16[512,256]{1,0:T(8,128)(2,1)S(1)}, bf16[512,256]{1,0:T(8,128)(2,1)S(1)}, u32[]{:S(2)}, u32[]{:S(2)}) collective-permute-start(bf16[512,256]{1,0:T(8,128)(2,1)S(1)} %shard_map.70), channel_id=1, source_target_pairs={{0,16},{8,24},{4,12},{20,28},{28,20},{1,17},{9,25},{5,13},{21,29},... | collective-permute-start | bytes 786440 | tf_op jit(solution)/shard_map/ppermute | solution.py:319
  24.0 8.1 %collective-permute-start.6 = (bf16[640,256]{1,0:T(8,128)(2,1)S(1)}, bf16[640,256]{1,0:T(8,128)(2,1)S(1)}, u32[]{:S(2)}, u32[]{:S(2)}) collective-permute-start(bf16[640,256]{1,0:T(8,128)(2,1)S(1)} %shard_map.71), channel_id=1, source_target_pairs={{0,16},{8,24},{4,12},{20,28},{28,20},{1,17},{9,25},{5,13},{21,29},... | collective-permute-start | bytes 983048 | tf_op jit(solution)/shard_map/ppermute | solution.py:319
  32.2 3.1 %collective-permute-start.7 = (bf16[2,48,256]{2,1,0:T(8,128)(2,1)S(1)}, bf16[2,48,256]{2,1,0:T(8,128)(2,1)S(1)}, u32[]{:S(2)}, u32[]{:S(2)}) collective-permute-start(bf16[2,48,256]{2,1,0:T(8,128)(2,1)S(1)} %shard_map.77), channel_id=1, source_target_pairs={{0,4},{4,0},{1,5},{5,1},{2,6},{6,2},{3,7},{7,3},{8,12},{12,8},{9,1... | collective-permute-start | bytes 147464 | tf_op jit(solution)/shard_map/ppermute | solution.py:51

commit v16 on v15

--- a/solution.py
+++ b/solution.py
@@ -125,6 +125,34 @@
     up = jnp.where(row == 0, is_core(1) * above, pltpu.roll(column, 1, 0))
     down = jnp.where(row == rows - 1, is_core(0) * below, pltpu.roll(column, rows - 1, 0))
     return jnp.concatenate([up, column, down], axis=1)
+
+
+SLAB = 8
+
+
+def add_columns(cells, columns):
+    rows, cols, wide = cells.shape
+    col = lax.broadcasted_iota(jnp.int32, (rows, SLAB, wide), 1)
+
+    def slab(start):
+        total = 0.0
+        for at, column in columns:
+            if start <= at < start + SLAB:
+                total = jnp.where(col == at - start, column, total)
+        return cells[:, start : start + SLAB] + total
+
+    middle = [cells[:, SLAB : cols - SLAB]] if cols > 2 * SLAB else []
+    return jnp.concatenate([slab(0), *middle, slab(cols - SLAB)], axis=1)
+
+
+def with_column(cells, at, column):
+    rows, cols, wide = cells.shape
+    start = 0 if at == 0 else cols - SLAB
+    col = lax.broadcasted_iota(jnp.int32, (rows, SLAB, wide), 1)
+    slab = jnp.where(col == at - start, column, cells[:, start : start + SLAB])
+    if at == 0:
+        return jnp.concatenate([slab, cells[:, SLAB:]], axis=1)
+    return jnp.concatenate([cells[:, :start], slab], axis=1)
 
 
 def halves(channels):
@@ -160,10 +188,10 @@
             total = dot(cells, weight_ref, 1, lanes).reshape(tile)
             first = dot(cells, weight_ref, 0, lanes).reshape(tile)
             spill_ref[1, here, lanes] = first[:, cols - 1, :]
-            total += jnp.where(col == 0, 0.0, pltpu.roll(first, 1, 1))
+            total += with_column(pltpu.roll(first, 1, 1), 0, 0.0)
             last = dot(cells, weight_ref, 2, lanes).reshape(tile)
             spill_ref[0, here, lanes] = last[:, 0, :]
-            total += jnp.where(col == cols - 1, 0.0, pltpu.roll(last, cols - 1, 1))
+            total += with_column(pltpu.roll(last, cols - 1, 1), cols - 1, 0.0)
             total_ref[frame, :, :, lanes] = total
             totals.append(total)
         states.append(end_state(totals, pole_ref, lanes))
@@ -504,7 +532,6 @@
 def tile_sum(tile, inputs, lanes, room, lhs_ref, weight_ref):
     count, rows, cols, wide = tile
     size = rows * cols
-    col = lax.broadcasted_iota(jnp.int32, tile[1:], 1)
 
     def beside(cells):
         return cells.reshape(rows, 1, wide) if room else 0.0
@@ -515,10 +542,10 @@
         total = dot(lhs_ref[at + room : end], weight_ref, 1, lanes, inputs).reshape(tile[1:])
         first = dot(lhs_ref[at:end], weight_ref, 0, lanes, inputs)
         shifted = pltpu.roll(first[room:].reshape(tile[1:]), 1, 1)
-        total += jnp.where(col == 0, beside(first[:room]), shifted)
+        total += with_column(shifted, 0, beside(first[:room]))
         last = dot(lhs_ref[at + room : end + room], weight_ref, 2, lanes, inputs)
         shifted = pltpu.roll(last[:size].reshape(tile[1:]), cols - 1, 1)
-        yield total + jnp.where(col == cols - 1, beside(last[size:]), shifted)
+        yield total + with_column(shifted, cols - 1, beside(last[size:]))
 
 
 def strip_slots(count, rows, cols):
@@ -542,17 +569,13 @@
     reached = row_of(middle[room : room + given])
     reached += jnp.where(col == 0, 0.0, pltpu.roll(row_of(first[:given]), 1, 1))
     reached += jnp.where(col == cols - 1, 0.0, pltpu.roll(row_of(last[2 * room :]), cols - 1, 1))
-    row = lax.broadcasted_iota(jnp.int32, tile, 1)
-    col = lax.broadcasted_iota(jnp.int32, tile, 2)
-    total = jnp.where(row == inner_row(rows), reached.reshape(count, 1, cols, wide), 0.0)
-    for at, cells in (
+    columns = [
         (0, first[given : given + room] + middle[:room]),
         (1, first[given + room :]),
         (cols - 2, last[:room]),
         (cols - 1, middle[room + given :] + last[room : 2 * room]),
-    ):
-        total += jnp.where(col == at, cells.reshape(count, rows, 1, wide), 0.0)
-    return total
+    ]
+    return [(at, cells.reshape(count, rows, 1, wide)) for at, cells in columns], reached
 
 
 def further_kernel(inputs, lanes, lhs_ref, weight_ref, out_ref):
@@ -588,10 +611,14 @@
 
     for part, lanes in enumerate(parts):
         tile = (count, rows, cols, lanes.stop - lanes.start)
-        strips = strip_sum(tile, parts[0], lanes, strip_lhs_ref, weight_ref)
+        columns, reached = strip_sum(tile, parts[0], lanes, strip_lhs_ref, weight_ref)
         tiles = tile_sum(tile, parts[1], lanes, rows, lhs_ref, weight_ref)
         for frame, total in enumerate(tiles):
-            total += before_refs[part][frame] + strips[frame]
+            total += before_refs[part][frame]
+            total = add_columns(total, [(at, cells[frame]) for at, cells in columns])
+            row = reached[frame][None]
+            ends = total[:1] + is_core(1) * row, total[rows - 1 :] + is_core(0) * row
+            total = jnp.concatenate([ends[0], total[1 : rows - 1], ends[1]], axis=0)
             held_ref[frame, :, :, lanes] = total.astype(held_ref.dtype)
             store(frame, part).start()
     for part in range(len(parts)):

time: 40.7 us -> 40.4 us (level)
  no operation moved by 1% of the time
where the time goes in v16:
time: 40.4 us; the launch traced here: 39.9 us
  Pallas kernels  16.8 us (42%)
  starting transfers between devices  12.5 us (31%)
  waiting for transfers between devices  8.85 us (22%)
  local copies, waits for them, and re-layouts  1.36 us (3%)
  between operations  0.41 us (1%)
    pallas_call x16, Pallas kernels, call(): pl.pallas_call(kernel, in_specs=[WHOLE] * len(args), out_specs=out_specs...  16.8 us
    ppermute x2, waiting for transfers between devices, exchange_four(): got = lax.ppermute(end, axes, first_round)  4.83 us
    ppermute x2, starting transfers between devices, exchange_four(): arrivals.append((got, lax.ppermute(relayed, axes, second_round)))  4.07 us
    ppermute x3, starting transfers between devices, swap_cores(): return lax.ppermute(array, 'sx', [(0, 1), (1, 0)])  3.35 us
    ppermute x2, starting transfers between devices, exchange_four(): got = lax.ppermute(end, axes, first_round)  2.7 us
    ppermute x2, waiting for transfers between devices, exchange_four(): arrivals.append((got, lax.ppermute(relayed, axes, second_round)))  2.43 us
    ppermute x1, starting transfers between devices, trade_columns(): return (got, lax.ppermute(columns, ('sx', 'sy'), pairs))  2.33 us
    unnamed x16, local copies, waits for them, and re-layouts  1.35 us
  transfers between devices with their start and end apart: 8, of which 6 were waited for; matrix products, arithmetic and copies ran while one was open for 0% of the time, Pallas kernels for 29%

profile of v16, /device:TPU:23, one launch (start us, length us, event | category | flops | bytes accessed | tf_op | source)
XLA Modules:
  0.0 39.9 jit_solution(12741018258856390364)
XLA Ops:
  0.0 0.0 copy-start
  0.0 0.0 copy-start.2
  0.0 1.3 %copy-done.2 = bf16[2,32,16,512]{3,2,1,0:T(8,128)(2,1)S(1)} copy-done((bf16[2,32,16,512]{3,2,1,0:T(8,128)(2,1)S(1)}, bf16[2,32,16,512]{3,2,1,0:T(8,128)(2,1)}, u32[]{:S(2)}) %copy-start.2) | copy-done | bytes 1048600
  1.3 0.0 copy-start.3
  1.3 0.3 shard_map.64
  1.7 0.0 copy-done
  1.7 0.0 copy-start.1
  1.7 0.0 copy-start.4
  1.7 0.3 shard_map.65
  2.0 0.7 %collective-permute-start = (bf16[192,512]{1,0:T(8,128)(2,1)S(1)}, bf16[192,512]{1,0:T(8,128)(2,1)S(1)}, u32[]{:S(2)}, u32[]{:S(2)}) collective-permute-start(bf16[192,512]{1,0:T(8,128)(2,1)S(1)} %get-tuple-element.31), channel_id=1, source_target_pairs={{0,4},{4,0},{1,5},{5,1},{2,6},{6,2},{3,7},{7,3},{8,12},{12,8},{9,1... | collective-permute-start | bytes 589832 | tf_op jit(solution)/shard_map/ppermute | solution.py:51
  2.7 0.0 copy-done.3
  2.7 0.2 shard_map.66._
  2.9 0.9 %collective-permute-done.got_ref = bf16[192,512]{1,0:T(8,128)(2,1)S(1)} collective-permute-done((bf16[192,512]{1,0:T(8,128)(2,1)S(1)}, bf16[192,512]{1,0:T(8,128)(2,1)S(1)}, u32[]{:S(2)}, u32[]{:S(2)}) %collective-permute-start) | collective-permute-done | bytes 196640 | tf_op jit(solution)/shard_map/ppermute | solution.py:51
  3.8 2.3 %collective-permute-start.1 = (bf16[5,64,512]{2,1,0:T(8,128)(2,1)S(1)}, bf16[5,64,512]{2,1,0:T(8,128)(2,1)S(1)}, u32[]{:S(2)}, u32[]{:S(2)}) collective-permute-start(bf16[5,64,512]{2,1,0:T(8,128)(2,1)S(1)} %pad_maximum_fusion), channel_id=1, source_target_pairs={{0,5},{1,6},{2,7},{5,0},{6,1},{7,2},{8,13},{9,14},{10,15},{13,8},{... | collective-permute-start | bytes 983048 | tf_op jit(solution)/shard_map/ppermute | solution.py:95
  6.2 0.0 copy-done.1
  6.2 0.0 copy-done.4
  6.2 5.3 %shard_map.67 = (f32[2,32,16,512]{3,2,1,0:T(8,128)S(1)}, f32[2,64,512]{2,1,0:T(8,128)S(1)}, bf16[512,256]{1,0:T(8,128)(2,1)S(1)}, bf16[1024,1536]{1,0:T(8,128)(2,1)S(1)}) custom-call(bf16[1024,1536]{1,0:T(8,128)(2,1)S(1)} %shard_map.66._, bf16[192,512]{1,0:T(8,128)(2,1)S(1)} %collective-permute-done.got_ref, ...), custom_call_target="tpu_custom_call", output_to_operand_aliasing={{3}: (0, {})} | custom-call | flops 4831838208 | bytes 13830144 | tf_op jit(solution)/shard_map/pallas_call | solution.py:21
  11.5 0.7 %collective-permute-done.1.mine_ref = bf16[5,64,512]{2,1,0:T(8,128)(2,1)S(1)} collective-permute-done((bf16[5,64,512]{2,1,0:T(8,128)(2,1)S(1)}, bf16[5,64,512]{2,1,0:T(8,128)(2,1)S(1)}, u32[]{:S(2)}, u32[]{:S(2)}) %collective-permute-start.1) | collective-permute-done | bytes 327712 | tf_op jit(solution)/shard_map/ppermute | solution.py:95
  12.2 0.6 %collective-permute-start.2 = (bf16[5,64,512]{2,1,0:T(8,128)(2,1)S(1)}, bf16[5,64,512]{2,1,0:T(8,128)(2,1)S(1)}, u32[]{:S(2)}, u32[]{:S(2)}) collective-permute-start(bf16[5,64,512]{2,1,0:T(8,128)(2,1)S(1)} %collective-permute-done.1.mine_ref), channel_id=1, source_target_pairs={{0,4},{4,0},{1,5},{5,1},{2,6},{6,2},{3,7},{7,3},{8,12},{12,8},{9,1... | collective-permute-start | bytes 983048 | tf_op jit(solution)/shard_map/ppermute | solution.py:51
  12.9 1.3 %collective-permute-start.3 = (bf16[512,256]{1,0:T(8,128)(2,1)S(1)}, bf16[512,256]{1,0:T(8,128)(2,1)S(1)}, u32[]{:S(2)}, u32[]{:S(2)}) collective-permute-start(bf16[512,256]{1,0:T(8,128)(2,1)S(1)} %get-tuple-element.39.end_ref), channel_id=1, source_target_pairs={{0,8},{8,0},{16,24},{4,20},{12,28},{1,9},{9,1},{17,25},{5,21},{13,... | collective-permute-start | bytes 786440 | tf_op jit(solution)/shard_map/ppermute | solution.py:344
  14.1 0.0 collective-permute-done.2.theirs_ref
  14.2 0.2 shard_map.68
  14.3 0.0 slice-start
  14.4 0.0 copy-start.5
  14.4 0.0 slice-start.1
  14.4 1.0 %shard_map.69 = (f32[2,32,16,256]{3,2,1,0:T(8,128)S(1)}, f32[2,64,256]{2,1,0:T(8,128)S(1)}, f32[2,128,256]{2,1,0:T(8,128)S(1)}, bf16[640,256]{1,0:T(8,128)(2,1)S(1)}) custom-call(bf16[256,1536]{1,0:T(8,128)(2,1)S(1)} %get-tuple-element.35.lhs_ref, bf16[3,3,512,512]{3,2,1,0:T(8,128)(2,1)S(1)} %copy-done.1, ...), custom_call_target="tpu_custom_call" | custom-call | flops 603979776 | bytes 9635840 | tf_op jit(solution)/shard_map/pallas_call | solution.py:21
  15.4 1.4 %collective-permute-start.5 = (bf16[640,256]{1,0:T(8,128)(2,1)S(1)}, bf16[640,256]{1,0:T(8,128)(2,1)S(1)}, u32[]{:S(2)}, u32[]{:S(2)}) collective-permute-start(bf16[640,256]{1,0:T(8,128)(2,1)S(1)} %get-tuple-element.40.end_ref), channel_id=1, source_target_pairs={{0,8},{8,0},{16,24},{4,20},{12,28},{1,9},{9,1},{17,25},{5,21},{13,... | collective-permute-start | bytes 983048 | tf_op jit(solution)/shard_map/ppermute | solution.py:344
  16.8 3.4 %collective-permute-done.3.got_ref.refs_4_.refs_8_ = bf16[512,256]{1,0:T(8,128)(2,1)S(1)} collective-permute-done((bf16[512,256]{1,0:T(8,128)(2,1)S(1)}, bf16[512,256]{1,0:T(8,128)(2,1)S(1)}, u32[]{:S(2)}, u32[]{:S(2)}) %collective-permute-start.3) | collective-permute-done | bytes 262176 | tf_op jit(solution)/shard_map/ppermute | solution.py:344
  20.3 0.2 shard_map.70
  20.4 1.9 %collective-permute-start.4 = (bf16[512,256]{1,0:T(8,128)(2,1)S(1)}, bf16[512,256]{1,0:T(8,128)(2,1)S(1)}, u32[]{:S(2)}, u32[]{:S(2)}) collective-permute-start(bf16[512,256]{1,0:T(8,128)(2,1)S(1)} %shard_map.70), channel_id=1, source_target_pairs={{0,16},{8,24},{4,12},{20,28},{28,20},{1,17},{9,25},{5,13},{21,29},... | collective-permute-start | bytes 786440 | tf_op jit(solution)/shard_map/ppermute | solution.py:347
  22.4 1.4 %collective-permute-done.5.got_ref.refs_6_.refs_10_.refs_5_ = bf16[640,256]{1,0:T(8,128)(2,1)S(1)} collective-permute-done((bf16[640,256]{1,0:T(8,128)(2,1)S(1)}, bf16[640,256]{1,0:T(8,128)(2,1)S(1)}, u32[]{:S(2)}, u32[]{:S(2)}) %collective-permute-start.5) | collective-permute-done | bytes 327712 | tf_op jit(solution)/shard_map/ppermute | solution.py:344
  23.8 0.2 shard_map.71
  24.0 2.1 %collective-permute-start.6 = (bf16[640,256]{1,0:T(8,128)(2,1)S(1)}, bf16[640,256]{1,0:T(8,128)(2,1)S(1)}, u32[]{:S(2)}, u32[]{:S(2)}) collective-permute-start(bf16[640,256]{1,0:T(8,128)(2,1)S(1)} %shard_map.71), channel_id=1, source_target_pairs={{0,16},{8,24},{4,12},{20,28},{28,20},{1,17},{9,25},{5,13},{21,29},... | collective-permute-start | bytes 983048 | tf_op jit(solution)/shard_map/ppermute | solution.py:347
  26.1 1.7 %collective-permute-done.4.refs_5_.refs_9_ = bf16[512,256]{1,0:T(8,128)(2,1)S(1)} collective-permute-done((bf16[512,256]{1,0:T(8,128)(2,1)S(1)}, bf16[512,256]{1,0:T(8,128)(2,1)S(1)}, u32[]{:S(2)}, u32[]{:S(2)}) %collective-permute-start.4) | collective-permute-done | bytes 262176 | tf_op jit(solution)/shard_map/ppermute | solution.py:347
  27.8 0.0 copy-done.5
  27.8 0.6 %shard_map.72.lhs_ref = bf16[1024,768]{1,0:T(8,128)(2,1)S(1)} custom-call(f32[2,32,16,512]{3,2,1,0:T(8,128)S(1)} %get-tuple-element.36.total_ref.refs_0_, f32[32,16,512]{2,1,0:T(8,128)S(1)} %copy-done, s32[1,512]{1,0:T(1,128)S(1)} %bitcast.9, f32[1,512]{1,0:T(1,128)S(1)} %bitcast.13, bf16[512,256]{1,0:T(8,128)(2,1)S(1)} %collective-permute-done.3.got_ref.refs_4_.refs_8_, ...), custom_call_target="tpu_custom_call" | custom-call | bytes 5246976 | tf_op jit(solution)/shard_map/pallas_call | solution.py:21
  28.5 0.0 slice-done
  28.5 0.0 slice-done.1
  28.5 1.4 %shard_map.73.refs_0_ = f32[2,32,16,256]{3,2,1,0:T(8,128)S(1)} custom-call(bf16[1024,768]{1,0:T(8,128)(2,1)S(1)} %shard_map.72.lhs_ref, bf16[3,3,512,512]{3,2,1,0:T(8,128)(2,1)S(1)} %bitcast.4), custom_call_target="tpu_custom_call" | custom-call | flops 1207959552 | bytes 7340032 | tf_op jit(solution)/shard_map/pallas_call | solution.py:21
  29.9 1.4 %shard_map.74.refs_1_ = f32[2,32,16,256]{3,2,1,0:T(8,128)S(1)} custom-call(bf16[1024,768]{1,0:T(8,128)(2,1)S(1)} %shard_map.72.lhs_ref, bf16[3,3,512,512]{3,2,1,0:T(8,128)(2,1)S(1)} %bitcast.4), custom_call_target="tpu_custom_call" | custom-call | flops 1207959552 | bytes 7340032 | tf_op jit(solution)/shard_map/pallas_call | solution.py:21
  31.3 0.1 shard_map.76.refs_5_.refs_2_
  31.4 0.7 %collective-permute-done.6.refs_7_.refs_11_.refs_6_ = bf16[640,256]{1,0:T(8,128)(2,1)S(1)} collective-permute-done((bf16[640,256]{1,0:T(8,128)(2,1)S(1)}, bf16[640,256]{1,0:T(8,128)(2,1)S(1)}, u32[]{:S(2)}, u32[]{:S(2)}) %collective-permute-start.6) | collective-permute-done | bytes 327712 | tf_op jit(solution)/shard_map/ppermute | solution.py:347
  32.1 0.1 shard_map.77
  32.2 2.0 %collective-permute-start.7 = (bf16[2,48,256]{2,1,0:T(8,128)(2,1)S(1)}, bf16[2,48,256]{2,1,0:T(8,128)(2,1)S(1)}, u32[]{:S(2)}, u32[]{:S(2)}) collective-permute-start(bf16[2,48,256]{2,1,0:T(8,128)(2,1)S(1)} %shard_map.77), channel_id=1, source_target_pairs={{0,4},{4,0},{1,5},{5,1},{2,6},{6,2},{3,7},{7,3},{8,12},{12,8},{9,1... | collective-permute-start | bytes 147464 | tf_op jit(solution)/shard_map/ppermute | solution.py:51
  34.2 0.4 shard_map.78
  34.6 0.7 %shard_map.75._ = bf16[1152,768]{1,0:T(8,128)(2,1)S(1)} custom-call(f32[2,32,16,256]{3,2,1,0:T(8,128)S(1)} %get-tuple-element.38.refs_0_.refs_1_, f32[32,16,512]{2,1,0:T(8,128)S(1)} %copy-done, s32[1,512]{1,0:T(1,128)S(1)} %bitcast.12, f32[1,512]{1,0:T(1,128)S(1)} %bitcast.16, bf16[512,256]{1,0:T(8,128)(2,1)S(1)} %collective-permute-done.3.got_ref.refs_4_.refs_8_, ...), custom_call_target="tpu_custom_call" | custom-call | bytes 5050368 | tf_op jit(solution)/shard_map/pallas_call | solution.py:21
  35.3 0.0 collective-permute-done.7.got_ref
  35.3 4.5 %shard_map.79 = (bf16[2,32,16,512]{3,2,1,0:T(8,128)(2,1)}, bf16[1152,768]{1,0:T(8,128)(2,1)S(1)}) custom-call(bf16[1152,768]{1,0:T(8,128)(2,1)S(1)} %shard_map.75._, bf16[2,48,256]{2,1,0:T(8,128)(2,1)S(1)} %collective-permute-done.7.got_ref, bf16[2,64,256]{2,1,0:T(8,128)(2,1)S(1)} %get-tuple-element.46.beside_ref, ...), custom_call_target="tpu_custom_call", output_to_operand_aliasing={{1}: (0, {})} | custom-call | flops 2415919104 | bytes 11649024 | tf_op jit(solution)/shard_map/pallas_call | solution.py:21
  (3 shorter events, 0.0 us)
Async XLA Ops:
  0.0 1.7 %copy-start = (f32[32,16,512]{2,1,0:T(8,128)S(1)}, f32[32,16,512]{2,1,0:T(8,128)}, u32[]{:S(2)}) copy-start(f32[32,16,512]{2,1,0:T(8,128)} %refs_4_.1) | copy-start | bytes 3145732
  0.0 1.3 %copy-start.2 = (bf16[2,32,16,512]{3,2,1,0:T(8,128)(2,1)S(1)}, bf16[2,32,16,512]{3,2,1,0:T(8,128)(2,1)}, u32[]{:S(2)}) copy-start(bf16[2,32,16,512]{3,2,1,0:T(8,128)(2,1)} %cells_ref.3) | copy-start | bytes 3145732
  1.3 1.4 %copy-start.3 = (bf16[2,32,16,512]{3,2,1,0:T(8,128)(2,1)S(1)}, bf16[2,32,16,512]{3,2,1,0:T(8,128)(2,1)}, u32[]{:S(2)}) copy-start(bf16[2,32,16,512]{3,2,1,0:T(8,128)(2,1)} %cells_ref.3) | copy-start | bytes 3145732
  1.7 4.5 %copy-start.1 = (bf16[3,3,512,512]{3,2,1,0:T(8,128)(2,1)S(1)}, bf16[3,3,512,512]{3,2,1,0:T(8,128)(2,1)}, u32[]{:S(2)}) copy-start(bf16[3,3,512,512]{3,2,1,0:T(8,128)(2,1)} %weight_ref.6) | copy-start | bytes 14155780
  1.7 4.5 %copy-start.4 = (s32[512]{0:T(512)S(1)}, s32[512]{0:T(512)}, u32[]{:S(2)}) copy-start(s32[512]{0:T(512)} %param.9) | copy-start | bytes 6148
  2.0 1.8 %collective-permute-start = (bf16[192,512]{1,0:T(8,128)(2,1)S(1)}, bf16[192,512]{1,0:T(8,128)(2,1)S(1)}, u32[]{:S(2)}, u32[]{:S(2)}) collective-permute-start(bf16[192,512]{1,0:T(8,128)(2,1)S(1)} %get-tuple-element.31), channel_id=1, source_target_pairs={{0,4},{4,0},{1,5},{5,1},{2,6},{6,2},{3,7},{7,3},{8,12},{12,8},{9,1... | collective-permute-start | bytes 589832 | tf_op jit(solution)/shard_map/ppermute | solution.py:51
  3.8 8.4 %collective-permute-start.1 = (bf16[5,64,512]{2,1,0:T(8,128)(2,1)S(1)}, bf16[5,64,512]{2,1,0:T(8,128)(2,1)S(1)}, u32[]{:S(2)}, u32[]{:S(2)}) collective-permute-start(bf16[5,64,512]{2,1,0:T(8,128)(2,1)S(1)} %pad_maximum_fusion), channel_id=1, source_target_pairs={{0,5},{1,6},{2,7},{5,0},{6,1},{7,2},{8,13},{9,14},{10,15},{13,8},{... | collective-permute-start | bytes 983048 | tf_op jit(solution)/shard_map/ppermute | solution.py:95
  12.2 1.9 %collective-permute-start.2 = (bf16[5,64,512]{2,1,0:T(8,128)(2,1)S(1)}, bf16[5,64,512]{2,1,0:T(8,128)(2,1)S(1)}, u32[]{:S(2)}, u32[]{:S(2)}) collective-permute-start(bf16[5,64,512]{2,1,0:T(8,128)(2,1)S(1)} %collective-permute-done.1.mine_ref), channel_id=1, source_target_pairs={{0,4},{4,0},{1,5},{5,1},{2,6},{6,2},{3,7},{7,3},{8,12},{12,8},{9,1... | collective-permute-start | bytes 983048 | tf_op jit(solution)/shard_map/ppermute | solution.py:51
  12.9 7.4 %collective-permute-start.3 = (bf16[512,256]{1,0:T(8,128)(2,1)S(1)}, bf16[512,256]{1,0:T(8,128)(2,1)S(1)}, u32[]{:S(2)}, u32[]{:S(2)}) collective-permute-start(bf16[512,256]{1,0:T(8,128)(2,1)S(1)} %get-tuple-element.39.end_ref), channel_id=1, source_target_pairs={{0,8},{8,0},{16,24},{4,20},{12,28},{1,9},{9,1},{17,25},{5,21},{13,... | collective-permute-start | bytes 786440 | tf_op jit(solution)/shard_map/ppermute | solution.py:344
  14.3 14.1 %slice-start = ((s8[4718592]{0:T(1024)(128)(4,1)}), s8[4194304]{0:T(1024)(128)(4,1)S(1)}, s32[]{:S(2)}) async-start(s8[4718592]{0:T(1024)(128)(4,1)} %bitcast.3), calls=%async_computation | async-start | bytes 8388608
  14.4 13.5 %copy-start.5 = (f32[512]{0:T(512)S(1)}, f32[512]{0:T(512)}, u32[]{:S(2)}) copy-start(f32[512]{0:T(512)} %param.10) | copy-start | bytes 6148
  14.4 14.1 %slice-start.1 = ((s8[4718592]{0:T(1024)(128)(4,1)}), s8[524288]{0:T(1024)(128)(4,1)S(1)}, s32[]{:S(2)}) async-start(s8[4718592]{0:T(1024)(128)(4,1)} %bitcast.3), calls=%async_computation.1 | async-start | bytes 1048576
  15.4 8.4 %collective-permute-start.5 = (bf16[640,256]{1,0:T(8,128)(2,1)S(1)}, bf16[640,256]{1,0:T(8,128)(2,1)S(1)}, u32[]{:S(2)}, u32[]{:S(2)}) collective-permute-start(bf16[640,256]{1,0:T(8,128)(2,1)S(1)} %get-tuple-element.40.end_ref), channel_id=1, source_target_pairs={{0,8},{8,0},{16,24},{4,20},{12,28},{1,9},{9,1},{17,25},{5,21},{13,... | collective-permute-start | bytes 983048 | tf_op jit(solution)/shard_map/ppermute | solution.py:344
  20.4 7.4 %collective-permute-start.4 = (bf16[512,256]{1,0:T(8,128)(2,1)S(1)}, bf16[512,256]{1,0:T(8,128)(2,1)S(1)}, u32[]{:S(2)}, u32[]{:S(2)}) collective-permute-start(bf16[512,256]{1,0:T(8,128)(2,1)S(1)} %shard_map.70), channel_id=1, source_target_pairs={{0,16},{8,24},{4,12},{20,28},{28,20},{1,17},{9,25},{5,13},{21,29},... | collective-permute-start | bytes 786440 | tf_op jit(solution)/shard_map/ppermute | solution.py:347
  24.0 8.1 %collective-permute-start.6 = (bf16[640,256]{1,0:T(8,128)(2,1)S(1)}, bf16[640,256]{1,0:T(8,128)(2,1)S(1)}, u32[]{:S(2)}, u32[]{:S(2)}) collective-permute-start(bf16[640,256]{1,0:T(8,128)(2,1)S(1)} %shard_map.71), channel_id=1, source_target_pairs={{0,16},{8,24},{4,12},{20,28},{28,20},{1,17},{9,25},{5,13},{21,29},... | collective-permute-start | bytes 983048 | tf_op jit(solution)/shard_map/ppermute | solution.py:347
  32.2 3.1 %collective-permute-start.7 = (bf16[2,48,256]{2,1,0:T(8,128)(2,1)S(1)}, bf16[2,48,256]{2,1,0:T(8,128)(2,1)S(1)}, u32[]{:S(2)}, u32[]{:S(2)}) collective-permute-start(bf16[2,48,256]{2,1,0:T(8,128)(2,1)S(1)} %shard_map.77), channel_id=1, source_target_pairs={{0,4},{4,0},{1,5},{5,1},{2,6},{6,2},{3,7},{7,3},{8,12},{12,8},{9,1... | collective-permute-start | bytes 147464 | tf_op jit(solution)/shard_map/ppermute | solution.py:51

commit v17 on v16

--- a/solution.py
+++ b/solution.py
@@ -397,9 +397,6 @@
     first = lanes.start == 0
     held = lanes if first else slice(None)
     block = 8
-    if first:
-        for frame in range(count):
-            put_row(lhs_ref, frame * stride + room, size, jnp.zeros((cols, wide), lhs_ref.dtype))
     for row in range(0, rows, block):
         here = slice(row, row + block)
         drives = [drive_ref[frame, here, :, held] for frame in range(count)]
@@ -414,6 +411,17 @@
             put_cells(lhs_ref, frame * stride + room, size, cols, row * cols, tile)
 
 
+def middle_kernel(lanes, *refs):
+    total_ref, start_ref, pole_ref, scale_ref, *arrived_refs, give_ref = refs
+    count, rows, cols, _ = total_ref.shape
+    mix = Mix(lanes, count, pole_ref, scale_ref)
+    inner = inner_row(rows)
+    drives = [total_ref[frame, inner, :, lanes] for frame in range(count)]
+    entry = mix.entry(arrived_refs, pl.ds(pl.multiple_of(inner * cols, cols), cols))
+    for frame, cells in enumerate(mix(drives, entry, start_ref[inner, :, lanes])):
+        give_ref[frame] = no_border(cells, 0).astype(give_ref.dtype)
+
+
 def strip_start_kernel(start_ref, sides_ref, out_ref):
     rows, cols, _ = start_ref.shape
     start = start_ref[...]
@@ -429,7 +437,7 @@
 
 
 def give_kernel(parts, rounds, *refs):
-    total_ref, drive_ref, beside_ref, strips_ref, *refs = refs
+    drive_ref, beside_ref, strips_ref, *refs = refs
     start_ref, strip_start_ref, pole_ref, scale_ref, *arrived_refs, give_ref = refs
     early_refs, late_refs = arrived_refs[:rounds], arrived_refs[rounds:]
     count, rows, cols, wide = drive_ref.shape
@@ -455,8 +463,6 @@
     entry = put_back(late.entry(late_refs, row), late.entry(early_refs, row), 0)
     drives = [drive_ref[frame, inner] for frame in range(count)]
     tile = late(drives, entry, start_ref[inner, :, parts[1]])
-    drives = [total_ref[frame, inner, :, parts[0]] for frame in range(count)]
-    first = early(drives, early.entry(early_refs, row), start_ref[inner, :, parts[0]])
 
     slots = [(0, 0), (1, 3)]
     entry = rows_of([(i, end(late.entry(late_refs, near(size + i * rows)))) for i, _ in slots])
@@ -484,13 +490,12 @@
         for frame in range(count)
     ]
     strips = early(drives, entry, start)
-    for frame, cells in enumerate(zip(tile, first, beside, strips)):
+    for frame, cells in enumerate(zip(tile, beside, strips)):
         give_ref[frame, :cols] = cells[0].astype(give_ref.dtype)
-        ends = jnp.where(which < 2, cells[2], cells[3])
+        ends = jnp.where(which < 2, cells[1], cells[2])
         ends = jnp.where((which == 0) | (which == 2), inside(0) * ends, ends)
         ends = jnp.where((which == 1) | (which == 5), inside(3) * ends, ends)
-        give_ref[frame, cols : 2 * cols] = ends.astype(give_ref.dtype)
-        give_ref[frame, 2 * cols :] = no_border(cells[1], 0).astype(give_ref.dtype)
+        give_ref[frame, cols:] = ends.astype(give_ref.dtype)
 
 
 def late_kernel(parts, rounds, *refs):
@@ -548,34 +553,27 @@
         yield total + with_column(shifted, cols - 1, beside(last[size:]))
 
 
-def strip_slots(count, rows, cols):
-    room, given = count * rows, count * cols
-    strips = [given, given + room, 2 * given + 2 * room, 2 * given + 3 * room]
-    return strips, [0, given + 2 * room, 2 * given + 4 * room]
-
-
 def strip_sum(tile, inputs, lanes, lhs_ref, weight_ref):
     count, rows, cols, wide = tile
-    room, given = count * rows, count * cols
-    strips, _ = strip_slots(count, rows, cols)
-    first = dot(lhs_ref[: strips[1] + room], weight_ref, 0, lanes, inputs)
-    middle = dot(lhs_ref[strips[1] : strips[2] + room], weight_ref, 1, lanes, inputs)
-    last = dot(lhs_ref[strips[2] :], weight_ref, 2, lanes, inputs)
-    col = lax.broadcasted_iota(jnp.int32, (count, cols, wide), 1)
-
-    def row_of(cells):
-        return cells.reshape(count, cols, wide)
-
-    reached = row_of(middle[room : room + given])
-    reached += jnp.where(col == 0, 0.0, pltpu.roll(row_of(first[:given]), 1, 1))
-    reached += jnp.where(col == cols - 1, 0.0, pltpu.roll(row_of(last[2 * room :]), cols - 1, 1))
+    room = count * rows
+    first = dot(lhs_ref[: 2 * room], weight_ref, 0, lanes, inputs)
+    middle = dot(lhs_ref[room : 3 * room], weight_ref, 1, lanes, inputs)
+    last = dot(lhs_ref[2 * room :], weight_ref, 2, lanes, inputs)
     columns = [
-        (0, first[given : given + room] + middle[:room]),
-        (1, first[given + room :]),
+        (0, first[:room] + middle[:room]),
+        (1, first[room:]),
         (cols - 2, last[:room]),
-        (cols - 1, middle[room + given :] + last[room : 2 * room]),
+        (cols - 1, middle[room:] + last[room:]),
     ]
-    return [(at, cells.reshape(count, rows, 1, wide)) for at, cells in columns], reached
+    return [(at, cells.reshape(count, rows, 1, wide)) for at, cells in columns]
+
+
+def opening_kernel(inputs, lanes, _, got_ref, weight_ref, out_ref, lhs_ref):
+    count, rows, cols, _ = out_ref.shape
+    size = rows * cols
+    for frame in range(count):
+        put_row(lhs_ref, frame * size, size, got_ref[frame])
+    further_kernel(inputs, lanes, lhs_ref, weight_ref, out_ref)
 
 
 def further_kernel(inputs, lanes, lhs_ref, weight_ref, out_ref):
@@ -589,21 +587,15 @@
 ):
     *before_refs, out_ref, lhs_ref, held_ref, strip_lhs_ref, sems = refs
     count, rows, cols, _ = held_ref.shape
-    size = rows * cols
+    size, room = rows * cols, count * rows
     stride = size + 2 * rows
-    strips_at, given_at = strip_slots(count, rows, cols)
     for frame in range(count):
         at = frame * stride
         put_row(lhs_ref, at + rows, size, got_ref[frame, :cols])
-        ends = got_ref[frame, cols : 2 * cols]
+        ends = got_ref[frame, cols:]
         put_columns_taps(lhs_ref, (at, at + rows + size), beside_ref[frame], ends)
-        slots = [slot + frame * rows for slot in strips_at]
+        slots = [slot * room + frame * rows for slot in range(4)]
         put_columns_taps(strip_lhs_ref, slots, strips_ref[frame], ends.astype(jnp.float32)[2:])
-        given = got_ref[frame, 2 * cols :].astype(jnp.float32)
-        given = [is_core(1) * given, jnp.zeros_like(given), is_core(0) * given]
-        given = jnp.concatenate(given, axis=1).astype(strip_lhs_ref.dtype)
-        for at in given_at:
-            strip_lhs_ref[at + frame * cols : at + (frame + 1) * cols] = given
 
     def store(frame, part):
         here = (frame, slice(None), slice(None), parts[part])
@@ -611,14 +603,11 @@
 
     for part, lanes in enumerate(parts):
         tile = (count, rows, cols, lanes.stop - lanes.start)
-        columns, reached = strip_sum(tile, parts[0], lanes, strip_lhs_ref, weight_ref)
+        columns = strip_sum(tile, parts[0], lanes, strip_lhs_ref, weight_ref)
         tiles = tile_sum(tile, parts[1], lanes, rows, lhs_ref, weight_ref)
         for frame, total in enumerate(tiles):
             total += before_refs[part][frame]
             total = add_columns(total, [(at, cells[frame]) for at, cells in columns])
-            row = reached[frame][None]
-            ends = total[:1] + is_core(1) * row, total[rows - 1 :] + is_core(0) * row
-            total = jnp.concatenate([ends[0], total[1 : rows - 1], ends[1]], axis=0)
             held_ref[frame, :, :, lanes] = total.astype(held_ref.dtype)
             store(frame, part).start()
     for part in range(len(parts)):
@@ -713,20 +702,36 @@
 
     mixing = (start_state, pole, scale)
     taps = of((count * size, 3 * half), narrow)
+    give = call(
+        functools.partial(middle_kernel, parts[0]),
+        of((count, cols, half), narrow),
+        total,
+        *mixing,
+        *early,
+    )
     lhs = call(functools.partial(mixed_kernel, parts[0], rounds), taps, total, *mixing, *early)
     strip_start = call(strip_start_kernel, of((4 * rows, channels), jnp.float32), start_state, sides)
     flops = 18 * inner.size * half
-    first_sum, second_sum = (
-        call(
-            functools.partial(further_kernel, parts[0], lanes), inner, lhs, output_weight, flops=flops
-        )
-        for lanes in parts
+    first_sum, lhs = call(
+        functools.partial(opening_kernel, parts[0], parts[0]),
+        (inner, taps),
+        lhs,
+        swap_cores(give),
+        output_weight,
+        aliases={0: 1},
+        flops=flops,
+    )
+    second_sum = call(
+        functools.partial(further_kernel, parts[0], parts[1]),
+        inner,
+        lhs,
+        output_weight,
+        flops=flops,
     )
     *late, first_sum, second_sum = lax.optimization_barrier((*late, first_sum, second_sum))
     give = call(
         functools.partial(give_kernel, parts, rounds),
-        of((count, 3 * cols, half), narrow),
-        total,
+        of((count, 2 * cols, half), narrow),
         drive,
         beside,
         strips,
@@ -765,7 +770,7 @@
         aliases={0: 1},
         scratch=[
             pltpu.VMEM(frames.shape, narrow),
-            pltpu.VMEM((4 * room + 3 * count * cols, 3 * half), narrow),
+            pltpu.VMEM((4 * room, 3 * half), narrow),
             pltpu.SemaphoreType.DMA((count, len(parts))),
         ],
         flops=2 * flops,

time: 40.4 us -> 40 us (0.990)
  waiting for transfers between devices: 8.85 us -> 8.1 us
  starting transfers between devices: 12.5 us -> 13.1 us
    ppermute x2, waiting for transfers between devices: 2.43 us -> 1.73 us  [exchange_four(): arrivals.append((got, lax.ppermute(relayed, axes, second_round)))]
    ppermute x2, starting transfers between devices: 4.07 us -> 4.6 us  [exchange_four(): arrivals.append((got, lax.ppermute(relayed, axes, second_round)))]
    ppermute x3 -> x4, starting transfers between devices: 3.35 us -> 3.57 us  [swap_cores(): return lax.ppermute(array, 'sx', [(0, 1), (1, 0)])]
    pallas_call x16 -> x17, Pallas kernels: 16.8 us -> 16.7 us  [call(): pl.pallas_call(kernel, in_specs=[WHOLE] * len(args), out_specs=out_specs...]
    ppermute x3 -> x4, waiting for transfers between devices: 0.87 us -> 0.95 us  [swap_cores(): return lax.ppermute(array, 'sx', [(0, 1), (1, 0)])]
  transfers between devices with their start and end apart: 8 -> 9, of which waited for: 6 -> 6; matrix products, arithmetic and copies ran while one was open for 0% -> 0% of each run, Pallas kernels for 29% -> 29%
where the time goes in v17:
time: 40 us; the launch traced here: 39.8 us
  Pallas kernels  16.7 us (42%)
  starting transfers between devices  13.1 us (33%)
  waiting for transfers between devices  8.1 us (20%)
  local copies, waits for them, and re-layouts  1.51 us (4%)
  between operations  0.4 us (1%)
    pallas_call x17, Pallas kernels, call(): pl.pallas_call(kernel, in_specs=[WHOLE] * len(args), out_specs=out_specs...  16.7 us
    ppermute x2, waiting for transfers between devices, exchange_four(): got = lax.ppermute(end, axes, first_round)  4.71 us
    ppermute x2, starting transfers between devices, exchange_four(): arrivals.append((got, lax.ppermute(relayed, axes, second_round)))  4.6 us
    ppermute x4, starting transfers between devices, swap_cores(): return lax.ppermute(array, 'sx', [(0, 1), (1, 0)])  3.57 us
    ppermute x2, starting transfers between devices, exchange_four(): got = lax.ppermute(end, axes, first_round)  2.57 us
    ppermute x1, starting transfers between devices, trade_columns(): return (got, lax.ppermute(columns, ('sx', 'sy'), pairs))  2.33 us
    ppermute x2, waiting for transfers between devices, exchange_four(): arrivals.append((got, lax.ppermute(relayed, axes, second_round)))  1.73 us
    unnamed x16, local copies, waits for them, and re-layouts  1.5 us
  transfers between devices with their start and end apart: 9, of which 6 were waited for; matrix products, arithmetic and copies ran while one was open for 0% of the time, Pallas kernels for 29%

profile of v17, /device:TPU:23, one launch (start us, length us, event | category | flops | bytes accessed | tf_op | source)
XLA Modules:
  0.0 39.8 jit_solution(10793310657921901446)
XLA Ops:
  0.0 0.0 copy-start
  0.0 0.0 copy-start.2
  0.0 1.3 %copy-done.2 = bf16[2,32,16,512]{3,2,1,0:T(8,128)(2,1)S(1)} copy-done((bf16[2,32,16,512]{3,2,1,0:T(8,128)(2,1)S(1)}, bf16[2,32,16,512]{3,2,1,0:T(8,128)(2,1)}, u32[]{:S(2)}) %copy-start.2) | copy-done | bytes 1048600
  1.3 0.3 shard_map.64
  1.7 0.0 copy-start.3
  1.7 0.0 copy-done
  1.7 0.3 shard_map.65
  2.0 0.0 copy-start.1
  2.0 0.0 copy-start.4
  2.0 0.7 %collective-permute-start = (bf16[192,512]{1,0:T(8,128)(2,1)S(1)}, bf16[192,512]{1,0:T(8,128)(2,1)S(1)}, u32[]{:S(2)}, u32[]{:S(2)}) collective-permute-start(bf16[192,512]{1,0:T(8,128)(2,1)S(1)} %get-tuple-element.33), channel_id=1, source_target_pairs={{0,4},{4,0},{1,5},{5,1},{2,6},{6,2},{3,7},{7,3},{8,12},{12,8},{9,1... | collective-permute-start | bytes 589832 | tf_op jit(solution)/shard_map/ppermute | solution.py:51
  2.7 0.2 copy-done.3
  2.9 0.2 shard_map.66._
  3.1 0.7 %collective-permute-done.got_ref = bf16[192,512]{1,0:T(8,128)(2,1)S(1)} collective-permute-done((bf16[192,512]{1,0:T(8,128)(2,1)S(1)}, bf16[192,512]{1,0:T(8,128)(2,1)S(1)}, u32[]{:S(2)}, u32[]{:S(2)}) %collective-permute-start) | collective-permute-done | bytes 196640 | tf_op jit(solution)/shard_map/ppermute | solution.py:51
  3.8 2.3 %collective-permute-start.1 = (bf16[5,64,512]{2,1,0:T(8,128)(2,1)S(1)}, bf16[5,64,512]{2,1,0:T(8,128)(2,1)S(1)}, u32[]{:S(2)}, u32[]{:S(2)}) collective-permute-start(bf16[5,64,512]{2,1,0:T(8,128)(2,1)S(1)} %pad_maximum_fusion), channel_id=1, source_target_pairs={{0,5},{1,6},{2,7},{5,0},{6,1},{7,2},{8,13},{9,14},{10,15},{13,8},{... | collective-permute-start | bytes 983048 | tf_op jit(solution)/shard_map/ppermute | solution.py:95
  6.2 0.0 copy-done.1
  6.2 0.0 copy-done.4
  6.2 5.3 %shard_map.67 = (f32[2,32,16,512]{3,2,1,0:T(8,128)S(1)}, f32[2,64,512]{2,1,0:T(8,128)S(1)}, bf16[512,256]{1,0:T(8,128)(2,1)S(1)}, bf16[1024,1536]{1,0:T(8,128)(2,1)S(1)}) custom-call(bf16[1024,1536]{1,0:T(8,128)(2,1)S(1)} %shard_map.66._, bf16[192,512]{1,0:T(8,128)(2,1)S(1)} %collective-permute-done.got_ref, ...), custom_call_target="tpu_custom_call", output_to_operand_aliasing={{3}: (0, {})} | custom-call | flops 4831838208 | bytes 13830144 | tf_op jit(solution)/shard_map/pallas_call | solution.py:21
  11.5 0.7 %collective-permute-done.1.mine_ref = bf16[5,64,512]{2,1,0:T(8,128)(2,1)S(1)} collective-permute-done((bf16[5,64,512]{2,1,0:T(8,128)(2,1)S(1)}, bf16[5,64,512]{2,1,0:T(8,128)(2,1)S(1)}, u32[]{:S(2)}, u32[]{:S(2)}) %collective-permute-start.1) | collective-permute-done | bytes 327712 | tf_op jit(solution)/shard_map/ppermute | solution.py:95
  12.2 0.6 %collective-permute-start.2 = (bf16[5,64,512]{2,1,0:T(8,128)(2,1)S(1)}, bf16[5,64,512]{2,1,0:T(8,128)(2,1)S(1)}, u32[]{:S(2)}, u32[]{:S(2)}) collective-permute-start(bf16[5,64,512]{2,1,0:T(8,128)(2,1)S(1)} %collective-permute-done.1.mine_ref), channel_id=1, source_target_pairs={{0,4},{4,0},{1,5},{5,1},{2,6},{6,2},{3,7},{7,3},{8,12},{12,8},{9,1... | collective-permute-start | bytes 983048 | tf_op jit(solution)/shard_map/ppermute | solution.py:51
  12.9 1.3 %collective-permute-start.3 = (bf16[512,256]{1,0:T(8,128)(2,1)S(1)}, bf16[512,256]{1,0:T(8,128)(2,1)S(1)}, u32[]{:S(2)}, u32[]{:S(2)}) collective-permute-start(bf16[512,256]{1,0:T(8,128)(2,1)S(1)} %get-tuple-element.41.end_ref), channel_id=1, source_target_pairs={{0,8},{8,0},{16,24},{4,20},{12,28},{1,9},{9,1},{17,25},{5,21},{13,... | collective-permute-start | bytes 786440 | tf_op jit(solution)/shard_map/ppermute | solution.py:344
  14.2 0.0 collective-permute-done.2.theirs_ref
  14.2 0.2 shard_map.68
  14.3 0.0 copy-start.5
  14.4 1.0 %shard_map.69 = (f32[2,32,16,256]{3,2,1,0:T(8,128)S(1)}, f32[2,64,256]{2,1,0:T(8,128)S(1)}, f32[2,128,256]{2,1,0:T(8,128)S(1)}, bf16[640,256]{1,0:T(8,128)(2,1)S(1)}) custom-call(bf16[256,1536]{1,0:T(8,128)(2,1)S(1)} %get-tuple-element.37.lhs_ref, bf16[3,3,512,512]{3,2,1,0:T(8,128)(2,1)S(1)} %copy-done.1, ...), custom_call_target="tpu_custom_call" | custom-call | flops 603979776 | bytes 9635840 | tf_op jit(solution)/shard_map/pallas_call | solution.py:21
  15.4 1.3 %collective-permute-start.5 = (bf16[640,256]{1,0:T(8,128)(2,1)S(1)}, bf16[640,256]{1,0:T(8,128)(2,1)S(1)}, u32[]{:S(2)}, u32[]{:S(2)}) collective-permute-start(bf16[640,256]{1,0:T(8,128)(2,1)S(1)} %get-tuple-element.42.end_ref), channel_id=1, source_target_pairs={{0,8},{8,0},{16,24},{4,20},{12,28},{1,9},{9,1},{17,25},{5,21},{13,... | collective-permute-start | bytes 983048 | tf_op jit(solution)/shard_map/ppermute | solution.py:344
  16.7 3.6 %collective-permute-done.3.got_ref.refs_4_.refs_7_ = bf16[512,256]{1,0:T(8,128)(2,1)S(1)} collective-permute-done((bf16[512,256]{1,0:T(8,128)(2,1)S(1)}, bf16[512,256]{1,0:T(8,128)(2,1)S(1)}, u32[]{:S(2)}, u32[]{:S(2)}) %collective-permute-start.3) | collective-permute-done | bytes 262176 | tf_op jit(solution)/shard_map/ppermute | solution.py:344
  20.3 0.0 slice-start
  20.3 0.2 shard_map.70
  20.4 2.2 %collective-permute-start.4 = (bf16[512,256]{1,0:T(8,128)(2,1)S(1)}, bf16[512,256]{1,0:T(8,128)(2,1)S(1)}, u32[]{:S(2)}, u32[]{:S(2)}) collective-permute-start(bf16[512,256]{1,0:T(8,128)(2,1)S(1)} %shard_map.70), channel_id=1, source_target_pairs={{0,16},{8,24},{4,12},{20,28},{28,20},{1,17},{9,25},{5,13},{21,29},... | collective-permute-start | bytes 786440 | tf_op jit(solution)/shard_map/ppermute | solution.py:347
  22.6 1.1 %collective-permute-done.5.got_ref.refs_6_.refs_9_.refs_5_ = bf16[640,256]{1,0:T(8,128)(2,1)S(1)} collective-permute-done((bf16[640,256]{1,0:T(8,128)(2,1)S(1)}, bf16[640,256]{1,0:T(8,128)(2,1)S(1)}, u32[]{:S(2)}, u32[]{:S(2)}) %collective-permute-start.5) | collective-permute-done | bytes 327712 | tf_op jit(solution)/shard_map/ppermute | solution.py:344
  23.8 0.2 shard_map.71
  24.0 2.4 %collective-permute-start.6 = (bf16[640,256]{1,0:T(8,128)(2,1)S(1)}, bf16[640,256]{1,0:T(8,128)(2,1)S(1)}, u32[]{:S(2)}, u32[]{:S(2)}) collective-permute-start(bf16[640,256]{1,0:T(8,128)(2,1)S(1)} %shard_map.71), channel_id=1, source_target_pairs={{0,16},{8,24},{4,12},{20,28},{28,20},{1,17},{9,25},{5,13},{21,29},... | collective-permute-start | bytes 983048 | tf_op jit(solution)/shard_map/ppermute | solution.py:347
  26.4 1.7 %collective-permute-done.4.refs_5_.refs_8_ = bf16[512,256]{1,0:T(8,128)(2,1)S(1)} collective-permute-done((bf16[512,256]{1,0:T(8,128)(2,1)S(1)}, bf16[512,256]{1,0:T(8,128)(2,1)S(1)}, u32[]{:S(2)}, u32[]{:S(2)}) %collective-permute-start.4) | collective-permute-done | bytes 262176 | tf_op jit(solution)/shard_map/ppermute | solution.py:347
  28.1 0.0 copy-done.5
  28.1 0.0 slice-start.1
  28.2 1.8 %collective-permute-start.7 = (bf16[2,16,256]{2,1,0:T(8,128)(2,1)S(1)}, bf16[2,16,256]{2,1,0:T(8,128)(2,1)S(1)}, u32[]{:S(2)}, u32[]{:S(2)}) collective-permute-start(bf16[2,16,256]{2,1,0:T(8,128)(2,1)S(1)} %shard_map.73), channel_id=1, source_target_pairs={{0,4},{4,0},{1,5},{5,1},{2,6},{6,2},{3,7},{7,3},{8,12},{12,8},{9,1... | collective-permute-start | bytes 49160 | tf_op jit(solution)/shard_map/ppermute | solution.py:51
  30.0 0.6 %shard_map.72._ = bf16[1024,768]{1,0:T(8,128)(2,1)S(1)} custom-call(f32[2,32,16,512]{3,2,1,0:T(8,128)S(1)} %get-tuple-element.38.total_ref.refs_0_, f32[32,16,512]{2,1,0:T(8,128)S(1)} %copy-done, s32[1,512]{1,0:T(1,128)S(1)} %bitcast.10, f32[1,512]{1,0:T(1,128)S(1)} %bitcast.15, bf16[512,256]{1,0:T(8,128)(2,1)S(1)} %collective-permute-done.3.got_ref.refs_4_.refs_7_, ...), custom_call_target="tpu_custom_call" | custom-call | bytes 5246976 | tf_op jit(solution)/shard_map/pallas_call | solution.py:21
  30.6 0.2 collective-permute-done.7.got_ref
  30.8 0.0 slice-done
  30.8 0.0 slice-done.1
  30.8 1.4 %shard_map.74 = (f32[2,32,16,256]{3,2,1,0:T(8,128)S(1)}, bf16[1024,768]{1,0:T(8,128)(2,1)S(1)}) custom-call(bf16[1024,768]{1,0:T(8,128)(2,1)S(1)} %shard_map.72._, bf16[2,16,256]{2,1,0:T(8,128)(2,1)S(1)} %collective-permute-done.7.got_ref, bf16[3,3,512,512]{3,2,1,0:T(8,128)(2,1)S(1)} %bitcast.4), custom_call_target="tpu_custom_call", output_to_operand_aliasing={{1}: (0, {})} | custom-call | flops 1207959552 | bytes 8929280 | tf_op jit(solution)/shard_map/pallas_call | solution.py:21
  32.2 1.4 %shard_map.75.refs_1_ = f32[2,32,16,256]{3,2,1,0:T(8,128)S(1)} custom-call(bf16[1024,768]{1,0:T(8,128)(2,1)S(1)} %get-tuple-element.44.lhs_ref, bf16[3,3,512,512]{3,2,1,0:T(8,128)(2,1)S(1)} %bitcast.4), custom_call_target="tpu_custom_call" | custom-call | flops 1207959552 | bytes 7340032 | tf_op jit(solution)/shard_map/pallas_call | solution.py:21
  33.6 0.1 shard_map.77.refs_4_.refs_2_
  33.7 0.0 collective-permute-done.6.refs_7_.refs_10_.refs_6_
  33.7 0.1 shard_map.78
  33.8 0.4 %collective-permute-start.8 = (bf16[2,32,256]{2,1,0:T(8,128)(2,1)S(1)}, bf16[2,32,256]{2,1,0:T(8,128)(2,1)S(1)}, u32[]{:S(2)}, u32[]{:S(2)}) collective-permute-start(bf16[2,32,256]{2,1,0:T(8,128)(2,1)S(1)} %shard_map.78), channel_id=1, source_target_pairs={{0,4},{4,0},{1,5},{5,1},{2,6},{6,2},{3,7},{7,3},{8,12},{12,8},{9,1... | collective-permute-start | bytes 98312 | tf_op jit(solution)/shard_map/ppermute | solution.py:51
  34.3 0.4 shard_map.79
  34.6 0.7 %shard_map.76._ = bf16[1152,768]{1,0:T(8,128)(2,1)S(1)} custom-call(f32[2,32,16,256]{3,2,1,0:T(8,128)S(1)} %get-tuple-element.40.refs_0_, f32[32,16,512]{2,1,0:T(8,128)S(1)} %copy-done, s32[1,512]{1,0:T(1,128)S(1)} %bitcast.13, f32[1,512]{1,0:T(1,128)S(1)} %bitcast.18, bf16[512,256]{1,0:T(8,128)(2,1)S(1)} %collective-permute-done.3.got_ref.refs_4_.refs_7_, ...), custom_call_target="tpu_custom_call" | custom-call | bytes 5050368 | tf_op jit(solution)/shard_map/pallas_call | solution.py:21
  35.4 0.0 collective-permute-done.8.got_ref
  35.4 4.3 %shard_map.80 = (bf16[2,32,16,512]{3,2,1,0:T(8,128)(2,1)}, bf16[1152,768]{1,0:T(8,128)(2,1)S(1)}) custom-call(bf16[1152,768]{1,0:T(8,128)(2,1)S(1)} %shard_map.76._, bf16[2,32,256]{2,1,0:T(8,128)(2,1)S(1)} %collective-permute-done.8.got_ref, bf16[2,64,256]{2,1,0:T(8,128)(2,1)S(1)} %get-tuple-element.50.beside_ref, ...), custom_call_target="tpu_custom_call", output_to_operand_aliasing={{1}: (0, {})} | custom-call | flops 2415919104 | bytes 11632640 | tf_op jit(solution)/shard_map/pallas_call | solution.py:21
  (4 shorter events, 0.1 us)
Async XLA Ops:
  0.0 1.7 %copy-start = (f32[32,16,512]{2,1,0:T(8,128)S(1)}, f32[32,16,512]{2,1,0:T(8,128)}, u32[]{:S(2)}) copy-start(f32[32,16,512]{2,1,0:T(8,128)} %refs_3_.1) | copy-start | bytes 3145732
  0.0 1.3 %copy-start.2 = (bf16[2,32,16,512]{3,2,1,0:T(8,128)(2,1)S(1)}, bf16[2,32,16,512]{3,2,1,0:T(8,128)(2,1)}, u32[]{:S(2)}) copy-start(bf16[2,32,16,512]{3,2,1,0:T(8,128)(2,1)} %cells_ref.3) | copy-start | bytes 3145732
  1.7 1.2 %copy-start.3 = (bf16[2,32,16,512]{3,2,1,0:T(8,128)(2,1)S(1)}, bf16[2,32,16,512]{3,2,1,0:T(8,128)(2,1)}, u32[]{:S(2)}) copy-start(bf16[2,32,16,512]{3,2,1,0:T(8,128)(2,1)} %cells_ref.3) | copy-start | bytes 3145732
  2.0 4.2 %copy-start.1 = (bf16[3,3,512,512]{3,2,1,0:T(8,128)(2,1)S(1)}, bf16[3,3,512,512]{3,2,1,0:T(8,128)(2,1)}, u32[]{:S(2)}) copy-start(bf16[3,3,512,512]{3,2,1,0:T(8,128)(2,1)} %weight_ref.6) | copy-start | bytes 14155780
  2.0 4.2 %copy-start.4 = (s32[512]{0:T(512)S(1)}, s32[512]{0:T(512)}, u32[]{:S(2)}) copy-start(s32[512]{0:T(512)} %param.9) | copy-start | bytes 6148
  2.0 1.8 %collective-permute-start = (bf16[192,512]{1,0:T(8,128)(2,1)S(1)}, bf16[192,512]{1,0:T(8,128)(2,1)S(1)}, u32[]{:S(2)}, u32[]{:S(2)}) collective-permute-start(bf16[192,512]{1,0:T(8,128)(2,1)S(1)} %get-tuple-element.33), channel_id=1, source_target_pairs={{0,4},{4,0},{1,5},{5,1},{2,6},{6,2},{3,7},{7,3},{8,12},{12,8},{9,1... | collective-permute-start | bytes 589832 | tf_op jit(solution)/shard_map/ppermute | solution.py:51
  3.8 8.4 %collective-permute-start.1 = (bf16[5,64,512]{2,1,0:T(8,128)(2,1)S(1)}, bf16[5,64,512]{2,1,0:T(8,128)(2,1)S(1)}, u32[]{:S(2)}, u32[]{:S(2)}) collective-permute-start(bf16[5,64,512]{2,1,0:T(8,128)(2,1)S(1)} %pad_maximum_fusion), channel_id=1, source_target_pairs={{0,5},{1,6},{2,7},{5,0},{6,1},{7,2},{8,13},{9,14},{10,15},{13,8},{... | collective-permute-start | bytes 983048 | tf_op jit(solution)/shard_map/ppermute | solution.py:95
  12.2 1.9 %collective-permute-start.2 = (bf16[5,64,512]{2,1,0:T(8,128)(2,1)S(1)}, bf16[5,64,512]{2,1,0:T(8,128)(2,1)S(1)}, u32[]{:S(2)}, u32[]{:S(2)}) collective-permute-start(bf16[5,64,512]{2,1,0:T(8,128)(2,1)S(1)} %collective-permute-done.1.mine_ref), channel_id=1, source_target_pairs={{0,4},{4,0},{1,5},{5,1},{2,6},{6,2},{3,7},{7,3},{8,12},{12,8},{9,1... | collective-permute-start | bytes 983048 | tf_op jit(solution)/shard_map/ppermute | solution.py:51
  12.9 7.4 %collective-permute-start.3 = (bf16[512,256]{1,0:T(8,128)(2,1)S(1)}, bf16[512,256]{1,0:T(8,128)(2,1)S(1)}, u32[]{:S(2)}, u32[]{:S(2)}) collective-permute-start(bf16[512,256]{1,0:T(8,128)(2,1)S(1)} %get-tuple-element.41.end_ref), channel_id=1, source_target_pairs={{0,8},{8,0},{16,24},{4,20},{12,28},{1,9},{9,1},{17,25},{5,21},{13,... | collective-permute-start | bytes 786440 | tf_op jit(solution)/shard_map/ppermute | solution.py:344
  14.3 13.8 %copy-start.5 = (f32[512]{0:T(512)S(1)}, f32[512]{0:T(512)}, u32[]{:S(2)}) copy-start(f32[512]{0:T(512)} %param.10) | copy-start | bytes 6148
  15.4 8.4 %collective-permute-start.5 = (bf16[640,256]{1,0:T(8,128)(2,1)S(1)}, bf16[640,256]{1,0:T(8,128)(2,1)S(1)}, u32[]{:S(2)}, u32[]{:S(2)}) collective-permute-start(bf16[640,256]{1,0:T(8,128)(2,1)S(1)} %get-tuple-element.42.end_ref), channel_id=1, source_target_pairs={{0,8},{8,0},{16,24},{4,20},{12,28},{1,9},{9,1},{17,25},{5,21},{13,... | collective-permute-start | bytes 983048 | tf_op jit(solution)/shard_map/ppermute | solution.py:344
  20.3 10.6 %slice-start = ((s8[4718592]{0:T(1024)(128)(4,1)}), s8[4194304]{0:T(1024)(128)(4,1)S(1)}, s32[]{:S(2)}) async-start(s8[4718592]{0:T(1024)(128)(4,1)} %bitcast.3), calls=%async_computation | async-start | bytes 8388608
  20.4 7.7 %collective-permute-start.4 = (bf16[512,256]{1,0:T(8,128)(2,1)S(1)}, bf16[512,256]{1,0:T(8,128)(2,1)S(1)}, u32[]{:S(2)}, u32[]{:S(2)}) collective-permute-start(bf16[512,256]{1,0:T(8,128)(2,1)S(1)} %shard_map.70), channel_id=1, source_target_pairs={{0,16},{8,24},{4,12},{20,28},{28,20},{1,17},{9,25},{5,13},{21,29},... | collective-permute-start | bytes 786440 | tf_op jit(solution)/shard_map/ppermute | solution.py:347
  24.0 9.7 %collective-permute-start.6 = (bf16[640,256]{1,0:T(8,128)(2,1)S(1)}, bf16[640,256]{1,0:T(8,128)(2,1)S(1)}, u32[]{:S(2)}, u32[]{:S(2)}) collective-permute-start(bf16[640,256]{1,0:T(8,128)(2,1)S(1)} %shard_map.71), channel_id=1, source_target_pairs={{0,16},{8,24},{4,12},{20,28},{28,20},{1,17},{9,25},{5,13},{21,29},... | collective-permute-start | bytes 983048 | tf_op jit(solution)/shard_map/ppermute | solution.py:347
  28.1 2.7 %slice-start.1 = ((s8[4718592]{0:T(1024)(128)(4,1)}), s8[524288]{0:T(1024)(128)(4,1)S(1)}, s32[]{:S(2)}) async-start(s8[4718592]{0:T(1024)(128)(4,1)} %bitcast.3), calls=%async_computation.1 | async-start | bytes 1048576
  28.2 2.6 %collective-permute-start.7 = (bf16[2,16,256]{2,1,0:T(8,128)(2,1)S(1)}, bf16[2,16,256]{2,1,0:T(8,128)(2,1)S(1)}, u32[]{:S(2)}, u32[]{:S(2)}) collective-permute-start(bf16[2,16,256]{2,1,0:T(8,128)(2,1)S(1)} %shard_map.73), channel_id=1, source_target_pairs={{0,4},{4,0},{1,5},{5,1},{2,6},{6,2},{3,7},{7,3},{8,12},{12,8},{9,1... | collective-permute-start | bytes 49160 | tf_op jit(solution)/shard_map/ppermute | solution.py:51
  33.8 1.5 %collective-permute-start.8 = (bf16[2,32,256]{2,1,0:T(8,128)(2,1)S(1)}, bf16[2,32,256]{2,1,0:T(8,128)(2,1)S(1)}, u32[]{:S(2)}, u32[]{:S(2)}) collective-permute-start(bf16[2,32,256]{2,1,0:T(8,128)(2,1)S(1)} %shard_map.78), channel_id=1, source_target_pairs={{0,4},{4,0},{1,5},{5,1},{2,6},{6,2},{3,7},{7,3},{8,12},{12,8},{9,1... | collective-permute-start | bytes 98312 | tf_op jit(solution)/shard_map/ppermute | solution.py:51

commit v18 on v17

--- a/solution.py
+++ b/solution.py
@@ -128,31 +128,6 @@
 
 
 SLAB = 8
-
-
-def add_columns(cells, columns):
-    rows, cols, wide = cells.shape
-    col = lax.broadcasted_iota(jnp.int32, (rows, SLAB, wide), 1)
-
-    def slab(start):
-        total = 0.0
-        for at, column in columns:
-            if start <= at < start + SLAB:
-                total = jnp.where(col == at - start, column, total)
-        return cells[:, start : start + SLAB] + total
-
-    middle = [cells[:, SLAB : cols - SLAB]] if cols > 2 * SLAB else []
-    return jnp.concatenate([slab(0), *middle, slab(cols - SLAB)], axis=1)
-
-
-def with_column(cells, at, column):
-    rows, cols, wide = cells.shape
-    start = 0 if at == 0 else cols - SLAB
-    col = lax.broadcasted_iota(jnp.int32, (rows, SLAB, wide), 1)
-    slab = jnp.where(col == at - start, column, cells[:, start : start + SLAB])
-    if at == 0:
-        return jnp.concatenate([slab, cells[:, SLAB:]], axis=1)
-    return jnp.concatenate([cells[:, :start], slab], axis=1)
 
 
 def halves(channels):
@@ -188,15 +163,20 @@
             total = dot(cells, weight_ref, 1, lanes).reshape(tile)
             first = dot(cells, weight_ref, 0, lanes).reshape(tile)
             spill_ref[1, here, lanes] = first[:, cols - 1, :]
-            total += with_column(pltpu.roll(first, 1, 1), 0, 0.0)
+            total += jnp.where(col == 0, 0.0, pltpu.roll(first, 1, 1))
             last = dot(cells, weight_ref, 2, lanes).reshape(tile)
             spill_ref[0, here, lanes] = last[:, 0, :]
-            total += with_column(pltpu.roll(last, cols - 1, 1), cols - 1, 0.0)
+            total += jnp.where(col == cols - 1, 0.0, pltpu.roll(last, cols - 1, 1))
             total_ref[frame, :, :, lanes] = total
             totals.append(total)
         states.append(end_state(totals, pole_ref, lanes))
-    state = jnp.where(col == 0, pltpu.roll(states[1], cols - 1, 1), states[0])
-    state = jnp.where(col == cols - 1, pltpu.roll(states[1], 1, 1), state)
+    state, other = states
+    col = lax.broadcasted_iota(jnp.int32, (rows, SLAB, state.shape[2]), 1)
+    last = slice(cols - SLAB, cols)
+    left = jnp.where(col == 0, pltpu.roll(other[:, :SLAB], SLAB - 1, 1), state[:, :SLAB])
+    right = jnp.where(col == SLAB - 1, pltpu.roll(other[:, last], 1, 1), state[:, last])
+    middle = [state[:, SLAB : cols - SLAB]] if cols > 2 * SLAB else []
+    state = jnp.concatenate([left, *middle, right], axis=1)
     end_ref[...] = state.reshape(end_ref.shape).astype(end_ref.dtype)
 
 
@@ -537,6 +517,7 @@
 def tile_sum(tile, inputs, lanes, room, lhs_ref, weight_ref):
     count, rows, cols, wide = tile
     size = rows * cols
+    col = lax.broadcasted_iota(jnp.int32, tile[1:], 1)
 
     def beside(cells):
         return cells.reshape(rows, 1, wide) if room else 0.0
@@ -547,10 +528,10 @@
         total = dot(lhs_ref[at + room : end], weight_ref, 1, lanes, inputs).reshape(tile[1:])
         first = dot(lhs_ref[at:end], weight_ref, 0, lanes, inputs)
         shifted = pltpu.roll(first[room:].reshape(tile[1:]), 1, 1)
-        total += with_column(shifted, 0, beside(first[:room]))
+        total += jnp.where(col == 0, beside(first[:room]), shifted)
         last = dot(lhs_ref[at + room : end + room], weight_ref, 2, lanes, inputs)
         shifted = pltpu.roll(last[:size].reshape(tile[1:]), cols - 1, 1)
-        yield total + with_column(shifted, cols - 1, beside(last[size:]))
+        yield total + jnp.where(col == cols - 1, beside(last[size:]), shifted)
 
 
 def strip_sum(tile, inputs, lanes, lhs_ref, weight_ref):
@@ -559,13 +540,16 @@
     first = dot(lhs_ref[: 2 * room], weight_ref, 0, lanes, inputs)
     middle = dot(lhs_ref[room : 3 * room], weight_ref, 1, lanes, inputs)
     last = dot(lhs_ref[2 * room :], weight_ref, 2, lanes, inputs)
-    columns = [
+    col = lax.broadcasted_iota(jnp.int32, tile, 2)
+    total = 0.0
+    for at, cells in (
         (0, first[:room] + middle[:room]),
         (1, first[room:]),
         (cols - 2, last[:room]),
         (cols - 1, middle[room:] + last[room:]),
-    ]
-    return [(at, cells.reshape(count, rows, 1, wide)) for at, cells in columns]
+    ):
+        total = jnp.where(col == at, cells.reshape(count, rows, 1, wide), total)
+    return total
 
 
 def opening_kernel(inputs, lanes, _, got_ref, weight_ref, out_ref, lhs_ref):
@@ -603,11 +587,10 @@
 
     for part, lanes in enumerate(parts):
         tile = (count, rows, cols, lanes.stop - lanes.start)
-        columns = strip_sum(tile, parts[0], lanes, strip_lhs_ref, weight_ref)
+        strips = strip_sum(tile, parts[0], lanes, strip_lhs_ref, weight_ref)
         tiles = tile_sum(tile, parts[1], lanes, rows, lhs_ref, weight_ref)
         for frame, total in enumerate(tiles):
-            total += before_refs[part][frame]
-            total = add_columns(total, [(at, cells[frame]) for at, cells in columns])
+            total += before_refs[part][frame] + strips[frame]
             held_ref[frame, :, :, lanes] = total.astype(held_ref.dtype)
             store(frame, part).start()
     for part in range(len(parts)):

time: 40 us -> 40 us (level)
  no operation moved by 1% of the time
where the time goes in v18:
time: 40 us; the launch traced here: 39.7 us
  Pallas kernels  16.6 us (42%)
  starting transfers between devices  13 us (32%)
  waiting for transfers between devices  8.13 us (20%)
  local copies, waits for them, and re-layouts  1.51 us (4%)
  between operations  0.4 us (1%)
    pallas_call x17, Pallas kernels, call(): pl.pallas_call(kernel, in_specs=[WHOLE] * len(args), out_specs=out_specs...  16.6 us
    ppermute x2, waiting for transfers between devices, exchange_four(): got = lax.ppermute(end, axes, first_round)  4.7 us
    ppermute x2, starting transfers between devices, exchange_four(): arrivals.append((got, lax.ppermute(relayed, axes, second_round)))  4.6 us
    ppermute x4, starting transfers between devices, swap_cores(): return lax.ppermute(array, 'sx', [(0, 1), (1, 0)])  3.53 us
    ppermute x2, starting transfers between devices, exchange_four(): got = lax.ppermute(end, axes, first_round)  2.57 us
    ppermute x1, starting transfers between devices, trade_columns(): return (got, lax.ppermute(columns, ('sx', 'sy'), pairs))  2.33 us
    ppermute x2, waiting for transfers between devices, exchange_four(): arrivals.append((got, lax.ppermute(relayed, axes, second_round)))  1.73 us
    unnamed x16, local copies, waits for them, and re-layouts  1.5 us
  transfers between devices with their start and end apart: 9, of which 6 were waited for; matrix products, arithmetic and copies ran while one was open for 0% of the time, Pallas kernels for 29%

profile of v18, /device:TPU:23, one launch (start us, length us, event | category | flops | bytes accessed | tf_op | source)
XLA Modules:
  0.0 39.7 jit_solution(8801082812170826636)
XLA Ops:
  0.0 0.0 copy-start
  0.0 0.0 copy-start.2
  0.0 1.3 %copy-done.2 = bf16[2,32,16,512]{3,2,1,0:T(8,128)(2,1)S(1)} copy-done((bf16[2,32,16,512]{3,2,1,0:T(8,128)(2,1)S(1)}, bf16[2,32,16,512]{3,2,1,0:T(8,128)(2,1)}, u32[]{:S(2)}) %copy-start.2) | copy-done | bytes 1048600
  1.3 0.3 shard_map.64
  1.7 0.0 copy-start.3
  1.7 0.0 copy-done
  1.7 0.3 shard_map.65
  2.0 0.0 copy-start.1
  2.0 0.0 copy-start.4
  2.0 0.7 %collective-permute-start = (bf16[192,512]{1,0:T(8,128)(2,1)S(1)}, bf16[192,512]{1,0:T(8,128)(2,1)S(1)}, u32[]{:S(2)}, u32[]{:S(2)}) collective-permute-start(bf16[192,512]{1,0:T(8,128)(2,1)S(1)} %get-tuple-element.33), channel_id=1, source_target_pairs={{0,4},{4,0},{1,5},{5,1},{2,6},{6,2},{3,7},{7,3},{8,12},{12,8},{9,1... | collective-permute-start | bytes 589832 | tf_op jit(solution)/shard_map/ppermute | solution.py:51
  2.7 0.2 copy-done.3
  2.9 0.2 shard_map.66._
  3.1 0.7 %collective-permute-done.got_ref = bf16[192,512]{1,0:T(8,128)(2,1)S(1)} collective-permute-done((bf16[192,512]{1,0:T(8,128)(2,1)S(1)}, bf16[192,512]{1,0:T(8,128)(2,1)S(1)}, u32[]{:S(2)}, u32[]{:S(2)}) %collective-permute-start) | collective-permute-done | bytes 196640 | tf_op jit(solution)/shard_map/ppermute | solution.py:51
  3.8 2.3 %collective-permute-start.1 = (bf16[5,64,512]{2,1,0:T(8,128)(2,1)S(1)}, bf16[5,64,512]{2,1,0:T(8,128)(2,1)S(1)}, u32[]{:S(2)}, u32[]{:S(2)}) collective-permute-start(bf16[5,64,512]{2,1,0:T(8,128)(2,1)S(1)} %pad_maximum_fusion), channel_id=1, source_target_pairs={{0,5},{1,6},{2,7},{5,0},{6,1},{7,2},{8,13},{9,14},{10,15},{13,8},{... | collective-permute-start | bytes 983048 | tf_op jit(solution)/shard_map/ppermute | solution.py:95
  6.2 0.0 copy-done.1
  6.2 0.0 copy-done.4
  6.2 5.3 %shard_map.67 = (f32[2,32,16,512]{3,2,1,0:T(8,128)S(1)}, f32[2,64,512]{2,1,0:T(8,128)S(1)}, bf16[512,256]{1,0:T(8,128)(2,1)S(1)}, bf16[1024,1536]{1,0:T(8,128)(2,1)S(1)}) custom-call(bf16[1024,1536]{1,0:T(8,128)(2,1)S(1)} %shard_map.66._, bf16[192,512]{1,0:T(8,128)(2,1)S(1)} %collective-permute-done.got_ref, ...), custom_call_target="tpu_custom_call", output_to_operand_aliasing={{3}: (0, {})} | custom-call | flops 4831838208 | bytes 13830144 | tf_op jit(solution)/shard_map/pallas_call | solution.py:21
  11.5 0.8 %collective-permute-done.1.mine_ref = bf16[5,64,512]{2,1,0:T(8,128)(2,1)S(1)} collective-permute-done((bf16[5,64,512]{2,1,0:T(8,128)(2,1)S(1)}, bf16[5,64,512]{2,1,0:T(8,128)(2,1)S(1)}, u32[]{:S(2)}, u32[]{:S(2)}) %collective-permute-start.1) | collective-permute-done | bytes 327712 | tf_op jit(solution)/shard_map/ppermute | solution.py:95
  12.2 0.6 %collective-permute-start.2 = (bf16[5,64,512]{2,1,0:T(8,128)(2,1)S(1)}, bf16[5,64,512]{2,1,0:T(8,128)(2,1)S(1)}, u32[]{:S(2)}, u32[]{:S(2)}) collective-permute-start(bf16[5,64,512]{2,1,0:T(8,128)(2,1)S(1)} %collective-permute-done.1.mine_ref), channel_id=1, source_target_pairs={{0,4},{4,0},{1,5},{5,1},{2,6},{6,2},{3,7},{7,3},{8,12},{12,8},{9,1... | collective-permute-start | bytes 983048 | tf_op jit(solution)/shard_map/ppermute | solution.py:51
  12.8 1.3 %collective-permute-start.3 = (bf16[512,256]{1,0:T(8,128)(2,1)S(1)}, bf16[512,256]{1,0:T(8,128)(2,1)S(1)}, u32[]{:S(2)}, u32[]{:S(2)}) collective-permute-start(bf16[512,256]{1,0:T(8,128)(2,1)S(1)} %get-tuple-element.41.end_ref), channel_id=1, source_target_pairs={{0,8},{8,0},{16,24},{4,20},{12,28},{1,9},{9,1},{17,25},{5,21},{13,... | collective-permute-start | bytes 786440 | tf_op jit(solution)/shard_map/ppermute | solution.py:324
  14.1 0.0 collective-permute-done.2.theirs_ref
  14.1 0.2 shard_map.68
  14.3 0.0 copy-start.5
  14.3 1.0 %shard_map.69 = (f32[2,32,16,256]{3,2,1,0:T(8,128)S(1)}, f32[2,64,256]{2,1,0:T(8,128)S(1)}, f32[2,128,256]{2,1,0:T(8,128)S(1)}, bf16[640,256]{1,0:T(8,128)(2,1)S(1)}) custom-call(bf16[256,1536]{1,0:T(8,128)(2,1)S(1)} %get-tuple-element.37.lhs_ref, bf16[3,3,512,512]{3,2,1,0:T(8,128)(2,1)S(1)} %copy-done.1, ...), custom_call_target="tpu_custom_call" | custom-call | flops 603979776 | bytes 9635840 | tf_op jit(solution)/shard_map/pallas_call | solution.py:21
  15.4 1.3 %collective-permute-start.5 = (bf16[640,256]{1,0:T(8,128)(2,1)S(1)}, bf16[640,256]{1,0:T(8,128)(2,1)S(1)}, u32[]{:S(2)}, u32[]{:S(2)}) collective-permute-start(bf16[640,256]{1,0:T(8,128)(2,1)S(1)} %get-tuple-element.42.end_ref), channel_id=1, source_target_pairs={{0,8},{8,0},{16,24},{4,20},{12,28},{1,9},{9,1},{17,25},{5,21},{13,... | collective-permute-start | bytes 983048 | tf_op jit(solution)/shard_map/ppermute | solution.py:324
  16.7 3.6 %collective-permute-done.3.got_ref.refs_4_.refs_7_ = bf16[512,256]{1,0:T(8,128)(2,1)S(1)} collective-permute-done((bf16[512,256]{1,0:T(8,128)(2,1)S(1)}, bf16[512,256]{1,0:T(8,128)(2,1)S(1)}, u32[]{:S(2)}, u32[]{:S(2)}) %collective-permute-start.3) | collective-permute-done | bytes 262176 | tf_op jit(solution)/shard_map/ppermute | solution.py:324
  20.2 0.0 slice-start
  20.2 0.2 shard_map.70
  20.4 2.2 %collective-permute-start.4 = (bf16[512,256]{1,0:T(8,128)(2,1)S(1)}, bf16[512,256]{1,0:T(8,128)(2,1)S(1)}, u32[]{:S(2)}, u32[]{:S(2)}) collective-permute-start(bf16[512,256]{1,0:T(8,128)(2,1)S(1)} %shard_map.70), channel_id=1, source_target_pairs={{0,16},{8,24},{4,12},{20,28},{28,20},{1,17},{9,25},{5,13},{21,29},... | collective-permute-start | bytes 786440 | tf_op jit(solution)/shard_map/ppermute | solution.py:327
  22.6 1.1 %collective-permute-done.5.got_ref.refs_6_.refs_9_.refs_5_ = bf16[640,256]{1,0:T(8,128)(2,1)S(1)} collective-permute-done((bf16[640,256]{1,0:T(8,128)(2,1)S(1)}, bf16[640,256]{1,0:T(8,128)(2,1)S(1)}, u32[]{:S(2)}, u32[]{:S(2)}) %collective-permute-start.5) | collective-permute-done | bytes 327712 | tf_op jit(solution)/shard_map/ppermute | solution.py:324
  23.7 0.2 shard_map.71
  23.9 2.4 %collective-permute-start.6 = (bf16[640,256]{1,0:T(8,128)(2,1)S(1)}, bf16[640,256]{1,0:T(8,128)(2,1)S(1)}, u32[]{:S(2)}, u32[]{:S(2)}) collective-permute-start(bf16[640,256]{1,0:T(8,128)(2,1)S(1)} %shard_map.71), channel_id=1, source_target_pairs={{0,16},{8,24},{4,12},{20,28},{28,20},{1,17},{9,25},{5,13},{21,29},... | collective-permute-start | bytes 983048 | tf_op jit(solution)/shard_map/ppermute | solution.py:327
  26.3 1.7 %collective-permute-done.4.refs_5_.refs_8_ = bf16[512,256]{1,0:T(8,128)(2,1)S(1)} collective-permute-done((bf16[512,256]{1,0:T(8,128)(2,1)S(1)}, bf16[512,256]{1,0:T(8,128)(2,1)S(1)}, u32[]{:S(2)}, u32[]{:S(2)}) %collective-permute-start.4) | collective-permute-done | bytes 262176 | tf_op jit(solution)/shard_map/ppermute | solution.py:327
  28.1 0.0 copy-done.5
  28.1 0.0 slice-start.1
  28.1 1.8 %collective-permute-start.7 = (bf16[2,16,256]{2,1,0:T(8,128)(2,1)S(1)}, bf16[2,16,256]{2,1,0:T(8,128)(2,1)S(1)}, u32[]{:S(2)}, u32[]{:S(2)}) collective-permute-start(bf16[2,16,256]{2,1,0:T(8,128)(2,1)S(1)} %shard_map.73), channel_id=1, source_target_pairs={{0,4},{4,0},{1,5},{5,1},{2,6},{6,2},{3,7},{7,3},{8,12},{12,8},{9,1... | collective-permute-start | bytes 49160 | tf_op jit(solution)/shard_map/ppermute | solution.py:51
  29.9 0.6 %shard_map.72._ = bf16[1024,768]{1,0:T(8,128)(2,1)S(1)} custom-call(f32[2,32,16,512]{3,2,1,0:T(8,128)S(1)} %get-tuple-element.38.total_ref.refs_0_, f32[32,16,512]{2,1,0:T(8,128)S(1)} %copy-done, s32[1,512]{1,0:T(1,128)S(1)} %bitcast.10, f32[1,512]{1,0:T(1,128)S(1)} %bitcast.15, bf16[512,256]{1,0:T(8,128)(2,1)S(1)} %collective-permute-done.3.got_ref.refs_4_.refs_7_, ...), custom_call_target="tpu_custom_call" | custom-call | bytes 5246976 | tf_op jit(solution)/shard_map/pallas_call | solution.py:21
  30.5 0.2 collective-permute-done.7.got_ref
  30.8 0.0 slice-done
  30.8 0.0 slice-done.1
  30.8 1.4 %shard_map.74 = (f32[2,32,16,256]{3,2,1,0:T(8,128)S(1)}, bf16[1024,768]{1,0:T(8,128)(2,1)S(1)}) custom-call(bf16[1024,768]{1,0:T(8,128)(2,1)S(1)} %shard_map.72._, bf16[2,16,256]{2,1,0:T(8,128)(2,1)S(1)} %collective-permute-done.7.got_ref, bf16[3,3,512,512]{3,2,1,0:T(8,128)(2,1)S(1)} %bitcast.4), custom_call_target="tpu_custom_call", output_to_operand_aliasing={{1}: (0, {})} | custom-call | flops 1207959552 | bytes 8929280 | tf_op jit(solution)/shard_map/pallas_call | solution.py:21
  32.2 1.4 %shard_map.75.refs_1_ = f32[2,32,16,256]{3,2,1,0:T(8,128)S(1)} custom-call(bf16[1024,768]{1,0:T(8,128)(2,1)S(1)} %get-tuple-element.44.lhs_ref, bf16[3,3,512,512]{3,2,1,0:T(8,128)(2,1)S(1)} %bitcast.4), custom_call_target="tpu_custom_call" | custom-call | flops 1207959552 | bytes 7340032 | tf_op jit(solution)/shard_map/pallas_call | solution.py:21
  33.6 0.1 shard_map.77.refs_4_.refs_2_
  33.7 0.0 collective-permute-done.6.refs_7_.refs_10_.refs_6_
  33.7 0.1 shard_map.78
  33.8 0.4 %collective-permute-start.8 = (bf16[2,32,256]{2,1,0:T(8,128)(2,1)S(1)}, bf16[2,32,256]{2,1,0:T(8,128)(2,1)S(1)}, u32[]{:S(2)}, u32[]{:S(2)}) collective-permute-start(bf16[2,32,256]{2,1,0:T(8,128)(2,1)S(1)} %shard_map.78), channel_id=1, source_target_pairs={{0,4},{4,0},{1,5},{5,1},{2,6},{6,2},{3,7},{7,3},{8,12},{12,8},{9,1... | collective-permute-start | bytes 98312 | tf_op jit(solution)/shard_map/ppermute | solution.py:51
  34.2 0.4 shard_map.79
  34.6 0.7 %shard_map.76._ = bf16[1152,768]{1,0:T(8,128)(2,1)S(1)} custom-call(f32[2,32,16,256]{3,2,1,0:T(8,128)S(1)} %get-tuple-element.40.refs_0_, f32[32,16,512]{2,1,0:T(8,128)S(1)} %copy-done, s32[1,512]{1,0:T(1,128)S(1)} %bitcast.13, f32[1,512]{1,0:T(1,128)S(1)} %bitcast.18, bf16[512,256]{1,0:T(8,128)(2,1)S(1)} %collective-permute-done.3.got_ref.refs_4_.refs_7_, ...), custom_call_target="tpu_custom_call" | custom-call | bytes 5050368 | tf_op jit(solution)/shard_map/pallas_call | solution.py:21
  35.3 0.0 collective-permute-done.8.got_ref
  35.3 4.3 %shard_map.80 = (bf16[2,32,16,512]{3,2,1,0:T(8,128)(2,1)}, bf16[1152,768]{1,0:T(8,128)(2,1)S(1)}) custom-call(bf16[1152,768]{1,0:T(8,128)(2,1)S(1)} %shard_map.76._, bf16[2,32,256]{2,1,0:T(8,128)(2,1)S(1)} %collective-permute-done.8.got_ref, bf16[2,64,256]{2,1,0:T(8,128)(2,1)S(1)} %get-tuple-element.50.beside_ref, ...), custom_call_target="tpu_custom_call", output_to_operand_aliasing={{1}: (0, {})} | custom-call | flops 2415919104 | bytes 11632640 | tf_op jit(solution)/shard_map/pallas_call | solution.py:21
  (4 shorter events, 0.1 us)
Async XLA Ops:
  0.0 1.7 %copy-start = (f32[32,16,512]{2,1,0:T(8,128)S(1)}, f32[32,16,512]{2,1,0:T(8,128)}, u32[]{:S(2)}) copy-start(f32[32,16,512]{2,1,0:T(8,128)} %refs_3_.1) | copy-start | bytes 3145732
  0.0 1.3 %copy-start.2 = (bf16[2,32,16,512]{3,2,1,0:T(8,128)(2,1)S(1)}, bf16[2,32,16,512]{3,2,1,0:T(8,128)(2,1)}, u32[]{:S(2)}) copy-start(bf16[2,32,16,512]{3,2,1,0:T(8,128)(2,1)} %cells_ref.3) | copy-start | bytes 3145732
  1.7 1.2 %copy-start.3 = (bf16[2,32,16,512]{3,2,1,0:T(8,128)(2,1)S(1)}, bf16[2,32,16,512]{3,2,1,0:T(8,128)(2,1)}, u32[]{:S(2)}) copy-start(bf16[2,32,16,512]{3,2,1,0:T(8,128)(2,1)} %cells_ref.3) | copy-start | bytes 3145732
  2.0 4.2 %copy-start.1 = (bf16[3,3,512,512]{3,2,1,0:T(8,128)(2,1)S(1)}, bf16[3,3,512,512]{3,2,1,0:T(8,128)(2,1)}, u32[]{:S(2)}) copy-start(bf16[3,3,512,512]{3,2,1,0:T(8,128)(2,1)} %weight_ref.6) | copy-start | bytes 14155780
  2.0 4.2 %copy-start.4 = (s32[512]{0:T(512)S(1)}, s32[512]{0:T(512)}, u32[]{:S(2)}) copy-start(s32[512]{0:T(512)} %param.9) | copy-start | bytes 6148
  2.0 1.8 %collective-permute-start = (bf16[192,512]{1,0:T(8,128)(2,1)S(1)}, bf16[192,512]{1,0:T(8,128)(2,1)S(1)}, u32[]{:S(2)}, u32[]{:S(2)}) collective-permute-start(bf16[192,512]{1,0:T(8,128)(2,1)S(1)} %get-tuple-element.33), channel_id=1, source_target_pairs={{0,4},{4,0},{1,5},{5,1},{2,6},{6,2},{3,7},{7,3},{8,12},{12,8},{9,1... | collective-permute-start | bytes 589832 | tf_op jit(solution)/shard_map/ppermute | solution.py:51
  3.8 8.4 %collective-permute-start.1 = (bf16[5,64,512]{2,1,0:T(8,128)(2,1)S(1)}, bf16[5,64,512]{2,1,0:T(8,128)(2,1)S(1)}, u32[]{:S(2)}, u32[]{:S(2)}) collective-permute-start(bf16[5,64,512]{2,1,0:T(8,128)(2,1)S(1)} %pad_maximum_fusion), channel_id=1, source_target_pairs={{0,5},{1,6},{2,7},{5,0},{6,1},{7,2},{8,13},{9,14},{10,15},{13,8},{... | collective-permute-start | bytes 983048 | tf_op jit(solution)/shard_map/ppermute | solution.py:95
  12.2 1.9 %collective-permute-start.2 = (bf16[5,64,512]{2,1,0:T(8,128)(2,1)S(1)}, bf16[5,64,512]{2,1,0:T(8,128)(2,1)S(1)}, u32[]{:S(2)}, u32[]{:S(2)}) collective-permute-start(bf16[5,64,512]{2,1,0:T(8,128)(2,1)S(1)} %collective-permute-done.1.mine_ref), channel_id=1, source_target_pairs={{0,4},{4,0},{1,5},{5,1},{2,6},{6,2},{3,7},{7,3},{8,12},{12,8},{9,1... | collective-permute-start | bytes 983048 | tf_op jit(solution)/shard_map/ppermute | solution.py:51
  12.8 7.4 %collective-permute-start.3 = (bf16[512,256]{1,0:T(8,128)(2,1)S(1)}, bf16[512,256]{1,0:T(8,128)(2,1)S(1)}, u32[]{:S(2)}, u32[]{:S(2)}) collective-permute-start(bf16[512,256]{1,0:T(8,128)(2,1)S(1)} %get-tuple-element.41.end_ref), channel_id=1, source_target_pairs={{0,8},{8,0},{16,24},{4,20},{12,28},{1,9},{9,1},{17,25},{5,21},{13,... | collective-permute-start | bytes 786440 | tf_op jit(solution)/shard_map/ppermute | solution.py:324
  14.3 13.8 %copy-start.5 = (f32[512]{0:T(512)S(1)}, f32[512]{0:T(512)}, u32[]{:S(2)}) copy-start(f32[512]{0:T(512)} %param.10) | copy-start | bytes 6148
  15.4 8.4 %collective-permute-start.5 = (bf16[640,256]{1,0:T(8,128)(2,1)S(1)}, bf16[640,256]{1,0:T(8,128)(2,1)S(1)}, u32[]{:S(2)}, u32[]{:S(2)}) collective-permute-start(bf16[640,256]{1,0:T(8,128)(2,1)S(1)} %get-tuple-element.42.end_ref), channel_id=1, source_target_pairs={{0,8},{8,0},{16,24},{4,20},{12,28},{1,9},{9,1},{17,25},{5,21},{13,... | collective-permute-start | bytes 983048 | tf_op jit(solution)/shard_map/ppermute | solution.py:324
  20.2 10.6 %slice-start = ((s8[4718592]{0:T(1024)(128)(4,1)}), s8[4194304]{0:T(1024)(128)(4,1)S(1)}, s32[]{:S(2)}) async-start(s8[4718592]{0:T(1024)(128)(4,1)} %bitcast.3), calls=%async_computation | async-start | bytes 8388608
  20.4 7.7 %collective-permute-start.4 = (bf16[512,256]{1,0:T(8,128)(2,1)S(1)}, bf16[512,256]{1,0:T(8,128)(2,1)S(1)}, u32[]{:S(2)}, u32[]{:S(2)}) collective-permute-start(bf16[512,256]{1,0:T(8,128)(2,1)S(1)} %shard_map.70), channel_id=1, source_target_pairs={{0,16},{8,24},{4,12},{20,28},{28,20},{1,17},{9,25},{5,13},{21,29},... | collective-permute-start | bytes 786440 | tf_op jit(solution)/shard_map/ppermute | solution.py:327
  23.9 9.7 %collective-permute-start.6 = (bf16[640,256]{1,0:T(8,128)(2,1)S(1)}, bf16[640,256]{1,0:T(8,128)(2,1)S(1)}, u32[]{:S(2)}, u32[]{:S(2)}) collective-permute-start(bf16[640,256]{1,0:T(8,128)(2,1)S(1)} %shard_map.71), channel_id=1, source_target_pairs={{0,16},{8,24},{4,12},{20,28},{28,20},{1,17},{9,25},{5,13},{21,29},... | collective-permute-start | bytes 983048 | tf_op jit(solution)/shard_map/ppermute | solution.py:327
  28.1 2.7 %slice-start.1 = ((s8[4718592]{0:T(1024)(128)(4,1)}), s8[524288]{0:T(1024)(128)(4,1)S(1)}, s32[]{:S(2)}) async-start(s8[4718592]{0:T(1024)(128)(4,1)} %bitcast.3), calls=%async_computation.1 | async-start | bytes 1048576
  28.1 2.6 %collective-permute-start.7 = (bf16[2,16,256]{2,1,0:T(8,128)(2,1)S(1)}, bf16[2,16,256]{2,1,0:T(8,128)(2,1)S(1)}, u32[]{:S(2)}, u32[]{:S(2)}) collective-permute-start(bf16[2,16,256]{2,1,0:T(8,128)(2,1)S(1)} %shard_map.73), channel_id=1, source_target_pairs={{0,4},{4,0},{1,5},{5,1},{2,6},{6,2},{3,7},{7,3},{8,12},{12,8},{9,1... | collective-permute-start | bytes 49160 | tf_op jit(solution)/shard_map/ppermute | solution.py:51
  33.8 1.5 %collective-permute-start.8 = (bf16[2,32,256]{2,1,0:T(8,128)(2,1)S(1)}, bf16[2,32,256]{2,1,0:T(8,128)(2,1)S(1)}, u32[]{:S(2)}, u32[]{:S(2)}) collective-permute-start(bf16[2,32,256]{2,1,0:T(8,128)(2,1)S(1)} %shard_map.78), channel_id=1, source_target_pairs={{0,4},{4,0},{1,5},{5,1},{2,6},{6,2},{3,7},{7,3},{8,12},{12,8},{9,1... | collective-permute-start | bytes 98312 | tf_op jit(solution)/shard_map/ppermute | solution.py:51

commit v19 on v18

--- a/solution.py
+++ b/solution.py
@@ -59,31 +59,36 @@
     keep_ref[index] = (zero * right + one * left).astype(keep_ref.dtype)
 
 
+def columns_of(tile, wide_ref, picked):
+    rows, cols, channels = tile.shape
+    parts, _, lanes = wide_ref.shape
+    tile = tile.reshape(rows * cols, channels)
+    for part in range(parts):
+        wide_ref[part] = tile[:, part * lanes : (part + 1) * lanes]
+    return [
+        jnp.concatenate(
+            [wide_ref[part, pl.ds(col, rows, stride=cols), :] for part in range(parts)], axis=1
+        )
+        for col in picked
+    ]
+
+
 def edges_kernel(cells_ref, give_ref, keep_ref, wide_ref):
     count, rows, cols, channels = cells_ref.shape
     for frame in range(count):
         give_ref[frame * cols : (frame + 1) * cols] = cells_ref[frame, inner_row(rows)]
-        tile = cells_ref[frame].reshape(rows * cols, channels).astype(jnp.float32)
-        lanes = wide_ref.shape[-1]
-        for part in range(channels // lanes):
-            wide_ref[frame, part] = tile[:, part * lanes : (part + 1) * lanes]
-
-        def column(col):
-            parts = [
-                wide_ref[frame, part, pl.ds(col, rows, stride=cols), :]
-                for part in range(channels // lanes)
-            ]
-            return jnp.concatenate(parts, axis=1)
-
+        tile = cells_ref[frame].astype(jnp.float32)
+        picked = (0, 1, cols - 1, cols - 2)
+        columns = columns_of(tile, wide_ref.at[frame], picked)
         for depth in range(2):
-            left, right = column(depth), column(cols - 1 - depth)
+            left, right = columns[depth], columns[2 + depth]
             put_columns(2 * frame + depth, left, right, give_ref, keep_ref)
 
 
-def start_edges_kernel(start_ref, _, __, give_ref, keep_ref):
-    tile, cols = start_ref[...], start_ref.shape[1]
-    index = keep_ref.shape[0] - 1
-    put_columns(index, tile[:, 0, :], tile[:, cols - 1, :], give_ref, keep_ref)
+def start_edges_kernel(start_ref, _, __, give_ref, keep_ref, wide_ref):
+    cols = start_ref.shape[1]
+    left, right = columns_of(start_ref[...], wide_ref, (0, cols - 1))
+    put_columns(keep_ref.shape[0] - 1, left, right, give_ref, keep_ref)
 
 
 def trade_columns(give, keep, at):
@@ -623,6 +628,7 @@
         start_state,
         *edges,
         aliases={1: 0, 2: 1},
+        scratch=[pltpu.VMEM((channels // 128, size, 128), jnp.float32)],
     )
     got, mine = trade_columns(give, keep, count * cols)
     taps = of((count * size, wide), narrow)
@@ -695,6 +701,7 @@
     lhs = call(functools.partial(mixed_kernel, parts[0], rounds), taps, total, *mixing, *early)
     strip_start = call(strip_start_kernel, of((4 * rows, channels), jnp.float32), start_state, sides)
     flops = 18 * inner.size * half
+    lhs, strip_start = lax.optimization_barrier((lhs, strip_start))
     first_sum, lhs = call(
         functools.partial(opening_kernel, parts[0], parts[0]),
         (inner, taps),

time: 40 us -> 40 us (level)
    ppermute x2, starting transfers between devices: 4.6 us -> 4.07 us  [exchange_four(): arrivals.append((got, lax.ppermute(relayed, axes, second_round)))]
where the time goes in v19:
time: 40 us; the launch traced here: 39.5 us
  Pallas kernels  16.5 us (41%)
  starting transfers between devices  12.9 us (32%)
  waiting for transfers between devices  8.04 us (20%)
  local copies, waits for them, and re-layouts  1.67 us (4%)
  between operations  0.41 us (1%)
    pallas_call x17, Pallas kernels, call(): pl.pallas_call(kernel, in_specs=[WHOLE] * len(args), out_specs=out_specs...  16.5 us
    ppermute x2, waiting for transfers between devices, exchange_four(): got = lax.ppermute(end, axes, first_round)  4.83 us
    ppermute x2, starting transfers between devices, exchange_four(): arrivals.append((got, lax.ppermute(relayed, axes, second_round)))  4.07 us
    ppermute x4, starting transfers between devices, swap_cores(): return lax.ppermute(array, 'sx', [(0, 1), (1, 0)])  3.8 us
    ppermute x2, starting transfers between devices, exchange_four(): got = lax.ppermute(end, axes, first_round)  2.7 us
    ppermute x1, starting transfers between devices, trade_columns(): return (got, lax.ppermute(columns, ('sx', 'sy'), pairs))  2.33 us
    ppermute x2, waiting for transfers between devices, exchange_four(): arrivals.append((got, lax.ppermute(relayed, axes, second_round)))  1.73 us
    unnamed x16, local copies, waits for them, and re-layouts  1.66 us
  transfers between devices with their start and end apart: 9, of which 6 were waited for; matrix products, arithmetic and copies ran while one was open for 0% of the time, Pallas kernels for 29%

profile of v19, /device:TPU:23, one launch (start us, length us, event | category | flops | bytes accessed | tf_op | source)
XLA Modules:
  0.0 39.5 jit_solution(8022386603314614586)
XLA Ops:
  0.0 0.0 copy-start
  0.0 0.0 copy-start.2
  0.0 1.3 %copy-done.2 = bf16[2,32,16,512]{3,2,1,0:T(8,128)(2,1)S(1)} copy-done((bf16[2,32,16,512]{3,2,1,0:T(8,128)(2,1)S(1)}, bf16[2,32,16,512]{3,2,1,0:T(8,128)(2,1)}, u32[]{:S(2)}) %copy-start.2) | copy-done | bytes 1048600
  1.3 0.4 shard_map.64
  1.7 0.0 copy-start.3
  1.7 0.0 copy-done
  1.7 0.1 shard_map.65
  1.8 0.0 copy-start.1
  1.9 0.0 copy-start.4
  1.9 0.7 %collective-permute-start = (bf16[192,512]{1,0:T(8,128)(2,1)S(1)}, bf16[192,512]{1,0:T(8,128)(2,1)S(1)}, u32[]{:S(2)}, u32[]{:S(2)}) collective-permute-start(bf16[192,512]{1,0:T(8,128)(2,1)S(1)} %get-tuple-element.35), channel_id=1, source_target_pairs={{0,4},{4,0},{1,5},{5,1},{2,6},{6,2},{3,7},{7,3},{8,12},{12,8},{9,1... | collective-permute-start | bytes 589832 | tf_op jit(solution)/shard_map/ppermute | solution.py:51
  2.6 0.3 copy-done.3
  2.9 0.2 shard_map.66._
  3.1 0.6 %collective-permute-done.got_ref = bf16[192,512]{1,0:T(8,128)(2,1)S(1)} collective-permute-done((bf16[192,512]{1,0:T(8,128)(2,1)S(1)}, bf16[192,512]{1,0:T(8,128)(2,1)S(1)}, u32[]{:S(2)}, u32[]{:S(2)}) %collective-permute-start) | collective-permute-done | bytes 196640 | tf_op jit(solution)/shard_map/ppermute | solution.py:51
  3.7 2.3 %collective-permute-start.1 = (bf16[5,64,512]{2,1,0:T(8,128)(2,1)S(1)}, bf16[5,64,512]{2,1,0:T(8,128)(2,1)S(1)}, u32[]{:S(2)}, u32[]{:S(2)}) collective-permute-start(bf16[5,64,512]{2,1,0:T(8,128)(2,1)S(1)} %pad_maximum_fusion), channel_id=1, source_target_pairs={{0,5},{1,6},{2,7},{5,0},{6,1},{7,2},{8,13},{9,14},{10,15},{13,8},{... | collective-permute-start | bytes 983048 | tf_op jit(solution)/shard_map/ppermute | solution.py:100
  6.1 0.0 copy-done.1
  6.1 0.0 copy-done.4
  6.1 5.3 %shard_map.67 = (f32[2,32,16,512]{3,2,1,0:T(8,128)S(1)}, f32[2,64,512]{2,1,0:T(8,128)S(1)}, bf16[512,256]{1,0:T(8,128)(2,1)S(1)}, bf16[1024,1536]{1,0:T(8,128)(2,1)S(1)}) custom-call(bf16[1024,1536]{1,0:T(8,128)(2,1)S(1)} %shard_map.66._, bf16[192,512]{1,0:T(8,128)(2,1)S(1)} %collective-permute-done.got_ref, ...), custom_call_target="tpu_custom_call", output_to_operand_aliasing={{3}: (0, {})} | custom-call | flops 4831838208 | bytes 13830144 | tf_op jit(solution)/shard_map/pallas_call | solution.py:21
  11.3 0.8 %collective-permute-done.1.mine_ref = bf16[5,64,512]{2,1,0:T(8,128)(2,1)S(1)} collective-permute-done((bf16[5,64,512]{2,1,0:T(8,128)(2,1)S(1)}, bf16[5,64,512]{2,1,0:T(8,128)(2,1)S(1)}, u32[]{:S(2)}, u32[]{:S(2)}) %collective-permute-start.1) | collective-permute-done | bytes 327712 | tf_op jit(solution)/shard_map/ppermute | solution.py:100
  12.1 0.6 %collective-permute-start.2 = (bf16[5,64,512]{2,1,0:T(8,128)(2,1)S(1)}, bf16[5,64,512]{2,1,0:T(8,128)(2,1)S(1)}, u32[]{:S(2)}, u32[]{:S(2)}) collective-permute-start(bf16[5,64,512]{2,1,0:T(8,128)(2,1)S(1)} %collective-permute-done.1.mine_ref), channel_id=1, source_target_pairs={{0,4},{4,0},{1,5},{5,1},{2,6},{6,2},{3,7},{7,3},{8,12},{12,8},{9,1... | collective-permute-start | bytes 983048 | tf_op jit(solution)/shard_map/ppermute | solution.py:51
  12.7 1.3 %collective-permute-start.3 = (bf16[512,256]{1,0:T(8,128)(2,1)S(1)}, bf16[512,256]{1,0:T(8,128)(2,1)S(1)}, u32[]{:S(2)}, u32[]{:S(2)}) collective-permute-start(bf16[512,256]{1,0:T(8,128)(2,1)S(1)} %get-tuple-element.43.end_ref), channel_id=1, source_target_pairs={{0,8},{8,0},{16,24},{4,20},{12,28},{1,9},{9,1},{17,25},{5,21},{13,... | collective-permute-start | bytes 786440 | tf_op jit(solution)/shard_map/ppermute | solution.py:329
  14.0 0.0 collective-permute-done.2.theirs_ref
  14.0 0.2 shard_map.68
  14.2 0.0 copy-start.5
  14.2 0.0 slice-start
  14.2 1.0 %shard_map.69 = (f32[2,32,16,256]{3,2,1,0:T(8,128)S(1)}, f32[2,64,256]{2,1,0:T(8,128)S(1)}, f32[2,128,256]{2,1,0:T(8,128)S(1)}, bf16[640,256]{1,0:T(8,128)(2,1)S(1)}) custom-call(bf16[256,1536]{1,0:T(8,128)(2,1)S(1)} %get-tuple-element.39.lhs_ref, bf16[3,3,512,512]{3,2,1,0:T(8,128)(2,1)S(1)} %copy-done.1, ...), custom_call_target="tpu_custom_call" | custom-call | flops 603979776 | bytes 9635840 | tf_op jit(solution)/shard_map/pallas_call | solution.py:21
  15.2 1.4 %collective-permute-start.5 = (bf16[640,256]{1,0:T(8,128)(2,1)S(1)}, bf16[640,256]{1,0:T(8,128)(2,1)S(1)}, u32[]{:S(2)}, u32[]{:S(2)}) collective-permute-start(bf16[640,256]{1,0:T(8,128)(2,1)S(1)} %get-tuple-element.44.end_ref), channel_id=1, source_target_pairs={{0,8},{8,0},{16,24},{4,20},{12,28},{1,9},{9,1},{17,25},{5,21},{13,... | collective-permute-start | bytes 983048 | tf_op jit(solution)/shard_map/ppermute | solution.py:329
  16.7 3.4 %collective-permute-done.3.got_ref.refs_4_.refs_7_ = bf16[512,256]{1,0:T(8,128)(2,1)S(1)} collective-permute-done((bf16[512,256]{1,0:T(8,128)(2,1)S(1)}, bf16[512,256]{1,0:T(8,128)(2,1)S(1)}, u32[]{:S(2)}, u32[]{:S(2)}) %collective-permute-start.3) | collective-permute-done | bytes 262176 | tf_op jit(solution)/shard_map/ppermute | solution.py:329
  20.1 0.2 shard_map.70
  20.3 1.9 %collective-permute-start.4 = (bf16[512,256]{1,0:T(8,128)(2,1)S(1)}, bf16[512,256]{1,0:T(8,128)(2,1)S(1)}, u32[]{:S(2)}, u32[]{:S(2)}) collective-permute-start(bf16[512,256]{1,0:T(8,128)(2,1)S(1)} %shard_map.70), channel_id=1, source_target_pairs={{0,16},{8,24},{4,12},{20,28},{28,20},{1,17},{9,25},{5,13},{21,29},... | collective-permute-start | bytes 786440 | tf_op jit(solution)/shard_map/ppermute | solution.py:332
  22.2 1.4 %collective-permute-done.5.got_ref.refs_6_.refs_9_.refs_5_ = bf16[640,256]{1,0:T(8,128)(2,1)S(1)} collective-permute-done((bf16[640,256]{1,0:T(8,128)(2,1)S(1)}, bf16[640,256]{1,0:T(8,128)(2,1)S(1)}, u32[]{:S(2)}, u32[]{:S(2)}) %collective-permute-start.5) | collective-permute-done | bytes 327712 | tf_op jit(solution)/shard_map/ppermute | solution.py:329
  23.6 0.2 shard_map.71
  23.8 2.1 %collective-permute-start.6 = (bf16[640,256]{1,0:T(8,128)(2,1)S(1)}, bf16[640,256]{1,0:T(8,128)(2,1)S(1)}, u32[]{:S(2)}, u32[]{:S(2)}) collective-permute-start(bf16[640,256]{1,0:T(8,128)(2,1)S(1)} %shard_map.71), channel_id=1, source_target_pairs={{0,16},{8,24},{4,12},{20,28},{28,20},{1,17},{9,25},{5,13},{21,29},... | collective-permute-start | bytes 983048 | tf_op jit(solution)/shard_map/ppermute | solution.py:332
  25.9 1.7 %collective-permute-done.4.refs_5_.refs_8_ = bf16[512,256]{1,0:T(8,128)(2,1)S(1)} collective-permute-done((bf16[512,256]{1,0:T(8,128)(2,1)S(1)}, bf16[512,256]{1,0:T(8,128)(2,1)S(1)}, u32[]{:S(2)}, u32[]{:S(2)}) %collective-permute-start.4) | collective-permute-done | bytes 262176 | tf_op jit(solution)/shard_map/ppermute | solution.py:332
  27.7 0.0 copy-done.5
  27.7 0.0 slice-start.1
  27.7 1.8 %collective-permute-start.7 = (bf16[2,16,256]{2,1,0:T(8,128)(2,1)S(1)}, bf16[2,16,256]{2,1,0:T(8,128)(2,1)S(1)}, u32[]{:S(2)}, u32[]{:S(2)}) collective-permute-start(bf16[2,16,256]{2,1,0:T(8,128)(2,1)S(1)} %shard_map.74), channel_id=1, source_target_pairs={{0,4},{4,0},{1,5},{5,1},{2,6},{6,2},{3,7},{7,3},{8,12},{12,8},{9,1... | collective-permute-start | bytes 49160 | tf_op jit(solution)/shard_map/ppermute | solution.py:51
  29.5 0.6 %shard_map.72._ = bf16[1024,768]{1,0:T(8,128)(2,1)S(1)} custom-call(f32[2,32,16,512]{3,2,1,0:T(8,128)S(1)} %get-tuple-element.40.total_ref.refs_0_, f32[32,16,512]{2,1,0:T(8,128)S(1)} %copy-done, s32[1,512]{1,0:T(1,128)S(1)} %bitcast.10, f32[1,512]{1,0:T(1,128)S(1)} %bitcast.15, bf16[512,256]{1,0:T(8,128)(2,1)S(1)} %collective-permute-done.3.got_ref.refs_4_.refs_7_, ...), custom_call_target="tpu_custom_call" | custom-call | bytes 5246976 | tf_op jit(solution)/shard_map/pallas_call | solution.py:21
  30.1 0.1 shard_map.73.refs_4_.refs_2_
  30.2 0.1 collective-permute-done.7.got_ref
  30.4 0.0 slice-done
  30.4 0.0 slice-done.1
  30.4 1.4 %shard_map.75 = (f32[2,32,16,256]{3,2,1,0:T(8,128)S(1)}, bf16[1024,768]{1,0:T(8,128)(2,1)S(1)}) custom-call(bf16[1024,768]{1,0:T(8,128)(2,1)S(1)} %shard_map.72._, bf16[2,16,256]{2,1,0:T(8,128)(2,1)S(1)} %collective-permute-done.7.got_ref, bf16[3,3,512,512]{3,2,1,0:T(8,128)(2,1)S(1)} %bitcast.4), custom_call_target="tpu_custom_call", output_to_operand_aliasing={{1}: (0, {})} | custom-call | flops 1207959552 | bytes 8929280 | tf_op jit(solution)/shard_map/pallas_call | solution.py:21
  31.8 1.4 %shard_map.76.refs_1_ = f32[2,32,16,256]{3,2,1,0:T(8,128)S(1)} custom-call(bf16[1024,768]{1,0:T(8,128)(2,1)S(1)} %get-tuple-element.48.lhs_ref, bf16[3,3,512,512]{3,2,1,0:T(8,128)(2,1)S(1)} %bitcast.4), custom_call_target="tpu_custom_call" | custom-call | flops 1207959552 | bytes 7340032 | tf_op jit(solution)/shard_map/pallas_call | solution.py:21
  33.2 0.0 collective-permute-done.6.refs_7_.refs_10_.refs_6_
  33.2 0.1 shard_map.78
  33.3 0.7 %collective-permute-start.8 = (bf16[2,32,256]{2,1,0:T(8,128)(2,1)S(1)}, bf16[2,32,256]{2,1,0:T(8,128)(2,1)S(1)}, u32[]{:S(2)}, u32[]{:S(2)}) collective-permute-start(bf16[2,32,256]{2,1,0:T(8,128)(2,1)S(1)} %shard_map.78), channel_id=1, source_target_pairs={{0,4},{4,0},{1,5},{5,1},{2,6},{6,2},{3,7},{7,3},{8,12},{12,8},{9,1... | collective-permute-start | bytes 98312 | tf_op jit(solution)/shard_map/ppermute | solution.py:51
  34.0 0.4 shard_map.79
  34.4 0.7 %shard_map.77._ = bf16[1152,768]{1,0:T(8,128)(2,1)S(1)} custom-call(f32[2,32,16,256]{3,2,1,0:T(8,128)S(1)} %get-tuple-element.42.refs_0_, f32[32,16,512]{2,1,0:T(8,128)S(1)} %copy-done, s32[1,512]{1,0:T(1,128)S(1)} %bitcast.13, f32[1,512]{1,0:T(1,128)S(1)} %bitcast.18, bf16[512,256]{1,0:T(8,128)(2,1)S(1)} %collective-permute-done.3.got_ref.refs_4_.refs_7_, ...), custom_call_target="tpu_custom_call" | custom-call | bytes 5050368 | tf_op jit(solution)/shard_map/pallas_call | solution.py:21
  35.1 0.0 collective-permute-done.8.got_ref
  35.1 4.2 %shard_map.80 = (bf16[2,32,16,512]{3,2,1,0:T(8,128)(2,1)}, bf16[1152,768]{1,0:T(8,128)(2,1)S(1)}) custom-call(bf16[1152,768]{1,0:T(8,128)(2,1)S(1)} %shard_map.77._, bf16[2,32,256]{2,1,0:T(8,128)(2,1)S(1)} %collective-permute-done.8.got_ref, bf16[2,64,256]{2,1,0:T(8,128)(2,1)S(1)} %get-tuple-element.54.beside_ref, ...), custom_call_target="tpu_custom_call", output_to_operand_aliasing={{1}: (0, {})} | custom-call | flops 2415919104 | bytes 11632640 | tf_op jit(solution)/shard_map/pallas_call | solution.py:21
  (4 shorter events, 0.1 us)
Async XLA Ops:
  0.0 1.7 %copy-start = (f32[32,16,512]{2,1,0:T(8,128)S(1)}, f32[32,16,512]{2,1,0:T(8,128)}, u32[]{:S(2)}) copy-start(f32[32,16,512]{2,1,0:T(8,128)} %refs_3_.1) | copy-start | bytes 3145732
  0.0 1.3 %copy-start.2 = (bf16[2,32,16,512]{3,2,1,0:T(8,128)(2,1)S(1)}, bf16[2,32,16,512]{3,2,1,0:T(8,128)(2,1)}, u32[]{:S(2)}) copy-start(bf16[2,32,16,512]{3,2,1,0:T(8,128)(2,1)} %cells_ref.3) | copy-start | bytes 3145732
  1.7 1.2 %copy-start.3 = (bf16[2,32,16,512]{3,2,1,0:T(8,128)(2,1)S(1)}, bf16[2,32,16,512]{3,2,1,0:T(8,128)(2,1)}, u32[]{:S(2)}) copy-start(bf16[2,32,16,512]{3,2,1,0:T(8,128)(2,1)} %cells_ref.3) | copy-start | bytes 3145732
  1.8 4.2 %copy-start.1 = (bf16[3,3,512,512]{3,2,1,0:T(8,128)(2,1)S(1)}, bf16[3,3,512,512]{3,2,1,0:T(8,128)(2,1)}, u32[]{:S(2)}) copy-start(bf16[3,3,512,512]{3,2,1,0:T(8,128)(2,1)} %weight_ref.6) | copy-start | bytes 14155780
  1.9 4.2 %copy-start.4 = (s32[512]{0:T(512)S(1)}, s32[512]{0:T(512)}, u32[]{:S(2)}) copy-start(s32[512]{0:T(512)} %param.9) | copy-start | bytes 6148
  1.9 1.8 %collective-permute-start = (bf16[192,512]{1,0:T(8,128)(2,1)S(1)}, bf16[192,512]{1,0:T(8,128)(2,1)S(1)}, u32[]{:S(2)}, u32[]{:S(2)}) collective-permute-start(bf16[192,512]{1,0:T(8,128)(2,1)S(1)} %get-tuple-element.35), channel_id=1, source_target_pairs={{0,4},{4,0},{1,5},{5,1},{2,6},{6,2},{3,7},{7,3},{8,12},{12,8},{9,1... | collective-permute-start | bytes 589832 | tf_op jit(solution)/shard_map/ppermute | solution.py:51
  3.7 8.4 %collective-permute-start.1 = (bf16[5,64,512]{2,1,0:T(8,128)(2,1)S(1)}, bf16[5,64,512]{2,1,0:T(8,128)(2,1)S(1)}, u32[]{:S(2)}, u32[]{:S(2)}) collective-permute-start(bf16[5,64,512]{2,1,0:T(8,128)(2,1)S(1)} %pad_maximum_fusion), channel_id=1, source_target_pairs={{0,5},{1,6},{2,7},{5,0},{6,1},{7,2},{8,13},{9,14},{10,15},{13,8},{... | collective-permute-start | bytes 983048 | tf_op jit(solution)/shard_map/ppermute | solution.py:100
  12.1 1.9 %collective-permute-start.2 = (bf16[5,64,512]{2,1,0:T(8,128)(2,1)S(1)}, bf16[5,64,512]{2,1,0:T(8,128)(2,1)S(1)}, u32[]{:S(2)}, u32[]{:S(2)}) collective-permute-start(bf16[5,64,512]{2,1,0:T(8,128)(2,1)S(1)} %collective-permute-done.1.mine_ref), channel_id=1, source_target_pairs={{0,4},{4,0},{1,5},{5,1},{2,6},{6,2},{3,7},{7,3},{8,12},{12,8},{9,1... | collective-permute-start | bytes 983048 | tf_op jit(solution)/shard_map/ppermute | solution.py:51
  12.7 7.4 %collective-permute-start.3 = (bf16[512,256]{1,0:T(8,128)(2,1)S(1)}, bf16[512,256]{1,0:T(8,128)(2,1)S(1)}, u32[]{:S(2)}, u32[]{:S(2)}) collective-permute-start(bf16[512,256]{1,0:T(8,128)(2,1)S(1)} %get-tuple-element.43.end_ref), channel_id=1, source_target_pairs={{0,8},{8,0},{16,24},{4,20},{12,28},{1,9},{9,1},{17,25},{5,21},{13,... | collective-permute-start | bytes 786440 | tf_op jit(solution)/shard_map/ppermute | solution.py:329
  14.2 13.5 %copy-start.5 = (f32[512]{0:T(512)S(1)}, f32[512]{0:T(512)}, u32[]{:S(2)}) copy-start(f32[512]{0:T(512)} %param.10) | copy-start | bytes 6148
  14.2 16.2 %slice-start = ((s8[4718592]{0:T(1024)(128)(4,1)}), s8[4194304]{0:T(1024)(128)(4,1)S(1)}, s32[]{:S(2)}) async-start(s8[4718592]{0:T(1024)(128)(4,1)} %bitcast.3), calls=%async_computation | async-start | bytes 8388608
  15.2 8.4 %collective-permute-start.5 = (bf16[640,256]{1,0:T(8,128)(2,1)S(1)}, bf16[640,256]{1,0:T(8,128)(2,1)S(1)}, u32[]{:S(2)}, u32[]{:S(2)}) collective-permute-start(bf16[640,256]{1,0:T(8,128)(2,1)S(1)} %get-tuple-element.44.end_ref), channel_id=1, source_target_pairs={{0,8},{8,0},{16,24},{4,20},{12,28},{1,9},{9,1},{17,25},{5,21},{13,... | collective-permute-start | bytes 983048 | tf_op jit(solution)/shard_map/ppermute | solution.py:329
  20.3 7.4 %collective-permute-start.4 = (bf16[512,256]{1,0:T(8,128)(2,1)S(1)}, bf16[512,256]{1,0:T(8,128)(2,1)S(1)}, u32[]{:S(2)}, u32[]{:S(2)}) collective-permute-start(bf16[512,256]{1,0:T(8,128)(2,1)S(1)} %shard_map.70), channel_id=1, source_target_pairs={{0,16},{8,24},{4,12},{20,28},{28,20},{1,17},{9,25},{5,13},{21,29},... | collective-permute-start | bytes 786440 | tf_op jit(solution)/shard_map/ppermute | solution.py:332
  23.8 9.4 %collective-permute-start.6 = (bf16[640,256]{1,0:T(8,128)(2,1)S(1)}, bf16[640,256]{1,0:T(8,128)(2,1)S(1)}, u32[]{:S(2)}, u32[]{:S(2)}) collective-permute-start(bf16[640,256]{1,0:T(8,128)(2,1)S(1)} %shard_map.71), channel_id=1, source_target_pairs={{0,16},{8,24},{4,12},{20,28},{28,20},{1,17},{9,25},{5,13},{21,29},... | collective-permute-start | bytes 983048 | tf_op jit(solution)/shard_map/ppermute | solution.py:332
  27.7 2.7 %slice-start.1 = ((s8[4718592]{0:T(1024)(128)(4,1)}), s8[524288]{0:T(1024)(128)(4,1)S(1)}, s32[]{:S(2)}) async-start(s8[4718592]{0:T(1024)(128)(4,1)} %bitcast.3), calls=%async_computation.1 | async-start | bytes 1048576
  27.7 2.6 %collective-permute-start.7 = (bf16[2,16,256]{2,1,0:T(8,128)(2,1)S(1)}, bf16[2,16,256]{2,1,0:T(8,128)(2,1)S(1)}, u32[]{:S(2)}, u32[]{:S(2)}) collective-permute-start(bf16[2,16,256]{2,1,0:T(8,128)(2,1)S(1)} %shard_map.74), channel_id=1, source_target_pairs={{0,4},{4,0},{1,5},{5,1},{2,6},{6,2},{3,7},{7,3},{8,12},{12,8},{9,1... | collective-permute-start | bytes 49160 | tf_op jit(solution)/shard_map/ppermute | solution.py:51
  33.3 1.8 %collective-permute-start.8 = (bf16[2,32,256]{2,1,0:T(8,128)(2,1)S(1)}, bf16[2,32,256]{2,1,0:T(8,128)(2,1)S(1)}, u32[]{:S(2)}, u32[]{:S(2)}) collective-permute-start(bf16[2,32,256]{2,1,0:T(8,128)(2,1)S(1)} %shard_map.78), channel_id=1, source_target_pairs={{0,4},{4,0},{1,5},{5,1},{2,6},{6,2},{3,7},{7,3},{8,12},{12,8},{9,1... | collective-permute-start | bytes 98312 | tf_op jit(solution)/shard_map/ppermute | solution.py:51

commit v20 on v19

--- a/solution.py
+++ b/solution.py
@@ -333,6 +333,12 @@
     return arrivals
 
 
+def gelu(x):
+    slope = math.sqrt(2.0 / math.pi)
+    half = 0.5 * x
+    return half + half * jnp.tanh(x * (slope + (slope * 0.044715) * (x * x)))
+
+
 class Mix:
     def __init__(self, lanes, count, pole_ref, scale_ref):
         self.rate = rate_of(pole_ref)[:, lanes]
@@ -355,7 +361,7 @@
         state = reach * start + entry.reshape(start.shape)
         for drive in drives:
             state = decay * state + drive
-            yield jax.nn.gelu(self.scale * state)
+            yield gelu(self.scale * state)
 
 
 def no_border(cells, axis):

time: 40 us -> 40 us (level)
  no operation moved by 1% of the time
where the time goes in v20:
time: 40 us; the launch traced here: 39.5 us
  Pallas kernels  16.4 us (41%)
  starting transfers between devices  12.9 us (32%)
  waiting for transfers between devices  8.08 us (20%)
  local copies, waits for them, and re-layouts  1.67 us (4%)
  between operations  0.41 us (1%)
    pallas_call x17, Pallas kernels, call(): pl.pallas_call(kernel, in_specs=[WHOLE] * len(args), out_specs=out_specs...  16.4 us
    ppermute x2, waiting for transfers between devices, exchange_four(): got = lax.ppermute(end, axes, first_round)  4.83 us
    ppermute x2, starting transfers between devices, exchange_four(): arrivals.append((got, lax.ppermute(relayed, axes, second_round)))  4.07 us
    ppermute x4, starting transfers between devices, swap_cores(): return lax.ppermute(array, 'sx', [(0, 1), (1, 0)])  3.8 us
    ppermute x2, starting transfers between devices, exchange_four(): got = lax.ppermute(end, axes, first_round)  2.7 us
    ppermute x1, starting transfers between devices, trade_columns(): return (got, lax.ppermute(columns, ('sx', 'sy'), pairs))  2.33 us
    ppermute x2, waiting for transfers between devices, exchange_four(): arrivals.append((got, lax.ppermute(relayed, axes, second_round)))  1.73 us
    unnamed x16, local copies, waits for them, and re-layouts  1.66 us
  transfers between devices with their start and end apart: 9, of which 6 were waited for; matrix products, arithmetic and copies ran while one was open for 0% of the time, Pallas kernels for 29%

profile of v20, /device:TPU:23, one launch (start us, length us, event | category | flops | bytes accessed | tf_op | source)
XLA Modules:
  0.0 39.5 jit_solution(10129297804463004965)
XLA Ops:
  0.0 0.0 copy-start
  0.0 0.0 copy-start.2
  0.0 1.3 %copy-done.2 = bf16[2,32,16,512]{3,2,1,0:T(8,128)(2,1)S(1)} copy-done((bf16[2,32,16,512]{3,2,1,0:T(8,128)(2,1)S(1)}, bf16[2,32,16,512]{3,2,1,0:T(8,128)(2,1)}, u32[]{:S(2)}) %copy-start.2) | copy-done | bytes 1048600
  1.3 0.4 shard_map.64
  1.7 0.0 copy-start.3
  1.7 0.0 copy-done
  1.7 0.1 shard_map.65
  1.8 0.0 copy-start.1
  1.9 0.0 copy-start.4
  1.9 0.7 %collective-permute-start = (bf16[192,512]{1,0:T(8,128)(2,1)S(1)}, bf16[192,512]{1,0:T(8,128)(2,1)S(1)}, u32[]{:S(2)}, u32[]{:S(2)}) collective-permute-start(bf16[192,512]{1,0:T(8,128)(2,1)S(1)} %get-tuple-element.35), channel_id=1, source_target_pairs={{0,4},{4,0},{1,5},{5,1},{2,6},{6,2},{3,7},{7,3},{8,12},{12,8},{9,1... | collective-permute-start | bytes 589832 | tf_op jit(solution)/shard_map/ppermute | solution.py:51
  2.6 0.3 copy-done.3
  2.9 0.2 shard_map.66._
  3.1 0.6 %collective-permute-done.got_ref = bf16[192,512]{1,0:T(8,128)(2,1)S(1)} collective-permute-done((bf16[192,512]{1,0:T(8,128)(2,1)S(1)}, bf16[192,512]{1,0:T(8,128)(2,1)S(1)}, u32[]{:S(2)}, u32[]{:S(2)}) %collective-permute-start) | collective-permute-done | bytes 196640 | tf_op jit(solution)/shard_map/ppermute | solution.py:51
  3.7 2.3 %collective-permute-start.1 = (bf16[5,64,512]{2,1,0:T(8,128)(2,1)S(1)}, bf16[5,64,512]{2,1,0:T(8,128)(2,1)S(1)}, u32[]{:S(2)}, u32[]{:S(2)}) collective-permute-start(bf16[5,64,512]{2,1,0:T(8,128)(2,1)S(1)} %pad_maximum_fusion), channel_id=1, source_target_pairs={{0,5},{1,6},{2,7},{5,0},{6,1},{7,2},{8,13},{9,14},{10,15},{13,8},{... | collective-permute-start | bytes 983048 | tf_op jit(solution)/shard_map/ppermute | solution.py:100
  6.1 0.0 copy-done.1
  6.1 0.0 copy-done.4
  6.1 5.3 %shard_map.67 = (f32[2,32,16,512]{3,2,1,0:T(8,128)S(1)}, f32[2,64,512]{2,1,0:T(8,128)S(1)}, bf16[512,256]{1,0:T(8,128)(2,1)S(1)}, bf16[1024,1536]{1,0:T(8,128)(2,1)S(1)}) custom-call(bf16[1024,1536]{1,0:T(8,128)(2,1)S(1)} %shard_map.66._, bf16[192,512]{1,0:T(8,128)(2,1)S(1)} %collective-permute-done.got_ref, ...), custom_call_target="tpu_custom_call", output_to_operand_aliasing={{3}: (0, {})} | custom-call | flops 4831838208 | bytes 13830144 | tf_op jit(solution)/shard_map/pallas_call | solution.py:21
  11.3 0.8 %collective-permute-done.1.mine_ref = bf16[5,64,512]{2,1,0:T(8,128)(2,1)S(1)} collective-permute-done((bf16[5,64,512]{2,1,0:T(8,128)(2,1)S(1)}, bf16[5,64,512]{2,1,0:T(8,128)(2,1)S(1)}, u32[]{:S(2)}, u32[]{:S(2)}) %collective-permute-start.1) | collective-permute-done | bytes 327712 | tf_op jit(solution)/shard_map/ppermute | solution.py:100
  12.1 0.6 %collective-permute-start.2 = (bf16[5,64,512]{2,1,0:T(8,128)(2,1)S(1)}, bf16[5,64,512]{2,1,0:T(8,128)(2,1)S(1)}, u32[]{:S(2)}, u32[]{:S(2)}) collective-permute-start(bf16[5,64,512]{2,1,0:T(8,128)(2,1)S(1)} %collective-permute-done.1.mine_ref), channel_id=1, source_target_pairs={{0,4},{4,0},{1,5},{5,1},{2,6},{6,2},{3,7},{7,3},{8,12},{12,8},{9,1... | collective-permute-start | bytes 983048 | tf_op jit(solution)/shard_map/ppermute | solution.py:51
  12.7 1.3 %collective-permute-start.3 = (bf16[512,256]{1,0:T(8,128)(2,1)S(1)}, bf16[512,256]{1,0:T(8,128)(2,1)S(1)}, u32[]{:S(2)}, u32[]{:S(2)}) collective-permute-start(bf16[512,256]{1,0:T(8,128)(2,1)S(1)} %get-tuple-element.43.end_ref), channel_id=1, source_target_pairs={{0,8},{8,0},{16,24},{4,20},{12,28},{1,9},{9,1},{17,25},{5,21},{13,... | collective-permute-start | bytes 786440 | tf_op jit(solution)/shard_map/ppermute | solution.py:329
  14.0 0.0 collective-permute-done.2.theirs_ref
  14.0 0.2 shard_map.68
  14.2 0.0 copy-start.5
  14.2 0.0 slice-start
  14.2 1.0 %shard_map.69 = (f32[2,32,16,256]{3,2,1,0:T(8,128)S(1)}, f32[2,64,256]{2,1,0:T(8,128)S(1)}, f32[2,128,256]{2,1,0:T(8,128)S(1)}, bf16[640,256]{1,0:T(8,128)(2,1)S(1)}) custom-call(bf16[256,1536]{1,0:T(8,128)(2,1)S(1)} %get-tuple-element.39.lhs_ref, bf16[3,3,512,512]{3,2,1,0:T(8,128)(2,1)S(1)} %copy-done.1, ...), custom_call_target="tpu_custom_call" | custom-call | flops 603979776 | bytes 9635840 | tf_op jit(solution)/shard_map/pallas_call | solution.py:21
  15.2 1.4 %collective-permute-start.5 = (bf16[640,256]{1,0:T(8,128)(2,1)S(1)}, bf16[640,256]{1,0:T(8,128)(2,1)S(1)}, u32[]{:S(2)}, u32[]{:S(2)}) collective-permute-start(bf16[640,256]{1,0:T(8,128)(2,1)S(1)} %get-tuple-element.44.end_ref), channel_id=1, source_target_pairs={{0,8},{8,0},{16,24},{4,20},{12,28},{1,9},{9,1},{17,25},{5,21},{13,... | collective-permute-start | bytes 983048 | tf_op jit(solution)/shard_map/ppermute | solution.py:329
  16.7 3.4 %collective-permute-done.3.got_ref.refs_4_.refs_7_ = bf16[512,256]{1,0:T(8,128)(2,1)S(1)} collective-permute-done((bf16[512,256]{1,0:T(8,128)(2,1)S(1)}, bf16[512,256]{1,0:T(8,128)(2,1)S(1)}, u32[]{:S(2)}, u32[]{:S(2)}) %collective-permute-start.3) | collective-permute-done | bytes 262176 | tf_op jit(solution)/shard_map/ppermute | solution.py:329
  20.1 0.2 shard_map.70
  20.3 1.9 %collective-permute-start.4 = (bf16[512,256]{1,0:T(8,128)(2,1)S(1)}, bf16[512,256]{1,0:T(8,128)(2,1)S(1)}, u32[]{:S(2)}, u32[]{:S(2)}) collective-permute-start(bf16[512,256]{1,0:T(8,128)(2,1)S(1)} %shard_map.70), channel_id=1, source_target_pairs={{0,16},{8,24},{4,12},{20,28},{28,20},{1,17},{9,25},{5,13},{21,29},... | collective-permute-start | bytes 786440 | tf_op jit(solution)/shard_map/ppermute | solution.py:332
  22.2 1.4 %collective-permute-done.5.got_ref.refs_6_.refs_9_.refs_5_ = bf16[640,256]{1,0:T(8,128)(2,1)S(1)} collective-permute-done((bf16[640,256]{1,0:T(8,128)(2,1)S(1)}, bf16[640,256]{1,0:T(8,128)(2,1)S(1)}, u32[]{:S(2)}, u32[]{:S(2)}) %collective-permute-start.5) | collective-permute-done | bytes 327712 | tf_op jit(solution)/shard_map/ppermute | solution.py:329
  23.6 0.2 shard_map.71
  23.8 2.1 %collective-permute-start.6 = (bf16[640,256]{1,0:T(8,128)(2,1)S(1)}, bf16[640,256]{1,0:T(8,128)(2,1)S(1)}, u32[]{:S(2)}, u32[]{:S(2)}) collective-permute-start(bf16[640,256]{1,0:T(8,128)(2,1)S(1)} %shard_map.71), channel_id=1, source_target_pairs={{0,16},{8,24},{4,12},{20,28},{28,20},{1,17},{9,25},{5,13},{21,29},... | collective-permute-start | bytes 983048 | tf_op jit(solution)/shard_map/ppermute | solution.py:332
  25.9 1.7 %collective-permute-done.4.refs_5_.refs_8_ = bf16[512,256]{1,0:T(8,128)(2,1)S(1)} collective-permute-done((bf16[512,256]{1,0:T(8,128)(2,1)S(1)}, bf16[512,256]{1,0:T(8,128)(2,1)S(1)}, u32[]{:S(2)}, u32[]{:S(2)}) %collective-permute-start.4) | collective-permute-done | bytes 262176 | tf_op jit(solution)/shard_map/ppermute | solution.py:332
  27.7 0.0 copy-done.5
  27.7 0.0 slice-start.1
  27.7 1.8 %collective-permute-start.7 = (bf16[2,16,256]{2,1,0:T(8,128)(2,1)S(1)}, bf16[2,16,256]{2,1,0:T(8,128)(2,1)S(1)}, u32[]{:S(2)}, u32[]{:S(2)}) collective-permute-start(bf16[2,16,256]{2,1,0:T(8,128)(2,1)S(1)} %shard_map.74), channel_id=1, source_target_pairs={{0,4},{4,0},{1,5},{5,1},{2,6},{6,2},{3,7},{7,3},{8,12},{12,8},{9,1... | collective-permute-start | bytes 49160 | tf_op jit(solution)/shard_map/ppermute | solution.py:51
  29.5 0.6 %shard_map.72._ = bf16[1024,768]{1,0:T(8,128)(2,1)S(1)} custom-call(f32[2,32,16,512]{3,2,1,0:T(8,128)S(1)} %get-tuple-element.40.total_ref.refs_0_, f32[32,16,512]{2,1,0:T(8,128)S(1)} %copy-done, s32[1,512]{1,0:T(1,128)S(1)} %bitcast.10, f32[1,512]{1,0:T(1,128)S(1)} %bitcast.15, bf16[512,256]{1,0:T(8,128)(2,1)S(1)} %collective-permute-done.3.got_ref.refs_4_.refs_7_, ...), custom_call_target="tpu_custom_call" | custom-call | bytes 5246976 | tf_op jit(solution)/shard_map/pallas_call | solution.py:21
  30.1 0.1 shard_map.73.refs_4_.refs_2_
  30.2 0.2 collective-permute-done.7.got_ref
  30.4 0.0 slice-done
  30.4 0.0 slice-done.1
  30.4 1.4 %shard_map.75 = (f32[2,32,16,256]{3,2,1,0:T(8,128)S(1)}, bf16[1024,768]{1,0:T(8,128)(2,1)S(1)}) custom-call(bf16[1024,768]{1,0:T(8,128)(2,1)S(1)} %shard_map.72._, bf16[2,16,256]{2,1,0:T(8,128)(2,1)S(1)} %collective-permute-done.7.got_ref, bf16[3,3,512,512]{3,2,1,0:T(8,128)(2,1)S(1)} %bitcast.4), custom_call_target="tpu_custom_call", output_to_operand_aliasing={{1}: (0, {})} | custom-call | flops 1207959552 | bytes 8929280 | tf_op jit(solution)/shard_map/pallas_call | solution.py:21
  31.8 1.4 %shard_map.76.refs_1_ = f32[2,32,16,256]{3,2,1,0:T(8,128)S(1)} custom-call(bf16[1024,768]{1,0:T(8,128)(2,1)S(1)} %get-tuple-element.48.lhs_ref, bf16[3,3,512,512]{3,2,1,0:T(8,128)(2,1)S(1)} %bitcast.4), custom_call_target="tpu_custom_call" | custom-call | flops 1207959552 | bytes 7340032 | tf_op jit(solution)/shard_map/pallas_call | solution.py:21
  33.2 0.0 collective-permute-done.6.refs_7_.refs_10_.refs_6_
  33.2 0.1 shard_map.78
  33.3 0.7 %collective-permute-start.8 = (bf16[2,32,256]{2,1,0:T(8,128)(2,1)S(1)}, bf16[2,32,256]{2,1,0:T(8,128)(2,1)S(1)}, u32[]{:S(2)}, u32[]{:S(2)}) collective-permute-start(bf16[2,32,256]{2,1,0:T(8,128)(2,1)S(1)} %shard_map.78), channel_id=1, source_target_pairs={{0,4},{4,0},{1,5},{5,1},{2,6},{6,2},{3,7},{7,3},{8,12},{12,8},{9,1... | collective-permute-start | bytes 98312 | tf_op jit(solution)/shard_map/ppermute | solution.py:51
  34.0 0.3 shard_map.79
  34.4 0.7 %shard_map.77._ = bf16[1152,768]{1,0:T(8,128)(2,1)S(1)} custom-call(f32[2,32,16,256]{3,2,1,0:T(8,128)S(1)} %get-tuple-element.42.refs_0_, f32[32,16,512]{2,1,0:T(8,128)S(1)} %copy-done, s32[1,512]{1,0:T(1,128)S(1)} %bitcast.13, f32[1,512]{1,0:T(1,128)S(1)} %bitcast.18, bf16[512,256]{1,0:T(8,128)(2,1)S(1)} %collective-permute-done.3.got_ref.refs_4_.refs_7_, ...), custom_call_target="tpu_custom_call" | custom-call | bytes 5050368 | tf_op jit(solution)/shard_map/pallas_call | solution.py:21
  35.1 0.0 collective-permute-done.8.got_ref
  35.1 4.2 %shard_map.80 = (bf16[2,32,16,512]{3,2,1,0:T(8,128)(2,1)}, bf16[1152,768]{1,0:T(8,128)(2,1)S(1)}) custom-call(bf16[1152,768]{1,0:T(8,128)(2,1)S(1)} %shard_map.77._, bf16[2,32,256]{2,1,0:T(8,128)(2,1)S(1)} %collective-permute-done.8.got_ref, bf16[2,64,256]{2,1,0:T(8,128)(2,1)S(1)} %get-tuple-element.54.beside_ref, ...), custom_call_target="tpu_custom_call", output_to_operand_aliasing={{1}: (0, {})} | custom-call | flops 2415919104 | bytes 11632640 | tf_op jit(solution)/shard_map/pallas_call | solution.py:21
  (4 shorter events, 0.1 us)
Async XLA Ops:
  0.0 1.7 %copy-start = (f32[32,16,512]{2,1,0:T(8,128)S(1)}, f32[32,16,512]{2,1,0:T(8,128)}, u32[]{:S(2)}) copy-start(f32[32,16,512]{2,1,0:T(8,128)} %refs_3_.1) | copy-start | bytes 3145732
  0.0 1.3 %copy-start.2 = (bf16[2,32,16,512]{3,2,1,0:T(8,128)(2,1)S(1)}, bf16[2,32,16,512]{3,2,1,0:T(8,128)(2,1)}, u32[]{:S(2)}) copy-start(bf16[2,32,16,512]{3,2,1,0:T(8,128)(2,1)} %cells_ref.3) | copy-start | bytes 3145732
  1.7 1.2 %copy-start.3 = (bf16[2,32,16,512]{3,2,1,0:T(8,128)(2,1)S(1)}, bf16[2,32,16,512]{3,2,1,0:T(8,128)(2,1)}, u32[]{:S(2)}) copy-start(bf16[2,32,16,512]{3,2,1,0:T(8,128)(2,1)} %cells_ref.3) | copy-start | bytes 3145732
  1.8 4.2 %copy-start.1 = (bf16[3,3,512,512]{3,2,1,0:T(8,128)(2,1)S(1)}, bf16[3,3,512,512]{3,2,1,0:T(8,128)(2,1)}, u32[]{:S(2)}) copy-start(bf16[3,3,512,512]{3,2,1,0:T(8,128)(2,1)} %weight_ref.6) | copy-start | bytes 14155780
  1.9 4.2 %copy-start.4 = (s32[512]{0:T(512)S(1)}, s32[512]{0:T(512)}, u32[]{:S(2)}) copy-start(s32[512]{0:T(512)} %param.9) | copy-start | bytes 6148
  1.9 1.8 %collective-permute-start = (bf16[192,512]{1,0:T(8,128)(2,1)S(1)}, bf16[192,512]{1,0:T(8,128)(2,1)S(1)}, u32[]{:S(2)}, u32[]{:S(2)}) collective-permute-start(bf16[192,512]{1,0:T(8,128)(2,1)S(1)} %get-tuple-element.35), channel_id=1, source_target_pairs={{0,4},{4,0},{1,5},{5,1},{2,6},{6,2},{3,7},{7,3},{8,12},{12,8},{9,1... | collective-permute-start | bytes 589832 | tf_op jit(solution)/shard_map/ppermute | solution.py:51
  3.7 8.4 %collective-permute-start.1 = (bf16[5,64,512]{2,1,0:T(8,128)(2,1)S(1)}, bf16[5,64,512]{2,1,0:T(8,128)(2,1)S(1)}, u32[]{:S(2)}, u32[]{:S(2)}) collective-permute-start(bf16[5,64,512]{2,1,0:T(8,128)(2,1)S(1)} %pad_maximum_fusion), channel_id=1, source_target_pairs={{0,5},{1,6},{2,7},{5,0},{6,1},{7,2},{8,13},{9,14},{10,15},{13,8},{... | collective-permute-start | bytes 983048 | tf_op jit(solution)/shard_map/ppermute | solution.py:100
  12.1 1.9 %collective-permute-start.2 = (bf16[5,64,512]{2,1,0:T(8,128)(2,1)S(1)}, bf16[5,64,512]{2,1,0:T(8,128)(2,1)S(1)}, u32[]{:S(2)}, u32[]{:S(2)}) collective-permute-start(bf16[5,64,512]{2,1,0:T(8,128)(2,1)S(1)} %collective-permute-done.1.mine_ref), channel_id=1, source_target_pairs={{0,4},{4,0},{1,5},{5,1},{2,6},{6,2},{3,7},{7,3},{8,12},{12,8},{9,1... | collective-permute-start | bytes 983048 | tf_op jit(solution)/shard_map/ppermute | solution.py:51
  12.7 7.4 %collective-permute-start.3 = (bf16[512,256]{1,0:T(8,128)(2,1)S(1)}, bf16[512,256]{1,0:T(8,128)(2,1)S(1)}, u32[]{:S(2)}, u32[]{:S(2)}) collective-permute-start(bf16[512,256]{1,0:T(8,128)(2,1)S(1)} %get-tuple-element.43.end_ref), channel_id=1, source_target_pairs={{0,8},{8,0},{16,24},{4,20},{12,28},{1,9},{9,1},{17,25},{5,21},{13,... | collective-permute-start | bytes 786440 | tf_op jit(solution)/shard_map/ppermute | solution.py:329
  14.2 13.5 %copy-start.5 = (f32[512]{0:T(512)S(1)}, f32[512]{0:T(512)}, u32[]{:S(2)}) copy-start(f32[512]{0:T(512)} %param.10) | copy-start | bytes 6148
  14.2 16.2 %slice-start = ((s8[4718592]{0:T(1024)(128)(4,1)}), s8[4194304]{0:T(1024)(128)(4,1)S(1)}, s32[]{:S(2)}) async-start(s8[4718592]{0:T(1024)(128)(4,1)} %bitcast.3), calls=%async_computation | async-start | bytes 8388608
  15.2 8.4 %collective-permute-start.5 = (bf16[640,256]{1,0:T(8,128)(2,1)S(1)}, bf16[640,256]{1,0:T(8,128)(2,1)S(1)}, u32[]{:S(2)}, u32[]{:S(2)}) collective-permute-start(bf16[640,256]{1,0:T(8,128)(2,1)S(1)} %get-tuple-element.44.end_ref), channel_id=1, source_target_pairs={{0,8},{8,0},{16,24},{4,20},{12,28},{1,9},{9,1},{17,25},{5,21},{13,... | collective-permute-start | bytes 983048 | tf_op jit(solution)/shard_map/ppermute | solution.py:329
  20.3 7.4 %collective-permute-start.4 = (bf16[512,256]{1,0:T(8,128)(2,1)S(1)}, bf16[512,256]{1,0:T(8,128)(2,1)S(1)}, u32[]{:S(2)}, u32[]{:S(2)}) collective-permute-start(bf16[512,256]{1,0:T(8,128)(2,1)S(1)} %shard_map.70), channel_id=1, source_target_pairs={{0,16},{8,24},{4,12},{20,28},{28,20},{1,17},{9,25},{5,13},{21,29},... | collective-permute-start | bytes 786440 | tf_op jit(solution)/shard_map/ppermute | solution.py:332
  23.8 9.4 %collective-permute-start.6 = (bf16[640,256]{1,0:T(8,128)(2,1)S(1)}, bf16[640,256]{1,0:T(8,128)(2,1)S(1)}, u32[]{:S(2)}, u32[]{:S(2)}) collective-permute-start(bf16[640,256]{1,0:T(8,128)(2,1)S(1)} %shard_map.71), channel_id=1, source_target_pairs={{0,16},{8,24},{4,12},{20,28},{28,20},{1,17},{9,25},{5,13},{21,29},... | collective-permute-start | bytes 983048 | tf_op jit(solution)/shard_map/ppermute | solution.py:332
  27.7 2.7 %slice-start.1 = ((s8[4718592]{0:T(1024)(128)(4,1)}), s8[524288]{0:T(1024)(128)(4,1)S(1)}, s32[]{:S(2)}) async-start(s8[4718592]{0:T(1024)(128)(4,1)} %bitcast.3), calls=%async_computation.1 | async-start | bytes 1048576
  27.7 2.6 %collective-permute-start.7 = (bf16[2,16,256]{2,1,0:T(8,128)(2,1)S(1)}, bf16[2,16,256]{2,1,0:T(8,128)(2,1)S(1)}, u32[]{:S(2)}, u32[]{:S(2)}) collective-permute-start(bf16[2,16,256]{2,1,0:T(8,128)(2,1)S(1)} %shard_map.74), channel_id=1, source_target_pairs={{0,4},{4,0},{1,5},{5,1},{2,6},{6,2},{3,7},{7,3},{8,12},{12,8},{9,1... | collective-permute-start | bytes 49160 | tf_op jit(solution)/shard_map/ppermute | solution.py:51
  33.3 1.7 %collective-permute-start.8 = (bf16[2,32,256]{2,1,0:T(8,128)(2,1)S(1)}, bf16[2,32,256]{2,1,0:T(8,128)(2,1)S(1)}, u32[]{:S(2)}, u32[]{:S(2)}) collective-permute-start(bf16[2,32,256]{2,1,0:T(8,128)(2,1)S(1)} %shard_map.78), channel_id=1, source_target_pairs={{0,4},{4,0},{1,5},{5,1},{2,6},{6,2},{3,7},{7,3},{8,12},{12,8},{9,1... | collective-permute-start | bytes 98312 | tf_op jit(solution)/shard_map/ppermute | solution.py:51

commit v21 on v20

--- a/solution.py
+++ b/solution.py
@@ -371,9 +371,17 @@
 
 def put_back(late, early, axis):
     cols = late.shape[axis]
-    col = lax.broadcasted_iota(jnp.int32, late.shape, axis)
-    late = jnp.where(col == 1, pltpu.roll(early, 1, axis), late)
-    return jnp.where(col == cols - 2, pltpu.roll(early, cols - 1, axis), late)
+
+    def slab(cells, start):
+        return lax.slice_in_dim(cells, start, start + SLAB, axis=axis)
+
+    first, last = slab(late, 0), slab(late, cols - SLAB)
+    col = lax.broadcasted_iota(jnp.int32, first.shape, axis)
+    first = jnp.where(col == 1, pltpu.roll(slab(early, 0), 1, axis), first)
+    moved = pltpu.roll(slab(early, cols - SLAB), SLAB - 1, axis)
+    last = jnp.where(col == SLAB - 2, moved, last)
+    middle = [lax.slice_in_dim(late, SLAB, cols - SLAB, axis=axis)] if cols > 2 * SLAB else []
+    return jnp.concatenate([first, *middle, last], axis=axis)
 
 
 def mixed_kernel(lanes, rounds, *refs):

time: 40 us -> 39.9 us (level)
  no operation moved by 1% of the time
where the time goes in v21:
time: 39.9 us; the launch traced here: 39.5 us
  Pallas kernels  16.4 us (41%)
  starting transfers between devices  12.9 us (32%)
  waiting for transfers between devices  8.08 us (20%)
  local copies, waits for them, and re-layouts  1.67 us (4%)
  between operations  0.41 us (1%)
    pallas_call x17, Pallas kernels, call(): pl.pallas_call(kernel, in_specs=[WHOLE] * len(args), out_specs=out_specs...  16.4 us
    ppermute x2, waiting for transfers between devices, exchange_four(): got = lax.ppermute(end, axes, first_round)  4.83 us
    ppermute x2, starting transfers between devices, exchange_four(): arrivals.append((got, lax.ppermute(relayed, axes, second_round)))  4.07 us
    ppermute x4, starting transfers between devices, swap_cores(): return lax.ppermute(array, 'sx', [(0, 1), (1, 0)])  3.8 us
    ppermute x2, starting transfers between devices, exchange_four(): got = lax.ppermute(end, axes, first_round)  2.7 us
    ppermute x1, starting transfers between devices, trade_columns(): return (got, lax.ppermute(columns, ('sx', 'sy'), pairs))  2.33 us
    ppermute x2, waiting for transfers between devices, exchange_four(): arrivals.append((got, lax.ppermute(relayed, axes, second_round)))  1.73 us
    unnamed x16, local copies, waits for them, and re-layouts  1.66 us
  transfers between devices with their start and end apart: 9, of which 6 were waited for; matrix products, arithmetic and copies ran while one was open for 0% of the time, Pallas kernels for 29%

profile of v21, /device:TPU:23, one launch (start us, length us, event | category | flops | bytes accessed | tf_op | source)
XLA Modules:
  0.0 39.5 jit_solution(9978570364694111497)
XLA Ops:
  0.0 0.0 copy-start
  0.0 0.0 copy-start.2
  0.0 1.3 %copy-done.2 = bf16[2,32,16,512]{3,2,1,0:T(8,128)(2,1)S(1)} copy-done((bf16[2,32,16,512]{3,2,1,0:T(8,128)(2,1)S(1)}, bf16[2,32,16,512]{3,2,1,0:T(8,128)(2,1)}, u32[]{:S(2)}) %copy-start.2) | copy-done | bytes 1048600
  1.3 0.4 shard_map.64
  1.7 0.0 copy-start.3
  1.7 0.0 copy-done
  1.7 0.1 shard_map.65
  1.8 0.0 copy-start.1
  1.9 0.0 copy-start.4
  1.9 0.7 %collective-permute-start = (bf16[192,512]{1,0:T(8,128)(2,1)S(1)}, bf16[192,512]{1,0:T(8,128)(2,1)S(1)}, u32[]{:S(2)}, u32[]{:S(2)}) collective-permute-start(bf16[192,512]{1,0:T(8,128)(2,1)S(1)} %get-tuple-element.35), channel_id=1, source_target_pairs={{0,4},{4,0},{1,5},{5,1},{2,6},{6,2},{3,7},{7,3},{8,12},{12,8},{9,1... | collective-permute-start | bytes 589832 | tf_op jit(solution)/shard_map/ppermute | solution.py:51
  2.6 0.3 copy-done.3
  2.9 0.2 shard_map.66._
  3.1 0.6 %collective-permute-done.got_ref = bf16[192,512]{1,0:T(8,128)(2,1)S(1)} collective-permute-done((bf16[192,512]{1,0:T(8,128)(2,1)S(1)}, bf16[192,512]{1,0:T(8,128)(2,1)S(1)}, u32[]{:S(2)}, u32[]{:S(2)}) %collective-permute-start) | collective-permute-done | bytes 196640 | tf_op jit(solution)/shard_map/ppermute | solution.py:51
  3.7 2.3 %collective-permute-start.1 = (bf16[5,64,512]{2,1,0:T(8,128)(2,1)S(1)}, bf16[5,64,512]{2,1,0:T(8,128)(2,1)S(1)}, u32[]{:S(2)}, u32[]{:S(2)}) collective-permute-start(bf16[5,64,512]{2,1,0:T(8,128)(2,1)S(1)} %pad_maximum_fusion), channel_id=1, source_target_pairs={{0,5},{1,6},{2,7},{5,0},{6,1},{7,2},{8,13},{9,14},{10,15},{13,8},{... | collective-permute-start | bytes 983048 | tf_op jit(solution)/shard_map/ppermute | solution.py:100
  6.1 0.0 copy-done.1
  6.1 0.0 copy-done.4
  6.1 5.3 %shard_map.67 = (f32[2,32,16,512]{3,2,1,0:T(8,128)S(1)}, f32[2,64,512]{2,1,0:T(8,128)S(1)}, bf16[512,256]{1,0:T(8,128)(2,1)S(1)}, bf16[1024,1536]{1,0:T(8,128)(2,1)S(1)}) custom-call(bf16[1024,1536]{1,0:T(8,128)(2,1)S(1)} %shard_map.66._, bf16[192,512]{1,0:T(8,128)(2,1)S(1)} %collective-permute-done.got_ref, ...), custom_call_target="tpu_custom_call", output_to_operand_aliasing={{3}: (0, {})} | custom-call | flops 4831838208 | bytes 13830144 | tf_op jit(solution)/shard_map/pallas_call | solution.py:21
  11.3 0.8 %collective-permute-done.1.mine_ref = bf16[5,64,512]{2,1,0:T(8,128)(2,1)S(1)} collective-permute-done((bf16[5,64,512]{2,1,0:T(8,128)(2,1)S(1)}, bf16[5,64,512]{2,1,0:T(8,128)(2,1)S(1)}, u32[]{:S(2)}, u32[]{:S(2)}) %collective-permute-start.1) | collective-permute-done | bytes 327712 | tf_op jit(solution)/shard_map/ppermute | solution.py:100
  12.1 0.6 %collective-permute-start.2 = (bf16[5,64,512]{2,1,0:T(8,128)(2,1)S(1)}, bf16[5,64,512]{2,1,0:T(8,128)(2,1)S(1)}, u32[]{:S(2)}, u32[]{:S(2)}) collective-permute-start(bf16[5,64,512]{2,1,0:T(8,128)(2,1)S(1)} %collective-permute-done.1.mine_ref), channel_id=1, source_target_pairs={{0,4},{4,0},{1,5},{5,1},{2,6},{6,2},{3,7},{7,3},{8,12},{12,8},{9,1... | collective-permute-start | bytes 983048 | tf_op jit(solution)/shard_map/ppermute | solution.py:51
  12.7 1.3 %collective-permute-start.3 = (bf16[512,256]{1,0:T(8,128)(2,1)S(1)}, bf16[512,256]{1,0:T(8,128)(2,1)S(1)}, u32[]{:S(2)}, u32[]{:S(2)}) collective-permute-start(bf16[512,256]{1,0:T(8,128)(2,1)S(1)} %get-tuple-element.43.end_ref), channel_id=1, source_target_pairs={{0,8},{8,0},{16,24},{4,20},{12,28},{1,9},{9,1},{17,25},{5,21},{13,... | collective-permute-start | bytes 786440 | tf_op jit(solution)/shard_map/ppermute | solution.py:329
  14.0 0.0 collective-permute-done.2.theirs_ref
  14.0 0.2 shard_map.68
  14.2 0.0 copy-start.5
  14.2 0.0 slice-start
  14.2 1.0 %shard_map.69 = (f32[2,32,16,256]{3,2,1,0:T(8,128)S(1)}, f32[2,64,256]{2,1,0:T(8,128)S(1)}, f32[2,128,256]{2,1,0:T(8,128)S(1)}, bf16[640,256]{1,0:T(8,128)(2,1)S(1)}) custom-call(bf16[256,1536]{1,0:T(8,128)(2,1)S(1)} %get-tuple-element.39.lhs_ref, bf16[3,3,512,512]{3,2,1,0:T(8,128)(2,1)S(1)} %copy-done.1, ...), custom_call_target="tpu_custom_call" | custom-call | flops 603979776 | bytes 9635840 | tf_op jit(solution)/shard_map/pallas_call | solution.py:21
  15.2 1.4 %collective-permute-start.5 = (bf16[640,256]{1,0:T(8,128)(2,1)S(1)}, bf16[640,256]{1,0:T(8,128)(2,1)S(1)}, u32[]{:S(2)}, u32[]{:S(2)}) collective-permute-start(bf16[640,256]{1,0:T(8,128)(2,1)S(1)} %get-tuple-element.44.end_ref), channel_id=1, source_target_pairs={{0,8},{8,0},{16,24},{4,20},{12,28},{1,9},{9,1},{17,25},{5,21},{13,... | collective-permute-start | bytes 983048 | tf_op jit(solution)/shard_map/ppermute | solution.py:329
  16.7 3.4 %collective-permute-done.3.got_ref.refs_4_.refs_7_ = bf16[512,256]{1,0:T(8,128)(2,1)S(1)} collective-permute-done((bf16[512,256]{1,0:T(8,128)(2,1)S(1)}, bf16[512,256]{1,0:T(8,128)(2,1)S(1)}, u32[]{:S(2)}, u32[]{:S(2)}) %collective-permute-start.3) | collective-permute-done | bytes 262176 | tf_op jit(solution)/shard_map/ppermute | solution.py:329
  20.1 0.2 shard_map.70
  20.3 1.9 %collective-permute-start.4 = (bf16[512,256]{1,0:T(8,128)(2,1)S(1)}, bf16[512,256]{1,0:T(8,128)(2,1)S(1)}, u32[]{:S(2)}, u32[]{:S(2)}) collective-permute-start(bf16[512,256]{1,0:T(8,128)(2,1)S(1)} %shard_map.70), channel_id=1, source_target_pairs={{0,16},{8,24},{4,12},{20,28},{28,20},{1,17},{9,25},{5,13},{21,29},... | collective-permute-start | bytes 786440 | tf_op jit(solution)/shard_map/ppermute | solution.py:332
  22.2 1.4 %collective-permute-done.5.got_ref.refs_6_.refs_9_.refs_5_ = bf16[640,256]{1,0:T(8,128)(2,1)S(1)} collective-permute-done((bf16[640,256]{1,0:T(8,128)(2,1)S(1)}, bf16[640,256]{1,0:T(8,128)(2,1)S(1)}, u32[]{:S(2)}, u32[]{:S(2)}) %collective-permute-start.5) | collective-permute-done | bytes 327712 | tf_op jit(solution)/shard_map/ppermute | solution.py:329
  23.6 0.2 shard_map.71
  23.8 2.1 %collective-permute-start.6 = (bf16[640,256]{1,0:T(8,128)(2,1)S(1)}, bf16[640,256]{1,0:T(8,128)(2,1)S(1)}, u32[]{:S(2)}, u32[]{:S(2)}) collective-permute-start(bf16[640,256]{1,0:T(8,128)(2,1)S(1)} %shard_map.71), channel_id=1, source_target_pairs={{0,16},{8,24},{4,12},{20,28},{28,20},{1,17},{9,25},{5,13},{21,29},... | collective-permute-start | bytes 983048 | tf_op jit(solution)/shard_map/ppermute | solution.py:332
  25.9 1.7 %collective-permute-done.4.refs_5_.refs_8_ = bf16[512,256]{1,0:T(8,128)(2,1)S(1)} collective-permute-done((bf16[512,256]{1,0:T(8,128)(2,1)S(1)}, bf16[512,256]{1,0:T(8,128)(2,1)S(1)}, u32[]{:S(2)}, u32[]{:S(2)}) %collective-permute-start.4) | collective-permute-done | bytes 262176 | tf_op jit(solution)/shard_map/ppermute | solution.py:332
  27.7 0.0 copy-done.5
  27.7 0.0 slice-start.1
  27.7 1.8 %collective-permute-start.7 = (bf16[2,16,256]{2,1,0:T(8,128)(2,1)S(1)}, bf16[2,16,256]{2,1,0:T(8,128)(2,1)S(1)}, u32[]{:S(2)}, u32[]{:S(2)}) collective-permute-start(bf16[2,16,256]{2,1,0:T(8,128)(2,1)S(1)} %shard_map.74), channel_id=1, source_target_pairs={{0,4},{4,0},{1,5},{5,1},{2,6},{6,2},{3,7},{7,3},{8,12},{12,8},{9,1... | collective-permute-start | bytes 49160 | tf_op jit(solution)/shard_map/ppermute | solution.py:51
  29.5 0.6 %shard_map.72._ = bf16[1024,768]{1,0:T(8,128)(2,1)S(1)} custom-call(f32[2,32,16,512]{3,2,1,0:T(8,128)S(1)} %get-tuple-element.40.total_ref.refs_0_, f32[32,16,512]{2,1,0:T(8,128)S(1)} %copy-done, s32[1,512]{1,0:T(1,128)S(1)} %bitcast.10, f32[1,512]{1,0:T(1,128)S(1)} %bitcast.15, bf16[512,256]{1,0:T(8,128)(2,1)S(1)} %collective-permute-done.3.got_ref.refs_4_.refs_7_, ...), custom_call_target="tpu_custom_call" | custom-call | bytes 5246976 | tf_op jit(solution)/shard_map/pallas_call | solution.py:21
  30.1 0.1 shard_map.73.refs_4_.refs_2_
  30.2 0.2 collective-permute-done.7.got_ref
  30.4 0.0 slice-done
  30.4 0.0 slice-done.1
  30.4 1.4 %shard_map.75 = (f32[2,32,16,256]{3,2,1,0:T(8,128)S(1)}, bf16[1024,768]{1,0:T(8,128)(2,1)S(1)}) custom-call(bf16[1024,768]{1,0:T(8,128)(2,1)S(1)} %shard_map.72._, bf16[2,16,256]{2,1,0:T(8,128)(2,1)S(1)} %collective-permute-done.7.got_ref, bf16[3,3,512,512]{3,2,1,0:T(8,128)(2,1)S(1)} %bitcast.4), custom_call_target="tpu_custom_call", output_to_operand_aliasing={{1}: (0, {})} | custom-call | flops 1207959552 | bytes 8929280 | tf_op jit(solution)/shard_map/pallas_call | solution.py:21
  31.8 1.4 %shard_map.76.refs_1_ = f32[2,32,16,256]{3,2,1,0:T(8,128)S(1)} custom-call(bf16[1024,768]{1,0:T(8,128)(2,1)S(1)} %get-tuple-element.48.lhs_ref, bf16[3,3,512,512]{3,2,1,0:T(8,128)(2,1)S(1)} %bitcast.4), custom_call_target="tpu_custom_call" | custom-call | flops 1207959552 | bytes 7340032 | tf_op jit(solution)/shard_map/pallas_call | solution.py:21
  33.2 0.0 collective-permute-done.6.refs_7_.refs_10_.refs_6_
  33.2 0.1 shard_map.78
  33.3 0.7 %collective-permute-start.8 = (bf16[2,32,256]{2,1,0:T(8,128)(2,1)S(1)}, bf16[2,32,256]{2,1,0:T(8,128)(2,1)S(1)}, u32[]{:S(2)}, u32[]{:S(2)}) collective-permute-start(bf16[2,32,256]{2,1,0:T(8,128)(2,1)S(1)} %shard_map.78), channel_id=1, source_target_pairs={{0,4},{4,0},{1,5},{5,1},{2,6},{6,2},{3,7},{7,3},{8,12},{12,8},{9,1... | collective-permute-start | bytes 98312 | tf_op jit(solution)/shard_map/ppermute | solution.py:51
  34.0 0.3 shard_map.79
  34.4 0.7 %shard_map.77._ = bf16[1152,768]{1,0:T(8,128)(2,1)S(1)} custom-call(f32[2,32,16,256]{3,2,1,0:T(8,128)S(1)} %get-tuple-element.42.refs_0_, f32[32,16,512]{2,1,0:T(8,128)S(1)} %copy-done, s32[1,512]{1,0:T(1,128)S(1)} %bitcast.13, f32[1,512]{1,0:T(1,128)S(1)} %bitcast.18, bf16[512,256]{1,0:T(8,128)(2,1)S(1)} %collective-permute-done.3.got_ref.refs_4_.refs_7_, ...), custom_call_target="tpu_custom_call" | custom-call | bytes 5050368 | tf_op jit(solution)/shard_map/pallas_call | solution.py:21
  35.0 0.0 collective-permute-done.8.got_ref
  35.0 4.2 %shard_map.80 = (bf16[2,32,16,512]{3,2,1,0:T(8,128)(2,1)}, bf16[1152,768]{1,0:T(8,128)(2,1)S(1)}) custom-call(bf16[1152,768]{1,0:T(8,128)(2,1)S(1)} %shard_map.77._, bf16[2,32,256]{2,1,0:T(8,128)(2,1)S(1)} %collective-permute-done.8.got_ref, bf16[2,64,256]{2,1,0:T(8,128)(2,1)S(1)} %get-tuple-element.54.beside_ref, ...), custom_call_target="tpu_custom_call", output_to_operand_aliasing={{1}: (0, {})} | custom-call | flops 2415919104 | bytes 11632640 | tf_op jit(solution)/shard_map/pallas_call | solution.py:21
  (4 shorter events, 0.1 us)
Async XLA Ops:
  0.0 1.7 %copy-start = (f32[32,16,512]{2,1,0:T(8,128)S(1)}, f32[32,16,512]{2,1,0:T(8,128)}, u32[]{:S(2)}) copy-start(f32[32,16,512]{2,1,0:T(8,128)} %refs_3_.1) | copy-start | bytes 3145732
  0.0 1.3 %copy-start.2 = (bf16[2,32,16,512]{3,2,1,0:T(8,128)(2,1)S(1)}, bf16[2,32,16,512]{3,2,1,0:T(8,128)(2,1)}, u32[]{:S(2)}) copy-start(bf16[2,32,16,512]{3,2,1,0:T(8,128)(2,1)} %cells_ref.3) | copy-start | bytes 3145732
  1.7 1.2 %copy-start.3 = (bf16[2,32,16,512]{3,2,1,0:T(8,128)(2,1)S(1)}, bf16[2,32,16,512]{3,2,1,0:T(8,128)(2,1)}, u32[]{:S(2)}) copy-start(bf16[2,32,16,512]{3,2,1,0:T(8,128)(2,1)} %cells_ref.3) | copy-start | bytes 3145732
  1.8 4.2 %copy-start.1 = (bf16[3,3,512,512]{3,2,1,0:T(8,128)(2,1)S(1)}, bf16[3,3,512,512]{3,2,1,0:T(8,128)(2,1)}, u32[]{:S(2)}) copy-start(bf16[3,3,512,512]{3,2,1,0:T(8,128)(2,1)} %weight_ref.6) | copy-start | bytes 14155780
  1.9 4.2 %copy-start.4 = (s32[512]{0:T(512)S(1)}, s32[512]{0:T(512)}, u32[]{:S(2)}) copy-start(s32[512]{0:T(512)} %param.9) | copy-start | bytes 6148
  1.9 1.8 %collective-permute-start = (bf16[192,512]{1,0:T(8,128)(2,1)S(1)}, bf16[192,512]{1,0:T(8,128)(2,1)S(1)}, u32[]{:S(2)}, u32[]{:S(2)}) collective-permute-start(bf16[192,512]{1,0:T(8,128)(2,1)S(1)} %get-tuple-element.35), channel_id=1, source_target_pairs={{0,4},{4,0},{1,5},{5,1},{2,6},{6,2},{3,7},{7,3},{8,12},{12,8},{9,1... | collective-permute-start | bytes 589832 | tf_op jit(solution)/shard_map/ppermute | solution.py:51
  3.7 8.4 %collective-permute-start.1 = (bf16[5,64,512]{2,1,0:T(8,128)(2,1)S(1)}, bf16[5,64,512]{2,1,0:T(8,128)(2,1)S(1)}, u32[]{:S(2)}, u32[]{:S(2)}) collective-permute-start(bf16[5,64,512]{2,1,0:T(8,128)(2,1)S(1)} %pad_maximum_fusion), channel_id=1, source_target_pairs={{0,5},{1,6},{2,7},{5,0},{6,1},{7,2},{8,13},{9,14},{10,15},{13,8},{... | collective-permute-start | bytes 983048 | tf_op jit(solution)/shard_map/ppermute | solution.py:100
  12.1 1.9 %collective-permute-start.2 = (bf16[5,64,512]{2,1,0:T(8,128)(2,1)S(1)}, bf16[5,64,512]{2,1,0:T(8,128)(2,1)S(1)}, u32[]{:S(2)}, u32[]{:S(2)}) collective-permute-start(bf16[5,64,512]{2,1,0:T(8,128)(2,1)S(1)} %collective-permute-done.1.mine_ref), channel_id=1, source_target_pairs={{0,4},{4,0},{1,5},{5,1},{2,6},{6,2},{3,7},{7,3},{8,12},{12,8},{9,1... | collective-permute-start | bytes 983048 | tf_op jit(solution)/shard_map/ppermute | solution.py:51
  12.7 7.4 %collective-permute-start.3 = (bf16[512,256]{1,0:T(8,128)(2,1)S(1)}, bf16[512,256]{1,0:T(8,128)(2,1)S(1)}, u32[]{:S(2)}, u32[]{:S(2)}) collective-permute-start(bf16[512,256]{1,0:T(8,128)(2,1)S(1)} %get-tuple-element.43.end_ref), channel_id=1, source_target_pairs={{0,8},{8,0},{16,24},{4,20},{12,28},{1,9},{9,1},{17,25},{5,21},{13,... | collective-permute-start | bytes 786440 | tf_op jit(solution)/shard_map/ppermute | solution.py:329
  14.2 13.5 %copy-start.5 = (f32[512]{0:T(512)S(1)}, f32[512]{0:T(512)}, u32[]{:S(2)}) copy-start(f32[512]{0:T(512)} %param.10) | copy-start | bytes 6148
  14.2 16.2 %slice-start = ((s8[4718592]{0:T(1024)(128)(4,1)}), s8[4194304]{0:T(1024)(128)(4,1)S(1)}, s32[]{:S(2)}) async-start(s8[4718592]{0:T(1024)(128)(4,1)} %bitcast.3), calls=%async_computation | async-start | bytes 8388608
  15.2 8.4 %collective-permute-start.5 = (bf16[640,256]{1,0:T(8,128)(2,1)S(1)}, bf16[640,256]{1,0:T(8,128)(2,1)S(1)}, u32[]{:S(2)}, u32[]{:S(2)}) collective-permute-start(bf16[640,256]{1,0:T(8,128)(2,1)S(1)} %get-tuple-element.44.end_ref), channel_id=1, source_target_pairs={{0,8},{8,0},{16,24},{4,20},{12,28},{1,9},{9,1},{17,25},{5,21},{13,... | collective-permute-start | bytes 983048 | tf_op jit(solution)/shard_map/ppermute | solution.py:329
  20.3 7.4 %collective-permute-start.4 = (bf16[512,256]{1,0:T(8,128)(2,1)S(1)}, bf16[512,256]{1,0:T(8,128)(2,1)S(1)}, u32[]{:S(2)}, u32[]{:S(2)}) collective-permute-start(bf16[512,256]{1,0:T(8,128)(2,1)S(1)} %shard_map.70), channel_id=1, source_target_pairs={{0,16},{8,24},{4,12},{20,28},{28,20},{1,17},{9,25},{5,13},{21,29},... | collective-permute-start | bytes 786440 | tf_op jit(solution)/shard_map/ppermute | solution.py:332
  23.8 9.4 %collective-permute-start.6 = (bf16[640,256]{1,0:T(8,128)(2,1)S(1)}, bf16[640,256]{1,0:T(8,128)(2,1)S(1)}, u32[]{:S(2)}, u32[]{:S(2)}) collective-permute-start(bf16[640,256]{1,0:T(8,128)(2,1)S(1)} %shard_map.71), channel_id=1, source_target_pairs={{0,16},{8,24},{4,12},{20,28},{28,20},{1,17},{9,25},{5,13},{21,29},... | collective-permute-start | bytes 983048 | tf_op jit(solution)/shard_map/ppermute | solution.py:332
  27.7 2.7 %slice-start.1 = ((s8[4718592]{0:T(1024)(128)(4,1)}), s8[524288]{0:T(1024)(128)(4,1)S(1)}, s32[]{:S(2)}) async-start(s8[4718592]{0:T(1024)(128)(4,1)} %bitcast.3), calls=%async_computation.1 | async-start | bytes 1048576
  27.7 2.6 %collective-permute-start.7 = (bf16[2,16,256]{2,1,0:T(8,128)(2,1)S(1)}, bf16[2,16,256]{2,1,0:T(8,128)(2,1)S(1)}, u32[]{:S(2)}, u32[]{:S(2)}) collective-permute-start(bf16[2,16,256]{2,1,0:T(8,128)(2,1)S(1)} %shard_map.74), channel_id=1, source_target_pairs={{0,4},{4,0},{1,5},{5,1},{2,6},{6,2},{3,7},{7,3},{8,12},{12,8},{9,1... | collective-permute-start | bytes 49160 | tf_op jit(solution)/shard_map/ppermute | solution.py:51
  33.3 1.7 %collective-permute-start.8 = (bf16[2,32,256]{2,1,0:T(8,128)(2,1)S(1)}, bf16[2,32,256]{2,1,0:T(8,128)(2,1)S(1)}, u32[]{:S(2)}, u32[]{:S(2)}) collective-permute-start(bf16[2,32,256]{2,1,0:T(8,128)(2,1)S(1)} %shard_map.78), channel_id=1, source_target_pairs={{0,4},{4,0},{1,5},{5,1},{2,6},{6,2},{3,7},{7,3},{8,12},{12,8},{9,1... | collective-permute-start | bytes 98312 | tf_op jit(solution)/shard_map/ppermute | solution.py:51

commit v22 on v21

--- a/solution.py
+++ b/solution.py
@@ -559,16 +559,13 @@
     first = dot(lhs_ref[: 2 * room], weight_ref, 0, lanes, inputs)
     middle = dot(lhs_ref[room : 3 * room], weight_ref, 1, lanes, inputs)
     last = dot(lhs_ref[2 * room :], weight_ref, 2, lanes, inputs)
-    col = lax.broadcasted_iota(jnp.int32, tile, 2)
-    total = 0.0
-    for at, cells in (
+    columns = [
         (0, first[:room] + middle[:room]),
         (1, first[room:]),
         (cols - 2, last[:room]),
         (cols - 1, middle[room:] + last[room:]),
-    ):
-        total = jnp.where(col == at, cells.reshape(count, rows, 1, wide), total)
-    return total
+    ]
+    return [(at, cells.reshape(count, rows, 1, wide)) for at, cells in columns]
 
 
 def opening_kernel(inputs, lanes, _, got_ref, weight_ref, out_ref, lhs_ref):
@@ -606,10 +603,14 @@
 
     for part, lanes in enumerate(parts):
         tile = (count, rows, cols, lanes.stop - lanes.start)
-        strips = strip_sum(tile, parts[0], lanes, strip_lhs_ref, weight_ref)
+        col = lax.broadcasted_iota(jnp.int32, tile[1:], 1)
+        columns = strip_sum(tile, parts[0], lanes, strip_lhs_ref, weight_ref)
         tiles = tile_sum(tile, parts[1], lanes, rows, lhs_ref, weight_ref)
         for frame, total in enumerate(tiles):
-            total += before_refs[part][frame] + strips[frame]
+            strips = 0.0
+            for at, cells in columns:
+                strips = jnp.where(col == at, cells[frame], strips)
+            total += before_refs[part][frame] + strips
             held_ref[frame, :, :, lanes] = total.astype(held_ref.dtype)
             store(frame, part).start()
     for part in range(len(parts)):

time: 39.9 us -> 39.9 us (level)
  no operation moved by 1% of the time
where the time goes in v22:
time: 39.9 us; the launch traced here: 39.5 us
  Pallas kernels  16.4 us (41%)
  starting transfers between devices  12.9 us (32%)
  waiting for transfers between devices  8.08 us (20%)
  local copies, waits for them, and re-layouts  1.67 us (4%)
  between operations  0.41 us (1%)
    pallas_call x17, Pallas kernels, call(): pl.pallas_call(kernel, in_specs=[WHOLE] * len(args), out_specs=out_specs...  16.4 us
    ppermute x2, waiting for transfers between devices, exchange_four(): got = lax.ppermute(end, axes, first_round)  4.83 us
    ppermute x2, starting transfers between devices, exchange_four(): arrivals.append((got, lax.ppermute(relayed, axes, second_round)))  4.07 us
    ppermute x4, starting transfers between devices, swap_cores(): return lax.ppermute(array, 'sx', [(0, 1), (1, 0)])  3.8 us
    ppermute x2, starting transfers between devices, exchange_four(): got = lax.ppermute(end, axes, first_round)  2.7 us
    ppermute x1, starting transfers between devices, trade_columns(): return (got, lax.ppermute(columns, ('sx', 'sy'), pairs))  2.33 us
    ppermute x2, waiting for transfers between devices, exchange_four(): arrivals.append((got, lax.ppermute(relayed, axes, second_round)))  1.73 us
    unnamed x16, local copies, waits for them, and re-layouts  1.66 us
  transfers between devices with their start and end apart: 9, of which 6 were waited for; matrix products, arithmetic and copies ran while one was open for 0% of the time, Pallas kernels for 29%

profile of v22, /device:TPU:23, one launch (start us, length us, event | category | flops | bytes accessed | tf_op | source)
XLA Modules:
  0.0 39.5 jit_solution(15546142520305683535)
XLA Ops:
  0.0 0.0 copy-start
  0.0 0.0 copy-start.2
  0.0 1.3 %copy-done.2 = bf16[2,32,16,512]{3,2,1,0:T(8,128)(2,1)S(1)} copy-done((bf16[2,32,16,512]{3,2,1,0:T(8,128)(2,1)S(1)}, bf16[2,32,16,512]{3,2,1,0:T(8,128)(2,1)}, u32[]{:S(2)}) %copy-start.2) | copy-done | bytes 1048600
  1.3 0.4 shard_map.64
  1.7 0.0 copy-start.3
  1.7 0.0 copy-done
  1.7 0.1 shard_map.65
  1.8 0.0 copy-start.1
  1.9 0.0 copy-start.4
  1.9 0.7 %collective-permute-start = (bf16[192,512]{1,0:T(8,128)(2,1)S(1)}, bf16[192,512]{1,0:T(8,128)(2,1)S(1)}, u32[]{:S(2)}, u32[]{:S(2)}) collective-permute-start(bf16[192,512]{1,0:T(8,128)(2,1)S(1)} %get-tuple-element.35), channel_id=1, source_target_pairs={{0,4},{4,0},{1,5},{5,1},{2,6},{6,2},{3,7},{7,3},{8,12},{12,8},{9,1... | collective-permute-start | bytes 589832 | tf_op jit(solution)/shard_map/ppermute | solution.py:51
  2.6 0.3 copy-done.3
  2.9 0.2 shard_map.66._
  3.1 0.6 %collective-permute-done.got_ref = bf16[192,512]{1,0:T(8,128)(2,1)S(1)} collective-permute-done((bf16[192,512]{1,0:T(8,128)(2,1)S(1)}, bf16[192,512]{1,0:T(8,128)(2,1)S(1)}, u32[]{:S(2)}, u32[]{:S(2)}) %collective-permute-start) | collective-permute-done | bytes 196640 | tf_op jit(solution)/shard_map/ppermute | solution.py:51
  3.7 2.3 %collective-permute-start.1 = (bf16[5,64,512]{2,1,0:T(8,128)(2,1)S(1)}, bf16[5,64,512]{2,1,0:T(8,128)(2,1)S(1)}, u32[]{:S(2)}, u32[]{:S(2)}) collective-permute-start(bf16[5,64,512]{2,1,0:T(8,128)(2,1)S(1)} %pad_maximum_fusion), channel_id=1, source_target_pairs={{0,5},{1,6},{2,7},{5,0},{6,1},{7,2},{8,13},{9,14},{10,15},{13,8},{... | collective-permute-start | bytes 983048 | tf_op jit(solution)/shard_map/ppermute | solution.py:100
  6.1 0.0 copy-done.1
  6.1 0.0 copy-done.4
  6.1 5.3 %shard_map.67 = (f32[2,32,16,512]{3,2,1,0:T(8,128)S(1)}, f32[2,64,512]{2,1,0:T(8,128)S(1)}, bf16[512,256]{1,0:T(8,128)(2,1)S(1)}, bf16[1024,1536]{1,0:T(8,128)(2,1)S(1)}) custom-call(bf16[1024,1536]{1,0:T(8,128)(2,1)S(1)} %shard_map.66._, bf16[192,512]{1,0:T(8,128)(2,1)S(1)} %collective-permute-done.got_ref, ...), custom_call_target="tpu_custom_call", output_to_operand_aliasing={{3}: (0, {})} | custom-call | flops 4831838208 | bytes 13830144 | tf_op jit(solution)/shard_map/pallas_call | solution.py:21
  11.3 0.8 %collective-permute-done.1.mine_ref = bf16[5,64,512]{2,1,0:T(8,128)(2,1)S(1)} collective-permute-done((bf16[5,64,512]{2,1,0:T(8,128)(2,1)S(1)}, bf16[5,64,512]{2,1,0:T(8,128)(2,1)S(1)}, u32[]{:S(2)}, u32[]{:S(2)}) %collective-permute-start.1) | collective-permute-done | bytes 327712 | tf_op jit(solution)/shard_map/ppermute | solution.py:100
  12.1 0.6 %collective-permute-start.2 = (bf16[5,64,512]{2,1,0:T(8,128)(2,1)S(1)}, bf16[5,64,512]{2,1,0:T(8,128)(2,1)S(1)}, u32[]{:S(2)}, u32[]{:S(2)}) collective-permute-start(bf16[5,64,512]{2,1,0:T(8,128)(2,1)S(1)} %collective-permute-done.1.mine_ref), channel_id=1, source_target_pairs={{0,4},{4,0},{1,5},{5,1},{2,6},{6,2},{3,7},{7,3},{8,12},{12,8},{9,1... | collective-permute-start | bytes 983048 | tf_op jit(solution)/shard_map/ppermute | solution.py:51
  12.7 1.3 %collective-permute-start.3 = (bf16[512,256]{1,0:T(8,128)(2,1)S(1)}, bf16[512,256]{1,0:T(8,128)(2,1)S(1)}, u32[]{:S(2)}, u32[]{:S(2)}) collective-permute-start(bf16[512,256]{1,0:T(8,128)(2,1)S(1)} %get-tuple-element.43.end_ref), channel_id=1, source_target_pairs={{0,8},{8,0},{16,24},{4,20},{12,28},{1,9},{9,1},{17,25},{5,21},{13,... | collective-permute-start | bytes 786440 | tf_op jit(solution)/shard_map/ppermute | solution.py:329
  14.0 0.0 collective-permute-done.2.theirs_ref
  14.0 0.2 shard_map.68
  14.2 0.0 copy-start.5
  14.2 0.0 slice-start
  14.2 1.0 %shard_map.69 = (f32[2,32,16,256]{3,2,1,0:T(8,128)S(1)}, f32[2,64,256]{2,1,0:T(8,128)S(1)}, f32[2,128,256]{2,1,0:T(8,128)S(1)}, bf16[640,256]{1,0:T(8,128)(2,1)S(1)}) custom-call(bf16[256,1536]{1,0:T(8,128)(2,1)S(1)} %get-tuple-element.39.lhs_ref, bf16[3,3,512,512]{3,2,1,0:T(8,128)(2,1)S(1)} %copy-done.1, ...), custom_call_target="tpu_custom_call" | custom-call | flops 603979776 | bytes 9635840 | tf_op jit(solution)/shard_map/pallas_call | solution.py:21
  15.2 1.4 %collective-permute-start.5 = (bf16[640,256]{1,0:T(8,128)(2,1)S(1)}, bf16[640,256]{1,0:T(8,128)(2,1)S(1)}, u32[]{:S(2)}, u32[]{:S(2)}) collective-permute-start(bf16[640,256]{1,0:T(8,128)(2,1)S(1)} %get-tuple-element.44.end_ref), channel_id=1, source_target_pairs={{0,8},{8,0},{16,24},{4,20},{12,28},{1,9},{9,1},{17,25},{5,21},{13,... | collective-permute-start | bytes 983048 | tf_op jit(solution)/shard_map/ppermute | solution.py:329
  16.7 3.4 %collective-permute-done.3.got_ref.refs_4_.refs_7_ = bf16[512,256]{1,0:T(8,128)(2,1)S(1)} collective-permute-done((bf16[512,256]{1,0:T(8,128)(2,1)S(1)}, bf16[512,256]{1,0:T(8,128)(2,1)S(1)}, u32[]{:S(2)}, u32[]{:S(2)}) %collective-permute-start.3) | collective-permute-done | bytes 262176 | tf_op jit(solution)/shard_map/ppermute | solution.py:329
  20.1 0.2 shard_map.70
  20.3 1.9 %collective-permute-start.4 = (bf16[512,256]{1,0:T(8,128)(2,1)S(1)}, bf16[512,256]{1,0:T(8,128)(2,1)S(1)}, u32[]{:S(2)}, u32[]{:S(2)}) collective-permute-start(bf16[512,256]{1,0:T(8,128)(2,1)S(1)} %shard_map.70), channel_id=1, source_target_pairs={{0,16},{8,24},{4,12},{20,28},{28,20},{1,17},{9,25},{5,13},{21,29},... | collective-permute-start | bytes 786440 | tf_op jit(solution)/shard_map/ppermute | solution.py:332
  22.2 1.4 %collective-permute-done.5.got_ref.refs_6_.refs_9_.refs_5_ = bf16[640,256]{1,0:T(8,128)(2,1)S(1)} collective-permute-done((bf16[640,256]{1,0:T(8,128)(2,1)S(1)}, bf16[640,256]{1,0:T(8,128)(2,1)S(1)}, u32[]{:S(2)}, u32[]{:S(2)}) %collective-permute-start.5) | collective-permute-done | bytes 327712 | tf_op jit(solution)/shard_map/ppermute | solution.py:329
  23.6 0.2 shard_map.71
  23.8 2.1 %collective-permute-start.6 = (bf16[640,256]{1,0:T(8,128)(2,1)S(1)}, bf16[640,256]{1,0:T(8,128)(2,1)S(1)}, u32[]{:S(2)}, u32[]{:S(2)}) collective-permute-start(bf16[640,256]{1,0:T(8,128)(2,1)S(1)} %shard_map.71), channel_id=1, source_target_pairs={{0,16},{8,24},{4,12},{20,28},{28,20},{1,17},{9,25},{5,13},{21,29},... | collective-permute-start | bytes 983048 | tf_op jit(solution)/shard_map/ppermute | solution.py:332
  25.9 1.7 %collective-permute-done.4.refs_5_.refs_8_ = bf16[512,256]{1,0:T(8,128)(2,1)S(1)} collective-permute-done((bf16[512,256]{1,0:T(8,128)(2,1)S(1)}, bf16[512,256]{1,0:T(8,128)(2,1)S(1)}, u32[]{:S(2)}, u32[]{:S(2)}) %collective-permute-start.4) | collective-permute-done | bytes 262176 | tf_op jit(solution)/shard_map/ppermute | solution.py:332
  27.7 0.0 copy-done.5
  27.7 0.0 slice-start.1
  27.7 1.8 %collective-permute-start.7 = (bf16[2,16,256]{2,1,0:T(8,128)(2,1)S(1)}, bf16[2,16,256]{2,1,0:T(8,128)(2,1)S(1)}, u32[]{:S(2)}, u32[]{:S(2)}) collective-permute-start(bf16[2,16,256]{2,1,0:T(8,128)(2,1)S(1)} %shard_map.74), channel_id=1, source_target_pairs={{0,4},{4,0},{1,5},{5,1},{2,6},{6,2},{3,7},{7,3},{8,12},{12,8},{9,1... | collective-permute-start | bytes 49160 | tf_op jit(solution)/shard_map/ppermute | solution.py:51
  29.5 0.6 %shard_map.72._ = bf16[1024,768]{1,0:T(8,128)(2,1)S(1)} custom-call(f32[2,32,16,512]{3,2,1,0:T(8,128)S(1)} %get-tuple-element.40.total_ref.refs_0_, f32[32,16,512]{2,1,0:T(8,128)S(1)} %copy-done, s32[1,512]{1,0:T(1,128)S(1)} %bitcast.10, f32[1,512]{1,0:T(1,128)S(1)} %bitcast.15, bf16[512,256]{1,0:T(8,128)(2,1)S(1)} %collective-permute-done.3.got_ref.refs_4_.refs_7_, ...), custom_call_target="tpu_custom_call" | custom-call | bytes 5246976 | tf_op jit(solution)/shard_map/pallas_call | solution.py:21
  30.1 0.1 shard_map.73.refs_4_.refs_2_
  30.2 0.2 collective-permute-done.7.got_ref
  30.4 0.0 slice-done
  30.4 0.0 slice-done.1
  30.4 1.4 %shard_map.75 = (f32[2,32,16,256]{3,2,1,0:T(8,128)S(1)}, bf16[1024,768]{1,0:T(8,128)(2,1)S(1)}) custom-call(bf16[1024,768]{1,0:T(8,128)(2,1)S(1)} %shard_map.72._, bf16[2,16,256]{2,1,0:T(8,128)(2,1)S(1)} %collective-permute-done.7.got_ref, bf16[3,3,512,512]{3,2,1,0:T(8,128)(2,1)S(1)} %bitcast.4), custom_call_target="tpu_custom_call", output_to_operand_aliasing={{1}: (0, {})} | custom-call | flops 1207959552 | bytes 8929280 | tf_op jit(solution)/shard_map/pallas_call | solution.py:21
  31.8 1.4 %shard_map.76.refs_1_ = f32[2,32,16,256]{3,2,1,0:T(8,128)S(1)} custom-call(bf16[1024,768]{1,0:T(8,128)(2,1)S(1)} %get-tuple-element.48.lhs_ref, bf16[3,3,512,512]{3,2,1,0:T(8,128)(2,1)S(1)} %bitcast.4), custom_call_target="tpu_custom_call" | custom-call | flops 1207959552 | bytes 7340032 | tf_op jit(solution)/shard_map/pallas_call | solution.py:21
  33.2 0.0 collective-permute-done.6.refs_7_.refs_10_.refs_6_
  33.2 0.1 shard_map.78
  33.3 0.7 %collective-permute-start.8 = (bf16[2,32,256]{2,1,0:T(8,128)(2,1)S(1)}, bf16[2,32,256]{2,1,0:T(8,128)(2,1)S(1)}, u32[]{:S(2)}, u32[]{:S(2)}) collective-permute-start(bf16[2,32,256]{2,1,0:T(8,128)(2,1)S(1)} %shard_map.78), channel_id=1, source_target_pairs={{0,4},{4,0},{1,5},{5,1},{2,6},{6,2},{3,7},{7,3},{8,12},{12,8},{9,1... | collective-permute-start | bytes 98312 | tf_op jit(solution)/shard_map/ppermute | solution.py:51
  34.0 0.3 shard_map.79
  34.4 0.7 %shard_map.77._ = bf16[1152,768]{1,0:T(8,128)(2,1)S(1)} custom-call(f32[2,32,16,256]{3,2,1,0:T(8,128)S(1)} %get-tuple-element.42.refs_0_, f32[32,16,512]{2,1,0:T(8,128)S(1)} %copy-done, s32[1,512]{1,0:T(1,128)S(1)} %bitcast.13, f32[1,512]{1,0:T(1,128)S(1)} %bitcast.18, bf16[512,256]{1,0:T(8,128)(2,1)S(1)} %collective-permute-done.3.got_ref.refs_4_.refs_7_, ...), custom_call_target="tpu_custom_call" | custom-call | bytes 5050368 | tf_op jit(solution)/shard_map/pallas_call | solution.py:21
  35.0 0.0 collective-permute-done.8.got_ref
  35.0 4.2 %shard_map.80 = (bf16[2,32,16,512]{3,2,1,0:T(8,128)(2,1)}, bf16[1152,768]{1,0:T(8,128)(2,1)S(1)}) custom-call(bf16[1152,768]{1,0:T(8,128)(2,1)S(1)} %shard_map.77._, bf16[2,32,256]{2,1,0:T(8,128)(2,1)S(1)} %collective-permute-done.8.got_ref, bf16[2,64,256]{2,1,0:T(8,128)(2,1)S(1)} %get-tuple-element.54.beside_ref, ...), custom_call_target="tpu_custom_call", output_to_operand_aliasing={{1}: (0, {})} | custom-call | flops 2415919104 | bytes 11632640 | tf_op jit(solution)/shard_map/pallas_call | solution.py:21
  (4 shorter events, 0.1 us)
Async XLA Ops:
  0.0 1.7 %copy-start = (f32[32,16,512]{2,1,0:T(8,128)S(1)}, f32[32,16,512]{2,1,0:T(8,128)}, u32[]{:S(2)}) copy-start(f32[32,16,512]{2,1,0:T(8,128)} %refs_3_.1) | copy-start | bytes 3145732
  0.0 1.3 %copy-start.2 = (bf16[2,32,16,512]{3,2,1,0:T(8,128)(2,1)S(1)}, bf16[2,32,16,512]{3,2,1,0:T(8,128)(2,1)}, u32[]{:S(2)}) copy-start(bf16[2,32,16,512]{3,2,1,0:T(8,128)(2,1)} %cells_ref.3) | copy-start | bytes 3145732
  1.7 1.2 %copy-start.3 = (bf16[2,32,16,512]{3,2,1,0:T(8,128)(2,1)S(1)}, bf16[2,32,16,512]{3,2,1,0:T(8,128)(2,1)}, u32[]{:S(2)}) copy-start(bf16[2,32,16,512]{3,2,1,0:T(8,128)(2,1)} %cells_ref.3) | copy-start | bytes 3145732
  1.8 4.2 %copy-start.1 = (bf16[3,3,512,512]{3,2,1,0:T(8,128)(2,1)S(1)}, bf16[3,3,512,512]{3,2,1,0:T(8,128)(2,1)}, u32[]{:S(2)}) copy-start(bf16[3,3,512,512]{3,2,1,0:T(8,128)(2,1)} %weight_ref.6) | copy-start | bytes 14155780
  1.9 4.2 %copy-start.4 = (s32[512]{0:T(512)S(1)}, s32[512]{0:T(512)}, u32[]{:S(2)}) copy-start(s32[512]{0:T(512)} %param.9) | copy-start | bytes 6148
  1.9 1.8 %collective-permute-start = (bf16[192,512]{1,0:T(8,128)(2,1)S(1)}, bf16[192,512]{1,0:T(8,128)(2,1)S(1)}, u32[]{:S(2)}, u32[]{:S(2)}) collective-permute-start(bf16[192,512]{1,0:T(8,128)(2,1)S(1)} %get-tuple-element.35), channel_id=1, source_target_pairs={{0,4},{4,0},{1,5},{5,1},{2,6},{6,2},{3,7},{7,3},{8,12},{12,8},{9,1... | collective-permute-start | bytes 589832 | tf_op jit(solution)/shard_map/ppermute | solution.py:51
  3.7 8.4 %collective-permute-start.1 = (bf16[5,64,512]{2,1,0:T(8,128)(2,1)S(1)}, bf16[5,64,512]{2,1,0:T(8,128)(2,1)S(1)}, u32[]{:S(2)}, u32[]{:S(2)}) collective-permute-start(bf16[5,64,512]{2,1,0:T(8,128)(2,1)S(1)} %pad_maximum_fusion), channel_id=1, source_target_pairs={{0,5},{1,6},{2,7},{5,0},{6,1},{7,2},{8,13},{9,14},{10,15},{13,8},{... | collective-permute-start | bytes 983048 | tf_op jit(solution)/shard_map/ppermute | solution.py:100
  12.1 1.9 %collective-permute-start.2 = (bf16[5,64,512]{2,1,0:T(8,128)(2,1)S(1)}, bf16[5,64,512]{2,1,0:T(8,128)(2,1)S(1)}, u32[]{:S(2)}, u32[]{:S(2)}) collective-permute-start(bf16[5,64,512]{2,1,0:T(8,128)(2,1)S(1)} %collective-permute-done.1.mine_ref), channel_id=1, source_target_pairs={{0,4},{4,0},{1,5},{5,1},{2,6},{6,2},{3,7},{7,3},{8,12},{12,8},{9,1... | collective-permute-start | bytes 983048 | tf_op jit(solution)/shard_map/ppermute | solution.py:51
  12.7 7.4 %collective-permute-start.3 = (bf16[512,256]{1,0:T(8,128)(2,1)S(1)}, bf16[512,256]{1,0:T(8,128)(2,1)S(1)}, u32[]{:S(2)}, u32[]{:S(2)}) collective-permute-start(bf16[512,256]{1,0:T(8,128)(2,1)S(1)} %get-tuple-element.43.end_ref), channel_id=1, source_target_pairs={{0,8},{8,0},{16,24},{4,20},{12,28},{1,9},{9,1},{17,25},{5,21},{13,... | collective-permute-start | bytes 786440 | tf_op jit(solution)/shard_map/ppermute | solution.py:329
  14.2 13.5 %copy-start.5 = (f32[512]{0:T(512)S(1)}, f32[512]{0:T(512)}, u32[]{:S(2)}) copy-start(f32[512]{0:T(512)} %param.10) | copy-start | bytes 6148
  14.2 16.2 %slice-start = ((s8[4718592]{0:T(1024)(128)(4,1)}), s8[4194304]{0:T(1024)(128)(4,1)S(1)}, s32[]{:S(2)}) async-start(s8[4718592]{0:T(1024)(128)(4,1)} %bitcast.3), calls=%async_computation | async-start | bytes 8388608
  15.2 8.4 %collective-permute-start.5 = (bf16[640,256]{1,0:T(8,128)(2,1)S(1)}, bf16[640,256]{1,0:T(8,128)(2,1)S(1)}, u32[]{:S(2)}, u32[]{:S(2)}) collective-permute-start(bf16[640,256]{1,0:T(8,128)(2,1)S(1)} %get-tuple-element.44.end_ref), channel_id=1, source_target_pairs={{0,8},{8,0},{16,24},{4,20},{12,28},{1,9},{9,1},{17,25},{5,21},{13,... | collective-permute-start | bytes 983048 | tf_op jit(solution)/shard_map/ppermute | solution.py:329
  20.3 7.4 %collective-permute-start.4 = (bf16[512,256]{1,0:T(8,128)(2,1)S(1)}, bf16[512,256]{1,0:T(8,128)(2,1)S(1)}, u32[]{:S(2)}, u32[]{:S(2)}) collective-permute-start(bf16[512,256]{1,0:T(8,128)(2,1)S(1)} %shard_map.70), channel_id=1, source_target_pairs={{0,16},{8,24},{4,12},{20,28},{28,20},{1,17},{9,25},{5,13},{21,29},... | collective-permute-start | bytes 786440 | tf_op jit(solution)/shard_map/ppermute | solution.py:332
  23.8 9.4 %collective-permute-start.6 = (bf16[640,256]{1,0:T(8,128)(2,1)S(1)}, bf16[640,256]{1,0:T(8,128)(2,1)S(1)}, u32[]{:S(2)}, u32[]{:S(2)}) collective-permute-start(bf16[640,256]{1,0:T(8,128)(2,1)S(1)} %shard_map.71), channel_id=1, source_target_pairs={{0,16},{8,24},{4,12},{20,28},{28,20},{1,17},{9,25},{5,13},{21,29},... | collective-permute-start | bytes 983048 | tf_op jit(solution)/shard_map/ppermute | solution.py:332
  27.7 2.7 %slice-start.1 = ((s8[4718592]{0:T(1024)(128)(4,1)}), s8[524288]{0:T(1024)(128)(4,1)S(1)}, s32[]{:S(2)}) async-start(s8[4718592]{0:T(1024)(128)(4,1)} %bitcast.3), calls=%async_computation.1 | async-start | bytes 1048576
  27.7 2.6 %collective-permute-start.7 = (bf16[2,16,256]{2,1,0:T(8,128)(2,1)S(1)}, bf16[2,16,256]{2,1,0:T(8,128)(2,1)S(1)}, u32[]{:S(2)}, u32[]{:S(2)}) collective-permute-start(bf16[2,16,256]{2,1,0:T(8,128)(2,1)S(1)} %shard_map.74), channel_id=1, source_target_pairs={{0,4},{4,0},{1,5},{5,1},{2,6},{6,2},{3,7},{7,3},{8,12},{12,8},{9,1... | collective-permute-start | bytes 49160 | tf_op jit(solution)/shard_map/ppermute | solution.py:51
  33.3 1.7 %collective-permute-start.8 = (bf16[2,32,256]{2,1,0:T(8,128)(2,1)S(1)}, bf16[2,32,256]{2,1,0:T(8,128)(2,1)S(1)}, u32[]{:S(2)}, u32[]{:S(2)}) collective-permute-start(bf16[2,32,256]{2,1,0:T(8,128)(2,1)S(1)} %shard_map.78), channel_id=1, source_target_pairs={{0,4},{4,0},{1,5},{5,1},{2,6},{6,2},{3,7},{7,3},{8,12},{12,8},{9,1... | collective-permute-start | bytes 98312 | tf_op jit(solution)/shard_map/ppermute | solution.py:51

commit v23 on v22

--- a/solution.py
+++ b/solution.py
@@ -159,21 +159,17 @@
         put_row(lhs_ref, frame * size, size, got_ref[frame * cols : (frame + 1) * cols])
     states = []
     for lanes in halves(weight_ref.shape[-1]):
-        tile = (rows, cols, lanes.stop - lanes.start)
-        col = lax.broadcasted_iota(jnp.int32, tile, 1)
-        totals = []
-        for frame in range(count):
-            cells = lhs_ref[frame * size : (frame + 1) * size]
-            here = slice(frame * rows, (frame + 1) * rows)
-            total = dot(cells, weight_ref, 1, lanes).reshape(tile)
-            first = dot(cells, weight_ref, 0, lanes).reshape(tile)
-            spill_ref[1, here, lanes] = first[:, cols - 1, :]
-            total += jnp.where(col == 0, 0.0, pltpu.roll(first, 1, 1))
-            last = dot(cells, weight_ref, 2, lanes).reshape(tile)
-            spill_ref[0, here, lanes] = last[:, 0, :]
-            total += jnp.where(col == cols - 1, 0.0, pltpu.roll(last, cols - 1, 1))
-            total_ref[frame, :, :, lanes] = total
-            totals.append(total)
+        tile = (count, rows, cols, lanes.stop - lanes.start)
+        col = lax.broadcasted_iota(jnp.int32, tile, 2)
+        total = dot(lhs_ref[...], weight_ref, 1, lanes).reshape(tile)
+        first = dot(lhs_ref[...], weight_ref, 0, lanes).reshape(tile)
+        spill_ref[1, :, lanes] = first[:, :, cols - 1, :].reshape(count * rows, -1)
+        total += jnp.where(col == 0, 0.0, pltpu.roll(first, 1, 2))
+        last = dot(lhs_ref[...], weight_ref, 2, lanes).reshape(tile)
+        spill_ref[0, :, lanes] = last[:, :, 0, :].reshape(count * rows, -1)
+        total += jnp.where(col == cols - 1, 0.0, pltpu.roll(last, cols - 1, 2))
+        total_ref[:, :, :, lanes] = total
+        totals = [total[frame] for frame in range(count)]
         states.append(end_state(totals, pole_ref, lanes))
     state, other = states
     col = lax.broadcasted_iota(jnp.int32, (rows, SLAB, state.shape[2]), 1)

time: 39.9 us -> 39.9 us (level)
  no operation moved by 1% of the time
where the time goes in v23:
time: 39.9 us; the launch traced here: 39.4 us
  Pallas kernels  16.3 us (41%)
  starting transfers between devices  12.8 us (32%)
  waiting for transfers between devices  8.15 us (20%)
  local copies, waits for them, and re-layouts  1.67 us (4%)
  between operations  0.41 us (1%)
    pallas_call x17, Pallas kernels, call(): pl.pallas_call(kernel, in_specs=[WHOLE] * len(args), out_specs=out_specs...  16.3 us
    ppermute x2, waiting for transfers between devices, exchange_four(): got = lax.ppermute(end, axes, first_round)  4.83 us
    ppermute x2, starting transfers between devices, exchange_four(): arrivals.append((got, lax.ppermute(relayed, axes, second_round)))  4.07 us
    ppermute x4, starting transfers between devices, swap_cores(): return lax.ppermute(array, 'sx', [(0, 1), (1, 0)])  3.73 us
    ppermute x2, starting transfers between devices, exchange_four(): got = lax.ppermute(end, axes, first_round)  2.7 us
    ppermute x1, starting transfers between devices, trade_columns(): return (got, lax.ppermute(columns, ('sx', 'sy'), pairs))  2.33 us
    ppermute x2, waiting for transfers between devices, exchange_four(): arrivals.append((got, lax.ppermute(relayed, axes, second_round)))  1.73 us
    unnamed x16, local copies, waits for them, and re-layouts  1.66 us
  transfers between devices with their start and end apart: 9, of which 6 were waited for; matrix products, arithmetic and copies ran while one was open for 0% of the time, Pallas kernels for 29%

profile of v23, /device:TPU:23, one launch (start us, length us, event | category | flops | bytes accessed | tf_op | source)
XLA Modules:
  0.0 39.4 jit_solution(4750553703504351026)
XLA Ops:
  0.0 0.0 copy-start
  0.0 0.0 copy-start.2
  0.0 1.3 %copy-done.2 = bf16[2,32,16,512]{3,2,1,0:T(8,128)(2,1)S(1)} copy-done((bf16[2,32,16,512]{3,2,1,0:T(8,128)(2,1)S(1)}, bf16[2,32,16,512]{3,2,1,0:T(8,128)(2,1)}, u32[]{:S(2)}) %copy-start.2) | copy-done | bytes 1048600
  1.3 0.4 shard_map.64
  1.7 0.0 copy-start.3
  1.7 0.0 copy-done
  1.7 0.1 shard_map.65
  1.8 0.0 copy-start.1
  1.9 0.0 copy-start.4
  1.9 0.7 %collective-permute-start = (bf16[192,512]{1,0:T(8,128)(2,1)S(1)}, bf16[192,512]{1,0:T(8,128)(2,1)S(1)}, u32[]{:S(2)}, u32[]{:S(2)}) collective-permute-start(bf16[192,512]{1,0:T(8,128)(2,1)S(1)} %get-tuple-element.35), channel_id=1, source_target_pairs={{0,4},{4,0},{1,5},{5,1},{2,6},{6,2},{3,7},{7,3},{8,12},{12,8},{9,1... | collective-permute-start | bytes 589832 | tf_op jit(solution)/shard_map/ppermute | solution.py:51
  2.6 0.3 copy-done.3
  2.9 0.2 shard_map.66._
  3.1 0.6 %collective-permute-done.got_ref = bf16[192,512]{1,0:T(8,128)(2,1)S(1)} collective-permute-done((bf16[192,512]{1,0:T(8,128)(2,1)S(1)}, bf16[192,512]{1,0:T(8,128)(2,1)S(1)}, u32[]{:S(2)}, u32[]{:S(2)}) %collective-permute-start) | collective-permute-done | bytes 196640 | tf_op jit(solution)/shard_map/ppermute | solution.py:51
  3.7 2.3 %collective-permute-start.1 = (bf16[5,64,512]{2,1,0:T(8,128)(2,1)S(1)}, bf16[5,64,512]{2,1,0:T(8,128)(2,1)S(1)}, u32[]{:S(2)}, u32[]{:S(2)}) collective-permute-start(bf16[5,64,512]{2,1,0:T(8,128)(2,1)S(1)} %pad_maximum_fusion), channel_id=1, source_target_pairs={{0,5},{1,6},{2,7},{5,0},{6,1},{7,2},{8,13},{9,14},{10,15},{13,8},{... | collective-permute-start | bytes 983048 | tf_op jit(solution)/shard_map/ppermute | solution.py:100
  6.1 0.0 copy-done.1
  6.1 0.0 copy-done.4
  6.1 5.2 %shard_map.67 = (f32[2,32,16,512]{3,2,1,0:T(8,128)S(1)}, f32[2,64,512]{2,1,0:T(8,128)S(1)}, bf16[512,256]{1,0:T(8,128)(2,1)S(1)}, bf16[1024,1536]{1,0:T(8,128)(2,1)S(1)}) custom-call(bf16[1024,1536]{1,0:T(8,128)(2,1)S(1)} %shard_map.66._, bf16[192,512]{1,0:T(8,128)(2,1)S(1)} %collective-permute-done.got_ref, ...), custom_call_target="tpu_custom_call", output_to_operand_aliasing={{3}: (0, {})} | custom-call | flops 4831838208 | bytes 13830144 | tf_op jit(solution)/shard_map/pallas_call | solution.py:21
  11.3 0.8 %collective-permute-done.1.mine_ref = bf16[5,64,512]{2,1,0:T(8,128)(2,1)S(1)} collective-permute-done((bf16[5,64,512]{2,1,0:T(8,128)(2,1)S(1)}, bf16[5,64,512]{2,1,0:T(8,128)(2,1)S(1)}, u32[]{:S(2)}, u32[]{:S(2)}) %collective-permute-start.1) | collective-permute-done | bytes 327712 | tf_op jit(solution)/shard_map/ppermute | solution.py:100
  12.1 0.5 %collective-permute-start.2 = (bf16[5,64,512]{2,1,0:T(8,128)(2,1)S(1)}, bf16[5,64,512]{2,1,0:T(8,128)(2,1)S(1)}, u32[]{:S(2)}, u32[]{:S(2)}) collective-permute-start(bf16[5,64,512]{2,1,0:T(8,128)(2,1)S(1)} %collective-permute-done.1.mine_ref), channel_id=1, source_target_pairs={{0,4},{4,0},{1,5},{5,1},{2,6},{6,2},{3,7},{7,3},{8,12},{12,8},{9,1... | collective-permute-start | bytes 983048 | tf_op jit(solution)/shard_map/ppermute | solution.py:51
  12.6 1.3 %collective-permute-start.3 = (bf16[512,256]{1,0:T(8,128)(2,1)S(1)}, bf16[512,256]{1,0:T(8,128)(2,1)S(1)}, u32[]{:S(2)}, u32[]{:S(2)}) collective-permute-start(bf16[512,256]{1,0:T(8,128)(2,1)S(1)} %get-tuple-element.43.end_ref), channel_id=1, source_target_pairs={{0,8},{8,0},{16,24},{4,20},{12,28},{1,9},{9,1},{17,25},{5,21},{13,... | collective-permute-start | bytes 786440 | tf_op jit(solution)/shard_map/ppermute | solution.py:325
  13.9 0.0 collective-permute-done.2.theirs_ref
  13.9 0.2 shard_map.68
  14.1 0.0 copy-start.5
  14.1 0.0 slice-start
  14.1 1.0 %shard_map.69 = (f32[2,32,16,256]{3,2,1,0:T(8,128)S(1)}, f32[2,64,256]{2,1,0:T(8,128)S(1)}, f32[2,128,256]{2,1,0:T(8,128)S(1)}, bf16[640,256]{1,0:T(8,128)(2,1)S(1)}) custom-call(bf16[256,1536]{1,0:T(8,128)(2,1)S(1)} %get-tuple-element.39.lhs_ref, bf16[3,3,512,512]{3,2,1,0:T(8,128)(2,1)S(1)} %copy-done.1, ...), custom_call_target="tpu_custom_call" | custom-call | flops 603979776 | bytes 9635840 | tf_op jit(solution)/shard_map/pallas_call | solution.py:21
  15.2 1.4 %collective-permute-start.5 = (bf16[640,256]{1,0:T(8,128)(2,1)S(1)}, bf16[640,256]{1,0:T(8,128)(2,1)S(1)}, u32[]{:S(2)}, u32[]{:S(2)}) collective-permute-start(bf16[640,256]{1,0:T(8,128)(2,1)S(1)} %get-tuple-element.44.end_ref), channel_id=1, source_target_pairs={{0,8},{8,0},{16,24},{4,20},{12,28},{1,9},{9,1},{17,25},{5,21},{13,... | collective-permute-start | bytes 983048 | tf_op jit(solution)/shard_map/ppermute | solution.py:325
  16.6 3.4 %collective-permute-done.3.got_ref.refs_4_.refs_7_ = bf16[512,256]{1,0:T(8,128)(2,1)S(1)} collective-permute-done((bf16[512,256]{1,0:T(8,128)(2,1)S(1)}, bf16[512,256]{1,0:T(8,128)(2,1)S(1)}, u32[]{:S(2)}, u32[]{:S(2)}) %collective-permute-start.3) | collective-permute-done | bytes 262176 | tf_op jit(solution)/shard_map/ppermute | solution.py:325
  20.0 0.2 shard_map.70
  20.2 1.9 %collective-permute-start.4 = (bf16[512,256]{1,0:T(8,128)(2,1)S(1)}, bf16[512,256]{1,0:T(8,128)(2,1)S(1)}, u32[]{:S(2)}, u32[]{:S(2)}) collective-permute-start(bf16[512,256]{1,0:T(8,128)(2,1)S(1)} %shard_map.70), channel_id=1, source_target_pairs={{0,16},{8,24},{4,12},{20,28},{28,20},{1,17},{9,25},{5,13},{21,29},... | collective-permute-start | bytes 786440 | tf_op jit(solution)/shard_map/ppermute | solution.py:328
  22.1 1.4 %collective-permute-done.5.got_ref.refs_6_.refs_9_.refs_5_ = bf16[640,256]{1,0:T(8,128)(2,1)S(1)} collective-permute-done((bf16[640,256]{1,0:T(8,128)(2,1)S(1)}, bf16[640,256]{1,0:T(8,128)(2,1)S(1)}, u32[]{:S(2)}, u32[]{:S(2)}) %collective-permute-start.5) | collective-permute-done | bytes 327712 | tf_op jit(solution)/shard_map/ppermute | solution.py:325
  23.5 0.2 shard_map.71
  23.7 2.1 %collective-permute-start.6 = (bf16[640,256]{1,0:T(8,128)(2,1)S(1)}, bf16[640,256]{1,0:T(8,128)(2,1)S(1)}, u32[]{:S(2)}, u32[]{:S(2)}) collective-permute-start(bf16[640,256]{1,0:T(8,128)(2,1)S(1)} %shard_map.71), channel_id=1, source_target_pairs={{0,16},{8,24},{4,12},{20,28},{28,20},{1,17},{9,25},{5,13},{21,29},... | collective-permute-start | bytes 983048 | tf_op jit(solution)/shard_map/ppermute | solution.py:328
  25.9 1.7 %collective-permute-done.4.refs_5_.refs_8_ = bf16[512,256]{1,0:T(8,128)(2,1)S(1)} collective-permute-done((bf16[512,256]{1,0:T(8,128)(2,1)S(1)}, bf16[512,256]{1,0:T(8,128)(2,1)S(1)}, u32[]{:S(2)}, u32[]{:S(2)}) %collective-permute-start.4) | collective-permute-done | bytes 262176 | tf_op jit(solution)/shard_map/ppermute | solution.py:328
  27.6 0.0 copy-done.5
  27.6 0.0 slice-start.1
  27.7 1.8 %collective-permute-start.7 = (bf16[2,16,256]{2,1,0:T(8,128)(2,1)S(1)}, bf16[2,16,256]{2,1,0:T(8,128)(2,1)S(1)}, u32[]{:S(2)}, u32[]{:S(2)}) collective-permute-start(bf16[2,16,256]{2,1,0:T(8,128)(2,1)S(1)} %shard_map.74), channel_id=1, source_target_pairs={{0,4},{4,0},{1,5},{5,1},{2,6},{6,2},{3,7},{7,3},{8,12},{12,8},{9,1... | collective-permute-start | bytes 49160 | tf_op jit(solution)/shard_map/ppermute | solution.py:51
  29.5 0.6 %shard_map.72._ = bf16[1024,768]{1,0:T(8,128)(2,1)S(1)} custom-call(f32[2,32,16,512]{3,2,1,0:T(8,128)S(1)} %get-tuple-element.40.total_ref.refs_0_, f32[32,16,512]{2,1,0:T(8,128)S(1)} %copy-done, s32[1,512]{1,0:T(1,128)S(1)} %bitcast.10, f32[1,512]{1,0:T(1,128)S(1)} %bitcast.15, bf16[512,256]{1,0:T(8,128)(2,1)S(1)} %collective-permute-done.3.got_ref.refs_4_.refs_7_, ...), custom_call_target="tpu_custom_call" | custom-call | bytes 5246976 | tf_op jit(solution)/shard_map/pallas_call | solution.py:21
  30.0 0.1 shard_map.73.refs_4_.refs_2_
  30.1 0.2 collective-permute-done.7.got_ref
  30.3 0.0 slice-done
  30.3 0.0 slice-done.1
  30.3 1.4 %shard_map.75 = (f32[2,32,16,256]{3,2,1,0:T(8,128)S(1)}, bf16[1024,768]{1,0:T(8,128)(2,1)S(1)}) custom-call(bf16[1024,768]{1,0:T(8,128)(2,1)S(1)} %shard_map.72._, bf16[2,16,256]{2,1,0:T(8,128)(2,1)S(1)} %collective-permute-done.7.got_ref, bf16[3,3,512,512]{3,2,1,0:T(8,128)(2,1)S(1)} %bitcast.4), custom_call_target="tpu_custom_call", output_to_operand_aliasing={{1}: (0, {})} | custom-call | flops 1207959552 | bytes 8929280 | tf_op jit(solution)/shard_map/pallas_call | solution.py:21
  31.7 1.4 %shard_map.76.refs_1_ = f32[2,32,16,256]{3,2,1,0:T(8,128)S(1)} custom-call(bf16[1024,768]{1,0:T(8,128)(2,1)S(1)} %get-tuple-element.48.lhs_ref, bf16[3,3,512,512]{3,2,1,0:T(8,128)(2,1)S(1)} %bitcast.4), custom_call_target="tpu_custom_call" | custom-call | flops 1207959552 | bytes 7340032 | tf_op jit(solution)/shard_map/pallas_call | solution.py:21
  33.1 0.0 collective-permute-done.6.refs_7_.refs_10_.refs_6_
  33.1 0.1 shard_map.78
  33.2 0.7 %collective-permute-start.8 = (bf16[2,32,256]{2,1,0:T(8,128)(2,1)S(1)}, bf16[2,32,256]{2,1,0:T(8,128)(2,1)S(1)}, u32[]{:S(2)}, u32[]{:S(2)}) collective-permute-start(bf16[2,32,256]{2,1,0:T(8,128)(2,1)S(1)} %shard_map.78), channel_id=1, source_target_pairs={{0,4},{4,0},{1,5},{5,1},{2,6},{6,2},{3,7},{7,3},{8,12},{12,8},{9,1... | collective-permute-start | bytes 98312 | tf_op jit(solution)/shard_map/ppermute | solution.py:51
  33.9 0.3 shard_map.79
  34.3 0.7 %shard_map.77._ = bf16[1152,768]{1,0:T(8,128)(2,1)S(1)} custom-call(f32[2,32,16,256]{3,2,1,0:T(8,128)S(1)} %get-tuple-element.42.refs_0_, f32[32,16,512]{2,1,0:T(8,128)S(1)} %copy-done, s32[1,512]{1,0:T(1,128)S(1)} %bitcast.13, f32[1,512]{1,0:T(1,128)S(1)} %bitcast.18, bf16[512,256]{1,0:T(8,128)(2,1)S(1)} %collective-permute-done.3.got_ref.refs_4_.refs_7_, ...), custom_call_target="tpu_custom_call" | custom-call | bytes 5050368 | tf_op jit(solution)/shard_map/pallas_call | solution.py:21
  35.0 0.0 collective-permute-done.8.got_ref
  35.0 4.2 %shard_map.80 = (bf16[2,32,16,512]{3,2,1,0:T(8,128)(2,1)}, bf16[1152,768]{1,0:T(8,128)(2,1)S(1)}) custom-call(bf16[1152,768]{1,0:T(8,128)(2,1)S(1)} %shard_map.77._, bf16[2,32,256]{2,1,0:T(8,128)(2,1)S(1)} %collective-permute-done.8.got_ref, bf16[2,64,256]{2,1,0:T(8,128)(2,1)S(1)} %get-tuple-element.54.beside_ref, ...), custom_call_target="tpu_custom_call", output_to_operand_aliasing={{1}: (0, {})} | custom-call | flops 2415919104 | bytes 11632640 | tf_op jit(solution)/shard_map/pallas_call | solution.py:21
  (4 shorter events, 0.1 us)
Async XLA Ops:
  0.0 1.7 %copy-start = (f32[32,16,512]{2,1,0:T(8,128)S(1)}, f32[32,16,512]{2,1,0:T(8,128)}, u32[]{:S(2)}) copy-start(f32[32,16,512]{2,1,0:T(8,128)} %refs_3_.1) | copy-start | bytes 3145732
  0.0 1.3 %copy-start.2 = (bf16[2,32,16,512]{3,2,1,0:T(8,128)(2,1)S(1)}, bf16[2,32,16,512]{3,2,1,0:T(8,128)(2,1)}, u32[]{:S(2)}) copy-start(bf16[2,32,16,512]{3,2,1,0:T(8,128)(2,1)} %cells_ref.3) | copy-start | bytes 3145732
  1.7 1.2 %copy-start.3 = (bf16[2,32,16,512]{3,2,1,0:T(8,128)(2,1)S(1)}, bf16[2,32,16,512]{3,2,1,0:T(8,128)(2,1)}, u32[]{:S(2)}) copy-start(bf16[2,32,16,512]{3,2,1,0:T(8,128)(2,1)} %cells_ref.3) | copy-start | bytes 3145732
  1.8 4.2 %copy-start.1 = (bf16[3,3,512,512]{3,2,1,0:T(8,128)(2,1)S(1)}, bf16[3,3,512,512]{3,2,1,0:T(8,128)(2,1)}, u32[]{:S(2)}) copy-start(bf16[3,3,512,512]{3,2,1,0:T(8,128)(2,1)} %weight_ref.6) | copy-start | bytes 14155780
  1.9 4.2 %copy-start.4 = (s32[512]{0:T(512)S(1)}, s32[512]{0:T(512)}, u32[]{:S(2)}) copy-start(s32[512]{0:T(512)} %param.9) | copy-start | bytes 6148
  1.9 1.8 %collective-permute-start = (bf16[192,512]{1,0:T(8,128)(2,1)S(1)}, bf16[192,512]{1,0:T(8,128)(2,1)S(1)}, u32[]{:S(2)}, u32[]{:S(2)}) collective-permute-start(bf16[192,512]{1,0:T(8,128)(2,1)S(1)} %get-tuple-element.35), channel_id=1, source_target_pairs={{0,4},{4,0},{1,5},{5,1},{2,6},{6,2},{3,7},{7,3},{8,12},{12,8},{9,1... | collective-permute-start | bytes 589832 | tf_op jit(solution)/shard_map/ppermute | solution.py:51
  3.7 8.4 %collective-permute-start.1 = (bf16[5,64,512]{2,1,0:T(8,128)(2,1)S(1)}, bf16[5,64,512]{2,1,0:T(8,128)(2,1)S(1)}, u32[]{:S(2)}, u32[]{:S(2)}) collective-permute-start(bf16[5,64,512]{2,1,0:T(8,128)(2,1)S(1)} %pad_maximum_fusion), channel_id=1, source_target_pairs={{0,5},{1,6},{2,7},{5,0},{6,1},{7,2},{8,13},{9,14},{10,15},{13,8},{... | collective-permute-start | bytes 983048 | tf_op jit(solution)/shard_map/ppermute | solution.py:100
  12.1 1.8 %collective-permute-start.2 = (bf16[5,64,512]{2,1,0:T(8,128)(2,1)S(1)}, bf16[5,64,512]{2,1,0:T(8,128)(2,1)S(1)}, u32[]{:S(2)}, u32[]{:S(2)}) collective-permute-start(bf16[5,64,512]{2,1,0:T(8,128)(2,1)S(1)} %collective-permute-done.1.mine_ref), channel_id=1, source_target_pairs={{0,4},{4,0},{1,5},{5,1},{2,6},{6,2},{3,7},{7,3},{8,12},{12,8},{9,1... | collective-permute-start | bytes 983048 | tf_op jit(solution)/shard_map/ppermute | solution.py:51
  12.6 7.4 %collective-permute-start.3 = (bf16[512,256]{1,0:T(8,128)(2,1)S(1)}, bf16[512,256]{1,0:T(8,128)(2,1)S(1)}, u32[]{:S(2)}, u32[]{:S(2)}) collective-permute-start(bf16[512,256]{1,0:T(8,128)(2,1)S(1)} %get-tuple-element.43.end_ref), channel_id=1, source_target_pairs={{0,8},{8,0},{16,24},{4,20},{12,28},{1,9},{9,1},{17,25},{5,21},{13,... | collective-permute-start | bytes 786440 | tf_op jit(solution)/shard_map/ppermute | solution.py:325
  14.1 13.5 %copy-start.5 = (f32[512]{0:T(512)S(1)}, f32[512]{0:T(512)}, u32[]{:S(2)}) copy-start(f32[512]{0:T(512)} %param.10) | copy-start | bytes 6148
  14.1 16.2 %slice-start = ((s8[4718592]{0:T(1024)(128)(4,1)}), s8[4194304]{0:T(1024)(128)(4,1)S(1)}, s32[]{:S(2)}) async-start(s8[4718592]{0:T(1024)(128)(4,1)} %bitcast.3), calls=%async_computation | async-start | bytes 8388608
  15.2 8.4 %collective-permute-start.5 = (bf16[640,256]{1,0:T(8,128)(2,1)S(1)}, bf16[640,256]{1,0:T(8,128)(2,1)S(1)}, u32[]{:S(2)}, u32[]{:S(2)}) collective-permute-start(bf16[640,256]{1,0:T(8,128)(2,1)S(1)} %get-tuple-element.44.end_ref), channel_id=1, source_target_pairs={{0,8},{8,0},{16,24},{4,20},{12,28},{1,9},{9,1},{17,25},{5,21},{13,... | collective-permute-start | bytes 983048 | tf_op jit(solution)/shard_map/ppermute | solution.py:325
  20.2 7.4 %collective-permute-start.4 = (bf16[512,256]{1,0:T(8,128)(2,1)S(1)}, bf16[512,256]{1,0:T(8,128)(2,1)S(1)}, u32[]{:S(2)}, u32[]{:S(2)}) collective-permute-start(bf16[512,256]{1,0:T(8,128)(2,1)S(1)} %shard_map.70), channel_id=1, source_target_pairs={{0,16},{8,24},{4,12},{20,28},{28,20},{1,17},{9,25},{5,13},{21,29},... | collective-permute-start | bytes 786440 | tf_op jit(solution)/shard_map/ppermute | solution.py:328
  23.7 9.4 %collective-permute-start.6 = (bf16[640,256]{1,0:T(8,128)(2,1)S(1)}, bf16[640,256]{1,0:T(8,128)(2,1)S(1)}, u32[]{:S(2)}, u32[]{:S(2)}) collective-permute-start(bf16[640,256]{1,0:T(8,128)(2,1)S(1)} %shard_map.71), channel_id=1, source_target_pairs={{0,16},{8,24},{4,12},{20,28},{28,20},{1,17},{9,25},{5,13},{21,29},... | collective-permute-start | bytes 983048 | tf_op jit(solution)/shard_map/ppermute | solution.py:328
  27.6 2.7 %slice-start.1 = ((s8[4718592]{0:T(1024)(128)(4,1)}), s8[524288]{0:T(1024)(128)(4,1)S(1)}, s32[]{:S(2)}) async-start(s8[4718592]{0:T(1024)(128)(4,1)} %bitcast.3), calls=%async_computation.1 | async-start | bytes 1048576
  27.7 2.6 %collective-permute-start.7 = (bf16[2,16,256]{2,1,0:T(8,128)(2,1)S(1)}, bf16[2,16,256]{2,1,0:T(8,128)(2,1)S(1)}, u32[]{:S(2)}, u32[]{:S(2)}) collective-permute-start(bf16[2,16,256]{2,1,0:T(8,128)(2,1)S(1)} %shard_map.74), channel_id=1, source_target_pairs={{0,4},{4,0},{1,5},{5,1},{2,6},{6,2},{3,7},{7,3},{8,12},{12,8},{9,1... | collective-permute-start | bytes 49160 | tf_op jit(solution)/shard_map/ppermute | solution.py:51
  33.2 1.7 %collective-permute-start.8 = (bf16[2,32,256]{2,1,0:T(8,128)(2,1)S(1)}, bf16[2,32,256]{2,1,0:T(8,128)(2,1)S(1)}, u32[]{:S(2)}, u32[]{:S(2)}) collective-permute-start(bf16[2,32,256]{2,1,0:T(8,128)(2,1)S(1)} %shard_map.78), channel_id=1, source_target_pairs={{0,4},{4,0},{1,5},{5,1},{2,6},{6,2},{3,7},{7,3},{8,12},{12,8},{9,1... | collective-permute-start | bytes 98312 | tf_op jit(solution)/shard_map/ppermute | solution.py:51

commit v24 on v22

--- a/solution.py
+++ b/solution.py
@@ -395,7 +395,7 @@
     mix = Mix(lanes, count, pole_ref, scale_ref)
     first = lanes.start == 0
     held = lanes if first else slice(None)
-    block = 8
+    block = 4
     for row in range(0, rows, block):
         here = slice(row, row + block)
         drives = [drive_ref[frame, here, :, held] for frame in range(count)]

time: 39.9 us -> 39.9 us (level)
  no operation moved by 1% of the time
where the time goes in v24:
time: 39.9 us; the launch traced here: 39.4 us
  Pallas kernels  16.4 us (41%)
  starting transfers between devices  12.9 us (32%)
  waiting for transfers between devices  8.08 us (20%)
  local copies, waits for them, and re-layouts  1.67 us (4%)
  between operations  0.41 us (1%)
    pallas_call x17, Pallas kernels, call(): pl.pallas_call(kernel, in_specs=[WHOLE] * len(args), out_specs=out_specs...  16.4 us
    ppermute x2, waiting for transfers between devices, exchange_four(): got = lax.ppermute(end, axes, first_round)  4.83 us
    ppermute x2, starting transfers between devices, exchange_four(): arrivals.append((got, lax.ppermute(relayed, axes, second_round)))  4.07 us
    ppermute x4, starting transfers between devices, swap_cores(): return lax.ppermute(array, 'sx', [(0, 1), (1, 0)])  3.8 us
    ppermute x2, starting transfers between devices, exchange_four(): got = lax.ppermute(end, axes, first_round)  2.7 us
    ppermute x1, starting transfers between devices, trade_columns(): return (got, lax.ppermute(columns, ('sx', 'sy'), pairs))  2.33 us
    ppermute x2, waiting for transfers between devices, exchange_four(): arrivals.append((got, lax.ppermute(relayed, axes, second_round)))  1.73 us
    unnamed x16, local copies, waits for them, and re-layouts  1.66 us
  transfers between devices with their start and end apart: 9, of which 6 were waited for; matrix products, arithmetic and copies ran while one was open for 0% of the time, Pallas kernels for 29%

profile of v24, /device:TPU:23, one launch (start us, length us, event | category | flops | bytes accessed | tf_op | source)
XLA Modules:
  0.0 39.4 jit_solution(17806489387596637010)
XLA Ops:
  0.0 0.0 copy-start
  0.0 0.0 copy-start.2
  0.0 1.3 %copy-done.2 = bf16[2,32,16,512]{3,2,1,0:T(8,128)(2,1)S(1)} copy-done((bf16[2,32,16,512]{3,2,1,0:T(8,128)(2,1)S(1)}, bf16[2,32,16,512]{3,2,1,0:T(8,128)(2,1)}, u32[]{:S(2)}) %copy-start.2) | copy-done | bytes 1048600
  1.3 0.4 shard_map.64
  1.7 0.0 copy-start.3
  1.7 0.0 copy-done
  1.7 0.1 shard_map.65
  1.8 0.0 copy-start.1
  1.9 0.0 copy-start.4
  1.9 0.7 %collective-permute-start = (bf16[192,512]{1,0:T(8,128)(2,1)S(1)}, bf16[192,512]{1,0:T(8,128)(2,1)S(1)}, u32[]{:S(2)}, u32[]{:S(2)}) collective-permute-start(bf16[192,512]{1,0:T(8,128)(2,1)S(1)} %get-tuple-element.35), channel_id=1, source_target_pairs={{0,4},{4,0},{1,5},{5,1},{2,6},{6,2},{3,7},{7,3},{8,12},{12,8},{9,1... | collective-permute-start | bytes 589832 | tf_op jit(solution)/shard_map/ppermute | solution.py:51
  2.6 0.3 copy-done.3
  2.9 0.2 shard_map.66._
  3.1 0.6 %collective-permute-done.got_ref = bf16[192,512]{1,0:T(8,128)(2,1)S(1)} collective-permute-done((bf16[192,512]{1,0:T(8,128)(2,1)S(1)}, bf16[192,512]{1,0:T(8,128)(2,1)S(1)}, u32[]{:S(2)}, u32[]{:S(2)}) %collective-permute-start) | collective-permute-done | bytes 196640 | tf_op jit(solution)/shard_map/ppermute | solution.py:51
  3.7 2.3 %collective-permute-start.1 = (bf16[5,64,512]{2,1,0:T(8,128)(2,1)S(1)}, bf16[5,64,512]{2,1,0:T(8,128)(2,1)S(1)}, u32[]{:S(2)}, u32[]{:S(2)}) collective-permute-start(bf16[5,64,512]{2,1,0:T(8,128)(2,1)S(1)} %pad_maximum_fusion), channel_id=1, source_target_pairs={{0,5},{1,6},{2,7},{5,0},{6,1},{7,2},{8,13},{9,14},{10,15},{13,8},{... | collective-permute-start | bytes 983048 | tf_op jit(solution)/shard_map/ppermute | solution.py:100
  6.1 0.0 copy-done.1
  6.1 0.0 copy-done.4
  6.1 5.3 %shard_map.67 = (f32[2,32,16,512]{3,2,1,0:T(8,128)S(1)}, f32[2,64,512]{2,1,0:T(8,128)S(1)}, bf16[512,256]{1,0:T(8,128)(2,1)S(1)}, bf16[1024,1536]{1,0:T(8,128)(2,1)S(1)}) custom-call(bf16[1024,1536]{1,0:T(8,128)(2,1)S(1)} %shard_map.66._, bf16[192,512]{1,0:T(8,128)(2,1)S(1)} %collective-permute-done.got_ref, ...), custom_call_target="tpu_custom_call", output_to_operand_aliasing={{3}: (0, {})} | custom-call | flops 4831838208 | bytes 13830144 | tf_op jit(solution)/shard_map/pallas_call | solution.py:21
  11.3 0.8 %collective-permute-done.1.mine_ref = bf16[5,64,512]{2,1,0:T(8,128)(2,1)S(1)} collective-permute-done((bf16[5,64,512]{2,1,0:T(8,128)(2,1)S(1)}, bf16[5,64,512]{2,1,0:T(8,128)(2,1)S(1)}, u32[]{:S(2)}, u32[]{:S(2)}) %collective-permute-start.1) | collective-permute-done | bytes 327712 | tf_op jit(solution)/shard_map/ppermute | solution.py:100
  12.1 0.6 %collective-permute-start.2 = (bf16[5,64,512]{2,1,0:T(8,128)(2,1)S(1)}, bf16[5,64,512]{2,1,0:T(8,128)(2,1)S(1)}, u32[]{:S(2)}, u32[]{:S(2)}) collective-permute-start(bf16[5,64,512]{2,1,0:T(8,128)(2,1)S(1)} %collective-permute-done.1.mine_ref), channel_id=1, source_target_pairs={{0,4},{4,0},{1,5},{5,1},{2,6},{6,2},{3,7},{7,3},{8,12},{12,8},{9,1... | collective-permute-start | bytes 983048 | tf_op jit(solution)/shard_map/ppermute | solution.py:51
  12.7 1.3 %collective-permute-start.3 = (bf16[512,256]{1,0:T(8,128)(2,1)S(1)}, bf16[512,256]{1,0:T(8,128)(2,1)S(1)}, u32[]{:S(2)}, u32[]{:S(2)}) collective-permute-start(bf16[512,256]{1,0:T(8,128)(2,1)S(1)} %get-tuple-element.43.end_ref), channel_id=1, source_target_pairs={{0,8},{8,0},{16,24},{4,20},{12,28},{1,9},{9,1},{17,25},{5,21},{13,... | collective-permute-start | bytes 786440 | tf_op jit(solution)/shard_map/ppermute | solution.py:329
  14.0 0.0 collective-permute-done.2.theirs_ref
  14.0 0.2 shard_map.68
  14.2 0.0 copy-start.5
  14.2 0.0 slice-start
  14.2 1.0 %shard_map.69 = (f32[2,32,16,256]{3,2,1,0:T(8,128)S(1)}, f32[2,64,256]{2,1,0:T(8,128)S(1)}, f32[2,128,256]{2,1,0:T(8,128)S(1)}, bf16[640,256]{1,0:T(8,128)(2,1)S(1)}) custom-call(bf16[256,1536]{1,0:T(8,128)(2,1)S(1)} %get-tuple-element.39.lhs_ref, bf16[3,3,512,512]{3,2,1,0:T(8,128)(2,1)S(1)} %copy-done.1, ...), custom_call_target="tpu_custom_call" | custom-call | flops 603979776 | bytes 9635840 | tf_op jit(solution)/shard_map/pallas_call | solution.py:21
  15.2 1.4 %collective-permute-start.5 = (bf16[640,256]{1,0:T(8,128)(2,1)S(1)}, bf16[640,256]{1,0:T(8,128)(2,1)S(1)}, u32[]{:S(2)}, u32[]{:S(2)}) collective-permute-start(bf16[640,256]{1,0:T(8,128)(2,1)S(1)} %get-tuple-element.44.end_ref), channel_id=1, source_target_pairs={{0,8},{8,0},{16,24},{4,20},{12,28},{1,9},{9,1},{17,25},{5,21},{13,... | collective-permute-start | bytes 983048 | tf_op jit(solution)/shard_map/ppermute | solution.py:329
  16.7 3.4 %collective-permute-done.3.got_ref.refs_4_.refs_7_ = bf16[512,256]{1,0:T(8,128)(2,1)S(1)} collective-permute-done((bf16[512,256]{1,0:T(8,128)(2,1)S(1)}, bf16[512,256]{1,0:T(8,128)(2,1)S(1)}, u32[]{:S(2)}, u32[]{:S(2)}) %collective-permute-start.3) | collective-permute-done | bytes 262176 | tf_op jit(solution)/shard_map/ppermute | solution.py:329
  20.1 0.2 shard_map.70
  20.3 1.9 %collective-permute-start.4 = (bf16[512,256]{1,0:T(8,128)(2,1)S(1)}, bf16[512,256]{1,0:T(8,128)(2,1)S(1)}, u32[]{:S(2)}, u32[]{:S(2)}) collective-permute-start(bf16[512,256]{1,0:T(8,128)(2,1)S(1)} %shard_map.70), channel_id=1, source_target_pairs={{0,16},{8,24},{4,12},{20,28},{28,20},{1,17},{9,25},{5,13},{21,29},... | collective-permute-start | bytes 786440 | tf_op jit(solution)/shard_map/ppermute | solution.py:332
  22.2 1.4 %collective-permute-done.5.got_ref.refs_6_.refs_9_.refs_5_ = bf16[640,256]{1,0:T(8,128)(2,1)S(1)} collective-permute-done((bf16[640,256]{1,0:T(8,128)(2,1)S(1)}, bf16[640,256]{1,0:T(8,128)(2,1)S(1)}, u32[]{:S(2)}, u32[]{:S(2)}) %collective-permute-start.5) | collective-permute-done | bytes 327712 | tf_op jit(solution)/shard_map/ppermute | solution.py:329
  23.6 0.2 shard_map.71
  23.8 2.1 %collective-permute-start.6 = (bf16[640,256]{1,0:T(8,128)(2,1)S(1)}, bf16[640,256]{1,0:T(8,128)(2,1)S(1)}, u32[]{:S(2)}, u32[]{:S(2)}) collective-permute-start(bf16[640,256]{1,0:T(8,128)(2,1)S(1)} %shard_map.71), channel_id=1, source_target_pairs={{0,16},{8,24},{4,12},{20,28},{28,20},{1,17},{9,25},{5,13},{21,29},... | collective-permute-start | bytes 983048 | tf_op jit(solution)/shard_map/ppermute | solution.py:332
  25.9 1.7 %collective-permute-done.4.refs_5_.refs_8_ = bf16[512,256]{1,0:T(8,128)(2,1)S(1)} collective-permute-done((bf16[512,256]{1,0:T(8,128)(2,1)S(1)}, bf16[512,256]{1,0:T(8,128)(2,1)S(1)}, u32[]{:S(2)}, u32[]{:S(2)}) %collective-permute-start.4) | collective-permute-done | bytes 262176 | tf_op jit(solution)/shard_map/ppermute | solution.py:332
  27.7 0.0 copy-done.5
  27.7 0.0 slice-start.1
  27.7 1.8 %collective-permute-start.7 = (bf16[2,16,256]{2,1,0:T(8,128)(2,1)S(1)}, bf16[2,16,256]{2,1,0:T(8,128)(2,1)S(1)}, u32[]{:S(2)}, u32[]{:S(2)}) collective-permute-start(bf16[2,16,256]{2,1,0:T(8,128)(2,1)S(1)} %shard_map.74), channel_id=1, source_target_pairs={{0,4},{4,0},{1,5},{5,1},{2,6},{6,2},{3,7},{7,3},{8,12},{12,8},{9,1... | collective-permute-start | bytes 49160 | tf_op jit(solution)/shard_map/ppermute | solution.py:51
  29.5 0.6 %shard_map.72._ = bf16[1024,768]{1,0:T(8,128)(2,1)S(1)} custom-call(f32[2,32,16,512]{3,2,1,0:T(8,128)S(1)} %get-tuple-element.40.total_ref.refs_0_, f32[32,16,512]{2,1,0:T(8,128)S(1)} %copy-done, s32[1,512]{1,0:T(1,128)S(1)} %bitcast.10, f32[1,512]{1,0:T(1,128)S(1)} %bitcast.15, bf16[512,256]{1,0:T(8,128)(2,1)S(1)} %collective-permute-done.3.got_ref.refs_4_.refs_7_, ...), custom_call_target="tpu_custom_call" | custom-call | bytes 5246976 | tf_op jit(solution)/shard_map/pallas_call | solution.py:21
  30.1 0.1 shard_map.73.refs_4_.refs_2_
  30.2 0.2 collective-permute-done.7.got_ref
  30.4 0.0 slice-done
  30.4 0.0 slice-done.1
  30.4 1.4 %shard_map.75 = (f32[2,32,16,256]{3,2,1,0:T(8,128)S(1)}, bf16[1024,768]{1,0:T(8,128)(2,1)S(1)}) custom-call(bf16[1024,768]{1,0:T(8,128)(2,1)S(1)} %shard_map.72._, bf16[2,16,256]{2,1,0:T(8,128)(2,1)S(1)} %collective-permute-done.7.got_ref, bf16[3,3,512,512]{3,2,1,0:T(8,128)(2,1)S(1)} %bitcast.4), custom_call_target="tpu_custom_call", output_to_operand_aliasing={{1}: (0, {})} | custom-call | flops 1207959552 | bytes 8929280 | tf_op jit(solution)/shard_map/pallas_call | solution.py:21
  31.8 1.4 %shard_map.76.refs_1_ = f32[2,32,16,256]{3,2,1,0:T(8,128)S(1)} custom-call(bf16[1024,768]{1,0:T(8,128)(2,1)S(1)} %get-tuple-element.48.lhs_ref, bf16[3,3,512,512]{3,2,1,0:T(8,128)(2,1)S(1)} %bitcast.4), custom_call_target="tpu_custom_call" | custom-call | flops 1207959552 | bytes 7340032 | tf_op jit(solution)/shard_map/pallas_call | solution.py:21
  33.2 0.0 collective-permute-done.6.refs_7_.refs_10_.refs_6_
  33.2 0.1 shard_map.78
  33.3 0.7 %collective-permute-start.8 = (bf16[2,32,256]{2,1,0:T(8,128)(2,1)S(1)}, bf16[2,32,256]{2,1,0:T(8,128)(2,1)S(1)}, u32[]{:S(2)}, u32[]{:S(2)}) collective-permute-start(bf16[2,32,256]{2,1,0:T(8,128)(2,1)S(1)} %shard_map.78), channel_id=1, source_target_pairs={{0,4},{4,0},{1,5},{5,1},{2,6},{6,2},{3,7},{7,3},{8,12},{12,8},{9,1... | collective-permute-start | bytes 98312 | tf_op jit(solution)/shard_map/ppermute | solution.py:51
  34.0 0.3 shard_map.79
  34.4 0.7 %shard_map.77._ = bf16[1152,768]{1,0:T(8,128)(2,1)S(1)} custom-call(f32[2,32,16,256]{3,2,1,0:T(8,128)S(1)} %get-tuple-element.42.refs_0_, f32[32,16,512]{2,1,0:T(8,128)S(1)} %copy-done, s32[1,512]{1,0:T(1,128)S(1)} %bitcast.13, f32[1,512]{1,0:T(1,128)S(1)} %bitcast.18, bf16[512,256]{1,0:T(8,128)(2,1)S(1)} %collective-permute-done.3.got_ref.refs_4_.refs_7_, ...), custom_call_target="tpu_custom_call" | custom-call | bytes 5050368 | tf_op jit(solution)/shard_map/pallas_call | solution.py:21
  35.0 0.0 collective-permute-done.8.got_ref
  35.0 4.2 %shard_map.80 = (bf16[2,32,16,512]{3,2,1,0:T(8,128)(2,1)}, bf16[1152,768]{1,0:T(8,128)(2,1)S(1)}) custom-call(bf16[1152,768]{1,0:T(8,128)(2,1)S(1)} %shard_map.77._, bf16[2,32,256]{2,1,0:T(8,128)(2,1)S(1)} %collective-permute-done.8.got_ref, bf16[2,64,256]{2,1,0:T(8,128)(2,1)S(1)} %get-tuple-element.54.beside_ref, ...), custom_call_target="tpu_custom_call", output_to_operand_aliasing={{1}: (0, {})} | custom-call | flops 2415919104 | bytes 11632640 | tf_op jit(solution)/shard_map/pallas_call | solution.py:21
  (4 shorter events, 0.1 us)
Async XLA Ops:
  0.0 1.7 %copy-start = (f32[32,16,512]{2,1,0:T(8,128)S(1)}, f32[32,16,512]{2,1,0:T(8,128)}, u32[]{:S(2)}) copy-start(f32[32,16,512]{2,1,0:T(8,128)} %refs_3_.1) | copy-start | bytes 3145732
  0.0 1.3 %copy-start.2 = (bf16[2,32,16,512]{3,2,1,0:T(8,128)(2,1)S(1)}, bf16[2,32,16,512]{3,2,1,0:T(8,128)(2,1)}, u32[]{:S(2)}) copy-start(bf16[2,32,16,512]{3,2,1,0:T(8,128)(2,1)} %cells_ref.3) | copy-start | bytes 3145732
  1.7 1.2 %copy-start.3 = (bf16[2,32,16,512]{3,2,1,0:T(8,128)(2,1)S(1)}, bf16[2,32,16,512]{3,2,1,0:T(8,128)(2,1)}, u32[]{:S(2)}) copy-start(bf16[2,32,16,512]{3,2,1,0:T(8,128)(2,1)} %cells_ref.3) | copy-start | bytes 3145732
  1.8 4.2 %copy-start.1 = (bf16[3,3,512,512]{3,2,1,0:T(8,128)(2,1)S(1)}, bf16[3,3,512,512]{3,2,1,0:T(8,128)(2,1)}, u32[]{:S(2)}) copy-start(bf16[3,3,512,512]{3,2,1,0:T(8,128)(2,1)} %weight_ref.6) | copy-start | bytes 14155780
  1.9 4.2 %copy-start.4 = (s32[512]{0:T(512)S(1)}, s32[512]{0:T(512)}, u32[]{:S(2)}) copy-start(s32[512]{0:T(512)} %param.9) | copy-start | bytes 6148
  1.9 1.8 %collective-permute-start = (bf16[192,512]{1,0:T(8,128)(2,1)S(1)}, bf16[192,512]{1,0:T(8,128)(2,1)S(1)}, u32[]{:S(2)}, u32[]{:S(2)}) collective-permute-start(bf16[192,512]{1,0:T(8,128)(2,1)S(1)} %get-tuple-element.35), channel_id=1, source_target_pairs={{0,4},{4,0},{1,5},{5,1},{2,6},{6,2},{3,7},{7,3},{8,12},{12,8},{9,1... | collective-permute-start | bytes 589832 | tf_op jit(solution)/shard_map/ppermute | solution.py:51
  3.7 8.4 %collective-permute-start.1 = (bf16[5,64,512]{2,1,0:T(8,128)(2,1)S(1)}, bf16[5,64,512]{2,1,0:T(8,128)(2,1)S(1)}, u32[]{:S(2)}, u32[]{:S(2)}) collective-permute-start(bf16[5,64,512]{2,1,0:T(8,128)(2,1)S(1)} %pad_maximum_fusion), channel_id=1, source_target_pairs={{0,5},{1,6},{2,7},{5,0},{6,1},{7,2},{8,13},{9,14},{10,15},{13,8},{... | collective-permute-start | bytes 983048 | tf_op jit(solution)/shard_map/ppermute | solution.py:100
  12.1 1.9 %collective-permute-start.2 = (bf16[5,64,512]{2,1,0:T(8,128)(2,1)S(1)}, bf16[5,64,512]{2,1,0:T(8,128)(2,1)S(1)}, u32[]{:S(2)}, u32[]{:S(2)}) collective-permute-start(bf16[5,64,512]{2,1,0:T(8,128)(2,1)S(1)} %collective-permute-done.1.mine_ref), channel_id=1, source_target_pairs={{0,4},{4,0},{1,5},{5,1},{2,6},{6,2},{3,7},{7,3},{8,12},{12,8},{9,1... | collective-permute-start | bytes 983048 | tf_op jit(solution)/shard_map/ppermute | solution.py:51
  12.7 7.4 %collective-permute-start.3 = (bf16[512,256]{1,0:T(8,128)(2,1)S(1)}, bf16[512,256]{1,0:T(8,128)(2,1)S(1)}, u32[]{:S(2)}, u32[]{:S(2)}) collective-permute-start(bf16[512,256]{1,0:T(8,128)(2,1)S(1)} %get-tuple-element.43.end_ref), channel_id=1, source_target_pairs={{0,8},{8,0},{16,24},{4,20},{12,28},{1,9},{9,1},{17,25},{5,21},{13,... | collective-permute-start | bytes 786440 | tf_op jit(solution)/shard_map/ppermute | solution.py:329
  14.2 13.5 %copy-start.5 = (f32[512]{0:T(512)S(1)}, f32[512]{0:T(512)}, u32[]{:S(2)}) copy-start(f32[512]{0:T(512)} %param.10) | copy-start | bytes 6148
  14.2 16.2 %slice-start = ((s8[4718592]{0:T(1024)(128)(4,1)}), s8[4194304]{0:T(1024)(128)(4,1)S(1)}, s32[]{:S(2)}) async-start(s8[4718592]{0:T(1024)(128)(4,1)} %bitcast.3), calls=%async_computation | async-start | bytes 8388608
  15.2 8.4 %collective-permute-start.5 = (bf16[640,256]{1,0:T(8,128)(2,1)S(1)}, bf16[640,256]{1,0:T(8,128)(2,1)S(1)}, u32[]{:S(2)}, u32[]{:S(2)}) collective-permute-start(bf16[640,256]{1,0:T(8,128)(2,1)S(1)} %get-tuple-element.44.end_ref), channel_id=1, source_target_pairs={{0,8},{8,0},{16,24},{4,20},{12,28},{1,9},{9,1},{17,25},{5,21},{13,... | collective-permute-start | bytes 983048 | tf_op jit(solution)/shard_map/ppermute | solution.py:329
  20.3 7.4 %collective-permute-start.4 = (bf16[512,256]{1,0:T(8,128)(2,1)S(1)}, bf16[512,256]{1,0:T(8,128)(2,1)S(1)}, u32[]{:S(2)}, u32[]{:S(2)}) collective-permute-start(bf16[512,256]{1,0:T(8,128)(2,1)S(1)} %shard_map.70), channel_id=1, source_target_pairs={{0,16},{8,24},{4,12},{20,28},{28,20},{1,17},{9,25},{5,13},{21,29},... | collective-permute-start | bytes 786440 | tf_op jit(solution)/shard_map/ppermute | solution.py:332
  23.8 9.4 %collective-permute-start.6 = (bf16[640,256]{1,0:T(8,128)(2,1)S(1)}, bf16[640,256]{1,0:T(8,128)(2,1)S(1)}, u32[]{:S(2)}, u32[]{:S(2)}) collective-permute-start(bf16[640,256]{1,0:T(8,128)(2,1)S(1)} %shard_map.71), channel_id=1, source_target_pairs={{0,16},{8,24},{4,12},{20,28},{28,20},{1,17},{9,25},{5,13},{21,29},... | collective-permute-start | bytes 983048 | tf_op jit(solution)/shard_map/ppermute | solution.py:332
  27.7 2.7 %slice-start.1 = ((s8[4718592]{0:T(1024)(128)(4,1)}), s8[524288]{0:T(1024)(128)(4,1)S(1)}, s32[]{:S(2)}) async-start(s8[4718592]{0:T(1024)(128)(4,1)} %bitcast.3), calls=%async_computation.1 | async-start | bytes 1048576
  27.7 2.6 %collective-permute-start.7 = (bf16[2,16,256]{2,1,0:T(8,128)(2,1)S(1)}, bf16[2,16,256]{2,1,0:T(8,128)(2,1)S(1)}, u32[]{:S(2)}, u32[]{:S(2)}) collective-permute-start(bf16[2,16,256]{2,1,0:T(8,128)(2,1)S(1)} %shard_map.74), channel_id=1, source_target_pairs={{0,4},{4,0},{1,5},{5,1},{2,6},{6,2},{3,7},{7,3},{8,12},{12,8},{9,1... | collective-permute-start | bytes 49160 | tf_op jit(solution)/shard_map/ppermute | solution.py:51
  33.3 1.7 %collective-permute-start.8 = (bf16[2,32,256]{2,1,0:T(8,128)(2,1)S(1)}, bf16[2,32,256]{2,1,0:T(8,128)(2,1)S(1)}, u32[]{:S(2)}, u32[]{:S(2)}) collective-permute-start(bf16[2,32,256]{2,1,0:T(8,128)(2,1)S(1)} %shard_map.78), channel_id=1, source_target_pairs={{0,4},{4,0},{1,5},{5,1},{2,6},{6,2},{3,7},{7,3},{8,12},{12,8},{9,1... | collective-permute-start | bytes 98312 | tf_op jit(solution)/shard_map/ppermute | solution.py:51
